TPU v7x, 32 devices: a whole 2x2x4 slice. The times are simulated.
32 devices in a mesh: dp: 4 (over y, x), seq: 8 (over z, core).
Axes of the slice: x: 2, y: 2, z: 4, core: 2. Of those that a mesh axis runs over, the one named last changes fastest.
Arguments:
- caption_states: bfloat16 [4, 64, 4096], P('dp', None, 'seq'), may hold values from -1600 to 1600
- caption_gain: float32 [4096], P('seq'), may hold values from 0.25 to 2.5
- text_proj: bfloat16 [4096, 4608], P('seq'), may hold values from -0.09375 to 0.09375
- caption_len: int32 [4], P('dp'), may hold values from 1 to 64, 160 in all
- slot_source: int32 [4, 64], P('dp'), may hold values from 0 to 63, each once within a row
- query_gain: float32 [128], replicated, may hold values from 0.5 to 2
- key_gain: float32 [128], replicated, may hold values from 0.5 to 2
- image_q: bfloat16 [4, 1024, 1536], P('dp', 'seq'), may hold values from -34 to 34
- image_k: bfloat16 [4, 1024, 1536], P('dp', 'seq'), may hold values from -6.5 to 6.5
- image_v: bfloat16 [4, 1024, 1536], P('dp', 'seq'), may hold values from -6 to 6
- out_weight: bfloat16 [3072, 1536], replicated, may hold values from -0.15625 to 0.15625
- gate: float32 [4, 3072], P('dp'), may hold values from -4 to 4
- d_out: bfloat16 [4, 1024, 3072], P('dp', 'seq'), may hold values from -5 to 5
Outputs:
- image_out: bfloat16 [4, 1024, 3072], P('dp', 'seq')
- text_attn: bfloat16 [4, 64, 1536], P('dp', 'seq')
- d_attn: bfloat16 [4, 1024, 1536], P('dp', 'seq')
- grad_wo: float32 [3072, 1536], P(('dp', 'seq'))
- grad_gate: float32 [4, 3072], P('dp', 'seq')
Inputs may be any that keep to these rules, and one draw needn't show every extreme that they name: `caption_len`: caption lengths in tokens; the longest is 64. `slot_source`: each row is a permutation: every caption row of the sequence sits in exactly one slot; slots whose row is not below the caption's length are padding.
All inputs are finite; a program needn't handle non-finite values. No bound on the sum of `caption_len` on one device may be relied on, other than what follows from the above.
Results may differ from a plain program's by a relative error of at most 0.0095.
Values may be sent and summed in bfloat16 or wider, within the bound.
No kernel may reach another device: no remote copies, remote signals or barrier semaphores. Data moves between devices by JAX's collectives and lax.ppermute only.
A program may use at most 128 MiB of HBM per device.

v0:
```python
import jax
import jax.numpy as jnp
from jax import lax
from jax.sharding import PartitionSpec as P

DT5 = 4096


neg_big = -1e30
eps_norm = 1e-06


def head_norm(values_in, gain_vec):
    shaped = values_in.reshape(values_in.shape[0], -1, gain_vec.shape[0])
    normed = (
        shaped * lax.rsqrt(jnp.mean(shaped * shaped, axis=-1, keepdims=True) + eps_norm) * gain_vec
    )
    return normed.reshape(values_in.shape).astype(jnp.bfloat16)


def text_heads(summed, squares, query_gain, key_gain, inner_width):
    factor = lax.rsqrt(squares / DT5 + eps_norm)
    normed = summed * factor[:, None]
    text_query = head_norm(normed[:, :inner_width], query_gain)
    text_key = head_norm(normed[:, inner_width : 2 * inner_width], key_gain)
    text_value = normed[:, 2 * inner_width :].astype(jnp.bfloat16)
    return (text_query, text_key, text_value)


def start_state(query_heads):
    query_count, head_count, head_size = query_heads.shape
    return (
        jnp.full((head_count, query_count), neg_big, jnp.float32),
        jnp.zeros((head_count, query_count), jnp.float32),
        jnp.zeros((head_count, query_count, head_size), jnp.float32),
    )


def attend(running, query_heads, key_rows, value_rows, usable):
    max_old, total_old, weighted = running
    count_keys = key_rows.shape[0]
    head_size = query_heads.shape[2]
    key_heads = key_rows.reshape(count_keys, -1, head_size)
    value_heads = value_rows.reshape(count_keys, -1, head_size)
    scores = jnp.einsum(
        "qhd,khd->hqk", query_heads, key_heads, preferred_element_type=jnp.float32
    ) * head_size ** (-0.5)
    scores = jnp.where(usable[None, None, :], scores, neg_big)
    max_new = jnp.maximum(max_old, jnp.max(scores, axis=-1))
    weights_now = jnp.where(usable[None, None, :], jnp.exp(scores - max_new[..., None]), 0.0)
    total_new = jnp.sum(weights_now, axis=-1)
    weighted = jnp.einsum(
        "hqk,khd->hqd",
        weights_now.astype(jnp.bfloat16),
        value_heads,
        preferred_element_type=jnp.float32,
    )
    return (max_new, total_new, weighted)


def on_device(
    caption_states,
    caption_gain,
    text_proj,
    caption_len,
    slot_source,
    query_gain,
    key_gain,
    image_q,
    image_k,
    image_v,
    out_weight,
    gate,
    d_out,
):
    seq_count = lax.axis_size("seq")
    seq_index = lax.axis_index("seq")
    slot_total = slot_source.shape[1]
    slot_local = slot_total // seq_count
    image_local = image_q.shape[1]
    inner_width = image_q.shape[2]
    head_size = query_gain.shape[0]
    sources = slot_source[0]
    picked = jnp.take(caption_states[0], sources, axis=0).astype(jnp.float32)
    scaled_rows = (picked * caption_gain).astype(jnp.bfloat16)
    partial_proj = jnp.dot(scaled_rows, text_proj, preferred_element_type=jnp.float32)
    partial_squares = jnp.sum(picked * picked, axis=1)
    usable_slots = sources < caption_len[0]
    own_usable = lax.dynamic_slice_in_dim(usable_slots, seq_index * slot_local, slot_local)
    summed, squares = (
        lax.psum_scatter(partial_proj, "seq", scatter_dimension=0, tiled=True),
        lax.psum_scatter(partial_squares, "seq", scatter_dimension=0, tiled=True),
    )
    text_query, text_key, text_value = text_heads(
        summed, squares, query_gain, key_gain, inner_width
    )
    queries = jnp.concatenate([image_q[0], text_query], axis=0)
    query_heads = queries.reshape(queries.shape[0], -1, head_size)
    key_rows = jnp.concatenate([image_k[0], text_key], axis=0)
    value_rows = jnp.concatenate([image_v[0], text_value], axis=0)
    usable_all = jnp.concatenate(
        [
            jnp.ones((seq_count, image_local), dtype=jnp.bool_),
            usable_slots.reshape(seq_count, slot_local),
        ],
        axis=1,
    ).reshape(-1)
    running = attend(
        start_state(query_heads),
        query_heads,
        lax.all_gather(key_rows, "seq", axis=0, tiled=True),
        lax.all_gather(value_rows, "seq", axis=0, tiled=True),
        usable_all,
    )
    max_final, total_final, weighted = running
    attention = (
        jnp.transpose(weighted / total_final[..., None], (1, 0, 2))
        .reshape(-1, inner_width)
        .astype(jnp.bfloat16)
    )
    image_attn = attention[:image_local]
    text_attn = jnp.where(own_usable[:, None], attention[image_local:], jnp.zeros((), jnp.bfloat16))
    projected = lax.dot_general(
        image_attn, out_weight, (((1,), (1,)), ((), ())), preferred_element_type=jnp.float32
    )
    gate_row = gate[0]
    image_out = (gate_row * projected).astype(jnp.bfloat16)
    cotangent = d_out[0].astype(jnp.float32)
    gated_grad = (gate_row * cotangent).astype(jnp.bfloat16)
    gate_term = jnp.sum(projected * cotangent, axis=0)
    d_attn = jnp.dot(gated_grad, out_weight, preferred_element_type=jnp.float32).astype(
        jnp.bfloat16
    )
    grad_wo = lax.psum_scatter(
        lax.dot_general(
            gated_grad, image_attn, (((0,), (0,)), ((), ())), preferred_element_type=jnp.float32
        ),
        ("dp", "seq"),
        scatter_dimension=0,
        tiled=True,
    )
    grad_gate = lax.psum_scatter(gate_term, "seq", scatter_dimension=0, tiled=True)
    return (image_out[None], text_attn[None], d_attn[None], grad_wo, grad_gate[None])


def solution(mesh):
    in_specs = (
        P("dp", None, "seq"),
        P("seq"),
        P("seq", None),
        P("dp"),
        P("dp", None),
        P(),
        P(),
        P("dp", "seq", None),
        P("dp", "seq", None),
        P("dp", "seq", None),
        P(),
        P("dp", None),
        P("dp", "seq", None),
    )
    out_specs = (
        P("dp", "seq", None),
        P("dp", "seq", None),
        P("dp", "seq", None),
        P(("dp", "seq"), None),
        P("dp", "seq"),
    )
    return jax.shard_map(
        on_device, mesh=mesh, in_specs=in_specs, out_specs=out_specs, check_vma=False
    )
```

profile of v0, /device:TPU:0, one launch (start us, length us, event | category | flops | bytes accessed | tf_op | source)
XLA Modules:
  0.0 364.1 jit_solution(13260516382563535716)
XLA Ops:
  7.2 0.0 copy-start
  7.2 0.0 copy-start.10
  7.2 0.0 copy-start.9
  7.2 0.0 copy-start.8
  7.3 0.0 reduce-scatter.3.cloned.1.call-start
  8.0 0.7 fusion.42
  8.7 0.7 bitcast_compare_fusion
  9.4 0.7 gather_fusion
  10.1 4.3 %fusion.32 = f32[64,4608]{1,0:T(8,128)} fusion(bf16[512,4608]{1,0:T(8,128)(2,1)} %param.15, f32[512]{0:T(512)} %param.14, bf16[64,512]{1,0:T(8,128)(2,1)S(1)} %gather_fusion, pred[64]{0:T(512)(128)(4,1)S(1)} %get-tuple-element.12), kind=kOutput, calls=%fused_computation.35 | convolution fusion | flops 302120960 | bytes 5965888 | tf_op jit(solution)/shard_map/dot_general | solution.py:86
  14.4 0.0 reduce-scatter.3.cloned.1.call-update
  14.5 0.0 all-gather.3.cloned.1.call-start
  14.5 0.6 dynamic-slice
  15.8 0.2 fusion.31
  15.9 18.2 %all-reduce.1 = f32[64]{0:T(128)S(1)} all-reduce(f32[64]{0:T(128)S(1)} %fusion.31), channel_id=3, replica_groups=mesh['dp'=4,'seq'=8] {'seq'}, use_global_device_ids=true, to_apply=%region_2.3.clone | all-reduce | flops 64 | bytes 512
  34.2 0.1 fusion.44
  34.2 16.0 %reduce-scatter.3.cloned.1.call-done = f32[8,4608]{1,0:T(8,128)} async-done(((f32[64,4608]{1,0:T(8,128)}), f32[8,4608]{1,0:T(8,128)}) %reduce-scatter.3.cloned.1.call-update) | async-done | bytes 147472 | tf_op jit(solution)/shard_map/reduce_scatter | solution.py:91
  50.2 1.0 broadcast_multiply_fusion
  51.2 0.1 bitcast_reduce_fusion.1
  51.3 0.1 fusion.39
  51.4 0.8 pad_maximum_fusion
  52.2 0.0 all-gather.3.cloned.1.call-update
  52.2 0.0 all-gather.5.cloned.1.call-start
  52.3 0.8 pad_maximum_fusion.1
  53.1 0.0 all-gather.5.cloned.1.call-update
  53.1 0.0 reduce-scatter.5.cloned.1.call-start
  53.2 0.1 lt.40
  53.3 0.1 broadcast_in_dim.67
  53.4 0.2 copy.25
  53.6 0.2 copy.26
  53.9 36.6 %all-gather.3.cloned.1.call-done = bf16[1088,1536]{1,0:T(8,128)(2,1)} async-done(((bf16[136,1536]{1,0:T(8,128)(2,1)}), bf16[1088,1536]{1,0:T(8,128)(2,1)}) %all-gather.3.cloned.1.call-update) | async-done | bytes 3342352 | tf_op jit(solution)/shard_map/all_gather | solution.py:111
  90.5 5.5 %copy.27 = bf16[1088,1536]{0,1:T(8,128)(2,1)} copy(bf16[1088,1536]{1,0:T(8,128)(2,1)} %all-gather.3.cloned.1.call-done) | data formatting | bytes 6684672 | tf_op jit(solution)/shard_map/all_gather | solution.py:111
  96.0 3.5 fusion
  99.6 3.0 copy-done.1
  102.5 2.1 fusion.1
  104.7 26.8 %all-gather.5.cloned.1.call-done = bf16[1088,1536]{1,0:T(8,128)(2,1)} async-done(((bf16[136,1536]{1,0:T(8,128)(2,1)}), bf16[1088,1536]{1,0:T(8,128)(2,1)}) %all-gather.5.cloned.1.call-update) | async-done | bytes 3342352 | tf_op jit(solution)/shard_map/all_gather | solution.py:112
  131.5 5.5 %copy.29 = bf16[1088,1536]{0,1:T(8,128)(2,1)} copy(bf16[1088,1536]{1,0:T(8,128)(2,1)} %all-gather.5.cloned.1.call-done) | data formatting | bytes 6684672 | tf_op jit(solution)/shard_map/all_gather | solution.py:112
  137.0 6.4 %fusion.19 = bf16[136,12,128]{2,0,1:T(8,128)(2,1)S(1)} fusion(bf16[1088,12,128]{0,2,1:T(8,128)(2,1)} %bitcast.79, f32[12,136,1088]{2,1,0:T(8,128)} %copy-done.1, f32[12,136]{1,0:T(8,128)S(1)} %broadcast_maximum_fusion, pred[1088]{0:T(1024)(128)(4,1)S(1)} %broadcast_in_dim.67, f32[136,12]{0,1:T(8,128)S(1)} %bitcast.86), kind=kOutput, calls=%fused_computation.21 | convolution fusion | flops 463853568 | bytes 10876736 | tf_op jit(solution)/shard_map/hqk,khd->hqd/dot_general | solution.py:52
  143.5 0.2 copy.31
  143.7 8.1 %fusion.23 = f32[3072,1536]{1,0:T(8,128)} fusion(bf16[128,1536]{0,1:T(8,128)(2,1)S(1)} %bitcast.77, bf16[1,128,3072]{2,1,0:T(8,128)(2,1)S(1)} %copy-done.2, f32[3072]{0:T(1024)S(1)} %bitcast.81), kind=kOutput, calls=%fused_computation.23 | convolution fusion | flops 1209139200 | bytes 20066304 | tf_op jit(solution)/shard_map/dot_general | solution.py:135
  151.8 0.0 reduce-scatter.5.cloned.1.call-update
  152.5 0.1 dynamic_slice.3
  152.5 5.8 %fusion.10 = bf16[1,128,1536]{2,1,0:T(8,128)(2,1)} fusion(bf16[3072,1536]{1,0:T(8,128)(2,1)} %param.23, bf16[1,128,3072]{2,1,0:T(8,128)(2,1)S(1)} %copy-done.2, f32[3072]{0:T(1024)S(1)} %bitcast.82), kind=kOutput, calls=%fused_computation.13 | convolution fusion | flops 1209335808 | bytes 10629120 | tf_op jit(solution)/shard_map/dot_general | solution.py:131
  158.4 8.6 %fusion.12 = (f32[3072]{0:T(1024)S(1)}, bf16[1,128,3072]{2,1,0:T(8,128)(2,1)}) fusion(bf16[1,128,3072]{2,1,0:T(8,128)(2,1)S(1)} %copy-done.2, f32[3072]{0:T(1024)S(1)} %bitcast.83, bf16[128,1536]{0,1:T(8,128)(2,1)S(1)} %bitcast.78, bf16[3072,1536]{1,0:T(8,128)(2,1)} %param.23), kind=kOutput, calls=%fused_computation.17 | convolution fusion | flops 1209922560 | bytes 11427840 | tf_op jit(solution)/shard_map/dot_general | solution.py:123
  167.0 26.8 %all-reduce.2 = f32[3072]{0:T(1024)S(1)} all-reduce(f32[3072]{0:T(1024)S(1)} %get-tuple-element.7), channel_id=5, replica_groups=mesh['dp'=4,'seq'=8] {'seq'}, use_global_device_ids=true, to_apply=%region_9.10.clone | all-reduce | flops 3072 | bytes 24576
  193.8 0.1 dynamic-slice.3
  193.8 0.6 broadcast_in_dim.79
  194.4 0.7 fusion.41
  195.1 162.5 %reduce-scatter.5.cloned.1.call-done = f32[96,1536]{1,0:T(8,128)} async-done(((f32[3072,1536]{1,0:T(8,128)}), f32[96,1536]{1,0:T(8,128)}) %reduce-scatter.5.cloned.1.call-update) | async-done | bytes 589840 | tf_op jit(solution)/shard_map/reduce_scatter | solution.py:134
  (25 shorter events, 0.1 us)
Async XLA Ops:
  7.2 2.2 copy-start
  7.2 7.3 %copy-start.10 = (u32[32]{0:T(128)S(1)}, u32[32]{0:T(128)}, u32[]{:S(2)}) copy-start(u32[32]{0:T(128)} %constant.59) | copy-start | bytes 388
  7.2 46.0 %copy-start.9 = (s32[1,64]{1,0:T(1,128)S(1)}, s32[1,64]{1,0:T(1,128)}, u32[]{:S(2)}) copy-start(s32[1,64]{1,0:T(1,128)} %param.17) | copy-start | bytes 772
  7.2 27.0 %copy-start.8 = (f32[128]{0:T(128)S(1)}, f32[128]{0:T(128)}, u32[]{:S(2)}) copy-start(f32[128]{0:T(128)} %param.18) | copy-start | bytes 1540
  7.2 27.0 %copy-start.7 = (f32[128]{0:T(128)S(1)}, f32[128]{0:T(128)}, u32[]{:S(2)}) copy-start(f32[128]{0:T(128)} %param.19) | copy-start | bytes 1540
  7.2 44.2 %copy-start.4 = (bf16[1,128,1536]{2,1,0:T(8,128)(2,1)S(1)}, bf16[1,128,1536]{2,1,0:T(8,128)(2,1)}, u32[]{:S(2)}) copy-start(bf16[1,128,1536]{2,1,0:T(8,128)(2,1)} %param.21) | copy-start | bytes 1179652
  7.2 45.1 %copy-start.5 = (bf16[1,128,1536]{2,1,0:T(8,128)(2,1)S(1)}, bf16[1,128,1536]{2,1,0:T(8,128)(2,1)}, u32[]{:S(2)}) copy-start(bf16[1,128,1536]{2,1,0:T(8,128)(2,1)} %param.22) | copy-start | bytes 1179652
  7.2 46.2 %copy-start.6 = (bf16[1,128,1536]{2,1,0:T(8,128)(2,1)S(1)}, bf16[1,128,1536]{2,1,0:T(8,128)(2,1)}, u32[]{:S(2)}) copy-start(bf16[1,128,1536]{2,1,0:T(8,128)(2,1)} %param.20) | copy-start | bytes 1179652
  7.3 43.0 %reduce-scatter.3.cloned.1.call-start = ((), (), s32[]{:S(2)}) async-start(), calls=%async_computation.2 | async-start | bytes 1327104 | tf_op jit(solution)/shard_map/reduce_scatter | solution.py:91
  14.5 76.0 %all-gather.3.cloned.1.call-start = ((), (), s32[]{:S(2)}) async-start(), calls=%async_computation.3 | async-start | bytes 3760128 | tf_op jit(solution)/shard_map/all_gather | solution.py:111
  52.2 79.2 %all-gather.5.cloned.1.call-start = ((), (), s32[]{:S(2)}) async-start(), calls=%async_computation.4 | async-start | bytes 3760128 | tf_op jit(solution)/shard_map/all_gather | solution.py:112
  53.1 304.5 %reduce-scatter.5.cloned.1.call-start = ((), (), s32[]{:S(2)}) async-start(), calls=%async_computation.5 | async-start | bytes 19464192 | tf_op jit(solution)/shard_map/reduce_scatter | solution.py:134
  99.6 3.0 copy-start.1
  137.0 6.7 %copy-start.2 = (bf16[1,128,3072]{2,1,0:T(8,128)(2,1)S(1)}, bf16[1,128,3072]{2,1,0:T(8,128)(2,1)}, u32[]{:S(2)}) copy-start(bf16[1,128,3072]{2,1,0:T(8,128)(2,1)} %param.25) | copy-start | bytes 2359300
  137.0 6.7 %copy-start.3 = (f32[1,3072]{1,0:T(1,128)S(1)}, f32[1,3072]{1,0:T(1,128)}, u32[]{:S(2)}) copy-start(f32[1,3072]{1,0:T(1,128)} %param.24) | copy-start | bytes 36868
Sparse Core Ops, SparseCore 0:
  14.6 35.5 reduce-scatter.2
  52.4 38.0 all-gather.2
  92.7 38.7 all-gather.4
  151.9 205.6 reduce-scatter.4
where the time goes:
time: 365 us; the launch traced here: 364 us
  waiting for transfers between devices  242 us (66%)
  blocking collectives  45 us (12%)
  matrix products  36.8 us (10%)
  local copies, waits for them, and re-layouts  17 us (5%)
  between operations  16 us (4%)
  other arithmetic  7.18 us (2%)
    reduce_scatter x1, waiting for transfers between devices, on_device(): lax.psum_scatter(lax.dot_general(gated_grad, image_attn, (((0,), (0,)), (...  163 us
    unnamed x2, blocking collectives  45 us
    all_gather x1, waiting for transfers between devices, on_device(): lax.all_gather(key_rows, 'seq', axis=0, tiled=True)  36.6 us
    all_gather x1, waiting for transfers between devices, on_device(): lax.all_gather(value_rows, 'seq', axis=0, tiled=True)  26.8 us
    reduce_scatter x1, waiting for transfers between devices, on_device(): lax.psum_scatter(partial_proj, 'seq', scatter_dimension=0, tiled=True)  16 us
    dot_general x1, matrix products, on_device(): lax.dot_general(image_attn, out_weight, (((1,), (1,)), ((), ())), preferr...  8.57 us
    dot_general x1, matrix products, on_device(): lax.dot_general(gated_grad, image_attn, (((0,), (0,)), ((), ())), preferr...  8.07 us
  transfers between devices with their start and end apart: 4, of which 4 were waited for; matrix products, arithmetic and copies ran while one was open for 8% of the time, Pallas kernels for 0%

commit v1 on v0

v1 whole, which is shorter than its diff:
```python
import math
import functools
import jax
import jax.numpy as jnp
from jax import lax
from jax.experimental import pallas as pl
from jax.experimental.pallas import tpu as pltpu
from jax.sharding import PartitionSpec as P

DT5 = 4096
CORES = 2
GROUPS = 4

eps_norm = 1e-06
f32 = jnp.float32
bf16 = jnp.bfloat16


def head_norm(values_in, gain_vec):
    shaped = values_in.reshape(values_in.shape[0], -1, gain_vec.shape[0])
    normed = (
        shaped * lax.rsqrt(jnp.mean(shaped * shaped, axis=-1, keepdims=True) + eps_norm) * gain_vec
    )
    return normed.reshape(values_in.shape).astype(bf16)


def attention_kernel(pieces, head_size, *refs):
    n_q, n_kv, n_tkv = pieces
    q_refs = refs[:n_q]
    tq_ref = refs[n_q]
    kv_refs = refs[n_q + 1 : n_q + 1 + n_kv]
    tkv_refs = refs[n_q + 1 + n_kv : n_q + 1 + n_kv + n_tkv]
    bias_ref = refs[n_q + 1 + n_kv + n_tkv]
    out_refs = refs[n_q + 2 + n_kv + n_tkv :]
    width = q_refs[0].shape[1]
    factor = head_size ** (-0.5) * math.log2(math.e)
    bias = bias_ref[...]
    for head in range(width // head_size):
        cols = slice(head * head_size, (head + 1) * head_size)
        vcols = slice(width + head * head_size, width + (head + 1) * head_size)
        keys = jnp.concatenate([r[:, cols] for r in kv_refs], axis=0)
        values = jnp.concatenate([r[:, vcols] for r in kv_refs], axis=0)
        tkeys = jnp.concatenate([r[:, cols] for r in tkv_refs], axis=0)
        tvalues = jnp.concatenate([r[:, vcols] for r in tkv_refs], axis=0)
        for q_ref, out_ref in zip(tuple(q_refs) + (tq_ref,), out_refs):
            q = q_ref[:, cols]
            nt = (((1,), (1,)), ((), ()))
            s_img = lax.dot_general(q, keys, nt, preferred_element_type=f32)
            s_txt = lax.dot_general(q, tkeys, nt, preferred_element_type=f32) + bias
            top = jnp.maximum(
                jnp.max(s_img, axis=1, keepdims=True), jnp.max(s_txt, axis=1, keepdims=True)
            )
            p_img = jnp.exp2((s_img - top) * factor)
            p_txt = jnp.exp2((s_txt - top) * factor)
            total = jnp.sum(p_img, axis=1, keepdims=True) + jnp.sum(p_txt, axis=1, keepdims=True)
            acc = jnp.dot(p_img.astype(bf16), values, preferred_element_type=f32)
            acc = acc + jnp.dot(p_txt.astype(bf16), tvalues, preferred_element_type=f32)
            out_ref[:, cols] = (acc / total).astype(bf16)


def attention(queries, text_q, keyvals, text_keyvals, bias, head_size):
    args = tuple(queries) + (text_q,) + tuple(keyvals) + tuple(text_keyvals) + (bias,)
    outs = [jax.ShapeDtypeStruct(q.shape, bf16) for q in tuple(queries) + (text_q,)]
    vmem = pl.BlockSpec(memory_space=pltpu.VMEM)
    rows = sum(q.shape[0] for q in queries) + text_q.shape[0]
    cols = sum(k.shape[0] for k in keyvals) + sum(k.shape[0] for k in text_keyvals)
    width = text_q.shape[1]
    return pl.pallas_call(
        functools.partial(
            attention_kernel, (len(queries), len(keyvals), len(text_keyvals)), head_size
        ),
        out_shape=outs,
        in_specs=[vmem] * len(args),
        out_specs=[vmem] * len(outs),
        compiler_params=pltpu.CompilerParams(vmem_limit_bytes=32 * 1024 * 1024),
        cost_estimate=pl.CostEstimate(
            flops=4 * rows * cols * width,
            bytes_accessed=4 * (rows + cols) * width,
            transcendentals=rows * cols * width // head_size,
        ),
    )(*args)


def grad_kernel(n_pieces, *refs):
    left = refs[0]
    pieces = refs[1 : 1 + n_pieces]
    out = refs[1 + n_pieces]
    depth = pieces[0].shape[0]
    block = 256
    for start in range(0, out.shape[1], block):
        cols = slice(start, start + block)
        right = jnp.concatenate([p[:, cols] for p in pieces], axis=0)
        out[:, cols] = jnp.dot(left[...], right, preferred_element_type=f32).astype(bf16)


def grad_product(left, pieces):
    vmem = pl.BlockSpec(memory_space=pltpu.VMEM)
    rows, depth, width = left.shape[0], left.shape[1], pieces[0].shape[1]
    return pl.pallas_call(
        functools.partial(grad_kernel, len(pieces)),
        out_shape=jax.ShapeDtypeStruct((rows, width), bf16),
        in_specs=[vmem] * (1 + len(pieces)),
        out_specs=vmem,
        compiler_params=pltpu.CompilerParams(vmem_limit_bytes=32 * 1024 * 1024),
        cost_estimate=pl.CostEstimate(
            flops=2 * rows * depth * width,
            bytes_accessed=2 * (rows * depth + depth * width + rows * width),
            transcendentals=0,
        ),
    )(left, *pieces)


def on_device(
    caption_states,
    caption_gain,
    text_proj,
    caption_len,
    slot_source,
    query_gain,
    key_gain,
    image_q,
    image_k,
    image_v,
    out_weight,
    gate,
    d_out,
):
    n_dp = lax.axis_size("dp")
    n_seq = lax.axis_size("seq")
    G, C = GROUPS, CORES
    O = n_seq // (G * C)
    OC = O * C
    dp = lax.axis_index("dp")
    seq = lax.axis_index("seq")
    z = (seq // C) % G
    oc = (seq // (G * C)) * C + seq % C

    def place(oc_at, z_at):
        return ((oc_at // C) * G + z_at) * C + oc_at % C

    def to_z(x, k):
        perm = [(place(a, b), place(a, b ^ k)) for a in range(OC) for b in range(G)]
        return lax.ppermute(x, "seq", perm)

    def to_oc(x, j):
        perm = [(place(a, b), place(a ^ j, b)) for a in range(OC) for b in range(G)]
        return lax.ppermute(x, "seq", perm)

    def to_dp(x, k):
        return lax.ppermute(x, "dp", [(a, a ^ k) for a in range(n_dp)])

    def part(x, index, size, axis):
        return lax.dynamic_slice_in_dim(x, index * size, size, axis)

    slot_total = slot_source.shape[1]
    slot_local = slot_total // n_seq
    image_local = image_q.shape[1]
    inner_width = image_q.shape[2]
    model_width = out_weight.shape[0]
    head_size = query_gain.shape[0]
    gw = inner_width // G
    q_all, k_all, v_all = image_q[0], image_k[0], image_v[0]

    kv_own = [
        jnp.concatenate([part(k_all, z ^ k, gw, 1), part(v_all, z ^ k, gw, 1)], axis=1)
        for k in range(G)
    ]
    kv_near = [kv_own[0]] + [to_z(kv_own[k], k) for k in range(1, G)]
    q_own = [part(q_all, z ^ k, gw, 1) for k in range(G)]
    q_pieces = [q_own[0]] + [to_z(q_own[k], k) for k in range(1, G)]
    kv_pieces = list(kv_near)
    for j in range(1, OC):
        kv_pieces += [to_oc(p, j) for p in kv_near]

    sources = slot_source[0].reshape(O, G, C, slot_local)
    sources = jnp.transpose(sources, (0, 2, 1, 3)).reshape(-1)
    picked = jnp.take(caption_states[0], sources, axis=0).astype(f32)
    scaled_rows = (picked * caption_gain).astype(bf16)
    partial_proj = jnp.dot(scaled_rows, text_proj, preferred_element_type=f32)
    partial_squares = jnp.sum(picked * picked, axis=1, keepdims=True)
    usable = (sources < caption_len[0]).astype(jnp.int32).reshape(OC, G * slot_local)
    text_rows = G * slot_local

    def message(values, squares):
        high = lax.reduce_precision(squares, 8, 7)
        low = squares - high
        tail = jnp.concatenate(
            [high, low, jnp.zeros((squares.shape[0], 126), f32)], axis=1
        ).astype(bf16)
        return jnp.concatenate([values.astype(bf16), tail], axis=1)

    def opened(got):
        got = got.astype(f32)
        width = got.shape[1] - 128
        return got[:, :width], got[:, width : width + 1] + got[:, width + 1 : width + 2]

    chip_proj = part(partial_proj, oc, text_rows, 0)
    chip_squares = part(partial_squares, oc, text_rows, 0)
    for j in range(1, OC):
        sent = message(
            part(partial_proj, oc ^ j, text_rows, 0), part(partial_squares, oc ^ j, text_rows, 0)
        )
        more_proj, more_squares = opened(to_oc(sent, j))
        chip_proj = chip_proj + more_proj
        chip_squares = chip_squares + more_squares
    chip_proj = chip_proj.reshape(text_rows, 3, inner_width)

    def group_cols(index):
        return part(chip_proj, index, gw, 2).reshape(text_rows, 3 * gw)

    summed, squares = group_cols(z), chip_squares
    for k in range(1, G):
        more, more_squares = opened(to_z(message(group_cols(z ^ k), chip_squares), k))
        summed = summed + more
        squares = squares + more_squares
    normed = summed * lax.rsqrt(squares / DT5 + eps_norm)
    text_q = head_norm(normed[:, :gw], query_gain)
    text_k = head_norm(normed[:, gw : 2 * gw], key_gain)
    text_kv = jnp.concatenate([text_k, normed[:, 2 * gw :].astype(bf16)], axis=1)
    text_kvs = [text_kv] + [to_oc(text_kv, j) for j in range(1, OC)]
    usable_keys = jnp.concatenate([part(usable, oc ^ j, 1, 0) for j in range(OC)], axis=1)
    bias = jnp.where(usable_keys > 0, 0.0, -1e30).astype(f32)

    gate_row = gate[0]
    cotangent = d_out[0].astype(f32)
    gated_grad = (gate_row * cotangent).astype(bf16)
    R = model_width // (n_dp * n_seq)
    gg_t = gated_grad.T.reshape(n_dp, O, G, C, R, image_local)
    gg_t = jnp.transpose(gg_t, (0, 1, 3, 2, 4, 5)).reshape(n_dp, OC, G * R, image_local)
    gg_dp = []
    for k in range(n_dp):
        sel = lax.dynamic_index_in_dim(gg_t, dp ^ k, 0, keepdims=False)
        gg_dp.append(sel if k == 0 else to_dp(sel, k))
    gg_left = []
    for j in range(OC):
        sel = [lax.dynamic_index_in_dim(g, oc ^ j, 0, keepdims=False) for g in gg_dp]
        if j:
            sent = to_oc(jnp.stack(sel), j)
            sel = [sent[k] for k in range(n_dp)]
        gg_left += sel
    left = jnp.concatenate(gg_left, axis=1)
    d_attn = jnp.dot(gated_grad, out_weight, preferred_element_type=f32).astype(bf16)

    outs = attention(q_pieces, text_q, kv_pieces, text_kvs, bias, head_size)
    text_out = outs[-1]

    back = []
    for k in range(G):
        rows = jnp.concatenate([outs[k], part(text_out, z ^ k, slot_local, 0)], axis=0)
        back.append(rows if k == 0 else to_z(rows, k))
    attn = jnp.zeros((image_local + slot_local, inner_width), bf16)
    for k in range(G):
        attn = lax.dynamic_update_slice_in_dim(attn, back[k], (z ^ k) * gw, 1)
    image_attn = attn[:image_local]
    own_usable = part((slot_source[0] < caption_len[0]), seq, slot_local, 0)
    text_attn = jnp.where(own_usable[:, None], attn[image_local:], jnp.zeros((), bf16))

    attn_dp = [image_attn] + [to_dp(image_attn, k) for k in range(1, n_dp)]
    attn_pieces = list(attn_dp)
    for j in range(1, OC):
        attn_pieces += [to_oc(p, j) for p in attn_dp]

    projected = lax.dot_general(
        image_attn, out_weight, (((1,), (1,)), ((), ())), preferred_element_type=f32
    )
    image_out = (gate_row * projected).astype(bf16)
    gate_term = jnp.sum(projected * cotangent, axis=0)

    grad = grad_product(left, attn_pieces).reshape(G, R, inner_width)
    grad_wo = lax.dynamic_index_in_dim(grad, z, 0, keepdims=False).astype(f32)
    for k in range(1, G):
        sent = to_z(lax.dynamic_index_in_dim(grad, z ^ k, 0, keepdims=False), k)
        grad_wo = grad_wo + sent.astype(f32)

    gate_term = jnp.transpose(gate_term.reshape(O, G, C, -1), (0, 2, 1, 3)).reshape(OC, G, 1, -1)
    gate_chip = lax.dynamic_index_in_dim(gate_term, oc, 0, keepdims=False)
    for j in range(1, OC):
        gate_chip = gate_chip + to_oc(
            lax.dynamic_index_in_dim(gate_term, oc ^ j, 0, keepdims=False), j
        )
    grad_gate = lax.dynamic_index_in_dim(gate_chip, z, 0, keepdims=False)
    for k in range(1, G):
        grad_gate = grad_gate + to_z(
            lax.dynamic_index_in_dim(gate_chip, z ^ k, 0, keepdims=False), k
        )
    return (image_out[None], text_attn[None], d_attn[None], grad_wo, grad_gate)


def solution(mesh):
    in_specs = (
        P("dp", None, "seq"),
        P("seq"),
        P("seq", None),
        P("dp"),
        P("dp", None),
        P(),
        P(),
        P("dp", "seq", None),
        P("dp", "seq", None),
        P("dp", "seq", None),
        P(),
        P("dp", None),
        P("dp", "seq", None),
    )
    out_specs = (
        P("dp", "seq", None),
        P("dp", "seq", None),
        P("dp", "seq", None),
        P(("dp", "seq"), None),
        P("dp", "seq"),
    )
    return jax.shard_map(
        on_device, mesh=mesh, in_specs=in_specs, out_specs=out_specs, check_vma=False
    )
```

time: 365 us -> 151 us (0.41)
  the two profiles are of different devices: /device:TPU:0 before, /device:TPU:8 now
where the time goes in v1:
time: 151 us
  waiting for transfers between devices  68.1 us (45%)
  starting transfers between devices  37.8 us (25%)
  matrix products  17.2 us (11%)
  local copies, waits for them, and re-layouts  9.67 us (6%)
  other arithmetic  8.5 us (6%)
  Pallas kernels  7.21 us (5%)
  between operations  2.01 us (1%)
    ppermute x18, waiting for transfers between devices, to_z(): return lax.ppermute(x, 'seq', perm)  47.2 us
    ppermute x18, starting transfers between devices, to_z(): return lax.ppermute(x, 'seq', perm)  28.3 us
    ppermute x6, waiting for transfers between devices, to_dp(): return lax.ppermute(x, 'dp', [(a, a ^ k) for a in range(n_dp)])  19.8 us
    ppermute x6, starting transfers between devices, to_dp(): return lax.ppermute(x, 'dp', [(a, a ^ k) for a in range(n_dp)])  8.14 us
    dot_general x1, matrix products, on_device(): lax.dot_general(image_attn, out_weight, (((1,), (1,)), ((), ())), preferr...  8.05 us
    dot_general x1, matrix products, on_device(): jnp.dot(gated_grad, out_weight, preferred_element_type=f32).astype(bf16)  5.84 us
    pallas_call x1, Pallas kernels, attention(): pl.pallas_call(functools.partial(attention_kernel, (len(queries), len(key...  5.83 us
    dot_general x1, matrix products, on_device(): partial_proj = jnp.dot(scaled_rows, text_proj, preferred_element_type=f32)  3.34 us
  transfers between devices with their start and end apart: 36, of which 14 were waited for; matrix products, arithmetic and copies ran while one was open for 12% of the time, Pallas kernels for 1%

profile of v1, /device:TPU:8, one launch (start us, length us, event | category | flops | bytes accessed | tf_op | source)
XLA Modules:
  0.0 150.5 jit_solution(7198177709390090237)
XLA Ops:
  1.2 1.3 reduce.5
  2.8 0.7 gather_fusion
  3.7 3.3 %fusion.15 = f32[64,4608]{1,0:T(8,128)S(1)} fusion(bf16[512,4608]{1,0:T(8,128)(2,1)} %param.15, f32[512]{0:T(512)} %param.14, bf16[64,512]{1,0:T(8,128)(2,1)S(1)} %gather_fusion, pred[64]{0:T(512)(128)(4,1)S(1)} %compare_and_fusion), kind=kOutput, calls=%fused_computation.66 | convolution fusion | flops 302120960 | bytes 5965888 | tf_op jit(solution)/shard_map/dot_general | solution.py:179
  7.4 0.8 concatenate.63
  8.2 1.1 dynamic-slice_bitcast_fusion.7
  9.4 0.7 pad_maximum_fusion.2
  10.1 3.1 %collective-permute-start.8 = (bf16[128,768]{1,0:T(8,128)(2,1)S(1)}, bf16[128,768]{1,0:T(8,128)(2,1)S(1)}, u32[]{:S(2)}, u32[]{:S(2)}) collective-permute-start(bf16[128,768]{1,0:T(8,128)(2,1)S(1)} %pad_maximum_fusion.3), channel_id=1, source_target_pairs={{0,4},{2,6},{4,0},{6,2},{1,5},{3,7},{5,1},{7,3},{8,12},{10,14},{12... | collective-permute-start | bytes 589832 | tf_op jit(solution)/shard_map/ppermute | solution.py:143
  13.2 0.7 copy.43
  14.7 0.7 dynamic-slice_bitcast_fusion.15
  15.9 0.7 pad_maximum_fusion.4
  16.7 5.8 %fusion = bf16[1,128,1536]{2,1,0:T(8,128)(2,1)} fusion(bf16[3072,1536]{1,0:T(8,128)(2,1)} %param.23, bf16[1,128,3072]{2,1,0:T(8,128)(2,1)S(1)} %copy-done.1, f32[3072]{0:T(1024)S(1)} %bitcast.171), kind=kOutput, calls=%fused_computation.2 | convolution fusion | flops 1209335808 | bytes 10629120 | tf_op jit(solution)/shard_map/dot_general | solution.py:242
  22.6 1.0 convert_element_type.90
  23.6 0.9 slice_add_fusion
  24.5 1.5 reshape.180
  26.4 1.6 %collective-permute-start.4 = (bf16[32,1280]{1,0:T(8,128)(2,1)S(1)}, bf16[32,1280]{1,0:T(8,128)(2,1)S(1)}, u32[]{:S(2)}, u32[]{:S(2)}) collective-permute-start(bf16[32,1280]{1,0:T(8,128)(2,1)S(1)} %concatenate.64), channel_id=1, source_target_pairs={{0,2},{2,0},{4,6},{6,4},{1,3},{3,1},{5,7},{7,5},{8,10},{10,8},{12,... | collective-permute-start | bytes 245768 | tf_op jit(solution)/shard_map/ppermute | solution.py:143
  28.6 1.6 %collective-permute-start.6 = (bf16[32,1280]{1,0:T(8,128)(2,1)S(1)}, bf16[32,1280]{1,0:T(8,128)(2,1)S(1)}, u32[]{:S(2)}, u32[]{:S(2)}) collective-permute-start(bf16[32,1280]{1,0:T(8,128)(2,1)S(1)} %concatenate.66), channel_id=1, source_target_pairs={{0,6},{2,4},{4,2},{6,0},{1,7},{3,5},{5,3},{7,1},{8,14},{10,12},{12... | collective-permute-start | bytes 245768 | tf_op jit(solution)/shard_map/ppermute | solution.py:143
  30.3 1.3 collective-permute-done.4
  31.6 5.9 %collective-permute-done.5 = bf16[32,1280]{1,0:T(8,128)(2,1)S(1)} collective-permute-done((bf16[32,1280]{1,0:T(8,128)(2,1)S(1)}, bf16[32,1280]{1,0:T(8,128)(2,1)S(1)}, u32[]{:S(2)}, u32[]{:S(2)}) %collective-permute-start.5) | collective-permute-done | bytes 81952 | tf_op jit(solution)/shard_map/ppermute | solution.py:143
  37.5 4.9 %collective-permute-start = (bf16[128,384]{1,0:T(8,128)(2,1)}, bf16[128,384]{1,0:T(8,128)(2,1)S(1)}, u32[]{:S(2)}, u32[]{:S(2)}) collective-permute-start(bf16[128,384]{1,0:T(8,128)(2,1)} %get-tuple-element.38), channel_id=1, source_target_pairs={{0,2},{2,0},{4,6},{6,4},{1,3},{3,1},{5,7},{7,5},{8,10},{10,8},{12,... | collective-permute-start | bytes 294920 | tf_op jit(solution)/shard_map/ppermute | solution.py:143
  43.6 1.8 %collective-permute-done.refs_1_ = bf16[128,384]{1,0:T(8,128)(2,1)S(1)} collective-permute-done((bf16[128,384]{1,0:T(8,128)(2,1)}, bf16[128,384]{1,0:T(8,128)(2,1)S(1)}, u32[]{:S(2)}, u32[]{:S(2)}) %collective-permute-start) | collective-permute-done | bytes 98336 | tf_op jit(solution)/shard_map/ppermute | solution.py:143
  45.4 3.1 %collective-permute-done.1.refs_2_ = bf16[128,384]{1,0:T(8,128)(2,1)S(1)} collective-permute-done((bf16[128,384]{1,0:T(8,128)(2,1)}, bf16[128,384]{1,0:T(8,128)(2,1)S(1)}, u32[]{:S(2)}, u32[]{:S(2)}) %collective-permute-start.1) | collective-permute-done | bytes 98336 | tf_op jit(solution)/shard_map/ppermute | solution.py:143
  48.5 1.1 collective-permute-start.2
  50.2 4.0 %collective-permute-done.2.refs_3_ = bf16[128,384]{1,0:T(8,128)(2,1)S(1)} collective-permute-done((bf16[128,384]{1,0:T(8,128)(2,1)S(1)}, bf16[128,384]{1,0:T(8,128)(2,1)S(1)}, u32[]{:S(2)}, u32[]{:S(2)}) %collective-permute-start.2) | collective-permute-done | bytes 98336 | tf_op jit(solution)/shard_map/ppermute | solution.py:143
  54.4 1.1 collective-permute-done.14.refs_14_
  55.4 5.8 %shard_map.164 = (bf16[128,384]{1,0:T(8,128)(2,1)S(1)}, bf16[128,384]{1,0:T(8,128)(2,1)S(1)}, bf16[128,384]{1,0:T(8,128)(2,1)S(1)}, bf16[128,384]{1,0:T(8,128)(2,1)S(1)}, bf16[32,384]{1,0:T(8,128)(2,1)S(1)}) custom-call(bf16[128,384]{1,0:T(8,128)(2,1)S(1)} %get-tuple-element.39.refs_0_, bf16[128,384]{1,0:T(8,128)(2,1)S(1)} %collective-permute-done.refs_1_, ...), custom_call_target="tpu_custom_call" | custom-call | flops 909115392 | bytes 2506752 | tf_op jit(solution)/shard_map/pallas_call | solution.py:68
  61.5 6.0 %collective-permute-start.16 = (bf16[136,384]{1,0:T(8,128)(2,1)S(1)}, bf16[136,384]{1,0:T(8,128)(2,1)S(1)}, u32[]{:S(2)}, u32[]{:S(2)}) collective-permute-start(bf16[136,384]{1,0:T(8,128)(2,1)S(1)} %pad_maximum_fusion.6), channel_id=1, source_target_pairs={{0,4},{2,6},{4,0},{6,2},{1,5},{3,7},{5,1},{7,3},{8,12},{10,14},{12... | collective-permute-start | bytes 313352 | tf_op jit(solution)/shard_map/ppermute | solution.py:143
  67.6 6.4 %collective-permute-done.15 = bf16[136,384]{1,0:T(8,128)(2,1)S(1)} collective-permute-done((bf16[136,384]{1,0:T(8,128)(2,1)S(1)}, bf16[136,384]{1,0:T(8,128)(2,1)S(1)}, u32[]{:S(2)}, u32[]{:S(2)}) %collective-permute-start.15) | collective-permute-done | bytes 104480 | tf_op jit(solution)/shard_map/ppermute | solution.py:143
  74.1 8.0 %fusion.2 = (f32[3072]{0:T(1024)S(1)}, bf16[1,128,3072]{2,1,0:T(8,128)(2,1)}, bf16[3072,128]{0,1:T(8,128)(2,1)}) fusion(bf16[1,128,3072]{2,1,0:T(8,128)(2,1)S(1)} %copy-done.1, f32[3072]{0:T(1024)S(1)} %bitcast.172, bf16[3072,1536]{1,0:T(8,128)(2,1)} %param.23, bf16[136,1536]{1,0:T(8,128)(2,1)S(1)} %constant_dynamic-update-slice_fusion), kind=kOutput, calls=%fused_computation.6 | convolution fusion | flops 1210708992 | bytes 12214272 | tf_op jit(solution)/shard_map/dot_general | solution.py:263
  82.2 1.6 %collective-permute-start.22 = (bf16[128,1536]{1,0:T(8,128)(2,1)S(1)}, bf16[128,1536]{1,0:T(8,128)(2,1)S(1)}, u32[]{:S(2)}, u32[]{:S(2)}) collective-permute-start(bf16[128,1536]{1,0:T(8,128)(2,1)S(1)} %slice.102.refs_1_), channel_id=1, source_target_pairs={{0,8},{8,0},{16,24},{24,16},{1,9},{9,1},{17,25},{25,17},{2,10},{10... | collective-permute-start | bytes 1179656 | tf_op jit(solution)/shard_map/ppermute | solution.py:150
  83.8 1.5 %collective-permute-start.23 = (bf16[128,1536]{1,0:T(8,128)(2,1)S(1)}, bf16[128,1536]{1,0:T(8,128)(2,1)S(1)}, u32[]{:S(2)}, u32[]{:S(2)}) collective-permute-start(bf16[128,1536]{1,0:T(8,128)(2,1)S(1)} %slice.102.refs_1_), channel_id=1, source_target_pairs={{0,16},{8,24},{16,0},{24,8},{1,17},{9,25},{17,1},{25,9},{2,18},{10... | collective-permute-start | bytes 1179656 | tf_op jit(solution)/shard_map/ppermute | solution.py:150
  85.9 1.5 copy.44
  87.5 2.5 %collective-permute-start.20 = (bf16[2,384,128]{2,1,0:T(8,128)(2,1)S(1)}, bf16[2,384,128]{2,1,0:T(8,128)(2,1)S(1)}, u32[]{:S(2)}, u32[]{:S(2)}) collective-permute-start(bf16[2,384,128]{2,1,0:T(8,128)(2,1)S(1)} %get-tuple-element.23), channel_id=1, source_target_pairs={{0,24},{8,16},{16,8},{24,0},{1,25},{9,17},{17,9},{25,1},{2,26},{10... | collective-permute-start | bytes 589832 | tf_op jit(solution)/shard_map/ppermute | solution.py:150
  90.1 0.6 collective-permute-start.19
  90.7 15.7 %collective-permute-done.20 = bf16[2,384,128]{2,1,0:T(8,128)(2,1)S(1)} collective-permute-done((bf16[2,384,128]{2,1,0:T(8,128)(2,1)S(1)}, bf16[2,384,128]{2,1,0:T(8,128)(2,1)S(1)}, u32[]{:S(2)}, u32[]{:S(2)}) %collective-permute-start.20) | collective-permute-done | bytes 196640 | tf_op jit(solution)/shard_map/ppermute | solution.py:150
  106.3 1.5 collective-permute-start.18
  107.8 2.8 %collective-permute-done.19 = bf16[2,384,128]{2,1,0:T(8,128)(2,1)S(1)} collective-permute-done((bf16[2,384,128]{2,1,0:T(8,128)(2,1)S(1)}, bf16[2,384,128]{2,1,0:T(8,128)(2,1)S(1)}, u32[]{:S(2)}, u32[]{:S(2)}) %collective-permute-start.19) | collective-permute-done | bytes 196640 | tf_op jit(solution)/shard_map/ppermute | solution.py:150
  110.7 1.3 collective-permute-done.18
  112.3 3.2 %collective-permute-start.33 = (f32[1,384]{1,0:T(1,128)S(1)}, f32[1,384]{1,0:T(1,128)S(1)}, u32[]{:S(2)}, u32[]{:S(2)}) collective-permute-start(f32[1,384]{1,0:T(1,128)S(1)} %get-tuple-element.49), channel_id=1, source_target_pairs={{0,2},{2,0},{4,6},{6,4},{1,3},{3,1},{5,7},{7,5},{8,10},{10,8},{12,... | collective-permute-start | bytes 4616 | tf_op jit(solution)/shard_map/ppermute | solution.py:143
  116.4 1.1 collective-permute-start.34
  117.5 1.4 collective-permute-start.35
  118.9 1.4 shard_map.165
  120.3 2.1 %collective-permute-start.29 = (bf16[96,1536]{1,0:T(8,128)(2,1)S(1)}, bf16[96,1536]{1,0:T(8,128)(2,1)S(1)}, u32[]{:S(2)}, u32[]{:S(2)}) collective-permute-start(bf16[96,1536]{1,0:T(8,128)(2,1)S(1)} %get-tuple-element.19), channel_id=1, source_target_pairs={{0,2},{2,0},{4,6},{6,4},{1,3},{3,1},{5,7},{7,5},{8,10},{10,8},{12,... | collective-permute-start | bytes 884744 | tf_op jit(solution)/shard_map/ppermute | solution.py:143
  122.5 1.4 collective-permute-start.31
  123.9 0.7 fusion.22
  125.2 8.6 %collective-permute-done.29 = bf16[96,1536]{1,0:T(8,128)(2,1)S(1)} collective-permute-done((bf16[96,1536]{1,0:T(8,128)(2,1)S(1)}, bf16[96,1536]{1,0:T(8,128)(2,1)S(1)}, u32[]{:S(2)}, u32[]{:S(2)}) %collective-permute-start.29) | collective-permute-done | bytes 294944 | tf_op jit(solution)/shard_map/ppermute | solution.py:143
  133.7 8.9 %collective-permute-done.30 = bf16[96,1536]{1,0:T(8,128)(2,1)S(1)} collective-permute-done((bf16[96,1536]{1,0:T(8,128)(2,1)S(1)}, bf16[96,1536]{1,0:T(8,128)(2,1)S(1)}, u32[]{:S(2)}, u32[]{:S(2)}) %collective-permute-start.30) | collective-permute-done | bytes 294944 | tf_op jit(solution)/shard_map/ppermute | solution.py:143
  142.6 7.0 %collective-permute-done.31 = bf16[96,1536]{1,0:T(8,128)(2,1)S(1)} collective-permute-done((bf16[96,1536]{1,0:T(8,128)(2,1)S(1)}, bf16[96,1536]{1,0:T(8,128)(2,1)S(1)}, u32[]{:S(2)}, u32[]{:S(2)}) %collective-permute-start.31) | collective-permute-done | bytes 294944 | tf_op jit(solution)/shard_map/ppermute | solution.py:143
  149.6 1.0 fusion.7
  (147 shorter events, 7.9 us)
Async XLA Ops:
  0.6 2.2 %copy-start = (bf16[1,64,512]{2,1,0:T(8,128)(2,1)S(1)}, bf16[1,64,512]{2,1,0:T(8,128)(2,1)}, u32[]{:S(2)}) copy-start(bf16[1,64,512]{2,1,0:T(8,128)(2,1)} %param.13) | copy-start | bytes 196612
  7.0 1.2 copy-start.3
  7.1 7.6 %copy-start.2 = (bf16[1,128,1536]{2,1,0:T(8,128)(2,1)S(1)}, bf16[1,128,1536]{2,1,0:T(8,128)(2,1)}, u32[]{:S(2)}) copy-start(bf16[1,128,1536]{2,1,0:T(8,128)(2,1)} %param.20) | copy-start | bytes 1179652
  8.2 14.4 %collective-permute-start.3 = (bf16[32,4736]{1,0:T(8,128)(2,1)}, bf16[32,4736]{1,0:T(8,128)(2,1)}, u32[]{:S(2)}, u32[]{:S(2)}) collective-permute-start(bf16[32,4736]{1,0:T(8,128)(2,1)} %concatenate.63), channel_id=1, source_target_pairs={{0,1},{2,3},{4,5},{6,7},{1,0},{3,2},{5,4},{7,6},{8,9},{10,11},{12,... | collective-permute-start | bytes 909320 | tf_op jit(solution)/shard_map/ppermute | solution.py:147
  8.2 7.2 %copy-start.9 = (s32[1,64]{1,0:T(1,128)S(1)}, s32[1,64]{1,0:T(1,128)}, u32[]{:S(2)}) copy-start(s32[1,64]{1,0:T(1,128)} %param.17) | copy-start | bytes 772
  9.4 7.3 %copy-start.1 = (bf16[1,128,3072]{2,1,0:T(8,128)(2,1)S(1)}, bf16[1,128,3072]{2,1,0:T(8,128)(2,1)}, u32[]{:S(2)}) copy-start(bf16[1,128,3072]{2,1,0:T(8,128)(2,1)} %param.25) | copy-start | bytes 2359300
  9.4 7.3 %copy-start.4 = (f32[1,3072]{1,0:T(1,128)S(1)}, f32[1,3072]{1,0:T(1,128)}, u32[]{:S(2)}) copy-start(f32[1,3072]{1,0:T(1,128)} %param.24) | copy-start | bytes 36868
  10.1 39.5 %collective-permute-start.7 = (bf16[128,768]{1,0:T(8,128)(2,1)}, bf16[128,768]{1,0:T(8,128)(2,1)S(1)}, u32[]{:S(2)}, u32[]{:S(2)}) collective-permute-start(bf16[128,768]{1,0:T(8,128)(2,1)} %pad_maximum_fusion.2), channel_id=1, source_target_pairs={{0,2},{2,0},{4,6},{6,4},{1,3},{3,1},{5,7},{7,5},{8,10},{10,8},{12,... | collective-permute-start | bytes 589832 | tf_op jit(solution)/shard_map/ppermute | solution.py:143
  10.1 39.5 %collective-permute-start.8 = (bf16[128,768]{1,0:T(8,128)(2,1)S(1)}, bf16[128,768]{1,0:T(8,128)(2,1)S(1)}, u32[]{:S(2)}, u32[]{:S(2)}) collective-permute-start(bf16[128,768]{1,0:T(8,128)(2,1)S(1)} %pad_maximum_fusion.3), channel_id=1, source_target_pairs={{0,4},{2,6},{4,0},{6,2},{1,5},{3,7},{5,1},{7,3},{8,12},{10,14},{12... | collective-permute-start | bytes 589832 | tf_op jit(solution)/shard_map/ppermute | solution.py:143
  16.7 5.9 %copy-start.7 = (f32[128]{0:T(128)S(1)}, f32[128]{0:T(128)}, u32[]{:S(2)}) copy-start(f32[128]{0:T(128)} %param.19) | copy-start | bytes 1540
  16.7 5.9 %copy-start.8 = (f32[128]{0:T(128)S(1)}, f32[128]{0:T(128)}, u32[]{:S(2)}) copy-start(f32[128]{0:T(128)} %param.18) | copy-start | bytes 1540
  24.5 1.7 %copy-start.6 = (f32[32,1]{1,0:T(8,128)S(1)}, f32[32,1]{1,0:T(8,128)}, u32[]{:S(2)}) copy-start(f32[32,1]{1,0:T(8,128)} %copy.43) | copy-start | bytes 388
  26.4 5.2 %collective-permute-start.4 = (bf16[32,1280]{1,0:T(8,128)(2,1)S(1)}, bf16[32,1280]{1,0:T(8,128)(2,1)S(1)}, u32[]{:S(2)}, u32[]{:S(2)}) collective-permute-start(bf16[32,1280]{1,0:T(8,128)(2,1)S(1)} %concatenate.64), channel_id=1, source_target_pairs={{0,2},{2,0},{4,6},{6,4},{1,3},{3,1},{5,7},{7,5},{8,10},{10,8},{12,... | collective-permute-start | bytes 245768 | tf_op jit(solution)/shard_map/ppermute | solution.py:143
  28.1 9.4 %collective-permute-start.5 = (bf16[32,1280]{1,0:T(8,128)(2,1)S(1)}, bf16[32,1280]{1,0:T(8,128)(2,1)S(1)}, u32[]{:S(2)}, u32[]{:S(2)}) collective-permute-start(bf16[32,1280]{1,0:T(8,128)(2,1)S(1)} %concatenate.65), channel_id=1, source_target_pairs={{0,4},{2,6},{4,0},{6,2},{1,5},{3,7},{5,1},{7,3},{8,12},{10,14},{12... | collective-permute-start | bytes 245768 | tf_op jit(solution)/shard_map/ppermute | solution.py:143
  28.6 14.1 %collective-permute-start.6 = (bf16[32,1280]{1,0:T(8,128)(2,1)S(1)}, bf16[32,1280]{1,0:T(8,128)(2,1)S(1)}, u32[]{:S(2)}, u32[]{:S(2)}) collective-permute-start(bf16[32,1280]{1,0:T(8,128)(2,1)S(1)} %concatenate.66), channel_id=1, source_target_pairs={{0,6},{2,4},{4,2},{6,0},{1,7},{3,5},{5,3},{7,1},{8,14},{10,12},{12... | collective-permute-start | bytes 245768 | tf_op jit(solution)/shard_map/ppermute | solution.py:143
  30.3 18.3 %copy-start.5 = (bf16[128,384]{1,0:T(8,128)(2,1)S(1)}, bf16[128,384]{1,0:T(8,128)(2,1)}, u32[]{:S(2)}) copy-start(bf16[128,384]{1,0:T(8,128)(2,1)} %get-tuple-element.37) | copy-start | bytes 294916
  30.3 23.9 %copy-start.10 = (pred[1,64]{1,0:T(4,128)(4,1)S(1)}, pred[1,64]{1,0:T(4,128)(4,1)}, u32[]{:S(2)}) copy-start(pred[1,64]{1,0:T(4,128)(4,1)} %broadcast_compare_fusion) | copy-start | bytes 196
  31.6 18.6 %collective-permute-start.9 = (bf16[128,768]{1,0:T(8,128)(2,1)}, bf16[128,768]{1,0:T(8,128)(2,1)S(1)}, u32[]{:S(2)}, u32[]{:S(2)}) collective-permute-start(bf16[128,768]{1,0:T(8,128)(2,1)} %pad_maximum_fusion.4), channel_id=1, source_target_pairs={{0,6},{2,4},{4,2},{6,0},{1,7},{3,5},{5,3},{7,1},{8,14},{10,12},{12... | collective-permute-start | bytes 589832 | tf_op jit(solution)/shard_map/ppermute | solution.py:143
  37.5 8.0 %collective-permute-start = (bf16[128,384]{1,0:T(8,128)(2,1)}, bf16[128,384]{1,0:T(8,128)(2,1)S(1)}, u32[]{:S(2)}, u32[]{:S(2)}) collective-permute-start(bf16[128,384]{1,0:T(8,128)(2,1)} %get-tuple-element.38), channel_id=1, source_target_pairs={{0,2},{2,0},{4,6},{6,4},{1,3},{3,1},{5,7},{7,5},{8,10},{10,8},{12,... | collective-permute-start | bytes 294920 | tf_op jit(solution)/shard_map/ppermute | solution.py:143
  42.7 5.8 %collective-permute-start.1 = (bf16[128,384]{1,0:T(8,128)(2,1)}, bf16[128,384]{1,0:T(8,128)(2,1)S(1)}, u32[]{:S(2)}, u32[]{:S(2)}) collective-permute-start(bf16[128,384]{1,0:T(8,128)(2,1)} %get-tuple-element.40), channel_id=1, source_target_pairs={{0,4},{2,6},{4,0},{6,2},{1,5},{3,7},{5,1},{7,3},{8,12},{10,14},{12... | collective-permute-start | bytes 294920 | tf_op jit(solution)/shard_map/ppermute | solution.py:143
  45.4 8.9 %collective-permute-start.10 = (bf16[128,768]{1,0:T(8,128)(2,1)S(1)}, bf16[128,768]{1,0:T(8,128)(2,1)S(1)}, u32[]{:S(2)}, u32[]{:S(2)}) collective-permute-start(bf16[128,768]{1,0:T(8,128)(2,1)S(1)} %pad_maximum_fusion.1.refs_5_), channel_id=1, source_target_pairs={{0,1},{2,3},{4,5},{6,7},{1,0},{3,2},{5,4},{7,6},{8,9},{10,11},{12,... | collective-permute-start | bytes 589832 | tf_op jit(solution)/shard_map/ppermute | solution.py:147
  48.5 5.7 %collective-permute-start.2 = (bf16[128,384]{1,0:T(8,128)(2,1)S(1)}, bf16[128,384]{1,0:T(8,128)(2,1)S(1)}, u32[]{:S(2)}, u32[]{:S(2)}) collective-permute-start(bf16[128,384]{1,0:T(8,128)(2,1)S(1)} %copy-done.5), channel_id=1, source_target_pairs={{0,6},{2,4},{4,2},{6,0},{1,7},{3,5},{5,3},{7,1},{8,14},{10,12},{12... | collective-permute-start | bytes 294920 | tf_op jit(solution)/shard_map/ppermute | solution.py:143
  49.6 4.7 %collective-permute-start.11 = (bf16[128,768]{1,0:T(8,128)(2,1)S(1)}, bf16[128,768]{1,0:T(8,128)(2,1)S(1)}, u32[]{:S(2)}, u32[]{:S(2)}) collective-permute-start(bf16[128,768]{1,0:T(8,128)(2,1)S(1)} %collective-permute-done.7.refs_6_), channel_id=1, source_target_pairs={{0,1},{2,3},{4,5},{6,7},{1,0},{3,2},{5,4},{7,6},{8,9},{10,11},{12,... | collective-permute-start | bytes 589832 | tf_op jit(solution)/shard_map/ppermute | solution.py:147
  49.6 4.7 %collective-permute-start.12 = (bf16[128,768]{1,0:T(8,128)(2,1)S(1)}, bf16[128,768]{1,0:T(8,128)(2,1)S(1)}, u32[]{:S(2)}, u32[]{:S(2)}) collective-permute-start(bf16[128,768]{1,0:T(8,128)(2,1)S(1)} %collective-permute-done.8.refs_7_), channel_id=1, source_target_pairs={{0,1},{2,3},{4,5},{6,7},{1,0},{3,2},{5,4},{7,6},{8,9},{10,11},{12,... | collective-permute-start | bytes 589832 | tf_op jit(solution)/shard_map/ppermute | solution.py:147
  50.1 4.2 %collective-permute-start.13 = (bf16[128,768]{1,0:T(8,128)(2,1)S(1)}, bf16[128,768]{1,0:T(8,128)(2,1)S(1)}, u32[]{:S(2)}, u32[]{:S(2)}) collective-permute-start(bf16[128,768]{1,0:T(8,128)(2,1)S(1)} %collective-permute-done.9.refs_8_), channel_id=1, source_target_pairs={{0,1},{2,3},{4,5},{6,7},{1,0},{3,2},{5,4},{7,6},{8,9},{10,11},{12,... | collective-permute-start | bytes 589832 | tf_op jit(solution)/shard_map/ppermute | solution.py:147
  54.2 1.2 collective-permute-start.14
  61.3 12.8 %collective-permute-start.17 = (bf16[136,384]{1,0:T(8,128)(2,1)S(1)}, bf16[136,384]{1,0:T(8,128)(2,1)S(1)}, u32[]{:S(2)}, u32[]{:S(2)}) collective-permute-start(bf16[136,384]{1,0:T(8,128)(2,1)S(1)} %pad_maximum_fusion.7), channel_id=1, source_target_pairs={{0,6},{2,4},{4,2},{6,0},{1,7},{3,5},{5,3},{7,1},{8,14},{10,12},{12... | collective-permute-start | bytes 313352 | tf_op jit(solution)/shard_map/ppermute | solution.py:143
  61.5 12.6 %collective-permute-start.16 = (bf16[136,384]{1,0:T(8,128)(2,1)S(1)}, bf16[136,384]{1,0:T(8,128)(2,1)S(1)}, u32[]{:S(2)}, u32[]{:S(2)}) collective-permute-start(bf16[136,384]{1,0:T(8,128)(2,1)S(1)} %pad_maximum_fusion.6), channel_id=1, source_target_pairs={{0,4},{2,6},{4,0},{6,2},{1,5},{3,7},{5,1},{7,3},{8,12},{10,14},{12... | collective-permute-start | bytes 313352 | tf_op jit(solution)/shard_map/ppermute | solution.py:143
  67.5 6.5 %collective-permute-start.15 = (bf16[136,384]{1,0:T(8,128)(2,1)S(1)}, bf16[136,384]{1,0:T(8,128)(2,1)S(1)}, u32[]{:S(2)}, u32[]{:S(2)}) collective-permute-start(bf16[136,384]{1,0:T(8,128)(2,1)S(1)} %pad_maximum_fusion.5), channel_id=1, source_target_pairs={{0,2},{2,0},{4,6},{6,4},{1,3},{3,1},{5,7},{7,5},{8,10},{10,8},{12,... | collective-permute-start | bytes 313352 | tf_op jit(solution)/shard_map/ppermute | solution.py:143
  82.2 30.1 %collective-permute-start.22 = (bf16[128,1536]{1,0:T(8,128)(2,1)S(1)}, bf16[128,1536]{1,0:T(8,128)(2,1)S(1)}, u32[]{:S(2)}, u32[]{:S(2)}) collective-permute-start(bf16[128,1536]{1,0:T(8,128)(2,1)S(1)} %slice.102.refs_1_), channel_id=1, source_target_pairs={{0,8},{8,0},{16,24},{24,16},{1,9},{9,1},{17,25},{25,17},{2,10},{10... | collective-permute-start | bytes 1179656 | tf_op jit(solution)/shard_map/ppermute | solution.py:150
  83.8 31.8 %collective-permute-start.23 = (bf16[128,1536]{1,0:T(8,128)(2,1)S(1)}, bf16[128,1536]{1,0:T(8,128)(2,1)S(1)}, u32[]{:S(2)}, u32[]{:S(2)}) collective-permute-start(bf16[128,1536]{1,0:T(8,128)(2,1)S(1)} %slice.102.refs_1_), channel_id=1, source_target_pairs={{0,16},{8,24},{16,0},{24,8},{1,17},{9,25},{17,1},{25,9},{2,18},{10... | collective-permute-start | bytes 1179656 | tf_op jit(solution)/shard_map/ppermute | solution.py:150
  85.3 30.4 %collective-permute-start.24 = (bf16[128,1536]{1,0:T(8,128)(2,1)S(1)}, bf16[128,1536]{1,0:T(8,128)(2,1)S(1)}, u32[]{:S(2)}, u32[]{:S(2)}) collective-permute-start(bf16[128,1536]{1,0:T(8,128)(2,1)S(1)} %slice.102.refs_1_), channel_id=1, source_target_pairs={{0,24},{8,16},{16,8},{24,0},{1,25},{9,17},{17,9},{25,1},{2,26},{10... | collective-permute-start | bytes 1179656 | tf_op jit(solution)/shard_map/ppermute | solution.py:150
  85.8 4.3 %collective-permute-start.32 = (f32[4,1,384]{2,1,0:T(1,128)S(1)}, f32[4,1,384]{2,1,0:T(1,128)S(1)}, u32[]{:S(2)}, u32[]{:S(2)}) collective-permute-start(f32[4,1,384]{2,1,0:T(1,128)S(1)} %fusion.34), channel_id=1, source_target_pairs={{0,1},{2,3},{4,5},{6,7},{1,0},{3,2},{5,4},{7,6},{8,9},{10,11},{12,... | collective-permute-start | bytes 18440 | tf_op jit(solution)/shard_map/ppermute | solution.py:147
  87.5 18.8 %collective-permute-start.20 = (bf16[2,384,128]{2,1,0:T(8,128)(2,1)S(1)}, bf16[2,384,128]{2,1,0:T(8,128)(2,1)S(1)}, u32[]{:S(2)}, u32[]{:S(2)}) collective-permute-start(bf16[2,384,128]{2,1,0:T(8,128)(2,1)S(1)} %get-tuple-element.23), channel_id=1, source_target_pairs={{0,24},{8,16},{16,8},{24,0},{1,25},{9,17},{17,9},{25,1},{2,26},{10... | collective-permute-start | bytes 589832 | tf_op jit(solution)/shard_map/ppermute | solution.py:150
  90.1 20.6 %collective-permute-start.19 = (bf16[2,384,128]{2,1,0:T(8,128)(2,1)S(1)}, bf16[2,384,128]{2,1,0:T(8,128)(2,1)S(1)}, u32[]{:S(2)}, u32[]{:S(2)}) collective-permute-start(bf16[2,384,128]{2,1,0:T(8,128)(2,1)S(1)} %get-tuple-element.24), channel_id=1, source_target_pairs={{0,16},{8,24},{16,0},{24,8},{1,17},{9,25},{17,1},{25,9},{2,18},{10... | collective-permute-start | bytes 589832 | tf_op jit(solution)/shard_map/ppermute | solution.py:150
  106.3 5.7 %collective-permute-start.18 = (bf16[2,384,128]{2,1,0:T(8,128)(2,1)S(1)}, bf16[2,384,128]{2,1,0:T(8,128)(2,1)S(1)}, u32[]{:S(2)}, u32[]{:S(2)}) collective-permute-start(bf16[2,384,128]{2,1,0:T(8,128)(2,1)S(1)} %get-tuple-element.25), channel_id=1, source_target_pairs={{0,8},{8,0},{16,24},{24,16},{1,9},{9,1},{17,25},{25,17},{2,10},{10... | collective-permute-start | bytes 589832 | tf_op jit(solution)/shard_map/ppermute | solution.py:150
  110.7 5.7 %collective-permute-start.25 = (bf16[128,1536]{1,0:T(8,128)(2,1)S(1)}, bf16[128,1536]{1,0:T(8,128)(2,1)S(1)}, u32[]{:S(2)}, u32[]{:S(2)}) collective-permute-start(bf16[128,1536]{1,0:T(8,128)(2,1)S(1)} %slice.102.refs_1_), channel_id=1, source_target_pairs={{0,1},{2,3},{4,5},{6,7},{1,0},{3,2},{5,4},{7,6},{8,9},{10,11},{12,... | collective-permute-start | bytes 1179656 | tf_op jit(solution)/shard_map/ppermute | solution.py:147
  112.1 4.0 %collective-permute-start.21 = (bf16[4,384,128]{2,1,0:T(8,128)(2,1)S(1)}, bf16[4,384,128]{2,1,0:T(8,128)(2,1)S(1)}, u32[]{:S(2)}, u32[]{:S(2)}) collective-permute-start(bf16[4,384,128]{2,1,0:T(8,128)(2,1)S(1)} %pad_maximum_fusion), channel_id=1, source_target_pairs={{0,1},{2,3},{4,5},{6,7},{1,0},{3,2},{5,4},{7,6},{8,9},{10,11},{12,... | collective-permute-start | bytes 1179656 | tf_op jit(solution)/shard_map/ppermute | solution.py:147
  112.3 10.2 %collective-permute-start.33 = (f32[1,384]{1,0:T(1,128)S(1)}, f32[1,384]{1,0:T(1,128)S(1)}, u32[]{:S(2)}, u32[]{:S(2)}) collective-permute-start(f32[1,384]{1,0:T(1,128)S(1)} %get-tuple-element.49), channel_id=1, source_target_pairs={{0,2},{2,0},{4,6},{6,4},{1,3},{3,1},{5,7},{7,5},{8,10},{10,8},{12,... | collective-permute-start | bytes 4616 | tf_op jit(solution)/shard_map/ppermute | solution.py:143
  115.5 1.9 %collective-permute-start.26 = (bf16[128,1536]{1,0:T(8,128)(2,1)S(1)}, bf16[128,1536]{1,0:T(8,128)(2,1)S(1)}, u32[]{:S(2)}, u32[]{:S(2)}) collective-permute-start(bf16[128,1536]{1,0:T(8,128)(2,1)S(1)} %collective-permute-done.22.refs_2_), channel_id=1, source_target_pairs={{0,1},{2,3},{4,5},{6,7},{1,0},{3,2},{5,4},{7,6},{8,9},{10,11},{12,... | collective-permute-start | bytes 1179656 | tf_op jit(solution)/shard_map/ppermute | solution.py:147
  115.7 3.1 %collective-permute-start.27 = (bf16[128,1536]{1,0:T(8,128)(2,1)S(1)}, bf16[128,1536]{1,0:T(8,128)(2,1)S(1)}, u32[]{:S(2)}, u32[]{:S(2)}) collective-permute-start(bf16[128,1536]{1,0:T(8,128)(2,1)S(1)} %collective-permute-done.23.refs_3_), channel_id=1, source_target_pairs={{0,1},{2,3},{4,5},{6,7},{1,0},{3,2},{5,4},{7,6},{8,9},{10,11},{12,... | collective-permute-start | bytes 1179656 | tf_op jit(solution)/shard_map/ppermute | solution.py:147
  116.0 2.8 %collective-permute-start.28 = (bf16[128,1536]{1,0:T(8,128)(2,1)S(1)}, bf16[128,1536]{1,0:T(8,128)(2,1)S(1)}, u32[]{:S(2)}, u32[]{:S(2)}) collective-permute-start(bf16[128,1536]{1,0:T(8,128)(2,1)S(1)} %collective-permute-done.24.refs_4_), channel_id=1, source_target_pairs={{0,1},{2,3},{4,5},{6,7},{1,0},{3,2},{5,4},{7,6},{8,9},{10,11},{12,... | collective-permute-start | bytes 1179656 | tf_op jit(solution)/shard_map/ppermute | solution.py:147
  116.4 8.2 %collective-permute-start.34 = (f32[1,384]{1,0:T(1,128)S(1)}, f32[1,384]{1,0:T(1,128)S(1)}, u32[]{:S(2)}, u32[]{:S(2)}) collective-permute-start(f32[1,384]{1,0:T(1,128)S(1)} %get-tuple-element.51), channel_id=1, source_target_pairs={{0,4},{2,6},{4,0},{6,2},{1,5},{3,7},{5,1},{7,3},{8,12},{10,14},{12... | collective-permute-start | bytes 4616 | tf_op jit(solution)/shard_map/ppermute | solution.py:143
  117.5 7.2 %collective-permute-start.35 = (f32[1,384]{1,0:T(1,128)S(1)}, f32[1,384]{1,0:T(1,128)S(1)}, u32[]{:S(2)}, u32[]{:S(2)}) collective-permute-start(f32[1,384]{1,0:T(1,128)S(1)} %get-tuple-element.50), channel_id=1, source_target_pairs={{0,6},{2,4},{4,2},{6,0},{1,7},{3,5},{5,3},{7,1},{8,14},{10,12},{12... | collective-permute-start | bytes 4616 | tf_op jit(solution)/shard_map/ppermute | solution.py:143
  120.3 13.4 %collective-permute-start.29 = (bf16[96,1536]{1,0:T(8,128)(2,1)S(1)}, bf16[96,1536]{1,0:T(8,128)(2,1)S(1)}, u32[]{:S(2)}, u32[]{:S(2)}) collective-permute-start(bf16[96,1536]{1,0:T(8,128)(2,1)S(1)} %get-tuple-element.19), channel_id=1, source_target_pairs={{0,2},{2,0},{4,6},{6,4},{1,3},{3,1},{5,7},{7,5},{8,10},{10,8},{12,... | collective-permute-start | bytes 884744 | tf_op jit(solution)/shard_map/ppermute | solution.py:143
  122.4 20.2 %collective-permute-start.30 = (bf16[96,1536]{1,0:T(8,128)(2,1)S(1)}, bf16[96,1536]{1,0:T(8,128)(2,1)S(1)}, u32[]{:S(2)}, u32[]{:S(2)}) collective-permute-start(bf16[96,1536]{1,0:T(8,128)(2,1)S(1)} %get-tuple-element.21), channel_id=1, source_target_pairs={{0,4},{2,6},{4,0},{6,2},{1,5},{3,7},{5,1},{7,3},{8,12},{10,14},{12... | collective-permute-start | bytes 884744 | tf_op jit(solution)/shard_map/ppermute | solution.py:143
  122.5 27.0 %collective-permute-start.31 = (bf16[96,1536]{1,0:T(8,128)(2,1)S(1)}, bf16[96,1536]{1,0:T(8,128)(2,1)S(1)}, u32[]{:S(2)}, u32[]{:S(2)}) collective-permute-start(bf16[96,1536]{1,0:T(8,128)(2,1)S(1)} %get-tuple-element.20), channel_id=1, source_target_pairs={{0,6},{2,4},{4,2},{6,0},{1,7},{3,5},{5,3},{7,1},{8,14},{10,12},{12... | collective-permute-start | bytes 884744 | tf_op jit(solution)/shard_map/ppermute | solution.py:143

commit v2 on v1

v2 whole, which is shorter than its diff:
```python
import math
import functools
import jax
import jax.numpy as jnp
from jax import lax
from jax.experimental import pallas as pl
from jax.experimental.pallas import tpu as pltpu
from jax.sharding import PartitionSpec as P

DT5 = 4096
CORES = 2
GROUPS = 4

eps_norm = 1e-06
f32 = jnp.float32
bf16 = jnp.bfloat16


def head_norm(values_in, gain_vec):
    shaped = values_in.reshape(values_in.shape[0], -1, gain_vec.shape[0])
    normed = (
        shaped * lax.rsqrt(jnp.mean(shaped * shaped, axis=-1, keepdims=True) + eps_norm) * gain_vec
    )
    return normed.reshape(values_in.shape).astype(bf16)


def attention_kernel(n_kv, n_tkv, row_block, head_size, *refs):
    qkv_ref, tq_ref = refs[:2]
    kv_refs = refs[2 : 2 + n_kv]
    tkv_refs = refs[2 + n_kv : 2 + n_kv + n_tkv]
    bias_ref, out_ref, tout_ref = refs[2 + n_kv + n_tkv :]
    width = tq_ref.shape[1]
    factor = head_size ** (-0.5) * math.log2(math.e)
    bias = bias_ref[...]
    blocks = [
        (qkv_ref, 2 * width, out_ref, slice(r, r + row_block))
        for r in range(0, out_ref.shape[0], row_block)
    ]
    blocks.append((tq_ref, 0, tout_ref, slice(0, tout_ref.shape[0])))
    for head in range(width // head_size):
        cols = slice(head * head_size, (head + 1) * head_size)
        vcols = slice(width + head * head_size, width + (head + 1) * head_size)
        keys = jnp.concatenate([r[:, cols] for r in kv_refs], axis=0)
        values = jnp.concatenate([r[:, vcols] for r in kv_refs], axis=0)
        tkeys = jnp.concatenate([r[:, cols] for r in tkv_refs], axis=0)
        tvalues = jnp.concatenate([r[:, vcols] for r in tkv_refs], axis=0)
        for q_ref, q_at, o_ref, rows in blocks:
            q = q_ref[rows, q_at + head * head_size : q_at + (head + 1) * head_size]
            nt = (((1,), (1,)), ((), ()))
            s_img = lax.dot_general(q, keys, nt, preferred_element_type=f32)
            s_txt = lax.dot_general(q, tkeys, nt, preferred_element_type=f32) + bias
            top = jnp.maximum(
                jnp.max(s_img, axis=1, keepdims=True), jnp.max(s_txt, axis=1, keepdims=True)
            )
            p_img = jnp.exp2((s_img - top) * factor)
            p_txt = jnp.exp2((s_txt - top) * factor)
            total = jnp.sum(p_img, axis=1, keepdims=True) + jnp.sum(p_txt, axis=1, keepdims=True)
            acc = jnp.dot(p_img.astype(bf16), values, preferred_element_type=f32)
            acc = acc + jnp.dot(p_txt.astype(bf16), tvalues, preferred_element_type=f32)
            o_ref[rows, cols] = (acc / total).astype(bf16)


def attention(qkv, text_q, keyvals, text_keyvals, bias, head_size):
    args = (qkv, text_q) + tuple(keyvals) + tuple(text_keyvals) + (bias,)
    width = text_q.shape[1]
    outs = [jax.ShapeDtypeStruct((x.shape[0], width), bf16) for x in (qkv, text_q)]
    vmem = pl.BlockSpec(memory_space=pltpu.VMEM)
    rows = qkv.shape[0] + text_q.shape[0]
    cols = sum(k.shape[0] for k in keyvals) + sum(k.shape[0] for k in text_keyvals)
    return pl.pallas_call(
        functools.partial(attention_kernel, len(keyvals), len(text_keyvals), 128, head_size),
        out_shape=outs,
        in_specs=[vmem] * len(args),
        out_specs=[vmem] * len(outs),
        compiler_params=pltpu.CompilerParams(vmem_limit_bytes=32 * 1024 * 1024),
        cost_estimate=pl.CostEstimate(
            flops=4 * rows * cols * width,
            bytes_accessed=4 * (rows + cols) * width,
            transcendentals=rows * cols * width // head_size,
        ),
    )(*args)


def grad_kernel(n_pieces, *refs):
    left = refs[0]
    pieces = refs[1 : 1 + n_pieces]
    out = refs[1 + n_pieces]
    block = 256
    for start in range(0, out.shape[1], block):
        cols = slice(start, start + block)
        right = jnp.concatenate([p[:, cols] for p in pieces], axis=0)
        out[:, cols] = jnp.dot(left[...], right, preferred_element_type=f32).astype(bf16)


def grad_product(left, pieces):
    vmem = pl.BlockSpec(memory_space=pltpu.VMEM)
    rows, depth = left.shape
    width = pieces[0].shape[1]
    return pl.pallas_call(
        functools.partial(grad_kernel, len(pieces)),
        out_shape=jax.ShapeDtypeStruct((rows, width), bf16),
        in_specs=[vmem] * (1 + len(pieces)),
        out_specs=vmem,
        compiler_params=pltpu.CompilerParams(vmem_limit_bytes=32 * 1024 * 1024),
        cost_estimate=pl.CostEstimate(
            flops=2 * rows * depth * width,
            bytes_accessed=2 * (rows * depth + depth * width + rows * width),
            transcendentals=0,
        ),
    )(left, *pieces)


def on_device(
    caption_states,
    caption_gain,
    text_proj,
    caption_len,
    slot_source,
    query_gain,
    key_gain,
    image_q,
    image_k,
    image_v,
    out_weight,
    gate,
    d_out,
):
    n_dp = lax.axis_size("dp")
    n_seq = lax.axis_size("seq")
    G, C = GROUPS, CORES
    O = n_seq // (G * C)
    OC = O * C
    seq = lax.axis_index("seq")
    oc = (seq // (G * C)) * C + seq % C

    def place(oc_at, z_at):
        return ((oc_at // C) * G + z_at) * C + oc_at % C

    def to_oc(x, j):
        perm = [(place(a, b), place(a ^ j, b)) for a in range(OC) for b in range(G)]
        return lax.ppermute(x, "seq", perm)

    def part(x, index, size, axis):
        return lax.dynamic_slice_in_dim(x, index * size, size, axis)

    z_groups = [[place(a, b) for b in range(G)] for a in range(OC)]

    def swap_z(x):
        return lax.all_to_all(x, "seq", 0, 0, axis_index_groups=z_groups, tiled=True)

    slot_total = slot_source.shape[1]
    slot_local = slot_total // n_seq
    image_local = image_q.shape[1]
    inner_width = image_q.shape[2]
    model_width = out_weight.shape[0]
    head_size = query_gain.shape[0]
    gw = inner_width // G
    q_all, k_all, v_all = image_q[0], image_k[0], image_v[0]

    qkv = jnp.concatenate(
        [
            jnp.concatenate([x[:, b * gw : (b + 1) * gw] for x in (k_all, v_all, q_all)], axis=1)
            for b in range(G)
        ],
        axis=0,
    )
    qkv = swap_z(qkv)
    kv_near = qkv[:, : 2 * gw]
    kv_pieces = [qkv] + [to_oc(kv_near, j) for j in range(1, OC)]

    sources = slot_source[0].reshape(O, G, C, slot_local)
    sources = jnp.transpose(sources, (0, 2, 1, 3)).reshape(-1)
    picked = jnp.take(caption_states[0], sources, axis=0).astype(f32)
    scaled_rows = (picked * caption_gain).astype(bf16)
    partial_proj = jnp.dot(scaled_rows, text_proj, preferred_element_type=f32)
    partial_squares = jnp.sum(picked * picked, axis=1, keepdims=True)
    usable = (sources < caption_len[0]).astype(jnp.int32).reshape(OC, G * slot_local)
    text_rows = G * slot_local

    def message(values, squares):
        high = lax.reduce_precision(squares, 8, 7)
        low = squares - high
        tail = jnp.concatenate(
            [high, low, jnp.zeros((squares.shape[0], 126), f32)], axis=1
        ).astype(bf16)
        return jnp.concatenate([values.astype(bf16), tail], axis=1)

    def opened(got):
        got = got.astype(f32)
        width = got.shape[-1] - 128
        return got[..., :width], got[..., width : width + 1] + got[..., width + 1 : width + 2]

    chip_proj = part(partial_proj, oc, text_rows, 0)
    chip_squares = part(partial_squares, oc, text_rows, 0)
    for j in range(1, OC):
        sent = message(
            part(partial_proj, oc ^ j, text_rows, 0), part(partial_squares, oc ^ j, text_rows, 0)
        )
        more_proj, more_squares = opened(to_oc(sent, j))
        chip_proj = chip_proj + more_proj
        chip_squares = chip_squares + more_squares
    sent = jnp.concatenate(
        [
            message(
                jnp.concatenate(
                    [
                        chip_proj[:, i * inner_width + b * gw : i * inner_width + (b + 1) * gw]
                        for i in range(3)
                    ],
                    axis=1,
                ),
                chip_squares,
            )
            for b in range(G)
        ],
        axis=0,
    )
    got, got_squares = opened(swap_z(sent).reshape(G, text_rows, -1))
    summed = jnp.sum(got, axis=0)
    squares = jnp.sum(got_squares, axis=0)
    normed = summed * lax.rsqrt(squares / DT5 + eps_norm)
    text_q = head_norm(normed[:, :gw], query_gain)
    text_k = head_norm(normed[:, gw : 2 * gw], key_gain)
    text_kv = jnp.concatenate([text_k, normed[:, 2 * gw :].astype(bf16)], axis=1)
    text_kvs = [text_kv] + [to_oc(text_kv, j) for j in range(1, OC)]
    usable_keys = jnp.concatenate([part(usable, oc ^ j, 1, 0) for j in range(OC)], axis=1)
    bias = jnp.where(usable_keys > 0, 0.0, -1e30).astype(f32)

    gate_row = gate[0]
    cotangent = d_out[0].astype(f32)
    gated_grad = (gate_row * cotangent).astype(bf16)
    R = model_width // (n_dp * n_seq)
    gg_t = gated_grad.T.reshape(n_dp, O, G, C, R, image_local)
    gg_t = jnp.transpose(gg_t, (0, 1, 3, 2, 4, 5)).reshape(n_dp, OC, G * R, image_local)
    gg_dp = lax.all_to_all(gg_t, "dp", 0, 0, tiled=True)
    gg_left = []
    for j in range(OC):
        sel = lax.dynamic_index_in_dim(gg_dp, oc ^ j, 1, keepdims=False)
        if j:
            sel = to_oc(sel, j)
        gg_left += [sel[k] for k in range(n_dp)]
    left = jnp.concatenate(gg_left, axis=1)
    d_attn = jnp.dot(gated_grad, out_weight, preferred_element_type=f32).astype(bf16)

    out, text_out = attention(qkv, text_q, kv_pieces, text_kvs, bias, head_size)

    rows = jnp.concatenate(
        [out.reshape(G, image_local, gw), text_out.reshape(G, slot_local, gw)], axis=1
    )
    back = swap_z(rows.reshape(-1, gw)).reshape(G, image_local + slot_local, gw)
    attn = jnp.concatenate([back[b] for b in range(G)], axis=1)
    image_attn = attn[:image_local]
    own_usable = part((slot_source[0] < caption_len[0]), seq, slot_local, 0)
    text_attn = jnp.where(own_usable[:, None], attn[image_local:], jnp.zeros((), bf16))

    attn_dp = lax.all_gather(image_attn, "dp", axis=0, tiled=True)
    attn_pieces = [attn_dp] + [to_oc(attn_dp, j) for j in range(1, OC)]

    projected = lax.dot_general(
        image_attn, out_weight, (((1,), (1,)), ((), ())), preferred_element_type=f32
    )
    image_out = (gate_row * projected).astype(bf16)
    gate_term = jnp.sum(projected * cotangent, axis=0)

    grad = swap_z(grad_product(left, attn_pieces)).reshape(G, R, inner_width)
    grad_wo = jnp.sum(grad.astype(f32), axis=0)

    gate_term = jnp.transpose(gate_term.reshape(O, G, C, -1), (0, 2, 1, 3)).reshape(OC, G, 1, -1)
    gate_chip = lax.dynamic_index_in_dim(gate_term, oc, 0, keepdims=False)
    for j in range(1, OC):
        gate_chip = gate_chip + to_oc(
            lax.dynamic_index_in_dim(gate_term, oc ^ j, 0, keepdims=False), j
        )
    grad_gate = jnp.sum(swap_z(gate_chip), axis=0)
    return (image_out[None], text_attn[None], d_attn[None], grad_wo, grad_gate)


def solution(mesh):
    in_specs = (
        P("dp", None, "seq"),
        P("seq"),
        P("seq", None),
        P("dp"),
        P("dp", None),
        P(),
        P(),
        P("dp", "seq", None),
        P("dp", "seq", None),
        P("dp", "seq", None),
        P(),
        P("dp", None),
        P("dp", "seq", None),
    )
    out_specs = (
        P("dp", "seq", None),
        P("dp", "seq", None),
        P("dp", "seq", None),
        P(("dp", "seq"), None),
        P("dp", "seq"),
    )
    return jax.shard_map(
        on_device, mesh=mesh, in_specs=in_specs, out_specs=out_specs, check_vma=False
    )
```

time: 151 us -> 180 us (1.19)
  the two profiles are of different devices: /device:TPU:8 before, /device:TPU:0 now
where the time goes in v2:
time: 180 us; the launch traced here: 179 us
  waiting for transfers between devices  70.7 us (39%)
  starting transfers between devices  24.5 us (14%)
  matrix products  17 us (9%)
  other arithmetic  16.2 us (9%)
  blocking collectives  15.3 us (8%)
  between operations  15.2 us (8%)
  local copies, waits for them, and re-layouts  11.8 us (7%)
  Pallas kernels  8.14 us (5%)
    all_to_all x4, waiting for transfers between devices, swap_z(): lax.all_to_all(x, 'seq', 0, 0, axis_index_groups=z_groups, tiled=True)  49.7 us
    all_to_all x4, starting transfers between devices, swap_z(): lax.all_to_all(x, 'seq', 0, 0, axis_index_groups=z_groups, tiled=True)  18.8 us
    all_gather x1, waiting for transfers between devices, on_device(): attn_dp = lax.all_gather(image_attn, 'dp', axis=0, tiled=True)  18.5 us
    all_to_all x1, blocking collectives, swap_z(): lax.all_to_all(x, 'seq', 0, 0, axis_index_groups=z_groups, tiled=True)  15.3 us
    concatenate x1, other arithmetic, on_device(): jnp.concatenate([jnp.concatenate([x[:, b * gw:(b + 1) * gw] for x in (k_a...  9.77 us
    dot_general x1, matrix products, on_device(): lax.dot_general(image_attn, out_weight, (((1,), (1,)), ((), ())), preferr...  7.71 us
    dot_general x1, matrix products, on_device(): jnp.dot(gated_grad, out_weight, preferred_element_type=f32).astype(bf16)  5.86 us
    pallas_call x1, Pallas kernels, attention(): pl.pallas_call(functools.partial(attention_kernel, len(keyvals), len(text...  5.7 us
  transfers between devices with their start and end apart: 12, of which 6 were waited for; matrix products, arithmetic and copies ran while one was open for 19% of the time, Pallas kernels for 1%

profile of v2, /device:TPU:0, one launch (start us, length us, event | category | flops | bytes accessed | tf_op | source)
XLA Modules:
  0.0 178.8 jit_solution(15071810911373122143)
XLA Ops:
  7.2 0.5 broadcast.125
  7.7 1.3 reduce.5
  9.4 0.7 gather_fusion
  10.1 0.2 fusion.8
  10.3 0.1 copy.60
  10.4 0.1 copy.59
  10.6 3.4 %fusion.17 = f32[64,4608]{1,0:T(8,128)S(1)} fusion(bf16[512,4608]{1,0:T(8,128)(2,1)} %param.15, f32[512]{0:T(512)} %param.14, bf16[64,512]{1,0:T(8,128)(2,1)S(1)} %gather_fusion, pred[64]{0:T(512)(128)(4,1)S(1)} %compare_and_fusion), kind=kOutput, calls=%fused_computation.45 | convolution fusion | flops 302120960 | bytes 5965888 | tf_op jit(solution)/shard_map/dot_general | solution.py:175
  14.1 0.8 concatenate.81
  14.9 0.5 collective-permute-start
  15.6 1.2 collective-permute-done
  17.0 0.1 concatenate.82
  17.2 0.1 concatenate.84
  17.3 0.7 pad_maximum_fusion.2
  18.1 6.2 %all-to-all-start.1 = ((bf16[4,32,1280]{2,1,0:T(8,128)(2,1)}), bf16[4,32,1280]{2,1,0:T(8,128)(2,1)S(1)}, u32[]{:S(2)}, u32[]{:S(2)}) async-start(bf16[4,32,1280]{2,1,0:T(8,128)(2,1)} %bitcast.12), calls=%async_computation.1 | async-start | bytes 655360 | tf_op jit(solution)/shard_map/all_to_all | solution.py:149
  24.3 9.8 %maximum_maximum_fusion = bf16[512,1152]{1,0:T(8,128)(2,1)} fusion(bf16[128,384]{1,0:T(8,128)(2,1)S(1)} %get-tuple-element.27, bf16[128,384]{1,0:T(8,128)(2,1)S(1)} %get-tuple-element.53, bf16[128,384]{1,0:T(8,128)(2,1)S(1)} %get-tuple-element.19, bf16[128,384]{1,0:T(8,128)(2,1)S(1)} %get-tuple-element.28, bf16[128,384]{1,0:T(8,128)(2,1)S(1)} %get-tuple-element.52, ...), kind=kLoop, calls=%fused_computation.9 | loop fusion | flops 14155776 | bytes 2359296 | tf_op jit(solution)/shard_map/concatenate | solution.py:160
  34.1 0.8 all-to-all-done.1
  35.0 4.2 %all-to-all-start = ((bf16[4,128,1152]{2,1,0:T(8,128)(2,1)}), bf16[4,128,1152]{2,1,0:T(8,128)(2,1)S(1)}, u32[]{:S(2)}, u32[]{:S(2)}) async-start(bf16[4,128,1152]{2,1,0:T(8,128)(2,1)} %bitcast.4), calls=%async_computation | async-start | bytes 2359296 | tf_op jit(solution)/shard_map/all_to_all | solution.py:149
  40.0 0.2 fusion.19
  40.4 0.1 reduce_sum.78
  40.5 26.9 %all-to-all-done = bf16[4,128,1152]{2,1,0:T(8,128)(2,1)S(1)} async-done(((bf16[4,128,1152]{2,1,0:T(8,128)(2,1)}), bf16[4,128,1152]{2,1,0:T(8,128)(2,1)S(1)}, u32[]{:S(2)}, u32[]{:S(2)}) %all-to-all-start) | async-done | bytes 1179680 | tf_op jit(solution)/shard_map/all_to_all | solution.py:149
  67.7 0.1 reduce_sum.77
  67.9 0.1 mul.124
  68.0 0.6 collective-permute-start.2
  68.7 1.3 collective-permute-done.2.refs_5_
  69.9 5.7 %shard_map.164 = (bf16[512,384]{1,0:T(8,128)(2,1)S(1)}, bf16[32,384]{1,0:T(8,128)(2,1)S(1)}) custom-call(bf16[512,1152]{1,0:T(8,128)(2,1)S(1)} %bitcast.117, bf16[32,384]{1,0:T(8,128)(2,1)S(1)} %get-tuple-element.43.refs_1_, bf16[512,1152]{1,0:T(8,128)(2,1)S(1)} %bitcast.118, bf16[512,768]{1,0:T(8,128)(2,1)S(1)} %collective-permute-done.1.refs_3_, ...), custom_call_target="tpu_custom_call" | custom-call | flops 909115392 | bytes 2506752 | tf_op jit(solution)/shard_map/pallas_call | solution.py:70
  75.7 15.3 %all_to_all.45 = bf16[4,136,384]{2,1,0:T(8,128)(2,1)S(1)} all-to-all(bf16[4,136,384]{2,1,0:T(8,128)(2,1)S(1)} %pad_maximum_fusion), channel_id=1, replica_groups={{0,2,4,6},{1,3,5,7},{8,10,12,14},{9,11,13,15},{16,18,20,22},{17,19,21,2..., dimensions={0} | all-to-all | bytes 835584 | tf_op jit(solution)/shard_map/all_to_all | solution.py:149
  91.1 0.8 slice.269
  91.9 7.7 %fusion.2 = (f32[3072]{0:T(1024)S(1)}, bf16[1,128,3072]{2,1,0:T(8,128)(2,1)}, bf16[3072,128]{0,1:T(8,128)(2,1)S(1)}) fusion(bf16[1,128,3072]{2,1,0:T(8,128)(2,1)S(1)} %copy-done.2, f32[3072]{0:T(1024)S(1)} %bitcast.127, bf16[3072,1536]{1,0:T(8,128)(2,1)} %param.23, bf16[136,1536]{1,0:T(8,128)(2,1)S(1)} %pad_maximum_fusion.1), kind=kOutput, calls=%fused_computation.7 | convolution fusion | flops 1210708992 | bytes 12214272 | tf_op jit(solution)/shard_map/dot_general | solution.py:259
  99.7 0.4 copy.62
  100.0 1.0 copy.63
  101.0 4.2 %all-to-all-start.3 = ((bf16[4,2,384,128]{3,2,1,0:T(8,128)(2,1)}), bf16[4,2,384,128]{3,2,1,0:T(8,128)(2,1)}, u32[]{:S(2)}, u32[]{:S(2)}) async-start(bf16[4,2,384,128]{3,2,1,0:T(8,128)(2,1)} %bitcast.30), calls=%async_computation.3 | async-start | bytes 1572864 | tf_op jit(solution)/shard_map/all_to_all | solution.py:235
  105.2 0.6 dynamic-slice_bitcast_fusion.5
  105.8 18.5 %all-gather.2.cloned.1.call-done.refs_1_ = bf16[512,1536]{1,0:T(8,128)(2,1)} async-done(((bf16[128,1536]{1,0:T(8,128)(2,1)}), bf16[512,1536]{1,0:T(8,128)(2,1)}) %all-gather.2.cloned.1.call-update) | async-done | bytes 1572880 | tf_op jit(solution)/shard_map/all_gather | solution.py:256
  124.4 1.4 bitcast_add_fusion
  125.8 3.3 %all-to-all-start.5 = ((f32[4,1,384]{2,1,0:T(1,128)}), f32[4,1,384]{2,1,0:T(1,128)S(1)}, u32[]{:S(2)}, u32[]{:S(2)}) async-start(f32[4,1,384]{2,1,0:T(1,128)} %bitcast_add_fusion), calls=%async_computation.5 | async-start | bytes 12288 | tf_op jit(solution)/shard_map/all_to_all | solution.py:149
  129.1 1.0 dynamic-slice_bitcast_fusion
  130.2 0.4 collective-permute-start.3
  130.5 0.9 fusion.16
  131.4 0.9 fusion.15
  132.4 0.9 fusion.14
  133.3 0.9 fusion.13
  134.4 2.4 %shard_map.165 = bf16[384,1536]{1,0:T(8,128)(2,1)} custom-call(bf16[384,1024]{1,0:T(8,128)(2,1)S(1)} %fusion.9.refs_0_, bf16[512,1536]{1,0:T(8,128)(2,1)S(1)} %copy-done.1, bf16[512,1536]{1,0:T(8,128)(2,1)S(1)} %collective-permute-done.4.refs_2_), custom_call_target="tpu_custom_call" | custom-call | flops 1207959552 | bytes 5111808 | tf_op jit(solution)/shard_map/pallas_call | solution.py:99
  136.9 4.9 %all-to-all-start.4 = ((bf16[4,96,1536]{2,1,0:T(8,128)(2,1)}), bf16[4,96,1536]{2,1,0:T(8,128)(2,1)S(1)}, u32[]{:S(2)}, u32[]{:S(2)}) async-start(bf16[4,96,1536]{2,1,0:T(8,128)(2,1)} %bitcast.40), calls=%async_computation.4 | async-start | bytes 2359296 | tf_op jit(solution)/shard_map/all_to_all | solution.py:149
  141.9 5.9 %fusion = bf16[1,128,1536]{2,1,0:T(8,128)(2,1)} fusion(bf16[3072,1536]{1,0:T(8,128)(2,1)} %param.23, bf16[1,128,3072]{2,1,0:T(8,128)(2,1)S(1)} %copy-done.3, f32[3072]{0:T(1024)S(1)} %bitcast.128), kind=kOutput, calls=%fused_computation.3 | convolution fusion | flops 1209335808 | bytes 10629120 | tf_op jit(solution)/shard_map/dot_general | solution.py:243
  147.8 0.7 fusion.25
  148.5 0.6 reduce_sum.82
  149.0 22.0 %all-to-all-done.4 = bf16[4,96,1536]{2,1,0:T(8,128)(2,1)S(1)} async-done(((bf16[4,96,1536]{2,1,0:T(8,128)(2,1)}), bf16[4,96,1536]{2,1,0:T(8,128)(2,1)S(1)}, u32[]{:S(2)}, u32[]{:S(2)}) %all-to-all-start.4) | async-done | bytes 1179680 | tf_op jit(solution)/shard_map/all_to_all | solution.py:149
  171.0 1.0 convert_reduce_fusion
  (90 shorter events, 2.2 us)
Async XLA Ops:
  7.2 2.2 %copy-start = (bf16[1,64,512]{2,1,0:T(8,128)(2,1)S(1)}, bf16[1,64,512]{2,1,0:T(8,128)(2,1)}, u32[]{:S(2)}) copy-start(bf16[1,64,512]{2,1,0:T(8,128)(2,1)} %param.13) | copy-start | bytes 196612
  9.1 1.3 copy-start.10
  10.5 4.8 %copy-start.6 = (bf16[1,128,1536]{2,1,0:T(8,128)(2,1)S(1)}, bf16[1,128,1536]{2,1,0:T(8,128)(2,1)}, u32[]{:S(2)}) copy-start(bf16[1,128,1536]{2,1,0:T(8,128)(2,1)} %param.20) | copy-start | bytes 1179652
  10.5 4.9 %copy-start.7 = (bf16[1,128,1536]{2,1,0:T(8,128)(2,1)S(1)}, bf16[1,128,1536]{2,1,0:T(8,128)(2,1)}, u32[]{:S(2)}) copy-start(bf16[1,128,1536]{2,1,0:T(8,128)(2,1)} %param.21) | copy-start | bytes 1179652
  10.6 4.9 %copy-start.8 = (bf16[1,128,1536]{2,1,0:T(8,128)(2,1)S(1)}, bf16[1,128,1536]{2,1,0:T(8,128)(2,1)}, u32[]{:S(2)}) copy-start(bf16[1,128,1536]{2,1,0:T(8,128)(2,1)} %param.22) | copy-start | bytes 1179652
  14.9 1.9 %collective-permute-start = (bf16[32,4736]{1,0:T(8,128)(2,1)}, bf16[32,4736]{1,0:T(8,128)(2,1)S(1)}, u32[]{:S(2)}, u32[]{:S(2)}) collective-permute-start(bf16[32,4736]{1,0:T(8,128)(2,1)} %concatenate.81), channel_id=1, source_target_pairs={{0,1},{2,3},{4,5},{6,7},{1,0},{3,2},{5,4},{7,6},{8,9},{10,11},{12,... | collective-permute-start | bytes 909320 | tf_op jit(solution)/shard_map/ppermute | solution.py:141
  18.1 16.9 %all-to-all-start.1 = ((bf16[4,32,1280]{2,1,0:T(8,128)(2,1)}), bf16[4,32,1280]{2,1,0:T(8,128)(2,1)S(1)}, u32[]{:S(2)}, u32[]{:S(2)}) async-start(bf16[4,32,1280]{2,1,0:T(8,128)(2,1)} %bitcast.12), calls=%async_computation.1 | async-start | bytes 655360 | tf_op jit(solution)/shard_map/all_to_all | solution.py:149
  24.3 15.5 %copy-start.11 = (s32[1,4,2,8]{3,2,1,0:T(2,128)S(1)}, s32[1,4,2,8]{3,2,1,0:T(2,128)}, u32[]{:S(2)}) copy-start(s32[1,4,2,8]{3,2,1,0:T(2,128)} %copy-done.10) | copy-start | bytes 772
  24.3 15.6 %copy-start.12 = (f32[128]{0:T(128)S(1)}, f32[128]{0:T(128)}, u32[]{:S(2)}) copy-start(f32[128]{0:T(128)} %param.19) | copy-start | bytes 1540
  24.3 15.6 %copy-start.13 = (f32[128]{0:T(128)S(1)}, f32[128]{0:T(128)}, u32[]{:S(2)}) copy-start(f32[128]{0:T(128)} %param.18) | copy-start | bytes 1540
  35.0 32.5 %all-to-all-start = ((bf16[4,128,1152]{2,1,0:T(8,128)(2,1)}), bf16[4,128,1152]{2,1,0:T(8,128)(2,1)S(1)}, u32[]{:S(2)}, u32[]{:S(2)}) async-start(bf16[4,128,1152]{2,1,0:T(8,128)(2,1)} %bitcast.4), calls=%async_computation | async-start | bytes 2359296 | tf_op jit(solution)/shard_map/all_to_all | solution.py:149
  39.2 85.1 %all-gather.2.cloned.1.call-start = ((), (), s32[]{:S(2)}) async-start(), calls=%async_computation.6 | async-start | bytes 1966080 | tf_op jit(solution)/shard_map/all_gather | solution.py:256
  67.5 2.4 %collective-permute-start.1 = (bf16[512,768]{1,0:T(8,128)(2,1)S(1)}, bf16[512,768]{1,0:T(8,128)(2,1)S(1)}, u32[]{:S(2)}, u32[]{:S(2)}) collective-permute-start(bf16[512,768]{1,0:T(8,128)(2,1)S(1)} %slice.262), channel_id=1, source_target_pairs={{0,1},{2,3},{4,5},{6,7},{1,0},{3,2},{5,4},{7,6},{8,9},{10,11},{12,... | collective-permute-start | bytes 2359304 | tf_op jit(solution)/shard_map/ppermute | solution.py:141
  68.0 1.9 %collective-permute-start.2 = (bf16[32,768]{1,0:T(8,128)(2,1)S(1)}, bf16[32,768]{1,0:T(8,128)(2,1)S(1)}, u32[]{:S(2)}, u32[]{:S(2)}) collective-permute-start(bf16[32,768]{1,0:T(8,128)(2,1)S(1)} %pad_maximum_fusion.3.refs_4_), channel_id=1, source_target_pairs={{0,1},{2,3},{4,5},{6,7},{1,0},{3,2},{5,4},{7,6},{8,9},{10,11},{12,... | collective-permute-start | bytes 147464 | tf_op jit(solution)/shard_map/ppermute | solution.py:141
  75.7 16.3 %copy-start.2 = (bf16[1,128,3072]{2,1,0:T(8,128)(2,1)S(1)}, bf16[1,128,3072]{2,1,0:T(8,128)(2,1)}, u32[]{:S(2)}) copy-start(bf16[1,128,3072]{2,1,0:T(8,128)(2,1)} %param.25) | copy-start | bytes 2359300
  75.7 16.3 %copy-start.9 = (f32[1,3072]{1,0:T(1,128)S(1)}, f32[1,3072]{1,0:T(1,128)}, u32[]{:S(2)}) copy-start(f32[1,3072]{1,0:T(1,128)} %param.24) | copy-start | bytes 36868
  91.1 0.9 copy-start.4
  101.0 24.8 %all-to-all-start.3 = ((bf16[4,2,384,128]{3,2,1,0:T(8,128)(2,1)}), bf16[4,2,384,128]{3,2,1,0:T(8,128)(2,1)}, u32[]{:S(2)}, u32[]{:S(2)}) async-start(bf16[4,2,384,128]{3,2,1,0:T(8,128)(2,1)} %bitcast.30), calls=%async_computation.3 | async-start | bytes 1572864 | tf_op jit(solution)/shard_map/all_to_all | solution.py:235
  105.8 18.6 %collective-permute-start.5 = (f32[4,1,384]{2,1,0:T(1,128)}, f32[4,1,384]{2,1,0:T(1,128)}, u32[]{:S(2)}, u32[]{:S(2)}) collective-permute-start(f32[4,1,384]{2,1,0:T(1,128)} %dynamic-slice_bitcast_fusion.5), channel_id=1, source_target_pairs={{0,1},{2,3},{4,5},{6,7},{1,0},{3,2},{5,4},{7,6},{8,9},{10,11},{12,... | collective-permute-start | bytes 18440 | tf_op jit(solution)/shard_map/ppermute | solution.py:141
  124.3 10.1 %copy-start.1 = (bf16[512,1536]{1,0:T(8,128)(2,1)S(1)}, bf16[512,1536]{1,0:T(8,128)(2,1)}, u32[]{:S(2)}) copy-start(bf16[512,1536]{1,0:T(8,128)(2,1)} %all-gather.2.cloned.1.call-done.refs_1_) | copy-start | bytes 4718596
  124.3 10.1 %collective-permute-start.4 = (bf16[512,1536]{1,0:T(8,128)(2,1)}, bf16[512,1536]{1,0:T(8,128)(2,1)S(1)}, u32[]{:S(2)}, u32[]{:S(2)}) collective-permute-start(bf16[512,1536]{1,0:T(8,128)(2,1)} %all-gather.2.cloned.1.call-done.refs_1_), channel_id=1, source_target_pairs={{0,1},{2,3},{4,5},{6,7},{1,0},{3,2},{5,4},{7,6},{8,9},{10,11},{12,... | collective-permute-start | bytes 4718600 | tf_op jit(solution)/shard_map/ppermute | solution.py:141
  125.8 11.1 %all-to-all-start.5 = ((f32[4,1,384]{2,1,0:T(1,128)}), f32[4,1,384]{2,1,0:T(1,128)S(1)}, u32[]{:S(2)}, u32[]{:S(2)}) async-start(f32[4,1,384]{2,1,0:T(1,128)} %bitcast_add_fusion), calls=%async_computation.5 | async-start | bytes 12288 | tf_op jit(solution)/shard_map/all_to_all | solution.py:149
  130.2 4.1 %collective-permute-start.3 = (bf16[4,384,128]{2,1,0:T(8,128)(2,1)S(1)}, bf16[4,384,128]{2,1,0:T(8,128)(2,1)S(1)}, u32[]{:S(2)}, u32[]{:S(2)}) collective-permute-start(bf16[4,384,128]{2,1,0:T(8,128)(2,1)S(1)} %dynamic-slice_bitcast_fusion), channel_id=1, source_target_pairs={{0,1},{2,3},{4,5},{6,7},{1,0},{3,2},{5,4},{7,6},{8,9},{10,11},{12,... | collective-permute-start | bytes 1179656 | tf_op jit(solution)/shard_map/ppermute | solution.py:141
  136.8 5.0 %copy-start.14 = (s32[1,64]{1,0:T(1,128)S(1)}, s32[1,64]{1,0:T(1,128)}, u32[]{:S(2)}) copy-start(s32[1,64]{1,0:T(1,128)} %param.17) | copy-start | bytes 772
  136.8 5.0 %copy-start.3 = (bf16[1,128,3072]{2,1,0:T(8,128)(2,1)S(1)}, bf16[1,128,3072]{2,1,0:T(8,128)(2,1)}, u32[]{:S(2)}) copy-start(bf16[1,128,3072]{2,1,0:T(8,128)(2,1)} %param.25) | copy-start | bytes 2359300
  136.9 34.1 %all-to-all-start.4 = ((bf16[4,96,1536]{2,1,0:T(8,128)(2,1)}), bf16[4,96,1536]{2,1,0:T(8,128)(2,1)S(1)}, u32[]{:S(2)}, u32[]{:S(2)}) async-start(bf16[4,96,1536]{2,1,0:T(8,128)(2,1)} %bitcast.40), calls=%async_computation.4 | async-start | bytes 2359296 | tf_op jit(solution)/shard_map/all_to_all | solution.py:149
  141.9 5.9 %copy-start.5 = (bf16[136,384]{1,0:T(8,128)(2,1)S(1)}, bf16[136,384]{1,0:T(8,128)(2,1)}, u32[]{:S(2)}) copy-start(bf16[136,384]{1,0:T(8,128)(2,1)} %copy-done.4) | copy-start | bytes 313348
Sparse Core Ops, SparseCore 0:
  92.0 32.2 all-gather.1

commit v3 on v1

v3 whole, which is shorter than its diff:
```python
import math
import functools
import jax
import jax.numpy as jnp
from jax import lax
from jax.experimental import pallas as pl
from jax.experimental.pallas import tpu as pltpu
from jax.sharding import PartitionSpec as P

DT5 = 4096
CORES = 2
GROUPS = 4

eps_norm = 1e-06
f32 = jnp.float32
bf16 = jnp.bfloat16


VMEM = pl.BlockSpec(memory_space=pltpu.VMEM)
SMEM = pl.BlockSpec(memory_space=pltpu.SMEM)
ANY = pl.BlockSpec(memory_space=pl.ANY)
TAIL = 128


def params():
    return pltpu.CompilerParams(vmem_limit_bytes=40 * 1024 * 1024)


def cost(flops, bytes_accessed, transcendentals=0):
    return pl.CostEstimate(
        flops=flops, bytes_accessed=bytes_accessed, transcendentals=transcendentals
    )


def pack_kernel(at_ref, k_ref, v_ref, q_ref, *outs):
    for g, out in enumerate(outs):
        width = out.shape[1] // 3
        at = pl.multiple_of(at_ref[g], 128)
        for i, ref in enumerate((k_ref, v_ref, q_ref)):
            out[:, i * width : (i + 1) * width] = ref[:, pl.ds(at, width)]


def pack(at, keys, values, queries, groups):
    rows, width = keys.shape
    shape = jax.ShapeDtypeStruct((rows, 3 * width // groups), bf16)
    return pl.pallas_call(
        pack_kernel,
        out_shape=[shape] * groups,
        in_specs=[SMEM, VMEM, VMEM, VMEM],
        out_specs=[VMEM] * groups,
        compiler_params=params(),
        cost_estimate=cost(0, 12 * rows * width),
    )(at, keys, values, queries)


def split_tail(squares):
    high = squares.astype(bf16).astype(f32)
    low = squares - high
    lane = lax.broadcasted_iota(jnp.int32, (squares.shape[0], TAIL), 1)
    return jnp.where(lane == 0, high, jnp.where(lane == 1, low, 0.0))


def text_kernel(at_ref, states_ref, gain_ref, pick_ref, wq_ref, wk_ref, wv_ref, own_ref, *msgs):
    del at_ref
    picked = jnp.dot(pick_ref[...], states_ref[...], preferred_element_type=f32)
    scaled = (picked * gain_ref[...]).astype(bf16)
    tail = split_tail(jnp.sum(picked * picked, axis=1, keepdims=True))
    rows = own_ref.shape[1]
    width = wq_ref.shape[1]
    for i, w_ref in enumerate((wq_ref, wk_ref, wv_ref)):
        got = jnp.dot(scaled, w_ref[...], preferred_element_type=f32)
        cols = slice(i * width, (i + 1) * width)
        own_ref[0, :, cols] = got[:rows]
        for j, msg in enumerate(msgs):
            msg[0, :, cols] = got[(j + 1) * rows : (j + 2) * rows].astype(bf16)
    own_ref[0, :, 3 * width :] = tail[:rows]
    for j, msg in enumerate(msgs):
        msg[0, :, 3 * width :] = tail[(j + 1) * rows : (j + 2) * rows].astype(bf16)


def text_project(at, states, gain, pick, text_proj, groups, parts):
    slots, depth = states.shape
    rows = pick.shape[0] // parts
    width = text_proj.shape[1] // (3 * groups)
    full = 3 * width + TAIL

    def whole(*shape):
        return pl.BlockSpec(shape, lambda g, at_ref: (0,) * len(shape))

    def weights(i):
        return pl.BlockSpec((depth, width), lambda g, at_ref: (0, i * groups + at_ref[g]))

    block = pl.BlockSpec((1, rows, full), lambda g, at_ref: (g, 0, 0))
    shapes = [jax.ShapeDtypeStruct((groups, rows, full), f32)]
    shapes += [jax.ShapeDtypeStruct((groups, rows, full), bf16)] * (parts - 1)
    return pl.pallas_call(
        text_kernel,
        grid_spec=pltpu.PrefetchScalarGridSpec(
            num_scalar_prefetch=1,
            grid=(groups,),
            in_specs=[
                whole(slots, depth),
                whole(1, depth),
                whole(pick.shape[0], slots),
                weights(0),
                weights(1),
                weights(2),
            ],
            out_specs=[block] * parts,
        ),
        out_shape=shapes,
        compiler_params=params(),
        cost_estimate=cost(
            2 * pick.shape[0] * depth * text_proj.shape[1], 2 * depth * text_proj.shape[1]
        ),
    )(at, states, gain, pick, text_proj, text_proj, text_proj)


def text_sum_kernel(n_got, own_ref, *refs):
    got, outs = refs[:n_got], refs[n_got:]
    for g, out in enumerate(outs):
        total = own_ref[g]
        for ref in got:
            total = total + ref[g].astype(f32)
        width = total.shape[1] - TAIL
        tail = total[:, width:]
        out[:, :width] = total[:, :width].astype(out.dtype)
        out[:, width:] = split_tail(tail[:, 0:1] + tail[:, 1:2]).astype(out.dtype)


def text_sum(own, got):
    groups, rows, full = own.shape
    shapes = [jax.ShapeDtypeStruct((rows, full), f32)]
    shapes += [jax.ShapeDtypeStruct((rows, full), bf16)] * (groups - 1)
    return pl.pallas_call(
        functools.partial(text_sum_kernel, len(got)),
        out_shape=shapes,
        in_specs=[VMEM] * (1 + len(got)),
        out_specs=[VMEM] * groups,
        compiler_params=params(),
        cost_estimate=cost(0, 8 * groups * rows * full),
    )(own, *got)


def text_norm_kernel(features, head_size, gains_ref, own_ref, *refs):
    got, (tq_ref, tkv_ref) = refs[:-2], refs[-2:]
    total = own_ref[...]
    for ref in got:
        total = total + ref[...].astype(f32)
    width = tq_ref.shape[1]
    squares = total[:, 3 * width : 3 * width + 1] + total[:, 3 * width + 1 : 3 * width + 2]
    normed = total[:, : 3 * width] * lax.rsqrt(squares / features + eps_norm)
    for i, out in enumerate((tq_ref, tkv_ref)):
        for head in range(width // head_size):
            cols = slice(head * head_size, (head + 1) * head_size)
            x = normed[:, i * width + head * head_size : i * width + (head + 1) * head_size]
            mean = jnp.mean(x * x, axis=1, keepdims=True)
            out[:, cols] = (x * lax.rsqrt(mean + eps_norm) * gains_ref[i : i + 1, :]).astype(bf16)
    tkv_ref[:, width:] = normed[:, 2 * width :].astype(bf16)


def text_norm(gains, own, got, features):
    rows, full = own.shape
    width = (full - TAIL) // 3
    return pl.pallas_call(
        functools.partial(text_norm_kernel, features, gains.shape[1]),
        out_shape=[
            jax.ShapeDtypeStruct((rows, width), bf16),
            jax.ShapeDtypeStruct((rows, 2 * width), bf16),
        ],
        in_specs=[VMEM] * (2 + len(got)),
        out_specs=[VMEM] * 2,
        compiler_params=params(),
        cost_estimate=cost(0, 8 * rows * full),
    )(gains, own, *got)


def attention_kernel(counts, width, head_size, *refs):
    n_q, n_kv, n_tkv, n_after = counts
    q_refs, refs = refs[:n_q], refs[n_q:]
    kv_refs, refs = refs[:n_kv], refs[n_kv:]
    tkv_refs, refs = refs[:n_tkv], refs[n_tkv:]
    bias_ref, out_refs = refs[0], refs[1 + n_after :]
    factor = head_size ** (-0.5) * math.log2(math.e)
    bias = bias_ref[...]
    nt = (((1,), (1,)), ((), ()))
    for head in range(width // head_size):
        cols = slice(head * head_size, (head + 1) * head_size)
        vcols = slice(width + head * head_size, width + (head + 1) * head_size)
        keys = jnp.concatenate([r[:, cols] for r in kv_refs], axis=0)
        values = jnp.concatenate([r[:, vcols] for r in kv_refs], axis=0)
        tkeys = jnp.concatenate([r[:, cols] for r in tkv_refs], axis=0)
        tvalues = jnp.concatenate([r[:, vcols] for r in tkv_refs], axis=0)
        for q_ref, out_ref in zip(q_refs, out_refs):
            at = q_ref.shape[1] - width + head * head_size
            q = q_ref[:, at : at + head_size]
            s_img = lax.dot_general(q, keys, nt, preferred_element_type=f32)
            s_txt = lax.dot_general(q, tkeys, nt, preferred_element_type=f32) + bias
            top = jnp.maximum(
                jnp.max(s_img, axis=1, keepdims=True), jnp.max(s_txt, axis=1, keepdims=True)
            )
            p_img = jnp.exp2((s_img - top) * factor)
            p_txt = jnp.exp2((s_txt - top) * factor)
            total = jnp.sum(p_img, axis=1, keepdims=True) + jnp.sum(p_txt, axis=1, keepdims=True)
            acc = jnp.dot(p_img.astype(bf16), values, preferred_element_type=f32)
            acc = acc + jnp.dot(p_txt.astype(bf16), tvalues, preferred_element_type=f32)
            out_ref[:, cols] = (acc / total).astype(bf16)


def attention(queries, keyvals, text_keyvals, bias, after, width, head_size):
    args = tuple(queries) + tuple(keyvals) + tuple(text_keyvals) + (bias,)
    counts = (len(queries), len(keyvals), len(text_keyvals), len(after))
    rows = sum(q.shape[0] for q in queries)
    cols = sum(k.shape[0] for k in keyvals) + sum(k.shape[0] for k in text_keyvals)
    return pl.pallas_call(
        functools.partial(attention_kernel, counts, width, head_size),
        out_shape=[jax.ShapeDtypeStruct((q.shape[0], width), bf16) for q in queries],
        in_specs=[VMEM] * len(args) + [ANY] * len(after),
        out_specs=[VMEM] * len(queries),
        compiler_params=params(),
        cost_estimate=cost(
            4 * rows * cols * width,
            4 * (rows + cols) * width,
            rows * cols * width // head_size,
        ),
    )(*args, *after)


def project_kernel(attn_ref, w_ref, gate_ref, d_out_ref, after_ref, out_ref, term_ref):
    del after_ref
    got = lax.dot_general(
        attn_ref[...], w_ref[...], (((1,), (1,)), ((), ())), preferred_element_type=f32
    )
    out_ref[...] = (got * gate_ref[...]).astype(bf16)
    term_ref[...] = jnp.sum(got * d_out_ref[...].astype(f32), axis=0, keepdims=True)


def project(attn, out_weight, gate, d_out, after):
    rows, inner = attn.shape
    model = out_weight.shape[0]
    block = 512
    return pl.pallas_call(
        project_kernel,
        grid=(model // block,),
        out_shape=[
            jax.ShapeDtypeStruct((rows, model), bf16),
            jax.ShapeDtypeStruct((1, model), f32),
        ],
        in_specs=[
            pl.BlockSpec((rows, inner), lambda i: (0, 0)),
            pl.BlockSpec((block, inner), lambda i: (i, 0)),
            pl.BlockSpec((1, block), lambda i: (0, i)),
            pl.BlockSpec((rows, block), lambda i: (0, i)),
            ANY,
        ],
        out_specs=[
            pl.BlockSpec((rows, block), lambda i: (0, i)),
            pl.BlockSpec((1, block), lambda i: (0, i)),
        ],
        compiler_params=params(),
        cost_estimate=cost(2 * rows * inner * model, 2 * inner * model),
    )(attn, out_weight, gate, d_out, after)


def grad_kernel(n_pieces, left_ref, *refs):
    pieces, outs = refs[:n_pieces], refs[n_pieces:]
    rows, width = outs[0].shape
    block = 256
    for start in range(0, width, block):
        cols = slice(start, start + block)
        right = jnp.concatenate([p[:, cols] for p in pieces], axis=0)
        got = jnp.dot(left_ref[...], right, preferred_element_type=f32)
        for g, out in enumerate(outs):
            out[:, cols] = got[g * rows : (g + 1) * rows].astype(out.dtype)


def grad_product(left, pieces, groups):
    total, depth = left.shape
    width = pieces[0].shape[1]
    shapes = [jax.ShapeDtypeStruct((total // groups, width), f32)]
    shapes += [jax.ShapeDtypeStruct((total // groups, width), bf16)] * (groups - 1)
    return pl.pallas_call(
        functools.partial(grad_kernel, len(pieces)),
        out_shape=shapes,
        in_specs=[VMEM] * (1 + len(pieces)),
        out_specs=[VMEM] * groups,
        compiler_params=params(),
        cost_estimate=cost(
            2 * total * depth * width, 2 * (total * depth + depth * width + total * width)
        ),
    )(left, *pieces)


def on_device(
    caption_states,
    caption_gain,
    text_proj,
    caption_len,
    slot_source,
    query_gain,
    key_gain,
    image_q,
    image_k,
    image_v,
    out_weight,
    gate,
    d_out,
):
    n_dp = lax.axis_size("dp")
    n_seq = lax.axis_size("seq")
    G, C = GROUPS, CORES
    O = n_seq // (G * C)
    OC = O * C
    dp = lax.axis_index("dp")
    seq = lax.axis_index("seq")
    z = (seq // C) % G
    oc = (seq // (G * C)) * C + seq % C

    def place(oc_at, z_at):
        return ((oc_at // C) * G + z_at) * C + oc_at % C

    def to_z(x, k):
        perm = [(place(a, b), place(a, b ^ k)) for a in range(OC) for b in range(G)]
        return lax.ppermute(x, "seq", perm)

    def to_oc(x, j):
        perm = [(place(a, b), place(a ^ j, b)) for a in range(OC) for b in range(G)]
        return lax.ppermute(x, "seq", perm)

    def to_dp(x, k):
        return lax.ppermute(x, "dp", [(a, a ^ k) for a in range(n_dp)])

    def part(x, index, size, axis):
        return lax.dynamic_slice_in_dim(x, index * size, size, axis)

    slot_total = slot_source.shape[1]
    slot_local = slot_total // n_seq
    image_local = image_q.shape[1]
    inner_width = image_q.shape[2]
    model_width = out_weight.shape[0]
    head_size = query_gain.shape[0]
    gw = inner_width // G
    far = [2, 3]
    near = [1, 0]
    z_order = z ^ jnp.arange(G, dtype=jnp.int32)
    oc_order = oc ^ jnp.arange(OC, dtype=jnp.int32)

    packed = pack(z_order * gw, image_k[0], image_v[0], image_q[0], G)
    qkv = {0: packed[0]}
    for k in far + near[:1]:
        qkv[k] = to_z(packed[k], k)
    kv_pieces = [qkv[k] for k in range(G)]
    for j in range(1, OC):
        kv_pieces += [to_oc(qkv[k][:, : 2 * gw], j) for k in range(G)]

    sources = slot_source[0].reshape(O, G, C, slot_local)
    sources = jnp.transpose(sources, (0, 2, 1, 3)).reshape(OC, G * slot_local)
    sources = jnp.take(sources, oc_order, axis=0)
    pick = (sources.reshape(-1, 1) == jnp.arange(slot_total, dtype=jnp.int32)).astype(bf16)
    bias = jnp.where(sources.reshape(1, -1) < caption_len[0], 0.0, -1e30).astype(f32)
    partials = text_project(
        z_order, caption_states[0], caption_gain[None], pick, text_proj, G, OC
    )
    got = [to_oc(partials[j], j) for j in range(1, OC)]
    sums = text_sum(partials[0], got)
    got = [to_z(sums[k], k) for k in range(1, G)]
    gains = jnp.stack([query_gain, key_gain])
    text_q, text_kv = text_norm(gains, sums[0], got, DT5)
    text_kvs = [text_kv] + [to_oc(text_kv, j) for j in range(1, OC)]

    gate_row = gate[0]
    gated_grad = (gate_row * d_out[0].astype(f32)).astype(bf16)
    R = model_width // (n_dp * n_seq)
    gg_t = gated_grad.T.reshape(n_dp, O, G, C, R, image_local)
    gg_t = jnp.transpose(gg_t, (0, 1, 3, 2, 4, 5)).reshape(n_dp, OC, G * R, image_local)
    gg_dp = []
    for k in range(n_dp):
        sel = lax.dynamic_index_in_dim(gg_t, dp ^ k, 0, keepdims=False)
        gg_dp.append(sel if k == 0 else to_dp(sel, k))
    gg_left = []
    for j in range(OC):
        sel = [lax.dynamic_index_in_dim(g, oc ^ j, 0, keepdims=False) for g in gg_dp]
        if j:
            sent = to_oc(jnp.stack(sel), j)
            sel = [sent[k] for k in range(n_dp)]
        gg_left += sel
    left = jnp.concatenate(gg_left, axis=1).reshape(G, R, -1)
    left = jnp.take(left, z_order, axis=0).reshape(G * R, -1)
    d_attn = jnp.dot(gated_grad, out_weight, preferred_element_type=f32).astype(bf16)

    first = attention(
        [text_q] + [qkv[k] for k in far],
        kv_pieces, text_kvs, bias, [left, d_attn], gw, head_size,
    )
    second = attention(
        [qkv[k] for k in near], kv_pieces, text_kvs, bias, [first[0]], gw, head_size
    )
    outs = dict(zip(far + near, first[1:] + second))

    attn = jnp.zeros((image_local + slot_local, inner_width), bf16)
    for k in far + near:
        rows = jnp.concatenate([outs[k], part(first[0], z ^ k, slot_local, 0)], axis=0)
        rows = to_z(rows, k) if k else rows
        attn = lax.dynamic_update_slice_in_dim(attn, rows, (z ^ k) * gw, 1)
    image_attn = attn[:image_local]
    own_usable = part(slot_source[0] < caption_len[0], seq, slot_local, 0)
    text_attn = jnp.where(own_usable[:, None], attn[image_local:], jnp.zeros((), bf16))

    attn_dp = [image_attn] + [to_dp(image_attn, k) for k in range(1, n_dp)]
    attn_pieces = list(attn_dp)
    for j in range(1, OC):
        attn_pieces += [to_oc(p, j) for p in attn_dp]

    image_out, gate_term = project(image_attn, out_weight, gate, d_out[0], attn_dp[1])

    grads = grad_product(left, attn_pieces, G)
    grad_wo = grads[0]
    for k in range(1, G):
        grad_wo = grad_wo + to_z(grads[k], k).astype(f32)

    gate_term = jnp.transpose(gate_term.reshape(O, G, C, -1), (0, 2, 1, 3)).reshape(OC, G, 1, -1)
    gate_chip = lax.dynamic_index_in_dim(gate_term, oc, 0, keepdims=False)
    for j in range(1, OC):
        gate_chip = gate_chip + to_oc(
            lax.dynamic_index_in_dim(gate_term, oc ^ j, 0, keepdims=False), j
        )
    grad_gate = lax.dynamic_index_in_dim(gate_chip, z, 0, keepdims=False)
    for k in range(1, G):
        grad_gate = grad_gate + to_z(
            lax.dynamic_index_in_dim(gate_chip, z ^ k, 0, keepdims=False), k
        )
    return (image_out[None], text_attn[None], d_attn[None], grad_wo, grad_gate)


def solution(mesh):
    in_specs = (
        P("dp", None, "seq"),
        P("seq"),
        P("seq", None),
        P("dp"),
        P("dp", None),
        P(),
        P(),
        P("dp", "seq", None),
        P("dp", "seq", None),
        P("dp", "seq", None),
        P(),
        P("dp", None),
        P("dp", "seq", None),
    )
    out_specs = (
        P("dp", "seq", None),
        P("dp", "seq", None),
        P("dp", "seq", None),
        P(("dp", "seq"), None),
        P("dp", "seq"),
    )
    return jax.shard_map(
        on_device, mesh=mesh, in_specs=in_specs, out_specs=out_specs, check_vma=False
    )
```

time: 151 us -> 147 us (0.974)
  the two profiles are of different devices: /device:TPU:8 before, /device:TPU:0 now
where the time goes in v3:
time: 147 us; the launch traced here: 144 us
  local copies, waits for them, and re-layouts  35.9 us (24%)
  starting transfers between devices  35.8 us (24%)
  waiting for transfers between devices  35.2 us (24%)
  Pallas kernels  21.2 us (14%)
  other arithmetic  9.14 us (6%)
  matrix products  5.09 us (3%)
  between operations  1.8 us (1%)
    ppermute x15, waiting for transfers between devices, to_z(): return lax.ppermute(x, 'seq', perm)  27.3 us
    ppermute x15, starting transfers between devices, to_z(): return lax.ppermute(x, 'seq', perm)  26.1 us
    unnamed x52, local copies, waits for them, and re-layouts  17.9 us
    ppermute x6, starting transfers between devices, to_dp(): return lax.ppermute(x, 'dp', [(a, a ^ k) for a in range(n_dp)])  8.12 us
    pallas_call x2, Pallas kernels, attention(): pl.pallas_call(functools.partial(attention_kernel, counts, width, head_si...  7.93 us
    ppermute x6, waiting for transfers between devices, to_dp(): return lax.ppermute(x, 'dp', [(a, a ^ k) for a in range(n_dp)])  7.92 us
    dynamic_slice x4, local copies, waits for them, and re-layouts, on_device(): lax.dynamic_index_in_dim(g, oc ^ j, 0, keepdims=False)  5.88 us
    dot_general x1, matrix products, on_device(): jnp.dot(gated_grad, out_weight, preferred_element_type=f32).astype(bf16)  5.09 us
  transfers between devices with their start and end apart: 33, of which 7 were waited for; matrix products, arithmetic and copies ran while one was open for 25% of the time, Pallas kernels for 12%

profile of v3, /device:TPU:0, one launch (start us, length us, event | category | flops | bytes accessed | tf_op | source)
XLA Modules:
  0.0 144.2 jit_solution(13652136635242320834)
XLA Ops:
  0.6 1.3 fusion
  2.5 0.9 dynamic-slice_bitcast_fusion
  3.4 3.9 %collective-permute-start.14 = (bf16[2,384,128]{2,1,0:T(8,128)(2,1)}, bf16[2,384,128]{2,1,0:T(8,128)(2,1)}, u32[]{:S(2)}, u32[]{:S(2)}) collective-permute-start(bf16[2,384,128]{2,1,0:T(8,128)(2,1)} %get-tuple-element.55), channel_id=1, source_target_pairs={{0,24},{8,16},{16,8},{24,0},{1,25},{9,17},{17,9},{25,1},{2,26},{10... | collective-permute-start | bytes 589832 | tf_op jit(solution)/shard_map/ppermute | solution.py:331
  10.7 2.3 %copy-done.1 = bf16[512,4608]{1,0:T(8,128)(2,1)S(1)} copy-done((bf16[512,4608]{1,0:T(8,128)(2,1)S(1)}, bf16[512,4608]{1,0:T(8,128)(2,1)}, u32[]{:S(2)}) %copy-start.1) | copy-done | bytes 4718616
  13.1 3.6 %shard_map.164 = (f32[4,32,1280]{2,1,0:T(8,128)S(1)}, bf16[4,32,1280]{2,1,0:T(8,128)(2,1)}) custom-call(s32[4]{0:T(128)S(1)} %get-tuple-element.75.at_ref, bf16[64,512]{1,0:T(8,128)(2,1)S(1)} %bitcast.80, f32[1,512]{1,0:T(1,128)S(1)} %bitcast.81, bf16[64,64]{1,0:T(8,128)(2,1)S(1)} %fusion.1.pick_ref, bf16[512,4608]{1,0:T(8,128)(2,1)S(1)} %copy-done.1, ...), custom_call_target="tpu_custom_call" | custom-call | flops 301989888 | bytes 4718592 | tf_op jit(solution)/shard_map/pallas_call | solution.py:96
  16.7 1.6 %shard_map.167 = (bf16[128,1152]{1,0:T(8,128)(2,1)S(1)}, bf16[128,1152]{1,0:T(8,128)(2,1)}, bf16[128,1152]{1,0:T(8,128)(2,1)}, bf16[128,1152]{1,0:T(8,128)(2,1)}) custom-call(s32[4]{0:T(128)S(1)} %get-tuple-element.76.at_ref, bf16[128,1536]{1,0:T(8,128)(2,1)S(1)} %bitcast.75, bf16[128,1536]{1,0:T(8,128)(2,1)S(1)} %bitcast.76, bf16[128,1536]{1,0:T(8,128)(2,1)S(1)} %bitcast.77), custom_call_target="tpu_custom_call" | custom-call | bytes 2359296 | tf_op jit(solution)/shard_map/pallas_call | solution.py:46
  18.2 3.1 %collective-permute-start.4 = (bf16[128,1152]{1,0:T(8,128)(2,1)}, bf16[128,1152]{1,0:T(8,128)(2,1)S(1)}, u32[]{:S(2)}, u32[]{:S(2)}) collective-permute-start(bf16[128,1152]{1,0:T(8,128)(2,1)} %get-tuple-element.35), channel_id=1, source_target_pairs={{0,4},{2,6},{4,0},{6,2},{1,5},{3,7},{5,1},{7,3},{8,12},{10,14},{12... | collective-permute-start | bytes 884744 | tf_op jit(solution)/shard_map/ppermute | solution.py:324
  21.3 5.1 %convolution_convert_fusion.refs_15_ = bf16[128,1536]{1,0:T(8,128)(2,1)S(1)} fusion(bf16[3072,1536]{1,0:T(8,128)(2,1)} %w_ref.1, f32[3072]{0:T(1024)S(1)} %bitcast.79, bf16[1,128,3072]{2,1,0:T(8,128)(2,1)S(1)} %copy-done.2), kind=kOutput, calls=%fused_computation.2 | convolution fusion | flops 1209335808 | bytes 10629120 | tf_op jit(solution)/shard_map/dot_general | solution.py:389
  26.4 1.1 dynamic-slice_bitcast_fusion.3
  28.2 1.4 collective-permute-start.5
  29.7 1.6 %constant_dynamic-slice_fusion.11 = (bf16[1,384,128]{2,1,0:T(8,128)(2,1)S(1)}, bf16[1,384,128]{2,1,0:T(8,128)(2,1)}) fusion(bf16[2,384,128]{2,1,0:T(8,128)(2,1)} %collective-permute-done.14, s32[]{:T(128)S(6)} %select_n.178, s32[]{:T(128)S(6)} %select_n.173), kind=kLoop, calls=%fused_computation.42 | loop fusion | bytes 393224 | tf_op jit(solution)/shard_map/jit(dynamic_index_in_dim)/dynamic_slice | solution.py:382
  31.5 1.6 %constant_dynamic-slice_fusion.12 = (bf16[1,384,128]{2,1,0:T(8,128)(2,1)S(1)}, bf16[1,384,128]{2,1,0:T(8,128)(2,1)}) fusion(bf16[2,384,128]{2,1,0:T(8,128)(2,1)} %collective-permute-done.13, s32[]{:T(128)S(6)} %select_n.178, s32[]{:T(128)S(6)} %select_n.173), kind=kLoop, calls=%fused_computation.43 | loop fusion | bytes 393224 | tf_op jit(solution)/shard_map/jit(dynamic_index_in_dim)/dynamic_slice | solution.py:382
  33.1 1.6 %constant_dynamic-slice_fusion.13 = (bf16[1,384,128]{2,1,0:T(8,128)(2,1)S(1)}, bf16[1,384,128]{2,1,0:T(8,128)(2,1)}) fusion(bf16[2,384,128]{2,1,0:T(8,128)(2,1)} %collective-permute-done.12, s32[]{:T(128)S(6)} %select_n.178, s32[]{:T(128)S(6)} %select_n.173), kind=kLoop, calls=%fused_computation.44 | loop fusion | bytes 393224 | tf_op jit(solution)/shard_map/jit(dynamic_index_in_dim)/dynamic_slice | solution.py:382
  37.1 1.5 %constant_dynamic-update-slice_fusion.6 = bf16[4,96,1024]{2,1,0:T(8,128)(2,1)} fusion(bf16[4,96,1024]{2,1,0:T(8,128)(2,1)} %constant_dynamic-update-slice_fusion.7, bf16[4,96,128]{2,1,0:T(8,128)(2,1)} %bitcast.91), kind=kLoop, calls=%fused_computation.26 | loop fusion | bytes 196608
  38.6 1.5 %constant_dynamic-update-slice_fusion.5 = bf16[4,96,1024]{2,1,0:T(8,128)(2,1)} fusion(bf16[4,96,1024]{2,1,0:T(8,128)(2,1)} %constant_dynamic-update-slice_fusion.6, bf16[4,96,128]{2,1,0:T(8,128)(2,1)} %bitcast.90), kind=kLoop, calls=%fused_computation.25 | loop fusion | bytes 196608
  40.3 1.9 %collective-permute-start.1 = (bf16[32,1280]{1,0:T(8,128)(2,1)S(1)}, bf16[32,1280]{1,0:T(8,128)(2,1)S(1)}, u32[]{:S(2)}, u32[]{:S(2)}) collective-permute-start(bf16[32,1280]{1,0:T(8,128)(2,1)S(1)} %get-tuple-element.31), channel_id=1, source_target_pairs={{0,2},{2,0},{4,6},{6,4},{1,3},{3,1},{5,7},{7,5},{8,10},{10,8},{12,... | collective-permute-start | bytes 245768 | tf_op jit(solution)/shard_map/ppermute | solution.py:324
  42.2 1.7 %collective-permute-start.2 = (bf16[32,1280]{1,0:T(8,128)(2,1)S(1)}, bf16[32,1280]{1,0:T(8,128)(2,1)S(1)}, u32[]{:S(2)}, u32[]{:S(2)}) collective-permute-start(bf16[32,1280]{1,0:T(8,128)(2,1)S(1)} %get-tuple-element.32), channel_id=1, source_target_pairs={{0,4},{2,6},{4,0},{6,2},{1,5},{3,7},{5,1},{7,3},{8,12},{10,14},{12... | collective-permute-start | bytes 245768 | tf_op jit(solution)/shard_map/ppermute | solution.py:324
  43.9 1.6 %collective-permute-start.3 = (bf16[32,1280]{1,0:T(8,128)(2,1)S(1)}, bf16[32,1280]{1,0:T(8,128)(2,1)S(1)}, u32[]{:S(2)}, u32[]{:S(2)}) collective-permute-start(bf16[32,1280]{1,0:T(8,128)(2,1)S(1)} %get-tuple-element.33), channel_id=1, source_target_pairs={{0,6},{2,4},{4,2},{6,0},{1,7},{3,5},{5,3},{7,1},{8,14},{10,12},{12... | collective-permute-start | bytes 245768 | tf_op jit(solution)/shard_map/ppermute | solution.py:324
  45.5 1.5 %constant_dynamic-update-slice_fusion.4 = bf16[4,96,1024]{2,1,0:T(8,128)(2,1)} fusion(bf16[4,96,1024]{2,1,0:T(8,128)(2,1)} %constant_dynamic-update-slice_fusion.5, bf16[4,96,128]{2,1,0:T(8,128)(2,1)} %bitcast.89), kind=kLoop, calls=%fused_computation.24 | loop fusion | bytes 196608
  49.1 2.7 %collective-permute-done.1.refs_0_ = bf16[32,1280]{1,0:T(8,128)(2,1)S(1)} collective-permute-done((bf16[32,1280]{1,0:T(8,128)(2,1)S(1)}, bf16[32,1280]{1,0:T(8,128)(2,1)S(1)}, u32[]{:S(2)}, u32[]{:S(2)}) %collective-permute-start.1) | collective-permute-done | bytes 81952 | tf_op jit(solution)/shard_map/ppermute | solution.py:324
  51.8 1.6 %collective-permute-done.2.refs_1_ = bf16[32,1280]{1,0:T(8,128)(2,1)S(1)} collective-permute-done((bf16[32,1280]{1,0:T(8,128)(2,1)S(1)}, bf16[32,1280]{1,0:T(8,128)(2,1)S(1)}, u32[]{:S(2)}, u32[]{:S(2)}) %collective-permute-start.2) | collective-permute-done | bytes 81952 | tf_op jit(solution)/shard_map/ppermute | solution.py:324
  54.0 0.9 shard_map.166
  55.4 1.1 fusion.17
  59.1 2.6 %gather_fusion.1 = bf16[4,96,1024]{2,1,0:T(8,128)(2,1)} fusion(bf16[4,96,1024]{2,1,0:T(8,128)(2,1)} %constant_dynamic-update-slice_fusion, s32[1024]{0:T(1024)S(1)} %get-tuple-element.77), kind=kCustom, calls=%fused_computation.1 | custom fusion | bytes 1572880 | tf_op jit(solution)/shard_map/jit(_take)/gather | solution.py:388
  61.8 1.3 bitcast_select_fusion.refs_14_.left_ref
  63.1 4.5 %shard_map.168 = (bf16[32,384]{1,0:T(8,128)(2,1)S(1)}, bf16[128,384]{1,0:T(8,128)(2,1)S(1)}, bf16[128,384]{1,0:T(8,128)(2,1)S(1)}) custom-call(bf16[32,384]{1,0:T(8,128)(2,1)S(1)} %copy-done.10, bf16[128,1152]{1,0:T(8,128)(2,1)S(1)} %collective-permute-done.4.refs_1_.refs_5_.refs_4_, bf16[128,1152]{1,0:T(8,128)(2,1)S(1)} %collective-permute-done.5.refs_2_.refs_6_.refs_5_, ...), custom_call_target="tpu_custom_call" | custom-call | flops 481296384 | bytes 2113536 | tf_op jit(solution)/shard_map/pallas_call | solution.py:215
  67.6 5.4 %collective-permute-start.16 = (bf16[136,384]{1,0:T(8,128)(2,1)S(1)}, bf16[136,384]{1,0:T(8,128)(2,1)S(1)}, u32[]{:S(2)}, u32[]{:S(2)}) collective-permute-start(bf16[136,384]{1,0:T(8,128)(2,1)S(1)} %pad_maximum_fusion.1), channel_id=1, source_target_pairs={{0,4},{2,6},{4,0},{6,2},{1,5},{3,7},{5,1},{7,3},{8,12},{10,14},{12... | collective-permute-start | bytes 313352 | tf_op jit(solution)/shard_map/ppermute | solution.py:324
  73.1 2.8 %collective-permute-start.17 = (bf16[136,384]{1,0:T(8,128)(2,1)S(1)}, bf16[136,384]{1,0:T(8,128)(2,1)S(1)}, u32[]{:S(2)}, u32[]{:S(2)}) collective-permute-start(bf16[136,384]{1,0:T(8,128)(2,1)S(1)} %pad_maximum_fusion.2), channel_id=1, source_target_pairs={{0,6},{2,4},{4,2},{6,0},{1,7},{3,5},{5,3},{7,1},{8,14},{10,12},{12... | collective-permute-start | bytes 313352 | tf_op jit(solution)/shard_map/ppermute | solution.py:324
  75.8 3.5 %shard_map.169 = (bf16[128,384]{1,0:T(8,128)(2,1)S(1)}, bf16[128,384]{1,0:T(8,128)(2,1)S(1)}) custom-call(bf16[128,1152]{1,0:T(8,128)(2,1)S(1)} %collective-permute-done.6.refs_4_.refs_0_.refs_3_, bf16[128,1152]{1,0:T(8,128)(2,1)S(1)} %get-tuple-element.37.refs_3_.refs_1_.refs_2_, bf16[128,1152]{1,0:T(8,128)(2,1)S(1)} %get-tuple-element.37.refs_3_.refs_1_.refs_2_, ...), custom_call_target="tpu_custom_call" | custom-call | flops 427819008 | bytes 2064384 | tf_op jit(solution)/shard_map/pallas_call | solution.py:215
  79.5 2.0 %collective-permute-done.17 = bf16[136,384]{1,0:T(8,128)(2,1)S(1)} collective-permute-done((bf16[136,384]{1,0:T(8,128)(2,1)S(1)}, bf16[136,384]{1,0:T(8,128)(2,1)S(1)}, u32[]{:S(2)}, u32[]{:S(2)}) %collective-permute-start.17) | collective-permute-done | bytes 104480 | tf_op jit(solution)/shard_map/ppermute | solution.py:324
  81.5 2.6 %collective-permute-done.18 = bf16[136,384]{1,0:T(8,128)(2,1)S(1)} collective-permute-done((bf16[136,384]{1,0:T(8,128)(2,1)S(1)}, bf16[136,384]{1,0:T(8,128)(2,1)S(1)}, u32[]{:S(2)}, u32[]{:S(2)}) %collective-permute-start.18) | collective-permute-done | bytes 104480 | tf_op jit(solution)/shard_map/ppermute | solution.py:324
  84.2 1.6 %collective-permute-start.19 = (bf16[128,1536]{1,0:T(8,128)(2,1)S(1)}, bf16[128,1536]{1,0:T(8,128)(2,1)S(1)}, u32[]{:S(2)}, u32[]{:S(2)}) collective-permute-start(bf16[128,1536]{1,0:T(8,128)(2,1)S(1)} %slice.51.attn_ref.refs_0_), channel_id=1, source_target_pairs={{0,8},{8,0},{16,24},{24,16},{1,9},{9,1},{17,25},{25,17},{2,10},{10... | collective-permute-start | bytes 1179656 | tf_op jit(solution)/shard_map/ppermute | solution.py:331
  85.8 1.6 %collective-permute-start.21 = (bf16[128,1536]{1,0:T(8,128)(2,1)S(1)}, bf16[128,1536]{1,0:T(8,128)(2,1)S(1)}, u32[]{:S(2)}, u32[]{:S(2)}) collective-permute-start(bf16[128,1536]{1,0:T(8,128)(2,1)S(1)} %slice.51.attn_ref.refs_0_), channel_id=1, source_target_pairs={{0,24},{8,16},{16,8},{24,0},{1,25},{9,17},{17,9},{25,1},{2,26},{10... | collective-permute-start | bytes 1179656 | tf_op jit(solution)/shard_map/ppermute | solution.py:331
  88.4 7.9 %collective-permute-done.19.after_ref.refs_1_ = bf16[128,1536]{1,0:T(8,128)(2,1)S(1)} collective-permute-done((bf16[128,1536]{1,0:T(8,128)(2,1)S(1)}, bf16[128,1536]{1,0:T(8,128)(2,1)S(1)}, u32[]{:S(2)}, u32[]{:S(2)}) %collective-permute-start.19) | collective-permute-done | bytes 393248 | tf_op jit(solution)/shard_map/ppermute | solution.py:331
  96.3 3.7 %copy-done = bf16[3072,1536]{1,0:T(8,128)(2,1)S(1)} copy-done((bf16[3072,1536]{1,0:T(8,128)(2,1)S(1)}, bf16[3072,1536]{1,0:T(8,128)(2,1)}, u32[]{:S(2)}) %copy-start) | copy-done | bytes 9437208
  100.0 4.7 %shard_map.170 = (bf16[128,3072]{1,0:T(8,128)(2,1)}, f32[1,3072]{1,0:T(1,128)S(1)}) custom-call(bf16[128,1536]{1,0:T(8,128)(2,1)S(1)} %slice.51.attn_ref.refs_0_, bf16[3072,1536]{1,0:T(8,128)(2,1)S(1)} %copy-done, f32[1,3072]{1,0:T(1,128)S(1)} %copy-done.7, bf16[128,3072]{1,0:T(8,128)(2,1)S(1)} %bitcast.73, ...), custom_call_target="tpu_custom_call" | custom-call | flops 1207959552 | bytes 9437184 | tf_op jit(solution)/shard_map/pallas_call | solution.py:242
  110.9 2.2 %collective-permute-start.32 = (f32[1,384]{1,0:T(1,128)S(1)}, f32[1,384]{1,0:T(1,128)S(1)}, u32[]{:S(2)}, u32[]{:S(2)}) collective-permute-start(f32[1,384]{1,0:T(1,128)S(1)} %get-tuple-element.73), channel_id=1, source_target_pairs={{0,6},{2,4},{4,2},{6,0},{1,7},{3,5},{5,3},{7,1},{8,14},{10,12},{12... | collective-permute-start | bytes 4616 | tf_op jit(solution)/shard_map/ppermute | solution.py:324
  113.1 1.0 collective-permute-start.31
  114.1 1.0 copy-done.13
  115.1 1.0 copy-done.15
  116.1 2.4 %shard_map.171 = (f32[96,1536]{1,0:T(8,128)S(1)}, bf16[96,1536]{1,0:T(8,128)(2,1)S(1)}, bf16[96,1536]{1,0:T(8,128)(2,1)S(1)}, bf16[96,1536]{1,0:T(8,128)(2,1)S(1)}) custom-call(bf16[384,1024]{1,0:T(8,128)(2,1)S(1)} %bitcast_select_fusion.refs_14_.left_ref, bf16[128,1536]{1,0:T(8,128)(2,1)S(1)} %slice.51.attn_ref.refs_0_, ...), custom_call_target="tpu_custom_call" | custom-call | flops 1207959552 | bytes 5111808 | tf_op jit(solution)/shard_map/pallas_call | solution.py:282
  118.5 1.3 collective-permute-start.26
  119.7 1.2 collective-permute-start.27
  121.0 2.0 %collective-permute-start.28 = (bf16[96,1536]{1,0:T(8,128)(2,1)S(1)}, bf16[96,1536]{1,0:T(8,128)(2,1)S(1)}, u32[]{:S(2)}, u32[]{:S(2)}) collective-permute-start(bf16[96,1536]{1,0:T(8,128)(2,1)S(1)} %get-tuple-element.49), channel_id=1, source_target_pairs={{0,6},{2,4},{4,2},{6,0},{1,7},{3,5},{5,3},{7,1},{8,14},{10,12},{12... | collective-permute-start | bytes 884744 | tf_op jit(solution)/shard_map/ppermute | solution.py:324
  122.9 1.4 fusion.2
  124.9 6.7 %collective-permute-done.26 = bf16[96,1536]{1,0:T(8,128)(2,1)S(1)} collective-permute-done((bf16[96,1536]{1,0:T(8,128)(2,1)S(1)}, bf16[96,1536]{1,0:T(8,128)(2,1)S(1)}, u32[]{:S(2)}, u32[]{:S(2)}) %collective-permute-start.26) | collective-permute-done | bytes 294944 | tf_op jit(solution)/shard_map/ppermute | solution.py:324
  131.7 11.6 %collective-permute-done.27 = bf16[96,1536]{1,0:T(8,128)(2,1)S(1)} collective-permute-done((bf16[96,1536]{1,0:T(8,128)(2,1)S(1)}, bf16[96,1536]{1,0:T(8,128)(2,1)S(1)}, u32[]{:S(2)}, u32[]{:S(2)}) %collective-permute-start.27) | collective-permute-done | bytes 294944 | tf_op jit(solution)/shard_map/ppermute | solution.py:324
  143.2 0.9 convert_add_fusion
  (135 shorter events, 20.6 us)
Async XLA Ops:
  2.3 6.7 %copy-start.20 = (s32[1,64]{1,0:T(1,128)S(1)}, s32[1,64]{1,0:T(1,128)}, u32[]{:S(2)}) copy-start(s32[1,64]{1,0:T(1,128)} %param.17) | copy-start | bytes 772
  2.3 8.4 %copy-start.8 = (bf16[1,64,512]{2,1,0:T(8,128)(2,1)S(1)}, bf16[1,64,512]{2,1,0:T(8,128)(2,1)}, u32[]{:S(2)}) copy-start(bf16[1,64,512]{2,1,0:T(8,128)(2,1)} %param.13) | copy-start | bytes 196612
  2.4 8.4 %copy-start.11 = (f32[512]{0:T(512)S(1)}, f32[512]{0:T(512)}, u32[]{:S(2)}) copy-start(f32[512]{0:T(512)} %param.14) | copy-start | bytes 6148
  2.4 8.3 %copy-start.16 = (bf16[4,1,2,4,96,128]{5,4,3,2,0,1:T(8,128)(2,1)}, bf16[4,1,2,4,96,128]{5,4,3,2,0,1:T(8,128)(2,1)S(1)}, u32[]{:S(2)}) copy-start(bf16[4,1,2,4,96,128]{5,4,3,2,0,1:T(8,128)(2,1)S(1)} %copy.21) | copy-start | bytes 2359300
  3.4 24.8 %collective-permute-start.14 = (bf16[2,384,128]{2,1,0:T(8,128)(2,1)}, bf16[2,384,128]{2,1,0:T(8,128)(2,1)}, u32[]{:S(2)}, u32[]{:S(2)}) collective-permute-start(bf16[2,384,128]{2,1,0:T(8,128)(2,1)} %get-tuple-element.55), channel_id=1, source_target_pairs={{0,24},{8,16},{16,8},{24,0},{1,25},{9,17},{17,9},{25,1},{2,26},{10... | collective-permute-start | bytes 589832 | tf_op jit(solution)/shard_map/ppermute | solution.py:331
  7.3 24.0 %collective-permute-start.13 = (bf16[2,384,128]{2,1,0:T(8,128)(2,1)}, bf16[2,384,128]{2,1,0:T(8,128)(2,1)}, u32[]{:S(2)}, u32[]{:S(2)}) collective-permute-start(bf16[2,384,128]{2,1,0:T(8,128)(2,1)} %get-tuple-element.56), channel_id=1, source_target_pairs={{0,16},{8,24},{16,0},{24,8},{1,17},{9,25},{17,1},{25,9},{2,18},{10... | collective-permute-start | bytes 589832 | tf_op jit(solution)/shard_map/ppermute | solution.py:331
  7.8 25.3 %collective-permute-start.12 = (bf16[2,384,128]{2,1,0:T(8,128)(2,1)}, bf16[2,384,128]{2,1,0:T(8,128)(2,1)}, u32[]{:S(2)}, u32[]{:S(2)}) collective-permute-start(bf16[2,384,128]{2,1,0:T(8,128)(2,1)} %get-tuple-element.57), channel_id=1, source_target_pairs={{0,8},{8,0},{16,24},{24,16},{1,9},{9,1},{17,25},{25,17},{2,10},{10... | collective-permute-start | bytes 589832 | tf_op jit(solution)/shard_map/ppermute | solution.py:331
  10.7 2.3 %copy-start.1 = (bf16[512,4608]{1,0:T(8,128)(2,1)S(1)}, bf16[512,4608]{1,0:T(8,128)(2,1)}, u32[]{:S(2)}) copy-start(bf16[512,4608]{1,0:T(8,128)(2,1)} %wv_ref.1) | copy-start | bytes 14155780
  13.1 3.6 %copy-start.4 = (bf16[1,128,1536]{2,1,0:T(8,128)(2,1)S(1)}, bf16[1,128,1536]{2,1,0:T(8,128)(2,1)}, u32[]{:S(2)}) copy-start(bf16[1,128,1536]{2,1,0:T(8,128)(2,1)} %param.21) | copy-start | bytes 1179652
  13.1 3.6 %copy-start.5 = (bf16[1,128,1536]{2,1,0:T(8,128)(2,1)S(1)}, bf16[1,128,1536]{2,1,0:T(8,128)(2,1)}, u32[]{:S(2)}) copy-start(bf16[1,128,1536]{2,1,0:T(8,128)(2,1)} %param.22) | copy-start | bytes 1179652
  13.1 3.6 %copy-start.6 = (bf16[1,128,1536]{2,1,0:T(8,128)(2,1)S(1)}, bf16[1,128,1536]{2,1,0:T(8,128)(2,1)}, u32[]{:S(2)}) copy-start(bf16[1,128,1536]{2,1,0:T(8,128)(2,1)} %param.20) | copy-start | bytes 1179652
  13.1 8.2 %copy-start.7 = (f32[1,3072]{1,0:T(1,128)S(1)}, f32[1,3072]{1,0:T(1,128)}, u32[]{:S(2)}) copy-start(f32[1,3072]{1,0:T(1,128)} %gate_ref.1) | copy-start | bytes 36868
  16.7 4.7 %copy-start.2 = (bf16[1,128,3072]{2,1,0:T(8,128)(2,1)S(1)}, bf16[1,128,3072]{2,1,0:T(8,128)(2,1)}, u32[]{:S(2)}) copy-start(bf16[1,128,3072]{2,1,0:T(8,128)(2,1)} %param.25) | copy-start | bytes 2359300
  16.7 23.5 %collective-permute-start = (bf16[4,32,1280]{2,1,0:T(8,128)(2,1)}, bf16[4,32,1280]{2,1,0:T(8,128)(2,1)S(1)}, u32[]{:S(2)}, u32[]{:S(2)}) collective-permute-start(bf16[4,32,1280]{2,1,0:T(8,128)(2,1)} %get-tuple-element.29), channel_id=1, source_target_pairs={{0,1},{2,3},{4,5},{6,7},{1,0},{3,2},{5,4},{7,6},{8,9},{10,11},{12,... | collective-permute-start | bytes 983048 | tf_op jit(solution)/shard_map/ppermute | solution.py:328
  18.2 24.0 %collective-permute-start.4 = (bf16[128,1152]{1,0:T(8,128)(2,1)}, bf16[128,1152]{1,0:T(8,128)(2,1)S(1)}, u32[]{:S(2)}, u32[]{:S(2)}) collective-permute-start(bf16[128,1152]{1,0:T(8,128)(2,1)} %get-tuple-element.35), channel_id=1, source_target_pairs={{0,4},{2,6},{4,0},{6,2},{1,5},{3,7},{5,1},{7,3},{8,12},{10,14},{12... | collective-permute-start | bytes 884744 | tf_op jit(solution)/shard_map/ppermute | solution.py:324
  21.3 6.9 %copy-start.18 = (f32[128]{0:T(128)S(1)}, f32[128]{0:T(128)}, u32[]{:S(2)}) copy-start(f32[128]{0:T(128)} %param.19) | copy-start | bytes 1540
  21.3 6.9 %copy-start.19 = (f32[128]{0:T(128)S(1)}, f32[128]{0:T(128)}, u32[]{:S(2)}) copy-start(f32[128]{0:T(128)} %param.18) | copy-start | bytes 1540
  26.4 36.7 %copy-start.3 = (bf16[128,1536]{1,0:T(8,128)(2,1)}, bf16[128,1536]{1,0:T(8,128)(2,1)S(1)}, u32[]{:S(2)}) copy-start(bf16[128,1536]{1,0:T(8,128)(2,1)S(1)} %convolution_convert_fusion.refs_15_) | copy-start | bytes 1179652
  28.2 15.7 %collective-permute-start.5 = (bf16[128,1152]{1,0:T(8,128)(2,1)}, bf16[128,1152]{1,0:T(8,128)(2,1)S(1)}, u32[]{:S(2)}, u32[]{:S(2)}) collective-permute-start(bf16[128,1152]{1,0:T(8,128)(2,1)} %get-tuple-element.36), channel_id=1, source_target_pairs={{0,6},{2,4},{4,2},{6,0},{1,7},{3,5},{5,3},{7,1},{8,14},{10,12},{12... | collective-permute-start | bytes 884744 | tf_op jit(solution)/shard_map/ppermute | solution.py:324
  31.2 17.2 %collective-permute-start.6 = (bf16[128,1152]{1,0:T(8,128)(2,1)}, bf16[128,1152]{1,0:T(8,128)(2,1)S(1)}, u32[]{:S(2)}, u32[]{:S(2)}) collective-permute-start(bf16[128,1152]{1,0:T(8,128)(2,1)} %get-tuple-element.38), channel_id=1, source_target_pairs={{0,2},{2,0},{4,6},{6,4},{1,3},{3,1},{5,7},{7,5},{8,10},{10,8},{12,... | collective-permute-start | bytes 884744 | tf_op jit(solution)/shard_map/ppermute | solution.py:324
  35.5 20.0 %collective-permute-start.15 = (bf16[4,384,128]{2,1,0:T(8,128)(2,1)}, bf16[4,384,128]{2,1,0:T(8,128)(2,1)}, u32[]{:S(2)}, u32[]{:S(2)}) collective-permute-start(bf16[4,384,128]{2,1,0:T(8,128)(2,1)} %pad_maximum_fusion), channel_id=1, source_target_pairs={{0,1},{2,3},{4,5},{6,7},{1,0},{3,2},{5,4},{7,6},{8,9},{10,11},{12,... | collective-permute-start | bytes 1179656 | tf_op jit(solution)/shard_map/ppermute | solution.py:328
  40.3 11.5 %collective-permute-start.1 = (bf16[32,1280]{1,0:T(8,128)(2,1)S(1)}, bf16[32,1280]{1,0:T(8,128)(2,1)S(1)}, u32[]{:S(2)}, u32[]{:S(2)}) collective-permute-start(bf16[32,1280]{1,0:T(8,128)(2,1)S(1)} %get-tuple-element.31), channel_id=1, source_target_pairs={{0,2},{2,0},{4,6},{6,4},{1,3},{3,1},{5,7},{7,5},{8,10},{10,8},{12,... | collective-permute-start | bytes 245768 | tf_op jit(solution)/shard_map/ppermute | solution.py:324
  42.2 11.2 %collective-permute-start.2 = (bf16[32,1280]{1,0:T(8,128)(2,1)S(1)}, bf16[32,1280]{1,0:T(8,128)(2,1)S(1)}, u32[]{:S(2)}, u32[]{:S(2)}) collective-permute-start(bf16[32,1280]{1,0:T(8,128)(2,1)S(1)} %get-tuple-element.32), channel_id=1, source_target_pairs={{0,4},{2,6},{4,0},{6,2},{1,5},{3,7},{5,1},{7,3},{8,12},{10,14},{12... | collective-permute-start | bytes 245768 | tf_op jit(solution)/shard_map/ppermute | solution.py:324
  43.9 9.6 %collective-permute-start.3 = (bf16[32,1280]{1,0:T(8,128)(2,1)S(1)}, bf16[32,1280]{1,0:T(8,128)(2,1)S(1)}, u32[]{:S(2)}, u32[]{:S(2)}) collective-permute-start(bf16[32,1280]{1,0:T(8,128)(2,1)S(1)} %get-tuple-element.33), channel_id=1, source_target_pairs={{0,6},{2,4},{4,2},{6,0},{1,7},{3,5},{5,3},{7,1},{8,14},{10,12},{12... | collective-permute-start | bytes 245768 | tf_op jit(solution)/shard_map/ppermute | solution.py:324
  48.4 14.6 %collective-permute-start.7 = (bf16[128,768]{1,0:T(8,128)(2,1)}, bf16[128,768]{1,0:T(8,128)(2,1)S(1)}, u32[]{:S(2)}, u32[]{:S(2)}) collective-permute-start(bf16[128,768]{1,0:T(8,128)(2,1)} %slice.30), channel_id=1, source_target_pairs={{0,1},{2,3},{4,5},{6,7},{1,0},{3,2},{5,4},{7,6},{8,9},{10,11},{12,... | collective-permute-start | bytes 589832 | tf_op jit(solution)/shard_map/ppermute | solution.py:328
  51.8 11.3 %collective-permute-start.9 = (bf16[128,768]{1,0:T(8,128)(2,1)}, bf16[128,768]{1,0:T(8,128)(2,1)S(1)}, u32[]{:S(2)}, u32[]{:S(2)}) collective-permute-start(bf16[128,768]{1,0:T(8,128)(2,1)} %slice.45), channel_id=1, source_target_pairs={{0,1},{2,3},{4,5},{6,7},{1,0},{3,2},{5,4},{7,6},{8,9},{10,11},{12,... | collective-permute-start | bytes 589832 | tf_op jit(solution)/shard_map/ppermute | solution.py:328
  53.4 9.6 %collective-permute-start.10 = (bf16[128,768]{1,0:T(8,128)(2,1)}, bf16[128,768]{1,0:T(8,128)(2,1)}, u32[]{:S(2)}, u32[]{:S(2)}) collective-permute-start(bf16[128,768]{1,0:T(8,128)(2,1)} %slice.46), channel_id=1, source_target_pairs={{0,1},{2,3},{4,5},{6,7},{1,0},{3,2},{5,4},{7,6},{8,9},{10,11},{12,... | collective-permute-start | bytes 589832 | tf_op jit(solution)/shard_map/ppermute | solution.py:328
  53.5 9.6 %collective-permute-start.8 = (bf16[128,768]{1,0:T(8,128)(2,1)}, bf16[128,768]{1,0:T(8,128)(2,1)}, u32[]{:S(2)}, u32[]{:S(2)}) collective-permute-start(bf16[128,768]{1,0:T(8,128)(2,1)} %slice.44), channel_id=1, source_target_pairs={{0,1},{2,3},{4,5},{6,7},{1,0},{3,2},{5,4},{7,6},{8,9},{10,11},{12,... | collective-permute-start | bytes 589832 | tf_op jit(solution)/shard_map/ppermute | solution.py:328
  55.4 7.6 %collective-permute-start.11 = (bf16[32,768]{1,0:T(8,128)(2,1)}, bf16[32,768]{1,0:T(8,128)(2,1)}, u32[]{:S(2)}, u32[]{:S(2)}) collective-permute-start(bf16[32,768]{1,0:T(8,128)(2,1)} %get-tuple-element.39.refs_11_.refs_10_), channel_id=1, source_target_pairs={{0,1},{2,3},{4,5},{6,7},{1,0},{3,2},{5,4},{7,6},{8,9},{10,11},{12,... | collective-permute-start | bytes 147464 | tf_op jit(solution)/shard_map/ppermute | solution.py:328
  67.6 11.8 %collective-permute-start.16 = (bf16[136,384]{1,0:T(8,128)(2,1)S(1)}, bf16[136,384]{1,0:T(8,128)(2,1)S(1)}, u32[]{:S(2)}, u32[]{:S(2)}) collective-permute-start(bf16[136,384]{1,0:T(8,128)(2,1)S(1)} %pad_maximum_fusion.1), channel_id=1, source_target_pairs={{0,4},{2,6},{4,0},{6,2},{1,5},{3,7},{5,1},{7,3},{8,12},{10,14},{12... | collective-permute-start | bytes 313352 | tf_op jit(solution)/shard_map/ppermute | solution.py:324
  73.1 8.4 %collective-permute-start.17 = (bf16[136,384]{1,0:T(8,128)(2,1)S(1)}, bf16[136,384]{1,0:T(8,128)(2,1)S(1)}, u32[]{:S(2)}, u32[]{:S(2)}) collective-permute-start(bf16[136,384]{1,0:T(8,128)(2,1)S(1)} %pad_maximum_fusion.2), channel_id=1, source_target_pairs={{0,6},{2,4},{4,2},{6,0},{1,7},{3,5},{5,3},{7,1},{8,14},{10,12},{12... | collective-permute-start | bytes 313352 | tf_op jit(solution)/shard_map/ppermute | solution.py:324
  79.3 8.6 %copy-start.21 = (s32[1,64]{1,0:T(1,128)S(1)}, s32[1,64]{1,0:T(1,128)}, u32[]{:S(2)}) copy-start(s32[1,64]{1,0:T(1,128)} %param.17) | copy-start | bytes 772
  79.3 4.8 %collective-permute-start.18 = (bf16[136,384]{1,0:T(8,128)(2,1)S(1)}, bf16[136,384]{1,0:T(8,128)(2,1)S(1)}, u32[]{:S(2)}, u32[]{:S(2)}) collective-permute-start(bf16[136,384]{1,0:T(8,128)(2,1)S(1)} %pad_maximum_fusion.3), channel_id=1, source_target_pairs={{0,2},{2,0},{4,6},{6,4},{1,3},{3,1},{5,7},{7,5},{8,10},{10,8},{12,... | collective-permute-start | bytes 313352 | tf_op jit(solution)/shard_map/ppermute | solution.py:324
  84.2 12.1 %collective-permute-start.19 = (bf16[128,1536]{1,0:T(8,128)(2,1)S(1)}, bf16[128,1536]{1,0:T(8,128)(2,1)S(1)}, u32[]{:S(2)}, u32[]{:S(2)}) collective-permute-start(bf16[128,1536]{1,0:T(8,128)(2,1)S(1)} %slice.51.attn_ref.refs_0_), channel_id=1, source_target_pairs={{0,8},{8,0},{16,24},{24,16},{1,9},{9,1},{17,25},{25,17},{2,10},{10... | collective-permute-start | bytes 1179656 | tf_op jit(solution)/shard_map/ppermute | solution.py:331
  85.8 21.3 %collective-permute-start.21 = (bf16[128,1536]{1,0:T(8,128)(2,1)S(1)}, bf16[128,1536]{1,0:T(8,128)(2,1)S(1)}, u32[]{:S(2)}, u32[]{:S(2)}) collective-permute-start(bf16[128,1536]{1,0:T(8,128)(2,1)S(1)} %slice.51.attn_ref.refs_0_), channel_id=1, source_target_pairs={{0,24},{8,16},{16,8},{24,0},{1,25},{9,17},{17,9},{25,1},{2,26},{10... | collective-permute-start | bytes 1179656 | tf_op jit(solution)/shard_map/ppermute | solution.py:331
  87.4 20.5 %collective-permute-start.20 = (bf16[128,1536]{1,0:T(8,128)(2,1)S(1)}, bf16[128,1536]{1,0:T(8,128)(2,1)S(1)}, u32[]{:S(2)}, u32[]{:S(2)}) collective-permute-start(bf16[128,1536]{1,0:T(8,128)(2,1)S(1)} %slice.51.attn_ref.refs_0_), channel_id=1, source_target_pairs={{0,16},{8,24},{16,0},{24,8},{1,17},{9,25},{17,1},{25,9},{2,18},{10... | collective-permute-start | bytes 1179656 | tf_op jit(solution)/shard_map/ppermute | solution.py:331
  88.4 22.5 %collective-permute-start.22 = (bf16[128,1536]{1,0:T(8,128)(2,1)S(1)}, bf16[128,1536]{1,0:T(8,128)(2,1)}, u32[]{:S(2)}, u32[]{:S(2)}) collective-permute-start(bf16[128,1536]{1,0:T(8,128)(2,1)S(1)} %slice.51.attn_ref.refs_0_), channel_id=1, source_target_pairs={{0,1},{2,3},{4,5},{6,7},{1,0},{3,2},{5,4},{7,6},{8,9},{10,11},{12,... | collective-permute-start | bytes 1179656 | tf_op jit(solution)/shard_map/ppermute | solution.py:328
  96.3 3.7 %copy-start = (bf16[3072,1536]{1,0:T(8,128)(2,1)S(1)}, bf16[3072,1536]{1,0:T(8,128)(2,1)}, u32[]{:S(2)}) copy-start(bf16[3072,1536]{1,0:T(8,128)(2,1)} %w_ref.1) | copy-start | bytes 28311556
  106.6 3.2 %collective-permute-start.29 = (f32[4,1,384]{2,1,0:T(1,128)}, f32[4,1,384]{2,1,0:T(1,128)}, u32[]{:S(2)}, u32[]{:S(2)}) collective-permute-start(f32[4,1,384]{2,1,0:T(1,128)} %fusion.5), channel_id=1, source_target_pairs={{0,1},{2,3},{4,5},{6,7},{1,0},{3,2},{5,4},{7,6},{8,9},{10,11},{12,... | collective-permute-start | bytes 18440 | tf_op jit(solution)/shard_map/ppermute | solution.py:328
  106.6 7.5 %collective-permute-start.23 = (bf16[128,1536]{1,0:T(8,128)(2,1)S(1)}, bf16[128,1536]{1,0:T(8,128)(2,1)S(1)}, u32[]{:S(2)}, u32[]{:S(2)}) collective-permute-start(bf16[128,1536]{1,0:T(8,128)(2,1)S(1)} %collective-permute-done.19.after_ref.refs_1_), channel_id=1, source_target_pairs={{0,1},{2,3},{4,5},{6,7},{1,0},{3,2},{5,4},{7,6},{8,9},{10,11},{12,... | collective-permute-start | bytes 1179656 | tf_op jit(solution)/shard_map/ppermute | solution.py:328
  107.1 6.0 %collective-permute-start.25 = (bf16[128,1536]{1,0:T(8,128)(2,1)S(1)}, bf16[128,1536]{1,0:T(8,128)(2,1)S(1)}, u32[]{:S(2)}, u32[]{:S(2)}) collective-permute-start(bf16[128,1536]{1,0:T(8,128)(2,1)S(1)} %collective-permute-done.21.refs_3_), channel_id=1, source_target_pairs={{0,1},{2,3},{4,5},{6,7},{1,0},{3,2},{5,4},{7,6},{8,9},{10,11},{12,... | collective-permute-start | bytes 1179656 | tf_op jit(solution)/shard_map/ppermute | solution.py:328
  107.9 6.2 %collective-permute-start.24 = (bf16[128,1536]{1,0:T(8,128)(2,1)S(1)}, bf16[128,1536]{1,0:T(8,128)(2,1)S(1)}, u32[]{:S(2)}, u32[]{:S(2)}) collective-permute-start(bf16[128,1536]{1,0:T(8,128)(2,1)S(1)} %collective-permute-done.20.refs_2_), channel_id=1, source_target_pairs={{0,1},{2,3},{4,5},{6,7},{1,0},{3,2},{5,4},{7,6},{8,9},{10,11},{12,... | collective-permute-start | bytes 1179656 | tf_op jit(solution)/shard_map/ppermute | solution.py:328
  110.5 10.4 %collective-permute-start.30 = (f32[1,384]{1,0:T(1,128)S(1)}, f32[1,384]{1,0:T(1,128)S(1)}, u32[]{:S(2)}, u32[]{:S(2)}) collective-permute-start(f32[1,384]{1,0:T(1,128)S(1)} %get-tuple-element.72), channel_id=1, source_target_pairs={{0,2},{2,0},{4,6},{6,4},{1,3},{3,1},{5,7},{7,5},{8,10},{10,8},{12,... | collective-permute-start | bytes 4616 | tf_op jit(solution)/shard_map/ppermute | solution.py:324
  110.9 13.5 %collective-permute-start.32 = (f32[1,384]{1,0:T(1,128)S(1)}, f32[1,384]{1,0:T(1,128)S(1)}, u32[]{:S(2)}, u32[]{:S(2)}) collective-permute-start(f32[1,384]{1,0:T(1,128)S(1)} %get-tuple-element.73), channel_id=1, source_target_pairs={{0,6},{2,4},{4,2},{6,0},{1,7},{3,5},{5,3},{7,1},{8,14},{10,12},{12... | collective-permute-start | bytes 4616 | tf_op jit(solution)/shard_map/ppermute | solution.py:324
  113.1 11.3 %collective-permute-start.31 = (f32[1,384]{1,0:T(1,128)S(1)}, f32[1,384]{1,0:T(1,128)S(1)}, u32[]{:S(2)}, u32[]{:S(2)}) collective-permute-start(f32[1,384]{1,0:T(1,128)S(1)} %get-tuple-element.74), channel_id=1, source_target_pairs={{0,4},{2,6},{4,0},{6,2},{1,5},{3,7},{5,1},{7,3},{8,12},{10,14},{12... | collective-permute-start | bytes 4616 | tf_op jit(solution)/shard_map/ppermute | solution.py:324
  118.5 13.2 %collective-permute-start.26 = (bf16[96,1536]{1,0:T(8,128)(2,1)S(1)}, bf16[96,1536]{1,0:T(8,128)(2,1)S(1)}, u32[]{:S(2)}, u32[]{:S(2)}) collective-permute-start(bf16[96,1536]{1,0:T(8,128)(2,1)S(1)} %get-tuple-element.47), channel_id=1, source_target_pairs={{0,2},{2,0},{4,6},{6,4},{1,3},{3,1},{5,7},{7,5},{8,10},{10,8},{12,... | collective-permute-start | bytes 884744 | tf_op jit(solution)/shard_map/ppermute | solution.py:324
  119.7 23.5 %collective-permute-start.27 = (bf16[96,1536]{1,0:T(8,128)(2,1)S(1)}, bf16[96,1536]{1,0:T(8,128)(2,1)S(1)}, u32[]{:S(2)}, u32[]{:S(2)}) collective-permute-start(bf16[96,1536]{1,0:T(8,128)(2,1)S(1)} %get-tuple-element.48), channel_id=1, source_target_pairs={{0,4},{2,6},{4,0},{6,2},{1,5},{3,7},{5,1},{7,3},{8,12},{10,14},{12... | collective-permute-start | bytes 884744 | tf_op jit(solution)/shard_map/ppermute | solution.py:324
  121.0 22.3 %collective-permute-start.28 = (bf16[96,1536]{1,0:T(8,128)(2,1)S(1)}, bf16[96,1536]{1,0:T(8,128)(2,1)S(1)}, u32[]{:S(2)}, u32[]{:S(2)}) collective-permute-start(bf16[96,1536]{1,0:T(8,128)(2,1)S(1)} %get-tuple-element.49), channel_id=1, source_target_pairs={{0,6},{2,4},{4,2},{6,0},{1,7},{3,5},{5,3},{7,1},{8,14},{10,12},{12... | collective-permute-start | bytes 884744 | tf_op jit(solution)/shard_map/ppermute | solution.py:324
  (7 other events, 7.1 us)

commit v4 on v3

v4 whole, which is shorter than its diff:
```python
import math
import functools
import jax
import jax.numpy as jnp
from jax import lax
from jax.experimental import pallas as pl
from jax.experimental.pallas import tpu as pltpu
from jax.sharding import PartitionSpec as P

DT5 = 4096
CORES = 2
GROUPS = 4

eps_norm = 1e-06
f32 = jnp.float32
bf16 = jnp.bfloat16


VMEM = pl.BlockSpec(memory_space=pltpu.VMEM)
SMEM = pl.BlockSpec(memory_space=pltpu.SMEM)
ANY = pl.BlockSpec(memory_space=pl.ANY)
HBM = pl.BlockSpec(memory_space=pltpu.HBM)
TAIL = 128


def params(mib=16):
    return pltpu.CompilerParams(vmem_limit_bytes=mib * 1024 * 1024)


def cost(flops, bytes_accessed, transcendentals=0):
    return pl.CostEstimate(
        flops=flops, bytes_accessed=bytes_accessed, transcendentals=transcendentals
    )


def split_tail(squares):
    high = squares.astype(bf16).astype(f32)
    low = squares - high
    lane = lax.broadcasted_iota(jnp.int32, (squares.shape[0], TAIL), 1)
    return jnp.where(lane == 0, high, jnp.where(lane == 1, low, 0.0))


def text_kernel(
    groups, place_of, meta_ref, len_ref, src_ref, states_ref, gain_ref, w_ref,
    k_ref, v_ref, q_ref, bias_ref, *refs
):
    packed, own_ref, refs = refs[:groups], refs[groups], refs[groups + 1 :]
    msgs, (w_all, sems) = refs[:-2], refs[-2:]
    rows = own_ref.shape[1]
    width = w_all.shape[3]
    slots = states_ref.shape[0]
    slot_local = rows // groups
    copies = []
    for g in range(groups):
        at = pl.multiple_of((meta_ref[0] ^ g) * width, 128)
        for i in range(3):
            cols = pl.ds(pl.multiple_of(at + i * groups * width, 128), width)
            copies.append(pltpu.make_async_copy(w_ref.at[:, cols], w_all.at[g, i], sems.at[g, i]))
            copies[-1].start()
    for g, out in enumerate(packed):
        at = pl.multiple_of((meta_ref[0] ^ g) * width, 128)
        for i, ref in enumerate((k_ref, v_ref, q_ref)):
            out[:, i * width : (i + 1) * width] = ref[:, pl.ds(at, width)]
    oc = meta_ref[1]

    def slot_at(row):
        part = row // rows
        z_at = (row % rows) // slot_local
        return place_of(oc ^ part, z_at) * slot_local + row % slot_local

    iota = functools.partial(lax.broadcasted_iota, jnp.int32, (slots, slots))
    sources = src_ref[...].astype(f32)
    chosen = (iota(1) == slot_at(iota(0))).astype(f32)
    source_col = jnp.sum(chosen * sources, axis=1, keepdims=True)
    pick = (iota(1).astype(f32) == source_col).astype(bf16)
    chosen_t = (iota(0) == slot_at(iota(1))).astype(bf16)
    source_row = jnp.dot(sources.astype(bf16), chosen_t, preferred_element_type=f32)
    bias_ref[...] = jnp.where(source_row < len_ref[0].astype(f32), 0.0, -1e30)

    picked = jnp.dot(pick, states_ref[...], preferred_element_type=f32)
    scaled = (picked * gain_ref[...]).astype(bf16)
    tail = split_tail(jnp.sum(picked * picked, axis=1, keepdims=True))
    for g in range(groups):
        for i in range(3):
            copies[3 * g + i].wait()
            got = jnp.dot(scaled, w_all[g, i], preferred_element_type=f32)
            cols = slice(i * width, (i + 1) * width)
            own_ref[g, :, cols] = got[:rows]
            for j, msg in enumerate(msgs):
                msg[g, :, cols] = got[(j + 1) * rows : (j + 2) * rows].astype(bf16)
        own_ref[g, :, 3 * width :] = tail[:rows]
        for j, msg in enumerate(msgs):
            msg[g, :, 3 * width :] = tail[(j + 1) * rows : (j + 2) * rows].astype(bf16)


def text_project(
    meta, length, sources, states, gain, text_proj, keys, values, queries, groups, parts, place_of
):
    slots, depth = states.shape
    rows = slots // parts
    width = text_proj.shape[1] // (3 * groups)
    full = 3 * width + TAIL
    shapes = [jax.ShapeDtypeStruct((1, slots), f32)]
    shapes += [jax.ShapeDtypeStruct((keys.shape[0], 3 * width), bf16)] * groups
    shapes += [jax.ShapeDtypeStruct((groups, rows, full), f32)]
    shapes += [jax.ShapeDtypeStruct((groups, rows, full), bf16)] * (parts - 1)
    return pl.pallas_call(
        functools.partial(text_kernel, groups, place_of),
        out_shape=shapes,
        in_specs=[SMEM, SMEM, VMEM, VMEM, VMEM, HBM, VMEM, VMEM, VMEM],
        out_specs=[VMEM] * (1 + groups + parts),
        scratch_shapes=[
            pltpu.VMEM((groups, 3, depth, width), bf16),
            pltpu.SemaphoreType.DMA((groups, 3)),
        ],
        compiler_params=params(60),
        cost_estimate=cost(
            2 * slots * depth * text_proj.shape[1], 2 * depth * text_proj.shape[1]
        ),
    )(meta, length, sources, states, gain, text_proj, keys, values, queries)


def text_sum_kernel(n_got, own_ref, *refs):
    got, outs = refs[:n_got], refs[n_got:]
    for g, out in enumerate(outs):
        total = own_ref[g]
        for ref in got:
            total = total + ref[g].astype(f32)
        width = total.shape[1] - TAIL
        tail = total[:, width:]
        out[:, :width] = total[:, :width].astype(out.dtype)
        out[:, width:] = split_tail(tail[:, 0:1] + tail[:, 1:2]).astype(out.dtype)


def text_sum(own, got):
    groups, rows, full = own.shape
    shapes = [jax.ShapeDtypeStruct((rows, full), f32)]
    shapes += [jax.ShapeDtypeStruct((rows, full), bf16)] * (groups - 1)
    return pl.pallas_call(
        functools.partial(text_sum_kernel, len(got)),
        out_shape=shapes,
        in_specs=[VMEM] * (1 + len(got)),
        out_specs=[VMEM] * groups,
        compiler_params=params(),
        cost_estimate=cost(0, 8 * groups * rows * full),
    )(own, *got)


def text_norm_kernel(features, head_size, through_ref, after_ref, qg_ref, kg_ref, own_ref, *refs):
    del through_ref, after_ref
    got, (_, tq_ref, tkv_ref) = refs[:-3], refs[-3:]
    total = own_ref[...]
    for ref in got:
        total = total + ref[...].astype(f32)
    width = tq_ref.shape[1]
    squares = total[:, 3 * width : 3 * width + 1] + total[:, 3 * width + 1 : 3 * width + 2]
    normed = total[:, : 3 * width] * lax.rsqrt(squares / features + eps_norm)
    for i, (out, gain_ref) in enumerate(((tq_ref, qg_ref), (tkv_ref, kg_ref))):
        for head in range(width // head_size):
            cols = slice(head * head_size, (head + 1) * head_size)
            x = normed[:, i * width + head * head_size : i * width + (head + 1) * head_size]
            mean = jnp.mean(x * x, axis=1, keepdims=True)
            out[:, cols] = (x * lax.rsqrt(mean + eps_norm) * gain_ref[...]).astype(bf16)
    tkv_ref[:, width:] = normed[:, 2 * width :].astype(bf16)


def text_norm(through, after, query_gain, key_gain, own, got, features):
    rows, full = own.shape
    width = (full - TAIL) // 3
    return pl.pallas_call(
        functools.partial(text_norm_kernel, features, query_gain.shape[1]),
        out_shape=[
            jax.ShapeDtypeStruct(through.shape, through.dtype),
            jax.ShapeDtypeStruct((rows, width), bf16),
            jax.ShapeDtypeStruct((rows, 2 * width), bf16),
        ],
        in_specs=[ANY] * 2 + [VMEM] * (3 + len(got)),
        out_specs=[ANY] + [VMEM] * 2,
        input_output_aliases={0: 0},
        compiler_params=params(),
        cost_estimate=cost(0, 8 * rows * full),
    )(through, after, query_gain, key_gain, own, *got)


def attention_kernel(counts, width, head_size, *refs):
    n_q, n_kv, n_tkv, n_through = counts
    refs = refs[n_through:]
    q_refs, refs = refs[:n_q], refs[n_q:]
    kv_refs, refs = refs[:n_kv], refs[n_kv:]
    tkv_refs, refs = refs[:n_tkv], refs[n_tkv:]
    bias_ref, out_refs = refs[0], refs[1 + n_through :]
    factor = head_size ** (-0.5) * math.log2(math.e)
    bias = bias_ref[...]
    nt = (((1,), (1,)), ((), ()))
    for head in range(width // head_size):
        cols = slice(head * head_size, (head + 1) * head_size)
        vcols = slice(width + head * head_size, width + (head + 1) * head_size)
        keys = jnp.concatenate([r[:, cols] for r in kv_refs], axis=0)
        values = jnp.concatenate([r[:, vcols] for r in kv_refs], axis=0)
        tkeys = jnp.concatenate([r[:, cols] for r in tkv_refs], axis=0)
        tvalues = jnp.concatenate([r[:, vcols] for r in tkv_refs], axis=0)
        for q_ref, out_ref in zip(q_refs, out_refs):
            at = q_ref.shape[1] - width + head * head_size
            q = q_ref[:, at : at + head_size]
            s_img = lax.dot_general(q, keys, nt, preferred_element_type=f32)
            s_txt = lax.dot_general(q, tkeys, nt, preferred_element_type=f32) + bias
            top = jnp.maximum(
                jnp.max(s_img, axis=1, keepdims=True), jnp.max(s_txt, axis=1, keepdims=True)
            )
            p_img = jnp.exp2((s_img - top) * factor)
            p_txt = jnp.exp2((s_txt - top) * factor)
            total = jnp.sum(p_img, axis=1, keepdims=True) + jnp.sum(p_txt, axis=1, keepdims=True)
            acc = jnp.dot(p_img.astype(bf16), values, preferred_element_type=f32)
            acc = acc + jnp.dot(p_txt.astype(bf16), tvalues, preferred_element_type=f32)
            out_ref[:, cols] = (acc / total).astype(bf16)


def attention(through, queries, keyvals, text_keyvals, bias, width, head_size):
    args = tuple(queries) + tuple(keyvals) + tuple(text_keyvals) + (bias,)
    counts = (len(queries), len(keyvals), len(text_keyvals), len(through))
    rows = sum(q.shape[0] for q in queries)
    cols = sum(k.shape[0] for k in keyvals) + sum(k.shape[0] for k in text_keyvals)
    return pl.pallas_call(
        functools.partial(attention_kernel, counts, width, head_size),
        out_shape=[jax.ShapeDtypeStruct(x.shape, x.dtype) for x in through]
        + [jax.ShapeDtypeStruct((q.shape[0], width), bf16) for q in queries],
        in_specs=[ANY] * len(through) + [VMEM] * len(args),
        out_specs=[ANY] * len(through) + [VMEM] * len(queries),
        input_output_aliases={i: i for i in range(len(through))},
        compiler_params=params(),
        cost_estimate=cost(
            4 * rows * cols * width,
            4 * (rows + cols) * width,
            rows * cols * width // head_size,
        ),
    )(*through, *args)


def assemble_kernel(groups, n_after, meta_ref, slots_ref, *refs):
    pieces, (image_ref, text_ref) = refs[:groups], refs[groups + n_after :]
    rows, width = image_ref.shape[0], pieces[0].shape[1]
    for k, piece in enumerate(pieces):
        at = pl.ds(pl.multiple_of((meta_ref[0] ^ k) * width, 128), width)
        image_ref[:, at] = piece[:rows, :]
        text = piece[rows:, :].astype(f32)
        text_ref[:, at] = jnp.where(slots_ref[...] > 0, text, 0.0).astype(bf16)


def assemble(meta, slots, pieces, after):
    groups = len(pieces)
    text_rows = slots.shape[0]
    rows, width = pieces[0].shape
    return pl.pallas_call(
        functools.partial(assemble_kernel, groups, len(after)),
        out_shape=[
            jax.ShapeDtypeStruct((rows - text_rows, groups * width), bf16),
            jax.ShapeDtypeStruct((text_rows, groups * width), bf16),
        ],
        in_specs=[SMEM] + [VMEM] * (1 + groups) + [ANY] * len(after),
        out_specs=[VMEM] * 2,
        compiler_params=params(),
        cost_estimate=cost(0, 4 * rows * groups * width),
    )(meta, slots, *pieces, *after)


def gated_kernel(n_dp, groups, parts, place_of, meta_ref, gate_ref, d_out_ref, w_ref, after_ref, d_attn_ref, *refs):
    del after_ref
    msgs, (w_all, turned, sems) = refs[:n_dp], refs[n_dp:]
    blocks, block = w_all.shape[:2]
    copies = []
    for i in range(blocks):
        rows = pl.ds(i * block, block)
        copies.append(pltpu.make_async_copy(w_ref.at[rows], w_all.at[i], sems.at[i]))
        copies[-1].start()
    gated = (gate_ref[...] * d_out_ref[...].astype(f32)).astype(bf16)
    turned[...] = gated.astype(f32).T
    rows = msgs[0].shape[2]
    z, oc, dp = meta_ref[0], meta_ref[1], meta_ref[2]
    for k, msg in enumerate(msgs):
        for j in range(parts):
            for g in range(groups):
                at = (dp ^ k) * (groups * parts) + place_of(oc ^ j, z ^ g)
                msg[j, g] = turned[pl.ds(pl.multiple_of(at * rows, 8), rows), :].astype(bf16)
    total = jnp.zeros(d_attn_ref.shape, f32)
    for i in range(blocks):
        copies[i].wait()
        total = total + jnp.dot(
            gated[:, i * block : (i + 1) * block], w_all[i], preferred_element_type=f32
        )
    d_attn_ref[...] = total.astype(bf16)


def gated(meta, gate, d_out, out_weight, after, n_dp, groups, parts, place_of):
    local, model = d_out.shape
    inner = out_weight.shape[1]
    rows = model // (n_dp * groups * parts)
    blocks = 6
    shapes = [jax.ShapeDtypeStruct((local, inner), bf16)]
    shapes += [jax.ShapeDtypeStruct((parts, groups, rows, local), bf16)] * n_dp
    return pl.pallas_call(
        functools.partial(gated_kernel, n_dp, groups, parts, place_of),
        out_shape=shapes,
        in_specs=[SMEM, VMEM, VMEM, HBM, ANY],
        out_specs=[VMEM] * (1 + n_dp),
        scratch_shapes=[
            pltpu.VMEM((blocks, model // blocks, inner), bf16),
            pltpu.VMEM((model, local), f32),
            pltpu.SemaphoreType.DMA((blocks,)),
        ],
        compiler_params=params(56),
        cost_estimate=cost(2 * local * inner * model, 2 * inner * model),
    )(meta, gate, d_out, out_weight, after)


def gather_kernel(n_dp, *refs):
    pieces, outs = refs[:n_dp], refs[n_dp:]
    for j, out in enumerate(outs):
        for k, piece in enumerate(pieces):
            out[k] = piece[j + 1]


def gather_parts(pieces):
    parts = pieces[0].shape[0]
    shape = (len(pieces),) + pieces[0].shape[1:]
    return pl.pallas_call(
        functools.partial(gather_kernel, len(pieces)),
        out_shape=[jax.ShapeDtypeStruct(shape, bf16)] * (parts - 1),
        in_specs=[VMEM] * len(pieces),
        out_specs=[VMEM] * (parts - 1),
        compiler_params=params(),
        cost_estimate=cost(0, 4 * math.prod(shape) * (parts - 1)),
    )(*pieces)


def project_kernel(groups, parts, place_of, meta_ref, attn_ref, w_ref, gate_ref, d_out_ref, after_ref, out_ref, *refs):
    del after_ref
    terms, (w_all, by_place, sems) = refs[:parts], refs[parts:]
    blocks, block = w_all.shape[:2]
    copies = []
    for i in range(blocks):
        rows = pl.ds(i * block, block)
        copies.append(pltpu.make_async_copy(w_ref.at[rows], w_all.at[i], sems.at[i]))
        copies[-1].start()
    sums = []
    for i in range(blocks):
        copies[i].wait()
        cols = slice(i * block, (i + 1) * block)
        got = lax.dot_general(
            attn_ref[...], w_all[i], (((1,), (1,)), ((), ())), preferred_element_type=f32
        )
        out_ref[:, cols] = (got * gate_ref[:, cols]).astype(bf16)
        sums.append(jnp.sum(got * d_out_ref[:, cols].astype(f32), axis=0, keepdims=True))
    sums = jnp.concatenate(sums, axis=1)
    places, width = by_place.shape
    for s in range(places):
        by_place[s : s + 1, :] = sums[:, s * width : (s + 1) * width]
    for j, term in enumerate(terms):
        for g in range(groups):
            at = place_of(meta_ref[1] ^ j, meta_ref[0] ^ g)
            term[g : g + 1, :] = by_place[pl.ds(at, 1), :]


def project(meta, attn, out_weight, gate, d_out, after, groups, parts, place_of):
    rows, inner = attn.shape
    model = out_weight.shape[0]
    blocks = 6
    width = model // (groups * parts)
    shapes = [jax.ShapeDtypeStruct((rows, model), bf16)]
    shapes += [jax.ShapeDtypeStruct((groups, width), f32)] * parts
    return pl.pallas_call(
        functools.partial(project_kernel, groups, parts, place_of),
        out_shape=shapes,
        in_specs=[SMEM, VMEM, HBM, VMEM, VMEM, ANY],
        out_specs=[VMEM] * (1 + parts),
        scratch_shapes=[
            pltpu.VMEM((blocks, model // blocks, inner), bf16),
            pltpu.VMEM((groups * parts, width), f32),
            pltpu.SemaphoreType.DMA((blocks,)),
        ],
        compiler_params=params(56),
        cost_estimate=cost(2 * rows * inner * model, 2 * inner * model),
    )(meta, attn, out_weight, gate, d_out, after)


def gate_kernel(n_got, *refs):
    total = refs[0][...]
    for ref in refs[1 : 1 + n_got]:
        total = total + ref[...]
    for g, out in enumerate(refs[1 + n_got :]):
        out[...] = total[g : g + 1]


def gate_sum(own, got):
    groups, width = own.shape
    return pl.pallas_call(
        functools.partial(gate_kernel, len(got)),
        out_shape=[jax.ShapeDtypeStruct((1, width), f32)] * groups,
        in_specs=[VMEM] * (1 + len(got)),
        out_specs=[VMEM] * groups,
        compiler_params=params(),
        cost_estimate=cost(0, 8 * groups * width),
    )(own, *got)


def grad_kernel(n_left, n_pieces, *refs):
    lefts, pieces, outs = refs[:n_left], refs[n_left : n_left + n_pieces], refs[n_left + n_pieces :]
    rows, width = outs[0].shape
    total = rows * len(outs)
    left = []
    for ref in lefts:
        left += [ref[i].reshape(total, -1) for i in range(ref.shape[0])]
    left = jnp.concatenate(left, axis=1)
    block = 256
    for start in range(0, width, block):
        cols = slice(start, start + block)
        right = jnp.concatenate([p[:, cols] for p in pieces], axis=0)
        got = jnp.dot(left, right, preferred_element_type=f32)
        for g, out in enumerate(outs):
            out[:, cols] = got[g * rows : (g + 1) * rows].astype(out.dtype)


def grad_product(lefts, pieces):
    groups, rows = lefts[0].shape[1:3]
    depth = pieces[0].shape[0] * len(pieces)
    width = pieces[0].shape[1]
    total = groups * rows
    shapes = [jax.ShapeDtypeStruct((rows, width), f32)]
    shapes += [jax.ShapeDtypeStruct((rows, width), bf16)] * (groups - 1)
    return pl.pallas_call(
        functools.partial(grad_kernel, len(lefts), len(pieces)),
        out_shape=shapes,
        in_specs=[VMEM] * (len(lefts) + len(pieces)),
        out_specs=[VMEM] * groups,
        compiler_params=params(),
        cost_estimate=cost(
            2 * total * depth * width, 2 * (total * depth + depth * width + total * width)
        ),
    )(*lefts, *pieces)


def on_device(
    caption_states,
    caption_gain,
    text_proj,
    caption_len,
    slot_source,
    query_gain,
    key_gain,
    image_q,
    image_k,
    image_v,
    out_weight,
    gate,
    d_out,
):
    n_dp = lax.axis_size("dp")
    n_seq = lax.axis_size("seq")
    G, C = GROUPS, CORES
    O = n_seq // (G * C)
    OC = O * C
    dp = lax.axis_index("dp")
    seq = lax.axis_index("seq")
    z = (seq // C) % G
    oc = (seq // (G * C)) * C + seq % C

    def place(oc_at, z_at):
        return ((oc_at // C) * G + z_at) * C + oc_at % C

    def to_z(x, k):
        perm = [(place(a, b), place(a, b ^ k)) for a in range(OC) for b in range(G)]
        return lax.ppermute(x, "seq", perm)

    def to_oc(x, j):
        perm = [(place(a, b), place(a ^ j, b)) for a in range(OC) for b in range(G)]
        return lax.ppermute(x, "seq", perm)

    def to_dp(x, k):
        return lax.ppermute(x, "dp", [(a, a ^ k) for a in range(n_dp)])

    def part(x, index, size, axis):
        return lax.dynamic_slice_in_dim(x, index * size, size, axis)

    slot_total = slot_source.shape[1]
    slot_local = slot_total // n_seq
    image_local = image_q.shape[1]
    inner_width = image_q.shape[2]
    model_width = out_weight.shape[0]
    head_size = query_gain.shape[0]
    gw = inner_width // G
    order = [2, 3, 1]
    meta = jnp.stack([z, oc, dp]).astype(jnp.int32)

    bias, *both = text_project(
        meta, caption_len, slot_source, caption_states[0], caption_gain[None], text_proj,
        image_k[0], image_v[0], image_q[0], G, OC, place,
    )
    packed, partials = both[:G], both[G:]
    qkv = {k: to_z(packed[k], k) for k in order}
    sums = text_sum(partials[0], [to_oc(partials[j], j) for j in range(1, OC)])
    d_attn, *gg = gated(meta, gate, d_out[0], out_weight, sums[0], n_dp, G, OC, place)
    got = [to_z(sums[k], k) for k in order]
    qkv[0], text_q, text_kv = text_norm(
        packed[0], d_attn, query_gain[None], key_gain[None], sums[0], got, DT5
    )
    text_kvs = [text_kv] + [to_oc(text_kv, j) for j in range(1, OC)]
    kv_pieces = [qkv[k] for k in range(G)]
    for j in range(1, OC):
        kv_pieces += [to_oc(qkv[k], j) for k in range(G)]

    queries = [text_q] + [qkv[k] for k in range(G)]
    found = list(attention(gg[1:], queries, kv_pieces, text_kvs, bias, gw, head_size))
    gg, text_out, outs = gg[:1] + found[: n_dp - 1], found[n_dp - 1], found[n_dp:]
    gg_dp = [gg[0]] + [to_dp(gg[k], k) for k in range(1, n_dp)]
    lefts = [g[:1] for g in gg_dp]
    lefts += [to_oc(g, j + 1) for j, g in enumerate(gather_parts(gg_dp))]

    back = []
    for k in range(G):
        rows = jnp.concatenate([outs[k], part(text_out, z ^ k, slot_local, 0)], axis=0)
        back.append(to_z(rows, k) if k else rows)
    own_slots = part(slot_source[0] < caption_len[0], seq, slot_local, 0)
    image_attn, text_attn = assemble(
        meta, own_slots.astype(jnp.int32)[:, None], back, gg_dp[1:]
    )

    attn_dp = [image_attn] + [to_dp(image_attn, k) for k in range(1, n_dp)]
    attn_pieces = list(attn_dp)
    for j in range(1, OC):
        attn_pieces += [to_oc(p, j) for p in attn_dp]

    grads = grad_product(lefts, attn_pieces)
    grad_wo = grads[0]
    for k in order:
        grad_wo = grad_wo + to_z(grads[k], k).astype(f32)

    image_out, *terms = project(
        meta, image_attn, out_weight, gate, d_out[0], grads[0], G, OC, place
    )
    terms = gate_sum(terms[0], [to_oc(terms[j], j) for j in range(1, OC)])
    grad_gate = terms[0]
    for k in order:
        grad_gate = grad_gate + to_z(terms[k], k)
    return (image_out[None], text_attn[None], d_attn[None], grad_wo, grad_gate)


def solution(mesh):
    in_specs = (
        P("dp", None, "seq"),
        P("seq"),
        P("seq", None),
        P("dp"),
        P("dp", None),
        P(),
        P(),
        P("dp", "seq", None),
        P("dp", "seq", None),
        P("dp", "seq", None),
        P(),
        P("dp", None),
        P("dp", "seq", None),
    )
    out_specs = (
        P("dp", "seq", None),
        P("dp", "seq", None),
        P("dp", "seq", None),
        P(("dp", "seq"), None),
        P("dp", "seq"),
    )
    return jax.shard_map(
        on_device, mesh=mesh, in_specs=in_specs, out_specs=out_specs, check_vma=False
    )
```

time: 147 us -> 132 us (0.90); the launches traced: 144 us -> 132 us
  local copies, waits for them, and re-layouts: 35.9 us -> 7.18 us
  waiting for transfers between devices: 35.2 us -> 60.6 us
  Pallas kernels: 21.2 us -> 28.7 us
  other arithmetic: 9.14 us -> 2.24 us
  matrix products: 5.09 us -> 0 us
  starting transfers between devices: 35.8 us -> 31.4 us
    ppermute x15, waiting for transfers between devices: 27.3 us -> 40.5 us  [to_z(): return lax.ppermute(x, 'seq', perm)]
    unnamed x52 -> x34, local copies, waits for them, and re-layouts: 17.9 us -> 7.05 us
    pallas_call x5 -> x8, Pallas kernels: 13.1 us -> 22.7 us  [the longest x1 7.51 us: project(): pl.pallas_call(functools.partial(project_kernel, groups, parts, place_of)...]
    ppermute x6, waiting for transfers between devices: 7.92 us -> 16.1 us  [to_dp(): return lax.ppermute(x, 'dp', [(a, a ^ k) for a in range(n_dp)])]
    dynamic_slice x4 -> x0, local copies, waits for them, and re-layouts: 5.88 us -> none  [on_device(): lax.dynamic_index_in_dim(g, oc ^ j, 0, keepdims=False)]
    dot_general x1 -> x0, matrix products: 5.09 us -> none  [on_device(): jnp.dot(gated_grad, out_weight, preferred_element_type=f32).astype(bf16)]
    ppermute x15, starting transfers between devices: 26.1 us -> 21.6 us  [to_z(): return lax.ppermute(x, 'seq', perm)]
    ppermute x12, waiting for transfers between devices: 0.03 us -> 4.09 us  [to_oc(): return lax.ppermute(x, 'seq', perm)]
  transfers between devices with their start and end apart: 33 -> 33, of which waited for: 7 -> 15; matrix products, arithmetic and copies ran while one was open for 25% -> 1% of each run, Pallas kernels for 12% -> 11%
where the time goes in v4:
time: 132 us
  waiting for transfers between devices  60.6 us (46%)
  starting transfers between devices  31.4 us (24%)
  Pallas kernels  28.7 us (22%)
  local copies, waits for them, and re-layouts  7.18 us (5%)
  other arithmetic  2.24 us (2%)
  between operations  1.63 us (1%)
    ppermute x15, waiting for transfers between devices, to_z(): return lax.ppermute(x, 'seq', perm)  40.5 us
    ppermute x15, starting transfers between devices, to_z(): return lax.ppermute(x, 'seq', perm)  21.6 us
    ppermute x6, waiting for transfers between devices, to_dp(): return lax.ppermute(x, 'dp', [(a, a ^ k) for a in range(n_dp)])  16.1 us
    pallas_call x1, Pallas kernels, project(): pl.pallas_call(functools.partial(project_kernel, groups, parts, place_of)...  7.51 us
    unnamed x34, local copies, waits for them, and re-layouts  7.05 us
    ppermute x6, starting transfers between devices, to_dp(): return lax.ppermute(x, 'dp', [(a, a ^ k) for a in range(n_dp)])  6.98 us
    pallas_call x1, Pallas kernels, gated(): pl.pallas_call(functools.partial(gated_kernel, n_dp, groups, parts, place...  6.16 us
    pallas_call x1, Pallas kernels, text_project(): pl.pallas_call(functools.partial(text_kernel, groups, place_of), out_shap...  6.15 us
  transfers between devices with their start and end apart: 33, of which 15 were waited for; matrix products, arithmetic and copies ran while one was open for 1% of the time, Pallas kernels for 11%

profile of v4, /device:TPU:0, one launch (start us, length us, event | category | flops | bytes accessed | tf_op | source)
XLA Modules:
  0.0 131.8 jit_solution(11470904026686756233)
XLA Ops:
  1.4 0.6 pad_add_fusion.meta_ref
  2.0 6.2 %shard_map.164 = (f32[1,64]{1,0:T(1,128)}, bf16[128,1152]{1,0:T(8,128)(2,1)}, bf16[128,1152]{1,0:T(8,128)(2,1)}, bf16[128,1152]{1,0:T(8,128)(2,1)}, bf16[128,115...) custom-call(s32[3]{0:T(128)} %pad_add_fusion.meta_ref, s32[1]{0:T(128)} %copy.27.len_ref, ...), custom_call_target="tpu_custom_call" | custom-call | flops 301989888 | bytes 4718592 | tf_op jit(solution)/shard_map/pallas_call | solution.py:107
  8.7 2.6 %collective-permute-start.4 = (bf16[128,1152]{1,0:T(8,128)(2,1)}, bf16[128,1152]{1,0:T(8,128)(2,1)S(1)}, u32[]{:S(2)}, u32[]{:S(2)}) collective-permute-start(bf16[128,1152]{1,0:T(8,128)(2,1)} %get-tuple-element.58), channel_id=1, source_target_pairs={{0,2},{2,0},{4,6},{6,4},{1,3},{3,1},{5,7},{7,5},{8,10},{10,8},{12,... | collective-permute-start | bytes 884744 | tf_op jit(solution)/shard_map/ppermute | solution.py:471
  11.3 2.6 %collective-permute-start.5 = (bf16[128,1152]{1,0:T(8,128)(2,1)}, bf16[128,1152]{1,0:T(8,128)(2,1)S(1)}, u32[]{:S(2)}, u32[]{:S(2)}) collective-permute-start(bf16[128,1152]{1,0:T(8,128)(2,1)} %get-tuple-element.59), channel_id=1, source_target_pairs={{0,4},{2,6},{4,0},{6,2},{1,5},{3,7},{5,1},{7,3},{8,12},{10,14},{12... | collective-permute-start | bytes 884744 | tf_op jit(solution)/shard_map/ppermute | solution.py:471
  13.9 1.1 copy-done.3
  15.2 0.7 copy-done.4
  15.9 1.9 %collective-permute-start.1 = (bf16[32,1280]{1,0:T(8,128)(2,1)S(1)}, bf16[32,1280]{1,0:T(8,128)(2,1)S(1)}, u32[]{:S(2)}, u32[]{:S(2)}) collective-permute-start(bf16[32,1280]{1,0:T(8,128)(2,1)S(1)} %get-tuple-element.53), channel_id=1, source_target_pairs={{0,4},{2,6},{4,0},{6,2},{1,5},{3,7},{5,1},{7,3},{8,12},{10,14},{12... | collective-permute-start | bytes 245768 | tf_op jit(solution)/shard_map/ppermute | solution.py:471
  17.8 1.9 %collective-permute-start.2 = (bf16[32,1280]{1,0:T(8,128)(2,1)S(1)}, bf16[32,1280]{1,0:T(8,128)(2,1)S(1)}, u32[]{:S(2)}, u32[]{:S(2)}) collective-permute-start(bf16[32,1280]{1,0:T(8,128)(2,1)S(1)} %get-tuple-element.54), channel_id=1, source_target_pairs={{0,6},{2,4},{4,2},{6,0},{1,7},{3,5},{5,3},{7,1},{8,14},{10,12},{12... | collective-permute-start | bytes 245768 | tf_op jit(solution)/shard_map/ppermute | solution.py:471
  19.7 5.3 %collective-permute-done.4.refs_5_.refs_9_ = bf16[128,1152]{1,0:T(8,128)(2,1)S(1)} collective-permute-done((bf16[128,1152]{1,0:T(8,128)(2,1)}, bf16[128,1152]{1,0:T(8,128)(2,1)S(1)}, u32[]{:S(2)}, u32[]{:S(2)}) %collective-permute-start.4) | collective-permute-done | bytes 294944 | tf_op jit(solution)/shard_map/ppermute | solution.py:471
  25.0 6.2 %shard_map.166 = (bf16[128,1536]{1,0:T(8,128)(2,1)}, bf16[2,4,96,128]{3,2,1,0:T(8,128)(2,1)}, bf16[2,4,96,128]{3,2,1,0:T(8,128)(2,1)}, bf16[2,4,96,128]{3,2,1,0:T(8,128)(2,1)}, bf16[2,4,96,128]{3,2,1,0:T(8,128)(2,1)}) custom-call(s32[3]{0:T(128)} %pad_add_fusion.meta_ref, f32[1,3072]{1,0:T(1,128)} %gate_ref.3, bf16[128,3072]{1,0:T(8,128)(2,1)} %bitcast.21, ...), custom_call_target="tpu_custom_call" | custom-call | flops 1207959552 | bytes 9437184 | tf_op jit(solution)/shard_map/pallas_call | solution.py:300
  31.2 7.3 %collective-permute-done.5.refs_6_.refs_10_ = bf16[128,1152]{1,0:T(8,128)(2,1)S(1)} collective-permute-done((bf16[128,1152]{1,0:T(8,128)(2,1)}, bf16[128,1152]{1,0:T(8,128)(2,1)S(1)}, u32[]{:S(2)}, u32[]{:S(2)}) %collective-permute-start.5) | collective-permute-done | bytes 294944 | tf_op jit(solution)/shard_map/ppermute | solution.py:471
  39.0 7.6 %collective-permute-done.1.refs_0_ = bf16[32,1280]{1,0:T(8,128)(2,1)S(1)} collective-permute-done((bf16[32,1280]{1,0:T(8,128)(2,1)S(1)}, bf16[32,1280]{1,0:T(8,128)(2,1)S(1)}, u32[]{:S(2)}, u32[]{:S(2)}) %collective-permute-start.1) | collective-permute-done | bytes 81952 | tf_op jit(solution)/shard_map/ppermute | solution.py:471
  46.7 1.0 copy-done.8
  48.7 1.0 collective-permute-done.11.refs_17_
  49.8 0.9 copy-done.9
  50.7 0.9 copy-done.10
  51.6 5.7 %shard_map.168 = (bf16[2,4,96,128]{3,2,1,0:T(8,128)(2,1)}, bf16[2,4,96,128]{3,2,1,0:T(8,128)(2,1)S(1)}, bf16[2,4,96,128]{3,2,1,0:T(8,128)(2,1)S(1)}, bf16[32,384...) custom-call(bf16[2,4,96,128]{3,2,1,0:T(8,128)(2,1)} %get-tuple-eleme, ...), custom_call_target="tpu_custom_call", output_to_operand_aliasing={{0}: (0, {}), {1}: (1, {}), {2}: (2, {})} | custom-call | flops 909115392 | bytes 2506752 | tf_op jit(solution)/shard_map/pallas_call | solution.py:223
  57.4 1.5 %collective-permute-start.12 = (bf16[136,384]{1,0:T(8,128)(2,1)S(1)}, bf16[136,384]{1,0:T(8,128)(2,1)S(1)}, u32[]{:S(2)}, u32[]{:S(2)}) collective-permute-start(bf16[136,384]{1,0:T(8,128)(2,1)S(1)} %pad_maximum_fusion.1), channel_id=1, source_target_pairs={{0,2},{2,0},{4,6},{6,4},{1,3},{3,1},{5,7},{7,5},{8,10},{10,8},{12,... | collective-permute-start | bytes 313352 | tf_op jit(solution)/shard_map/ppermute | solution.py:471
  58.9 1.7 %collective-permute-start.13 = (bf16[136,384]{1,0:T(8,128)(2,1)S(1)}, bf16[136,384]{1,0:T(8,128)(2,1)S(1)}, u32[]{:S(2)}, u32[]{:S(2)}) collective-permute-start(bf16[136,384]{1,0:T(8,128)(2,1)S(1)} %pad_maximum_fusion.2), channel_id=1, source_target_pairs={{0,4},{2,6},{4,0},{6,2},{1,5},{3,7},{5,1},{7,3},{8,12},{10,14},{12... | collective-permute-start | bytes 313352 | tf_op jit(solution)/shard_map/ppermute | solution.py:471
  60.6 1.5 %collective-permute-start.15 = (bf16[2,4,96,128]{3,2,1,0:T(8,128)(2,1)}, bf16[2,4,96,128]{3,2,1,0:T(8,128)(2,1)S(1)}, u32[]{:S(2)}, u32[]{:S(2)}) collective-permute-start(bf16[2,4,96,128]{3,2,1,0:T(8,128)(2,1)} %get-tuple-element.68), channel_id=1, source_target_pairs={{0,8},{8,0},{16,24},{24,16},{1,9},{9,1},{17,25},{25,17},{2,10},{10... | collective-permute-start | bytes 589832 | tf_op jit(solution)/shard_map/ppermute | solution.py:478
  62.1 1.5 %collective-permute-start.16 = (bf16[2,4,96,128]{3,2,1,0:T(8,128)(2,1)S(1)}, bf16[2,4,96,128]{3,2,1,0:T(8,128)(2,1)S(1)}, u32[]{:S(2)}, u32[]{:S(2)}) collective-permute-start(bf16[2,4,96,128]{3,2,1,0:T(8,128)(2,1)S(1)} %get-tuple-element.69), channel_id=1, source_target_pairs={{0,16},{8,24},{16,0},{24,8},{1,17},{9,25},{17,1},{25,9},{2,18},{10... | collective-permute-start | bytes 589832 | tf_op jit(solution)/shard_map/ppermute | solution.py:478
  64.2 1.7 %collective-permute-start.14 = (bf16[136,384]{1,0:T(8,128)(2,1)S(1)}, bf16[136,384]{1,0:T(8,128)(2,1)S(1)}, u32[]{:S(2)}, u32[]{:S(2)}) collective-permute-start(bf16[136,384]{1,0:T(8,128)(2,1)S(1)} %pad_maximum_fusion.3), channel_id=1, source_target_pairs={{0,6},{2,4},{4,2},{6,0},{1,7},{3,5},{5,3},{7,1},{8,14},{10,12},{12... | collective-permute-start | bytes 313352 | tf_op jit(solution)/shard_map/ppermute | solution.py:471
  65.9 1.1 collective-permute-done.13.refs_2_
  67.0 3.8 %collective-permute-done.14.refs_3_ = bf16[136,384]{1,0:T(8,128)(2,1)S(1)} collective-permute-done((bf16[136,384]{1,0:T(8,128)(2,1)S(1)}, bf16[136,384]{1,0:T(8,128)(2,1)S(1)}, u32[]{:S(2)}, u32[]{:S(2)}) %collective-permute-start.14) | collective-permute-done | bytes 104480 | tf_op jit(solution)/shard_map/ppermute | solution.py:471
  70.8 0.9 collective-permute-done.16.refs_5_.refs_2_
  71.7 1.0 collective-permute-done.17.refs_6_.refs_3_
  72.7 1.2 shard_map.169
  73.9 1.5 %collective-permute-start.21 = (bf16[128,1536]{1,0:T(8,128)(2,1)S(1)}, bf16[128,1536]{1,0:T(8,128)(2,1)S(1)}, u32[]{:S(2)}, u32[]{:S(2)}) collective-permute-start(bf16[128,1536]{1,0:T(8,128)(2,1)S(1)} %get-tuple-element.71.refs_5_.attn_ref), channel_id=1, source_target_pairs={{0,24},{8,16},{16,8},{24,0},{1,25},{9,17},{17,9},{25,1},{2,26},{10... | collective-permute-start | bytes 1179656 | tf_op jit(solution)/shard_map/ppermute | solution.py:478
  75.4 1.4 %collective-permute-start.20 = (bf16[128,1536]{1,0:T(8,128)(2,1)S(1)}, bf16[128,1536]{1,0:T(8,128)(2,1)S(1)}, u32[]{:S(2)}, u32[]{:S(2)}) collective-permute-start(bf16[128,1536]{1,0:T(8,128)(2,1)S(1)} %get-tuple-element.71.refs_5_.attn_ref), channel_id=1, source_target_pairs={{0,16},{8,24},{16,0},{24,8},{1,17},{9,25},{17,1},{25,9},{2,18},{10... | collective-permute-start | bytes 1179656 | tf_op jit(solution)/shard_map/ppermute | solution.py:478
  76.8 0.6 collective-permute-start.19
  77.4 0.9 copy-done.6
  78.3 0.6 collective-permute-start.18
  78.9 7.9 %collective-permute-done.21.refs_8_ = bf16[128,1536]{1,0:T(8,128)(2,1)S(1)} collective-permute-done((bf16[128,1536]{1,0:T(8,128)(2,1)S(1)}, bf16[128,1536]{1,0:T(8,128)(2,1)S(1)}, u32[]{:S(2)}, u32[]{:S(2)}) %collective-permute-start.21) | collective-permute-done | bytes 393248 | tf_op jit(solution)/shard_map/ppermute | solution.py:478
  86.8 6.3 %collective-permute-done.20.refs_7_ = bf16[128,1536]{1,0:T(8,128)(2,1)S(1)} collective-permute-done((bf16[128,1536]{1,0:T(8,128)(2,1)S(1)}, bf16[128,1536]{1,0:T(8,128)(2,1)S(1)}, u32[]{:S(2)}, u32[]{:S(2)}) %collective-permute-start.20) | collective-permute-done | bytes 393248 | tf_op jit(solution)/shard_map/ppermute | solution.py:478
  93.7 1.1 collective-permute-done.24.refs_11_
  95.4 1.4 %shard_map.171 = (f32[96,1536]{1,0:T(8,128)S(1)}, bf16[96,1536]{1,0:T(8,128)(2,1)S(1)}, bf16[96,1536]{1,0:T(8,128)(2,1)S(1)}, bf16[96,1536]{1,0:T(8,128)(2,1)S(1)}) custom-call(bf16[1,4,96,128]{3,2,1,0:T(8,128)(2,1)S(1)} %slice.12.refs_0_, bf16[1,4,96,128]{3,2,1,0:T(8,128)(2,1)S(1)} %slice.16.refs_1_, bf16[1,4,96,128]{3,2,1,0:T(8,128)(2,1)S(1)} %slice.17.refs_2_, ...), custom_call_target="tpu_custom_call" | custom-call | flops 1207959552 | bytes 5111808 | tf_op jit(solution)/shard_map/pallas_call | solution.py:429
  96.8 0.8 copy-done.1
  97.6 0.8 collective-permute-start.26
  98.4 2.5 %collective-permute-start.27 = (bf16[96,1536]{1,0:T(8,128)(2,1)S(1)}, bf16[96,1536]{1,0:T(8,128)(2,1)S(1)}, u32[]{:S(2)}, u32[]{:S(2)}) collective-permute-start(bf16[96,1536]{1,0:T(8,128)(2,1)S(1)} %get-tuple-element.77), channel_id=1, source_target_pairs={{0,6},{2,4},{4,2},{6,0},{1,7},{3,5},{5,3},{7,1},{8,14},{10,12},{12... | collective-permute-start | bytes 884744 | tf_op jit(solution)/shard_map/ppermute | solution.py:471
  101.1 7.5 %shard_map.172 = (bf16[128,3072]{1,0:T(8,128)(2,1)}, f32[4,384]{1,0:T(4,128)}, f32[4,384]{1,0:T(4,128)}) custom-call(s32[3]{0:T(128)} %pad_add_fusion.meta_ref, bf16[128,1536]{1,0:T(8,128)(2,1)} %copy-done.7, bf16[3072,1536]{1,0:T(8,128)(2,1)} %w_ref.5, f32[1,3072]{1,0:T(1,128)} %gate_ref.3, bf16[128,3072]{1,0:T(8,128)(2,1)} %bitcast.22, f32[96,1536]{1,0:T(8,128)} %copy-done.1), custom_call_target="tpu_custom_call" | custom-call | flops 1207959552 | bytes 9437184 | tf_op jit(solution)/shard_map/pallas_call | solution.py:370
  108.7 1.4 %collective-permute-done.29.refs_1_ = f32[4,384]{1,0:T(4,128)S(1)} collective-permute-done((f32[4,384]{1,0:T(4,128)}, f32[4,384]{1,0:T(4,128)S(1)}, u32[]{:S(2)}, u32[]{:S(2)}) %collective-permute-start.29) | collective-permute-done | bytes 6176 | tf_op jit(solution)/shard_map/ppermute | solution.py:475
  110.1 0.7 copy-done.12
  110.8 1.7 %collective-permute-start.30 = (f32[1,384]{1,0:T(1,128)S(1)}, f32[1,384]{1,0:T(1,128)S(1)}, u32[]{:S(2)}, u32[]{:S(2)}) collective-permute-start(f32[1,384]{1,0:T(1,128)S(1)} %get-tuple-element.82), channel_id=1, source_target_pairs={{0,4},{2,6},{4,0},{6,2},{1,5},{3,7},{5,1},{7,3},{8,12},{10,14},{12... | collective-permute-start | bytes 4616 | tf_op jit(solution)/shard_map/ppermute | solution.py:471
  112.4 2.5 %collective-permute-start.31 = (f32[1,384]{1,0:T(1,128)S(1)}, f32[1,384]{1,0:T(1,128)S(1)}, u32[]{:S(2)}, u32[]{:S(2)}) collective-permute-start(f32[1,384]{1,0:T(1,128)S(1)} %get-tuple-element.83), channel_id=1, source_target_pairs={{0,6},{2,4},{4,2},{6,0},{1,7},{3,5},{5,3},{7,1},{8,14},{10,12},{12... | collective-permute-start | bytes 4616 | tf_op jit(solution)/shard_map/ppermute | solution.py:471
  114.9 11.7 %collective-permute-done.30 = f32[1,384]{1,0:T(1,128)S(1)} collective-permute-done((f32[1,384]{1,0:T(1,128)S(1)}, f32[1,384]{1,0:T(1,128)S(1)}, u32[]{:S(2)}, u32[]{:S(2)}) %collective-permute-start.30) | collective-permute-done | bytes 1568 | tf_op jit(solution)/shard_map/ppermute | solution.py:471
  126.7 3.6 %collective-permute-done.32 = f32[1,384]{1,0:T(1,128)S(1)} collective-permute-done((f32[1,384]{1,0:T(1,128)S(1)}, f32[1,384]{1,0:T(1,128)S(1)}, u32[]{:S(2)}, u32[]{:S(2)}) %collective-permute-start.32) | collective-permute-done | bytes 1568 | tf_op jit(solution)/shard_map/ppermute | solution.py:471
  130.2 0.6 add_add_fusion
  130.8 0.9 convert_add_fusion
  (77 shorter events, 4.4 us)
Async XLA Ops:
  0.6 47.8 %copy-start.16 = (s32[1,64]{1,0:T(1,128)S(1)}, s32[1,64]{1,0:T(1,128)}, u32[]{:S(2)}) copy-start(s32[1,64]{1,0:T(1,128)} %src_ref.1) | copy-start | bytes 772
  0.6 46.0 %copy-start.14 = (f32[128]{0:T(128)S(1)}, f32[128]{0:T(128)}, u32[]{:S(2)}) copy-start(f32[128]{0:T(128)} %param.19) | copy-start | bytes 1540
  0.7 46.0 %copy-start.13 = (f32[128]{0:T(128)S(1)}, f32[128]{0:T(128)}, u32[]{:S(2)}) copy-start(f32[128]{0:T(128)} %param.18) | copy-start | bytes 1540
  2.0 70.7 %copy-start.11 = (s32[3]{0:T(128)S(1)}, s32[3]{0:T(128)}, u32[]{:S(2)}) copy-start(s32[3]{0:T(128)} %pad_add_fusion.meta_ref) | copy-start | bytes 40
  8.1 38.5 %copy-start = (bf16[128,1152]{1,0:T(8,128)(2,1)S(1)}, bf16[128,1152]{1,0:T(8,128)(2,1)}, u32[]{:S(2)}) copy-start(bf16[128,1152]{1,0:T(8,128)(2,1)} %get-tuple-element.51.through_ref) | copy-start | bytes 884740
  8.1 5.8 %collective-permute-start = (bf16[4,32,1280]{2,1,0:T(8,128)(2,1)}, bf16[4,32,1280]{2,1,0:T(8,128)(2,1)S(1)}, u32[]{:S(2)}, u32[]{:S(2)}) collective-permute-start(bf16[4,32,1280]{2,1,0:T(8,128)(2,1)} %get-tuple-element.46), channel_id=1, source_target_pairs={{0,1},{2,3},{4,5},{6,7},{1,0},{3,2},{5,4},{7,6},{8,9},{10,11},{12,... | collective-permute-start | bytes 983048 | tf_op jit(solution)/shard_map/ppermute | solution.py:475
  8.7 16.3 %collective-permute-start.4 = (bf16[128,1152]{1,0:T(8,128)(2,1)}, bf16[128,1152]{1,0:T(8,128)(2,1)S(1)}, u32[]{:S(2)}, u32[]{:S(2)}) collective-permute-start(bf16[128,1152]{1,0:T(8,128)(2,1)} %get-tuple-element.58), channel_id=1, source_target_pairs={{0,2},{2,0},{4,6},{6,4},{1,3},{3,1},{5,7},{7,5},{8,10},{10,8},{12,... | collective-permute-start | bytes 884744 | tf_op jit(solution)/shard_map/ppermute | solution.py:471
  11.3 27.2 %collective-permute-start.5 = (bf16[128,1152]{1,0:T(8,128)(2,1)}, bf16[128,1152]{1,0:T(8,128)(2,1)S(1)}, u32[]{:S(2)}, u32[]{:S(2)}) collective-permute-start(bf16[128,1152]{1,0:T(8,128)(2,1)} %get-tuple-element.59), channel_id=1, source_target_pairs={{0,4},{2,6},{4,0},{6,2},{1,5},{3,7},{5,1},{7,3},{8,12},{10,14},{12... | collective-permute-start | bytes 884744 | tf_op jit(solution)/shard_map/ppermute | solution.py:471
  13.9 24.6 %collective-permute-start.6 = (bf16[128,1152]{1,0:T(8,128)(2,1)}, bf16[128,1152]{1,0:T(8,128)(2,1)S(1)}, u32[]{:S(2)}, u32[]{:S(2)}) collective-permute-start(bf16[128,1152]{1,0:T(8,128)(2,1)} %get-tuple-element.60), channel_id=1, source_target_pairs={{0,6},{2,4},{4,2},{6,0},{1,7},{3,5},{5,3},{7,1},{8,14},{10,12},{12... | collective-permute-start | bytes 884744 | tf_op jit(solution)/shard_map/ppermute | solution.py:471
  13.9 1.1 copy-start.3
  15.0 34.8 %copy-start.15 = (f32[1,64]{1,0:T(1,128)S(1)}, f32[1,64]{1,0:T(1,128)}, u32[]{:S(2)}) copy-start(f32[1,64]{1,0:T(1,128)} %get-tuple-element.62.refs_18_) | copy-start | bytes 772
  15.9 30.8 %copy-start.5 = (f32[32,1280]{1,0:T(8,128)S(1)}, f32[32,1280]{1,0:T(8,128)}, u32[]{:S(2)}) copy-start(f32[32,1280]{1,0:T(8,128)} %copy-done.4) | copy-start | bytes 491524
  15.9 30.7 %collective-permute-start.1 = (bf16[32,1280]{1,0:T(8,128)(2,1)S(1)}, bf16[32,1280]{1,0:T(8,128)(2,1)S(1)}, u32[]{:S(2)}, u32[]{:S(2)}) collective-permute-start(bf16[32,1280]{1,0:T(8,128)(2,1)S(1)} %get-tuple-element.53), channel_id=1, source_target_pairs={{0,4},{2,6},{4,0},{6,2},{1,5},{3,7},{5,1},{7,3},{8,12},{10,14},{12... | collective-permute-start | bytes 245768 | tf_op jit(solution)/shard_map/ppermute | solution.py:471
  17.8 28.8 %collective-permute-start.2 = (bf16[32,1280]{1,0:T(8,128)(2,1)S(1)}, bf16[32,1280]{1,0:T(8,128)(2,1)S(1)}, u32[]{:S(2)}, u32[]{:S(2)}) collective-permute-start(bf16[32,1280]{1,0:T(8,128)(2,1)S(1)} %get-tuple-element.54), channel_id=1, source_target_pairs={{0,6},{2,4},{4,2},{6,0},{1,7},{3,5},{5,3},{7,1},{8,14},{10,12},{12... | collective-permute-start | bytes 245768 | tf_op jit(solution)/shard_map/ppermute | solution.py:471
  25.0 21.6 %collective-permute-start.3 = (bf16[32,1280]{1,0:T(8,128)(2,1)S(1)}, bf16[32,1280]{1,0:T(8,128)(2,1)S(1)}, u32[]{:S(2)}, u32[]{:S(2)}) collective-permute-start(bf16[32,1280]{1,0:T(8,128)(2,1)S(1)} %get-tuple-element.55), channel_id=1, source_target_pairs={{0,2},{2,0},{4,6},{6,4},{1,3},{3,1},{5,7},{7,5},{8,10},{10,8},{12,... | collective-permute-start | bytes 245768 | tf_op jit(solution)/shard_map/ppermute | solution.py:471
  38.5 11.2 %collective-permute-start.8 = (bf16[128,1152]{1,0:T(8,128)(2,1)S(1)}, bf16[128,1152]{1,0:T(8,128)(2,1)S(1)}, u32[]{:S(2)}, u32[]{:S(2)}) collective-permute-start(bf16[128,1152]{1,0:T(8,128)(2,1)S(1)} %collective-permute-done.4.refs_5_.refs_9_), channel_id=1, source_target_pairs={{0,1},{2,3},{4,5},{6,7},{1,0},{3,2},{5,4},{7,6},{8,9},{10,11},{12,... | collective-permute-start | bytes 884744 | tf_op jit(solution)/shard_map/ppermute | solution.py:475
  38.5 11.2 %collective-permute-start.9 = (bf16[128,1152]{1,0:T(8,128)(2,1)S(1)}, bf16[128,1152]{1,0:T(8,128)(2,1)S(1)}, u32[]{:S(2)}, u32[]{:S(2)}) collective-permute-start(bf16[128,1152]{1,0:T(8,128)(2,1)S(1)} %collective-permute-done.5.refs_6_.refs_10_), channel_id=1, source_target_pairs={{0,1},{2,3},{4,5},{6,7},{1,0},{3,2},{5,4},{7,6},{8,9},{10,11},{12,... | collective-permute-start | bytes 884744 | tf_op jit(solution)/shard_map/ppermute | solution.py:475
  46.6 3.2 %collective-permute-start.10 = (bf16[128,1152]{1,0:T(8,128)(2,1)S(1)}, bf16[128,1152]{1,0:T(8,128)(2,1)S(1)}, u32[]{:S(2)}, u32[]{:S(2)}) collective-permute-start(bf16[128,1152]{1,0:T(8,128)(2,1)S(1)} %collective-permute-done.6.refs_7_.refs_11_), channel_id=1, source_target_pairs={{0,1},{2,3},{4,5},{6,7},{1,0},{3,2},{5,4},{7,6},{8,9},{10,11},{12,... | collective-permute-start | bytes 884744 | tf_op jit(solution)/shard_map/ppermute | solution.py:475
  46.6 1.0 copy-start.8
  47.9 1.9 %collective-permute-start.7 = (bf16[128,1152]{1,0:T(8,128)(2,1)S(1)}, bf16[128,1152]{1,0:T(8,128)(2,1)S(1)}, u32[]{:S(2)}, u32[]{:S(2)}) collective-permute-start(bf16[128,1152]{1,0:T(8,128)(2,1)S(1)} %get-tuple-element.57.refs_4_.refs_8_), channel_id=1, source_target_pairs={{0,1},{2,3},{4,5},{6,7},{1,0},{3,2},{5,4},{7,6},{8,9},{10,11},{12,... | collective-permute-start | bytes 884744 | tf_op jit(solution)/shard_map/ppermute | solution.py:475
  48.5 1.3 collective-permute-start.11
  49.8 0.9 copy-start.9
  50.7 0.9 copy-start.10
  57.4 6.7 %collective-permute-start.12 = (bf16[136,384]{1,0:T(8,128)(2,1)S(1)}, bf16[136,384]{1,0:T(8,128)(2,1)S(1)}, u32[]{:S(2)}, u32[]{:S(2)}) collective-permute-start(bf16[136,384]{1,0:T(8,128)(2,1)S(1)} %pad_maximum_fusion.1), channel_id=1, source_target_pairs={{0,2},{2,0},{4,6},{6,4},{1,3},{3,1},{5,7},{7,5},{8,10},{10,8},{12,... | collective-permute-start | bytes 313352 | tf_op jit(solution)/shard_map/ppermute | solution.py:471
  58.9 8.1 %collective-permute-start.13 = (bf16[136,384]{1,0:T(8,128)(2,1)S(1)}, bf16[136,384]{1,0:T(8,128)(2,1)S(1)}, u32[]{:S(2)}, u32[]{:S(2)}) collective-permute-start(bf16[136,384]{1,0:T(8,128)(2,1)S(1)} %pad_maximum_fusion.2), channel_id=1, source_target_pairs={{0,4},{2,6},{4,0},{6,2},{1,5},{3,7},{5,1},{7,3},{8,12},{10,14},{12... | collective-permute-start | bytes 313352 | tf_op jit(solution)/shard_map/ppermute | solution.py:471
  60.6 10.2 %collective-permute-start.15 = (bf16[2,4,96,128]{3,2,1,0:T(8,128)(2,1)}, bf16[2,4,96,128]{3,2,1,0:T(8,128)(2,1)S(1)}, u32[]{:S(2)}, u32[]{:S(2)}) collective-permute-start(bf16[2,4,96,128]{3,2,1,0:T(8,128)(2,1)} %get-tuple-element.68), channel_id=1, source_target_pairs={{0,8},{8,0},{16,24},{24,16},{1,9},{9,1},{17,25},{25,17},{2,10},{10... | collective-permute-start | bytes 589832 | tf_op jit(solution)/shard_map/ppermute | solution.py:478
  62.1 9.6 %collective-permute-start.16 = (bf16[2,4,96,128]{3,2,1,0:T(8,128)(2,1)S(1)}, bf16[2,4,96,128]{3,2,1,0:T(8,128)(2,1)S(1)}, u32[]{:S(2)}, u32[]{:S(2)}) collective-permute-start(bf16[2,4,96,128]{3,2,1,0:T(8,128)(2,1)S(1)} %get-tuple-element.69), channel_id=1, source_target_pairs={{0,16},{8,24},{16,0},{24,8},{1,17},{9,25},{17,1},{25,9},{2,18},{10... | collective-permute-start | bytes 589832 | tf_op jit(solution)/shard_map/ppermute | solution.py:478
  63.6 9.0 %collective-permute-start.17 = (bf16[2,4,96,128]{3,2,1,0:T(8,128)(2,1)S(1)}, bf16[2,4,96,128]{3,2,1,0:T(8,128)(2,1)S(1)}, u32[]{:S(2)}, u32[]{:S(2)}) collective-permute-start(bf16[2,4,96,128]{3,2,1,0:T(8,128)(2,1)S(1)} %get-tuple-element.70), channel_id=1, source_target_pairs={{0,24},{8,16},{16,8},{24,0},{1,25},{9,17},{17,9},{25,1},{2,26},{10... | collective-permute-start | bytes 589832 | tf_op jit(solution)/shard_map/ppermute | solution.py:478
  64.2 6.6 %collective-permute-start.14 = (bf16[136,384]{1,0:T(8,128)(2,1)S(1)}, bf16[136,384]{1,0:T(8,128)(2,1)S(1)}, u32[]{:S(2)}, u32[]{:S(2)}) collective-permute-start(bf16[136,384]{1,0:T(8,128)(2,1)S(1)} %pad_maximum_fusion.3), channel_id=1, source_target_pairs={{0,6},{2,4},{4,2},{6,0},{1,7},{3,5},{5,3},{7,1},{8,14},{10,12},{12... | collective-permute-start | bytes 313352 | tf_op jit(solution)/shard_map/ppermute | solution.py:471
  73.9 27.2 %copy-start.7 = (bf16[128,1536]{1,0:T(8,128)(2,1)}, bf16[128,1536]{1,0:T(8,128)(2,1)S(1)}, u32[]{:S(2)}) copy-start(bf16[128,1536]{1,0:T(8,128)(2,1)S(1)} %get-tuple-element.71.refs_5_.attn_ref) | copy-start | bytes 1179652
  73.9 13.0 %collective-permute-start.21 = (bf16[128,1536]{1,0:T(8,128)(2,1)S(1)}, bf16[128,1536]{1,0:T(8,128)(2,1)S(1)}, u32[]{:S(2)}, u32[]{:S(2)}) collective-permute-start(bf16[128,1536]{1,0:T(8,128)(2,1)S(1)} %get-tuple-element.71.refs_5_.attn_ref), channel_id=1, source_target_pairs={{0,24},{8,16},{16,8},{24,0},{1,25},{9,17},{17,9},{25,1},{2,26},{10... | collective-permute-start | bytes 1179656 | tf_op jit(solution)/shard_map/ppermute | solution.py:478
  75.4 17.7 %collective-permute-start.20 = (bf16[128,1536]{1,0:T(8,128)(2,1)S(1)}, bf16[128,1536]{1,0:T(8,128)(2,1)S(1)}, u32[]{:S(2)}, u32[]{:S(2)}) collective-permute-start(bf16[128,1536]{1,0:T(8,128)(2,1)S(1)} %get-tuple-element.71.refs_5_.attn_ref), channel_id=1, source_target_pairs={{0,16},{8,24},{16,0},{24,8},{1,17},{9,25},{17,1},{25,9},{2,18},{10... | collective-permute-start | bytes 1179656 | tf_op jit(solution)/shard_map/ppermute | solution.py:478
  76.8 16.3 %collective-permute-start.19 = (bf16[128,1536]{1,0:T(8,128)(2,1)S(1)}, bf16[128,1536]{1,0:T(8,128)(2,1)S(1)}, u32[]{:S(2)}, u32[]{:S(2)}) collective-permute-start(bf16[128,1536]{1,0:T(8,128)(2,1)S(1)} %get-tuple-element.71.refs_5_.attn_ref), channel_id=1, source_target_pairs={{0,8},{8,0},{16,24},{24,16},{1,9},{9,1},{17,25},{25,17},{2,10},{10... | collective-permute-start | bytes 1179656 | tf_op jit(solution)/shard_map/ppermute | solution.py:478
  77.4 16.3 %collective-permute-start.22 = (bf16[128,1536]{1,0:T(8,128)(2,1)S(1)}, bf16[128,1536]{1,0:T(8,128)(2,1)S(1)}, u32[]{:S(2)}, u32[]{:S(2)}) collective-permute-start(bf16[128,1536]{1,0:T(8,128)(2,1)S(1)} %get-tuple-element.71.refs_5_.attn_ref), channel_id=1, source_target_pairs={{0,1},{2,3},{4,5},{6,7},{1,0},{3,2},{5,4},{7,6},{8,9},{10,11},{12,... | collective-permute-start | bytes 1179656 | tf_op jit(solution)/shard_map/ppermute | solution.py:475
  77.4 0.9 copy-start.6
  78.3 15.4 %collective-permute-start.18 = (bf16[4,4,96,128]{3,2,1,0:T(8,128)(2,1)S(1)}, bf16[4,4,96,128]{3,2,1,0:T(8,128)(2,1)S(1)}, u32[]{:S(2)}, u32[]{:S(2)}) collective-permute-start(bf16[4,4,96,128]{3,2,1,0:T(8,128)(2,1)S(1)} %shard_map.170), channel_id=1, source_target_pairs={{0,1},{2,3},{4,5},{6,7},{1,0},{3,2},{5,4},{7,6},{8,9},{10,11},{12,... | collective-permute-start | bytes 1179656 | tf_op jit(solution)/shard_map/ppermute | solution.py:475
  86.8 6.8 %collective-permute-start.25 = (bf16[128,1536]{1,0:T(8,128)(2,1)S(1)}, bf16[128,1536]{1,0:T(8,128)(2,1)S(1)}, u32[]{:S(2)}, u32[]{:S(2)}) collective-permute-start(bf16[128,1536]{1,0:T(8,128)(2,1)S(1)} %collective-permute-done.21.refs_8_), channel_id=1, source_target_pairs={{0,1},{2,3},{4,5},{6,7},{1,0},{3,2},{5,4},{7,6},{8,9},{10,11},{12,... | collective-permute-start | bytes 1179656 | tf_op jit(solution)/shard_map/ppermute | solution.py:475
  93.1 1.7 %collective-permute-start.24 = (bf16[128,1536]{1,0:T(8,128)(2,1)S(1)}, bf16[128,1536]{1,0:T(8,128)(2,1)S(1)}, u32[]{:S(2)}, u32[]{:S(2)}) collective-permute-start(bf16[128,1536]{1,0:T(8,128)(2,1)S(1)} %collective-permute-done.20.refs_7_), channel_id=1, source_target_pairs={{0,1},{2,3},{4,5},{6,7},{1,0},{3,2},{5,4},{7,6},{8,9},{10,11},{12,... | collective-permute-start | bytes 1179656 | tf_op jit(solution)/shard_map/ppermute | solution.py:475
  93.1 2.3 %collective-permute-start.23 = (bf16[128,1536]{1,0:T(8,128)(2,1)S(1)}, bf16[128,1536]{1,0:T(8,128)(2,1)S(1)}, u32[]{:S(2)}, u32[]{:S(2)}) collective-permute-start(bf16[128,1536]{1,0:T(8,128)(2,1)S(1)} %collective-permute-done.19.refs_6_), channel_id=1, source_target_pairs={{0,1},{2,3},{4,5},{6,7},{1,0},{3,2},{5,4},{7,6},{8,9},{10,11},{12,... | collective-permute-start | bytes 1179656 | tf_op jit(solution)/shard_map/ppermute | solution.py:475
  96.8 0.8 copy-start.1
  97.6 33.2 %copy-start.2 = (f32[96,1536]{1,0:T(8,128)S(1)}, f32[96,1536]{1,0:T(8,128)}, u32[]{:S(2)}) copy-start(f32[96,1536]{1,0:T(8,128)} %copy-done.1) | copy-start | bytes 1769476
  97.6 33.2 %collective-permute-start.26 = (bf16[96,1536]{1,0:T(8,128)(2,1)S(1)}, bf16[96,1536]{1,0:T(8,128)(2,1)S(1)}, u32[]{:S(2)}, u32[]{:S(2)}) collective-permute-start(bf16[96,1536]{1,0:T(8,128)(2,1)S(1)} %get-tuple-element.76), channel_id=1, source_target_pairs={{0,4},{2,6},{4,0},{6,2},{1,5},{3,7},{5,1},{7,3},{8,12},{10,14},{12... | collective-permute-start | bytes 884744 | tf_op jit(solution)/shard_map/ppermute | solution.py:471
  98.4 32.5 %collective-permute-start.27 = (bf16[96,1536]{1,0:T(8,128)(2,1)S(1)}, bf16[96,1536]{1,0:T(8,128)(2,1)S(1)}, u32[]{:S(2)}, u32[]{:S(2)}) collective-permute-start(bf16[96,1536]{1,0:T(8,128)(2,1)S(1)} %get-tuple-element.77), channel_id=1, source_target_pairs={{0,6},{2,4},{4,2},{6,0},{1,7},{3,5},{5,3},{7,1},{8,14},{10,12},{12... | collective-permute-start | bytes 884744 | tf_op jit(solution)/shard_map/ppermute | solution.py:471
  100.9 30.0 %collective-permute-start.28 = (bf16[96,1536]{1,0:T(8,128)(2,1)S(1)}, bf16[96,1536]{1,0:T(8,128)(2,1)S(1)}, u32[]{:S(2)}, u32[]{:S(2)}) collective-permute-start(bf16[96,1536]{1,0:T(8,128)(2,1)S(1)} %get-tuple-element.78), channel_id=1, source_target_pairs={{0,2},{2,0},{4,6},{6,4},{1,3},{3,1},{5,7},{7,5},{8,10},{10,8},{12,... | collective-permute-start | bytes 884744 | tf_op jit(solution)/shard_map/ppermute | solution.py:471
  108.6 1.4 %collective-permute-start.29 = (f32[4,384]{1,0:T(4,128)}, f32[4,384]{1,0:T(4,128)S(1)}, u32[]{:S(2)}, u32[]{:S(2)}) collective-permute-start(f32[4,384]{1,0:T(4,128)} %get-tuple-element.80), channel_id=1, source_target_pairs={{0,1},{2,3},{4,5},{6,7},{1,0},{3,2},{5,4},{7,6},{8,9},{10,11},{12,... | collective-permute-start | bytes 18440 | tf_op jit(solution)/shard_map/ppermute | solution.py:475
  110.8 15.9 %collective-permute-start.30 = (f32[1,384]{1,0:T(1,128)S(1)}, f32[1,384]{1,0:T(1,128)S(1)}, u32[]{:S(2)}, u32[]{:S(2)}) collective-permute-start(f32[1,384]{1,0:T(1,128)S(1)} %get-tuple-element.82), channel_id=1, source_target_pairs={{0,4},{2,6},{4,0},{6,2},{1,5},{3,7},{5,1},{7,3},{8,12},{10,14},{12... | collective-permute-start | bytes 4616 | tf_op jit(solution)/shard_map/ppermute | solution.py:471
  112.4 14.2 %collective-permute-start.31 = (f32[1,384]{1,0:T(1,128)S(1)}, f32[1,384]{1,0:T(1,128)S(1)}, u32[]{:S(2)}, u32[]{:S(2)}) collective-permute-start(f32[1,384]{1,0:T(1,128)S(1)} %get-tuple-element.83), channel_id=1, source_target_pairs={{0,6},{2,4},{4,2},{6,0},{1,7},{3,5},{5,3},{7,1},{8,14},{10,12},{12... | collective-permute-start | bytes 4616 | tf_op jit(solution)/shard_map/ppermute | solution.py:471
  126.7 3.6 %collective-permute-start.32 = (f32[1,384]{1,0:T(1,128)S(1)}, f32[1,384]{1,0:T(1,128)S(1)}, u32[]{:S(2)}, u32[]{:S(2)}) collective-permute-start(f32[1,384]{1,0:T(1,128)S(1)} %get-tuple-element.84), channel_id=1, source_target_pairs={{0,2},{2,0},{4,6},{6,4},{1,3},{3,1},{5,7},{7,5},{8,10},{10,8},{12,... | collective-permute-start | bytes 4616 | tf_op jit(solution)/shard_map/ppermute | solution.py:471
  (2 other events, 1.4 us)

commit v5 on v4

v5 whole, which is shorter than its diff:
```python
import math
import functools
import jax
import jax.numpy as jnp
from jax import lax
from jax.experimental import pallas as pl
from jax.experimental.pallas import tpu as pltpu
from jax.sharding import PartitionSpec as P

DT5 = 4096
CORES = 2
GROUPS = 4

eps_norm = 1e-06
f32 = jnp.float32
bf16 = jnp.bfloat16


VMEM = pl.BlockSpec(memory_space=pltpu.VMEM)
SMEM = pl.BlockSpec(memory_space=pltpu.SMEM)
ANY = pl.BlockSpec(memory_space=pl.ANY)


def params(mib=24):
    return pltpu.CompilerParams(vmem_limit_bytes=int(mib * 1024 * 1024))


def cost(flops, bytes_accessed, transcendentals=0):
    return pl.CostEstimate(
        flops=flops, bytes_accessed=bytes_accessed, transcendentals=transcendentals
    )


def split_tail(squares, width):
    high = squares.astype(bf16).astype(f32)
    low = squares - high
    lane = lax.broadcasted_iota(jnp.int32, (squares.shape[0], width), 1)
    return jnp.where(lane == 0, high, jnp.where(lane == 1, low, 0.0))


def joined(tail):
    return tail[:, 0:1] + tail[:, 1:2]


def text_kernel(
    groups, heads, place_of, meta_ref, len_ref, src_ref, states_ref, gain_ref, w_ref, bias_ref, own_ref, *msgs
):
    size = own_ref.shape[2]
    rows = own_ref.shape[1] // (3 * heads + 1)
    width = heads * size
    slots = states_ref.shape[0]
    slot_local = rows // groups

    def slot_at(row):
        z_at = (row % rows) // slot_local
        return place_of(meta_ref[1] ^ (row // rows), z_at) * slot_local + row % slot_local

    iota = functools.partial(lax.broadcasted_iota, jnp.int32, (slots, slots))
    sources = src_ref[...].astype(f32)
    chosen = (iota(1) == slot_at(iota(0))).astype(f32)
    source_col = jnp.sum(chosen * sources, axis=1, keepdims=True)
    pick = (iota(1).astype(f32) == source_col).astype(bf16)
    chosen_t = (iota(0) == slot_at(iota(1))).astype(bf16)
    source_row = jnp.dot(sources.astype(bf16), chosen_t, preferred_element_type=f32)
    bias_ref[...] = jnp.where(source_row < len_ref[0].astype(f32), 0.0, -1e30)

    picked = jnp.dot(pick, states_ref[...], preferred_element_type=f32)
    scaled = (picked * gain_ref[...]).astype(bf16)
    tail = split_tail(jnp.sum(picked * picked, axis=1, keepdims=True), size)
    for g in range(groups):
        for i in range(3):
            at = (i * groups + (meta_ref[0] ^ g)) * width
            got = jnp.dot(
                scaled, w_ref[:, pl.ds(pl.multiple_of(at, 128), width)], preferred_element_type=f32
            )
            for head in range(heads):
                part = got[:, head * size : (head + 1) * size]
                to = slice((i * heads + head) * rows, (i * heads + head + 1) * rows)
                own_ref[g, to, :] = part[:rows]
                for j, msg in enumerate(msgs):
                    msg[g, to, :] = part[(j + 1) * rows : (j + 2) * rows].astype(bf16)
        own_ref[g, 3 * heads * rows :, :] = tail[:rows]
        for j, msg in enumerate(msgs):
            msg[g, 3 * heads * rows :, :] = tail[(j + 1) * rows : (j + 2) * rows].astype(bf16)


def text_project(meta, length, sources, states, gain, text_proj, groups, parts, size, place_of):
    slots, depth = states.shape
    heads = text_proj.shape[1] // (3 * groups * size)
    block = (groups, (3 * heads + 1) * slots // parts, size)
    shapes = [jax.ShapeDtypeStruct((1, slots), f32), jax.ShapeDtypeStruct(block, f32)]
    shapes += [jax.ShapeDtypeStruct(block, bf16)] * (parts - 1)
    return pl.pallas_call(
        functools.partial(text_kernel, groups, heads, place_of),
        out_shape=shapes,
        in_specs=[SMEM, SMEM, VMEM, VMEM, VMEM, VMEM],
        out_specs=[VMEM] * (1 + parts),
        compiler_params=params(),
        cost_estimate=cost(
            2 * slots * depth * text_proj.shape[1], 2 * depth * text_proj.shape[1]
        ),
    )(meta, length, sources, states, gain, text_proj)


def pack_kernel(groups, n_got, meta_ref, k_ref, v_ref, q_ref, *refs):
    part_refs, (own_ref, *outs) = refs[: 1 + n_got], refs[1 + n_got :]
    rows = k_ref.shape[0]
    size = own_ref.shape[1]
    heads = k_ref.shape[1] // (groups * size)
    text_rows = own_ref.shape[0]
    tail_rows = text_rows // (3 * heads + 1)
    for g, out in enumerate(outs):
        for i, ref in enumerate((k_ref, v_ref, q_ref)):
            for head in range(heads):
                at = ((meta_ref[0] ^ g) * heads + head) * size
                to = (i * heads + head) * rows
                out[to : to + rows, :] = ref[:, pl.ds(pl.multiple_of(at, 128), size)]
        total = part_refs[0][g]
        for ref in part_refs[1:]:
            total = total + ref[g].astype(f32)
        tail = split_tail(joined(total[text_rows - tail_rows :]), size)
        total = jnp.concatenate([total[: text_rows - tail_rows], tail], axis=0)
        if g == 0:
            own_ref[...] = total
        else:
            out[3 * heads * rows :, :] = total.astype(bf16)


def pack(meta, keys, values, queries, partials, groups):
    rows = keys.shape[0]
    text_rows, size = partials[0].shape[1:]
    image_rows = 3 * rows * keys.shape[1] // (groups * size)
    shapes = [jax.ShapeDtypeStruct((text_rows, size), f32)]
    shapes += [jax.ShapeDtypeStruct((image_rows, size), bf16)]
    shapes += [jax.ShapeDtypeStruct((image_rows + text_rows, size), bf16)] * (groups - 1)
    return pl.pallas_call(
        functools.partial(pack_kernel, groups, len(partials) - 1),
        out_shape=shapes,
        in_specs=[SMEM] + [VMEM] * (3 + len(partials)),
        out_specs=[VMEM] * (1 + groups),
        compiler_params=params(),
        cost_estimate=cost(0, 12 * keys.size),
    )(meta, keys, values, queries, *partials)


def text_norm_kernel(features, qg_ref, kg_ref, own_ref, *refs):
    got, (tq_ref, tkv_ref) = refs[:-2], refs[-2:]
    size = own_ref.shape[1]
    total = own_ref[...]
    for ref in got:
        total = total + ref[ref.shape[0] - total.shape[0] :, :].astype(f32)
    width = tq_ref.shape[0]
    rows = total.shape[0] - 3 * width
    heads = width // rows
    rate = lax.rsqrt(joined(total[3 * width :]) / features + eps_norm)
    for i in range(3):
        for head in range(heads):
            at = (i * heads + head) * rows
            x = total[at : at + rows] * rate
            if i < 2:
                mean = jnp.sum(x * x, axis=1, keepdims=True) / size
                x = x * lax.rsqrt(mean + eps_norm) * (qg_ref, kg_ref)[i][...]
            if i == 0:
                tq_ref[at : at + rows, :] = x.astype(bf16)
            else:
                tkv_ref[at - width : at - width + rows, :] = x.astype(bf16)


def text_norm(query_gain, key_gain, own, got, features, heads):
    text_rows, size = own.shape
    width = text_rows // (3 * heads + 1) * heads
    return pl.pallas_call(
        functools.partial(text_norm_kernel, features),
        out_shape=[
            jax.ShapeDtypeStruct((width, size), bf16),
            jax.ShapeDtypeStruct((2 * width, size), bf16),
        ],
        in_specs=[VMEM] * (3 + len(got)),
        out_specs=[VMEM] * 2,
        compiler_params=params(),
        cost_estimate=cost(0, 40_000_000),
    )(query_gain, key_gain, own, *got)


def block_kernel(n_got, *refs):
    pieces, text_ref, out_ref = refs[:n_got], refs[n_got], refs[-1]
    rows = (out_ref.shape[0] - text_ref.shape[0]) // n_got
    for k, piece in enumerate(pieces):
        out_ref[k * rows : (k + 1) * rows, :] = piece[:rows, :]
    out_ref[n_got * rows :, :] = text_ref[...]


def block_of(pieces, text_kv, after):
    rows, size = pieces[0].shape
    total = rows // 3 * 2 * len(pieces) + text_kv.shape[0]
    return pl.pallas_call(
        functools.partial(block_kernel, len(pieces)),
        out_shape=jax.ShapeDtypeStruct((total, size), bf16),
        in_specs=[VMEM] * (len(pieces) + 1) + [ANY] * len(after),
        out_specs=VMEM,
        compiler_params=params(),
        cost_estimate=cost(0, 4 * total * size),
    )(*pieces, text_kv, *after)


def attention_kernel(n_pieces, n_blocks, rows, text_rows, *refs):
    pieces, refs = refs[:n_pieces], refs[n_pieces:]
    tq_ref, tkv_ref, refs = refs[0], refs[1], refs[2:]
    blocks, refs = refs[:n_blocks], refs[n_blocks:]
    bias_ref, out_refs, tout_ref = refs[0], refs[1:-1], refs[-1]
    size = tq_ref.shape[1]
    heads = tq_ref.shape[0] // text_rows
    factor = size ** (-0.5) * math.log2(math.e)
    bias = bias_ref[...]
    nt = (((1,), (1,)), ((), ()))
    own = 2 * heads * rows

    def with_ones(values):
        return jnp.concatenate([values, jnp.ones(values.shape, bf16)], axis=1)

    for head in range(heads):
        kv, tkv = [], []
        for i in range(2):
            at = (i * heads + head) * rows
            image = [p[at : at + rows, :] for p in pieces]
            text_at = (i * heads + head) * text_rows
            text = [tkv_ref[text_at : text_at + text_rows, :]]
            for b in blocks:
                image += [b[k * own + at : k * own + at + rows, :] for k in range(n_pieces)]
                start = n_pieces * own + text_at
                text.append(b[start : start + text_rows, :])
            kv.append(jnp.concatenate(image, axis=0))
            tkv.append(jnp.concatenate(text, axis=0))
        keys, values = kv[0], with_ones(kv[1])
        tkeys, tvalues = tkv[0], with_ones(tkv[1])
        cols = slice(head * size, (head + 1) * size)
        q_at = (2 * heads + head) * rows
        work = [(p[q_at : q_at + rows, :], out) for p, out in zip(pieces, out_refs)]
        work.append((tq_ref[head * text_rows : (head + 1) * text_rows, :], tout_ref))
        for q, out_ref in work:
            s_img = lax.dot_general(q, keys, nt, preferred_element_type=f32)
            s_txt = lax.dot_general(q, tkeys, nt, preferred_element_type=f32) + bias
            top = jnp.maximum(
                jnp.max(s_img, axis=1, keepdims=True), jnp.max(s_txt, axis=1, keepdims=True)
            )
            p_img = jnp.exp2((s_img - top) * factor).astype(bf16)
            p_txt = jnp.exp2((s_txt - top) * factor).astype(bf16)
            acc = jnp.dot(p_img, values, preferred_element_type=f32)
            acc = acc + jnp.dot(p_txt, tvalues, preferred_element_type=f32)
            out_ref[:, cols] = (acc[:, :size] / acc[:, size:]).astype(bf16)


def attention(pieces, text_q, text_kv, blocks, bias, rows, text_rows):
    size = text_q.shape[1]
    heads = text_q.shape[0] // text_rows
    queries = len(pieces) * rows + text_rows
    keys = (1 + len(blocks)) * queries
    args = tuple(pieces) + (text_q, text_kv) + tuple(blocks) + (bias,)
    shapes = [jax.ShapeDtypeStruct((rows, heads * size), bf16)] * len(pieces)
    shapes += [jax.ShapeDtypeStruct((text_rows, heads * size), bf16)]
    return pl.pallas_call(
        functools.partial(attention_kernel, len(pieces), len(blocks), rows, text_rows),
        out_shape=shapes,
        in_specs=[VMEM] * len(args),
        out_specs=[VMEM] * len(shapes),
        compiler_params=params(),
        cost_estimate=cost(
            4 * queries * keys * heads * size,
            4 * (queries + keys) * heads * size,
            queries * keys * heads,
        ),
    )(*args)


def gated_kernel(groups, parts, place_of, meta_ref, gate_ref, d_out_ref, *refs):
    msgs, turned = refs[:-1], refs[-1]
    gated = (gate_ref[...] * d_out_ref[...].astype(f32)).astype(bf16)
    turned[...] = gated.astype(f32).T
    rows = msgs[0].shape[2]
    z, oc, dp = meta_ref[0], meta_ref[1], meta_ref[2]
    for k, msg in enumerate(msgs):
        for j in range(parts):
            for g in range(groups):
                at = (dp ^ k) * (groups * parts) + place_of(oc ^ j, z ^ g)
                msg[j, g] = turned[pl.ds(pl.multiple_of(at * rows, 8), rows), :].astype(bf16)


def gated_parts(meta, gate, d_out, n_dp, groups, parts, place_of):
    local, model = d_out.shape
    rows = model // (n_dp * groups * parts)
    return pl.pallas_call(
        functools.partial(gated_kernel, groups, parts, place_of),
        out_shape=[jax.ShapeDtypeStruct((parts, groups, rows, local), bf16)] * n_dp,
        in_specs=[SMEM, VMEM, VMEM],
        out_specs=[VMEM] * n_dp,
        scratch_shapes=[pltpu.VMEM((model, local), f32)],
        compiler_params=params(),
        cost_estimate=cost(0, 4 * local * model),
    )(meta, gate, d_out)


def d_attn_kernel(gate_ref, d_out_ref, w_ref, out_ref):
    block = 512
    total = jnp.zeros(out_ref.shape, f32)
    for at in range(0, w_ref.shape[0], block):
        cols = slice(at, at + block)
        gated = (gate_ref[:, cols] * d_out_ref[:, cols].astype(f32)).astype(bf16)
        total = total + jnp.dot(gated, w_ref[cols, :], preferred_element_type=f32)
    out_ref[...] = total.astype(bf16)


def attn_gradient(gate, d_out, out_weight):
    local, model = d_out.shape
    inner = out_weight.shape[1]
    return pl.pallas_call(
        d_attn_kernel,
        out_shape=jax.ShapeDtypeStruct((local, inner), bf16),
        in_specs=[VMEM] * 3,
        out_specs=VMEM,
        compiler_params=params(),
        cost_estimate=cost(2 * local * inner * model, 2 * inner * model),
    )(gate, d_out, out_weight)


def gather_kernel(n_dp, *refs):
    pieces, outs = refs[:n_dp], refs[n_dp:]
    for j, out in enumerate(outs):
        for k, piece in enumerate(pieces):
            out[k] = piece[j + 1]


def gather_parts(pieces):
    parts = pieces[0].shape[0]
    shape = (len(pieces),) + pieces[0].shape[1:]
    return pl.pallas_call(
        functools.partial(gather_kernel, len(pieces)),
        out_shape=[jax.ShapeDtypeStruct(shape, bf16)] * (parts - 1),
        in_specs=[VMEM] * len(pieces),
        out_specs=[VMEM] * (parts - 1),
        compiler_params=params(),
        cost_estimate=cost(0, 4 * math.prod(shape) * (parts - 1)),
    )(*pieces)


def project_kernel(groups, parts, place_of, meta_ref, attn_ref, w_ref, gate_ref, d_out_ref, after_ref, out_ref, *refs):
    del after_ref
    terms, by_place = refs[:parts], refs[parts]
    block = 512
    sums = []
    for at in range(0, w_ref.shape[0], block):
        cols = slice(at, at + block)
        got = lax.dot_general(
            attn_ref[...], w_ref[cols, :], (((1,), (1,)), ((), ())), preferred_element_type=f32
        )
        out_ref[:, cols] = (got * gate_ref[:, cols]).astype(bf16)
        sums.append(jnp.sum(got * d_out_ref[:, cols].astype(f32), axis=0, keepdims=True))
    sums = jnp.concatenate(sums, axis=1)
    places, width = by_place.shape
    for s in range(places):
        by_place[s : s + 1, :] = sums[:, s * width : (s + 1) * width]
    for j, term in enumerate(terms):
        for g in range(groups):
            at = place_of(meta_ref[1] ^ j, meta_ref[0] ^ g)
            term[g : g + 1, :] = by_place[pl.ds(at, 1), :]


def project(meta, attn, out_weight, gate, d_out, after, groups, parts, place_of):
    rows, inner = attn.shape
    model = out_weight.shape[0]
    width = model // (groups * parts)
    shapes = [jax.ShapeDtypeStruct((rows, model), bf16)]
    shapes += [jax.ShapeDtypeStruct((groups, width), f32)] * parts
    return pl.pallas_call(
        functools.partial(project_kernel, groups, parts, place_of),
        out_shape=shapes,
        in_specs=[SMEM, VMEM, VMEM, VMEM, VMEM, ANY],
        out_specs=[VMEM] * (1 + parts),
        scratch_shapes=[pltpu.VMEM((groups * parts, width), f32)],
        compiler_params=params(),
        cost_estimate=cost(2 * rows * inner * model, 2 * inner * model),
    )(meta, attn, out_weight, gate, d_out, after)


def grad_kernel(n_left, n_pieces, *refs):
    lefts, refs = refs[:n_left], refs[n_left:]
    pieces, outs = refs[:n_pieces], refs[n_pieces:]
    rows, width = outs[0].shape
    total = rows * len(outs)
    left = []
    for ref in lefts:
        left += [ref[i].reshape(total, -1) for i in range(ref.shape[0])]
    left = jnp.concatenate(left, axis=1)
    block = 256
    for start in range(0, width, block):
        cols = slice(start, start + block)
        right = jnp.concatenate([p[:, cols] for p in pieces], axis=0)
        got = jnp.dot(left, right, preferred_element_type=f32)
        for g, out in enumerate(outs):
            out[:, cols] = got[g * rows : (g + 1) * rows].astype(out.dtype)


def grad_product(lefts, pieces):
    groups, rows = lefts[0].shape[1:3]
    depth = pieces[0].shape[0] * len(pieces)
    width = pieces[0].shape[1]
    total = groups * rows
    shapes = [jax.ShapeDtypeStruct((rows, width), f32)]
    shapes += [jax.ShapeDtypeStruct((rows, width), bf16)] * (groups - 1)
    return pl.pallas_call(
        functools.partial(grad_kernel, len(lefts), len(pieces)),
        out_shape=shapes,
        in_specs=[VMEM] * (len(lefts) + len(pieces)),
        out_specs=[VMEM] * groups,
        compiler_params=params(),
        cost_estimate=cost(
            2 * total * depth * width, 2 * (total * depth + depth * width + total * width)
        ),
    )(*lefts, *pieces)


def on_device(
    caption_states,
    caption_gain,
    text_proj,
    caption_len,
    slot_source,
    query_gain,
    key_gain,
    image_q,
    image_k,
    image_v,
    out_weight,
    gate,
    d_out,
):
    n_dp = lax.axis_size("dp")
    n_seq = lax.axis_size("seq")
    G, C = GROUPS, CORES
    O = n_seq // (G * C)
    OC = O * C
    dp = lax.axis_index("dp")
    seq = lax.axis_index("seq")
    z = (seq // C) % G
    oc = (seq // (G * C)) * C + seq % C

    def place(oc_at, z_at):
        return ((oc_at // C) * G + z_at) * C + oc_at % C

    def to_z(x, k):
        perm = [(place(a, b), place(a, b ^ k)) for a in range(OC) for b in range(G)]
        return lax.ppermute(x, "seq", perm)

    def to_oc(x, j):
        perm = [(place(a, b), place(a ^ j, b)) for a in range(OC) for b in range(G)]
        return lax.ppermute(x, "seq", perm)

    def to_dp(x, k):
        return lax.ppermute(x, "dp", [(a, a ^ k) for a in range(n_dp)])

    def part(x, index, size, axis):
        return lax.dynamic_slice_in_dim(x, index * size, size, axis)

    slot_total = slot_source.shape[1]
    slot_local = slot_total // n_seq
    image_local = image_q.shape[1]
    inner_width = image_q.shape[2]
    model_width = out_weight.shape[0]
    head_size = query_gain.shape[0]
    gw = inner_width // G
    order = [2, 3, 1]
    meta = jnp.stack([z, oc, dp]).astype(jnp.int32)

    heads = gw // head_size
    text_rows = G * slot_local
    bias, *partials = text_project(
        meta, caption_len, slot_source, caption_states[0], caption_gain[None], text_proj,
        G, OC, head_size, place,
    )
    partials = [partials[0]] + [to_oc(partials[j], j) for j in range(1, OC)]
    own, *packed = pack(meta, image_k[0], image_v[0], image_q[0], partials, G)
    pieces = {0: packed[0]}
    for k in order:
        pieces[k] = to_z(packed[k], k)
    pieces = [pieces[k] for k in range(G)]
    text_q, text_kv = text_norm(
        query_gain[None], key_gain[None], own, pieces[1:], DT5, heads
    )

    gg = gated_parts(meta, gate, d_out[0], n_dp, G, OC, place)
    gg_dp = [gg[0]] + [to_dp(gg[k], k) for k in range(1, n_dp)]
    lefts = [g[:1] for g in gg_dp]
    lefts += [to_oc(g, j + 1) for j, g in enumerate(gather_parts(gg_dp))]

    block = block_of(pieces, text_kv, gg_dp[1:])
    blocks = [to_oc(block, j) for j in range(1, OC)]
    *outs, text_out = attention(
        pieces, text_q, text_kv, blocks, bias, image_local, text_rows
    )
    d_attn = attn_gradient(gate, d_out[0], out_weight)

    attn = jnp.zeros((image_local + slot_local, inner_width), bf16)
    for k in order + [0]:
        rows = jnp.concatenate([outs[k], part(text_out, z ^ k, slot_local, 0)], axis=0)
        rows = to_z(rows, k) if k else rows
        attn = lax.dynamic_update_slice_in_dim(attn, rows, (z ^ k) * gw, 1)
    image_attn = attn[:image_local]
    own_usable = part(slot_source[0] < caption_len[0], seq, slot_local, 0)
    text_attn = jnp.where(own_usable[:, None], attn[image_local:], jnp.zeros((), bf16))

    pieces = [image_attn] + [to_dp(image_attn, k) for k in range(1, n_dp)]
    pieces = pieces + [to_oc(p, j) for j in range(1, OC) for p in pieces]
    grads = grad_product(lefts, pieces)
    grad_wo = grads[0]
    for k in order:
        grad_wo = grad_wo + to_z(grads[k], k).astype(f32)

    image_out, *terms = project(
        meta, image_attn, out_weight, gate, d_out[0], pieces[n_dp], G, OC, place
    )
    term = terms[0]
    for j in range(1, OC):
        term = term + to_oc(terms[j], j)
    term = term[:2] + to_z(term[2:], 2)
    grad_gate = term[:1] + to_z(term[1:], 1)
    return (image_out[None], text_attn[None], d_attn[None], grad_wo, grad_gate)


def solution(mesh):
    in_specs = (
        P("dp", None, "seq"),
        P("seq"),
        P("seq", None),
        P("dp"),
        P("dp", None),
        P(),
        P(),
        P("dp", "seq", None),
        P("dp", "seq", None),
        P("dp", "seq", None),
        P(),
        P("dp", None),
        P("dp", "seq", None),
    )
    out_specs = (
        P("dp", "seq", None),
        P("dp", "seq", None),
        P("dp", "seq", None),
        P(("dp", "seq"), None),
        P("dp", "seq"),
    )
    return jax.shard_map(
        on_device, mesh=mesh, in_specs=in_specs, out_specs=out_specs, check_vma=False
    )
```

time: 132 us -> 136 us (1.030)
  the two profiles are of different devices: /device:TPU:0 before, /device:TPU:9 now
where the time goes in v5:
time: 136 us; the launch traced here: 135 us
  waiting for transfers between devices  69.1 us (51%)
  starting transfers between devices  23.5 us (17%)
  Pallas kernels  18.5 us (14%)
  local copies, waits for them, and re-layouts  18.3 us (13%)
  other arithmetic  3.74 us (3%)
  between operations  1.63 us (1%)
    ppermute x11, waiting for transfers between devices, to_z(): return lax.ppermute(x, 'seq', perm)  58.3 us
    unnamed x46, local copies, waits for them, and re-layouts  18 us
    ppermute x11, starting transfers between devices, to_z(): return lax.ppermute(x, 'seq', perm)  11.1 us
    ppermute x6, waiting for transfers between devices, to_dp(): return lax.ppermute(x, 'dp', [(a, a ^ k) for a in range(n_dp)])  7.39 us
    ppermute x6, starting transfers between devices, to_dp(): return lax.ppermute(x, 'dp', [(a, a ^ k) for a in range(n_dp)])  7.2 us
    ppermute x8, starting transfers between devices, to_oc(): return lax.ppermute(x, 'seq', perm)  5.21 us
    pallas_call x1, Pallas kernels, attention(): pl.pallas_call(functools.partial(attention_kernel, len(pieces), len(block...  5.07 us
    pallas_call x1, Pallas kernels, project(): pl.pallas_call(functools.partial(project_kernel, groups, parts, place_of)...  4.59 us
  transfers between devices with their start and end apart: 25, of which 11 were waited for; matrix products, arithmetic and copies ran while one was open for 2% of the time, Pallas kernels for 8%

profile of v5, /device:TPU:9, one launch (start us, length us, event | category | flops | bytes accessed | tf_op | source)
XLA Modules:
  0.0 134.7 jit_solution(10776007720903399949)
XLA Ops:
  1.4 2.3 %copy-done.3 = bf16[512,4608]{1,0:T(8,128)(2,1)S(1)} copy-done((bf16[512,4608]{1,0:T(8,128)(2,1)S(1)}, bf16[512,4608]{1,0:T(8,128)(2,1)}, u32[]{:S(2)}) %copy-start.3) | copy-done | bytes 4718616
  3.7 0.8 copy-done.11
  4.6 0.7 copy-done.14
  5.9 1.6 %shard_map.164 = (f32[1,64]{1,0:T(1,128)S(1)}, f32[4,320,128]{2,1,0:T(8,128)S(1)}, bf16[4,320,128]{2,1,0:T(8,128)(2,1)S(1)}) custom-call(s32[3]{0:T(128)S(1)} %pad_add_fusion.meta_ref, s32[1]{0:T(128)} %copy.22.len_ref, s32[1,64]{1,0:T(1,128)S(1)} %copy-done.17, bf16[64,512]{1,0:T(8,128)(2,1)S(1)} %bitcast.25, f32[1,512]{1,0:T(1,128)S(1)} %bitcast.26, ...), custom_call_target="tpu_custom_call" | custom-call | flops 301989888 | bytes 4718592 | tf_op jit(solution)/shard_map/pallas_call | solution.py:93
  7.5 0.7 collective-permute-start
  8.3 1.3 collective-permute-done.refs_1_
  9.5 1.0 copy-done.4
  10.5 1.0 copy-done.5
  11.5 1.0 copy-done.6
  12.5 0.9 shard_map.165
  13.5 2.5 %collective-permute-start.2 = (bf16[1472,128]{1,0:T(8,128)(2,1)S(1)}, bf16[1472,128]{1,0:T(8,128)(2,1)S(1)}, u32[]{:S(2)}, u32[]{:S(2)}) collective-permute-start(bf16[1472,128]{1,0:T(8,128)(2,1)S(1)} %get-tuple-element.35), channel_id=1, source_target_pairs={{0,4},{2,6},{4,0},{6,2},{1,5},{3,7},{5,1},{7,3},{8,12},{10,14},{12... | collective-permute-start | bytes 1130504 | tf_op jit(solution)/shard_map/ppermute | solution.py:451
  16.1 1.1 copy-done.1
  17.2 0.7 copy-done.9
  18.0 0.9 shard_map.167
  18.9 1.3 collective-permute-start.4
  20.1 1.2 collective-permute-start.5
  21.4 7.7 %collective-permute-done.1.refs_0_.refs_1_ = bf16[1472,128]{1,0:T(8,128)(2,1)S(1)} collective-permute-done((bf16[1472,128]{1,0:T(8,128)(2,1)S(1)}, bf16[1472,128]{1,0:T(8,128)(2,1)S(1)}, u32[]{:S(2)}, u32[]{:S(2)}) %collective-permute-start.1) | collective-permute-done | bytes 376864 | tf_op jit(solution)/shard_map/ppermute | solution.py:451
  29.0 2.0 %collective-permute-start.6 = (bf16[2,4,96,128]{3,2,1,0:T(8,128)(2,1)S(1)}, bf16[2,4,96,128]{3,2,1,0:T(8,128)(2,1)S(1)}, u32[]{:S(2)}, u32[]{:S(2)}) collective-permute-start(bf16[2,4,96,128]{3,2,1,0:T(8,128)(2,1)S(1)} %get-tuple-element.42), channel_id=1, source_target_pairs={{0,24},{8,16},{16,8},{24,0},{1,25},{9,17},{17,9},{25,1},{2,26},{10... | collective-permute-start | bytes 589832 | tf_op jit(solution)/shard_map/ppermute | solution.py:458
  31.1 1.5 %collective-permute-done.2.refs_1_.refs_2_ = bf16[1472,128]{1,0:T(8,128)(2,1)S(1)} collective-permute-done((bf16[1472,128]{1,0:T(8,128)(2,1)S(1)}, bf16[1472,128]{1,0:T(8,128)(2,1)S(1)}, u32[]{:S(2)}, u32[]{:S(2)}) %collective-permute-start.2) | collective-permute-done | bytes 376864 | tf_op jit(solution)/shard_map/ppermute | solution.py:451
  32.6 16.1 %collective-permute-done.3.refs_2_.refs_3_ = bf16[1472,128]{1,0:T(8,128)(2,1)S(1)} collective-permute-done((bf16[1472,128]{1,0:T(8,128)(2,1)S(1)}, bf16[1472,128]{1,0:T(8,128)(2,1)S(1)}, u32[]{:S(2)}, u32[]{:S(2)}) %collective-permute-start.3) | collective-permute-done | bytes 376864 | tf_op jit(solution)/shard_map/ppermute | solution.py:451
  48.6 0.7 copy-done.15
  50.8 1.5 %collective-permute-start.7 = (bf16[3264,128]{1,0:T(8,128)(2,1)S(1)}, bf16[3264,128]{1,0:T(8,128)(2,1)}, u32[]{:S(2)}, u32[]{:S(2)}) collective-permute-start(bf16[3264,128]{1,0:T(8,128)(2,1)S(1)} %shard_map.168), channel_id=1, source_target_pairs={{0,1},{2,3},{4,5},{6,7},{1,0},{3,2},{5,4},{7,6},{8,9},{10,11},{12,... | collective-permute-start | bytes 2506760 | tf_op jit(solution)/shard_map/ppermute | solution.py:455
  52.3 2.1 %collective-permute-done.7.refs_6_ = bf16[3264,128]{1,0:T(8,128)(2,1)} collective-permute-done((bf16[3264,128]{1,0:T(8,128)(2,1)S(1)}, bf16[3264,128]{1,0:T(8,128)(2,1)}, u32[]{:S(2)}, u32[]{:S(2)}) %collective-permute-start.7) | collective-permute-done | bytes 835616 | tf_op jit(solution)/shard_map/ppermute | solution.py:455
  54.4 1.0 copy-done.8
  55.4 0.8 copy-done.13
  56.2 0.7 copy-done.19
  57.6 5.1 %shard_map.169 = (bf16[128,384]{1,0:T(8,128)(2,1)S(1)}, bf16[128,384]{1,0:T(8,128)(2,1)S(1)}, bf16[128,384]{1,0:T(8,128)(2,1)S(1)}, bf16[128,384]{1,0:T(8,128)(2,1)S(1)}, bf16[32,384]{1,0:T(8,128)(2,1)S(1)}) custom-call(bf16[1152,128]{1,0:T(8,128)(2,1)S(1)} %copy-done.8, bf16[1472,128]{1,0:T(8,128)(2,1)S(1)} %collective-permute-done.1.refs_0_.refs_1_, ...), custom_call_target="tpu_custom_call" | custom-call | flops 909115392 | bytes 2506752 | tf_op jit(solution)/shard_map/pallas_call | solution.py:261
  62.8 1.4 %collective-permute-start.9 = (bf16[136,384]{1,0:T(8,128)(2,1)S(1)}, bf16[136,384]{1,0:T(8,128)(2,1)S(1)}, u32[]{:S(2)}, u32[]{:S(2)}) collective-permute-start(bf16[136,384]{1,0:T(8,128)(2,1)S(1)} %pad_maximum_fusion.1), channel_id=1, source_target_pairs={{0,6},{2,4},{4,2},{6,0},{1,7},{3,5},{5,3},{7,1},{8,14},{10,12},{12... | collective-permute-start | bytes 313352 | tf_op jit(solution)/shard_map/ppermute | solution.py:451
  64.2 2.3 %collective-permute-start.10 = (bf16[136,384]{1,0:T(8,128)(2,1)S(1)}, bf16[136,384]{1,0:T(8,128)(2,1)S(1)}, u32[]{:S(2)}, u32[]{:S(2)}) collective-permute-start(bf16[136,384]{1,0:T(8,128)(2,1)S(1)} %pad_maximum_fusion.2), channel_id=1, source_target_pairs={{0,2},{2,0},{4,6},{6,4},{1,3},{3,1},{5,7},{7,5},{8,10},{10,8},{12,... | collective-permute-start | bytes 313352 | tf_op jit(solution)/shard_map/ppermute | solution.py:451
  66.5 1.4 %collective-permute-done.8 = bf16[136,384]{1,0:T(8,128)(2,1)S(1)} collective-permute-done((bf16[136,384]{1,0:T(8,128)(2,1)S(1)}, bf16[136,384]{1,0:T(8,128)(2,1)S(1)}, u32[]{:S(2)}, u32[]{:S(2)}) %collective-permute-start.8) | collective-permute-done | bytes 104480 | tf_op jit(solution)/shard_map/ppermute | solution.py:451
  67.9 5.9 %collective-permute-done.9 = bf16[136,384]{1,0:T(8,128)(2,1)S(1)} collective-permute-done((bf16[136,384]{1,0:T(8,128)(2,1)S(1)}, bf16[136,384]{1,0:T(8,128)(2,1)S(1)}, u32[]{:S(2)}, u32[]{:S(2)}) %collective-permute-start.9) | collective-permute-done | bytes 104480 | tf_op jit(solution)/shard_map/ppermute | solution.py:451
  74.0 0.9 collective-permute-start.11
  74.9 2.2 %collective-permute-start.15 = (bf16[128,1536]{1,0:T(8,128)(2,1)S(1)}, bf16[128,1536]{1,0:T(8,128)(2,1)S(1)}, u32[]{:S(2)}, u32[]{:S(2)}) collective-permute-start(bf16[128,1536]{1,0:T(8,128)(2,1)S(1)} %slice.40.attn_ref.refs_5_), channel_id=1, source_target_pairs={{0,24},{8,16},{16,8},{24,0},{1,25},{9,17},{17,9},{25,1},{2,26},{10... | collective-permute-start | bytes 1179656 | tf_op jit(solution)/shard_map/ppermute | solution.py:458
  77.6 0.7 broadcast_compare_fusion
  78.3 1.0 collective-permute-start.12
  79.3 3.7 %copy-done = bf16[3072,1536]{1,0:T(8,128)(2,1)S(1)} copy-done((bf16[3072,1536]{1,0:T(8,128)(2,1)S(1)}, bf16[3072,1536]{1,0:T(8,128)(2,1)}, u32[]{:S(2)}) %copy-start) | copy-done | bytes 9437208
  82.9 4.6 %shard_map.170 = (bf16[128,3072]{1,0:T(8,128)(2,1)}, f32[4,384]{1,0:T(4,128)S(1)}, f32[4,384]{1,0:T(4,128)S(1)}) custom-call(s32[3]{0:T(128)S(1)} %pad_add_fusion.meta_ref, bf16[128,1536]{1,0:T(8,128)(2,1)S(1)} %slice.40.attn_ref.refs_5_, bf16[3072,1536]{1,0:T(8,128)(2,1)S(1)} %copy-done, f32[1,3072]{1,0:T(1,128)S(1)} %copy-done.10, ...), custom_call_target="tpu_custom_call" | custom-call | flops 1207959552 | bytes 9437184 | tf_op jit(solution)/shard_map/pallas_call | solution.py:373
  88.0 7.4 %collective-permute-done.14.refs_7_ = bf16[128,1536]{1,0:T(8,128)(2,1)} collective-permute-done((bf16[128,1536]{1,0:T(8,128)(2,1)S(1)}, bf16[128,1536]{1,0:T(8,128)(2,1)}, u32[]{:S(2)}, u32[]{:S(2)}) %collective-permute-start.14) | collective-permute-done | bytes 393248 | tf_op jit(solution)/shard_map/ppermute | solution.py:458
  96.0 2.2 %shard_map.171 = bf16[128,1536]{1,0:T(8,128)(2,1)} custom-call(f32[1,3072]{1,0:T(1,128)S(1)} %copy-done.10, bf16[128,3072]{1,0:T(8,128)(2,1)S(1)} %bitcast.21, bf16[3072,1536]{1,0:T(8,128)(2,1)S(1)} %copy-done), custom_call_target="tpu_custom_call" | custom-call | flops 1207959552 | bytes 9437184 | tf_op jit(solution)/shard_map/pallas_call | solution.py:315
  98.9 2.7 %collective-permute-done.23 = f32[2,384]{1,0:T(2,128)S(1)} collective-permute-done((f32[2,384]{1,0:T(2,128)S(1)}, f32[2,384]{1,0:T(2,128)S(1)}, u32[]{:S(2)}, u32[]{:S(2)}) %collective-permute-start.23) | collective-permute-done | bytes 3104 | tf_op jit(solution)/shard_map/ppermute | solution.py:451
  102.1 3.0 %shard_map.173 = (f32[96,1536]{1,0:T(8,128)S(1)}, bf16[96,1536]{1,0:T(8,128)(2,1)S(1)}, bf16[96,1536]{1,0:T(8,128)(2,1)S(1)}, bf16[96,1536]{1,0:T(8,128)(2,1)S(1)}) custom-call(bf16[1,4,96,128]{3,2,1,0:T(8,128)(2,1)S(1)} %slice.32.refs_0_, bf16[1,4,96,128]{3,2,1,0:T(8,128)(2,1)S(1)} %slice.42.refs_1_, bf16[1,4,96,128]{3,2,1,0:T(8,128)(2,1)S(1)} %slice.43.refs_2_, ...), custom_call_target="tpu_custom_call" | custom-call | flops 1207959552 | bytes 5111808 | tf_op jit(solution)/shard_map/pallas_call | solution.py:409
  105.1 1.0 collective-permute-start.19
  106.0 1.3 %collective-permute-start.20 = (bf16[96,1536]{1,0:T(8,128)(2,1)S(1)}, bf16[96,1536]{1,0:T(8,128)(2,1)S(1)}, u32[]{:S(2)}, u32[]{:S(2)}) collective-permute-start(bf16[96,1536]{1,0:T(8,128)(2,1)S(1)} %get-tuple-element.53), channel_id=1, source_target_pairs={{0,6},{2,4},{4,2},{6,0},{1,7},{3,5},{5,3},{7,1},{8,14},{10,12},{12... | collective-permute-start | bytes 884744 | tf_op jit(solution)/shard_map/ppermute | solution.py:451
  107.4 1.3 collective-permute-start.21
  108.7 1.4 %fusion = bf16[1,8,1536]{2,1,0:T(8,128)(2,1)} fusion(bf16[136,1536]{1,0:T(8,128)(2,1)} %copy-done.22, pred[8]{0:T(512)(128)(4,1)S(1)} %fusion.1), kind=kLoop, calls=%fused_computation.6 | loop fusion | flops 12288 | bytes 49160 | tf_op jit(solution)/shard_map/broadcast_in_dim | solution.py:525
  110.7 14.4 %collective-permute-done.19 = bf16[96,1536]{1,0:T(8,128)(2,1)S(1)} collective-permute-done((bf16[96,1536]{1,0:T(8,128)(2,1)S(1)}, bf16[96,1536]{1,0:T(8,128)(2,1)S(1)}, u32[]{:S(2)}, u32[]{:S(2)}) %collective-permute-start.19) | collective-permute-done | bytes 294944 | tf_op jit(solution)/shard_map/ppermute | solution.py:451
  125.0 8.7 %collective-permute-done.20 = bf16[96,1536]{1,0:T(8,128)(2,1)S(1)} collective-permute-done((bf16[96,1536]{1,0:T(8,128)(2,1)S(1)}, bf16[96,1536]{1,0:T(8,128)(2,1)S(1)}, u32[]{:S(2)}, u32[]{:S(2)}) %collective-permute-start.20) | collective-permute-done | bytes 294944 | tf_op jit(solution)/shard_map/ppermute | solution.py:451
  133.8 0.9 convert_add_fusion
  (82 shorter events, 6.8 us)
Async XLA Ops:
  1.4 2.3 %copy-start.3 = (bf16[512,4608]{1,0:T(8,128)(2,1)S(1)}, bf16[512,4608]{1,0:T(8,128)(2,1)}, u32[]{:S(2)}) copy-start(bf16[512,4608]{1,0:T(8,128)(2,1)} %w_ref.3) | copy-start | bytes 14155780
  3.7 0.8 copy-start.11
  4.6 0.7 copy-start.14
  5.3 0.7 copy-start.17
  5.9 73.3 %copy-start.2 = (bf16[1,128,3072]{2,1,0:T(8,128)(2,1)S(1)}, bf16[1,128,3072]{2,1,0:T(8,128)(2,1)}, u32[]{:S(2)}) copy-start(bf16[1,128,3072]{2,1,0:T(8,128)(2,1)} %param.25) | copy-start | bytes 2359300
  5.9 73.3 %copy-start.10 = (f32[1,3072]{1,0:T(1,128)S(1)}, f32[1,3072]{1,0:T(1,128)}, u32[]{:S(2)}) copy-start(f32[1,3072]{1,0:T(1,128)} %gate_ref.5) | copy-start | bytes 36868
  7.5 2.0 %copy-start.20 = (f32[1,64]{1,0:T(1,128)}, f32[1,64]{1,0:T(1,128)S(1)}, u32[]{:S(2)}) copy-start(f32[1,64]{1,0:T(1,128)S(1)} %get-tuple-element.43.refs_7_) | copy-start | bytes 772
  7.5 2.0 %collective-permute-start = (bf16[4,320,128]{2,1,0:T(8,128)(2,1)S(1)}, bf16[4,320,128]{2,1,0:T(8,128)(2,1)S(1)}, u32[]{:S(2)}, u32[]{:S(2)}) collective-permute-start(bf16[4,320,128]{2,1,0:T(8,128)(2,1)S(1)} %get-tuple-element.32), channel_id=1, source_target_pairs={{0,1},{2,3},{4,5},{6,7},{1,0},{3,2},{5,4},{7,6},{8,9},{10,11},{12,... | collective-permute-start | bytes 983048 | tf_op jit(solution)/shard_map/ppermute | solution.py:455
  9.5 1.0 copy-start.4
  10.5 1.0 copy-start.5
  11.5 1.0 copy-start.6
  13.4 36.9 %copy-start.7 = (bf16[1152,128]{1,0:T(8,128)(2,1)}, bf16[1152,128]{1,0:T(8,128)(2,1)S(1)}, u32[]{:S(2)}) copy-start(bf16[1152,128]{1,0:T(8,128)(2,1)S(1)} %get-tuple-element.33.refs_0_) | copy-start | bytes 884740
  13.4 15.6 %collective-permute-start.1 = (bf16[1472,128]{1,0:T(8,128)(2,1)S(1)}, bf16[1472,128]{1,0:T(8,128)(2,1)S(1)}, u32[]{:S(2)}, u32[]{:S(2)}) collective-permute-start(bf16[1472,128]{1,0:T(8,128)(2,1)S(1)} %get-tuple-element.34), channel_id=1, source_target_pairs={{0,2},{2,0},{4,6},{6,4},{1,3},{3,1},{5,7},{7,5},{8,10},{10,8},{12,... | collective-permute-start | bytes 1130504 | tf_op jit(solution)/shard_map/ppermute | solution.py:451
  13.5 19.1 %collective-permute-start.2 = (bf16[1472,128]{1,0:T(8,128)(2,1)S(1)}, bf16[1472,128]{1,0:T(8,128)(2,1)S(1)}, u32[]{:S(2)}, u32[]{:S(2)}) collective-permute-start(bf16[1472,128]{1,0:T(8,128)(2,1)S(1)} %get-tuple-element.35), channel_id=1, source_target_pairs={{0,4},{2,6},{4,0},{6,2},{1,5},{3,7},{5,1},{7,3},{8,12},{10,14},{12... | collective-permute-start | bytes 1130504 | tf_op jit(solution)/shard_map/ppermute | solution.py:451
  15.9 32.7 %collective-permute-start.3 = (bf16[1472,128]{1,0:T(8,128)(2,1)S(1)}, bf16[1472,128]{1,0:T(8,128)(2,1)S(1)}, u32[]{:S(2)}, u32[]{:S(2)}) collective-permute-start(bf16[1472,128]{1,0:T(8,128)(2,1)S(1)} %get-tuple-element.36), channel_id=1, source_target_pairs={{0,6},{2,4},{4,2},{6,0},{1,7},{3,5},{5,3},{7,1},{8,14},{10,12},{12... | collective-permute-start | bytes 1130504 | tf_op jit(solution)/shard_map/ppermute | solution.py:451
  16.1 1.1 copy-start.1
  17.2 0.7 copy-start.9
  18.9 31.4 %collective-permute-start.4 = (bf16[2,4,96,128]{3,2,1,0:T(8,128)(2,1)S(1)}, bf16[2,4,96,128]{3,2,1,0:T(8,128)(2,1)S(1)}, u32[]{:S(2)}, u32[]{:S(2)}) collective-permute-start(bf16[2,4,96,128]{3,2,1,0:T(8,128)(2,1)S(1)} %get-tuple-element.40), channel_id=1, source_target_pairs={{0,8},{8,0},{16,24},{24,16},{1,9},{9,1},{17,25},{25,17},{2,10},{10... | collective-permute-start | bytes 589832 | tf_op jit(solution)/shard_map/ppermute | solution.py:458
  20.1 30.1 %collective-permute-start.5 = (bf16[2,4,96,128]{3,2,1,0:T(8,128)(2,1)S(1)}, bf16[2,4,96,128]{3,2,1,0:T(8,128)(2,1)S(1)}, u32[]{:S(2)}, u32[]{:S(2)}) collective-permute-start(bf16[2,4,96,128]{3,2,1,0:T(8,128)(2,1)S(1)} %get-tuple-element.41), channel_id=1, source_target_pairs={{0,16},{8,24},{16,0},{24,8},{1,17},{9,25},{17,1},{25,9},{2,18},{10... | collective-permute-start | bytes 589832 | tf_op jit(solution)/shard_map/ppermute | solution.py:458
  29.0 21.2 %collective-permute-start.6 = (bf16[2,4,96,128]{3,2,1,0:T(8,128)(2,1)S(1)}, bf16[2,4,96,128]{3,2,1,0:T(8,128)(2,1)S(1)}, u32[]{:S(2)}, u32[]{:S(2)}) collective-permute-start(bf16[2,4,96,128]{3,2,1,0:T(8,128)(2,1)S(1)} %get-tuple-element.42), channel_id=1, source_target_pairs={{0,24},{8,16},{16,8},{24,0},{1,25},{9,17},{17,9},{25,1},{2,26},{10... | collective-permute-start | bytes 589832 | tf_op jit(solution)/shard_map/ppermute | solution.py:458
  48.6 0.7 copy-start.15
  49.3 0.7 copy-start.16
  50.2 0.6 copy-start.12
  50.2 0.6 copy-start.18
  50.8 3.6 %collective-permute-start.7 = (bf16[3264,128]{1,0:T(8,128)(2,1)S(1)}, bf16[3264,128]{1,0:T(8,128)(2,1)}, u32[]{:S(2)}, u32[]{:S(2)}) collective-permute-start(bf16[3264,128]{1,0:T(8,128)(2,1)S(1)} %shard_map.168), channel_id=1, source_target_pairs={{0,1},{2,3},{4,5},{6,7},{1,0},{3,2},{5,4},{7,6},{8,9},{10,11},{12,... | collective-permute-start | bytes 2506760 | tf_op jit(solution)/shard_map/ppermute | solution.py:455
  54.4 1.0 copy-start.8
  55.4 0.8 copy-start.13
  56.2 0.7 copy-start.19
  56.9 0.7 copy-start.21
  62.7 5.1 %collective-permute-start.8 = (bf16[136,384]{1,0:T(8,128)(2,1)S(1)}, bf16[136,384]{1,0:T(8,128)(2,1)S(1)}, u32[]{:S(2)}, u32[]{:S(2)}) collective-permute-start(bf16[136,384]{1,0:T(8,128)(2,1)S(1)} %pad_maximum_fusion), channel_id=1, source_target_pairs={{0,4},{2,6},{4,0},{6,2},{1,5},{3,7},{5,1},{7,3},{8,12},{10,14},{12... | collective-permute-start | bytes 313352 | tf_op jit(solution)/shard_map/ppermute | solution.py:451
  62.8 11.0 %collective-permute-start.9 = (bf16[136,384]{1,0:T(8,128)(2,1)S(1)}, bf16[136,384]{1,0:T(8,128)(2,1)S(1)}, u32[]{:S(2)}, u32[]{:S(2)}) collective-permute-start(bf16[136,384]{1,0:T(8,128)(2,1)S(1)} %pad_maximum_fusion.1), channel_id=1, source_target_pairs={{0,6},{2,4},{4,2},{6,0},{1,7},{3,5},{5,3},{7,1},{8,14},{10,12},{12... | collective-permute-start | bytes 313352 | tf_op jit(solution)/shard_map/ppermute | solution.py:451
  64.2 9.7 %collective-permute-start.10 = (bf16[136,384]{1,0:T(8,128)(2,1)S(1)}, bf16[136,384]{1,0:T(8,128)(2,1)S(1)}, u32[]{:S(2)}, u32[]{:S(2)}) collective-permute-start(bf16[136,384]{1,0:T(8,128)(2,1)S(1)} %pad_maximum_fusion.2), channel_id=1, source_target_pairs={{0,2},{2,0},{4,6},{6,4},{1,3},{3,1},{5,7},{7,5},{8,10},{10,8},{12,... | collective-permute-start | bytes 313352 | tf_op jit(solution)/shard_map/ppermute | solution.py:451
  73.9 4.3 %copy-start.22 = (bf16[136,1536]{1,0:T(8,128)(2,1)}, bf16[136,1536]{1,0:T(8,128)(2,1)S(1)}, u32[]{:S(2)}) copy-start(bf16[136,1536]{1,0:T(8,128)(2,1)S(1)} %maximum_dynamic-update-slice_fusion) | copy-start | bytes 1253380
  74.0 5.3 %collective-permute-start.11 = (bf16[128,1536]{1,0:T(8,128)(2,1)S(1)}, bf16[128,1536]{1,0:T(8,128)(2,1)S(1)}, u32[]{:S(2)}, u32[]{:S(2)}) collective-permute-start(bf16[128,1536]{1,0:T(8,128)(2,1)S(1)} %slice.40.attn_ref.refs_5_), channel_id=1, source_target_pairs={{0,1},{2,3},{4,5},{6,7},{1,0},{3,2},{5,4},{7,6},{8,9},{10,11},{12,... | collective-permute-start | bytes 1179656 | tf_op jit(solution)/shard_map/ppermute | solution.py:455
  74.9 12.7 %collective-permute-start.15 = (bf16[128,1536]{1,0:T(8,128)(2,1)S(1)}, bf16[128,1536]{1,0:T(8,128)(2,1)S(1)}, u32[]{:S(2)}, u32[]{:S(2)}) collective-permute-start(bf16[128,1536]{1,0:T(8,128)(2,1)S(1)} %slice.40.attn_ref.refs_5_), channel_id=1, source_target_pairs={{0,24},{8,16},{16,8},{24,0},{1,25},{9,17},{17,9},{25,1},{2,26},{10... | collective-permute-start | bytes 1179656 | tf_op jit(solution)/shard_map/ppermute | solution.py:458
  77.1 18.3 %collective-permute-start.14 = (bf16[128,1536]{1,0:T(8,128)(2,1)S(1)}, bf16[128,1536]{1,0:T(8,128)(2,1)}, u32[]{:S(2)}, u32[]{:S(2)}) collective-permute-start(bf16[128,1536]{1,0:T(8,128)(2,1)S(1)} %slice.40.attn_ref.refs_5_), channel_id=1, source_target_pairs={{0,16},{8,24},{16,0},{24,8},{1,17},{9,25},{17,1},{25,9},{2,18},{10... | collective-permute-start | bytes 1179656 | tf_op jit(solution)/shard_map/ppermute | solution.py:458
  77.3 18.6 %collective-permute-start.13 = (bf16[128,1536]{1,0:T(8,128)(2,1)S(1)}, bf16[128,1536]{1,0:T(8,128)(2,1)}, u32[]{:S(2)}, u32[]{:S(2)}) collective-permute-start(bf16[128,1536]{1,0:T(8,128)(2,1)S(1)} %slice.40.attn_ref.refs_5_), channel_id=1, source_target_pairs={{0,8},{8,0},{16,24},{24,16},{1,9},{9,1},{17,25},{25,17},{2,10},{10... | collective-permute-start | bytes 1179656 | tf_op jit(solution)/shard_map/ppermute | solution.py:458
  78.3 23.8 %collective-permute-start.12 = (bf16[4,4,96,128]{3,2,1,0:T(8,128)(2,1)S(1)}, bf16[4,4,96,128]{3,2,1,0:T(8,128)(2,1)}, u32[]{:S(2)}, u32[]{:S(2)}) collective-permute-start(bf16[4,4,96,128]{3,2,1,0:T(8,128)(2,1)S(1)} %shard_map.172), channel_id=1, source_target_pairs={{0,1},{2,3},{4,5},{6,7},{1,0},{3,2},{5,4},{7,6},{8,9},{10,11},{12,... | collective-permute-start | bytes 1179656 | tf_op jit(solution)/shard_map/ppermute | solution.py:455
  79.2 3.7 %copy-start = (bf16[3072,1536]{1,0:T(8,128)(2,1)S(1)}, bf16[3072,1536]{1,0:T(8,128)(2,1)}, u32[]{:S(2)}) copy-start(bf16[3072,1536]{1,0:T(8,128)(2,1)} %w_ref.5) | copy-start | bytes 28311556
  87.5 10.6 %collective-permute-start.22 = (f32[4,384]{1,0:T(4,128)S(1)}, f32[4,384]{1,0:T(4,128)S(1)}, u32[]{:S(2)}, u32[]{:S(2)}) collective-permute-start(f32[4,384]{1,0:T(4,128)S(1)} %get-tuple-element.56), channel_id=1, source_target_pairs={{0,1},{2,3},{4,5},{6,7},{1,0},{3,2},{5,4},{7,6},{8,9},{10,11},{12,... | collective-permute-start | bytes 18440 | tf_op jit(solution)/shard_map/ppermute | solution.py:455
  87.6 14.5 %collective-permute-start.18 = (bf16[128,1536]{1,0:T(8,128)(2,1)S(1)}, bf16[128,1536]{1,0:T(8,128)(2,1)}, u32[]{:S(2)}, u32[]{:S(2)}) collective-permute-start(bf16[128,1536]{1,0:T(8,128)(2,1)S(1)} %collective-permute-done.15.refs_8_), channel_id=1, source_target_pairs={{0,1},{2,3},{4,5},{6,7},{1,0},{3,2},{5,4},{7,6},{8,9},{10,11},{12,... | collective-permute-start | bytes 1179656 | tf_op jit(solution)/shard_map/ppermute | solution.py:455
  95.4 6.6 %collective-permute-start.17 = (bf16[128,1536]{1,0:T(8,128)(2,1)}, bf16[128,1536]{1,0:T(8,128)(2,1)}, u32[]{:S(2)}, u32[]{:S(2)}) collective-permute-start(bf16[128,1536]{1,0:T(8,128)(2,1)} %collective-permute-done.14.refs_7_), channel_id=1, source_target_pairs={{0,1},{2,3},{4,5},{6,7},{1,0},{3,2},{5,4},{7,6},{8,9},{10,11},{12,... | collective-permute-start | bytes 1179656 | tf_op jit(solution)/shard_map/ppermute | solution.py:455
  95.9 6.2 %collective-permute-start.16 = (bf16[128,1536]{1,0:T(8,128)(2,1)}, bf16[128,1536]{1,0:T(8,128)(2,1)}, u32[]{:S(2)}, u32[]{:S(2)}) collective-permute-start(bf16[128,1536]{1,0:T(8,128)(2,1)} %collective-permute-done.13.refs_6_), channel_id=1, source_target_pairs={{0,1},{2,3},{4,5},{6,7},{1,0},{3,2},{5,4},{7,6},{8,9},{10,11},{12,... | collective-permute-start | bytes 1179656 | tf_op jit(solution)/shard_map/ppermute | solution.py:455
  98.2 3.4 %collective-permute-start.23 = (f32[2,384]{1,0:T(2,128)S(1)}, f32[2,384]{1,0:T(2,128)S(1)}, u32[]{:S(2)}, u32[]{:S(2)}) collective-permute-start(f32[2,384]{1,0:T(2,128)S(1)} %slice.46), channel_id=1, source_target_pairs={{0,4},{2,6},{4,0},{6,2},{1,5},{3,7},{5,1},{7,3},{8,12},{10,14},{12... | collective-permute-start | bytes 9224 | tf_op jit(solution)/shard_map/ppermute | solution.py:451
  101.6 8.5 %collective-permute-start.24 = (f32[1,384]{1,0:T(1,128)S(1)}, f32[1,384]{1,0:T(1,128)S(1)}, u32[]{:S(2)}, u32[]{:S(2)}) collective-permute-start(f32[1,384]{1,0:T(1,128)S(1)} %slice.48), channel_id=1, source_target_pairs={{0,2},{2,0},{4,6},{6,4},{1,3},{3,1},{5,7},{7,5},{8,10},{10,8},{12,... | collective-permute-start | bytes 4616 | tf_op jit(solution)/shard_map/ppermute | solution.py:451
  105.1 20.0 %collective-permute-start.19 = (bf16[96,1536]{1,0:T(8,128)(2,1)S(1)}, bf16[96,1536]{1,0:T(8,128)(2,1)S(1)}, u32[]{:S(2)}, u32[]{:S(2)}) collective-permute-start(bf16[96,1536]{1,0:T(8,128)(2,1)S(1)} %get-tuple-element.52), channel_id=1, source_target_pairs={{0,4},{2,6},{4,0},{6,2},{1,5},{3,7},{5,1},{7,3},{8,12},{10,14},{12... | collective-permute-start | bytes 884744 | tf_op jit(solution)/shard_map/ppermute | solution.py:451
  106.0 27.7 %collective-permute-start.20 = (bf16[96,1536]{1,0:T(8,128)(2,1)S(1)}, bf16[96,1536]{1,0:T(8,128)(2,1)S(1)}, u32[]{:S(2)}, u32[]{:S(2)}) collective-permute-start(bf16[96,1536]{1,0:T(8,128)(2,1)S(1)} %get-tuple-element.53), channel_id=1, source_target_pairs={{0,6},{2,4},{4,2},{6,0},{1,7},{3,5},{5,3},{7,1},{8,14},{10,12},{12... | collective-permute-start | bytes 884744 | tf_op jit(solution)/shard_map/ppermute | solution.py:451
  107.4 26.4 %collective-permute-start.21 = (bf16[96,1536]{1,0:T(8,128)(2,1)S(1)}, bf16[96,1536]{1,0:T(8,128)(2,1)S(1)}, u32[]{:S(2)}, u32[]{:S(2)}) collective-permute-start(bf16[96,1536]{1,0:T(8,128)(2,1)S(1)} %get-tuple-element.54), channel_id=1, source_target_pairs={{0,2},{2,0},{4,6},{6,4},{1,3},{3,1},{5,7},{7,5},{8,10},{10,8},{12,... | collective-permute-start | bytes 884744 | tf_op jit(solution)/shard_map/ppermute | solution.py:451

commit v6 on v5

v6 whole, which is shorter than its diff:
```python
import math
import functools
import jax
import jax.numpy as jnp
from jax import lax
from jax.experimental import pallas as pl
from jax.experimental.pallas import tpu as pltpu
from jax.sharding import PartitionSpec as P

DT5 = 4096
CORES = 2
GROUPS = 4

eps_norm = 1e-06
f32 = jnp.float32
bf16 = jnp.bfloat16
EXTRA = 16


VMEM = pl.BlockSpec(memory_space=pltpu.VMEM)
SMEM = pl.BlockSpec(memory_space=pltpu.SMEM)
ANY = pl.BlockSpec(memory_space=pl.ANY)


def params(mib=24):
    return pltpu.CompilerParams(vmem_limit_bytes=int(mib * 1024 * 1024))


def cost(flops, bytes_accessed, transcendentals=0):
    return pl.CostEstimate(
        flops=flops, bytes_accessed=bytes_accessed, transcendentals=transcendentals
    )


def split_tail(squares, width):
    high = squares.astype(bf16).astype(f32)
    low = squares - high
    lane = lax.broadcasted_iota(jnp.int32, (squares.shape[0], width), 1)
    return jnp.where(lane == 0, high, jnp.where(lane == 1, low, 0.0))


def joined(tail):
    return tail[:, 0:1] + tail[:, 1:2]


def text_kernel(
    groups, heads, place_of, meta_ref, len_ref, src_ref, states_ref, gain_ref, qg_ref, kg_ref,
    w_ref, k_ref, v_ref, q_ref, own_ref, *refs
):
    packed, refs = refs[:groups], refs[groups:]
    msgs, (w_all, w_sems, pack_sems) = refs[:-3], refs[-3:]
    size = own_ref.shape[2]
    rows = (own_ref.shape[1] - EXTRA) // (3 * heads + 1)
    width = heads * size
    slots = states_ref.shape[0]
    slot_local = rows // groups
    copies = []
    for g in range(groups):
        for i in range(3):
            at = (i * groups + (meta_ref[0] ^ g)) * width
            cols = pl.ds(pl.multiple_of(at, 128), width)
            copies.append(pltpu.make_async_copy(w_ref.at[:, cols], w_all.at[g, i], w_sems.at[g, i]))
            copies[-1].start()
    packs = []
    local = k_ref.shape[0]
    for g, out in enumerate(packed):
        for i, ref in enumerate((k_ref, v_ref, q_ref)):
            for head in range(heads):
                at = ((meta_ref[0] ^ g) * heads + head) * size
                source = ref.at[:, pl.ds(pl.multiple_of(at, 128), size)]
                target = out.at[pl.ds((i * heads + head) * local, local), :]
                sem = pack_sems.at[g, i * heads + head]
                packs.append(pltpu.make_async_copy(source, target, sem))
                packs[-1].start()

    def slot_at(row):
        z_at = (row % rows) // slot_local
        return place_of(meta_ref[1] ^ (row // rows), z_at) * slot_local + row % slot_local

    iota = functools.partial(lax.broadcasted_iota, jnp.int32, (slots, slots))
    sources = src_ref[...].astype(f32)
    chosen = (iota(1) == slot_at(iota(0))).astype(f32)
    source_col = jnp.sum(chosen * sources, axis=1, keepdims=True)
    pick = (iota(1).astype(f32) == source_col).astype(bf16)
    chosen_t = (iota(0) == slot_at(iota(1))).astype(bf16)
    source_row = jnp.dot(sources.astype(bf16), chosen_t, preferred_element_type=f32)
    bias = jnp.where(source_row < len_ref[0].astype(f32), 0.0, -1e30)
    end = own_ref.shape[1] - EXTRA
    own_ref[0, end:, :] = jnp.zeros((EXTRA, size), f32)
    own_ref[0, end : end + 1, :] = qg_ref[...]
    own_ref[0, end + 1 : end + 2, :] = kg_ref[...]
    own_ref[0, end + 2 : end + 3, :slots] = bias

    picked = jnp.dot(pick, states_ref[...], preferred_element_type=f32)
    scaled = (picked * gain_ref[...]).astype(bf16)
    tail = split_tail(jnp.sum(picked * picked, axis=1, keepdims=True), size)
    for g in range(groups):
        for i in range(3):
            copies[3 * g + i].wait()
            got = jnp.dot(scaled, w_all[g, i], preferred_element_type=f32)
            for head in range(heads):
                part = got[:, head * size : (head + 1) * size]
                to = slice((i * heads + head) * rows, (i * heads + head + 1) * rows)
                own_ref[g, to, :] = part[:rows]
                for j, msg in enumerate(msgs):
                    msg[g, to, :] = part[(j + 1) * rows : (j + 2) * rows].astype(bf16)
        own_ref[g, 3 * heads * rows : end, :] = tail[:rows]
        for j, msg in enumerate(msgs):
            msg[g, 3 * heads * rows :, :] = tail[(j + 1) * rows : (j + 2) * rows].astype(bf16)
    for copy in packs:
        copy.wait()


def text_project(
    meta, length, sources, states, gain, query_gain, key_gain, text_proj, keys, values, queries,
    groups, parts, place_of
):
    slots, depth = states.shape
    size = query_gain.shape[1]
    local = keys.shape[0]
    heads = text_proj.shape[1] // (3 * groups * size)
    text_rows = (3 * heads + 1) * slots // parts
    shapes = [jax.ShapeDtypeStruct((groups, text_rows + EXTRA, size), f32)]
    for g in range(groups):
        rows = 3 * heads * local + (text_rows if g else 0)
        shapes.append(jax.ShapeDtypeStruct((rows, size), bf16))
    shapes += [jax.ShapeDtypeStruct((groups, text_rows, size), bf16)] * (parts - 1)
    return pl.pallas_call(
        functools.partial(text_kernel, groups, heads, place_of),
        out_shape=shapes,
        in_specs=[SMEM, SMEM] + [VMEM] * 5 + [ANY] * 4,
        out_specs=[VMEM] + [ANY] * groups + [VMEM] * (parts - 1),
        scratch_shapes=[
            pltpu.VMEM((groups, 3, depth, heads * size), bf16),
            pltpu.SemaphoreType.DMA((groups, 3)),
            pltpu.SemaphoreType.DMA((groups, 3 * heads)),
        ],
        compiler_params=params(60),
        cost_estimate=cost(
            2 * slots * depth * text_proj.shape[1], 2 * depth * text_proj.shape[1]
        ),
    )(
        meta, length, sources, states, gain, query_gain, key_gain, text_proj, keys, values, queries
    )


def pack_kernel(n_got, n_out, tail_rows, *refs):
    own_ref, got, refs = refs[0], refs[1 : 1 + n_got], refs[1 + n_got + n_out :]
    kept_ref, outs, (stage, sems) = refs[0], refs[1 : 1 + n_out], refs[1 + n_out :]
    text_rows, size = stage.shape[1:]
    copies = []
    for g in list(range(1, n_out + 1)) + [0]:
        total = own_ref[g, :text_rows, :]
        for ref in got:
            total = total + ref[g].astype(f32)
        tail = split_tail(joined(total[text_rows - tail_rows :]), size)
        total = jnp.concatenate([total[: text_rows - tail_rows], tail], axis=0)
        if g == 0:
            kept_ref[:text_rows, :] = total
            kept_ref[text_rows:, :] = own_ref[0, text_rows:, :]
        else:
            stage[g - 1] = total.astype(bf16)
            start = outs[g - 1].shape[0] - text_rows
            target = outs[g - 1].at[pl.ds(start, text_rows), :]
            copies.append(pltpu.make_async_copy(stage.at[g - 1], target, sems.at[g - 1]))
            copies[-1].start()
    for copy in copies:
        copy.wait()


def pack(own, got, packed, tail_rows):
    groups, rows, size = own.shape
    text_rows = rows - EXTRA
    n = len(packed)
    shapes = [jax.ShapeDtypeStruct((rows, size), f32)]
    shapes += [jax.ShapeDtypeStruct(p.shape, bf16) for p in packed]
    return pl.pallas_call(
        functools.partial(pack_kernel, len(got), n, tail_rows),
        out_shape=shapes,
        in_specs=[VMEM] * (1 + len(got)) + [ANY] * n,
        out_specs=[VMEM] + [ANY] * n,
        input_output_aliases={1 + len(got) + i: 1 + i for i in range(n)},
        scratch_shapes=[pltpu.VMEM((n, text_rows, size), bf16), pltpu.SemaphoreType.DMA((n,))],
        compiler_params=params(60),
        cost_estimate=cost(0, 8 * groups * rows * size),
    )(own, *got, *packed)


def block_kernel(features, heads, n_got, near_ref, own_hbm, *refs):
    got, (out_ref, _, _, own_ref, sems) = refs[:n_got], refs[-5:]
    size = own_ref.shape[1]
    image_rows = near_ref.shape[0]
    copies = [
        pltpu.make_async_copy(own_hbm, own_ref, sems.at[0]),
        pltpu.make_async_copy(near_ref, out_ref.at[pl.ds(0, image_rows), :], sems.at[1]),
    ]
    for copy in copies:
        copy.start()
    kv_rows = image_rows // 3 * 2
    for k, ref in enumerate(got):
        at = image_rows + k * kv_rows
        out_ref[at : at + kv_rows, :] = ref[:kv_rows, :]
    copies[0].wait()
    text_rows = own_ref.shape[0] - EXTRA
    rows = text_rows // (3 * heads + 1)
    total = own_ref[:text_rows, :]
    for ref in got:
        total = total + ref[image_rows:, :].astype(f32)
    rate = lax.rsqrt(joined(total[3 * heads * rows :]) / features + eps_norm)
    end = image_rows + n_got * kv_rows
    for i in range(3):
        for head in range(heads):
            at = (i * heads + head) * rows
            x = total[at : at + rows] * rate
            if i < 2:
                mean = jnp.sum(x * x, axis=1, keepdims=True) / size
                gain = own_ref[text_rows + i : text_rows + i + 1, :]
                x = x * lax.rsqrt(mean + eps_norm) * gain
            out_ref[end + at : end + at + rows, :] = x.astype(bf16)
    bias = own_ref[text_rows + 2 : text_rows + 3, :]
    at = end + 3 * heads * rows
    out_ref[at:, :] = jnp.broadcast_to(bias, (EXTRA, size)).astype(bf16)
    copies[1].wait()


def block_of(near, own, got, after, features, heads):
    image_rows, size = near.shape
    text_rows = own.shape[0] - EXTRA
    total = image_rows + image_rows // 3 * 2 * len(got)
    total += text_rows // (3 * heads + 1) * 3 * heads + EXTRA
    return pl.pallas_call(
        functools.partial(block_kernel, features, heads, len(got)),
        out_shape=[
            jax.ShapeDtypeStruct((total, size), bf16),
            jax.ShapeDtypeStruct(near.shape, bf16),
            jax.ShapeDtypeStruct(own.shape, f32),
        ],
        in_specs=[ANY] * 2 + [VMEM] * len(got) + [ANY] * len(after),
        out_specs=[VMEM, ANY, ANY],
        input_output_aliases={0: 1, 1: 2},
        scratch_shapes=[pltpu.VMEM(own.shape, f32), pltpu.SemaphoreType.DMA((2,))],
        compiler_params=params(),
        cost_estimate=cost(0, 4 * total * size),
    )(near, own, *got, *after)[0]


def attention_kernel(n_far, n_blocks, heads, rows, text_rows, *refs):
    far, refs = refs[:n_far], refs[n_far:]
    blocks, refs = refs[:n_blocks], refs[n_blocks:]
    out_refs, tout_ref = refs[:-1], refs[-1]
    size = blocks[0].shape[1]
    factor = size ** (-0.5) * math.log2(math.e)
    nt = (((1,), (1,)), ((), ()))
    near = 3 * heads * rows
    kv_rows = 2 * heads * rows
    starts = [0] + [near + k * kv_rows for k in range(n_far)]
    text = near + n_far * kv_rows
    end = text + 3 * heads * text_rows
    bias = blocks[0][end : end + EXTRA, :][:1, : n_blocks * text_rows].astype(f32)

    def with_ones(values):
        return jnp.concatenate([values, jnp.ones(values.shape, bf16)], axis=1)

    for head in range(heads):
        kv, tkv = [], []
        for i in range(2):
            at = (i * heads + head) * rows
            text_at = text + ((i + 1) * heads + head) * text_rows
            image = [b[start + at : start + at + rows, :] for b in blocks for start in starts]
            kv.append(jnp.concatenate(image, axis=0))
            tkv.append(jnp.concatenate([b[text_at : text_at + text_rows, :] for b in blocks], axis=0))
        keys, values = kv[0], with_ones(kv[1])
        tkeys, tvalues = tkv[0], with_ones(tkv[1])
        cols = slice(head * size, (head + 1) * size)
        q_at = (2 * heads + head) * rows
        work = [
            (ref[q_at : q_at + rows, :], out) for ref, out in zip((blocks[0],) + far, out_refs)
        ]
        tq_at = text + head * text_rows
        work.append((blocks[0][tq_at : tq_at + text_rows, :], tout_ref))
        for q, out_ref in work:
            s_img = lax.dot_general(q, keys, nt, preferred_element_type=f32)
            s_txt = lax.dot_general(q, tkeys, nt, preferred_element_type=f32) + bias
            top = jnp.maximum(
                jnp.max(s_img, axis=1, keepdims=True), jnp.max(s_txt, axis=1, keepdims=True)
            )
            p_img = jnp.exp2((s_img - top) * factor).astype(bf16)
            p_txt = jnp.exp2((s_txt - top) * factor).astype(bf16)
            acc = jnp.dot(p_img, values, preferred_element_type=f32)
            acc = acc + jnp.dot(p_txt, tvalues, preferred_element_type=f32)
            out_ref[:, cols] = (acc[:, :size] / acc[:, size:]).astype(bf16)


def attention(far, blocks, heads, rows, text_rows):
    size = blocks[0].shape[1]
    queries = (1 + len(far)) * rows + text_rows
    keys = len(blocks) * queries
    shapes = [jax.ShapeDtypeStruct((rows, heads * size), bf16)] * (1 + len(far))
    shapes += [jax.ShapeDtypeStruct((text_rows, heads * size), bf16)]
    return pl.pallas_call(
        functools.partial(
            attention_kernel, len(far), len(blocks), heads, rows, text_rows
        ),
        out_shape=shapes,
        in_specs=[VMEM] * (len(far) + len(blocks)),
        out_specs=[VMEM] * len(shapes),
        compiler_params=params(),
        cost_estimate=cost(
            4 * queries * keys * heads * size,
            4 * (queries + keys) * heads * size,
            queries * keys * heads,
        ),
    )(*far, *blocks)


def gated_kernel(groups, parts, place_of, meta_ref, gate_ref, d_out_ref, *refs):
    msgs, turned = refs[:-1], refs[-1]
    gated = (gate_ref[...] * d_out_ref[...].astype(f32)).astype(bf16)
    turned[...] = gated.astype(f32).T
    rows = msgs[0].shape[2]
    z, oc, dp = meta_ref[0], meta_ref[1], meta_ref[2]
    for k, msg in enumerate(msgs):
        for j in range(parts):
            for g in range(groups):
                at = (dp ^ k) * (groups * parts) + place_of(oc ^ j, z ^ g)
                msg[j, g] = turned[pl.ds(pl.multiple_of(at * rows, 8), rows), :].astype(bf16)


def gated_parts(meta, gate, d_out, n_dp, groups, parts, place_of):
    local, model = d_out.shape
    rows = model // (n_dp * groups * parts)
    return pl.pallas_call(
        functools.partial(gated_kernel, groups, parts, place_of),
        out_shape=[jax.ShapeDtypeStruct((parts, groups, rows, local), bf16)] * n_dp,
        in_specs=[SMEM, VMEM, VMEM],
        out_specs=[VMEM] * n_dp,
        scratch_shapes=[pltpu.VMEM((model, local), f32)],
        compiler_params=params(60),
        cost_estimate=cost(0, 4 * local * model),
    )(meta, gate, d_out)


def d_attn_kernel(gate_ref, d_out_ref, w_ref, after_ref, out_ref):
    del after_ref
    block = 512
    total = jnp.zeros(out_ref.shape, f32)
    for at in range(0, w_ref.shape[0], block):
        cols = slice(at, at + block)
        gated = (gate_ref[:, cols] * d_out_ref[:, cols].astype(f32)).astype(bf16)
        total = total + jnp.dot(gated, w_ref[cols, :], preferred_element_type=f32)
    out_ref[...] = total.astype(bf16)


def attn_gradient(gate, d_out, out_weight, after):
    local, model = d_out.shape
    inner = out_weight.shape[1]
    return pl.pallas_call(
        d_attn_kernel,
        out_shape=jax.ShapeDtypeStruct((local, inner), bf16),
        in_specs=[VMEM] * 3 + [ANY],
        out_specs=VMEM,
        compiler_params=params(),
        cost_estimate=cost(2 * local * inner * model, 2 * inner * model),
    )(gate, d_out, out_weight, after)


def gather_kernel(n_dp, *refs):
    pieces, outs = refs[:n_dp], refs[n_dp:]
    for j, out in enumerate(outs):
        for k, piece in enumerate(pieces):
            out[k] = piece[j + 1]


def gather_parts(pieces):
    parts = pieces[0].shape[0]
    shape = (len(pieces),) + pieces[0].shape[1:]
    return pl.pallas_call(
        functools.partial(gather_kernel, len(pieces)),
        out_shape=[jax.ShapeDtypeStruct(shape, bf16)] * (parts - 1),
        in_specs=[VMEM] * len(pieces),
        out_specs=[VMEM] * (parts - 1),
        compiler_params=params(),
        cost_estimate=cost(0, 4 * math.prod(shape) * (parts - 1)),
    )(*pieces)


def project_kernel(
    groups, parts, place_of, meta_ref, attn_ref, w_ref, gate_ref, d_out_ref, out_ref, term_ref, *refs
):
    sent, by_place = refs[:-1], refs[-1]
    rows = attn_ref.shape[0]
    block = 512
    sums = []
    for at in range(0, w_ref.shape[0], block):
        cols = slice(at, at + block)
        got = lax.dot_general(
            attn_ref[...], w_ref[cols, :], (((1,), (1,)), ((), ())), preferred_element_type=f32
        )
        out_ref[:, cols] = (got * gate_ref[:, cols]).astype(bf16)
        sums.append(jnp.sum(got * d_out_ref[:, cols].astype(f32), axis=0, keepdims=True))
    sums = jnp.concatenate(sums, axis=1)
    places, width = by_place.shape
    for s in range(places):
        by_place[s : s + 1, :] = sums[:, s * width : (s + 1) * width]
    for g in range(groups):
        at = place_of(meta_ref[1], meta_ref[0] ^ g)
        term_ref[g : g + 1, :] = by_place[pl.ds(at, 1), :]
    for j, out in enumerate(sent):
        out[:rows, :] = attn_ref[...]
        line = [
            by_place[pl.ds(place_of(meta_ref[1] ^ (j + 1), meta_ref[0] ^ g), 1), :]
            for g in range(groups)
        ]
        line = jnp.concatenate(line, axis=1)
        line = jnp.concatenate(
            [line, jnp.zeros((1, attn_ref.shape[1] - groups * width), f32)], axis=1
        ) if attn_ref.shape[1] > groups * width else line
        high = line.astype(bf16).astype(f32)
        lines = [high, line - high, jnp.zeros((EXTRA - 2, line.shape[1]), f32)]
        out[rows:, :] = jnp.concatenate(lines, axis=0).astype(bf16)


def project(meta, attn, out_weight, gate, d_out, groups, parts, place_of):
    rows, inner = attn.shape
    model = out_weight.shape[0]
    width = model // (groups * parts)
    shapes = [jax.ShapeDtypeStruct((rows, model), bf16)]
    shapes += [jax.ShapeDtypeStruct((groups, width), f32)]
    shapes += [jax.ShapeDtypeStruct((rows + EXTRA, inner), bf16)] * (parts - 1)
    return pl.pallas_call(
        functools.partial(project_kernel, groups, parts, place_of),
        out_shape=shapes,
        in_specs=[SMEM, VMEM, VMEM, VMEM, VMEM],
        out_specs=[VMEM] * (1 + parts),
        scratch_shapes=[pltpu.VMEM((groups * parts, width), f32)],
        compiler_params=params(),
        cost_estimate=cost(2 * rows * inner * model, 2 * inner * model),
    )(meta, attn, out_weight, gate, d_out)


def grad_kernel(n_left, n_pieces, *refs):
    lefts, refs = refs[:n_left], refs[n_left:]
    pieces, refs = refs[:n_pieces], refs[n_pieces:]
    term_ref, outs, (kept_ref, sent_ref) = refs[0], refs[1:-2], refs[-2:]
    groups, rows, depth = lefts[0].shape[1:]
    width = pieces[0].shape[1]
    left = []
    for ref in lefts:
        left += [ref[i].reshape(groups * rows, depth) for i in range(ref.shape[0])]
    left = jnp.concatenate(left, axis=1)
    block = 256
    for start in range(0, width, block):
        right = jnp.concatenate([p[:depth, start : start + block] for p in pieces], axis=0)
        got = jnp.dot(left, right, preferred_element_type=f32)
        for g, out in enumerate(outs):
            out[:, start : start + block] = got[g * rows : (g + 1) * rows].astype(out.dtype)
    term = term_ref[...]
    size = term.shape[1]
    for p in pieces:
        if p.shape[0] > depth:
            lines = p[depth:, :].astype(f32)
            line = lines[0:1, :] + lines[1:2, :]
            term = term + jnp.concatenate(
                [line[:, g * size : (g + 1) * size] for g in range(groups)], axis=0
            )
    kept_ref[...] = term[: groups // 2]
    sent_ref[...] = term[groups // 2 :]


def grad_product(lefts, pieces, term):
    groups, rows, depth = lefts[0].shape[1:]
    width = pieces[0].shape[1]
    total = groups * rows
    depth = depth * len(pieces)
    shapes = [jax.ShapeDtypeStruct((rows, width), f32)]
    shapes += [jax.ShapeDtypeStruct((rows, width), bf16)] * (groups - 1)
    shapes += [jax.ShapeDtypeStruct((groups // 2, term.shape[1]), f32)] * 2
    return pl.pallas_call(
        functools.partial(grad_kernel, len(lefts), len(pieces)),
        out_shape=shapes,
        in_specs=[VMEM] * (len(lefts) + len(pieces) + 1),
        out_specs=[VMEM] * len(shapes),
        compiler_params=params(),
        cost_estimate=cost(
            2 * total * depth * width, 2 * (total * depth + depth * width + total * width)
        ),
    )(*lefts, *pieces, term)


def on_device(
    caption_states,
    caption_gain,
    text_proj,
    caption_len,
    slot_source,
    query_gain,
    key_gain,
    image_q,
    image_k,
    image_v,
    out_weight,
    gate,
    d_out,
):
    n_dp = lax.axis_size("dp")
    n_seq = lax.axis_size("seq")
    G, C = GROUPS, CORES
    O = n_seq // (G * C)
    OC = O * C
    dp = lax.axis_index("dp")
    seq = lax.axis_index("seq")
    z = (seq // C) % G
    oc = (seq // (G * C)) * C + seq % C

    def place(oc_at, z_at):
        return ((oc_at // C) * G + z_at) * C + oc_at % C

    def to_z(x, k):
        perm = [(place(a, b), place(a, b ^ k)) for a in range(OC) for b in range(G)]
        return lax.ppermute(x, "seq", perm)

    def to_oc(x, j):
        perm = [(place(a, b), place(a ^ j, b)) for a in range(OC) for b in range(G)]
        return lax.ppermute(x, "seq", perm)

    def to_dp(x, k):
        return lax.ppermute(x, "dp", [(a, a ^ k) for a in range(n_dp)])

    def part(x, index, size, axis):
        return lax.dynamic_slice_in_dim(x, index * size, size, axis)

    slot_total = slot_source.shape[1]
    slot_local = slot_total // n_seq
    image_local = image_q.shape[1]
    inner_width = image_q.shape[2]
    model_width = out_weight.shape[0]
    head_size = query_gain.shape[0]
    gw = inner_width // G
    order = [2, 3, 1]
    meta = jnp.stack([z, oc, dp]).astype(jnp.int32)

    heads = gw // head_size
    text_rows = G * slot_local
    own, *rest = text_project(
        meta, caption_len, slot_source, caption_states[0], caption_gain[None],
        query_gain[None], key_gain[None], text_proj, image_k[0], image_v[0], image_q[0],
        G, OC, place,
    )
    packed, sent = rest[:G], rest[G:]
    got = [to_oc(x, j + 1) for j, x in enumerate(sent)]
    own, *messages = pack(own, got, packed[1:], text_rows)
    far = {k: to_z(messages[k - 1], k) for k in order}
    far = [far[k] for k in range(1, G)]

    gg = gated_parts(meta, gate, d_out[0], n_dp, G, OC, place)
    gg_dp = [gg[0]] + [to_dp(gg[k], k) for k in range(1, n_dp)]
    lefts = [g[:1] for g in gg_dp]
    lefts += [to_oc(g, j + 1) for j, g in enumerate(gather_parts(gg_dp))]

    block = block_of(packed[0], own, far, gg_dp[1:], DT5, heads)
    blocks = [block] + [to_oc(block, j) for j in range(1, OC)]
    *outs, text_out = attention(far, blocks, heads, image_local, text_rows)

    attn = jnp.zeros((image_local + slot_local, inner_width), bf16)
    for k in order + [0]:
        rows = jnp.concatenate([outs[k], part(text_out, z ^ k, slot_local, 0)], axis=0)
        rows = to_z(rows, k) if k else rows
        attn = lax.dynamic_update_slice_in_dim(attn, rows, (z ^ k) * gw, 1)
    image_attn = attn[:image_local]
    own_usable = part(slot_source[0] < caption_len[0], seq, slot_local, 0)
    text_attn = jnp.where(own_usable[:, None], attn[image_local:], jnp.zeros((), bf16))

    pieces = [image_attn] + [to_dp(image_attn, k) for k in range(1, n_dp)]
    image_out, term, *sent = project(
        meta, image_attn, out_weight, gate, d_out[0], G, OC, place
    )
    for j in range(1, OC):
        pieces += [to_oc(sent[j - 1], j)] + [to_oc(p, j) for p in pieces[1:n_dp]]
    *grads, kept, sent = grad_product(lefts, pieces, term)
    grad_wo = grads[0]
    for k in order:
        grad_wo = grad_wo + to_z(grads[k], k).astype(f32)
    term = kept + to_z(sent, 2)
    grad_gate = term[:1] + to_z(term[1:], 1)
    d_attn = attn_gradient(gate, d_out[0], out_weight, grads[1])
    return (image_out[None], text_attn[None], d_attn[None], grad_wo, grad_gate)


def solution(mesh):
    in_specs = (
        P("dp", None, "seq"),
        P("seq"),
        P("seq", None),
        P("dp"),
        P("dp", None),
        P(),
        P(),
        P("dp", "seq", None),
        P("dp", "seq", None),
        P("dp", "seq", None),
        P(),
        P("dp", None),
        P("dp", "seq", None),
    )
    out_specs = (
        P("dp", "seq", None),
        P("dp", "seq", None),
        P("dp", "seq", None),
        P(("dp", "seq"), None),
        P("dp", "seq"),
    )
    return jax.shard_map(
        on_device, mesh=mesh, in_specs=in_specs, out_specs=out_specs, check_vma=False
    )
```

time: 136 us -> 166 us (1.22)
  the two profiles are of different devices: /device:TPU:9 before, /device:TPU:0 now
where the time goes in v6:
time: 166 us; the launch traced here: 164 us
  Pallas kernels  61.1 us (37%)
  waiting for transfers between devices  56.8 us (34%)
  starting transfers between devices  30.9 us (19%)
  local copies, waits for them, and re-layouts  10.2 us (6%)
  other arithmetic  2.87 us (2%)
  between operations  1.68 us (1%)
    pallas_call x1, Pallas kernels, text_project(): pl.pallas_call(functools.partial(text_kernel, groups, heads, place_of), o...  39.1 us
    ppermute x11, waiting for transfers between devices, to_z(): return lax.ppermute(x, 'seq', perm)  35.9 us
    ppermute x11, starting transfers between devices, to_z(): return lax.ppermute(x, 'seq', perm)  21.4 us
    ppermute x6, waiting for transfers between devices, to_dp(): return lax.ppermute(x, 'dp', [(a, a ^ k) for a in range(n_dp)])  16.1 us
    unnamed x20, local copies, waits for them, and re-layouts  9.99 us
    ppermute x6, starting transfers between devices, to_dp(): return lax.ppermute(x, 'dp', [(a, a ^ k) for a in range(n_dp)])  7.83 us
    pallas_call x1, Pallas kernels, attention(): pl.pallas_call(functools.partial(attention_kernel, len(far), len(blocks),...  5.37 us
    ppermute x7, waiting for transfers between devices, to_oc(): return lax.ppermute(x, 'seq', perm)  4.76 us
  transfers between devices with their start and end apart: 24, of which 12 were waited for; matrix products, arithmetic and copies ran while one was open for 1% of the time, Pallas kernels for 7%

profile of v6, /device:TPU:0, one launch (start us, length us, event | category | flops | bytes accessed | tf_op | source)
XLA Modules:
  0.0 163.5 jit_solution(13434261911334712555)
XLA Ops:
  1.4 0.6 pad_add_fusion.meta_ref
  2.0 39.1 %shard_map.164 = (f32[4,336,128]{2,1,0:T(8,128)}, bf16[1152,128]{1,0:T(8,128)(2,1)}, bf16[1472,128]{1,0:T(8,128)(2,1)}, bf16[1472,128]{1,0:T(8,128)(2,1)}, bf16[...) custom-call(s32[3]{0:T(128)} %pad_add_fusion.meta_ref, s32[1]{0:T(128)} %copy.32.len_ref, s32[1,64]{1,0:T(1,128)} %src_ref.1, ...), custom_call_target="tpu_custom_call" | custom-call | flops 301989888 | bytes 4718592 | tf_op jit(solution)/shard_map/pallas_call | solution.py:128
  41.1 0.5 collective-permute-start
  41.7 2.4 %shard_map.166 = (bf16[2,4,96,128]{3,2,1,0:T(8,128)(2,1)}, bf16[2,4,96,128]{3,2,1,0:T(8,128)(2,1)}, bf16[2,4,96,128]{3,2,1,0:T(8,128)(2,1)}, bf16[2,4,96,128]{3,2,1,0:T(8,128)(2,1)}) custom-call(s32[3]{0:T(128)} %pad_add_fusion.meta_ref, f32[1,3072]{1,0:T(1,128)} %gate_ref.5, bf16[128,3072]{1,0:T(8,128)(2,1)} %bitcast.19), custom_call_target="tpu_custom_call" | custom-call | bytes 1572864 | tf_op jit(solution)/shard_map/pallas_call | solution.py:332
  44.0 2.5 %collective-permute-start.4 = (bf16[2,4,96,128]{3,2,1,0:T(8,128)(2,1)}, bf16[2,4,96,128]{3,2,1,0:T(8,128)(2,1)S(1)}, u32[]{:S(2)}, u32[]{:S(2)}) collective-permute-start(bf16[2,4,96,128]{3,2,1,0:T(8,128)(2,1)} %get-tuple-element.44), channel_id=1, source_target_pairs={{0,8},{8,0},{16,24},{24,16},{1,9},{9,1},{17,25},{25,17},{2,10},{10... | collective-permute-start | bytes 589832 | tf_op jit(solution)/shard_map/ppermute | solution.py:527
  46.5 0.7 copy-done.8
  47.2 2.7 %shard_map.165 = (f32[336,128]{1,0:T(8,128)}, bf16[1472,128]{1,0:T(8,128)(2,1)}, bf16[1472,128]{1,0:T(8,128)(2,1)}, bf16[1472,128]{1,0:T(8,128)(2,1)}) custom-call(f32[4,336,128]{2,1,0:T(8,128)} %get-tuple-element.34.refs_0_, bf16[4,320,128]{2,1,0:T(8,128)(2,1)} %copy-done.8, ...), custom_call_target="tpu_custom_call", output_to_operand_aliasing={{1}: (2, {}), {2}: (3, {}), {3}: (4, {})} | custom-call | bytes 1376256 | tf_op jit(solution)/shard_map/pallas_call | solution.py:177
  50.0 1.6 %collective-permute-start.1 = (bf16[1472,128]{1,0:T(8,128)(2,1)}, bf16[1472,128]{1,0:T(8,128)(2,1)S(1)}, u32[]{:S(2)}, u32[]{:S(2)}) collective-permute-start(bf16[1472,128]{1,0:T(8,128)(2,1)} %get-tuple-element.39), channel_id=1, source_target_pairs={{0,2},{2,0},{4,6},{6,4},{1,3},{3,1},{5,7},{7,5},{8,10},{10,8},{12,... | collective-permute-start | bytes 1130504 | tf_op jit(solution)/shard_map/ppermute | solution.py:520
  51.6 2.6 %collective-permute-start.2 = (bf16[1472,128]{1,0:T(8,128)(2,1)}, bf16[1472,128]{1,0:T(8,128)(2,1)S(1)}, u32[]{:S(2)}, u32[]{:S(2)}) collective-permute-start(bf16[1472,128]{1,0:T(8,128)(2,1)} %get-tuple-element.40), channel_id=1, source_target_pairs={{0,4},{2,6},{4,0},{6,2},{1,5},{3,7},{5,1},{7,3},{8,12},{10,14},{12... | collective-permute-start | bytes 1130504 | tf_op jit(solution)/shard_map/ppermute | solution.py:520
  54.2 0.2 collective-permute-start.3
  54.4 1.5 collective-permute-start.5
  56.0 0.3 collective-permute-start.6
  56.2 8.9 %collective-permute-done.5.refs_4_.refs_2_ = bf16[2,4,96,128]{3,2,1,0:T(8,128)(2,1)S(1)} collective-permute-done((bf16[2,4,96,128]{3,2,1,0:T(8,128)(2,1)}, bf16[2,4,96,128]{3,2,1,0:T(8,128)(2,1)S(1)}, u32[]{:S(2)}, u32[]{:S(2)}) %collective-permute-start.5) | collective-permute-done | bytes 196640 | tf_op jit(solution)/shard_map/ppermute | solution.py:527
  65.1 3.6 %collective-permute-done.1.refs_0_ = bf16[1472,128]{1,0:T(8,128)(2,1)S(1)} collective-permute-done((bf16[1472,128]{1,0:T(8,128)(2,1)}, bf16[1472,128]{1,0:T(8,128)(2,1)S(1)}, u32[]{:S(2)}, u32[]{:S(2)}) %collective-permute-start.1) | collective-permute-done | bytes 376864 | tf_op jit(solution)/shard_map/ppermute | solution.py:520
  68.7 11.9 %collective-permute-done.2.refs_1_ = bf16[1472,128]{1,0:T(8,128)(2,1)S(1)} collective-permute-done((bf16[1472,128]{1,0:T(8,128)(2,1)}, bf16[1472,128]{1,0:T(8,128)(2,1)S(1)}, u32[]{:S(2)}, u32[]{:S(2)}) %collective-permute-start.2) | collective-permute-done | bytes 376864 | tf_op jit(solution)/shard_map/ppermute | solution.py:520
  80.5 1.0 copy-done.4
  81.5 0.9 copy-done.5
  82.4 1.5 shard_map.167
  84.1 2.8 %collective-permute-done.7.refs_4_ = bf16[3760,128]{1,0:T(8,128)(2,1)} collective-permute-done((bf16[3760,128]{1,0:T(8,128)(2,1)}, bf16[3760,128]{1,0:T(8,128)(2,1)}, u32[]{:S(2)}, u32[]{:S(2)}) %collective-permute-start.7) | collective-permute-done | bytes 962592 | tf_op jit(solution)/shard_map/ppermute | solution.py:524
  86.9 5.4 %shard_map.168 = (bf16[128,384]{1,0:T(8,128)(2,1)S(1)}, bf16[128,384]{1,0:T(8,128)(2,1)S(1)}, bf16[128,384]{1,0:T(8,128)(2,1)S(1)}, bf16[128,384]{1,0:T(8,128)(2,1)S(1)}, bf16[32,384]{1,0:T(8,128)(2,1)S(1)}) custom-call(bf16[1472,128]{1,0:T(8,128)(2,1)S(1)} %collective-permute-done.1.refs_0_, bf16[1472,128]{1,0:T(8,128)(2,1)S(1)} %collective-permute-done.2.refs_1_, ...), custom_call_target="tpu_custom_call" | custom-call | flops 909115392 | bytes 2506752 | tf_op jit(solution)/shard_map/pallas_call | solution.py:300
  92.3 8.7 %collective-permute-start.8 = (bf16[136,384]{1,0:T(8,128)(2,1)S(1)}, bf16[136,384]{1,0:T(8,128)(2,1)S(1)}, u32[]{:S(2)}, u32[]{:S(2)}) collective-permute-start(bf16[136,384]{1,0:T(8,128)(2,1)S(1)} %pad_maximum_fusion), channel_id=1, source_target_pairs={{0,4},{2,6},{4,0},{6,2},{1,5},{3,7},{5,1},{7,3},{8,12},{10,14},{12... | collective-permute-start | bytes 313352 | tf_op jit(solution)/shard_map/ppermute | solution.py:520
  101.1 1.4 collective-permute-start.9
  102.6 6.7 %collective-permute-done.8 = bf16[136,384]{1,0:T(8,128)(2,1)S(1)} collective-permute-done((bf16[136,384]{1,0:T(8,128)(2,1)S(1)}, bf16[136,384]{1,0:T(8,128)(2,1)S(1)}, u32[]{:S(2)}, u32[]{:S(2)}) %collective-permute-start.8) | collective-permute-done | bytes 104480 | tf_op jit(solution)/shard_map/ppermute | solution.py:520
  109.4 0.9 collective-permute-done.10
  110.4 1.6 collective-permute-start.14
  111.9 0.5 collective-permute-start.13
  112.4 1.5 collective-permute-start.12
  113.9 3.7 %copy-done = bf16[3072,1536]{1,0:T(8,128)(2,1)S(1)} copy-done((bf16[3072,1536]{1,0:T(8,128)(2,1)S(1)}, bf16[3072,1536]{1,0:T(8,128)(2,1)}, u32[]{:S(2)}) %copy-start) | copy-done | bytes 9437208
  117.6 4.7 %shard_map.169 = (bf16[128,3072]{1,0:T(8,128)(2,1)}, f32[4,384]{1,0:T(4,128)S(1)}, bf16[144,1536]{1,0:T(8,128)(2,1)}) custom-call(s32[3]{0:T(128)S(1)} %copy-done.7, bf16[128,1536]{1,0:T(8,128)(2,1)S(1)} %slice.32.attn_ref.refs_5_, bf16[3072,1536]{1,0:T(8,128)(2,1)S(1)} %copy-done, f32[1,3072]{1,0:T(1,128)S(1)} %copy-done.6, bf16[128,3072]{1,0:T(8,128)(2,1)S(1)} %bitcast.20), custom_call_target="tpu_custom_call" | custom-call | flops 1207959552 | bytes 9437184 | tf_op jit(solution)/shard_map/pallas_call | solution.py:430
  122.4 0.6 collective-permute-start.11
  123.0 0.6 collective-permute-done.14.refs_8_
  123.5 6.6 %collective-permute-done.13.refs_7_ = bf16[128,1536]{1,0:T(8,128)(2,1)} collective-permute-done((bf16[128,1536]{1,0:T(8,128)(2,1)S(1)}, bf16[128,1536]{1,0:T(8,128)(2,1)}, u32[]{:S(2)}, u32[]{:S(2)}) %collective-permute-start.13) | collective-permute-done | bytes 393248 | tf_op jit(solution)/shard_map/ppermute | solution.py:527
  130.2 0.1 collective-permute-done.12.refs_6_
  130.2 0.4 collective-permute-start.16
  130.8 1.4 collective-permute-done.17.refs_11_
  132.2 0.6 collective-permute-done.16.refs_10_
  132.8 3.1 %shard_map.171 = (f32[96,1536]{1,0:T(8,128)S(1)}, bf16[96,1536]{1,0:T(8,128)(2,1)S(1)}, bf16[96,1536]{1,0:T(8,128)(2,1)S(1)}, bf16[96,1536]{1,0:T(8,128)(2,1)S(1...) custom-call(bf16[1,4,96,128]{3,2,1,0:T(8,128)(2,1)S(1)} %slice.26.refs_0_, bf16[1,4,96,128]{3,2,1,0:T(8,128)(2,1)S(1)} %slice.34.refs_1_, ...), custom_call_target="tpu_custom_call" | custom-call | flops 1207959552 | bytes 5111808 | tf_op jit(solution)/shard_map/pallas_call | solution.py:478
  135.9 1.6 collective-permute-start.22
  137.5 0.7 fusion
  138.2 1.4 collective-permute-start.19
  139.6 1.7 %collective-permute-start.20 = (bf16[96,1536]{1,0:T(8,128)(2,1)S(1)}, bf16[96,1536]{1,0:T(8,128)(2,1)S(1)}, u32[]{:S(2)}, u32[]{:S(2)}) collective-permute-start(bf16[96,1536]{1,0:T(8,128)(2,1)S(1)} %get-tuple-element.60), channel_id=1, source_target_pairs={{0,6},{2,4},{4,2},{6,0},{1,7},{3,5},{5,3},{7,1},{8,14},{10,12},{12... | collective-permute-start | bytes 884744 | tf_op jit(solution)/shard_map/ppermute | solution.py:520
  141.2 0.4 collective-permute-start.21
  141.7 1.7 %collective-permute-start.23 = (f32[1,384]{1,0:T(1,128)S(1)}, f32[1,384]{1,0:T(1,128)S(1)}, u32[]{:S(2)}, u32[]{:S(2)}) collective-permute-start(f32[1,384]{1,0:T(1,128)S(1)} %slice.38), channel_id=1, source_target_pairs={{0,2},{2,0},{4,6},{6,4},{1,3},{3,1},{5,7},{7,5},{8,10},{10,8},{12,... | collective-permute-start | bytes 4616 | tf_op jit(solution)/shard_map/ppermute | solution.py:520
  143.3 3.7 %copy-done.1 = bf16[3072,1536]{1,0:T(8,128)(2,1)S(1)} copy-done((bf16[3072,1536]{1,0:T(8,128)(2,1)S(1)}, bf16[3072,1536]{1,0:T(8,128)(2,1)}, u32[]{:S(2)}) %copy-start.1) | copy-done | bytes 9437208
  147.0 2.1 %shard_map.172 = bf16[128,1536]{1,0:T(8,128)(2,1)} custom-call(f32[1,3072]{1,0:T(1,128)S(1)} %copy-done.6, bf16[128,3072]{1,0:T(8,128)(2,1)S(1)} %bitcast.21, bf16[3072,1536]{1,0:T(8,128)(2,1)S(1)} %copy-done.1, bf16[96,1536]{1,0:T(8,128)(2,1)S(1)} %get-tuple-element.57.after_ref), custom_call_target="tpu_custom_call" | custom-call | flops 1207959552 | bytes 9437184 | tf_op jit(solution)/shard_map/pallas_call | solution.py:357
  149.2 12.8 %collective-permute-done.23 = f32[1,384]{1,0:T(1,128)S(1)} collective-permute-done((f32[1,384]{1,0:T(1,128)S(1)}, f32[1,384]{1,0:T(1,128)S(1)}, u32[]{:S(2)}, u32[]{:S(2)}) %collective-permute-start.23) | collective-permute-done | bytes 1568 | tf_op jit(solution)/shard_map/ppermute | solution.py:520
  162.0 0.6 slice_add_fusion
  162.6 0.9 convert_add_fusion
  (51 shorter events, 0.6 us)
Async XLA Ops:
  0.6 113.3 %copy-start.6 = (f32[1,3072]{1,0:T(1,128)S(1)}, f32[1,3072]{1,0:T(1,128)}, u32[]{:S(2)}) copy-start(f32[1,3072]{1,0:T(1,128)} %gate_ref.5) | copy-start | bytes 36868
  0.6 113.3 %copy-start.2 = (bf16[1,128,3072]{2,1,0:T(8,128)(2,1)S(1)}, bf16[1,128,3072]{2,1,0:T(8,128)(2,1)}, u32[]{:S(2)}) copy-start(bf16[1,128,3072]{2,1,0:T(8,128)(2,1)} %param.25) | copy-start | bytes 2359300
  2.0 111.9 %copy-start.7 = (s32[3]{0:T(128)S(1)}, s32[3]{0:T(128)}, u32[]{:S(2)}) copy-start(s32[3]{0:T(128)} %pad_add_fusion.meta_ref) | copy-start | bytes 40
  41.1 5.4 %collective-permute-start = (bf16[4,320,128]{2,1,0:T(8,128)(2,1)}, bf16[4,320,128]{2,1,0:T(8,128)(2,1)S(1)}, u32[]{:S(2)}, u32[]{:S(2)}) collective-permute-start(bf16[4,320,128]{2,1,0:T(8,128)(2,1)} %get-tuple-element.35), channel_id=1, source_target_pairs={{0,1},{2,3},{4,5},{6,7},{1,0},{3,2},{5,4},{7,6},{8,9},{10,11},{12,... | collective-permute-start | bytes 983048 | tf_op jit(solution)/shard_map/ppermute | solution.py:524
  44.0 11.9 %collective-permute-start.4 = (bf16[2,4,96,128]{3,2,1,0:T(8,128)(2,1)}, bf16[2,4,96,128]{3,2,1,0:T(8,128)(2,1)S(1)}, u32[]{:S(2)}, u32[]{:S(2)}) collective-permute-start(bf16[2,4,96,128]{3,2,1,0:T(8,128)(2,1)} %get-tuple-element.44), channel_id=1, source_target_pairs={{0,8},{8,0},{16,24},{24,16},{1,9},{9,1},{17,25},{25,17},{2,10},{10... | collective-permute-start | bytes 589832 | tf_op jit(solution)/shard_map/ppermute | solution.py:527
  46.5 0.7 copy-start.8
  50.0 18.7 %collective-permute-start.1 = (bf16[1472,128]{1,0:T(8,128)(2,1)}, bf16[1472,128]{1,0:T(8,128)(2,1)S(1)}, u32[]{:S(2)}, u32[]{:S(2)}) collective-permute-start(bf16[1472,128]{1,0:T(8,128)(2,1)} %get-tuple-element.39), channel_id=1, source_target_pairs={{0,2},{2,0},{4,6},{6,4},{1,3},{3,1},{5,7},{7,5},{8,10},{10,8},{12,... | collective-permute-start | bytes 1130504 | tf_op jit(solution)/shard_map/ppermute | solution.py:520
  51.6 28.9 %collective-permute-start.2 = (bf16[1472,128]{1,0:T(8,128)(2,1)}, bf16[1472,128]{1,0:T(8,128)(2,1)S(1)}, u32[]{:S(2)}, u32[]{:S(2)}) collective-permute-start(bf16[1472,128]{1,0:T(8,128)(2,1)} %get-tuple-element.40), channel_id=1, source_target_pairs={{0,4},{2,6},{4,0},{6,2},{1,5},{3,7},{5,1},{7,3},{8,12},{10,14},{12... | collective-permute-start | bytes 1130504 | tf_op jit(solution)/shard_map/ppermute | solution.py:520
  54.2 26.3 %collective-permute-start.3 = (bf16[1472,128]{1,0:T(8,128)(2,1)}, bf16[1472,128]{1,0:T(8,128)(2,1)S(1)}, u32[]{:S(2)}, u32[]{:S(2)}) collective-permute-start(bf16[1472,128]{1,0:T(8,128)(2,1)} %get-tuple-element.41), channel_id=1, source_target_pairs={{0,6},{2,4},{4,2},{6,0},{1,7},{3,5},{5,3},{7,1},{8,14},{10,12},{12... | collective-permute-start | bytes 1130504 | tf_op jit(solution)/shard_map/ppermute | solution.py:520
  54.4 10.7 %collective-permute-start.5 = (bf16[2,4,96,128]{3,2,1,0:T(8,128)(2,1)}, bf16[2,4,96,128]{3,2,1,0:T(8,128)(2,1)S(1)}, u32[]{:S(2)}, u32[]{:S(2)}) collective-permute-start(bf16[2,4,96,128]{3,2,1,0:T(8,128)(2,1)} %get-tuple-element.45), channel_id=1, source_target_pairs={{0,16},{8,24},{16,0},{24,8},{1,17},{9,25},{17,1},{25,9},{2,18},{10... | collective-permute-start | bytes 589832 | tf_op jit(solution)/shard_map/ppermute | solution.py:527
  56.0 9.1 %collective-permute-start.6 = (bf16[2,4,96,128]{3,2,1,0:T(8,128)(2,1)}, bf16[2,4,96,128]{3,2,1,0:T(8,128)(2,1)S(1)}, u32[]{:S(2)}, u32[]{:S(2)}) collective-permute-start(bf16[2,4,96,128]{3,2,1,0:T(8,128)(2,1)} %get-tuple-element.46), channel_id=1, source_target_pairs={{0,24},{8,16},{16,8},{24,0},{1,25},{9,17},{17,9},{25,1},{2,26},{10... | collective-permute-start | bytes 589832 | tf_op jit(solution)/shard_map/ppermute | solution.py:527
  80.5 1.0 copy-start.4
  81.5 0.9 copy-start.5
  82.4 40.0 %copy-start.3 = (bf16[2,4,96,128]{3,2,1,0:T(8,128)(2,1)S(1)}, bf16[2,4,96,128]{3,2,1,0:T(8,128)(2,1)}, u32[]{:S(2)}) copy-start(bf16[2,4,96,128]{3,2,1,0:T(8,128)(2,1)} %get-tuple-element.54.refs_0_) | copy-start | bytes 589828
  84.0 46.7 %copy-start.9 = (s32[1,64]{1,0:T(1,128)S(1)}, s32[1,64]{1,0:T(1,128)}, u32[]{:S(2)}) copy-start(s32[1,64]{1,0:T(1,128)} %src_ref.1) | copy-start | bytes 772
  84.0 2.9 %collective-permute-start.7 = (bf16[3760,128]{1,0:T(8,128)(2,1)}, bf16[3760,128]{1,0:T(8,128)(2,1)}, u32[]{:S(2)}, u32[]{:S(2)}) collective-permute-start(bf16[3760,128]{1,0:T(8,128)(2,1)} %get-tuple-element.47.refs_3_), channel_id=1, source_target_pairs={{0,1},{2,3},{4,5},{6,7},{1,0},{3,2},{5,4},{7,6},{8,9},{10,11},{12,... | collective-permute-start | bytes 2887688 | tf_op jit(solution)/shard_map/ppermute | solution.py:524
  92.3 17.0 %collective-permute-start.8 = (bf16[136,384]{1,0:T(8,128)(2,1)S(1)}, bf16[136,384]{1,0:T(8,128)(2,1)S(1)}, u32[]{:S(2)}, u32[]{:S(2)}) collective-permute-start(bf16[136,384]{1,0:T(8,128)(2,1)S(1)} %pad_maximum_fusion), channel_id=1, source_target_pairs={{0,4},{2,6},{4,0},{6,2},{1,5},{3,7},{5,1},{7,3},{8,12},{10,14},{12... | collective-permute-start | bytes 313352 | tf_op jit(solution)/shard_map/ppermute | solution.py:520
  101.1 8.3 %collective-permute-start.9 = (bf16[136,384]{1,0:T(8,128)(2,1)S(1)}, bf16[136,384]{1,0:T(8,128)(2,1)S(1)}, u32[]{:S(2)}, u32[]{:S(2)}) collective-permute-start(bf16[136,384]{1,0:T(8,128)(2,1)S(1)} %pad_maximum_fusion.1), channel_id=1, source_target_pairs={{0,6},{2,4},{4,2},{6,0},{1,7},{3,5},{5,3},{7,1},{8,14},{10,12},{12... | collective-permute-start | bytes 313352 | tf_op jit(solution)/shard_map/ppermute | solution.py:520
  102.5 7.8 %collective-permute-start.10 = (bf16[136,384]{1,0:T(8,128)(2,1)S(1)}, bf16[136,384]{1,0:T(8,128)(2,1)S(1)}, u32[]{:S(2)}, u32[]{:S(2)}) collective-permute-start(bf16[136,384]{1,0:T(8,128)(2,1)S(1)} %pad_maximum_fusion.2), channel_id=1, source_target_pairs={{0,2},{2,0},{4,6},{6,4},{1,3},{3,1},{5,7},{7,5},{8,10},{10,8},{12,... | collective-permute-start | bytes 313352 | tf_op jit(solution)/shard_map/ppermute | solution.py:520
  110.4 13.2 %collective-permute-start.14 = (bf16[128,1536]{1,0:T(8,128)(2,1)S(1)}, bf16[128,1536]{1,0:T(8,128)(2,1)}, u32[]{:S(2)}, u32[]{:S(2)}) collective-permute-start(bf16[128,1536]{1,0:T(8,128)(2,1)S(1)} %slice.32.attn_ref.refs_5_), channel_id=1, source_target_pairs={{0,24},{8,16},{16,8},{24,0},{1,25},{9,17},{17,9},{25,1},{2,26},{10... | collective-permute-start | bytes 1179656 | tf_op jit(solution)/shard_map/ppermute | solution.py:527
  111.9 18.2 %collective-permute-start.13 = (bf16[128,1536]{1,0:T(8,128)(2,1)S(1)}, bf16[128,1536]{1,0:T(8,128)(2,1)}, u32[]{:S(2)}, u32[]{:S(2)}) collective-permute-start(bf16[128,1536]{1,0:T(8,128)(2,1)S(1)} %slice.32.attn_ref.refs_5_), channel_id=1, source_target_pairs={{0,16},{8,24},{16,0},{24,8},{1,17},{9,25},{17,1},{25,9},{2,18},{10... | collective-permute-start | bytes 1179656 | tf_op jit(solution)/shard_map/ppermute | solution.py:527
  112.4 17.8 %collective-permute-start.12 = (bf16[128,1536]{1,0:T(8,128)(2,1)S(1)}, bf16[128,1536]{1,0:T(8,128)(2,1)}, u32[]{:S(2)}, u32[]{:S(2)}) collective-permute-start(bf16[128,1536]{1,0:T(8,128)(2,1)S(1)} %slice.32.attn_ref.refs_5_), channel_id=1, source_target_pairs={{0,8},{8,0},{16,24},{24,16},{1,9},{9,1},{17,25},{25,17},{2,10},{10... | collective-permute-start | bytes 1179656 | tf_op jit(solution)/shard_map/ppermute | solution.py:527
  113.9 3.7 %copy-start = (bf16[3072,1536]{1,0:T(8,128)(2,1)S(1)}, bf16[3072,1536]{1,0:T(8,128)(2,1)}, u32[]{:S(2)}) copy-start(bf16[3072,1536]{1,0:T(8,128)(2,1)} %w_ref.5) | copy-start | bytes 28311556
  122.4 8.5 %collective-permute-start.15 = (bf16[144,1536]{1,0:T(8,128)(2,1)}, bf16[144,1536]{1,0:T(8,128)(2,1)S(1)}, u32[]{:S(2)}, u32[]{:S(2)}) collective-permute-start(bf16[144,1536]{1,0:T(8,128)(2,1)} %get-tuple-element.55), channel_id=1, source_target_pairs={{0,1},{2,3},{4,5},{6,7},{1,0},{3,2},{5,4},{7,6},{8,9},{10,11},{12,... | collective-permute-start | bytes 1327112 | tf_op jit(solution)/shard_map/ppermute | solution.py:524
  122.4 8.4 %collective-permute-start.11 = (bf16[4,4,96,128]{3,2,1,0:T(8,128)(2,1)S(1)}, bf16[4,4,96,128]{3,2,1,0:T(8,128)(2,1)}, u32[]{:S(2)}, u32[]{:S(2)}) collective-permute-start(bf16[4,4,96,128]{3,2,1,0:T(8,128)(2,1)S(1)} %shard_map.170), channel_id=1, source_target_pairs={{0,1},{2,3},{4,5},{6,7},{1,0},{3,2},{5,4},{7,6},{8,9},{10,11},{12,... | collective-permute-start | bytes 1179656 | tf_op jit(solution)/shard_map/ppermute | solution.py:524
  123.5 7.3 %collective-permute-start.18 = (bf16[128,1536]{1,0:T(8,128)(2,1)}, bf16[128,1536]{1,0:T(8,128)(2,1)}, u32[]{:S(2)}, u32[]{:S(2)}) collective-permute-start(bf16[128,1536]{1,0:T(8,128)(2,1)} %collective-permute-done.14.refs_8_), channel_id=1, source_target_pairs={{0,1},{2,3},{4,5},{6,7},{1,0},{3,2},{5,4},{7,6},{8,9},{10,11},{12,... | collective-permute-start | bytes 1179656 | tf_op jit(solution)/shard_map/ppermute | solution.py:524
  130.1 2.1 %collective-permute-start.17 = (bf16[128,1536]{1,0:T(8,128)(2,1)}, bf16[128,1536]{1,0:T(8,128)(2,1)}, u32[]{:S(2)}, u32[]{:S(2)}) collective-permute-start(bf16[128,1536]{1,0:T(8,128)(2,1)} %collective-permute-done.13.refs_7_), channel_id=1, source_target_pairs={{0,1},{2,3},{4,5},{6,7},{1,0},{3,2},{5,4},{7,6},{8,9},{10,11},{12,... | collective-permute-start | bytes 1179656 | tf_op jit(solution)/shard_map/ppermute | solution.py:524
  130.2 2.5 %collective-permute-start.16 = (bf16[128,1536]{1,0:T(8,128)(2,1)}, bf16[128,1536]{1,0:T(8,128)(2,1)}, u32[]{:S(2)}, u32[]{:S(2)}) collective-permute-start(bf16[128,1536]{1,0:T(8,128)(2,1)} %collective-permute-done.12.refs_6_), channel_id=1, source_target_pairs={{0,1},{2,3},{4,5},{6,7},{1,0},{3,2},{5,4},{7,6},{8,9},{10,11},{12,... | collective-permute-start | bytes 1179656 | tf_op jit(solution)/shard_map/ppermute | solution.py:524
  135.9 5.8 %collective-permute-start.22 = (f32[2,384]{1,0:T(2,128)S(1)}, f32[2,384]{1,0:T(2,128)S(1)}, u32[]{:S(2)}, u32[]{:S(2)}) collective-permute-start(f32[2,384]{1,0:T(2,128)S(1)} %get-tuple-element.62), channel_id=1, source_target_pairs={{0,4},{2,6},{4,0},{6,2},{1,5},{3,7},{5,1},{7,3},{8,12},{10,14},{12... | collective-permute-start | bytes 9224 | tf_op jit(solution)/shard_map/ppermute | solution.py:520
  138.2 24.4 %collective-permute-start.19 = (bf16[96,1536]{1,0:T(8,128)(2,1)S(1)}, bf16[96,1536]{1,0:T(8,128)(2,1)S(1)}, u32[]{:S(2)}, u32[]{:S(2)}) collective-permute-start(bf16[96,1536]{1,0:T(8,128)(2,1)S(1)} %get-tuple-element.59), channel_id=1, source_target_pairs={{0,4},{2,6},{4,0},{6,2},{1,5},{3,7},{5,1},{7,3},{8,12},{10,14},{12... | collective-permute-start | bytes 884744 | tf_op jit(solution)/shard_map/ppermute | solution.py:520
  139.6 23.0 %collective-permute-start.20 = (bf16[96,1536]{1,0:T(8,128)(2,1)S(1)}, bf16[96,1536]{1,0:T(8,128)(2,1)S(1)}, u32[]{:S(2)}, u32[]{:S(2)}) collective-permute-start(bf16[96,1536]{1,0:T(8,128)(2,1)S(1)} %get-tuple-element.60), channel_id=1, source_target_pairs={{0,6},{2,4},{4,2},{6,0},{1,7},{3,5},{5,3},{7,1},{8,14},{10,12},{12... | collective-permute-start | bytes 884744 | tf_op jit(solution)/shard_map/ppermute | solution.py:520
  141.2 21.3 %collective-permute-start.21 = (bf16[96,1536]{1,0:T(8,128)(2,1)S(1)}, bf16[96,1536]{1,0:T(8,128)(2,1)S(1)}, u32[]{:S(2)}, u32[]{:S(2)}) collective-permute-start(bf16[96,1536]{1,0:T(8,128)(2,1)S(1)} %get-tuple-element.57.after_ref), channel_id=1, source_target_pairs={{0,2},{2,0},{4,6},{6,4},{1,3},{3,1},{5,7},{7,5},{8,10},{10,8},{12,... | collective-permute-start | bytes 884744 | tf_op jit(solution)/shard_map/ppermute | solution.py:520
  141.7 20.3 %collective-permute-start.23 = (f32[1,384]{1,0:T(1,128)S(1)}, f32[1,384]{1,0:T(1,128)S(1)}, u32[]{:S(2)}, u32[]{:S(2)}) collective-permute-start(f32[1,384]{1,0:T(1,128)S(1)} %slice.38), channel_id=1, source_target_pairs={{0,2},{2,0},{4,6},{6,4},{1,3},{3,1},{5,7},{7,5},{8,10},{10,8},{12,... | collective-permute-start | bytes 4616 | tf_op jit(solution)/shard_map/ppermute | solution.py:520
  143.3 3.7 %copy-start.1 = (bf16[3072,1536]{1,0:T(8,128)(2,1)S(1)}, bf16[3072,1536]{1,0:T(8,128)(2,1)}, u32[]{:S(2)}) copy-start(bf16[3072,1536]{1,0:T(8,128)(2,1)} %w_ref.5) | copy-start | bytes 28311556

commit v7 on v6

--- a/solution.py
+++ b/solution.py
@@ -48,7 +48,7 @@
     w_ref, k_ref, v_ref, q_ref, own_ref, *refs
 ):
     packed, refs = refs[:groups], refs[groups:]
-    msgs, (w_all, w_sems, pack_sems) = refs[:-3], refs[-3:]
+    msgs, (w_all, w_sems) = refs[:-2], refs[-2:]
     size = own_ref.shape[2]
     rows = (own_ref.shape[1] - EXTRA) // (3 * heads + 1)
     width = heads * size
@@ -61,17 +61,13 @@
             cols = pl.ds(pl.multiple_of(at, 128), width)
             copies.append(pltpu.make_async_copy(w_ref.at[:, cols], w_all.at[g, i], w_sems.at[g, i]))
             copies[-1].start()
-    packs = []
     local = k_ref.shape[0]
     for g, out in enumerate(packed):
         for i, ref in enumerate((k_ref, v_ref, q_ref)):
             for head in range(heads):
                 at = ((meta_ref[0] ^ g) * heads + head) * size
-                source = ref.at[:, pl.ds(pl.multiple_of(at, 128), size)]
-                target = out.at[pl.ds((i * heads + head) * local, local), :]
-                sem = pack_sems.at[g, i * heads + head]
-                packs.append(pltpu.make_async_copy(source, target, sem))
-                packs[-1].start()
+                to = (i * heads + head) * local
+                out[to : to + local, :] = ref[:, pl.ds(pl.multiple_of(at, 128), size)]
 
     def slot_at(row):
         z_at = (row % rows) // slot_local
@@ -107,8 +103,6 @@
         own_ref[g, 3 * heads * rows : end, :] = tail[:rows]
         for j, msg in enumerate(msgs):
             msg[g, 3 * heads * rows :, :] = tail[(j + 1) * rows : (j + 2) * rows].astype(bf16)
-    for copy in packs:
-        copy.wait()
 
 
 def text_project(
@@ -128,12 +122,11 @@
     return pl.pallas_call(
         functools.partial(text_kernel, groups, heads, place_of),
         out_shape=shapes,
-        in_specs=[SMEM, SMEM] + [VMEM] * 5 + [ANY] * 4,
-        out_specs=[VMEM] + [ANY] * groups + [VMEM] * (parts - 1),
+        in_specs=[SMEM, SMEM] + [VMEM] * 5 + [ANY] + [VMEM] * 3,
+        out_specs=[VMEM] * (groups + parts),
         scratch_shapes=[
             pltpu.VMEM((groups, 3, depth, heads * size), bf16),
             pltpu.SemaphoreType.DMA((groups, 3)),
-            pltpu.SemaphoreType.DMA((groups, 3 * heads)),
         ],
         compiler_params=params(60),
         cost_estimate=cost(
@@ -223,7 +216,7 @@
     copies[1].wait()
 
 
-def block_of(near, own, got, after, features, heads):
+def block_of(near, own, got, mark, features, heads):
     image_rows, size = near.shape
     text_rows = own.shape[0] - EXTRA
     total = image_rows + image_rows // 3 * 2 * len(got)
@@ -235,13 +228,13 @@
             jax.ShapeDtypeStruct(near.shape, bf16),
             jax.ShapeDtypeStruct(own.shape, f32),
         ],
-        in_specs=[ANY] * 2 + [VMEM] * len(got) + [ANY] * len(after),
+        in_specs=[ANY] * 2 + [VMEM] * len(got) + [SMEM],
         out_specs=[VMEM, ANY, ANY],
         input_output_aliases={0: 1, 1: 2},
         scratch_shapes=[pltpu.VMEM(own.shape, f32), pltpu.SemaphoreType.DMA((2,))],
         compiler_params=params(),
         cost_estimate=cost(0, 4 * total * size),
-    )(near, own, *got, *after)[0]
+    )(near, own, *got, mark)[0]
 
 
 def attention_kernel(n_far, n_blocks, heads, rows, text_rows, *refs):
@@ -313,8 +306,29 @@
     )(*far, *blocks)
 
 
+def assemble_kernel(groups, n_after, meta_ref, *refs):
+    pieces, out_ref = refs[:groups], refs[groups + n_after]
+    rows, width = out_ref.shape[0], pieces[0].shape[1]
+    for k, piece in enumerate(pieces):
+        at = pl.multiple_of((meta_ref[0] ^ k) * width, 128)
+        out_ref[:, pl.ds(at, width)] = piece[:rows, :]
+
+
+def assemble(meta, pieces, after, rows):
+    groups, width = len(pieces), pieces[0].shape[1]
+    return pl.pallas_call(
+        functools.partial(assemble_kernel, groups, len(after)),
+        out_shape=jax.ShapeDtypeStruct((rows, groups * width), bf16),
+        in_specs=[SMEM] + [VMEM] * groups + [ANY] * len(after),
+        out_specs=VMEM,
+        compiler_params=params(),
+        cost_estimate=cost(0, 4 * rows * groups * width),
+    )(meta, *pieces, *after)
+
+
 def gated_kernel(groups, parts, place_of, meta_ref, gate_ref, d_out_ref, *refs):
-    msgs, turned = refs[:-1], refs[-1]
+    msgs, mark_ref, turned = refs[:-2], refs[-2], refs[-1]
+    mark_ref[0] = meta_ref[0]
     gated = (gate_ref[...] * d_out_ref[...].astype(f32)).astype(bf16)
     turned[...] = gated.astype(f32).T
     rows = msgs[0].shape[2]
@@ -331,9 +345,10 @@
     rows = model // (n_dp * groups * parts)
     return pl.pallas_call(
         functools.partial(gated_kernel, groups, parts, place_of),
-        out_shape=[jax.ShapeDtypeStruct((parts, groups, rows, local), bf16)] * n_dp,
+        out_shape=[jax.ShapeDtypeStruct((parts, groups, rows, local), bf16)] * n_dp
+        + [jax.ShapeDtypeStruct((1,), jnp.int32)],
         in_specs=[SMEM, VMEM, VMEM],
-        out_specs=[VMEM] * n_dp,
+        out_specs=[VMEM] * n_dp + [SMEM],
         scratch_shapes=[pltpu.VMEM((model, local), f32)],
         compiler_params=params(60),
         cost_estimate=cost(0, 4 * local * model),
@@ -472,8 +487,7 @@
     width = pieces[0].shape[1]
     total = groups * rows
     depth = depth * len(pieces)
-    shapes = [jax.ShapeDtypeStruct((rows, width), f32)]
-    shapes += [jax.ShapeDtypeStruct((rows, width), bf16)] * (groups - 1)
+    shapes = [jax.ShapeDtypeStruct((rows, width), (f32, bf16)[g % 2]) for g in range(groups)]
     shapes += [jax.ShapeDtypeStruct((groups // 2, term.shape[1]), f32)] * 2
     return pl.pallas_call(
         functools.partial(grad_kernel, len(lefts), len(pieces)),
@@ -552,23 +566,24 @@
     far = {k: to_z(messages[k - 1], k) for k in order}
     far = [far[k] for k in range(1, G)]
 
-    gg = gated_parts(meta, gate, d_out[0], n_dp, G, OC, place)
+    *gg, mark = gated_parts(meta, gate, d_out[0], n_dp, G, OC, place)
+    block = block_of(packed[0], own, far, mark, DT5, heads)
+    blocks = [block] + [to_oc(block, j) for j in range(1, OC)]
+    *outs, text_out = attention(far, blocks, heads, image_local, text_rows)
+
+    back = []
+    for k in range(G):
+        rows = jnp.concatenate([outs[k], part(text_out, z ^ k, slot_local, 0)], axis=0)
+        back.append(to_z(rows, k) if k else rows)
     gg_dp = [gg[0]] + [to_dp(gg[k], k) for k in range(1, n_dp)]
     lefts = [g[:1] for g in gg_dp]
     lefts += [to_oc(g, j + 1) for j, g in enumerate(gather_parts(gg_dp))]
-
-    block = block_of(packed[0], own, far, gg_dp[1:], DT5, heads)
-    blocks = [block] + [to_oc(block, j) for j in range(1, OC)]
-    *outs, text_out = attention(far, blocks, heads, image_local, text_rows)
-
-    attn = jnp.zeros((image_local + slot_local, inner_width), bf16)
-    for k in order + [0]:
-        rows = jnp.concatenate([outs[k], part(text_out, z ^ k, slot_local, 0)], axis=0)
-        rows = to_z(rows, k) if k else rows
-        attn = lax.dynamic_update_slice_in_dim(attn, rows, (z ^ k) * gw, 1)
-    image_attn = attn[:image_local]
+    image_attn = assemble(meta, back, gg_dp[1:], image_local)
+    text_attn = jnp.zeros((slot_local, inner_width), bf16)
     own_usable = part(slot_source[0] < caption_len[0], seq, slot_local, 0)
-    text_attn = jnp.where(own_usable[:, None], attn[image_local:], jnp.zeros((), bf16))
+    for k in range(G):
+        rows = jnp.where(own_usable[:, None], back[k][image_local:], jnp.zeros((), bf16))
+        text_attn = lax.dynamic_update_slice_in_dim(text_attn, rows, (z ^ k) * gw, 1)
 
     pieces = [image_attn] + [to_dp(image_attn, k) for k in range(1, n_dp)]
     image_out, term, *sent = project(
@@ -577,9 +592,8 @@
     for j in range(1, OC):
         pieces += [to_oc(sent[j - 1], j)] + [to_oc(p, j) for p in pieces[1:n_dp]]
     *grads, kept, sent = grad_product(lefts, pieces, term)
-    grad_wo = grads[0]
-    for k in order:
-        grad_wo = grad_wo + to_z(grads[k], k).astype(f32)
+    pair = grads[2] + to_z(grads[3], 1).astype(f32)
+    grad_wo = grads[0] + to_z(pair.astype(bf16), 2).astype(f32) + to_z(grads[1], 1).astype(f32)
     term = kept + to_z(sent, 2)
     grad_gate = term[:1] + to_z(term[1:], 1)
     d_attn = attn_gradient(gate, d_out[0], out_weight, grads[1])

time: 166 us -> 132 us (0.80); the launches traced: 164 us -> 131 us
  Pallas kernels: 61.1 us -> 29.8 us
  waiting for transfers between devices: 56.8 us -> 52 us
  starting transfers between devices: 30.9 us -> 35.2 us
    pallas_call x1, Pallas kernels: 39.1 us -> 6.39 us  [text_project(): pl.pallas_call(functools.partial(text_kernel, groups, heads, place_of), o...]
    ppermute x6, waiting for transfers between devices: 16.1 us -> 5.07 us  [to_dp(): return lax.ppermute(x, 'dp', [(a, a ^ k) for a in range(n_dp)])]
    ppermute x11, waiting for transfers between devices: 35.9 us -> 43.5 us  [to_z(): return lax.ppermute(x, 'seq', perm)]
    ppermute x11, starting transfers between devices: 21.4 us -> 26.6 us  [to_z(): return lax.ppermute(x, 'seq', perm)]
    unnamed x20 -> x22, local copies, waits for them, and re-layouts: 9.99 us -> 9.99 us
  transfers between devices with their start and end apart: 24 -> 24, of which waited for: 12 -> 12; matrix products, arithmetic and copies ran while one was open for 1% -> 1% of each run, Pallas kernels for 7% -> 11%
where the time goes in v7:
time: 132 us; the launch traced here: 131 us
  waiting for transfers between devices  52 us (39%)
  starting transfers between devices  35.2 us (27%)
  Pallas kernels  29.8 us (23%)
  local copies, waits for them, and re-layouts  10.1 us (8%)
  other arithmetic  2.55 us (2%)
  between operations  1.62 us (1%)
    ppermute x11, waiting for transfers between devices, to_z(): return lax.ppermute(x, 'seq', perm)  43.5 us
    ppermute x11, starting transfers between devices, to_z(): return lax.ppermute(x, 'seq', perm)  26.6 us
    unnamed x22, local copies, waits for them, and re-layouts  9.99 us
    ppermute x6, starting transfers between devices, to_dp(): return lax.ppermute(x, 'dp', [(a, a ^ k) for a in range(n_dp)])  7.11 us
    pallas_call x1, Pallas kernels, text_project(): pl.pallas_call(functools.partial(text_kernel, groups, heads, place_of), o...  6.39 us
    pallas_call x1, Pallas kernels, attention(): pl.pallas_call(functools.partial(attention_kernel, len(far), len(blocks),...  5.38 us
    ppermute x6, waiting for transfers between devices, to_dp(): return lax.ppermute(x, 'dp', [(a, a ^ k) for a in range(n_dp)])  5.07 us
    pallas_call x1, Pallas kernels, project(): pl.pallas_call(functools.partial(project_kernel, groups, parts, place_of)...  4.72 us
  transfers between devices with their start and end apart: 24, of which 12 were waited for; matrix products, arithmetic and copies ran while one was open for 1% of the time, Pallas kernels for 11%

profile of v7, /device:TPU:0, one launch (start us, length us, event | category | flops | bytes accessed | tf_op | source)
XLA Modules:
  0.0 131.3 jit_solution(5758527765763832591)
XLA Ops:
  1.4 0.7 pad_add_fusion.meta_ref
  2.1 6.4 %shard_map.164 = (f32[4,336,128]{2,1,0:T(8,128)}, bf16[1152,128]{1,0:T(8,128)(2,1)}, bf16[1472,128]{1,0:T(8,128)(2,1)}, bf16[1472,128]{1,0:T(8,128)(2,1)}, bf16[...) custom-call(s32[3]{0:T(128)} %pad_add_fusion.meta_ref, s32[1]{0:T(128)} %copy.32.len_ref, s32[1,64]{1,0:T(1,128)} %src_ref.1, ...), custom_call_target="tpu_custom_call" | custom-call | flops 301989888 | bytes 4718592 | tf_op jit(solution)/shard_map/pallas_call | solution.py:122
  8.5 0.5 collective-permute-start
  9.0 1.5 %collective-permute-done.refs_1_ = bf16[4,320,128]{2,1,0:T(8,128)(2,1)S(1)} collective-permute-done((bf16[4,320,128]{2,1,0:T(8,128)(2,1)}, bf16[4,320,128]{2,1,0:T(8,128)(2,1)S(1)}, u32[]{:S(2)}, u32[]{:S(2)}) %collective-permute-start) | collective-permute-done | bytes 327712 | tf_op jit(solution)/shard_map/ppermute | solution.py:538
  10.5 0.7 copy-done.8
  11.2 2.7 %shard_map.165 = (f32[336,128]{1,0:T(8,128)}, bf16[1472,128]{1,0:T(8,128)(2,1)}, bf16[1472,128]{1,0:T(8,128)(2,1)}, bf16[1472,128]{1,0:T(8,128)(2,1)}) custom-call(f32[4,336,128]{2,1,0:T(8,128)} %get-tuple-element.35.refs_0_, bf16[4,320,128]{2,1,0:T(8,128)(2,1)} %copy-done.8, ...), custom_call_target="tpu_custom_call", output_to_operand_aliasing={{1}: (2, {}), {2}: (3, {}), {3}: (4, {})} | custom-call | bytes 1376256 | tf_op jit(solution)/shard_map/pallas_call | solution.py:170
  13.9 3.0 %collective-permute-start.1 = (bf16[1472,128]{1,0:T(8,128)(2,1)}, bf16[1472,128]{1,0:T(8,128)(2,1)S(1)}, u32[]{:S(2)}, u32[]{:S(2)}) collective-permute-start(bf16[1472,128]{1,0:T(8,128)(2,1)} %get-tuple-element.40), channel_id=1, source_target_pairs={{0,2},{2,0},{4,6},{6,4},{1,3},{3,1},{5,7},{7,5},{8,10},{10,8},{12,... | collective-permute-start | bytes 1130504 | tf_op jit(solution)/shard_map/ppermute | solution.py:534
  16.9 2.6 %collective-permute-start.2 = (bf16[1472,128]{1,0:T(8,128)(2,1)}, bf16[1472,128]{1,0:T(8,128)(2,1)S(1)}, u32[]{:S(2)}, u32[]{:S(2)}) collective-permute-start(bf16[1472,128]{1,0:T(8,128)(2,1)} %get-tuple-element.41), channel_id=1, source_target_pairs={{0,4},{2,6},{4,0},{6,2},{1,5},{3,7},{5,1},{7,3},{8,12},{10,14},{12... | collective-permute-start | bytes 1130504 | tf_op jit(solution)/shard_map/ppermute | solution.py:534
  19.5 2.3 %shard_map.166 = (bf16[2,4,96,128]{3,2,1,0:T(8,128)(2,1)}, bf16[2,4,96,128]{3,2,1,0:T(8,128)(2,1)}, bf16[2,4,96,128]{3,2,1,0:T(8,128)(2,1)}, bf16[2,4,96,128]{3,2,1,0:T(8,128)(2,1)}, s32[1]{0:T(128)}) custom-call(s32[3]{0:T(128)} %pad_add_fusion.meta_ref, f32[1,3072]{1,0:T(1,128)} %gate_ref.5, bf16[128,3072]{1,0:T(8,128)(2,1)} %bitcast.31), custom_call_target="tpu_custom_call" | custom-call | bytes 1572864 | tf_op jit(solution)/shard_map/pallas_call | solution.py:346
  21.9 11.8 %collective-permute-done.1.refs_0_ = bf16[1472,128]{1,0:T(8,128)(2,1)S(1)} collective-permute-done((bf16[1472,128]{1,0:T(8,128)(2,1)}, bf16[1472,128]{1,0:T(8,128)(2,1)S(1)}, u32[]{:S(2)}, u32[]{:S(2)}) %collective-permute-start.1) | collective-permute-done | bytes 376864 | tf_op jit(solution)/shard_map/ppermute | solution.py:534
  33.7 12.2 %collective-permute-done.2.refs_1_ = bf16[1472,128]{1,0:T(8,128)(2,1)S(1)} collective-permute-done((bf16[1472,128]{1,0:T(8,128)(2,1)}, bf16[1472,128]{1,0:T(8,128)(2,1)S(1)}, u32[]{:S(2)}, u32[]{:S(2)}) %collective-permute-start.2) | collective-permute-done | bytes 376864 | tf_op jit(solution)/shard_map/ppermute | solution.py:534
  45.9 1.0 copy-done.4
  46.8 0.9 copy-done.5
  47.7 2.4 %shard_map.167 = (bf16[3760,128]{1,0:T(8,128)(2,1)}, bf16[1152,128]{1,0:T(8,128)(2,1)S(1)}, f32[336,128]{1,0:T(8,128)S(1)}) custom-call(bf16[1152,128]{1,0:T(8,128)(2,1)S(1)} %copy-done.4, f32[336,128]{1,0:T(8,128)S(1)} %copy-done.5, bf16[1472,128]{1,0:T(8,128)(2,1)S(1)} %collective-permute-done.1.refs_0_, ...), custom_call_target="tpu_custom_call", output_to_operand_aliasing={{1}: (0, {}), {2}: (1, {})} | custom-call | bytes 1925120 | tf_op jit(solution)/shard_map/pallas_call | solution.py:224
  50.2 1.6 %collective-permute-start.8 = (bf16[2,4,96,128]{3,2,1,0:T(8,128)(2,1)}, bf16[2,4,96,128]{3,2,1,0:T(8,128)(2,1)S(1)}, u32[]{:S(2)}, u32[]{:S(2)}) collective-permute-start(bf16[2,4,96,128]{3,2,1,0:T(8,128)(2,1)} %get-tuple-element.52), channel_id=1, source_target_pairs={{0,8},{8,0},{16,24},{24,16},{1,9},{9,1},{17,25},{25,17},{2,10},{10... | collective-permute-start | bytes 589832 | tf_op jit(solution)/shard_map/ppermute | solution.py:541
  51.7 1.5 %collective-permute-start.9 = (bf16[2,4,96,128]{3,2,1,0:T(8,128)(2,1)}, bf16[2,4,96,128]{3,2,1,0:T(8,128)(2,1)S(1)}, u32[]{:S(2)}, u32[]{:S(2)}) collective-permute-start(bf16[2,4,96,128]{3,2,1,0:T(8,128)(2,1)} %get-tuple-element.53), channel_id=1, source_target_pairs={{0,16},{8,24},{16,0},{24,8},{1,17},{9,25},{17,1},{25,9},{2,18},{10... | collective-permute-start | bytes 589832 | tf_op jit(solution)/shard_map/ppermute | solution.py:541
  53.3 0.5 collective-permute-start.10
  53.8 5.4 %shard_map.168 = (bf16[128,384]{1,0:T(8,128)(2,1)S(1)}, bf16[128,384]{1,0:T(8,128)(2,1)S(1)}, bf16[128,384]{1,0:T(8,128)(2,1)S(1)}, bf16[128,384]{1,0:T(8,128)(2,1)S(1)}, bf16[32,384]{1,0:T(8,128)(2,1)S(1)}) custom-call(bf16[1472,128]{1,0:T(8,128)(2,1)S(1)} %collective-permute-done.1.refs_0_, bf16[1472,128]{1,0:T(8,128)(2,1)S(1)} %collective-permute-done.2.refs_1_, ...), custom_call_target="tpu_custom_call" | custom-call | flops 909115392 | bytes 2506752 | tf_op jit(solution)/shard_map/pallas_call | solution.py:293
  59.3 7.6 %collective-permute-start.5 = (bf16[136,384]{1,0:T(8,128)(2,1)S(1)}, bf16[136,384]{1,0:T(8,128)(2,1)S(1)}, u32[]{:S(2)}, u32[]{:S(2)}) collective-permute-start(bf16[136,384]{1,0:T(8,128)(2,1)S(1)} %pad_maximum_fusion.1), channel_id=1, source_target_pairs={{0,2},{2,0},{4,6},{6,4},{1,3},{3,1},{5,7},{7,5},{8,10},{10,8},{12,... | collective-permute-start | bytes 313352 | tf_op jit(solution)/shard_map/ppermute | solution.py:534
  66.9 1.1 collective-permute-start.6
  68.1 1.5 %collective-permute-start.7 = (bf16[136,384]{1,0:T(8,128)(2,1)S(1)}, bf16[136,384]{1,0:T(8,128)(2,1)S(1)}, u32[]{:S(2)}, u32[]{:S(2)}) collective-permute-start(bf16[136,384]{1,0:T(8,128)(2,1)S(1)} %pad_maximum_fusion.3), channel_id=1, source_target_pairs={{0,6},{2,4},{4,2},{6,0},{1,7},{3,5},{5,3},{7,1},{8,14},{10,12},{12... | collective-permute-start | bytes 313352 | tf_op jit(solution)/shard_map/ppermute | solution.py:534
  69.7 0.6 collective-permute-done.5.refs_1_
  70.2 7.4 %collective-permute-done.6.refs_2_ = bf16[136,384]{1,0:T(8,128)(2,1)S(1)} collective-permute-done((bf16[136,384]{1,0:T(8,128)(2,1)S(1)}, bf16[136,384]{1,0:T(8,128)(2,1)S(1)}, u32[]{:S(2)}, u32[]{:S(2)}) %collective-permute-start.6) | collective-permute-done | bytes 104480 | tf_op jit(solution)/shard_map/ppermute | solution.py:534
  77.6 0.6 shard_map.169.attn_ref.refs_5_
  78.2 2.5 %collective-permute-start.14 = (bf16[128,1536]{1,0:T(8,128)(2,1)S(1)}, bf16[128,1536]{1,0:T(8,128)(2,1)}, u32[]{:S(2)}, u32[]{:S(2)}) collective-permute-start(bf16[128,1536]{1,0:T(8,128)(2,1)S(1)} %shard_map.169.attn_ref.refs_5_), channel_id=1, source_target_pairs={{0,24},{8,16},{16,8},{24,0},{1,25},{9,17},{17,9},{25,1},{2,26},{10... | collective-permute-start | bytes 1179656 | tf_op jit(solution)/shard_map/ppermute | solution.py:541
  80.7 0.5 collective-permute-start.13
  81.2 0.5 collective-permute-start.12
  81.8 3.7 %copy-done = bf16[3072,1536]{1,0:T(8,128)(2,1)S(1)} copy-done((bf16[3072,1536]{1,0:T(8,128)(2,1)S(1)}, bf16[3072,1536]{1,0:T(8,128)(2,1)}, u32[]{:S(2)}) %copy-start) | copy-done | bytes 9437208
  85.5 4.7 %shard_map.170 = (bf16[128,3072]{1,0:T(8,128)(2,1)}, f32[4,384]{1,0:T(4,128)S(1)}, bf16[144,1536]{1,0:T(8,128)(2,1)}) custom-call(s32[3]{0:T(128)S(1)} %copy-done.7, bf16[128,1536]{1,0:T(8,128)(2,1)S(1)} %shard_map.169.attn_ref.refs_5_, bf16[3072,1536]{1,0:T(8,128)(2,1)S(1)} %copy-done, f32[1,3072]{1,0:T(1,128)S(1)} %copy-done.6, bf16[128,3072]{1,0:T(8,128)(2,1)S(1)} %bitcast.32), custom_call_target="tpu_custom_call" | custom-call | flops 1207959552 | bytes 9437184 | tf_op jit(solution)/shard_map/pallas_call | solution.py:445
  90.2 0.6 collective-permute-start.11
  90.8 0.5 collective-permute-done.14.refs_8_
  91.3 4.4 %collective-permute-done.13.refs_7_ = bf16[128,1536]{1,0:T(8,128)(2,1)} collective-permute-done((bf16[128,1536]{1,0:T(8,128)(2,1)S(1)}, bf16[128,1536]{1,0:T(8,128)(2,1)}, u32[]{:S(2)}, u32[]{:S(2)}) %collective-permute-start.13) | collective-permute-done | bytes 393248 | tf_op jit(solution)/shard_map/ppermute | solution.py:541
  95.8 0.1 collective-permute-done.12.refs_6_
  95.9 0.4 collective-permute-start.16
  96.3 0.1 fusion.5
  96.4 1.4 %collective-permute-done.17.refs_11_ = bf16[128,1536]{1,0:T(8,128)(2,1)} collective-permute-done((bf16[128,1536]{1,0:T(8,128)(2,1)}, bf16[128,1536]{1,0:T(8,128)(2,1)}, u32[]{:S(2)}, u32[]{:S(2)}) %collective-permute-start.17) | collective-permute-done | bytes 393248 | tf_op jit(solution)/shard_map/ppermute | solution.py:538
  97.8 0.6 collective-permute-done.16.refs_10_
  98.4 3.1 %shard_map.172 = (f32[96,1536]{1,0:T(8,128)S(1)}, bf16[96,1536]{1,0:T(8,128)(2,1)S(1)}, f32[96,1536]{1,0:T(8,128)S(1)}, bf16[96,1536]{1,0:T(8,128)(2,1)S(1)}, f3...) custom-call(bf16[1,4,96,128]{3,2,1,0:T(8,128)(2,1)S(1)} %slice.30.refs_0_, bf16[1,4,96,128]{3,2,1,0:T(8,128)(2,1)S(1)} %slice.39.refs_1_, ...), custom_call_target="tpu_custom_call" | custom-call | flops 1207959552 | bytes 5111808 | tf_op jit(solution)/shard_map/pallas_call | solution.py:492
  101.5 3.4 %collective-permute-start.19 = (bf16[96,1536]{1,0:T(8,128)(2,1)S(1)}, bf16[96,1536]{1,0:T(8,128)(2,1)S(1)}, u32[]{:S(2)}, u32[]{:S(2)}) collective-permute-start(bf16[96,1536]{1,0:T(8,128)(2,1)S(1)} %get-tuple-element.62), channel_id=1, source_target_pairs={{0,2},{2,0},{4,6},{6,4},{1,3},{3,1},{5,7},{7,5},{8,10},{10,8},{12,... | collective-permute-start | bytes 884744 | tf_op jit(solution)/shard_map/ppermute | solution.py:534
  104.9 1.4 %collective-permute-start.22 = (f32[2,384]{1,0:T(2,128)S(1)}, f32[2,384]{1,0:T(2,128)S(1)}, u32[]{:S(2)}, u32[]{:S(2)}) collective-permute-start(f32[2,384]{1,0:T(2,128)S(1)} %get-tuple-element.64), channel_id=1, source_target_pairs={{0,4},{2,6},{4,0},{6,2},{1,5},{3,7},{5,1},{7,3},{8,12},{10,14},{12... | collective-permute-start | bytes 9224 | tf_op jit(solution)/shard_map/ppermute | solution.py:534
  106.4 2.0 %collective-permute-start.21 = (bf16[96,1536]{1,0:T(8,128)(2,1)S(1)}, bf16[96,1536]{1,0:T(8,128)(2,1)S(1)}, u32[]{:S(2)}, u32[]{:S(2)}) collective-permute-start(bf16[96,1536]{1,0:T(8,128)(2,1)S(1)} %get-tuple-element.59.after_ref), channel_id=1, source_target_pairs={{0,2},{2,0},{4,6},{6,4},{1,3},{3,1},{5,7},{7,5},{8,10},{10,8},{12,... | collective-permute-start | bytes 884744 | tf_op jit(solution)/shard_map/ppermute | solution.py:534
  108.4 3.9 %collective-permute-done.22 = f32[2,384]{1,0:T(2,128)S(1)} collective-permute-done((f32[2,384]{1,0:T(2,128)S(1)}, f32[2,384]{1,0:T(2,128)S(1)}, u32[]{:S(2)}, u32[]{:S(2)}) %collective-permute-start.22) | collective-permute-done | bytes 3104 | tf_op jit(solution)/shard_map/ppermute | solution.py:534
  112.3 3.9 %collective-permute-start.23 = (f32[1,384]{1,0:T(1,128)S(1)}, f32[1,384]{1,0:T(1,128)S(1)}, u32[]{:S(2)}, u32[]{:S(2)}) collective-permute-start(f32[1,384]{1,0:T(1,128)S(1)} %slice.43), channel_id=1, source_target_pairs={{0,2},{2,0},{4,6},{6,4},{1,3},{3,1},{5,7},{7,5},{8,10},{10,8},{12,... | collective-permute-start | bytes 4616 | tf_op jit(solution)/shard_map/ppermute | solution.py:534
  116.3 3.7 %copy-done.1 = bf16[3072,1536]{1,0:T(8,128)(2,1)S(1)} copy-done((bf16[3072,1536]{1,0:T(8,128)(2,1)S(1)}, bf16[3072,1536]{1,0:T(8,128)(2,1)}, u32[]{:S(2)}) %copy-start.1) | copy-done | bytes 9437208
  120.0 2.2 %shard_map.173 = bf16[128,1536]{1,0:T(8,128)(2,1)} custom-call(f32[1,3072]{1,0:T(1,128)S(1)} %copy-done.6, bf16[128,3072]{1,0:T(8,128)(2,1)S(1)} %bitcast.33, bf16[3072,1536]{1,0:T(8,128)(2,1)S(1)} %copy-done.1, bf16[96,1536]{1,0:T(8,128)(2,1)S(1)} %get-tuple-element.59.after_ref), custom_call_target="tpu_custom_call" | custom-call | flops 1207959552 | bytes 9437184 | tf_op jit(solution)/shard_map/pallas_call | solution.py:372
  122.2 0.6 slice_add_fusion
  122.7 7.7 %collective-permute-done.20 = bf16[96,1536]{1,0:T(8,128)(2,1)S(1)} collective-permute-done((bf16[96,1536]{1,0:T(8,128)(2,1)S(1)}, bf16[96,1536]{1,0:T(8,128)(2,1)S(1)}, u32[]{:S(2)}, u32[]{:S(2)}) %collective-permute-start.20) | collective-permute-done | bytes 294944 | tf_op jit(solution)/shard_map/ppermute | solution.py:534
  130.4 0.9 convert_add_fusion
  (54 shorter events, 0.7 us)
Async XLA Ops:
  0.6 53.1 %copy-start.10 = (s32[1,64]{1,0:T(1,128)S(1)}, s32[1,64]{1,0:T(1,128)}, u32[]{:S(2)}) copy-start(s32[1,64]{1,0:T(1,128)} %src_ref.1) | copy-start | bytes 772
  0.6 81.1 %copy-start.6 = (f32[1,3072]{1,0:T(1,128)S(1)}, f32[1,3072]{1,0:T(1,128)}, u32[]{:S(2)}) copy-start(f32[1,3072]{1,0:T(1,128)} %gate_ref.5) | copy-start | bytes 36868
  0.7 81.1 %copy-start.2 = (bf16[1,128,3072]{2,1,0:T(8,128)(2,1)S(1)}, bf16[1,128,3072]{2,1,0:T(8,128)(2,1)}, u32[]{:S(2)}) copy-start(bf16[1,128,3072]{2,1,0:T(8,128)(2,1)} %param.25) | copy-start | bytes 2359300
  2.1 75.5 %copy-start.7 = (s32[3]{0:T(128)S(1)}, s32[3]{0:T(128)}, u32[]{:S(2)}) copy-start(s32[3]{0:T(128)} %pad_add_fusion.meta_ref) | copy-start | bytes 40
  8.5 2.0 %collective-permute-start = (bf16[4,320,128]{2,1,0:T(8,128)(2,1)}, bf16[4,320,128]{2,1,0:T(8,128)(2,1)S(1)}, u32[]{:S(2)}, u32[]{:S(2)}) collective-permute-start(bf16[4,320,128]{2,1,0:T(8,128)(2,1)} %get-tuple-element.36), channel_id=1, source_target_pairs={{0,1},{2,3},{4,5},{6,7},{1,0},{3,2},{5,4},{7,6},{8,9},{10,11},{12,... | collective-permute-start | bytes 983048 | tf_op jit(solution)/shard_map/ppermute | solution.py:538
  10.5 0.7 copy-start.8
  13.9 19.8 %collective-permute-start.1 = (bf16[1472,128]{1,0:T(8,128)(2,1)}, bf16[1472,128]{1,0:T(8,128)(2,1)S(1)}, u32[]{:S(2)}, u32[]{:S(2)}) collective-permute-start(bf16[1472,128]{1,0:T(8,128)(2,1)} %get-tuple-element.40), channel_id=1, source_target_pairs={{0,2},{2,0},{4,6},{6,4},{1,3},{3,1},{5,7},{7,5},{8,10},{10,8},{12,... | collective-permute-start | bytes 1130504 | tf_op jit(solution)/shard_map/ppermute | solution.py:534
  16.9 28.9 %collective-permute-start.2 = (bf16[1472,128]{1,0:T(8,128)(2,1)}, bf16[1472,128]{1,0:T(8,128)(2,1)S(1)}, u32[]{:S(2)}, u32[]{:S(2)}) collective-permute-start(bf16[1472,128]{1,0:T(8,128)(2,1)} %get-tuple-element.41), channel_id=1, source_target_pairs={{0,4},{2,6},{4,0},{6,2},{1,5},{3,7},{5,1},{7,3},{8,12},{10,14},{12... | collective-permute-start | bytes 1130504 | tf_op jit(solution)/shard_map/ppermute | solution.py:534
  19.5 26.3 %collective-permute-start.3 = (bf16[1472,128]{1,0:T(8,128)(2,1)}, bf16[1472,128]{1,0:T(8,128)(2,1)S(1)}, u32[]{:S(2)}, u32[]{:S(2)}) collective-permute-start(bf16[1472,128]{1,0:T(8,128)(2,1)} %get-tuple-element.42), channel_id=1, source_target_pairs={{0,6},{2,4},{4,2},{6,0},{1,7},{3,5},{5,3},{7,1},{8,14},{10,12},{12... | collective-permute-start | bytes 1130504 | tf_op jit(solution)/shard_map/ppermute | solution.py:534
  21.9 68.3 %copy-start.3 = (bf16[2,4,96,128]{3,2,1,0:T(8,128)(2,1)S(1)}, bf16[2,4,96,128]{3,2,1,0:T(8,128)(2,1)}, u32[]{:S(2)}) copy-start(bf16[2,4,96,128]{3,2,1,0:T(8,128)(2,1)} %get-tuple-element.56.refs_0_) | copy-start | bytes 589828
  45.9 1.0 copy-start.4
  46.8 0.9 copy-start.5
  50.1 3.7 %collective-permute-start.4 = (bf16[3760,128]{1,0:T(8,128)(2,1)}, bf16[3760,128]{1,0:T(8,128)(2,1)}, u32[]{:S(2)}, u32[]{:S(2)}) collective-permute-start(bf16[3760,128]{1,0:T(8,128)(2,1)} %get-tuple-element.46.refs_3_), channel_id=1, source_target_pairs={{0,1},{2,3},{4,5},{6,7},{1,0},{3,2},{5,4},{7,6},{8,9},{10,11},{12,... | collective-permute-start | bytes 2887688 | tf_op jit(solution)/shard_map/ppermute | solution.py:538
  50.2 17.9 %collective-permute-start.8 = (bf16[2,4,96,128]{3,2,1,0:T(8,128)(2,1)}, bf16[2,4,96,128]{3,2,1,0:T(8,128)(2,1)S(1)}, u32[]{:S(2)}, u32[]{:S(2)}) collective-permute-start(bf16[2,4,96,128]{3,2,1,0:T(8,128)(2,1)} %get-tuple-element.52), channel_id=1, source_target_pairs={{0,8},{8,0},{16,24},{24,16},{1,9},{9,1},{17,25},{25,17},{2,10},{10... | collective-permute-start | bytes 589832 | tf_op jit(solution)/shard_map/ppermute | solution.py:541
  51.7 17.9 %collective-permute-start.9 = (bf16[2,4,96,128]{3,2,1,0:T(8,128)(2,1)}, bf16[2,4,96,128]{3,2,1,0:T(8,128)(2,1)S(1)}, u32[]{:S(2)}, u32[]{:S(2)}) collective-permute-start(bf16[2,4,96,128]{3,2,1,0:T(8,128)(2,1)} %get-tuple-element.53), channel_id=1, source_target_pairs={{0,16},{8,24},{16,0},{24,8},{1,17},{9,25},{17,1},{25,9},{2,18},{10... | collective-permute-start | bytes 589832 | tf_op jit(solution)/shard_map/ppermute | solution.py:541
  53.3 16.4 %collective-permute-start.10 = (bf16[2,4,96,128]{3,2,1,0:T(8,128)(2,1)}, bf16[2,4,96,128]{3,2,1,0:T(8,128)(2,1)S(1)}, u32[]{:S(2)}, u32[]{:S(2)}) collective-permute-start(bf16[2,4,96,128]{3,2,1,0:T(8,128)(2,1)} %get-tuple-element.54), channel_id=1, source_target_pairs={{0,24},{8,16},{16,8},{24,0},{1,25},{9,17},{17,9},{25,1},{2,26},{10... | collective-permute-start | bytes 589832 | tf_op jit(solution)/shard_map/ppermute | solution.py:541
  59.3 11.0 %collective-permute-start.5 = (bf16[136,384]{1,0:T(8,128)(2,1)S(1)}, bf16[136,384]{1,0:T(8,128)(2,1)S(1)}, u32[]{:S(2)}, u32[]{:S(2)}) collective-permute-start(bf16[136,384]{1,0:T(8,128)(2,1)S(1)} %pad_maximum_fusion.1), channel_id=1, source_target_pairs={{0,2},{2,0},{4,6},{6,4},{1,3},{3,1},{5,7},{7,5},{8,10},{10,8},{12,... | collective-permute-start | bytes 313352 | tf_op jit(solution)/shard_map/ppermute | solution.py:534
  66.9 10.7 %collective-permute-start.6 = (bf16[136,384]{1,0:T(8,128)(2,1)S(1)}, bf16[136,384]{1,0:T(8,128)(2,1)S(1)}, u32[]{:S(2)}, u32[]{:S(2)}) collective-permute-start(bf16[136,384]{1,0:T(8,128)(2,1)S(1)} %pad_maximum_fusion.2), channel_id=1, source_target_pairs={{0,4},{2,6},{4,0},{6,2},{1,5},{3,7},{5,1},{7,3},{8,12},{10,14},{12... | collective-permute-start | bytes 313352 | tf_op jit(solution)/shard_map/ppermute | solution.py:534
  68.1 9.5 %collective-permute-start.7 = (bf16[136,384]{1,0:T(8,128)(2,1)S(1)}, bf16[136,384]{1,0:T(8,128)(2,1)S(1)}, u32[]{:S(2)}, u32[]{:S(2)}) collective-permute-start(bf16[136,384]{1,0:T(8,128)(2,1)S(1)} %pad_maximum_fusion.3), channel_id=1, source_target_pairs={{0,6},{2,4},{4,2},{6,0},{1,7},{3,5},{5,3},{7,1},{8,14},{10,12},{12... | collective-permute-start | bytes 313352 | tf_op jit(solution)/shard_map/ppermute | solution.py:534
  78.2 13.1 %collective-permute-start.14 = (bf16[128,1536]{1,0:T(8,128)(2,1)S(1)}, bf16[128,1536]{1,0:T(8,128)(2,1)}, u32[]{:S(2)}, u32[]{:S(2)}) collective-permute-start(bf16[128,1536]{1,0:T(8,128)(2,1)S(1)} %shard_map.169.attn_ref.refs_5_), channel_id=1, source_target_pairs={{0,24},{8,16},{16,8},{24,0},{1,25},{9,17},{17,9},{25,1},{2,26},{10... | collective-permute-start | bytes 1179656 | tf_op jit(solution)/shard_map/ppermute | solution.py:541
  80.7 15.0 %collective-permute-start.13 = (bf16[128,1536]{1,0:T(8,128)(2,1)S(1)}, bf16[128,1536]{1,0:T(8,128)(2,1)}, u32[]{:S(2)}, u32[]{:S(2)}) collective-permute-start(bf16[128,1536]{1,0:T(8,128)(2,1)S(1)} %shard_map.169.attn_ref.refs_5_), channel_id=1, source_target_pairs={{0,16},{8,24},{16,0},{24,8},{1,17},{9,25},{17,1},{25,9},{2,18},{10... | collective-permute-start | bytes 1179656 | tf_op jit(solution)/shard_map/ppermute | solution.py:541
  81.2 14.6 %collective-permute-start.12 = (bf16[128,1536]{1,0:T(8,128)(2,1)S(1)}, bf16[128,1536]{1,0:T(8,128)(2,1)}, u32[]{:S(2)}, u32[]{:S(2)}) collective-permute-start(bf16[128,1536]{1,0:T(8,128)(2,1)S(1)} %shard_map.169.attn_ref.refs_5_), channel_id=1, source_target_pairs={{0,8},{8,0},{16,24},{24,16},{1,9},{9,1},{17,25},{25,17},{2,10},{10... | collective-permute-start | bytes 1179656 | tf_op jit(solution)/shard_map/ppermute | solution.py:541
  81.8 3.7 %copy-start = (bf16[3072,1536]{1,0:T(8,128)(2,1)S(1)}, bf16[3072,1536]{1,0:T(8,128)(2,1)}, u32[]{:S(2)}) copy-start(bf16[3072,1536]{1,0:T(8,128)(2,1)} %w_ref.5) | copy-start | bytes 28311556
  90.2 6.2 %collective-permute-start.15 = (bf16[144,1536]{1,0:T(8,128)(2,1)}, bf16[144,1536]{1,0:T(8,128)(2,1)S(1)}, u32[]{:S(2)}, u32[]{:S(2)}) collective-permute-start(bf16[144,1536]{1,0:T(8,128)(2,1)} %get-tuple-element.57), channel_id=1, source_target_pairs={{0,1},{2,3},{4,5},{6,7},{1,0},{3,2},{5,4},{7,6},{8,9},{10,11},{12,... | collective-permute-start | bytes 1327112 | tf_op jit(solution)/shard_map/ppermute | solution.py:538
  90.2 6.2 %collective-permute-start.11 = (bf16[4,4,96,128]{3,2,1,0:T(8,128)(2,1)S(1)}, bf16[4,4,96,128]{3,2,1,0:T(8,128)(2,1)}, u32[]{:S(2)}, u32[]{:S(2)}) collective-permute-start(bf16[4,4,96,128]{3,2,1,0:T(8,128)(2,1)S(1)} %shard_map.171), channel_id=1, source_target_pairs={{0,1},{2,3},{4,5},{6,7},{1,0},{3,2},{5,4},{7,6},{8,9},{10,11},{12,... | collective-permute-start | bytes 1179656 | tf_op jit(solution)/shard_map/ppermute | solution.py:538
  91.3 5.1 %collective-permute-start.18 = (bf16[128,1536]{1,0:T(8,128)(2,1)}, bf16[128,1536]{1,0:T(8,128)(2,1)}, u32[]{:S(2)}, u32[]{:S(2)}) collective-permute-start(bf16[128,1536]{1,0:T(8,128)(2,1)} %collective-permute-done.14.refs_8_), channel_id=1, source_target_pairs={{0,1},{2,3},{4,5},{6,7},{1,0},{3,2},{5,4},{7,6},{8,9},{10,11},{12,... | collective-permute-start | bytes 1179656 | tf_op jit(solution)/shard_map/ppermute | solution.py:538
  95.8 2.1 %collective-permute-start.17 = (bf16[128,1536]{1,0:T(8,128)(2,1)}, bf16[128,1536]{1,0:T(8,128)(2,1)}, u32[]{:S(2)}, u32[]{:S(2)}) collective-permute-start(bf16[128,1536]{1,0:T(8,128)(2,1)} %collective-permute-done.13.refs_7_), channel_id=1, source_target_pairs={{0,1},{2,3},{4,5},{6,7},{1,0},{3,2},{5,4},{7,6},{8,9},{10,11},{12,... | collective-permute-start | bytes 1179656 | tf_op jit(solution)/shard_map/ppermute | solution.py:538
  95.9 2.5 %collective-permute-start.16 = (bf16[128,1536]{1,0:T(8,128)(2,1)}, bf16[128,1536]{1,0:T(8,128)(2,1)}, u32[]{:S(2)}, u32[]{:S(2)}) collective-permute-start(bf16[128,1536]{1,0:T(8,128)(2,1)} %collective-permute-done.12.refs_6_), channel_id=1, source_target_pairs={{0,1},{2,3},{4,5},{6,7},{1,0},{3,2},{5,4},{7,6},{8,9},{10,11},{12,... | collective-permute-start | bytes 1179656 | tf_op jit(solution)/shard_map/ppermute | solution.py:538
  101.5 14.7 %collective-permute-start.19 = (bf16[96,1536]{1,0:T(8,128)(2,1)S(1)}, bf16[96,1536]{1,0:T(8,128)(2,1)S(1)}, u32[]{:S(2)}, u32[]{:S(2)}) collective-permute-start(bf16[96,1536]{1,0:T(8,128)(2,1)S(1)} %get-tuple-element.62), channel_id=1, source_target_pairs={{0,2},{2,0},{4,6},{6,4},{1,3},{3,1},{5,7},{7,5},{8,10},{10,8},{12,... | collective-permute-start | bytes 884744 | tf_op jit(solution)/shard_map/ppermute | solution.py:534
  104.9 7.4 %collective-permute-start.22 = (f32[2,384]{1,0:T(2,128)S(1)}, f32[2,384]{1,0:T(2,128)S(1)}, u32[]{:S(2)}, u32[]{:S(2)}) collective-permute-start(f32[2,384]{1,0:T(2,128)S(1)} %get-tuple-element.64), channel_id=1, source_target_pairs={{0,4},{2,6},{4,0},{6,2},{1,5},{3,7},{5,1},{7,3},{8,12},{10,14},{12... | collective-permute-start | bytes 9224 | tf_op jit(solution)/shard_map/ppermute | solution.py:534
  106.4 25.0 %copy-start.9 = (bf16[1,8,1536]{2,1,0:T(8,128)(2,1)}, bf16[1,8,1536]{2,1,0:T(8,128)(2,1)S(1)}, u32[]{:S(2)}) copy-start(bf16[1,8,1536]{2,1,0:T(8,128)(2,1)S(1)} %fusion.1) | copy-start | bytes 73732
  106.4 16.4 %collective-permute-start.21 = (bf16[96,1536]{1,0:T(8,128)(2,1)S(1)}, bf16[96,1536]{1,0:T(8,128)(2,1)S(1)}, u32[]{:S(2)}, u32[]{:S(2)}) collective-permute-start(bf16[96,1536]{1,0:T(8,128)(2,1)S(1)} %get-tuple-element.59.after_ref), channel_id=1, source_target_pairs={{0,2},{2,0},{4,6},{6,4},{1,3},{3,1},{5,7},{7,5},{8,10},{10,8},{12,... | collective-permute-start | bytes 884744 | tf_op jit(solution)/shard_map/ppermute | solution.py:534
  112.3 9.9 %collective-permute-start.23 = (f32[1,384]{1,0:T(1,128)S(1)}, f32[1,384]{1,0:T(1,128)S(1)}, u32[]{:S(2)}, u32[]{:S(2)}) collective-permute-start(f32[1,384]{1,0:T(1,128)S(1)} %slice.43), channel_id=1, source_target_pairs={{0,2},{2,0},{4,6},{6,4},{1,3},{3,1},{5,7},{7,5},{8,10},{10,8},{12,... | collective-permute-start | bytes 4616 | tf_op jit(solution)/shard_map/ppermute | solution.py:534
  116.3 14.2 %collective-permute-start.20 = (bf16[96,1536]{1,0:T(8,128)(2,1)S(1)}, bf16[96,1536]{1,0:T(8,128)(2,1)S(1)}, u32[]{:S(2)}, u32[]{:S(2)}) collective-permute-start(bf16[96,1536]{1,0:T(8,128)(2,1)S(1)} %add_convert_fusion), channel_id=1, source_target_pairs={{0,4},{2,6},{4,0},{6,2},{1,5},{3,7},{5,1},{7,3},{8,12},{10,14},{12... | collective-permute-start | bytes 884744 | tf_op jit(solution)/shard_map/ppermute | solution.py:534
  116.3 3.7 %copy-start.1 = (bf16[3072,1536]{1,0:T(8,128)(2,1)S(1)}, bf16[3072,1536]{1,0:T(8,128)(2,1)}, u32[]{:S(2)}) copy-start(bf16[3072,1536]{1,0:T(8,128)(2,1)} %w_ref.5) | copy-start | bytes 28311556

commit v8 on v7

--- a/solution.py
+++ b/solution.py
@@ -45,9 +45,8 @@
 
 def text_kernel(
     groups, heads, place_of, meta_ref, len_ref, src_ref, states_ref, gain_ref, qg_ref, kg_ref,
-    w_ref, k_ref, v_ref, q_ref, own_ref, *refs
+    w_ref, own_ref, *refs
 ):
-    packed, refs = refs[:groups], refs[groups:]
     msgs, (w_all, w_sems) = refs[:-2], refs[-2:]
     size = own_ref.shape[2]
     rows = (own_ref.shape[1] - EXTRA) // (3 * heads + 1)
@@ -61,14 +60,6 @@
             cols = pl.ds(pl.multiple_of(at, 128), width)
             copies.append(pltpu.make_async_copy(w_ref.at[:, cols], w_all.at[g, i], w_sems.at[g, i]))
             copies[-1].start()
-    local = k_ref.shape[0]
-    for g, out in enumerate(packed):
-        for i, ref in enumerate((k_ref, v_ref, q_ref)):
-            for head in range(heads):
-                at = ((meta_ref[0] ^ g) * heads + head) * size
-                to = (i * heads + head) * local
-                out[to : to + local, :] = ref[:, pl.ds(pl.multiple_of(at, 128), size)]
-
     def slot_at(row):
         z_at = (row % rows) // slot_local
         return place_of(meta_ref[1] ^ (row // rows), z_at) * slot_local + row % slot_local
@@ -106,24 +97,19 @@
 
 
 def text_project(
-    meta, length, sources, states, gain, query_gain, key_gain, text_proj, keys, values, queries,
-    groups, parts, place_of
+    meta, length, sources, states, gain, query_gain, key_gain, text_proj, groups, parts, place_of
 ):
     slots, depth = states.shape
     size = query_gain.shape[1]
-    local = keys.shape[0]
     heads = text_proj.shape[1] // (3 * groups * size)
     text_rows = (3 * heads + 1) * slots // parts
     shapes = [jax.ShapeDtypeStruct((groups, text_rows + EXTRA, size), f32)]
-    for g in range(groups):
-        rows = 3 * heads * local + (text_rows if g else 0)
-        shapes.append(jax.ShapeDtypeStruct((rows, size), bf16))
     shapes += [jax.ShapeDtypeStruct((groups, text_rows, size), bf16)] * (parts - 1)
     return pl.pallas_call(
         functools.partial(text_kernel, groups, heads, place_of),
         out_shape=shapes,
-        in_specs=[SMEM, SMEM] + [VMEM] * 5 + [ANY] + [VMEM] * 3,
-        out_specs=[VMEM] * (groups + parts),
+        in_specs=[SMEM, SMEM] + [VMEM] * 5 + [ANY],
+        out_specs=[VMEM] * parts,
         scratch_shapes=[
             pltpu.VMEM((groups, 3, depth, heads * size), bf16),
             pltpu.SemaphoreType.DMA((groups, 3)),
@@ -132,124 +118,118 @@
         cost_estimate=cost(
             2 * slots * depth * text_proj.shape[1], 2 * depth * text_proj.shape[1]
         ),
-    )(
-        meta, length, sources, states, gain, query_gain, key_gain, text_proj, keys, values, queries
-    )
-
-
-def pack_kernel(n_got, n_out, tail_rows, *refs):
-    own_ref, got, refs = refs[0], refs[1 : 1 + n_got], refs[1 + n_got + n_out :]
-    kept_ref, outs, (stage, sems) = refs[0], refs[1 : 1 + n_out], refs[1 + n_out :]
-    text_rows, size = stage.shape[1:]
-    copies = []
-    for g in list(range(1, n_out + 1)) + [0]:
+    )(meta, length, sources, states, gain, query_gain, key_gain, text_proj)
+
+
+def pack_kernel(groups, size, meta_ref, k_ref, v_ref, q_ref, *outs):
+    rows = k_ref.shape[0]
+    heads = k_ref.shape[1] // (groups * size)
+    for g, out in enumerate(outs):
+        for i, ref in enumerate((k_ref, v_ref, q_ref)):
+            for head in range(heads):
+                at = ((meta_ref[0] ^ g) * heads + head) * size
+                to = (i * heads + head) * rows
+                out[to : to + rows, :] = ref[:, pl.ds(pl.multiple_of(at, 128), size)]
+
+
+def pack(meta, keys, values, queries, groups, size):
+    rows, width = keys.shape
+    shape = jax.ShapeDtypeStruct((3 * rows * width // (groups * size), size), bf16)
+    return pl.pallas_call(
+        functools.partial(pack_kernel, groups, size),
+        out_shape=[shape] * groups,
+        in_specs=[SMEM] + [VMEM] * 3,
+        out_specs=[VMEM] * groups,
+        compiler_params=params(60),
+        cost_estimate=cost(0, 12 * rows * width),
+    )(meta, keys, values, queries)
+
+
+def text_sum_kernel(n_got, tail_rows, own_ref, *refs):
+    got, (keep_ref, send_ref) = refs[:n_got], refs[n_got:]
+    groups, text_rows, size = got[0].shape
+    for g in range(groups):
         total = own_ref[g, :text_rows, :]
         for ref in got:
             total = total + ref[g].astype(f32)
-        tail = split_tail(joined(total[text_rows - tail_rows :]), size)
-        total = jnp.concatenate([total[: text_rows - tail_rows], tail], axis=0)
-        if g == 0:
-            kept_ref[:text_rows, :] = total
-            kept_ref[text_rows:, :] = own_ref[0, text_rows:, :]
+        end = text_rows - tail_rows
+        tail = split_tail(joined(total[end:]), size)
+        if g % 2 == 0:
+            keep_ref[g // 2, :end, :] = total[:end]
+            keep_ref[g // 2, end:text_rows, :] = tail
+            keep_ref[g // 2, text_rows:, :] = own_ref[g, text_rows:, :]
         else:
-            stage[g - 1] = total.astype(bf16)
-            start = outs[g - 1].shape[0] - text_rows
-            target = outs[g - 1].at[pl.ds(start, text_rows), :]
-            copies.append(pltpu.make_async_copy(stage.at[g - 1], target, sems.at[g - 1]))
-            copies[-1].start()
-    for copy in copies:
-        copy.wait()
-
-
-def pack(own, got, packed, tail_rows):
+            send_ref[g // 2, :end, :] = total[:end].astype(bf16)
+            send_ref[g // 2, end:, :] = tail.astype(bf16)
+
+
+def text_sum(own, got, tail_rows):
     groups, rows, size = own.shape
-    text_rows = rows - EXTRA
-    n = len(packed)
-    shapes = [jax.ShapeDtypeStruct((rows, size), f32)]
-    shapes += [jax.ShapeDtypeStruct(p.shape, bf16) for p in packed]
-    return pl.pallas_call(
-        functools.partial(pack_kernel, len(got), n, tail_rows),
-        out_shape=shapes,
-        in_specs=[VMEM] * (1 + len(got)) + [ANY] * n,
-        out_specs=[VMEM] + [ANY] * n,
-        input_output_aliases={1 + len(got) + i: 1 + i for i in range(n)},
-        scratch_shapes=[pltpu.VMEM((n, text_rows, size), bf16), pltpu.SemaphoreType.DMA((n,))],
-        compiler_params=params(60),
+    return pl.pallas_call(
+        functools.partial(text_sum_kernel, len(got), tail_rows),
+        out_shape=[
+            jax.ShapeDtypeStruct((groups // 2, rows, size), f32),
+            jax.ShapeDtypeStruct((groups // 2, rows - EXTRA, size), bf16),
+        ],
+        in_specs=[VMEM] * (1 + len(got)),
+        out_specs=[VMEM] * 2,
+        compiler_params=params(),
         cost_estimate=cost(0, 8 * groups * rows * size),
-    )(own, *got, *packed)
-
-
-def block_kernel(features, heads, n_got, near_ref, own_hbm, *refs):
-    got, (out_ref, _, _, own_ref, sems) = refs[:n_got], refs[-5:]
-    size = own_ref.shape[1]
-    image_rows = near_ref.shape[0]
-    copies = [
-        pltpu.make_async_copy(own_hbm, own_ref, sems.at[0]),
-        pltpu.make_async_copy(near_ref, out_ref.at[pl.ds(0, image_rows), :], sems.at[1]),
-    ]
-    for copy in copies:
-        copy.start()
-    kv_rows = image_rows // 3 * 2
-    for k, ref in enumerate(got):
-        at = image_rows + k * kv_rows
-        out_ref[at : at + kv_rows, :] = ref[:kv_rows, :]
-    copies[0].wait()
-    text_rows = own_ref.shape[0] - EXTRA
+    )(own, *got)
+
+
+def block_kernel(features, heads, n_far, own_ref, got_ref, mark_ref, *refs):
+    del mark_ref
+    far, out_ref = refs[:n_far], refs[n_far]
+    kv_rows = far[0].shape[0] // 3 * 2
+    for k, ref in enumerate(far):
+        out_ref[k * kv_rows : (k + 1) * kv_rows, :] = ref[:kv_rows, :]
+    size = own_ref.shape[2]
+    text_rows = got_ref.shape[1]
     rows = text_rows // (3 * heads + 1)
-    total = own_ref[:text_rows, :]
-    for ref in got:
-        total = total + ref[image_rows:, :].astype(f32)
+    total = own_ref[0, :text_rows, :] + got_ref[0].astype(f32)
     rate = lax.rsqrt(joined(total[3 * heads * rows :]) / features + eps_norm)
-    end = image_rows + n_got * kv_rows
+    start = n_far * kv_rows
     for i in range(3):
         for head in range(heads):
             at = (i * heads + head) * rows
             x = total[at : at + rows] * rate
             if i < 2:
                 mean = jnp.sum(x * x, axis=1, keepdims=True) / size
-                gain = own_ref[text_rows + i : text_rows + i + 1, :]
+                gain = own_ref[0, text_rows + i : text_rows + i + 1, :]
                 x = x * lax.rsqrt(mean + eps_norm) * gain
-            out_ref[end + at : end + at + rows, :] = x.astype(bf16)
-    bias = own_ref[text_rows + 2 : text_rows + 3, :]
-    at = end + 3 * heads * rows
-    out_ref[at:, :] = jnp.broadcast_to(bias, (EXTRA, size)).astype(bf16)
-    copies[1].wait()
-
-
-def block_of(near, own, got, mark, features, heads):
-    image_rows, size = near.shape
-    text_rows = own.shape[0] - EXTRA
-    total = image_rows + image_rows // 3 * 2 * len(got)
-    total += text_rows // (3 * heads + 1) * 3 * heads + EXTRA
-    return pl.pallas_call(
-        functools.partial(block_kernel, features, heads, len(got)),
-        out_shape=[
-            jax.ShapeDtypeStruct((total, size), bf16),
-            jax.ShapeDtypeStruct(near.shape, bf16),
-            jax.ShapeDtypeStruct(own.shape, f32),
-        ],
-        in_specs=[ANY] * 2 + [VMEM] * len(got) + [SMEM],
-        out_specs=[VMEM, ANY, ANY],
-        input_output_aliases={0: 1, 1: 2},
-        scratch_shapes=[pltpu.VMEM(own.shape, f32), pltpu.SemaphoreType.DMA((2,))],
+            out_ref[start + at : start + at + rows, :] = x.astype(bf16)
+    bias = own_ref[0, text_rows + 2 : text_rows + 3, :]
+    start = start + 3 * heads * rows
+    out_ref[start:, :] = jnp.broadcast_to(bias, (EXTRA, size)).astype(bf16)
+
+
+def block_of(own, got, mark, far, features, heads):
+    rows, size = own.shape[1:]
+    total = (rows - EXTRA) // (3 * heads + 1) * 3 * heads + EXTRA
+    total += far[0].shape[0] // 3 * 2 * len(far)
+    return pl.pallas_call(
+        functools.partial(block_kernel, features, heads, len(far)),
+        out_shape=jax.ShapeDtypeStruct((total, size), bf16),
+        in_specs=[VMEM] * 2 + [SMEM] + [VMEM] * len(far),
+        out_specs=VMEM,
         compiler_params=params(),
         cost_estimate=cost(0, 4 * total * size),
-    )(near, own, *got, mark)[0]
-
-
-def attention_kernel(n_far, n_blocks, heads, rows, text_rows, *refs):
-    far, refs = refs[:n_far], refs[n_far:]
-    blocks, refs = refs[:n_blocks], refs[n_blocks:]
+    )(own, got, mark, *far)
+
+
+def attention_kernel(n_pieces, n_cores, heads, rows, text_rows, *refs):
+    pieces, refs = refs[:n_pieces], refs[n_pieces:]
+    nears, refs = refs[: n_cores - 1], refs[n_cores - 1 :]
+    blocks, refs = refs[:n_cores], refs[n_cores:]
     out_refs, tout_ref = refs[:-1], refs[-1]
     size = blocks[0].shape[1]
     factor = size ** (-0.5) * math.log2(math.e)
     nt = (((1,), (1,)), ((), ()))
-    near = 3 * heads * rows
     kv_rows = 2 * heads * rows
-    starts = [0] + [near + k * kv_rows for k in range(n_far)]
-    text = near + n_far * kv_rows
+    text = (n_pieces - 1) * kv_rows
     end = text + 3 * heads * text_rows
-    bias = blocks[0][end : end + EXTRA, :][:1, : n_blocks * text_rows].astype(f32)
+    bias = blocks[0][end : end + EXTRA, :][:1, : n_cores * text_rows].astype(f32)
 
     def with_ones(values):
         return jnp.concatenate([values, jnp.ones(values.shape, bf16)], axis=1)
@@ -258,17 +238,18 @@
         kv, tkv = [], []
         for i in range(2):
             at = (i * heads + head) * rows
+            image = [r[at : at + rows, :] for r in tuple(pieces) + tuple(nears)]
+            for b in blocks[1:]:
+                starts = [k * kv_rows + at for k in range(n_pieces - 1)]
+                image += [b[start : start + rows, :] for start in starts]
             text_at = text + ((i + 1) * heads + head) * text_rows
-            image = [b[start + at : start + at + rows, :] for b in blocks for start in starts]
             kv.append(jnp.concatenate(image, axis=0))
             tkv.append(jnp.concatenate([b[text_at : text_at + text_rows, :] for b in blocks], axis=0))
         keys, values = kv[0], with_ones(kv[1])
         tkeys, tvalues = tkv[0], with_ones(tkv[1])
         cols = slice(head * size, (head + 1) * size)
         q_at = (2 * heads + head) * rows
-        work = [
-            (ref[q_at : q_at + rows, :], out) for ref, out in zip((blocks[0],) + far, out_refs)
-        ]
+        work = [(ref[q_at : q_at + rows, :], out) for ref, out in zip(pieces, out_refs)]
         tq_at = text + head * text_rows
         work.append((blocks[0][tq_at : tq_at + text_rows, :], tout_ref))
         for q, out_ref in work:
@@ -284,18 +265,17 @@
             out_ref[:, cols] = (acc[:, :size] / acc[:, size:]).astype(bf16)
 
 
-def attention(far, blocks, heads, rows, text_rows):
+def attention(pieces, nears, blocks, heads, rows, text_rows):
     size = blocks[0].shape[1]
-    queries = (1 + len(far)) * rows + text_rows
+    n = len(pieces)
+    queries = n * rows + text_rows
     keys = len(blocks) * queries
-    shapes = [jax.ShapeDtypeStruct((rows, heads * size), bf16)] * (1 + len(far))
+    shapes = [jax.ShapeDtypeStruct((rows, heads * size), bf16)] * n
     shapes += [jax.ShapeDtypeStruct((text_rows, heads * size), bf16)]
     return pl.pallas_call(
-        functools.partial(
-            attention_kernel, len(far), len(blocks), heads, rows, text_rows
-        ),
+        functools.partial(attention_kernel, n, len(blocks), heads, rows, text_rows),
         out_shape=shapes,
-        in_specs=[VMEM] * (len(far) + len(blocks)),
+        in_specs=[VMEM] * (n + len(nears) + len(blocks)),
         out_specs=[VMEM] * len(shapes),
         compiler_params=params(),
         cost_estimate=cost(
@@ -303,7 +283,7 @@
             4 * (queries + keys) * heads * size,
             queries * keys * heads,
         ),
-    )(*far, *blocks)
+    )(*pieces, *nears, *blocks)
 
 
 def assemble_kernel(groups, n_after, meta_ref, *refs):
@@ -501,6 +481,25 @@
     )(*lefts, *pieces, term)
 
 
+def pair_kernel(own_ref, got_ref, gate_ref, out_ref, gate_out):
+    out_ref[...] = (own_ref[...] + got_ref[...].astype(f32)).astype(bf16)
+    gate_out[...] = gate_ref[...]
+
+
+def pair_sum(own, got, gate):
+    return pl.pallas_call(
+        pair_kernel,
+        out_shape=[
+            jax.ShapeDtypeStruct(got.shape, bf16),
+            jax.ShapeDtypeStruct(gate.shape, f32),
+        ],
+        in_specs=[VMEM] * 3,
+        out_specs=[VMEM] * 2,
+        compiler_params=params(),
+        cost_estimate=cost(0, 8 * own.size),
+    )(own, got, gate)
+
+
 def on_device(
     caption_states,
     caption_gain,
@@ -555,21 +554,23 @@
 
     heads = gw // head_size
     text_rows = G * slot_local
-    own, *rest = text_project(
+    packed = pack(meta, image_k[0], image_v[0], image_q[0], G, head_size)
+    images = [packed[0]] + [to_z(packed[k], k) for k in range(1, G)]
+    nears = [to_oc(packed[0], j) for j in range(1, OC)]
+
+    own, *sent = text_project(
         meta, caption_len, slot_source, caption_states[0], caption_gain[None],
-        query_gain[None], key_gain[None], text_proj, image_k[0], image_v[0], image_q[0],
-        G, OC, place,
+        query_gain[None], key_gain[None], text_proj, G, OC, place,
     )
-    packed, sent = rest[:G], rest[G:]
     got = [to_oc(x, j + 1) for j, x in enumerate(sent)]
-    own, *messages = pack(own, got, packed[1:], text_rows)
-    far = {k: to_z(messages[k - 1], k) for k in order}
-    far = [far[k] for k in range(1, G)]
+    own, sent = text_sum(own, got, text_rows)
+    own, sent = text_sum(own, [to_z(sent, 1)], text_rows)
+    got = to_z(sent, 2)
 
     *gg, mark = gated_parts(meta, gate, d_out[0], n_dp, G, OC, place)
-    block = block_of(packed[0], own, far, mark, DT5, heads)
+    block = block_of(own, got, mark, images[1:], DT5, heads)
     blocks = [block] + [to_oc(block, j) for j in range(1, OC)]
-    *outs, text_out = attention(far, blocks, heads, image_local, text_rows)
+    *outs, text_out = attention(images, nears, blocks, heads, image_local, text_rows)
 
     back = []
     for k in range(G):
@@ -592,8 +593,8 @@
     for j in range(1, OC):
         pieces += [to_oc(sent[j - 1], j)] + [to_oc(p, j) for p in pieces[1:n_dp]]
     *grads, kept, sent = grad_product(lefts, pieces, term)
-    pair = grads[2] + to_z(grads[3], 1).astype(f32)
-    grad_wo = grads[0] + to_z(pair.astype(bf16), 2).astype(f32) + to_z(grads[1], 1).astype(f32)
+    pair, sent = pair_sum(grads[2], to_z(grads[3], 1), sent)
+    grad_wo = grads[0] + to_z(pair, 2).astype(f32) + to_z(grads[1], 1).astype(f32)
     term = kept + to_z(sent, 2)
     grad_gate = term[:1] + to_z(term[1:], 1)
     d_attn = attn_gradient(gate, d_out[0], out_weight, grads[1])

time: 132 us -> 125 us (0.947)
  starting transfers between devices: 35.2 us -> 31.8 us
  Pallas kernels: 29.8 us -> 27.2 us
    ppermute x11 -> x13, starting transfers between devices: 26.6 us -> 23.1 us  [to_z(): return lax.ppermute(x, 'seq', perm)]
    pallas_call x3 -> x6, Pallas kernels: 10.5 us -> 8.75 us  [the longest x1 5.04 us: attention(): pl.pallas_call(functools.partial(attention_kernel, n, len(blocks), heads,...]
    ppermute x11 -> x13, waiting for transfers between devices: 43.5 us -> 41.9 us  [to_z(): return lax.ppermute(x, 'seq', perm)]
    unnamed x22 -> x20, local copies, waits for them, and re-layouts: 9.99 us -> 9.45 us
    ppermute x7 -> x8, waiting for transfers between devices: 3.44 us -> 3.74 us  [to_oc(): return lax.ppermute(x, 'seq', perm)]
  transfers between devices with their start and end apart: 24 -> 27, of which waited for: 12 -> 13; matrix products, arithmetic and copies ran while one was open for 1% -> 1% of each run, Pallas kernels for 11% -> 14%
where the time goes in v8:
time: 125 us
  waiting for transfers between devices  51.8 us (41%)
  starting transfers between devices  31.8 us (25%)
  Pallas kernels  27.2 us (22%)
  local copies, waits for them, and re-layouts  9.59 us (8%)
  other arithmetic  2.52 us (2%)
  between operations  1.66 us (1%)
    ppermute x13, waiting for transfers between devices, to_z(): return lax.ppermute(x, 'seq', perm)  41.9 us
    ppermute x13, starting transfers between devices, to_z(): return lax.ppermute(x, 'seq', perm)  23.1 us
    unnamed x20, local copies, waits for them, and re-layouts  9.45 us
    ppermute x6, starting transfers between devices, to_dp(): return lax.ppermute(x, 'dp', [(a, a ^ k) for a in range(n_dp)])  7.11 us
    ppermute x6, waiting for transfers between devices, to_dp(): return lax.ppermute(x, 'dp', [(a, a ^ k) for a in range(n_dp)])  6.24 us
    pallas_call x1, Pallas kernels, text_project(): pl.pallas_call(functools.partial(text_kernel, groups, heads, place_of), o...  5.36 us
    pallas_call x1, Pallas kernels, attention(): pl.pallas_call(functools.partial(attention_kernel, n, len(blocks), heads,...  5.04 us
    pallas_call x1, Pallas kernels, project(): pl.pallas_call(functools.partial(project_kernel, groups, parts, place_of)...  4.71 us
  transfers between devices with their start and end apart: 27, of which 13 were waited for; matrix products, arithmetic and copies ran while one was open for 1% of the time, Pallas kernels for 14%

profile of v8, /device:TPU:0, one launch (start us, length us, event | category | flops | bytes accessed | tf_op | source)
XLA Modules:
  0.0 124.6 jit_solution(16574606375371824533)
XLA Ops:
  1.4 0.7 pad_add_fusion.meta_ref
  2.1 5.4 %shard_map.165 = (f32[4,336,128]{2,1,0:T(8,128)}, bf16[4,320,128]{2,1,0:T(8,128)(2,1)}) custom-call(s32[3]{0:T(128)} %pad_add_fusion.meta_ref, s32[1]{0:T(128)} %copy.22.len_ref, s32[1,64]{1,0:T(1,128)} %src_ref.1, bf16[64,512]{1,0:T(8,128)(2,1)} %bitcast.38, f32[1,512]{1,0:T(1,128)} %bitcast.39, f32[1,128]{1,0:T(1,128)} %bitcast.40, f32[1,128]{1,0:T(1,128)} %bitcast.41, ...), custom_call_target="tpu_custom_call" | custom-call | flops 301989888 | bytes 4718592 | tf_op jit(solution)/shard_map/pallas_call | solution.py:108
  7.5 0.5 collective-permute-start.4
  8.0 2.4 %shard_map.164 = (bf16[1152,128]{1,0:T(8,128)(2,1)}, bf16[1152,128]{1,0:T(8,128)(2,1)}, bf16[1152,128]{1,0:T(8,128)(2,1)}, bf16[1152,128]{1,0:T(8,128)(2,1)}) custom-call(s32[3]{0:T(128)} %pad_add_fusion.meta_ref, bf16[128,1536]{1,0:T(8,128)(2,1)} %bitcast.35, bf16[128,1536]{1,0:T(8,128)(2,1)} %bitcast.36, bf16[128,1536]{1,0:T(8,128)(2,1)} %bitcast.37), custom_call_target="tpu_custom_call" | custom-call | bytes 2359296 | tf_op jit(solution)/shard_map/pallas_call | solution.py:138
  10.4 2.6 %collective-permute-start = (bf16[1152,128]{1,0:T(8,128)(2,1)}, bf16[1152,128]{1,0:T(8,128)(2,1)S(1)}, u32[]{:S(2)}, u32[]{:S(2)}) collective-permute-start(bf16[1152,128]{1,0:T(8,128)(2,1)} %get-tuple-element.37), channel_id=1, source_target_pairs={{0,2},{2,0},{4,6},{6,4},{1,3},{3,1},{5,7},{7,5},{8,10},{10,8},{12,... | collective-permute-start | bytes 884744 | tf_op jit(solution)/shard_map/ppermute | solution.py:533
  13.0 2.6 %collective-permute-start.1 = (bf16[1152,128]{1,0:T(8,128)(2,1)}, bf16[1152,128]{1,0:T(8,128)(2,1)S(1)}, u32[]{:S(2)}, u32[]{:S(2)}) collective-permute-start(bf16[1152,128]{1,0:T(8,128)(2,1)} %get-tuple-element.38), channel_id=1, source_target_pairs={{0,4},{2,6},{4,0},{6,2},{1,5},{3,7},{5,1},{7,3},{8,12},{10,14},{12... | collective-permute-start | bytes 884744 | tf_op jit(solution)/shard_map/ppermute | solution.py:533
  15.6 1.1 copy-done.3
  16.9 1.0 collective-permute-start.5
  17.8 19.2 %collective-permute-done.5.refs_0_ = bf16[2,320,128]{2,1,0:T(8,128)(2,1)S(1)} collective-permute-done((bf16[2,320,128]{2,1,0:T(8,128)(2,1)S(1)}, bf16[2,320,128]{2,1,0:T(8,128)(2,1)S(1)}, u32[]{:S(2)}, u32[]{:S(2)}) %collective-permute-start.5) | collective-permute-done | bytes 163872 | tf_op jit(solution)/shard_map/ppermute | solution.py:533
  37.2 2.9 %collective-permute-start.6 = (bf16[1,320,128]{2,1,0:T(8,128)(2,1)S(1)}, bf16[1,320,128]{2,1,0:T(8,128)(2,1)S(1)}, u32[]{:S(2)}, u32[]{:S(2)}) collective-permute-start(bf16[1,320,128]{2,1,0:T(8,128)(2,1)S(1)} %get-tuple-element.45), channel_id=1, source_target_pairs={{0,4},{2,6},{4,0},{6,2},{1,5},{3,7},{5,1},{7,3},{8,12},{10,14},{12... | collective-permute-start | bytes 245768 | tf_op jit(solution)/shard_map/ppermute | solution.py:533
  40.1 2.3 %shard_map.168 = (bf16[2,4,96,128]{3,2,1,0:T(8,128)(2,1)}, bf16[2,4,96,128]{3,2,1,0:T(8,128)(2,1)}, bf16[2,4,96,128]{3,2,1,0:T(8,128)(2,1)}, bf16[2,4,96,128]{3,2,1,0:T(8,128)(2,1)}, s32[1]{0:T(128)}) custom-call(s32[3]{0:T(128)} %pad_add_fusion.meta_ref, f32[1,3072]{1,0:T(1,128)} %gate_ref.5, bf16[128,3072]{1,0:T(8,128)(2,1)} %bitcast.31), custom_call_target="tpu_custom_call" | custom-call | bytes 1572864 | tf_op jit(solution)/shard_map/pallas_call | solution.py:326
  42.5 3.3 %collective-permute-done.6.got_ref = bf16[1,320,128]{2,1,0:T(8,128)(2,1)S(1)} collective-permute-done((bf16[1,320,128]{2,1,0:T(8,128)(2,1)S(1)}, bf16[1,320,128]{2,1,0:T(8,128)(2,1)S(1)}, u32[]{:S(2)}, u32[]{:S(2)}) %collective-permute-start.6) | collective-permute-done | bytes 81952 | tf_op jit(solution)/shard_map/ppermute | solution.py:533
  45.8 0.9 shard_map.169.refs_5_
  46.8 1.6 %collective-permute-start.11 = (bf16[2,4,96,128]{3,2,1,0:T(8,128)(2,1)}, bf16[2,4,96,128]{3,2,1,0:T(8,128)(2,1)S(1)}, u32[]{:S(2)}, u32[]{:S(2)}) collective-permute-start(bf16[2,4,96,128]{3,2,1,0:T(8,128)(2,1)} %get-tuple-element.52), channel_id=1, source_target_pairs={{0,8},{8,0},{16,24},{24,16},{1,9},{9,1},{17,25},{25,17},{2,10},{10... | collective-permute-start | bytes 589832 | tf_op jit(solution)/shard_map/ppermute | solution.py:540
  48.3 1.5 %collective-permute-start.12 = (bf16[2,4,96,128]{3,2,1,0:T(8,128)(2,1)}, bf16[2,4,96,128]{3,2,1,0:T(8,128)(2,1)S(1)}, u32[]{:S(2)}, u32[]{:S(2)}) collective-permute-start(bf16[2,4,96,128]{3,2,1,0:T(8,128)(2,1)} %get-tuple-element.53), channel_id=1, source_target_pairs={{0,16},{8,24},{16,0},{24,8},{1,17},{9,25},{17,1},{25,9},{2,18},{10... | collective-permute-start | bytes 589832 | tf_op jit(solution)/shard_map/ppermute | solution.py:540
  49.9 0.5 collective-permute-start.13
  50.4 1.7 %collective-permute-done.3.refs_4_ = bf16[1152,128]{1,0:T(8,128)(2,1)S(1)} collective-permute-done((bf16[1152,128]{1,0:T(8,128)(2,1)}, bf16[1152,128]{1,0:T(8,128)(2,1)S(1)}, u32[]{:S(2)}, u32[]{:S(2)}) %collective-permute-start.3) | collective-permute-done | bytes 294944 | tf_op jit(solution)/shard_map/ppermute | solution.py:537
  52.1 1.0 copy-done.7
  53.1 5.0 %shard_map.170 = (bf16[128,384]{1,0:T(8,128)(2,1)S(1)}, bf16[128,384]{1,0:T(8,128)(2,1)S(1)}, bf16[128,384]{1,0:T(8,128)(2,1)S(1)}, bf16[128,384]{1,0:T(8,128)(2,1)S(1)}, bf16[32,384]{1,0:T(8,128)(2,1)S(1)}) custom-call(bf16[1152,128]{1,0:T(8,128)(2,1)S(1)} %copy-done.7, bf16[1152,128]{1,0:T(8,128)(2,1)S(1)} %collective-permute-done.refs_0_.refs_1_, ...), custom_call_target="tpu_custom_call" | custom-call | flops 909115392 | bytes 2506752 | tf_op jit(solution)/shard_map/pallas_call | solution.py:275
  58.3 3.1 %collective-permute-start.9 = (bf16[136,384]{1,0:T(8,128)(2,1)S(1)}, bf16[136,384]{1,0:T(8,128)(2,1)S(1)}, u32[]{:S(2)}, u32[]{:S(2)}) collective-permute-start(bf16[136,384]{1,0:T(8,128)(2,1)S(1)} %pad_maximum_fusion.2), channel_id=1, source_target_pairs={{0,4},{2,6},{4,0},{6,2},{1,5},{3,7},{5,1},{7,3},{8,12},{10,14},{12... | collective-permute-start | bytes 313352 | tf_op jit(solution)/shard_map/ppermute | solution.py:533
  61.5 1.4 %collective-permute-start.10 = (bf16[136,384]{1,0:T(8,128)(2,1)S(1)}, bf16[136,384]{1,0:T(8,128)(2,1)S(1)}, u32[]{:S(2)}, u32[]{:S(2)}) collective-permute-start(bf16[136,384]{1,0:T(8,128)(2,1)S(1)} %pad_maximum_fusion.3), channel_id=1, source_target_pairs={{0,6},{2,4},{4,2},{6,0},{1,7},{3,5},{5,3},{7,1},{8,14},{10,12},{12... | collective-permute-start | bytes 313352 | tf_op jit(solution)/shard_map/ppermute | solution.py:533
  62.9 2.0 %collective-permute-done.8.refs_1_ = bf16[136,384]{1,0:T(8,128)(2,1)S(1)} collective-permute-done((bf16[136,384]{1,0:T(8,128)(2,1)S(1)}, bf16[136,384]{1,0:T(8,128)(2,1)S(1)}, u32[]{:S(2)}, u32[]{:S(2)}) %collective-permute-start.8) | collective-permute-done | bytes 104480 | tf_op jit(solution)/shard_map/ppermute | solution.py:533
  64.9 4.7 %collective-permute-done.9.refs_2_ = bf16[136,384]{1,0:T(8,128)(2,1)S(1)} collective-permute-done((bf16[136,384]{1,0:T(8,128)(2,1)S(1)}, bf16[136,384]{1,0:T(8,128)(2,1)S(1)}, u32[]{:S(2)}, u32[]{:S(2)}) %collective-permute-start.9) | collective-permute-done | bytes 104480 | tf_op jit(solution)/shard_map/ppermute | solution.py:533
  69.7 0.6 shard_map.171.attn_ref.refs_5_
  70.2 2.5 %collective-permute-start.17 = (bf16[128,1536]{1,0:T(8,128)(2,1)S(1)}, bf16[128,1536]{1,0:T(8,128)(2,1)}, u32[]{:S(2)}, u32[]{:S(2)}) collective-permute-start(bf16[128,1536]{1,0:T(8,128)(2,1)S(1)} %shard_map.171.attn_ref.refs_5_), channel_id=1, source_target_pairs={{0,24},{8,16},{16,8},{24,0},{1,25},{9,17},{17,9},{25,1},{2,26},{10... | collective-permute-start | bytes 1179656 | tf_op jit(solution)/shard_map/ppermute | solution.py:540
  72.8 0.5 collective-permute-start.16
  73.3 0.5 collective-permute-start.15
  73.8 3.7 %copy-done = bf16[3072,1536]{1,0:T(8,128)(2,1)S(1)} copy-done((bf16[3072,1536]{1,0:T(8,128)(2,1)S(1)}, bf16[3072,1536]{1,0:T(8,128)(2,1)}, u32[]{:S(2)}) %copy-start) | copy-done | bytes 9437208
  77.5 4.7 %shard_map.172 = (bf16[128,3072]{1,0:T(8,128)(2,1)}, f32[4,384]{1,0:T(4,128)S(1)}, bf16[144,1536]{1,0:T(8,128)(2,1)}) custom-call(s32[3]{0:T(128)S(1)} %copy-done.6, bf16[128,1536]{1,0:T(8,128)(2,1)S(1)} %shard_map.171.attn_ref.refs_5_, bf16[3072,1536]{1,0:T(8,128)(2,1)S(1)} %copy-done, f32[1,3072]{1,0:T(1,128)S(1)} %copy-done.5, bf16[128,3072]{1,0:T(8,128)(2,1)S(1)} %bitcast.32), custom_call_target="tpu_custom_call" | custom-call | flops 1207959552 | bytes 9437184 | tf_op jit(solution)/shard_map/pallas_call | solution.py:425
  82.2 0.6 collective-permute-start.14
  82.8 0.6 collective-permute-done.17.refs_8_
  83.4 5.5 %collective-permute-done.16.refs_7_ = bf16[128,1536]{1,0:T(8,128)(2,1)} collective-permute-done((bf16[128,1536]{1,0:T(8,128)(2,1)S(1)}, bf16[128,1536]{1,0:T(8,128)(2,1)}, u32[]{:S(2)}, u32[]{:S(2)}) %collective-permute-start.16) | collective-permute-done | bytes 393248 | tf_op jit(solution)/shard_map/ppermute | solution.py:540
  89.1 0.4 collective-permute-start.19
  89.6 1.5 %collective-permute-done.20.refs_11_ = bf16[128,1536]{1,0:T(8,128)(2,1)} collective-permute-done((bf16[128,1536]{1,0:T(8,128)(2,1)}, bf16[128,1536]{1,0:T(8,128)(2,1)}, u32[]{:S(2)}, u32[]{:S(2)}) %collective-permute-start.20) | collective-permute-done | bytes 393248 | tf_op jit(solution)/shard_map/ppermute | solution.py:537
  91.0 0.6 collective-permute-done.19.refs_10_
  91.6 3.2 %shard_map.174 = (f32[96,1536]{1,0:T(8,128)S(1)}, bf16[96,1536]{1,0:T(8,128)(2,1)S(1)}, f32[96,1536]{1,0:T(8,128)S(1)}, bf16[96,1536]{1,0:T(8,128)(2,1)S(1)}, f3...) custom-call(bf16[1,4,96,128]{3,2,1,0:T(8,128)(2,1)S(1)} %slice.30.refs_0_, bf16[1,4,96,128]{3,2,1,0:T(8,128)(2,1)S(1)} %slice.39.refs_1_, ...), custom_call_target="tpu_custom_call" | custom-call | flops 1207959552 | bytes 5111808 | tf_op jit(solution)/shard_map/pallas_call | solution.py:472
  94.8 3.2 %collective-permute-start.22 = (bf16[96,1536]{1,0:T(8,128)(2,1)S(1)}, bf16[96,1536]{1,0:T(8,128)(2,1)S(1)}, u32[]{:S(2)}, u32[]{:S(2)}) collective-permute-start(bf16[96,1536]{1,0:T(8,128)(2,1)S(1)} %get-tuple-element.62), channel_id=1, source_target_pairs={{0,2},{2,0},{4,6},{6,4},{1,3},{3,1},{5,7},{7,5},{8,10},{10,8},{12,... | collective-permute-start | bytes 884744 | tf_op jit(solution)/shard_map/ppermute | solution.py:533
  98.1 7.2 %collective-permute-done.22.got_ref = bf16[96,1536]{1,0:T(8,128)(2,1)S(1)} collective-permute-done((bf16[96,1536]{1,0:T(8,128)(2,1)S(1)}, bf16[96,1536]{1,0:T(8,128)(2,1)S(1)}, u32[]{:S(2)}, u32[]{:S(2)}) %collective-permute-start.22) | collective-permute-done | bytes 294944 | tf_op jit(solution)/shard_map/ppermute | solution.py:533
  105.4 2.7 %collective-permute-start.25 = (f32[2,384]{1,0:T(2,128)S(1)}, f32[2,384]{1,0:T(2,128)S(1)}, u32[]{:S(2)}, u32[]{:S(2)}) collective-permute-start(f32[2,384]{1,0:T(2,128)S(1)} %get-tuple-element.66), channel_id=1, source_target_pairs={{0,4},{2,6},{4,0},{6,2},{1,5},{3,7},{5,1},{7,3},{8,12},{10,14},{12... | collective-permute-start | bytes 9224 | tf_op jit(solution)/shard_map/ppermute | solution.py:533
  108.2 0.3 collective-permute-start.24
  108.4 1.7 %collective-permute-start.23 = (bf16[96,1536]{1,0:T(8,128)(2,1)S(1)}, bf16[96,1536]{1,0:T(8,128)(2,1)S(1)}, u32[]{:S(2)}, u32[]{:S(2)}) collective-permute-start(bf16[96,1536]{1,0:T(8,128)(2,1)S(1)} %get-tuple-element.64), channel_id=1, source_target_pairs={{0,4},{2,6},{4,0},{6,2},{1,5},{3,7},{5,1},{7,3},{8,12},{10,14},{12... | collective-permute-start | bytes 884744 | tf_op jit(solution)/shard_map/ppermute | solution.py:533
  110.2 1.6 %collective-permute-start.26 = (f32[1,384]{1,0:T(1,128)S(1)}, f32[1,384]{1,0:T(1,128)S(1)}, u32[]{:S(2)}, u32[]{:S(2)}) collective-permute-start(f32[1,384]{1,0:T(1,128)S(1)} %slice.43), channel_id=1, source_target_pairs={{0,2},{2,0},{4,6},{6,4},{1,3},{3,1},{5,7},{7,5},{8,10},{10,8},{12,... | collective-permute-start | bytes 4616 | tf_op jit(solution)/shard_map/ppermute | solution.py:533
  111.8 3.7 %copy-done.1 = bf16[3072,1536]{1,0:T(8,128)(2,1)S(1)} copy-done((bf16[3072,1536]{1,0:T(8,128)(2,1)S(1)}, bf16[3072,1536]{1,0:T(8,128)(2,1)}, u32[]{:S(2)}) %copy-start.1) | copy-done | bytes 9437208
  115.5 2.2 %shard_map.175 = bf16[128,1536]{1,0:T(8,128)(2,1)} custom-call(f32[1,3072]{1,0:T(1,128)S(1)} %copy-done.5, bf16[128,3072]{1,0:T(8,128)(2,1)S(1)} %bitcast.33, bf16[3072,1536]{1,0:T(8,128)(2,1)S(1)} %copy-done.1, bf16[96,1536]{1,0:T(8,128)(2,1)S(1)} %get-tuple-element.59.after_ref), custom_call_target="tpu_custom_call" | custom-call | flops 1207959552 | bytes 9437184 | tf_op jit(solution)/shard_map/pallas_call | solution.py:352
  117.6 3.8 %collective-permute-done.26 = f32[1,384]{1,0:T(1,128)S(1)} collective-permute-done((f32[1,384]{1,0:T(1,128)S(1)}, f32[1,384]{1,0:T(1,128)S(1)}, u32[]{:S(2)}, u32[]{:S(2)}) %collective-permute-start.26) | collective-permute-done | bytes 1568 | tf_op jit(solution)/shard_map/ppermute | solution.py:533
  121.4 0.6 slice_add_fusion
  122.0 1.7 %collective-permute-done.23 = bf16[96,1536]{1,0:T(8,128)(2,1)S(1)} collective-permute-done((bf16[96,1536]{1,0:T(8,128)(2,1)S(1)}, bf16[96,1536]{1,0:T(8,128)(2,1)S(1)}, u32[]{:S(2)}, u32[]{:S(2)}) %collective-permute-start.23) | collective-permute-done | bytes 294944 | tf_op jit(solution)/shard_map/ppermute | solution.py:533
  123.7 0.9 convert_add_fusion
  (60 shorter events, 1.2 us)
Async XLA Ops:
  0.6 49.7 %copy-start.9 = (s32[1,64]{1,0:T(1,128)S(1)}, s32[1,64]{1,0:T(1,128)}, u32[]{:S(2)}) copy-start(s32[1,64]{1,0:T(1,128)} %src_ref.1) | copy-start | bytes 772
  0.6 73.2 %copy-start.5 = (f32[1,3072]{1,0:T(1,128)S(1)}, f32[1,3072]{1,0:T(1,128)}, u32[]{:S(2)}) copy-start(f32[1,3072]{1,0:T(1,128)} %gate_ref.5) | copy-start | bytes 36868
  0.7 73.2 %copy-start.2 = (bf16[1,128,3072]{2,1,0:T(8,128)(2,1)S(1)}, bf16[1,128,3072]{2,1,0:T(8,128)(2,1)}, u32[]{:S(2)}) copy-start(bf16[1,128,3072]{2,1,0:T(8,128)(2,1)} %param.25) | copy-start | bytes 2359300
  2.1 67.6 %copy-start.6 = (s32[3]{0:T(128)S(1)}, s32[3]{0:T(128)}, u32[]{:S(2)}) copy-start(s32[3]{0:T(128)} %pad_add_fusion.meta_ref) | copy-start | bytes 40
  7.5 8.1 %collective-permute-start.4 = (bf16[4,320,128]{2,1,0:T(8,128)(2,1)}, bf16[4,320,128]{2,1,0:T(8,128)(2,1)S(1)}, u32[]{:S(2)}, u32[]{:S(2)}) collective-permute-start(bf16[4,320,128]{2,1,0:T(8,128)(2,1)} %get-tuple-element.41), channel_id=1, source_target_pairs={{0,1},{2,3},{4,5},{6,7},{1,0},{3,2},{5,4},{7,6},{8,9},{10,11},{12,... | collective-permute-start | bytes 983048 | tf_op jit(solution)/shard_map/ppermute | solution.py:537
  10.4 32.0 %collective-permute-start = (bf16[1152,128]{1,0:T(8,128)(2,1)}, bf16[1152,128]{1,0:T(8,128)(2,1)S(1)}, u32[]{:S(2)}, u32[]{:S(2)}) collective-permute-start(bf16[1152,128]{1,0:T(8,128)(2,1)} %get-tuple-element.37), channel_id=1, source_target_pairs={{0,2},{2,0},{4,6},{6,4},{1,3},{3,1},{5,7},{7,5},{8,10},{10,8},{12,... | collective-permute-start | bytes 884744 | tf_op jit(solution)/shard_map/ppermute | solution.py:533
  13.0 29.5 %collective-permute-start.1 = (bf16[1152,128]{1,0:T(8,128)(2,1)}, bf16[1152,128]{1,0:T(8,128)(2,1)S(1)}, u32[]{:S(2)}, u32[]{:S(2)}) collective-permute-start(bf16[1152,128]{1,0:T(8,128)(2,1)} %get-tuple-element.38), channel_id=1, source_target_pairs={{0,4},{2,6},{4,0},{6,2},{1,5},{3,7},{5,1},{7,3},{8,12},{10,14},{12... | collective-permute-start | bytes 884744 | tf_op jit(solution)/shard_map/ppermute | solution.py:533
  15.6 26.9 %collective-permute-start.2 = (bf16[1152,128]{1,0:T(8,128)(2,1)}, bf16[1152,128]{1,0:T(8,128)(2,1)S(1)}, u32[]{:S(2)}, u32[]{:S(2)}) collective-permute-start(bf16[1152,128]{1,0:T(8,128)(2,1)} %get-tuple-element.39), channel_id=1, source_target_pairs={{0,6},{2,4},{4,2},{6,0},{1,7},{3,5},{5,3},{7,1},{8,14},{10,12},{12... | collective-permute-start | bytes 884744 | tf_op jit(solution)/shard_map/ppermute | solution.py:533
  15.6 1.1 copy-start.3
  16.9 20.2 %collective-permute-start.5 = (bf16[2,320,128]{2,1,0:T(8,128)(2,1)S(1)}, bf16[2,320,128]{2,1,0:T(8,128)(2,1)S(1)}, u32[]{:S(2)}, u32[]{:S(2)}) collective-permute-start(bf16[2,320,128]{2,1,0:T(8,128)(2,1)S(1)} %get-tuple-element.43), channel_id=1, source_target_pairs={{0,2},{2,0},{4,6},{6,4},{1,3},{3,1},{5,7},{7,5},{8,10},{10,8},{12,... | collective-permute-start | bytes 491528 | tf_op jit(solution)/shard_map/ppermute | solution.py:533
  37.2 8.6 %collective-permute-start.6 = (bf16[1,320,128]{2,1,0:T(8,128)(2,1)S(1)}, bf16[1,320,128]{2,1,0:T(8,128)(2,1)S(1)}, u32[]{:S(2)}, u32[]{:S(2)}) collective-permute-start(bf16[1,320,128]{2,1,0:T(8,128)(2,1)S(1)} %get-tuple-element.45), channel_id=1, source_target_pairs={{0,4},{2,6},{4,0},{6,2},{1,5},{3,7},{5,1},{7,3},{8,12},{10,14},{12... | collective-permute-start | bytes 245768 | tf_op jit(solution)/shard_map/ppermute | solution.py:533
  42.4 39.8 %copy-start.4 = (bf16[2,4,96,128]{3,2,1,0:T(8,128)(2,1)S(1)}, bf16[2,4,96,128]{3,2,1,0:T(8,128)(2,1)}, u32[]{:S(2)}) copy-start(bf16[2,4,96,128]{3,2,1,0:T(8,128)(2,1)} %get-tuple-element.56.refs_0_) | copy-start | bytes 589828
  46.7 5.4 %collective-permute-start.7 = (bf16[2608,128]{1,0:T(8,128)(2,1)S(1)}, bf16[2608,128]{1,0:T(8,128)(2,1)}, u32[]{:S(2)}, u32[]{:S(2)}) collective-permute-start(bf16[2608,128]{1,0:T(8,128)(2,1)S(1)} %shard_map.169.refs_5_), channel_id=1, source_target_pairs={{0,1},{2,3},{4,5},{6,7},{1,0},{3,2},{5,4},{7,6},{8,9},{10,11},{12,... | collective-permute-start | bytes 2002952 | tf_op jit(solution)/shard_map/ppermute | solution.py:537
  46.8 14.7 %collective-permute-start.11 = (bf16[2,4,96,128]{3,2,1,0:T(8,128)(2,1)}, bf16[2,4,96,128]{3,2,1,0:T(8,128)(2,1)S(1)}, u32[]{:S(2)}, u32[]{:S(2)}) collective-permute-start(bf16[2,4,96,128]{3,2,1,0:T(8,128)(2,1)} %get-tuple-element.52), channel_id=1, source_target_pairs={{0,8},{8,0},{16,24},{24,16},{1,9},{9,1},{17,25},{25,17},{2,10},{10... | collective-permute-start | bytes 589832 | tf_op jit(solution)/shard_map/ppermute | solution.py:540
  48.3 14.6 %collective-permute-start.12 = (bf16[2,4,96,128]{3,2,1,0:T(8,128)(2,1)}, bf16[2,4,96,128]{3,2,1,0:T(8,128)(2,1)S(1)}, u32[]{:S(2)}, u32[]{:S(2)}) collective-permute-start(bf16[2,4,96,128]{3,2,1,0:T(8,128)(2,1)} %get-tuple-element.53), channel_id=1, source_target_pairs={{0,16},{8,24},{16,0},{24,8},{1,17},{9,25},{17,1},{25,9},{2,18},{10... | collective-permute-start | bytes 589832 | tf_op jit(solution)/shard_map/ppermute | solution.py:540
  49.9 13.1 %collective-permute-start.13 = (bf16[2,4,96,128]{3,2,1,0:T(8,128)(2,1)}, bf16[2,4,96,128]{3,2,1,0:T(8,128)(2,1)S(1)}, u32[]{:S(2)}, u32[]{:S(2)}) collective-permute-start(bf16[2,4,96,128]{3,2,1,0:T(8,128)(2,1)} %get-tuple-element.54), channel_id=1, source_target_pairs={{0,24},{8,16},{16,8},{24,0},{1,25},{9,17},{17,9},{25,1},{2,26},{10... | collective-permute-start | bytes 589832 | tf_op jit(solution)/shard_map/ppermute | solution.py:540
  50.3 1.8 %collective-permute-start.3 = (bf16[1152,128]{1,0:T(8,128)(2,1)}, bf16[1152,128]{1,0:T(8,128)(2,1)S(1)}, u32[]{:S(2)}, u32[]{:S(2)}) collective-permute-start(bf16[1152,128]{1,0:T(8,128)(2,1)} %get-tuple-element.36.refs_0_), channel_id=1, source_target_pairs={{0,1},{2,3},{4,5},{6,7},{1,0},{3,2},{5,4},{7,6},{8,9},{10,11},{12,... | collective-permute-start | bytes 884744 | tf_op jit(solution)/shard_map/ppermute | solution.py:537
  52.1 1.0 copy-start.7
  58.2 6.7 %collective-permute-start.8 = (bf16[136,384]{1,0:T(8,128)(2,1)S(1)}, bf16[136,384]{1,0:T(8,128)(2,1)S(1)}, u32[]{:S(2)}, u32[]{:S(2)}) collective-permute-start(bf16[136,384]{1,0:T(8,128)(2,1)S(1)} %pad_maximum_fusion.1), channel_id=1, source_target_pairs={{0,2},{2,0},{4,6},{6,4},{1,3},{3,1},{5,7},{7,5},{8,10},{10,8},{12,... | collective-permute-start | bytes 313352 | tf_op jit(solution)/shard_map/ppermute | solution.py:533
  58.3 11.4 %collective-permute-start.9 = (bf16[136,384]{1,0:T(8,128)(2,1)S(1)}, bf16[136,384]{1,0:T(8,128)(2,1)S(1)}, u32[]{:S(2)}, u32[]{:S(2)}) collective-permute-start(bf16[136,384]{1,0:T(8,128)(2,1)S(1)} %pad_maximum_fusion.2), channel_id=1, source_target_pairs={{0,4},{2,6},{4,0},{6,2},{1,5},{3,7},{5,1},{7,3},{8,12},{10,14},{12... | collective-permute-start | bytes 313352 | tf_op jit(solution)/shard_map/ppermute | solution.py:533
  61.5 8.2 %collective-permute-start.10 = (bf16[136,384]{1,0:T(8,128)(2,1)S(1)}, bf16[136,384]{1,0:T(8,128)(2,1)S(1)}, u32[]{:S(2)}, u32[]{:S(2)}) collective-permute-start(bf16[136,384]{1,0:T(8,128)(2,1)S(1)} %pad_maximum_fusion.3), channel_id=1, source_target_pairs={{0,6},{2,4},{4,2},{6,0},{1,7},{3,5},{5,3},{7,1},{8,14},{10,12},{12... | collective-permute-start | bytes 313352 | tf_op jit(solution)/shard_map/ppermute | solution.py:533
  70.2 13.2 %collective-permute-start.17 = (bf16[128,1536]{1,0:T(8,128)(2,1)S(1)}, bf16[128,1536]{1,0:T(8,128)(2,1)}, u32[]{:S(2)}, u32[]{:S(2)}) collective-permute-start(bf16[128,1536]{1,0:T(8,128)(2,1)S(1)} %shard_map.171.attn_ref.refs_5_), channel_id=1, source_target_pairs={{0,24},{8,16},{16,8},{24,0},{1,25},{9,17},{17,9},{25,1},{2,26},{10... | collective-permute-start | bytes 1179656 | tf_op jit(solution)/shard_map/ppermute | solution.py:540
  72.8 16.2 %collective-permute-start.16 = (bf16[128,1536]{1,0:T(8,128)(2,1)S(1)}, bf16[128,1536]{1,0:T(8,128)(2,1)}, u32[]{:S(2)}, u32[]{:S(2)}) collective-permute-start(bf16[128,1536]{1,0:T(8,128)(2,1)S(1)} %shard_map.171.attn_ref.refs_5_), channel_id=1, source_target_pairs={{0,16},{8,24},{16,0},{24,8},{1,17},{9,25},{17,1},{25,9},{2,18},{10... | collective-permute-start | bytes 1179656 | tf_op jit(solution)/shard_map/ppermute | solution.py:540
  73.3 15.8 %collective-permute-start.15 = (bf16[128,1536]{1,0:T(8,128)(2,1)S(1)}, bf16[128,1536]{1,0:T(8,128)(2,1)}, u32[]{:S(2)}, u32[]{:S(2)}) collective-permute-start(bf16[128,1536]{1,0:T(8,128)(2,1)S(1)} %shard_map.171.attn_ref.refs_5_), channel_id=1, source_target_pairs={{0,8},{8,0},{16,24},{24,16},{1,9},{9,1},{17,25},{25,17},{2,10},{10... | collective-permute-start | bytes 1179656 | tf_op jit(solution)/shard_map/ppermute | solution.py:540
  73.8 3.7 %copy-start = (bf16[3072,1536]{1,0:T(8,128)(2,1)S(1)}, bf16[3072,1536]{1,0:T(8,128)(2,1)}, u32[]{:S(2)}) copy-start(bf16[3072,1536]{1,0:T(8,128)(2,1)} %w_ref.5) | copy-start | bytes 28311556
  82.2 7.3 %collective-permute-start.18 = (bf16[144,1536]{1,0:T(8,128)(2,1)}, bf16[144,1536]{1,0:T(8,128)(2,1)}, u32[]{:S(2)}, u32[]{:S(2)}) collective-permute-start(bf16[144,1536]{1,0:T(8,128)(2,1)} %get-tuple-element.57), channel_id=1, source_target_pairs={{0,1},{2,3},{4,5},{6,7},{1,0},{3,2},{5,4},{7,6},{8,9},{10,11},{12,... | collective-permute-start | bytes 1327112 | tf_op jit(solution)/shard_map/ppermute | solution.py:537
  82.2 7.3 %collective-permute-start.14 = (bf16[4,4,96,128]{3,2,1,0:T(8,128)(2,1)S(1)}, bf16[4,4,96,128]{3,2,1,0:T(8,128)(2,1)}, u32[]{:S(2)}, u32[]{:S(2)}) collective-permute-start(bf16[4,4,96,128]{3,2,1,0:T(8,128)(2,1)S(1)} %shard_map.173), channel_id=1, source_target_pairs={{0,1},{2,3},{4,5},{6,7},{1,0},{3,2},{5,4},{7,6},{8,9},{10,11},{12,... | collective-permute-start | bytes 1179656 | tf_op jit(solution)/shard_map/ppermute | solution.py:537
  83.4 6.1 %collective-permute-start.21 = (bf16[128,1536]{1,0:T(8,128)(2,1)}, bf16[128,1536]{1,0:T(8,128)(2,1)}, u32[]{:S(2)}, u32[]{:S(2)}) collective-permute-start(bf16[128,1536]{1,0:T(8,128)(2,1)} %collective-permute-done.17.refs_8_), channel_id=1, source_target_pairs={{0,1},{2,3},{4,5},{6,7},{1,0},{3,2},{5,4},{7,6},{8,9},{10,11},{12,... | collective-permute-start | bytes 1179656 | tf_op jit(solution)/shard_map/ppermute | solution.py:537
  89.0 2.1 %collective-permute-start.20 = (bf16[128,1536]{1,0:T(8,128)(2,1)}, bf16[128,1536]{1,0:T(8,128)(2,1)}, u32[]{:S(2)}, u32[]{:S(2)}) collective-permute-start(bf16[128,1536]{1,0:T(8,128)(2,1)} %collective-permute-done.16.refs_7_), channel_id=1, source_target_pairs={{0,1},{2,3},{4,5},{6,7},{1,0},{3,2},{5,4},{7,6},{8,9},{10,11},{12,... | collective-permute-start | bytes 1179656 | tf_op jit(solution)/shard_map/ppermute | solution.py:537
  89.1 2.5 %collective-permute-start.19 = (bf16[128,1536]{1,0:T(8,128)(2,1)}, bf16[128,1536]{1,0:T(8,128)(2,1)}, u32[]{:S(2)}, u32[]{:S(2)}) collective-permute-start(bf16[128,1536]{1,0:T(8,128)(2,1)} %collective-permute-done.15.refs_6_), channel_id=1, source_target_pairs={{0,1},{2,3},{4,5},{6,7},{1,0},{3,2},{5,4},{7,6},{8,9},{10,11},{12,... | collective-permute-start | bytes 1179656 | tf_op jit(solution)/shard_map/ppermute | solution.py:537
  94.8 10.5 %collective-permute-start.22 = (bf16[96,1536]{1,0:T(8,128)(2,1)S(1)}, bf16[96,1536]{1,0:T(8,128)(2,1)S(1)}, u32[]{:S(2)}, u32[]{:S(2)}) collective-permute-start(bf16[96,1536]{1,0:T(8,128)(2,1)S(1)} %get-tuple-element.62), channel_id=1, source_target_pairs={{0,2},{2,0},{4,6},{6,4},{1,3},{3,1},{5,7},{7,5},{8,10},{10,8},{12,... | collective-permute-start | bytes 884744 | tf_op jit(solution)/shard_map/ppermute | solution.py:533
  105.4 4.8 %collective-permute-start.25 = (f32[2,384]{1,0:T(2,128)S(1)}, f32[2,384]{1,0:T(2,128)S(1)}, u32[]{:S(2)}, u32[]{:S(2)}) collective-permute-start(f32[2,384]{1,0:T(2,128)S(1)} %get-tuple-element.66), channel_id=1, source_target_pairs={{0,4},{2,6},{4,0},{6,2},{1,5},{3,7},{5,1},{7,3},{8,12},{10,14},{12... | collective-permute-start | bytes 9224 | tf_op jit(solution)/shard_map/ppermute | solution.py:533
  108.2 16.4 %copy-start.8 = (bf16[1,8,1536]{2,1,0:T(8,128)(2,1)}, bf16[1,8,1536]{2,1,0:T(8,128)(2,1)S(1)}, u32[]{:S(2)}) copy-start(bf16[1,8,1536]{2,1,0:T(8,128)(2,1)S(1)} %fusion.1) | copy-start | bytes 73732
  108.2 13.8 %collective-permute-start.24 = (bf16[96,1536]{1,0:T(8,128)(2,1)S(1)}, bf16[96,1536]{1,0:T(8,128)(2,1)S(1)}, u32[]{:S(2)}, u32[]{:S(2)}) collective-permute-start(bf16[96,1536]{1,0:T(8,128)(2,1)S(1)} %get-tuple-element.59.after_ref), channel_id=1, source_target_pairs={{0,2},{2,0},{4,6},{6,4},{1,3},{3,1},{5,7},{7,5},{8,10},{10,8},{12,... | collective-permute-start | bytes 884744 | tf_op jit(solution)/shard_map/ppermute | solution.py:533
  108.4 15.2 %collective-permute-start.23 = (bf16[96,1536]{1,0:T(8,128)(2,1)S(1)}, bf16[96,1536]{1,0:T(8,128)(2,1)S(1)}, u32[]{:S(2)}, u32[]{:S(2)}) collective-permute-start(bf16[96,1536]{1,0:T(8,128)(2,1)S(1)} %get-tuple-element.64), channel_id=1, source_target_pairs={{0,4},{2,6},{4,0},{6,2},{1,5},{3,7},{5,1},{7,3},{8,12},{10,14},{12... | collective-permute-start | bytes 884744 | tf_op jit(solution)/shard_map/ppermute | solution.py:533
  110.2 11.2 %collective-permute-start.26 = (f32[1,384]{1,0:T(1,128)S(1)}, f32[1,384]{1,0:T(1,128)S(1)}, u32[]{:S(2)}, u32[]{:S(2)}) collective-permute-start(f32[1,384]{1,0:T(1,128)S(1)} %slice.43), channel_id=1, source_target_pairs={{0,2},{2,0},{4,6},{6,4},{1,3},{3,1},{5,7},{7,5},{8,10},{10,8},{12,... | collective-permute-start | bytes 4616 | tf_op jit(solution)/shard_map/ppermute | solution.py:533
  111.8 3.7 %copy-start.1 = (bf16[3072,1536]{1,0:T(8,128)(2,1)S(1)}, bf16[3072,1536]{1,0:T(8,128)(2,1)}, u32[]{:S(2)}) copy-start(bf16[3072,1536]{1,0:T(8,128)(2,1)} %w_ref.5) | copy-start | bytes 28311556

commit v9 on v8

--- a/solution.py
+++ b/solution.py
@@ -45,8 +45,9 @@
 
 def text_kernel(
     groups, heads, place_of, meta_ref, len_ref, src_ref, states_ref, gain_ref, qg_ref, kg_ref,
-    w_ref, own_ref, *refs
+    k_ref, v_ref, q_ref, w_ref, own_ref, *refs
 ):
+    packed, refs = refs[:groups], refs[groups:]
     msgs, (w_all, w_sems) = refs[:-2], refs[-2:]
     size = own_ref.shape[2]
     rows = (own_ref.shape[1] - EXTRA) // (3 * heads + 1)
@@ -54,12 +55,19 @@
     slots = states_ref.shape[0]
     slot_local = rows // groups
     copies = []
-    for g in range(groups):
-        for i in range(3):
-            at = (i * groups + (meta_ref[0] ^ g)) * width
-            cols = pl.ds(pl.multiple_of(at, 128), width)
-            copies.append(pltpu.make_async_copy(w_ref.at[:, cols], w_all.at[g, i], w_sems.at[g, i]))
-            copies[-1].start()
+    block = w_all.shape[0] // w_sems.shape[0]
+    for i in range(w_sems.shape[0]):
+        part = pl.ds(i * block, block)
+        copies.append(pltpu.make_async_copy(w_ref.at[part], w_all.at[part], w_sems.at[i]))
+        copies[-1].start()
+    local = k_ref.shape[0]
+    for g, out in enumerate(packed):
+        for i, ref in enumerate((k_ref, v_ref, q_ref)):
+            for head in range(heads):
+                at = ((meta_ref[0] ^ g) * heads + head) * size
+                to = (i * heads + head) * local
+                out[to : to + local, :] = ref[:, pl.ds(pl.multiple_of(at, 128), size)]
+
     def slot_at(row):
         z_at = (row % rows) // slot_local
         return place_of(meta_ref[1] ^ (row // rows), z_at) * slot_local + row % slot_local
@@ -81,10 +89,13 @@
     picked = jnp.dot(pick, states_ref[...], preferred_element_type=f32)
     scaled = (picked * gain_ref[...]).astype(bf16)
     tail = split_tail(jnp.sum(picked * picked, axis=1, keepdims=True), size)
+    for copy in copies:
+        copy.wait()
     for g in range(groups):
         for i in range(3):
-            copies[3 * g + i].wait()
-            got = jnp.dot(scaled, w_all[g, i], preferred_element_type=f32)
+            at = (i * groups + (meta_ref[0] ^ g)) * width
+            columns = pl.ds(pl.multiple_of(at, 128), width)
+            got = jnp.dot(scaled, w_all[:, columns], preferred_element_type=f32)
             for head in range(heads):
                 part = got[:, head * size : (head + 1) * size]
                 to = slice((i * heads + head) * rows, (i * heads + head + 1) * rows)
@@ -97,52 +108,29 @@
 
 
 def text_project(
-    meta, length, sources, states, gain, query_gain, key_gain, text_proj, groups, parts, place_of
+    meta, length, sources, states, gain, query_gain, key_gain, keys, values, queries, text_proj,
+    groups, parts, place_of
 ):
     slots, depth = states.shape
     size = query_gain.shape[1]
     heads = text_proj.shape[1] // (3 * groups * size)
     text_rows = (3 * heads + 1) * slots // parts
     shapes = [jax.ShapeDtypeStruct((groups, text_rows + EXTRA, size), f32)]
+    shapes += [jax.ShapeDtypeStruct((3 * heads * keys.shape[0], size), bf16)] * groups
     shapes += [jax.ShapeDtypeStruct((groups, text_rows, size), bf16)] * (parts - 1)
     return pl.pallas_call(
         functools.partial(text_kernel, groups, heads, place_of),
         out_shape=shapes,
-        in_specs=[SMEM, SMEM] + [VMEM] * 5 + [ANY],
-        out_specs=[VMEM] * parts,
-        scratch_shapes=[
-            pltpu.VMEM((groups, 3, depth, heads * size), bf16),
-            pltpu.SemaphoreType.DMA((groups, 3)),
-        ],
+        in_specs=[SMEM, SMEM] + [VMEM] * 8 + [ANY],
+        out_specs=[VMEM] * (groups + parts),
+        scratch_shapes=[pltpu.VMEM(text_proj.shape, bf16), pltpu.SemaphoreType.DMA((4,))],
         compiler_params=params(60),
         cost_estimate=cost(
             2 * slots * depth * text_proj.shape[1], 2 * depth * text_proj.shape[1]
         ),
-    )(meta, length, sources, states, gain, query_gain, key_gain, text_proj)
-
-
-def pack_kernel(groups, size, meta_ref, k_ref, v_ref, q_ref, *outs):
-    rows = k_ref.shape[0]
-    heads = k_ref.shape[1] // (groups * size)
-    for g, out in enumerate(outs):
-        for i, ref in enumerate((k_ref, v_ref, q_ref)):
-            for head in range(heads):
-                at = ((meta_ref[0] ^ g) * heads + head) * size
-                to = (i * heads + head) * rows
-                out[to : to + rows, :] = ref[:, pl.ds(pl.multiple_of(at, 128), size)]
-
-
-def pack(meta, keys, values, queries, groups, size):
-    rows, width = keys.shape
-    shape = jax.ShapeDtypeStruct((3 * rows * width // (groups * size), size), bf16)
-    return pl.pallas_call(
-        functools.partial(pack_kernel, groups, size),
-        out_shape=[shape] * groups,
-        in_specs=[SMEM] + [VMEM] * 3,
-        out_specs=[VMEM] * groups,
-        compiler_params=params(60),
-        cost_estimate=cost(0, 12 * rows * width),
-    )(meta, keys, values, queries)
+    )(
+        meta, length, sources, states, gain, query_gain, key_gain, keys, values, queries, text_proj
+    )
 
 
 def text_sum_kernel(n_got, tail_rows, own_ref, *refs):
@@ -178,8 +166,8 @@
     )(own, *got)
 
 
-def block_kernel(features, heads, n_far, own_ref, got_ref, mark_ref, *refs):
-    del mark_ref
+def block_kernel(features, heads, n_far, own_ref, got_ref, after_ref, *refs):
+    del after_ref
     far, out_ref = refs[:n_far], refs[n_far]
     kv_rows = far[0].shape[0] // 3 * 2
     for k, ref in enumerate(far):
@@ -204,18 +192,18 @@
     out_ref[start:, :] = jnp.broadcast_to(bias, (EXTRA, size)).astype(bf16)
 
 
-def block_of(own, got, mark, far, features, heads):
+def block_of(own, got, after, far, features, heads):
     rows, size = own.shape[1:]
     total = (rows - EXTRA) // (3 * heads + 1) * 3 * heads + EXTRA
     total += far[0].shape[0] // 3 * 2 * len(far)
     return pl.pallas_call(
         functools.partial(block_kernel, features, heads, len(far)),
         out_shape=jax.ShapeDtypeStruct((total, size), bf16),
-        in_specs=[VMEM] * 2 + [SMEM] + [VMEM] * len(far),
+        in_specs=[VMEM] * 2 + [ANY] + [VMEM] * len(far),
         out_specs=VMEM,
         compiler_params=params(),
         cost_estimate=cost(0, 4 * total * size),
-    )(own, got, mark, *far)
+    )(own, got, after, *far)
 
 
 def attention_kernel(n_pieces, n_cores, heads, rows, text_rows, *refs):
@@ -307,8 +295,7 @@
 
 
 def gated_kernel(groups, parts, place_of, meta_ref, gate_ref, d_out_ref, *refs):
-    msgs, mark_ref, turned = refs[:-2], refs[-2], refs[-1]
-    mark_ref[0] = meta_ref[0]
+    msgs, turned = refs[:-1], refs[-1]
     gated = (gate_ref[...] * d_out_ref[...].astype(f32)).astype(bf16)
     turned[...] = gated.astype(f32).T
     rows = msgs[0].shape[2]
@@ -325,38 +312,13 @@
     rows = model // (n_dp * groups * parts)
     return pl.pallas_call(
         functools.partial(gated_kernel, groups, parts, place_of),
-        out_shape=[jax.ShapeDtypeStruct((parts, groups, rows, local), bf16)] * n_dp
-        + [jax.ShapeDtypeStruct((1,), jnp.int32)],
+        out_shape=[jax.ShapeDtypeStruct((parts, groups, rows, local), bf16)] * n_dp,
         in_specs=[SMEM, VMEM, VMEM],
-        out_specs=[VMEM] * n_dp + [SMEM],
+        out_specs=[VMEM] * n_dp,
         scratch_shapes=[pltpu.VMEM((model, local), f32)],
         compiler_params=params(60),
         cost_estimate=cost(0, 4 * local * model),
     )(meta, gate, d_out)
-
-
-def d_attn_kernel(gate_ref, d_out_ref, w_ref, after_ref, out_ref):
-    del after_ref
-    block = 512
-    total = jnp.zeros(out_ref.shape, f32)
-    for at in range(0, w_ref.shape[0], block):
-        cols = slice(at, at + block)
-        gated = (gate_ref[:, cols] * d_out_ref[:, cols].astype(f32)).astype(bf16)
-        total = total + jnp.dot(gated, w_ref[cols, :], preferred_element_type=f32)
-    out_ref[...] = total.astype(bf16)
-
-
-def attn_gradient(gate, d_out, out_weight, after):
-    local, model = d_out.shape
-    inner = out_weight.shape[1]
-    return pl.pallas_call(
-        d_attn_kernel,
-        out_shape=jax.ShapeDtypeStruct((local, inner), bf16),
-        in_specs=[VMEM] * 3 + [ANY],
-        out_specs=VMEM,
-        compiler_params=params(),
-        cost_estimate=cost(2 * local * inner * model, 2 * inner * model),
-    )(gate, d_out, out_weight, after)
 
 
 def gather_kernel(n_dp, *refs):
@@ -380,7 +342,8 @@
 
 
 def project_kernel(
-    groups, parts, place_of, meta_ref, attn_ref, w_ref, gate_ref, d_out_ref, out_ref, term_ref, *refs
+    groups, parts, place_of, meta_ref, attn_ref, w_ref, gate_ref, d_out_ref, out_ref, d_attn_ref,
+    term_ref, *refs
 ):
     sent, by_place = refs[:-1], refs[-1]
     rows = attn_ref.shape[0]
@@ -393,6 +356,12 @@
         )
         out_ref[:, cols] = (got * gate_ref[:, cols]).astype(bf16)
         sums.append(jnp.sum(got * d_out_ref[:, cols].astype(f32), axis=0, keepdims=True))
+    total = jnp.zeros(d_attn_ref.shape, f32)
+    for at in range(0, w_ref.shape[0], block):
+        cols = slice(at, at + block)
+        gated = (gate_ref[:, cols] * d_out_ref[:, cols].astype(f32)).astype(bf16)
+        total = total + jnp.dot(gated, w_ref[cols, :], preferred_element_type=f32)
+    d_attn_ref[...] = total.astype(bf16)
     sums = jnp.concatenate(sums, axis=1)
     places, width = by_place.shape
     for s in range(places):
@@ -419,59 +388,86 @@
     rows, inner = attn.shape
     model = out_weight.shape[0]
     width = model // (groups * parts)
-    shapes = [jax.ShapeDtypeStruct((rows, model), bf16)]
+    shapes = [jax.ShapeDtypeStruct((rows, model), bf16), jax.ShapeDtypeStruct((rows, inner), bf16)]
     shapes += [jax.ShapeDtypeStruct((groups, width), f32)]
     shapes += [jax.ShapeDtypeStruct((rows + EXTRA, inner), bf16)] * (parts - 1)
     return pl.pallas_call(
         functools.partial(project_kernel, groups, parts, place_of),
         out_shape=shapes,
         in_specs=[SMEM, VMEM, VMEM, VMEM, VMEM],
-        out_specs=[VMEM] * (1 + parts),
+        out_specs=[VMEM] * (2 + parts),
         scratch_shapes=[pltpu.VMEM((groups * parts, width), f32)],
         compiler_params=params(),
-        cost_estimate=cost(2 * rows * inner * model, 2 * inner * model),
+        cost_estimate=cost(4 * rows * inner * model, 2 * inner * model),
     )(meta, attn, out_weight, gate, d_out)
+
+
+def split_gate(gate, size):
+    short = -gate.shape[1] % size
+    if short:
+        gate = jnp.concatenate([gate, jnp.zeros((1, short), f32)], axis=1)
+    high = gate.astype(bf16).astype(f32)
+    lines = [p[:, at : at + size] for p in (high, gate - high) for at in range(0, gate.shape[1], size)]
+    return jnp.concatenate(lines + [jnp.zeros((EXTRA - len(lines), size), f32)], axis=0)
+
+
+def joined_gate(lines, width):
+    n = -(-width // lines.shape[1])
+    both = lines[:n] + lines[n : 2 * n]
+    return jnp.concatenate([both[i : i + 1] for i in range(n)], axis=1)[:, :width]
 
 
 def grad_kernel(n_left, n_pieces, *refs):
     lefts, refs = refs[:n_left], refs[n_left:]
     pieces, refs = refs[:n_pieces], refs[n_pieces:]
-    term_ref, outs, (kept_ref, sent_ref) = refs[0], refs[1:-2], refs[-2:]
+    term_ref, outs = refs[0], refs[1:]
     groups, rows, depth = lefts[0].shape[1:]
     width = pieces[0].shape[1]
+    size = outs[0].shape[1]
     left = []
     for ref in lefts:
         left += [ref[i].reshape(groups * rows, depth) for i in range(ref.shape[0])]
     left = jnp.concatenate(left, axis=1)
+    homes = [((outs[0], 0),), ((outs[1], 0), (outs[2], outs[1].shape[0]))]
+    homes += [((out, 0),) for out in outs[3:]]
+    half = outs[1].shape[0]
+
+    def put(g, at, value):
+        out, start = homes[g][-1] if at >= half else homes[g][0]
+        out[at - start : at - start + value.shape[0], :] = value.astype(out.dtype)
+
     block = 256
     for start in range(0, width, block):
         right = jnp.concatenate([p[:depth, start : start + block] for p in pieces], axis=0)
         got = jnp.dot(left, right, preferred_element_type=f32)
-        for g, out in enumerate(outs):
-            out[:, start : start + block] = got[g * rows : (g + 1) * rows].astype(out.dtype)
+        for g in range(groups):
+            for at in range(0, block, size):
+                put(g, (start + at) // size * rows, got[g * rows : (g + 1) * rows, at : at + size])
     term = term_ref[...]
-    size = term.shape[1]
+    each = term.shape[1]
     for p in pieces:
         if p.shape[0] > depth:
             lines = p[depth:, :].astype(f32)
             line = lines[0:1, :] + lines[1:2, :]
             term = term + jnp.concatenate(
-                [line[:, g * size : (g + 1) * size] for g in range(groups)], axis=0
+                [line[:, g * each : (g + 1) * each] for g in range(groups)], axis=0
             )
-    kept_ref[...] = term[: groups // 2]
-    sent_ref[...] = term[groups // 2 :]
+    for g in range(groups):
+        put(g, width // size * rows, split_gate(term[g : g + 1], size))
 
 
 def grad_product(lefts, pieces, term):
     groups, rows, depth = lefts[0].shape[1:]
     width = pieces[0].shape[1]
+    size = 128
     total = groups * rows
     depth = depth * len(pieces)
-    shapes = [jax.ShapeDtypeStruct((rows, width), (f32, bf16)[g % 2]) for g in range(groups)]
-    shapes += [jax.ShapeDtypeStruct((groups // 2, term.shape[1]), f32)] * 2
+    full = width // size * rows + EXTRA
+    half = width // size // 2 * rows
+    shapes = [(full, f32), (half, bf16), (full - half, bf16), (full, f32), (full, bf16)]
     return pl.pallas_call(
         functools.partial(grad_kernel, len(lefts), len(pieces)),
-        out_shape=shapes,
+        out_shape=[jax.ShapeDtypeStruct((n, size), kind) for n, kind in shapes],
         in_specs=[VMEM] * (len(lefts) + len(pieces) + 1),
         out_specs=[VMEM] * len(shapes),
         compiler_params=params(),
@@ -481,23 +477,52 @@
     )(*lefts, *pieces, term)
 
 
-def pair_kernel(own_ref, got_ref, gate_ref, out_ref, gate_out):
-    out_ref[...] = (own_ref[...] + got_ref[...].astype(f32)).astype(bf16)
-    gate_out[...] = gate_ref[...]
-
-
-def pair_sum(own, got, gate):
-    return pl.pallas_call(
-        pair_kernel,
+def pair_kernel(gate_width, own_ref, got_ref, out_ref):
+    total = own_ref[...] + got_ref[...].astype(f32)
+    end = total.shape[0] - EXTRA
+    out_ref[:end, :] = total[:end].astype(bf16)
+    gate = joined_gate(total[end:], gate_width)
+    out_ref[end:, :] = split_gate(gate, total.shape[1]).astype(bf16)
+
+
+def pair_sum(own, got, gate_width):
+    return pl.pallas_call(
+        functools.partial(pair_kernel, gate_width),
+        out_shape=jax.ShapeDtypeStruct(got.shape, bf16),
+        in_specs=[VMEM] * 2,
+        out_specs=VMEM,
+        compiler_params=params(),
+        cost_estimate=cost(0, 8 * own.size),
+    )(own, got)
+
+
+def final_kernel(own_ref, far_ref, low_ref, high_ref, out_ref, gate_ref):
+    size = own_ref.shape[1]
+    rows = out_ref.shape[0]
+    half = low_ref.shape[0]
+
+    def total(at, count):
+        ref, start = (high_ref, half) if at >= half else (low_ref, 0)
+        got = own_ref[at : at + count, :] + far_ref[at : at + count, :].astype(f32)
+        return got + ref[at - start : at - start + count, :].astype(f32)
+
+    for i in range(out_ref.shape[1] // size):
+        out_ref[:, i * size : (i + 1) * size] = total(i * rows, rows)
+    gate_ref[...] = joined_gate(total(own_ref.shape[0] - EXTRA, EXTRA), gate_ref.shape[1])
+
+
+def final_sum(own, far, low, high, rows, width, gate_width):
+    return pl.pallas_call(
+        final_kernel,
         out_shape=[
-            jax.ShapeDtypeStruct(got.shape, bf16),
-            jax.ShapeDtypeStruct(gate.shape, f32),
+            jax.ShapeDtypeStruct((rows, width), f32),
+            jax.ShapeDtypeStruct((1, gate_width), f32),
         ],
-        in_specs=[VMEM] * 3,
+        in_specs=[VMEM] * 4,
         out_specs=[VMEM] * 2,
         compiler_params=params(),
-        cost_estimate=cost(0, 8 * own.size),
-    )(own, got, gate)
+        cost_estimate=cost(0, 8 * rows * width),
+    )(own, far, low, high)
 
 
 def on_device(
@@ -554,21 +579,22 @@
 
     heads = gw // head_size
     text_rows = G * slot_local
-    packed = pack(meta, image_k[0], image_v[0], image_q[0], G, head_size)
+    own, *rest = text_project(
+        meta, caption_len, slot_source, caption_states[0], caption_gain[None],
+        query_gain[None], key_gain[None], image_k[0], image_v[0], image_q[0], text_proj,
+        G, OC, place,
+    )
+    packed, sent = rest[:G], rest[G:]
     images = [packed[0]] + [to_z(packed[k], k) for k in range(1, G)]
     nears = [to_oc(packed[0], j) for j in range(1, OC)]
-
-    own, *sent = text_project(
-        meta, caption_len, slot_source, caption_states[0], caption_gain[None],
-        query_gain[None], key_gain[None], text_proj, G, OC, place,
-    )
     got = [to_oc(x, j + 1) for j, x in enumerate(sent)]
     own, sent = text_sum(own, got, text_rows)
     own, sent = text_sum(own, [to_z(sent, 1)], text_rows)
     got = to_z(sent, 2)
 
-    *gg, mark = gated_parts(meta, gate, d_out[0], n_dp, G, OC, place)
-    block = block_of(own, got, mark, images[1:], DT5, heads)
+    gg = gated_parts(meta, gate, d_out[0], n_dp, G, OC, place)
+    gg_dp = [gg[0], to_dp(gg[1], 1)]
+    block = block_of(own, got, gg_dp[1], images[1:], DT5, heads)
     blocks = [block] + [to_oc(block, j) for j in range(1, OC)]
     *outs, text_out = attention(images, nears, blocks, heads, image_local, text_rows)
 
@@ -576,7 +602,7 @@
     for k in range(G):
         rows = jnp.concatenate([outs[k], part(text_out, z ^ k, slot_local, 0)], axis=0)
         back.append(to_z(rows, k) if k else rows)
-    gg_dp = [gg[0]] + [to_dp(gg[k], k) for k in range(1, n_dp)]
+    gg_dp += [to_dp(gg[k], k) for k in range(2, n_dp)]
     lefts = [g[:1] for g in gg_dp]
     lefts += [to_oc(g, j + 1) for j, g in enumerate(gather_parts(gg_dp))]
     image_attn = assemble(meta, back, gg_dp[1:], image_local)
@@ -587,17 +613,18 @@
         text_attn = lax.dynamic_update_slice_in_dim(text_attn, rows, (z ^ k) * gw, 1)
 
     pieces = [image_attn] + [to_dp(image_attn, k) for k in range(1, n_dp)]
-    image_out, term, *sent = project(
+    image_out, d_attn, term, *sent = project(
         meta, image_attn, out_weight, gate, d_out[0], G, OC, place
     )
     for j in range(1, OC):
         pieces += [to_oc(sent[j - 1], j)] + [to_oc(p, j) for p in pieces[1:n_dp]]
-    *grads, kept, sent = grad_product(lefts, pieces, term)
-    pair, sent = pair_sum(grads[2], to_z(grads[3], 1), sent)
-    grad_wo = grads[0] + to_z(pair, 2).astype(f32) + to_z(grads[1], 1).astype(f32)
-    term = kept + to_z(sent, 2)
-    grad_gate = term[:1] + to_z(term[1:], 1)
-    d_attn = attn_gradient(gate, d_out[0], out_weight, grads[1])
+    R = model_width // (n_dp * n_seq)
+    gate_width = model_width // n_seq
+    own, low, high, own_pair, far = grad_product(lefts, pieces, term)
+    pair = pair_sum(own_pair, to_z(far, 1), gate_width)
+    grad_wo, grad_gate = final_sum(
+        own, to_z(pair, 2), to_z(low, 1), to_z(high, 1), R, inner_width, gate_width
+    )
     return (image_out[None], text_attn[None], d_attn[None], grad_wo, grad_gate)
 
 

time: 125 us -> 118 us (0.944)
  Pallas kernels: 27.2 us -> 22.4 us
  local copies, waits for them, and re-layouts: 9.59 us -> 5.9 us
  waiting for transfers between devices: 51.8 us -> 55 us
  other arithmetic: 2.52 us -> 1.02 us
    ppermute x13 -> x12, waiting for transfers between devices: 41.9 us -> 46.4 us  [to_z(): return lax.ppermute(x, 'seq', perm)]
    unnamed x20 -> x18, local copies, waits for them, and re-layouts: 9.45 us -> 5.77 us
    pallas_call x3 -> x2, Pallas kernels: 4.63 us -> 0.99 us  [the longest x1 0.91 us: final_sum(): pl.pallas_call(final_kernel, out_shape=[jax.ShapeDtypeStruct((rows, width...]
    pallas_call x1, Pallas kernels: 3.23 us -> 1.39 us  [grad_product(): pl.pallas_call(functools.partial(grad_kernel, len(lefts), len(pieces)), o...]
    ppermute x13 -> x12, starting transfers between devices: 23.1 us -> 21.5 us  [to_z(): return lax.ppermute(x, 'seq', perm)]
    add x3 -> x0, other arithmetic: 1.48 us -> none  [the longest x1 0.91 us: on_device(): grads[0] + to_z(pair, 2).astype(f32) + to_z(grads[1], 1).astype(f32)]
  transfers between devices with their start and end apart: 27 -> 26, of which waited for: 13 -> 12; matrix products, arithmetic and copies ran while one was open for 1% -> 0% of each run, Pallas kernels for 14% -> 11%
where the time goes in v9:
time: 118 us; the launch traced here: 117 us
  waiting for transfers between devices  55 us (47%)
  starting transfers between devices  31.2 us (26%)
  Pallas kernels  22.4 us (19%)
  local copies, waits for them, and re-layouts  5.9 us (5%)
  between operations  1.62 us (1%)
    ppermute x12, waiting for transfers between devices, to_z(): return lax.ppermute(x, 'seq', perm)  46.4 us
    ppermute x12, starting transfers between devices, to_z(): return lax.ppermute(x, 'seq', perm)  21.5 us
    ppermute x6, starting transfers between devices, to_dp(): return lax.ppermute(x, 'dp', [(a, a ^ k) for a in range(n_dp)])  8.05 us
    pallas_call x1, Pallas kernels, text_project(): pl.pallas_call(functools.partial(text_kernel, groups, heads, place_of), o...  5.79 us
    unnamed x18, local copies, waits for them, and re-layouts  5.77 us
    pallas_call x1, Pallas kernels, project(): pl.pallas_call(functools.partial(project_kernel, groups, parts, place_of)...  5.66 us
    ppermute x6, waiting for transfers between devices, to_dp(): return lax.ppermute(x, 'dp', [(a, a ^ k) for a in range(n_dp)])  5.19 us
    pallas_call x1, Pallas kernels, attention(): pl.pallas_call(functools.partial(attention_kernel, n, len(blocks), heads,...  5.07 us
  transfers between devices with their start and end apart: 26, of which 12 were waited for; matrix products, arithmetic and copies ran while one was open for 0% of the time, Pallas kernels for 11%

profile of v9, /device:TPU:0, one launch (start us, length us, event | category | flops | bytes accessed | tf_op | source)
XLA Modules:
  0.0 117.2 jit_solution(6264265942156739413)
XLA Ops:
  1.4 0.7 pad_add_fusion.meta_ref
  2.1 5.8 %shard_map.164 = (f32[4,336,128]{2,1,0:T(8,128)}, bf16[1152,128]{1,0:T(8,128)(2,1)}, bf16[1152,128]{1,0:T(8,128)(2,1)}, bf16[1152,128]{1,0:T(8,128)(2,1)}, bf16[...) custom-call(s32[3]{0:T(128)} %pad_add_fusion.meta_ref, s32[1]{0:T(128)} %copy.22.len_ref, s32[1,64]{1,0:T(1,128)} %src_ref.1, ...), custom_call_target="tpu_custom_call" | custom-call | flops 301989888 | bytes 4718592 | tf_op jit(solution)/shard_map/pallas_call | solution.py:121
  7.9 0.5 collective-permute-start.4
  8.4 2.6 %collective-permute-start = (bf16[1152,128]{1,0:T(8,128)(2,1)}, bf16[1152,128]{1,0:T(8,128)(2,1)S(1)}, u32[]{:S(2)}, u32[]{:S(2)}) collective-permute-start(bf16[1152,128]{1,0:T(8,128)(2,1)} %get-tuple-element.36), channel_id=1, source_target_pairs={{0,2},{2,0},{4,6},{6,4},{1,3},{3,1},{5,7},{7,5},{8,10},{10,8},{12,... | collective-permute-start | bytes 884744 | tf_op jit(solution)/shard_map/ppermute | solution.py:558
  11.0 2.6 %collective-permute-start.1 = (bf16[1152,128]{1,0:T(8,128)(2,1)}, bf16[1152,128]{1,0:T(8,128)(2,1)S(1)}, u32[]{:S(2)}, u32[]{:S(2)}) collective-permute-start(bf16[1152,128]{1,0:T(8,128)(2,1)} %get-tuple-element.37), channel_id=1, source_target_pairs={{0,4},{2,6},{4,0},{6,2},{1,5},{3,7},{5,1},{7,3},{8,12},{10,14},{12... | collective-permute-start | bytes 884744 | tf_op jit(solution)/shard_map/ppermute | solution.py:558
  13.6 1.1 copy-done.2
  14.7 0.2 shard_map.165
  14.9 1.0 collective-permute-start.5
  15.9 2.3 %shard_map.167 = (bf16[2,4,96,128]{3,2,1,0:T(8,128)(2,1)}, bf16[2,4,96,128]{3,2,1,0:T(8,128)(2,1)}, bf16[2,4,96,128]{3,2,1,0:T(8,128)(2,1)}, bf16[2,4,96,128]{3,2,1,0:T(8,128)(2,1)}) custom-call(s32[3]{0:T(128)} %pad_add_fusion.meta_ref, f32[1,3072]{1,0:T(1,128)} %gate_ref.3, bf16[128,3072]{1,0:T(8,128)(2,1)} %bitcast.31), custom_call_target="tpu_custom_call" | custom-call | bytes 1572864 | tf_op jit(solution)/shard_map/pallas_call | solution.py:313
  18.2 1.5 %collective-permute-start.7 = (bf16[2,4,96,128]{3,2,1,0:T(8,128)(2,1)}, bf16[2,4,96,128]{3,2,1,0:T(8,128)(2,1)S(1)}, u32[]{:S(2)}, u32[]{:S(2)}) collective-permute-start(bf16[2,4,96,128]{3,2,1,0:T(8,128)(2,1)} %get-tuple-element.45), channel_id=1, source_target_pairs={{0,8},{8,0},{16,24},{24,16},{1,9},{9,1},{17,25},{25,17},{2,10},{10... | collective-permute-start | bytes 589832 | tf_op jit(solution)/shard_map/ppermute | solution.py:565
  19.7 15.3 %collective-permute-done.5.refs_0_ = bf16[2,320,128]{2,1,0:T(8,128)(2,1)S(1)} collective-permute-done((bf16[2,320,128]{2,1,0:T(8,128)(2,1)S(1)}, bf16[2,320,128]{2,1,0:T(8,128)(2,1)S(1)}, u32[]{:S(2)}, u32[]{:S(2)}) %collective-permute-start.5) | collective-permute-done | bytes 163872 | tf_op jit(solution)/shard_map/ppermute | solution.py:558
  35.0 0.2 shard_map.166
  35.2 2.9 %collective-permute-start.6 = (bf16[1,320,128]{2,1,0:T(8,128)(2,1)S(1)}, bf16[1,320,128]{2,1,0:T(8,128)(2,1)S(1)}, u32[]{:S(2)}, u32[]{:S(2)}) collective-permute-start(bf16[1,320,128]{2,1,0:T(8,128)(2,1)S(1)} %get-tuple-element.44), channel_id=1, source_target_pairs={{0,4},{2,6},{4,0},{6,2},{1,5},{3,7},{5,1},{7,3},{8,12},{10,14},{12... | collective-permute-start | bytes 245768 | tf_op jit(solution)/shard_map/ppermute | solution.py:558
  38.1 5.7 %collective-permute-done.6.got_ref = bf16[1,320,128]{2,1,0:T(8,128)(2,1)S(1)} collective-permute-done((bf16[1,320,128]{2,1,0:T(8,128)(2,1)S(1)}, bf16[1,320,128]{2,1,0:T(8,128)(2,1)S(1)}, u32[]{:S(2)}, u32[]{:S(2)}) %collective-permute-start.6) | collective-permute-done | bytes 81952 | tf_op jit(solution)/shard_map/ppermute | solution.py:558
  43.8 0.3 shard_map.168.refs_5_
  44.1 1.6 %collective-permute-start.12 = (bf16[2,4,96,128]{3,2,1,0:T(8,128)(2,1)}, bf16[2,4,96,128]{3,2,1,0:T(8,128)(2,1)S(1)}, u32[]{:S(2)}, u32[]{:S(2)}) collective-permute-start(bf16[2,4,96,128]{3,2,1,0:T(8,128)(2,1)} %get-tuple-element.51), channel_id=1, source_target_pairs={{0,16},{8,24},{16,0},{24,8},{1,17},{9,25},{17,1},{25,9},{2,18},{10... | collective-permute-start | bytes 589832 | tf_op jit(solution)/shard_map/ppermute | solution.py:565
  45.7 1.4 %collective-permute-start.13 = (bf16[2,4,96,128]{3,2,1,0:T(8,128)(2,1)}, bf16[2,4,96,128]{3,2,1,0:T(8,128)(2,1)S(1)}, u32[]{:S(2)}, u32[]{:S(2)}) collective-permute-start(bf16[2,4,96,128]{3,2,1,0:T(8,128)(2,1)} %get-tuple-element.52), channel_id=1, source_target_pairs={{0,24},{8,16},{16,8},{24,0},{1,25},{9,17},{17,9},{25,1},{2,26},{10... | collective-permute-start | bytes 589832 | tf_op jit(solution)/shard_map/ppermute | solution.py:565
  47.2 0.1 fusion.6
  47.2 1.7 %collective-permute-done.3.refs_4_ = bf16[1152,128]{1,0:T(8,128)(2,1)S(1)} collective-permute-done((bf16[1152,128]{1,0:T(8,128)(2,1)}, bf16[1152,128]{1,0:T(8,128)(2,1)S(1)}, u32[]{:S(2)}, u32[]{:S(2)}) %collective-permute-start.3) | collective-permute-done | bytes 294944 | tf_op jit(solution)/shard_map/ppermute | solution.py:562
  48.9 1.0 copy-done.6
  49.9 5.1 %shard_map.169 = (bf16[128,384]{1,0:T(8,128)(2,1)S(1)}, bf16[128,384]{1,0:T(8,128)(2,1)S(1)}, bf16[128,384]{1,0:T(8,128)(2,1)S(1)}, bf16[128,384]{1,0:T(8,128)(2,1)S(1)}, bf16[32,384]{1,0:T(8,128)(2,1)S(1)}) custom-call(bf16[1152,128]{1,0:T(8,128)(2,1)S(1)} %copy-done.6, bf16[1152,128]{1,0:T(8,128)(2,1)S(1)} %collective-permute-done.refs_0_.refs_1_, ...), custom_call_target="tpu_custom_call" | custom-call | flops 909115392 | bytes 2506752 | tf_op jit(solution)/shard_map/pallas_call | solution.py:263
  55.1 3.1 %collective-permute-start.10 = (bf16[136,384]{1,0:T(8,128)(2,1)S(1)}, bf16[136,384]{1,0:T(8,128)(2,1)S(1)}, u32[]{:S(2)}, u32[]{:S(2)}) collective-permute-start(bf16[136,384]{1,0:T(8,128)(2,1)S(1)} %pad_maximum_fusion.2), channel_id=1, source_target_pairs={{0,4},{2,6},{4,0},{6,2},{1,5},{3,7},{5,1},{7,3},{8,12},{10,14},{12... | collective-permute-start | bytes 313352 | tf_op jit(solution)/shard_map/ppermute | solution.py:558
  58.2 1.4 %collective-permute-start.11 = (bf16[136,384]{1,0:T(8,128)(2,1)S(1)}, bf16[136,384]{1,0:T(8,128)(2,1)S(1)}, u32[]{:S(2)}, u32[]{:S(2)}) collective-permute-start(bf16[136,384]{1,0:T(8,128)(2,1)S(1)} %pad_maximum_fusion.3), channel_id=1, source_target_pairs={{0,6},{2,4},{4,2},{6,0},{1,7},{3,5},{5,3},{7,1},{8,14},{10,12},{12... | collective-permute-start | bytes 313352 | tf_op jit(solution)/shard_map/ppermute | solution.py:558
  59.8 2.0 %collective-permute-done.9.refs_1_ = bf16[136,384]{1,0:T(8,128)(2,1)S(1)} collective-permute-done((bf16[136,384]{1,0:T(8,128)(2,1)S(1)}, bf16[136,384]{1,0:T(8,128)(2,1)S(1)}, u32[]{:S(2)}, u32[]{:S(2)}) %collective-permute-start.9) | collective-permute-done | bytes 104480 | tf_op jit(solution)/shard_map/ppermute | solution.py:558
  61.7 4.8 %collective-permute-done.10.refs_2_ = bf16[136,384]{1,0:T(8,128)(2,1)S(1)} collective-permute-done((bf16[136,384]{1,0:T(8,128)(2,1)S(1)}, bf16[136,384]{1,0:T(8,128)(2,1)S(1)}, u32[]{:S(2)}, u32[]{:S(2)}) %collective-permute-start.10) | collective-permute-done | bytes 104480 | tf_op jit(solution)/shard_map/ppermute | solution.py:558
  66.5 0.6 shard_map.170.attn_ref.refs_5_
  67.1 1.6 %collective-permute-start.17 = (bf16[128,1536]{1,0:T(8,128)(2,1)S(1)}, bf16[128,1536]{1,0:T(8,128)(2,1)S(1)}, u32[]{:S(2)}, u32[]{:S(2)}) collective-permute-start(bf16[128,1536]{1,0:T(8,128)(2,1)S(1)} %shard_map.170.attn_ref.refs_5_), channel_id=1, source_target_pairs={{0,24},{8,16},{16,8},{24,0},{1,25},{9,17},{17,9},{25,1},{2,26},{10... | collective-permute-start | bytes 1179656 | tf_op jit(solution)/shard_map/ppermute | solution.py:565
  68.7 0.5 collective-permute-start.16
  69.1 1.5 %collective-permute-start.15 = (bf16[128,1536]{1,0:T(8,128)(2,1)S(1)}, bf16[128,1536]{1,0:T(8,128)(2,1)S(1)}, u32[]{:S(2)}, u32[]{:S(2)}) collective-permute-start(bf16[128,1536]{1,0:T(8,128)(2,1)S(1)} %shard_map.170.attn_ref.refs_5_), channel_id=1, source_target_pairs={{0,8},{8,0},{16,24},{24,16},{1,9},{9,1},{17,25},{25,17},{2,10},{10... | collective-permute-start | bytes 1179656 | tf_op jit(solution)/shard_map/ppermute | solution.py:565
  70.7 3.7 %copy-done = bf16[3072,1536]{1,0:T(8,128)(2,1)S(1)} copy-done((bf16[3072,1536]{1,0:T(8,128)(2,1)S(1)}, bf16[3072,1536]{1,0:T(8,128)(2,1)}, u32[]{:S(2)}) %copy-start) | copy-done | bytes 9437208
  74.3 5.7 %shard_map.171 = (bf16[128,3072]{1,0:T(8,128)(2,1)}, bf16[128,1536]{1,0:T(8,128)(2,1)}, f32[4,384]{1,0:T(4,128)S(1)}, bf16[144,1536]{1,0:T(8,128)(2,1)S(1)}) custom-call(s32[3]{0:T(128)S(1)} %copy-done.5, bf16[128,1536]{1,0:T(8,128)(2,1)S(1)} %shard_map.170.attn_ref.refs_5_, bf16[3072,1536]{1,0:T(8,128)(2,1)S(1)} %copy-done, f32[1,3072]{1,0:T(1,128)S(1)} %copy-done.4, ...), custom_call_target="tpu_custom_call" | custom-call | flops 2415919104 | bytes 9437184 | tf_op jit(solution)/shard_map/pallas_call | solution.py:394
  80.0 0.6 collective-permute-start.14
  80.6 0.1 collective-permute-start.21
  80.7 5.1 %collective-permute-done.16.refs_7_ = bf16[128,1536]{1,0:T(8,128)(2,1)S(1)} collective-permute-done((bf16[128,1536]{1,0:T(8,128)(2,1)S(1)}, bf16[128,1536]{1,0:T(8,128)(2,1)S(1)}, u32[]{:S(2)}, u32[]{:S(2)}) %collective-permute-start.16) | collective-permute-done | bytes 393248 | tf_op jit(solution)/shard_map/ppermute | solution.py:565
  85.9 0.4 collective-permute-start.19
  86.4 1.1 collective-permute-done.20.refs_11_
  87.5 0.6 collective-permute-done.19.refs_10_
  88.1 1.4 %shard_map.173 = (f32[1168,128]{1,0:T(8,128)S(1)}, bf16[576,128]{1,0:T(8,128)(2,1)S(1)}, bf16[592,128]{1,0:T(8,128)(2,1)S(1)}, f32[1168,128]{1,0:T(8,128)S(1)}, bf16[1168,128]{1,0:T(8,128)(2,1)S(1)}) custom-call(bf16[1,4,96,128]{3,2,1,0:T(8,128)(2,1)S(1)} %slice.24.refs_0_, bf16[1,4,96,128]{3,2,1,0:T(8,128)(2,1)S(1)} %slice.31.refs_1_, ...), custom_call_target="tpu_custom_call" | custom-call | flops 1207959552 | bytes 5111808 | tf_op jit(solution)/shard_map/pallas_call | solution.py:468
  89.5 3.1 %collective-permute-start.22 = (bf16[1168,128]{1,0:T(8,128)(2,1)S(1)}, bf16[1168,128]{1,0:T(8,128)(2,1)S(1)}, u32[]{:S(2)}, u32[]{:S(2)}) collective-permute-start(bf16[1168,128]{1,0:T(8,128)(2,1)S(1)} %get-tuple-element.60), channel_id=1, source_target_pairs={{0,2},{2,0},{4,6},{6,4},{1,3},{3,1},{5,7},{7,5},{8,10},{10,8},{12,... | collective-permute-start | bytes 897032 | tf_op jit(solution)/shard_map/ppermute | solution.py:558
  92.6 7.3 %collective-permute-done.22.got_ref = bf16[1168,128]{1,0:T(8,128)(2,1)S(1)} collective-permute-done((bf16[1168,128]{1,0:T(8,128)(2,1)S(1)}, bf16[1168,128]{1,0:T(8,128)(2,1)S(1)}, u32[]{:S(2)}, u32[]{:S(2)}) %collective-permute-start.22) | collective-permute-done | bytes 299040 | tf_op jit(solution)/shard_map/ppermute | solution.py:558
  100.0 0.1 shard_map.174
  100.0 2.7 %collective-permute-start.23 = (bf16[1168,128]{1,0:T(8,128)(2,1)S(1)}, bf16[1168,128]{1,0:T(8,128)(2,1)S(1)}, u32[]{:S(2)}, u32[]{:S(2)}) collective-permute-start(bf16[1168,128]{1,0:T(8,128)(2,1)S(1)} %shard_map.174), channel_id=1, source_target_pairs={{0,4},{2,6},{4,0},{6,2},{1,5},{3,7},{5,1},{7,3},{8,12},{10,14},{12... | collective-permute-start | bytes 897032 | tf_op jit(solution)/shard_map/ppermute | solution.py:558
  102.8 0.1 fusion.3
  102.8 0.3 collective-permute-start.24
  103.1 1.7 %collective-permute-start.25 = (bf16[592,128]{1,0:T(8,128)(2,1)S(1)}, bf16[592,128]{1,0:T(8,128)(2,1)S(1)}, u32[]{:S(2)}, u32[]{:S(2)}) collective-permute-start(bf16[592,128]{1,0:T(8,128)(2,1)S(1)} %get-tuple-element.62), channel_id=1, source_target_pairs={{0,2},{2,0},{4,6},{6,4},{1,3},{3,1},{5,7},{7,5},{8,10},{10,8},{12,... | collective-permute-start | bytes 454664 | tf_op jit(solution)/shard_map/ppermute | solution.py:558
  104.9 8.5 %collective-permute-done.24.low_ref = bf16[576,128]{1,0:T(8,128)(2,1)S(1)} collective-permute-done((bf16[576,128]{1,0:T(8,128)(2,1)S(1)}, bf16[576,128]{1,0:T(8,128)(2,1)S(1)}, u32[]{:S(2)}, u32[]{:S(2)}) %collective-permute-start.24) | collective-permute-done | bytes 147488 | tf_op jit(solution)/shard_map/ppermute | solution.py:558
  113.4 2.9 %collective-permute-done.25.high_ref = bf16[592,128]{1,0:T(8,128)(2,1)S(1)} collective-permute-done((bf16[592,128]{1,0:T(8,128)(2,1)S(1)}, bf16[592,128]{1,0:T(8,128)(2,1)S(1)}, u32[]{:S(2)}, u32[]{:S(2)}) %collective-permute-start.25) | collective-permute-done | bytes 151584 | tf_op jit(solution)/shard_map/ppermute | solution.py:558
  116.3 0.9 shard_map.175
  (51 shorter events, 0.7 us)
Async XLA Ops:
  0.6 46.5 %copy-start.8 = (s32[1,64]{1,0:T(1,128)S(1)}, s32[1,64]{1,0:T(1,128)}, u32[]{:S(2)}) copy-start(s32[1,64]{1,0:T(1,128)} %src_ref.1) | copy-start | bytes 772
  0.6 70.0 %copy-start.4 = (f32[1,3072]{1,0:T(1,128)S(1)}, f32[1,3072]{1,0:T(1,128)}, u32[]{:S(2)}) copy-start(f32[1,3072]{1,0:T(1,128)} %gate_ref.3) | copy-start | bytes 36868
  0.7 70.0 %copy-start.1 = (bf16[1,128,3072]{2,1,0:T(8,128)(2,1)S(1)}, bf16[1,128,3072]{2,1,0:T(8,128)(2,1)}, u32[]{:S(2)}) copy-start(bf16[1,128,3072]{2,1,0:T(8,128)(2,1)} %param.25) | copy-start | bytes 2359300
  2.1 64.4 %copy-start.5 = (s32[3]{0:T(128)S(1)}, s32[3]{0:T(128)}, u32[]{:S(2)}) copy-start(s32[3]{0:T(128)} %pad_add_fusion.meta_ref) | copy-start | bytes 40
  7.9 5.8 %collective-permute-start.4 = (bf16[4,320,128]{2,1,0:T(8,128)(2,1)}, bf16[4,320,128]{2,1,0:T(8,128)(2,1)S(1)}, u32[]{:S(2)}, u32[]{:S(2)}) collective-permute-start(bf16[4,320,128]{2,1,0:T(8,128)(2,1)} %get-tuple-element.40), channel_id=1, source_target_pairs={{0,1},{2,3},{4,5},{6,7},{1,0},{3,2},{5,4},{7,6},{8,9},{10,11},{12,... | collective-permute-start | bytes 983048 | tf_op jit(solution)/shard_map/ppermute | solution.py:562
  8.4 29.7 %collective-permute-start = (bf16[1152,128]{1,0:T(8,128)(2,1)}, bf16[1152,128]{1,0:T(8,128)(2,1)S(1)}, u32[]{:S(2)}, u32[]{:S(2)}) collective-permute-start(bf16[1152,128]{1,0:T(8,128)(2,1)} %get-tuple-element.36), channel_id=1, source_target_pairs={{0,2},{2,0},{4,6},{6,4},{1,3},{3,1},{5,7},{7,5},{8,10},{10,8},{12,... | collective-permute-start | bytes 884744 | tf_op jit(solution)/shard_map/ppermute | solution.py:558
  11.0 27.1 %collective-permute-start.1 = (bf16[1152,128]{1,0:T(8,128)(2,1)}, bf16[1152,128]{1,0:T(8,128)(2,1)S(1)}, u32[]{:S(2)}, u32[]{:S(2)}) collective-permute-start(bf16[1152,128]{1,0:T(8,128)(2,1)} %get-tuple-element.37), channel_id=1, source_target_pairs={{0,4},{2,6},{4,0},{6,2},{1,5},{3,7},{5,1},{7,3},{8,12},{10,14},{12... | collective-permute-start | bytes 884744 | tf_op jit(solution)/shard_map/ppermute | solution.py:558
  13.6 24.5 %collective-permute-start.2 = (bf16[1152,128]{1,0:T(8,128)(2,1)}, bf16[1152,128]{1,0:T(8,128)(2,1)S(1)}, u32[]{:S(2)}, u32[]{:S(2)}) collective-permute-start(bf16[1152,128]{1,0:T(8,128)(2,1)} %get-tuple-element.38), channel_id=1, source_target_pairs={{0,6},{2,4},{4,2},{6,0},{1,7},{3,5},{5,3},{7,1},{8,14},{10,12},{12... | collective-permute-start | bytes 884744 | tf_op jit(solution)/shard_map/ppermute | solution.py:558
  13.6 1.1 copy-start.2
  14.9 20.1 %collective-permute-start.5 = (bf16[2,320,128]{2,1,0:T(8,128)(2,1)S(1)}, bf16[2,320,128]{2,1,0:T(8,128)(2,1)S(1)}, u32[]{:S(2)}, u32[]{:S(2)}) collective-permute-start(bf16[2,320,128]{2,1,0:T(8,128)(2,1)S(1)} %get-tuple-element.42), channel_id=1, source_target_pairs={{0,2},{2,0},{4,6},{6,4},{1,3},{3,1},{5,7},{7,5},{8,10},{10,8},{12,... | collective-permute-start | bytes 491528 | tf_op jit(solution)/shard_map/ppermute | solution.py:558
  18.2 19.9 %collective-permute-start.7 = (bf16[2,4,96,128]{3,2,1,0:T(8,128)(2,1)}, bf16[2,4,96,128]{3,2,1,0:T(8,128)(2,1)S(1)}, u32[]{:S(2)}, u32[]{:S(2)}) collective-permute-start(bf16[2,4,96,128]{3,2,1,0:T(8,128)(2,1)} %get-tuple-element.45), channel_id=1, source_target_pairs={{0,8},{8,0},{16,24},{24,16},{1,9},{9,1},{17,25},{25,17},{2,10},{10... | collective-permute-start | bytes 589832 | tf_op jit(solution)/shard_map/ppermute | solution.py:565
  35.0 45.0 %copy-start.3 = (bf16[2,4,96,128]{3,2,1,0:T(8,128)(2,1)S(1)}, bf16[2,4,96,128]{3,2,1,0:T(8,128)(2,1)}, u32[]{:S(2)}) copy-start(bf16[2,4,96,128]{3,2,1,0:T(8,128)(2,1)} %get-tuple-element.55.refs_0_) | copy-start | bytes 589828
  35.2 8.6 %collective-permute-start.6 = (bf16[1,320,128]{2,1,0:T(8,128)(2,1)S(1)}, bf16[1,320,128]{2,1,0:T(8,128)(2,1)S(1)}, u32[]{:S(2)}, u32[]{:S(2)}) collective-permute-start(bf16[1,320,128]{2,1,0:T(8,128)(2,1)S(1)} %get-tuple-element.44), channel_id=1, source_target_pairs={{0,4},{2,6},{4,0},{6,2},{1,5},{3,7},{5,1},{7,3},{8,12},{10,14},{12... | collective-permute-start | bytes 245768 | tf_op jit(solution)/shard_map/ppermute | solution.py:558
  44.1 4.9 %collective-permute-start.8 = (bf16[2608,128]{1,0:T(8,128)(2,1)S(1)}, bf16[2608,128]{1,0:T(8,128)(2,1)}, u32[]{:S(2)}, u32[]{:S(2)}) collective-permute-start(bf16[2608,128]{1,0:T(8,128)(2,1)S(1)} %shard_map.168.refs_5_), channel_id=1, source_target_pairs={{0,1},{2,3},{4,5},{6,7},{1,0},{3,2},{5,4},{7,6},{8,9},{10,11},{12,... | collective-permute-start | bytes 2002952 | tf_op jit(solution)/shard_map/ppermute | solution.py:562
  44.1 15.6 %collective-permute-start.12 = (bf16[2,4,96,128]{3,2,1,0:T(8,128)(2,1)}, bf16[2,4,96,128]{3,2,1,0:T(8,128)(2,1)S(1)}, u32[]{:S(2)}, u32[]{:S(2)}) collective-permute-start(bf16[2,4,96,128]{3,2,1,0:T(8,128)(2,1)} %get-tuple-element.51), channel_id=1, source_target_pairs={{0,16},{8,24},{16,0},{24,8},{1,17},{9,25},{17,1},{25,9},{2,18},{10... | collective-permute-start | bytes 589832 | tf_op jit(solution)/shard_map/ppermute | solution.py:565
  45.7 14.0 %collective-permute-start.13 = (bf16[2,4,96,128]{3,2,1,0:T(8,128)(2,1)}, bf16[2,4,96,128]{3,2,1,0:T(8,128)(2,1)S(1)}, u32[]{:S(2)}, u32[]{:S(2)}) collective-permute-start(bf16[2,4,96,128]{3,2,1,0:T(8,128)(2,1)} %get-tuple-element.52), channel_id=1, source_target_pairs={{0,24},{8,16},{16,8},{24,0},{1,25},{9,17},{17,9},{25,1},{2,26},{10... | collective-permute-start | bytes 589832 | tf_op jit(solution)/shard_map/ppermute | solution.py:565
  47.1 1.8 %collective-permute-start.3 = (bf16[1152,128]{1,0:T(8,128)(2,1)}, bf16[1152,128]{1,0:T(8,128)(2,1)S(1)}, u32[]{:S(2)}, u32[]{:S(2)}) collective-permute-start(bf16[1152,128]{1,0:T(8,128)(2,1)} %get-tuple-element.35.refs_0_), channel_id=1, source_target_pairs={{0,1},{2,3},{4,5},{6,7},{1,0},{3,2},{5,4},{7,6},{8,9},{10,11},{12,... | collective-permute-start | bytes 884744 | tf_op jit(solution)/shard_map/ppermute | solution.py:562
  48.9 1.0 copy-start.6
  55.0 6.7 %collective-permute-start.9 = (bf16[136,384]{1,0:T(8,128)(2,1)S(1)}, bf16[136,384]{1,0:T(8,128)(2,1)S(1)}, u32[]{:S(2)}, u32[]{:S(2)}) collective-permute-start(bf16[136,384]{1,0:T(8,128)(2,1)S(1)} %pad_maximum_fusion.1), channel_id=1, source_target_pairs={{0,2},{2,0},{4,6},{6,4},{1,3},{3,1},{5,7},{7,5},{8,10},{10,8},{12,... | collective-permute-start | bytes 313352 | tf_op jit(solution)/shard_map/ppermute | solution.py:558
  55.1 11.4 %collective-permute-start.10 = (bf16[136,384]{1,0:T(8,128)(2,1)S(1)}, bf16[136,384]{1,0:T(8,128)(2,1)S(1)}, u32[]{:S(2)}, u32[]{:S(2)}) collective-permute-start(bf16[136,384]{1,0:T(8,128)(2,1)S(1)} %pad_maximum_fusion.2), channel_id=1, source_target_pairs={{0,4},{2,6},{4,0},{6,2},{1,5},{3,7},{5,1},{7,3},{8,12},{10,14},{12... | collective-permute-start | bytes 313352 | tf_op jit(solution)/shard_map/ppermute | solution.py:558
  58.2 8.3 %collective-permute-start.11 = (bf16[136,384]{1,0:T(8,128)(2,1)S(1)}, bf16[136,384]{1,0:T(8,128)(2,1)S(1)}, u32[]{:S(2)}, u32[]{:S(2)}) collective-permute-start(bf16[136,384]{1,0:T(8,128)(2,1)S(1)} %pad_maximum_fusion.3), channel_id=1, source_target_pairs={{0,6},{2,4},{4,2},{6,0},{1,7},{3,5},{5,3},{7,1},{8,14},{10,12},{12... | collective-permute-start | bytes 313352 | tf_op jit(solution)/shard_map/ppermute | solution.py:558
  67.1 13.5 %collective-permute-start.17 = (bf16[128,1536]{1,0:T(8,128)(2,1)S(1)}, bf16[128,1536]{1,0:T(8,128)(2,1)S(1)}, u32[]{:S(2)}, u32[]{:S(2)}) collective-permute-start(bf16[128,1536]{1,0:T(8,128)(2,1)S(1)} %shard_map.170.attn_ref.refs_5_), channel_id=1, source_target_pairs={{0,24},{8,16},{16,8},{24,0},{1,25},{9,17},{17,9},{25,1},{2,26},{10... | collective-permute-start | bytes 1179656 | tf_op jit(solution)/shard_map/ppermute | solution.py:565
  68.7 17.2 %collective-permute-start.16 = (bf16[128,1536]{1,0:T(8,128)(2,1)S(1)}, bf16[128,1536]{1,0:T(8,128)(2,1)S(1)}, u32[]{:S(2)}, u32[]{:S(2)}) collective-permute-start(bf16[128,1536]{1,0:T(8,128)(2,1)S(1)} %shard_map.170.attn_ref.refs_5_), channel_id=1, source_target_pairs={{0,16},{8,24},{16,0},{24,8},{1,17},{9,25},{17,1},{25,9},{2,18},{10... | collective-permute-start | bytes 1179656 | tf_op jit(solution)/shard_map/ppermute | solution.py:565
  69.1 16.7 %collective-permute-start.15 = (bf16[128,1536]{1,0:T(8,128)(2,1)S(1)}, bf16[128,1536]{1,0:T(8,128)(2,1)S(1)}, u32[]{:S(2)}, u32[]{:S(2)}) collective-permute-start(bf16[128,1536]{1,0:T(8,128)(2,1)S(1)} %shard_map.170.attn_ref.refs_5_), channel_id=1, source_target_pairs={{0,8},{8,0},{16,24},{24,16},{1,9},{9,1},{17,25},{25,17},{2,10},{10... | collective-permute-start | bytes 1179656 | tf_op jit(solution)/shard_map/ppermute | solution.py:565
  70.7 3.7 %copy-start = (bf16[3072,1536]{1,0:T(8,128)(2,1)S(1)}, bf16[3072,1536]{1,0:T(8,128)(2,1)}, u32[]{:S(2)}) copy-start(bf16[3072,1536]{1,0:T(8,128)(2,1)} %w_ref.3) | copy-start | bytes 28311556
  80.0 6.4 %collective-permute-start.18 = (bf16[144,1536]{1,0:T(8,128)(2,1)S(1)}, bf16[144,1536]{1,0:T(8,128)(2,1)S(1)}, u32[]{:S(2)}, u32[]{:S(2)}) collective-permute-start(bf16[144,1536]{1,0:T(8,128)(2,1)S(1)} %get-tuple-element.56), channel_id=1, source_target_pairs={{0,1},{2,3},{4,5},{6,7},{1,0},{3,2},{5,4},{7,6},{8,9},{10,11},{12,... | collective-permute-start | bytes 1327112 | tf_op jit(solution)/shard_map/ppermute | solution.py:562
  80.0 6.4 %collective-permute-start.14 = (bf16[4,4,96,128]{3,2,1,0:T(8,128)(2,1)S(1)}, bf16[4,4,96,128]{3,2,1,0:T(8,128)(2,1)S(1)}, u32[]{:S(2)}, u32[]{:S(2)}) collective-permute-start(bf16[4,4,96,128]{3,2,1,0:T(8,128)(2,1)S(1)} %shard_map.172), channel_id=1, source_target_pairs={{0,1},{2,3},{4,5},{6,7},{1,0},{3,2},{5,4},{7,6},{8,9},{10,11},{12,... | collective-permute-start | bytes 1179656 | tf_op jit(solution)/shard_map/ppermute | solution.py:562
  80.6 5.8 %collective-permute-start.21 = (bf16[128,1536]{1,0:T(8,128)(2,1)S(1)}, bf16[128,1536]{1,0:T(8,128)(2,1)S(1)}, u32[]{:S(2)}, u32[]{:S(2)}) collective-permute-start(bf16[128,1536]{1,0:T(8,128)(2,1)S(1)} %collective-permute-done.17.refs_8_), channel_id=1, source_target_pairs={{0,1},{2,3},{4,5},{6,7},{1,0},{3,2},{5,4},{7,6},{8,9},{10,11},{12,... | collective-permute-start | bytes 1179656 | tf_op jit(solution)/shard_map/ppermute | solution.py:562
  85.8 1.7 %collective-permute-start.20 = (bf16[128,1536]{1,0:T(8,128)(2,1)S(1)}, bf16[128,1536]{1,0:T(8,128)(2,1)S(1)}, u32[]{:S(2)}, u32[]{:S(2)}) collective-permute-start(bf16[128,1536]{1,0:T(8,128)(2,1)S(1)} %collective-permute-done.16.refs_7_), channel_id=1, source_target_pairs={{0,1},{2,3},{4,5},{6,7},{1,0},{3,2},{5,4},{7,6},{8,9},{10,11},{12,... | collective-permute-start | bytes 1179656 | tf_op jit(solution)/shard_map/ppermute | solution.py:562
  85.9 2.2 %collective-permute-start.19 = (bf16[128,1536]{1,0:T(8,128)(2,1)S(1)}, bf16[128,1536]{1,0:T(8,128)(2,1)S(1)}, u32[]{:S(2)}, u32[]{:S(2)}) collective-permute-start(bf16[128,1536]{1,0:T(8,128)(2,1)S(1)} %collective-permute-done.15.refs_6_), channel_id=1, source_target_pairs={{0,1},{2,3},{4,5},{6,7},{1,0},{3,2},{5,4},{7,6},{8,9},{10,11},{12,... | collective-permute-start | bytes 1179656 | tf_op jit(solution)/shard_map/ppermute | solution.py:562
  89.5 10.5 %collective-permute-start.22 = (bf16[1168,128]{1,0:T(8,128)(2,1)S(1)}, bf16[1168,128]{1,0:T(8,128)(2,1)S(1)}, u32[]{:S(2)}, u32[]{:S(2)}) collective-permute-start(bf16[1168,128]{1,0:T(8,128)(2,1)S(1)} %get-tuple-element.60), channel_id=1, source_target_pairs={{0,2},{2,0},{4,6},{6,4},{1,3},{3,1},{5,7},{7,5},{8,10},{10,8},{12,... | collective-permute-start | bytes 897032 | tf_op jit(solution)/shard_map/ppermute | solution.py:558
  100.0 16.3 %collective-permute-start.23 = (bf16[1168,128]{1,0:T(8,128)(2,1)S(1)}, bf16[1168,128]{1,0:T(8,128)(2,1)S(1)}, u32[]{:S(2)}, u32[]{:S(2)}) collective-permute-start(bf16[1168,128]{1,0:T(8,128)(2,1)S(1)} %shard_map.174), channel_id=1, source_target_pairs={{0,4},{2,6},{4,0},{6,2},{1,5},{3,7},{5,1},{7,3},{8,12},{10,14},{12... | collective-permute-start | bytes 897032 | tf_op jit(solution)/shard_map/ppermute | solution.py:558
  102.8 10.6 %collective-permute-start.24 = (bf16[576,128]{1,0:T(8,128)(2,1)S(1)}, bf16[576,128]{1,0:T(8,128)(2,1)S(1)}, u32[]{:S(2)}, u32[]{:S(2)}) collective-permute-start(bf16[576,128]{1,0:T(8,128)(2,1)S(1)} %get-tuple-element.61), channel_id=1, source_target_pairs={{0,2},{2,0},{4,6},{6,4},{1,3},{3,1},{5,7},{7,5},{8,10},{10,8},{12,... | collective-permute-start | bytes 442376 | tf_op jit(solution)/shard_map/ppermute | solution.py:558
  103.1 13.2 %collective-permute-start.25 = (bf16[592,128]{1,0:T(8,128)(2,1)S(1)}, bf16[592,128]{1,0:T(8,128)(2,1)S(1)}, u32[]{:S(2)}, u32[]{:S(2)}) collective-permute-start(bf16[592,128]{1,0:T(8,128)(2,1)S(1)} %get-tuple-element.62), channel_id=1, source_target_pairs={{0,2},{2,0},{4,6},{6,4},{1,3},{3,1},{5,7},{7,5},{8,10},{10,8},{12,... | collective-permute-start | bytes 454664 | tf_op jit(solution)/shard_map/ppermute | solution.py:558
  104.9 12.3 %copy-start.7 = (bf16[1,8,1536]{2,1,0:T(8,128)(2,1)}, bf16[1,8,1536]{2,1,0:T(8,128)(2,1)S(1)}, u32[]{:S(2)}) copy-start(bf16[1,8,1536]{2,1,0:T(8,128)(2,1)S(1)} %fusion.1) | copy-start | bytes 73732

commit v10 on v9

--- a/solution.py
+++ b/solution.py
@@ -48,7 +48,7 @@
     k_ref, v_ref, q_ref, w_ref, own_ref, *refs
 ):
     packed, refs = refs[:groups], refs[groups:]
-    msgs, (w_all, w_sems) = refs[:-2], refs[-2:]
+    msgs, (w_all, loaded, stage, w_sems, in_sems, out_sems) = refs[:-6], refs[-6:]
     size = own_ref.shape[2]
     rows = (own_ref.shape[1] - EXTRA) // (3 * heads + 1)
     width = heads * size
@@ -60,13 +60,10 @@
         part = pl.ds(i * block, block)
         copies.append(pltpu.make_async_copy(w_ref.at[part], w_all.at[part], w_sems.at[i]))
         copies[-1].start()
-    local = k_ref.shape[0]
-    for g, out in enumerate(packed):
-        for i, ref in enumerate((k_ref, v_ref, q_ref)):
-            for head in range(heads):
-                at = ((meta_ref[0] ^ g) * heads + head) * size
-                to = (i * heads + head) * local
-                out[to : to + local, :] = ref[:, pl.ds(pl.multiple_of(at, 128), size)]
+    loads = []
+    for i, ref in enumerate((k_ref, v_ref, q_ref)):
+        loads.append(pltpu.make_async_copy(ref, loaded.at[i], in_sems.at[i]))
+        loads[-1].start()
 
     def slot_at(row):
         z_at = (row % rows) // slot_local
@@ -89,6 +86,18 @@
     picked = jnp.dot(pick, states_ref[...], preferred_element_type=f32)
     scaled = (picked * gain_ref[...]).astype(bf16)
     tail = split_tail(jnp.sum(picked * picked, axis=1, keepdims=True), size)
+    for copy in loads:
+        copy.wait()
+    local = loaded.shape[1]
+    stores = []
+    for g in range(groups):
+        for i in range(3):
+            for head in range(heads):
+                at = ((meta_ref[0] ^ g) * heads + head) * size
+                to = (i * heads + head) * local
+                stage[g, to : to + local, :] = loaded[i, :, pl.ds(pl.multiple_of(at, 128), size)]
+        stores.append(pltpu.make_async_copy(stage.at[g], packed[g], out_sems.at[g]))
+        stores[-1].start()
     for copy in copies:
         copy.wait()
     for g in range(groups):
@@ -105,6 +114,8 @@
         own_ref[g, 3 * heads * rows : end, :] = tail[:rows]
         for j, msg in enumerate(msgs):
             msg[g, 3 * heads * rows :, :] = tail[(j + 1) * rows : (j + 2) * rows].astype(bf16)
+    for copy in stores:
+        copy.wait()
 
 
 def text_project(
@@ -121,9 +132,16 @@
     return pl.pallas_call(
         functools.partial(text_kernel, groups, heads, place_of),
         out_shape=shapes,
-        in_specs=[SMEM, SMEM] + [VMEM] * 8 + [ANY],
-        out_specs=[VMEM] * (groups + parts),
-        scratch_shapes=[pltpu.VMEM(text_proj.shape, bf16), pltpu.SemaphoreType.DMA((4,))],
+        in_specs=[SMEM, SMEM] + [VMEM] * 5 + [ANY] * 4,
+        out_specs=[VMEM] + [ANY] * groups + [VMEM] * (parts - 1),
+        scratch_shapes=[
+            pltpu.VMEM(text_proj.shape, bf16),
+            pltpu.VMEM((3,) + keys.shape, bf16),
+            pltpu.VMEM((groups, 3 * heads * keys.shape[0], size), bf16),
+            pltpu.SemaphoreType.DMA((4,)),
+            pltpu.SemaphoreType.DMA((3,)),
+            pltpu.SemaphoreType.DMA((groups,)),
+        ],
         compiler_params=params(60),
         cost_estimate=cost(
             2 * slots * depth * text_proj.shape[1], 2 * depth * text_proj.shape[1]
@@ -166,18 +184,20 @@
     )(own, *got)
 
 
-def block_kernel(features, heads, n_far, own_ref, got_ref, after_ref, *refs):
-    del after_ref
-    far, out_ref = refs[:n_far], refs[n_far]
-    kv_rows = far[0].shape[0] // 3 * 2
-    for k, ref in enumerate(far):
-        out_ref[k * kv_rows : (k + 1) * kv_rows, :] = ref[:kv_rows, :]
+def block_kernel(features, heads, n_pieces, own_ref, got_ref, *refs):
+    pieces, out_ref = refs[:n_pieces], refs[-1]
+    near_rows = pieces[0].shape[0]
+    kv_rows = near_rows // 3 * 2
+    out_ref[:near_rows, :] = pieces[0][...]
+    for k, ref in enumerate(pieces[1:]):
+        at = near_rows + k * kv_rows
+        out_ref[at : at + kv_rows, :] = ref[:kv_rows, :]
     size = own_ref.shape[2]
     text_rows = got_ref.shape[1]
     rows = text_rows // (3 * heads + 1)
     total = own_ref[0, :text_rows, :] + got_ref[0].astype(f32)
     rate = lax.rsqrt(joined(total[3 * heads * rows :]) / features + eps_norm)
-    start = n_far * kv_rows
+    start = near_rows + (n_pieces - 1) * kv_rows
     for i in range(3):
         for head in range(heads):
             at = (i * heads + head) * rows
@@ -192,30 +212,31 @@
     out_ref[start:, :] = jnp.broadcast_to(bias, (EXTRA, size)).astype(bf16)
 
 
-def block_of(own, got, after, far, features, heads):
+def block_of(own, got, after, pieces, features, heads):
     rows, size = own.shape[1:]
     total = (rows - EXTRA) // (3 * heads + 1) * 3 * heads + EXTRA
-    total += far[0].shape[0] // 3 * 2 * len(far)
-    return pl.pallas_call(
-        functools.partial(block_kernel, features, heads, len(far)),
+    total += pieces[0].shape[0] // 3 * (2 * len(pieces) + 1)
+    return pl.pallas_call(
+        functools.partial(block_kernel, features, heads, len(pieces)),
         out_shape=jax.ShapeDtypeStruct((total, size), bf16),
-        in_specs=[VMEM] * 2 + [ANY] + [VMEM] * len(far),
+        in_specs=[VMEM] * (2 + len(pieces)) + [ANY] * len(after),
         out_specs=VMEM,
         compiler_params=params(),
         cost_estimate=cost(0, 4 * total * size),
-    )(own, got, after, *far)
-
-
-def attention_kernel(n_pieces, n_cores, heads, rows, text_rows, *refs):
-    pieces, refs = refs[:n_pieces], refs[n_pieces:]
-    nears, refs = refs[: n_cores - 1], refs[n_cores - 1 :]
+    )(own, got, *pieces, *after)
+
+
+def attention_kernel(n_far, n_cores, heads, rows, text_rows, *refs):
+    far, refs = refs[:n_far], refs[n_far:]
     blocks, refs = refs[:n_cores], refs[n_cores:]
     out_refs, tout_ref = refs[:-1], refs[-1]
     size = blocks[0].shape[1]
     factor = size ** (-0.5) * math.log2(math.e)
     nt = (((1,), (1,)), ((), ()))
     kv_rows = 2 * heads * rows
-    text = (n_pieces - 1) * kv_rows
+    near_rows = 3 * heads * rows
+    starts = [0] + [near_rows + k * kv_rows for k in range(n_far)]
+    text = near_rows + n_far * kv_rows
     end = text + 3 * heads * text_rows
     bias = blocks[0][end : end + EXTRA, :][:1, : n_cores * text_rows].astype(f32)
 
@@ -226,10 +247,7 @@
         kv, tkv = [], []
         for i in range(2):
             at = (i * heads + head) * rows
-            image = [r[at : at + rows, :] for r in tuple(pieces) + tuple(nears)]
-            for b in blocks[1:]:
-                starts = [k * kv_rows + at for k in range(n_pieces - 1)]
-                image += [b[start : start + rows, :] for start in starts]
+            image = [b[start + at : start + at + rows, :] for b in blocks for start in starts]
             text_at = text + ((i + 1) * heads + head) * text_rows
             kv.append(jnp.concatenate(image, axis=0))
             tkv.append(jnp.concatenate([b[text_at : text_at + text_rows, :] for b in blocks], axis=0))
@@ -237,7 +255,7 @@
         tkeys, tvalues = tkv[0], with_ones(tkv[1])
         cols = slice(head * size, (head + 1) * size)
         q_at = (2 * heads + head) * rows
-        work = [(ref[q_at : q_at + rows, :], out) for ref, out in zip(pieces, out_refs)]
+        work = [(ref[q_at : q_at + rows, :], out) for ref, out in zip((blocks[0],) + tuple(far), out_refs)]
         tq_at = text + head * text_rows
         work.append((blocks[0][tq_at : tq_at + text_rows, :], tout_ref))
         for q, out_ref in work:
@@ -253,17 +271,17 @@
             out_ref[:, cols] = (acc[:, :size] / acc[:, size:]).astype(bf16)
 
 
-def attention(pieces, nears, blocks, heads, rows, text_rows):
+def attention(far, blocks, heads, rows, text_rows):
     size = blocks[0].shape[1]
-    n = len(pieces)
+    n = 1 + len(far)
     queries = n * rows + text_rows
     keys = len(blocks) * queries
     shapes = [jax.ShapeDtypeStruct((rows, heads * size), bf16)] * n
     shapes += [jax.ShapeDtypeStruct((text_rows, heads * size), bf16)]
     return pl.pallas_call(
-        functools.partial(attention_kernel, n, len(blocks), heads, rows, text_rows),
+        functools.partial(attention_kernel, len(far), len(blocks), heads, rows, text_rows),
         out_shape=shapes,
-        in_specs=[VMEM] * (n + len(nears) + len(blocks)),
+        in_specs=[VMEM] * (len(far) + len(blocks)),
         out_specs=[VMEM] * len(shapes),
         compiler_params=params(),
         cost_estimate=cost(
@@ -271,7 +289,7 @@
             4 * (queries + keys) * heads * size,
             queries * keys * heads,
         ),
-    )(*pieces, *nears, *blocks)
+    )(*far, *blocks)
 
 
 def assemble_kernel(groups, n_after, meta_ref, *refs):
@@ -428,9 +446,9 @@
     for ref in lefts:
         left += [ref[i].reshape(groups * rows, depth) for i in range(ref.shape[0])]
     left = jnp.concatenate(left, axis=1)
-    homes = [((outs[0], 0),), ((outs[1], 0), (outs[2], outs[1].shape[0]))]
-    homes += [((out, 0),) for out in outs[3:]]
     half = outs[1].shape[0]
+    homes = [((outs[0], 0),)]
+    homes += [((outs[2 * g - 1], 0), (outs[2 * g], half)) for g in range(1, groups)]
 
     def put(g, at, value):
         out, start = homes[g][-1] if at >= half else homes[g][0]
@@ -464,7 +482,9 @@
     depth = depth * len(pieces)
     full = width // size * rows + EXTRA
     half = width // size // 2 * rows
-    shapes = [(full, f32), (half, bf16), (full - half, bf16), (full, f32), (full, bf16)]
+    shapes = [(full, f32)]
+    for kind in (bf16, f32, bf16):
+        shapes += [(half, kind), (full - half, kind)]
     return pl.pallas_call(
         functools.partial(grad_kernel, len(lefts), len(pieces)),
         out_shape=[jax.ShapeDtypeStruct((n, size), kind) for n, kind in shapes],
@@ -479,10 +499,13 @@
 
 def pair_kernel(gate_width, own_ref, got_ref, out_ref):
     total = own_ref[...] + got_ref[...].astype(f32)
-    end = total.shape[0] - EXTRA
-    out_ref[:end, :] = total[:end].astype(bf16)
-    gate = joined_gate(total[end:], gate_width)
-    out_ref[end:, :] = split_gate(gate, total.shape[1]).astype(bf16)
+    if not gate_width:
+        out_ref[...] = total.astype(bf16)
+    else:
+        end = total.shape[0] - EXTRA
+        out_ref[:end, :] = total[:end].astype(bf16)
+        gate = joined_gate(total[end:], gate_width)
+        out_ref[end:, :] = split_gate(gate, total.shape[1]).astype(bf16)
 
 
 def pair_sum(own, got, gate_width):
@@ -496,33 +519,35 @@
     )(own, got)
 
 
-def final_kernel(own_ref, far_ref, low_ref, high_ref, out_ref, gate_ref):
+def final_kernel(own_ref, far_low, far_high, near_low, near_high, out_ref, gate_ref):
     size = own_ref.shape[1]
     rows = out_ref.shape[0]
-    half = low_ref.shape[0]
+    half = far_low.shape[0]
 
     def total(at, count):
-        ref, start = (high_ref, half) if at >= half else (low_ref, 0)
-        got = own_ref[at : at + count, :] + far_ref[at : at + count, :].astype(f32)
-        return got + ref[at - start : at - start + count, :].astype(f32)
+        refs, start = ((far_high, near_high), half) if at >= half else ((far_low, near_low), 0)
+        got = own_ref[at : at + count, :]
+        for ref in refs:
+            got = got + ref[at - start : at - start + count, :].astype(f32)
+        return got
 
     for i in range(out_ref.shape[1] // size):
         out_ref[:, i * size : (i + 1) * size] = total(i * rows, rows)
     gate_ref[...] = joined_gate(total(own_ref.shape[0] - EXTRA, EXTRA), gate_ref.shape[1])
 
 
-def final_sum(own, far, low, high, rows, width, gate_width):
+def final_sum(own, far, near, rows, width, gate_width):
     return pl.pallas_call(
         final_kernel,
         out_shape=[
             jax.ShapeDtypeStruct((rows, width), f32),
             jax.ShapeDtypeStruct((1, gate_width), f32),
         ],
-        in_specs=[VMEM] * 4,
+        in_specs=[VMEM] * 5,
         out_specs=[VMEM] * 2,
         compiler_params=params(),
         cost_estimate=cost(0, 8 * rows * width),
-    )(own, far, low, high)
+    )(own, *far, *near)
 
 
 def on_device(
@@ -585,8 +610,10 @@
         G, OC, place,
     )
     packed, sent = rest[:G], rest[G:]
-    images = [packed[0]] + [to_z(packed[k], k) for k in range(1, G)]
-    nears = [to_oc(packed[0], j) for j in range(1, OC)]
+    images = {0: packed[0]}
+    for k in order:
+        images[k] = to_z(packed[k], k)
+    images = [images[k] for k in range(G)]
     got = [to_oc(x, j + 1) for j, x in enumerate(sent)]
     own, sent = text_sum(own, got, text_rows)
     own, sent = text_sum(own, [to_z(sent, 1)], text_rows)
@@ -594,14 +621,15 @@
 
     gg = gated_parts(meta, gate, d_out[0], n_dp, G, OC, place)
     gg_dp = [gg[0], to_dp(gg[1], 1)]
-    block = block_of(own, got, gg_dp[1], images[1:], DT5, heads)
+    block = block_of(own, got, gg_dp[1:], images, DT5, heads)
     blocks = [block] + [to_oc(block, j) for j in range(1, OC)]
-    *outs, text_out = attention(images, nears, blocks, heads, image_local, text_rows)
-
-    back = []
-    for k in range(G):
+    *outs, text_out = attention(images[1:], blocks, heads, image_local, text_rows)
+
+    back = {}
+    for k in order + [0]:
         rows = jnp.concatenate([outs[k], part(text_out, z ^ k, slot_local, 0)], axis=0)
-        back.append(to_z(rows, k) if k else rows)
+        back[k] = to_z(rows, k) if k else rows
+    back = [back[k] for k in range(G)]
     gg_dp += [to_dp(gg[k], k) for k in range(2, n_dp)]
     lefts = [g[:1] for g in gg_dp]
     lefts += [to_oc(g, j + 1) for j, g in enumerate(gather_parts(gg_dp))]
@@ -620,11 +648,12 @@
         pieces += [to_oc(sent[j - 1], j)] + [to_oc(p, j) for p in pieces[1:n_dp]]
     R = model_width // (n_dp * n_seq)
     gate_width = model_width // n_seq
-    own, low, high, own_pair, far = grad_product(lefts, pieces, term)
-    pair = pair_sum(own_pair, to_z(far, 1), gate_width)
-    grad_wo, grad_gate = final_sum(
-        own, to_z(pair, 2), to_z(low, 1), to_z(high, 1), R, inner_width, gate_width
-    )
+    own, *blocks = grad_product(lefts, pieces, term)
+    got = [to_z(x, 1) for x in blocks[4:]]
+    pairs = [pair_sum(blocks[2], got[0], 0), pair_sum(blocks[3], got[1], gate_width)]
+    far = [to_z(x, 2) for x in pairs]
+    near = [to_z(x, 1) for x in blocks[:2]]
+    grad_wo, grad_gate = final_sum(own, far, near, R, inner_width, gate_width)
     return (image_out[None], text_attn[None], d_attn[None], grad_wo, grad_gate)
 
 

time: 118 us -> 118 us (level)
  waiting for transfers between devices: 55 us -> 52.9 us
  Pallas kernels: 22.4 us -> 24.2 us
    pallas_call x1, Pallas kernels: 1.39 us -> 3.11 us  [grad_product(): pl.pallas_call(functools.partial(grad_kernel, len(lefts), len(pieces)), o...]
    ppermute x8 -> x7, waiting for transfers between devices: 3.4 us -> 1.97 us  [to_oc(): return lax.ppermute(x, 'seq', perm)]
    ppermute x12 -> x14, starting transfers between devices: 21.5 us -> 22 us  [to_z(): return lax.ppermute(x, 'seq', perm)]
    ppermute x12 -> x14, waiting for transfers between devices: 46.4 us -> 46.2 us  [to_z(): return lax.ppermute(x, 'seq', perm)]
  transfers between devices with their start and end apart: 26 -> 27, of which waited for: 12 -> 13; matrix products, arithmetic and copies ran while one was open for 0% -> 0% of each run, Pallas kernels for 11% -> 12%
where the time goes in v10:
time: 118 us; the launch traced here: 117 us
  waiting for transfers between devices  52.9 us (45%)
  starting transfers between devices  31.7 us (27%)
  Pallas kernels  24.2 us (21%)
  local copies, waits for them, and re-layouts  5.9 us (5%)
  between operations  1.61 us (1%)
    ppermute x14, waiting for transfers between devices, to_z(): return lax.ppermute(x, 'seq', perm)  46.2 us
    ppermute x14, starting transfers between devices, to_z(): return lax.ppermute(x, 'seq', perm)  22 us
    ppermute x6, starting transfers between devices, to_dp(): return lax.ppermute(x, 'dp', [(a, a ^ k) for a in range(n_dp)])  8.01 us
    unnamed x18, local copies, waits for them, and re-layouts  5.77 us
    pallas_call x1, Pallas kernels, project(): pl.pallas_call(functools.partial(project_kernel, groups, parts, place_of)...  5.73 us
    pallas_call x1, Pallas kernels, text_project(): pl.pallas_call(functools.partial(text_kernel, groups, heads, place_of), o...  5.66 us
    pallas_call x1, Pallas kernels, attention(): pl.pallas_call(functools.partial(attention_kernel, len(far), len(blocks),...  5.15 us
    ppermute x6, waiting for transfers between devices, to_dp(): return lax.ppermute(x, 'dp', [(a, a ^ k) for a in range(n_dp)])  4.74 us
  transfers between devices with their start and end apart: 27, of which 13 were waited for; matrix products, arithmetic and copies ran while one was open for 0% of the time, Pallas kernels for 12%

profile of v10, /device:TPU:0, one launch (start us, length us, event | category | flops | bytes accessed | tf_op | source)
XLA Modules:
  0.0 117.2 jit_solution(10943537853948415419)
XLA Ops:
  1.4 0.6 pad_add_fusion.meta_ref
  2.0 5.7 %shard_map.164 = (f32[4,336,128]{2,1,0:T(8,128)}, bf16[1152,128]{1,0:T(8,128)(2,1)}, bf16[1152,128]{1,0:T(8,128)(2,1)}, bf16[1152,128]{1,0:T(8,128)(2,1)}, bf16[...) custom-call(s32[3]{0:T(128)} %pad_add_fusion.meta_ref, s32[1]{0:T(128)} %copy.22.len_ref, s32[1,64]{1,0:T(1,128)} %src_ref.1, ...), custom_call_target="tpu_custom_call" | custom-call | flops 301989888 | bytes 4718592 | tf_op jit(solution)/shard_map/pallas_call | solution.py:132
  7.6 0.5 collective-permute-start.3
  8.2 2.7 %collective-permute-start = (bf16[1152,128]{1,0:T(8,128)(2,1)}, bf16[1152,128]{1,0:T(8,128)(2,1)S(1)}, u32[]{:S(2)}, u32[]{:S(2)}) collective-permute-start(bf16[1152,128]{1,0:T(8,128)(2,1)} %get-tuple-element.37), channel_id=1, source_target_pairs={{0,2},{2,0},{4,6},{6,4},{1,3},{3,1},{5,7},{7,5},{8,10},{10,8},{12,... | collective-permute-start | bytes 884744 | tf_op jit(solution)/shard_map/ppermute | solution.py:583
  10.8 2.6 %collective-permute-start.1 = (bf16[1152,128]{1,0:T(8,128)(2,1)}, bf16[1152,128]{1,0:T(8,128)(2,1)S(1)}, u32[]{:S(2)}, u32[]{:S(2)}) collective-permute-start(bf16[1152,128]{1,0:T(8,128)(2,1)} %get-tuple-element.38), channel_id=1, source_target_pairs={{0,4},{2,6},{4,0},{6,2},{1,5},{3,7},{5,1},{7,3},{8,12},{10,14},{12... | collective-permute-start | bytes 884744 | tf_op jit(solution)/shard_map/ppermute | solution.py:583
  13.4 1.1 copy-done.2
  14.5 0.2 shard_map.165
  14.7 1.0 collective-permute-start.4
  15.6 2.3 %shard_map.167 = (bf16[2,4,96,128]{3,2,1,0:T(8,128)(2,1)}, bf16[2,4,96,128]{3,2,1,0:T(8,128)(2,1)}, bf16[2,4,96,128]{3,2,1,0:T(8,128)(2,1)}, bf16[2,4,96,128]{3,2,1,0:T(8,128)(2,1)}) custom-call(s32[3]{0:T(128)} %pad_add_fusion.meta_ref, f32[1,3072]{1,0:T(1,128)} %gate_ref.3, bf16[128,3072]{1,0:T(8,128)(2,1)} %bitcast.31), custom_call_target="tpu_custom_call" | custom-call | bytes 1572864 | tf_op jit(solution)/shard_map/pallas_call | solution.py:331
  18.0 1.5 %collective-permute-start.6 = (bf16[2,4,96,128]{3,2,1,0:T(8,128)(2,1)}, bf16[2,4,96,128]{3,2,1,0:T(8,128)(2,1)S(1)}, u32[]{:S(2)}, u32[]{:S(2)}) collective-permute-start(bf16[2,4,96,128]{3,2,1,0:T(8,128)(2,1)} %get-tuple-element.47), channel_id=1, source_target_pairs={{0,8},{8,0},{16,24},{24,16},{1,9},{9,1},{17,25},{25,17},{2,10},{10... | collective-permute-start | bytes 589832 | tf_op jit(solution)/shard_map/ppermute | solution.py:590
  19.4 15.3 %collective-permute-done.4.refs_0_ = bf16[2,320,128]{2,1,0:T(8,128)(2,1)S(1)} collective-permute-done((bf16[2,320,128]{2,1,0:T(8,128)(2,1)S(1)}, bf16[2,320,128]{2,1,0:T(8,128)(2,1)S(1)}, u32[]{:S(2)}, u32[]{:S(2)}) %collective-permute-start.4) | collective-permute-done | bytes 163872 | tf_op jit(solution)/shard_map/ppermute | solution.py:583
  34.8 0.2 shard_map.166
  34.9 2.9 %collective-permute-start.5 = (bf16[1,320,128]{2,1,0:T(8,128)(2,1)S(1)}, bf16[1,320,128]{2,1,0:T(8,128)(2,1)S(1)}, u32[]{:S(2)}, u32[]{:S(2)}) collective-permute-start(bf16[1,320,128]{2,1,0:T(8,128)(2,1)S(1)} %get-tuple-element.45), channel_id=1, source_target_pairs={{0,4},{2,6},{4,0},{6,2},{1,5},{3,7},{5,1},{7,3},{8,12},{10,14},{12... | collective-permute-start | bytes 245768 | tf_op jit(solution)/shard_map/ppermute | solution.py:583
  37.9 5.7 %collective-permute-done.5.got_ref = bf16[1,320,128]{2,1,0:T(8,128)(2,1)S(1)} collective-permute-done((bf16[1,320,128]{2,1,0:T(8,128)(2,1)S(1)}, bf16[1,320,128]{2,1,0:T(8,128)(2,1)S(1)}, u32[]{:S(2)}, u32[]{:S(2)}) %collective-permute-start.5) | collective-permute-done | bytes 81952 | tf_op jit(solution)/shard_map/ppermute | solution.py:583
  43.6 1.0 copy-done.4
  44.5 0.3 shard_map.168.refs_3_
  44.9 1.6 %collective-permute-start.11 = (bf16[2,4,96,128]{3,2,1,0:T(8,128)(2,1)}, bf16[2,4,96,128]{3,2,1,0:T(8,128)(2,1)S(1)}, u32[]{:S(2)}, u32[]{:S(2)}) collective-permute-start(bf16[2,4,96,128]{3,2,1,0:T(8,128)(2,1)} %get-tuple-element.53), channel_id=1, source_target_pairs={{0,16},{8,24},{16,0},{24,8},{1,17},{9,25},{17,1},{25,9},{2,18},{10... | collective-permute-start | bytes 589832 | tf_op jit(solution)/shard_map/ppermute | solution.py:590
  46.5 1.4 %collective-permute-start.12 = (bf16[2,4,96,128]{3,2,1,0:T(8,128)(2,1)}, bf16[2,4,96,128]{3,2,1,0:T(8,128)(2,1)S(1)}, u32[]{:S(2)}, u32[]{:S(2)}) collective-permute-start(bf16[2,4,96,128]{3,2,1,0:T(8,128)(2,1)} %get-tuple-element.54), channel_id=1, source_target_pairs={{0,24},{8,16},{16,8},{24,0},{1,25},{9,17},{17,9},{25,1},{2,26},{10... | collective-permute-start | bytes 589832 | tf_op jit(solution)/shard_map/ppermute | solution.py:590
  48.0 5.2 %shard_map.169 = (bf16[128,384]{1,0:T(8,128)(2,1)S(1)}, bf16[128,384]{1,0:T(8,128)(2,1)S(1)}, bf16[128,384]{1,0:T(8,128)(2,1)S(1)}, bf16[128,384]{1,0:T(8,128)(2,1)S(1)}, bf16[32,384]{1,0:T(8,128)(2,1)S(1)}) custom-call(bf16[1152,128]{1,0:T(8,128)(2,1)S(1)} %collective-permute-done.refs_1_.refs_0_, ...), custom_call_target="tpu_custom_call" | custom-call | flops 909115392 | bytes 2506752 | tf_op jit(solution)/shard_map/pallas_call | solution.py:281
  53.3 3.1 %collective-permute-start.9 = (bf16[136,384]{1,0:T(8,128)(2,1)S(1)}, bf16[136,384]{1,0:T(8,128)(2,1)S(1)}, u32[]{:S(2)}, u32[]{:S(2)}) collective-permute-start(bf16[136,384]{1,0:T(8,128)(2,1)S(1)} %pad_maximum_fusion.2), channel_id=1, source_target_pairs={{0,4},{2,6},{4,0},{6,2},{1,5},{3,7},{5,1},{7,3},{8,12},{10,14},{12... | collective-permute-start | bytes 313352 | tf_op jit(solution)/shard_map/ppermute | solution.py:583
  56.4 1.4 %collective-permute-start.10 = (bf16[136,384]{1,0:T(8,128)(2,1)S(1)}, bf16[136,384]{1,0:T(8,128)(2,1)S(1)}, u32[]{:S(2)}, u32[]{:S(2)}) collective-permute-start(bf16[136,384]{1,0:T(8,128)(2,1)S(1)} %pad_maximum_fusion.3), channel_id=1, source_target_pairs={{0,6},{2,4},{4,2},{6,0},{1,7},{3,5},{5,3},{7,1},{8,14},{10,12},{12... | collective-permute-start | bytes 313352 | tf_op jit(solution)/shard_map/ppermute | solution.py:583
  57.9 1.5 %collective-permute-done.8.refs_1_ = bf16[136,384]{1,0:T(8,128)(2,1)S(1)} collective-permute-done((bf16[136,384]{1,0:T(8,128)(2,1)S(1)}, bf16[136,384]{1,0:T(8,128)(2,1)S(1)}, u32[]{:S(2)}, u32[]{:S(2)}) %collective-permute-start.8) | collective-permute-done | bytes 104480 | tf_op jit(solution)/shard_map/ppermute | solution.py:583
  59.4 5.2 %collective-permute-done.9.refs_2_ = bf16[136,384]{1,0:T(8,128)(2,1)S(1)} collective-permute-done((bf16[136,384]{1,0:T(8,128)(2,1)S(1)}, bf16[136,384]{1,0:T(8,128)(2,1)S(1)}, u32[]{:S(2)}, u32[]{:S(2)}) %collective-permute-start.9) | collective-permute-done | bytes 104480 | tf_op jit(solution)/shard_map/ppermute | solution.py:583
  64.6 0.6 shard_map.170.attn_ref.refs_5_
  65.2 2.1 %collective-permute-start.16 = (bf16[128,1536]{1,0:T(8,128)(2,1)S(1)}, bf16[128,1536]{1,0:T(8,128)(2,1)}, u32[]{:S(2)}, u32[]{:S(2)}) collective-permute-start(bf16[128,1536]{1,0:T(8,128)(2,1)S(1)} %shard_map.170.attn_ref.refs_5_), channel_id=1, source_target_pairs={{0,24},{8,16},{16,8},{24,0},{1,25},{9,17},{17,9},{25,1},{2,26},{10... | collective-permute-start | bytes 1179656 | tf_op jit(solution)/shard_map/ppermute | solution.py:590
  67.3 0.5 collective-permute-start.15
  67.8 1.0 collective-permute-start.14
  68.8 3.7 %copy-done = bf16[3072,1536]{1,0:T(8,128)(2,1)S(1)} copy-done((bf16[3072,1536]{1,0:T(8,128)(2,1)S(1)}, bf16[3072,1536]{1,0:T(8,128)(2,1)}, u32[]{:S(2)}) %copy-start) | copy-done | bytes 9437208
  72.5 5.7 %shard_map.171 = (bf16[128,3072]{1,0:T(8,128)(2,1)}, bf16[128,1536]{1,0:T(8,128)(2,1)}, f32[4,384]{1,0:T(4,128)S(1)}, bf16[144,1536]{1,0:T(8,128)(2,1)S(1)}) custom-call(s32[3]{0:T(128)S(1)} %copy-done.6, bf16[128,1536]{1,0:T(8,128)(2,1)S(1)} %shard_map.170.attn_ref.refs_5_, bf16[3072,1536]{1,0:T(8,128)(2,1)S(1)} %copy-done, f32[1,3072]{1,0:T(1,128)S(1)} %copy-done.5, ...), custom_call_target="tpu_custom_call" | custom-call | flops 2415919104 | bytes 9437184 | tf_op jit(solution)/shard_map/pallas_call | solution.py:412
  78.2 0.6 collective-permute-start.13
  78.8 0.1 collective-permute-start.20
  78.9 4.6 %collective-permute-done.15.refs_7_ = bf16[128,1536]{1,0:T(8,128)(2,1)} collective-permute-done((bf16[128,1536]{1,0:T(8,128)(2,1)S(1)}, bf16[128,1536]{1,0:T(8,128)(2,1)}, u32[]{:S(2)}, u32[]{:S(2)}) %collective-permute-start.15) | collective-permute-done | bytes 393248 | tf_op jit(solution)/shard_map/ppermute | solution.py:590
  83.6 0.4 collective-permute-start.18
  84.1 0.1 fusion.5
  84.2 1.4 %collective-permute-done.19.refs_11_ = bf16[128,1536]{1,0:T(8,128)(2,1)} collective-permute-done((bf16[128,1536]{1,0:T(8,128)(2,1)}, bf16[128,1536]{1,0:T(8,128)(2,1)}, u32[]{:S(2)}, u32[]{:S(2)}) %collective-permute-start.19) | collective-permute-done | bytes 393248 | tf_op jit(solution)/shard_map/ppermute | solution.py:587
  85.6 0.6 collective-permute-done.18.refs_10_
  86.2 3.1 %shard_map.173 = (f32[1168,128]{1,0:T(8,128)S(1)}, bf16[576,128]{1,0:T(8,128)(2,1)S(1)}, bf16[592,128]{1,0:T(8,128)(2,1)S(1)}, f32[576,128]{1,0:T(8,128)S(1)}, f...) custom-call(bf16[1,4,96,128]{3,2,1,0:T(8,128)(2,1)S(1)} %slice.24.refs_0_, ...), custom_call_target="tpu_custom_call" | custom-call | flops 1207959552 | bytes 5111808 | tf_op jit(solution)/shard_map/pallas_call | solution.py:488
  89.3 3.1 %collective-permute-start.21 = (bf16[576,128]{1,0:T(8,128)(2,1)S(1)}, bf16[576,128]{1,0:T(8,128)(2,1)S(1)}, u32[]{:S(2)}, u32[]{:S(2)}) collective-permute-start(bf16[576,128]{1,0:T(8,128)(2,1)S(1)} %get-tuple-element.62), channel_id=1, source_target_pairs={{0,2},{2,0},{4,6},{6,4},{1,3},{3,1},{5,7},{7,5},{8,10},{10,8},{12,... | collective-permute-start | bytes 442376 | tf_op jit(solution)/shard_map/ppermute | solution.py:583
  92.4 0.1 collective-permute-start.23
  92.5 1.9 %collective-permute-start.25 = (bf16[576,128]{1,0:T(8,128)(2,1)S(1)}, bf16[576,128]{1,0:T(8,128)(2,1)S(1)}, u32[]{:S(2)}, u32[]{:S(2)}) collective-permute-start(bf16[576,128]{1,0:T(8,128)(2,1)S(1)} %get-tuple-element.65), channel_id=1, source_target_pairs={{0,2},{2,0},{4,6},{6,4},{1,3},{3,1},{5,7},{7,5},{8,10},{10,8},{12,... | collective-permute-start | bytes 442376 | tf_op jit(solution)/shard_map/ppermute | solution.py:583
  94.6 2.5 %collective-permute-done.21.got_ref = bf16[576,128]{1,0:T(8,128)(2,1)S(1)} collective-permute-done((bf16[576,128]{1,0:T(8,128)(2,1)S(1)}, bf16[576,128]{1,0:T(8,128)(2,1)S(1)}, u32[]{:S(2)}, u32[]{:S(2)}) %collective-permute-start.21) | collective-permute-done | bytes 147488 | tf_op jit(solution)/shard_map/ppermute | solution.py:583
  97.0 3.0 %collective-permute-start.22 = (bf16[576,128]{1,0:T(8,128)(2,1)S(1)}, bf16[576,128]{1,0:T(8,128)(2,1)S(1)}, u32[]{:S(2)}, u32[]{:S(2)}) collective-permute-start(bf16[576,128]{1,0:T(8,128)(2,1)S(1)} %shard_map.174), channel_id=1, source_target_pairs={{0,4},{2,6},{4,0},{6,2},{1,5},{3,7},{5,1},{7,3},{8,12},{10,14},{12... | collective-permute-start | bytes 442376 | tf_op jit(solution)/shard_map/ppermute | solution.py:583
  100.1 5.0 %collective-permute-done.23.got_ref = bf16[592,128]{1,0:T(8,128)(2,1)S(1)} collective-permute-done((bf16[592,128]{1,0:T(8,128)(2,1)S(1)}, bf16[592,128]{1,0:T(8,128)(2,1)S(1)}, u32[]{:S(2)}, u32[]{:S(2)}) %collective-permute-start.23) | collective-permute-done | bytes 151584 | tf_op jit(solution)/shard_map/ppermute | solution.py:583
  105.2 0.1 fusion.1
  105.3 2.9 %collective-permute-done.25.near_low = bf16[576,128]{1,0:T(8,128)(2,1)S(1)} collective-permute-done((bf16[576,128]{1,0:T(8,128)(2,1)S(1)}, bf16[576,128]{1,0:T(8,128)(2,1)S(1)}, u32[]{:S(2)}, u32[]{:S(2)}) %collective-permute-start.25) | collective-permute-done | bytes 147488 | tf_op jit(solution)/shard_map/ppermute | solution.py:583
  108.2 2.9 %collective-permute-done.26.near_high = bf16[592,128]{1,0:T(8,128)(2,1)S(1)} collective-permute-done((bf16[592,128]{1,0:T(8,128)(2,1)S(1)}, bf16[592,128]{1,0:T(8,128)(2,1)S(1)}, u32[]{:S(2)}, u32[]{:S(2)}) %collective-permute-start.26) | collective-permute-done | bytes 151584 | tf_op jit(solution)/shard_map/ppermute | solution.py:583
  111.1 5.2 %collective-permute-done.24.far_high = bf16[592,128]{1,0:T(8,128)(2,1)S(1)} collective-permute-done((bf16[592,128]{1,0:T(8,128)(2,1)S(1)}, bf16[592,128]{1,0:T(8,128)(2,1)S(1)}, u32[]{:S(2)}, u32[]{:S(2)}) %collective-permute-start.24) | collective-permute-done | bytes 151584 | tf_op jit(solution)/shard_map/ppermute | solution.py:583
  116.3 0.9 shard_map.176
  (54 shorter events, 0.9 us)
Async XLA Ops:
  0.6 47.2 %copy-start.8 = (s32[1,64]{1,0:T(1,128)S(1)}, s32[1,64]{1,0:T(1,128)}, u32[]{:S(2)}) copy-start(s32[1,64]{1,0:T(1,128)} %src_ref.1) | copy-start | bytes 772
  0.6 68.1 %copy-start.5 = (f32[1,3072]{1,0:T(1,128)S(1)}, f32[1,3072]{1,0:T(1,128)}, u32[]{:S(2)}) copy-start(f32[1,3072]{1,0:T(1,128)} %gate_ref.3) | copy-start | bytes 36868
  0.7 68.1 %copy-start.1 = (bf16[1,128,3072]{2,1,0:T(8,128)(2,1)S(1)}, bf16[1,128,3072]{2,1,0:T(8,128)(2,1)}, u32[]{:S(2)}) copy-start(bf16[1,128,3072]{2,1,0:T(8,128)(2,1)} %param.25) | copy-start | bytes 2359300
  2.0 62.7 %copy-start.6 = (s32[3]{0:T(128)S(1)}, s32[3]{0:T(128)}, u32[]{:S(2)}) copy-start(s32[3]{0:T(128)} %pad_add_fusion.meta_ref) | copy-start | bytes 40
  7.6 5.8 %collective-permute-start.3 = (bf16[4,320,128]{2,1,0:T(8,128)(2,1)}, bf16[4,320,128]{2,1,0:T(8,128)(2,1)S(1)}, u32[]{:S(2)}, u32[]{:S(2)}) collective-permute-start(bf16[4,320,128]{2,1,0:T(8,128)(2,1)} %get-tuple-element.41), channel_id=1, source_target_pairs={{0,1},{2,3},{4,5},{6,7},{1,0},{3,2},{5,4},{7,6},{8,9},{10,11},{12,... | collective-permute-start | bytes 983048 | tf_op jit(solution)/shard_map/ppermute | solution.py:587
  8.2 29.7 %collective-permute-start = (bf16[1152,128]{1,0:T(8,128)(2,1)}, bf16[1152,128]{1,0:T(8,128)(2,1)S(1)}, u32[]{:S(2)}, u32[]{:S(2)}) collective-permute-start(bf16[1152,128]{1,0:T(8,128)(2,1)} %get-tuple-element.37), channel_id=1, source_target_pairs={{0,2},{2,0},{4,6},{6,4},{1,3},{3,1},{5,7},{7,5},{8,10},{10,8},{12,... | collective-permute-start | bytes 884744 | tf_op jit(solution)/shard_map/ppermute | solution.py:583
  10.8 27.1 %collective-permute-start.1 = (bf16[1152,128]{1,0:T(8,128)(2,1)}, bf16[1152,128]{1,0:T(8,128)(2,1)S(1)}, u32[]{:S(2)}, u32[]{:S(2)}) collective-permute-start(bf16[1152,128]{1,0:T(8,128)(2,1)} %get-tuple-element.38), channel_id=1, source_target_pairs={{0,4},{2,6},{4,0},{6,2},{1,5},{3,7},{5,1},{7,3},{8,12},{10,14},{12... | collective-permute-start | bytes 884744 | tf_op jit(solution)/shard_map/ppermute | solution.py:583
  13.4 24.5 %collective-permute-start.2 = (bf16[1152,128]{1,0:T(8,128)(2,1)}, bf16[1152,128]{1,0:T(8,128)(2,1)S(1)}, u32[]{:S(2)}, u32[]{:S(2)}) collective-permute-start(bf16[1152,128]{1,0:T(8,128)(2,1)} %get-tuple-element.39), channel_id=1, source_target_pairs={{0,6},{2,4},{4,2},{6,0},{1,7},{3,5},{5,3},{7,1},{8,14},{10,12},{12... | collective-permute-start | bytes 884744 | tf_op jit(solution)/shard_map/ppermute | solution.py:583
  13.4 1.1 copy-start.2
  14.7 20.1 %collective-permute-start.4 = (bf16[2,320,128]{2,1,0:T(8,128)(2,1)S(1)}, bf16[2,320,128]{2,1,0:T(8,128)(2,1)S(1)}, u32[]{:S(2)}, u32[]{:S(2)}) collective-permute-start(bf16[2,320,128]{2,1,0:T(8,128)(2,1)S(1)} %get-tuple-element.43), channel_id=1, source_target_pairs={{0,2},{2,0},{4,6},{6,4},{1,3},{3,1},{5,7},{7,5},{8,10},{10,8},{12,... | collective-permute-start | bytes 491528 | tf_op jit(solution)/shard_map/ppermute | solution.py:583
  18.0 19.9 %collective-permute-start.6 = (bf16[2,4,96,128]{3,2,1,0:T(8,128)(2,1)}, bf16[2,4,96,128]{3,2,1,0:T(8,128)(2,1)S(1)}, u32[]{:S(2)}, u32[]{:S(2)}) collective-permute-start(bf16[2,4,96,128]{3,2,1,0:T(8,128)(2,1)} %get-tuple-element.47), channel_id=1, source_target_pairs={{0,8},{8,0},{16,24},{24,16},{1,9},{9,1},{17,25},{25,17},{2,10},{10... | collective-permute-start | bytes 589832 | tf_op jit(solution)/shard_map/ppermute | solution.py:590
  34.9 8.6 %collective-permute-start.5 = (bf16[1,320,128]{2,1,0:T(8,128)(2,1)S(1)}, bf16[1,320,128]{2,1,0:T(8,128)(2,1)S(1)}, u32[]{:S(2)}, u32[]{:S(2)}) collective-permute-start(bf16[1,320,128]{2,1,0:T(8,128)(2,1)S(1)} %get-tuple-element.45), channel_id=1, source_target_pairs={{0,4},{2,6},{4,0},{6,2},{1,5},{3,7},{5,1},{7,3},{8,12},{10,14},{12... | collective-permute-start | bytes 245768 | tf_op jit(solution)/shard_map/ppermute | solution.py:583
  43.6 1.0 copy-start.4
  44.5 33.7 %copy-start.3 = (bf16[2,4,96,128]{3,2,1,0:T(8,128)(2,1)S(1)}, bf16[2,4,96,128]{3,2,1,0:T(8,128)(2,1)}, u32[]{:S(2)}) copy-start(bf16[2,4,96,128]{3,2,1,0:T(8,128)(2,1)} %get-tuple-element.57.refs_0_) | copy-start | bytes 589828
  44.8 3.2 %collective-permute-start.7 = (bf16[3760,128]{1,0:T(8,128)(2,1)S(1)}, bf16[3760,128]{1,0:T(8,128)(2,1)}, u32[]{:S(2)}, u32[]{:S(2)}) collective-permute-start(bf16[3760,128]{1,0:T(8,128)(2,1)S(1)} %shard_map.168.refs_3_), channel_id=1, source_target_pairs={{0,1},{2,3},{4,5},{6,7},{1,0},{3,2},{5,4},{7,6},{8,9},{10,11},{12,... | collective-permute-start | bytes 2887688 | tf_op jit(solution)/shard_map/ppermute | solution.py:587
  44.9 13.0 %collective-permute-start.11 = (bf16[2,4,96,128]{3,2,1,0:T(8,128)(2,1)}, bf16[2,4,96,128]{3,2,1,0:T(8,128)(2,1)S(1)}, u32[]{:S(2)}, u32[]{:S(2)}) collective-permute-start(bf16[2,4,96,128]{3,2,1,0:T(8,128)(2,1)} %get-tuple-element.53), channel_id=1, source_target_pairs={{0,16},{8,24},{16,0},{24,8},{1,17},{9,25},{17,1},{25,9},{2,18},{10... | collective-permute-start | bytes 589832 | tf_op jit(solution)/shard_map/ppermute | solution.py:590
  46.5 11.4 %collective-permute-start.12 = (bf16[2,4,96,128]{3,2,1,0:T(8,128)(2,1)}, bf16[2,4,96,128]{3,2,1,0:T(8,128)(2,1)S(1)}, u32[]{:S(2)}, u32[]{:S(2)}) collective-permute-start(bf16[2,4,96,128]{3,2,1,0:T(8,128)(2,1)} %get-tuple-element.54), channel_id=1, source_target_pairs={{0,24},{8,16},{16,8},{24,0},{1,25},{9,17},{17,9},{25,1},{2,26},{10... | collective-permute-start | bytes 589832 | tf_op jit(solution)/shard_map/ppermute | solution.py:590
  53.2 6.3 %collective-permute-start.8 = (bf16[136,384]{1,0:T(8,128)(2,1)S(1)}, bf16[136,384]{1,0:T(8,128)(2,1)S(1)}, u32[]{:S(2)}, u32[]{:S(2)}) collective-permute-start(bf16[136,384]{1,0:T(8,128)(2,1)S(1)} %pad_maximum_fusion.1), channel_id=1, source_target_pairs={{0,2},{2,0},{4,6},{6,4},{1,3},{3,1},{5,7},{7,5},{8,10},{10,8},{12,... | collective-permute-start | bytes 313352 | tf_op jit(solution)/shard_map/ppermute | solution.py:583
  53.3 11.4 %collective-permute-start.9 = (bf16[136,384]{1,0:T(8,128)(2,1)S(1)}, bf16[136,384]{1,0:T(8,128)(2,1)S(1)}, u32[]{:S(2)}, u32[]{:S(2)}) collective-permute-start(bf16[136,384]{1,0:T(8,128)(2,1)S(1)} %pad_maximum_fusion.2), channel_id=1, source_target_pairs={{0,4},{2,6},{4,0},{6,2},{1,5},{3,7},{5,1},{7,3},{8,12},{10,14},{12... | collective-permute-start | bytes 313352 | tf_op jit(solution)/shard_map/ppermute | solution.py:583
  56.4 8.3 %collective-permute-start.10 = (bf16[136,384]{1,0:T(8,128)(2,1)S(1)}, bf16[136,384]{1,0:T(8,128)(2,1)S(1)}, u32[]{:S(2)}, u32[]{:S(2)}) collective-permute-start(bf16[136,384]{1,0:T(8,128)(2,1)S(1)} %pad_maximum_fusion.3), channel_id=1, source_target_pairs={{0,6},{2,4},{4,2},{6,0},{1,7},{3,5},{5,3},{7,1},{8,14},{10,12},{12... | collective-permute-start | bytes 313352 | tf_op jit(solution)/shard_map/ppermute | solution.py:583
  65.2 13.6 %collective-permute-start.16 = (bf16[128,1536]{1,0:T(8,128)(2,1)S(1)}, bf16[128,1536]{1,0:T(8,128)(2,1)}, u32[]{:S(2)}, u32[]{:S(2)}) collective-permute-start(bf16[128,1536]{1,0:T(8,128)(2,1)S(1)} %shard_map.170.attn_ref.refs_5_), channel_id=1, source_target_pairs={{0,24},{8,16},{16,8},{24,0},{1,25},{9,17},{17,9},{25,1},{2,26},{10... | collective-permute-start | bytes 1179656 | tf_op jit(solution)/shard_map/ppermute | solution.py:590
  67.3 16.2 %collective-permute-start.15 = (bf16[128,1536]{1,0:T(8,128)(2,1)S(1)}, bf16[128,1536]{1,0:T(8,128)(2,1)}, u32[]{:S(2)}, u32[]{:S(2)}) collective-permute-start(bf16[128,1536]{1,0:T(8,128)(2,1)S(1)} %shard_map.170.attn_ref.refs_5_), channel_id=1, source_target_pairs={{0,16},{8,24},{16,0},{24,8},{1,17},{9,25},{17,1},{25,9},{2,18},{10... | collective-permute-start | bytes 1179656 | tf_op jit(solution)/shard_map/ppermute | solution.py:590
  67.8 15.8 %collective-permute-start.14 = (bf16[128,1536]{1,0:T(8,128)(2,1)S(1)}, bf16[128,1536]{1,0:T(8,128)(2,1)}, u32[]{:S(2)}, u32[]{:S(2)}) collective-permute-start(bf16[128,1536]{1,0:T(8,128)(2,1)S(1)} %shard_map.170.attn_ref.refs_5_), channel_id=1, source_target_pairs={{0,8},{8,0},{16,24},{24,16},{1,9},{9,1},{17,25},{25,17},{2,10},{10... | collective-permute-start | bytes 1179656 | tf_op jit(solution)/shard_map/ppermute | solution.py:590
  68.8 3.7 %copy-start = (bf16[3072,1536]{1,0:T(8,128)(2,1)S(1)}, bf16[3072,1536]{1,0:T(8,128)(2,1)}, u32[]{:S(2)}) copy-start(bf16[3072,1536]{1,0:T(8,128)(2,1)} %w_ref.3) | copy-start | bytes 28311556
  78.2 6.0 %collective-permute-start.17 = (bf16[144,1536]{1,0:T(8,128)(2,1)S(1)}, bf16[144,1536]{1,0:T(8,128)(2,1)S(1)}, u32[]{:S(2)}, u32[]{:S(2)}) collective-permute-start(bf16[144,1536]{1,0:T(8,128)(2,1)S(1)} %get-tuple-element.58), channel_id=1, source_target_pairs={{0,1},{2,3},{4,5},{6,7},{1,0},{3,2},{5,4},{7,6},{8,9},{10,11},{12,... | collective-permute-start | bytes 1327112 | tf_op jit(solution)/shard_map/ppermute | solution.py:587
  78.2 6.0 %collective-permute-start.13 = (bf16[4,4,96,128]{3,2,1,0:T(8,128)(2,1)S(1)}, bf16[4,4,96,128]{3,2,1,0:T(8,128)(2,1)}, u32[]{:S(2)}, u32[]{:S(2)}) collective-permute-start(bf16[4,4,96,128]{3,2,1,0:T(8,128)(2,1)S(1)} %shard_map.172), channel_id=1, source_target_pairs={{0,1},{2,3},{4,5},{6,7},{1,0},{3,2},{5,4},{7,6},{8,9},{10,11},{12,... | collective-permute-start | bytes 1179656 | tf_op jit(solution)/shard_map/ppermute | solution.py:587
  78.8 5.4 %collective-permute-start.20 = (bf16[128,1536]{1,0:T(8,128)(2,1)}, bf16[128,1536]{1,0:T(8,128)(2,1)}, u32[]{:S(2)}, u32[]{:S(2)}) collective-permute-start(bf16[128,1536]{1,0:T(8,128)(2,1)} %collective-permute-done.16.refs_8_), channel_id=1, source_target_pairs={{0,1},{2,3},{4,5},{6,7},{1,0},{3,2},{5,4},{7,6},{8,9},{10,11},{12,... | collective-permute-start | bytes 1179656 | tf_op jit(solution)/shard_map/ppermute | solution.py:587
  83.6 2.1 %collective-permute-start.19 = (bf16[128,1536]{1,0:T(8,128)(2,1)}, bf16[128,1536]{1,0:T(8,128)(2,1)}, u32[]{:S(2)}, u32[]{:S(2)}) collective-permute-start(bf16[128,1536]{1,0:T(8,128)(2,1)} %collective-permute-done.15.refs_7_), channel_id=1, source_target_pairs={{0,1},{2,3},{4,5},{6,7},{1,0},{3,2},{5,4},{7,6},{8,9},{10,11},{12,... | collective-permute-start | bytes 1179656 | tf_op jit(solution)/shard_map/ppermute | solution.py:587
  83.6 2.5 %collective-permute-start.18 = (bf16[128,1536]{1,0:T(8,128)(2,1)}, bf16[128,1536]{1,0:T(8,128)(2,1)}, u32[]{:S(2)}, u32[]{:S(2)}) collective-permute-start(bf16[128,1536]{1,0:T(8,128)(2,1)} %collective-permute-done.14.refs_6_), channel_id=1, source_target_pairs={{0,1},{2,3},{4,5},{6,7},{1,0},{3,2},{5,4},{7,6},{8,9},{10,11},{12,... | collective-permute-start | bytes 1179656 | tf_op jit(solution)/shard_map/ppermute | solution.py:587
  89.3 7.7 %collective-permute-start.21 = (bf16[576,128]{1,0:T(8,128)(2,1)S(1)}, bf16[576,128]{1,0:T(8,128)(2,1)S(1)}, u32[]{:S(2)}, u32[]{:S(2)}) collective-permute-start(bf16[576,128]{1,0:T(8,128)(2,1)S(1)} %get-tuple-element.62), channel_id=1, source_target_pairs={{0,2},{2,0},{4,6},{6,4},{1,3},{3,1},{5,7},{7,5},{8,10},{10,8},{12,... | collective-permute-start | bytes 442376 | tf_op jit(solution)/shard_map/ppermute | solution.py:583
  92.4 12.7 %collective-permute-start.23 = (bf16[592,128]{1,0:T(8,128)(2,1)S(1)}, bf16[592,128]{1,0:T(8,128)(2,1)S(1)}, u32[]{:S(2)}, u32[]{:S(2)}) collective-permute-start(bf16[592,128]{1,0:T(8,128)(2,1)S(1)} %get-tuple-element.64), channel_id=1, source_target_pairs={{0,2},{2,0},{4,6},{6,4},{1,3},{3,1},{5,7},{7,5},{8,10},{10,8},{12,... | collective-permute-start | bytes 454664 | tf_op jit(solution)/shard_map/ppermute | solution.py:583
  92.5 15.7 %collective-permute-start.25 = (bf16[576,128]{1,0:T(8,128)(2,1)S(1)}, bf16[576,128]{1,0:T(8,128)(2,1)S(1)}, u32[]{:S(2)}, u32[]{:S(2)}) collective-permute-start(bf16[576,128]{1,0:T(8,128)(2,1)S(1)} %get-tuple-element.65), channel_id=1, source_target_pairs={{0,2},{2,0},{4,6},{6,4},{1,3},{3,1},{5,7},{7,5},{8,10},{10,8},{12,... | collective-permute-start | bytes 442376 | tf_op jit(solution)/shard_map/ppermute | solution.py:583
  94.5 16.6 %collective-permute-start.26 = (bf16[592,128]{1,0:T(8,128)(2,1)S(1)}, bf16[592,128]{1,0:T(8,128)(2,1)S(1)}, u32[]{:S(2)}, u32[]{:S(2)}) collective-permute-start(bf16[592,128]{1,0:T(8,128)(2,1)S(1)} %get-tuple-element.66), channel_id=1, source_target_pairs={{0,2},{2,0},{4,6},{6,4},{1,3},{3,1},{5,7},{7,5},{8,10},{10,8},{12,... | collective-permute-start | bytes 454664 | tf_op jit(solution)/shard_map/ppermute | solution.py:583
  97.0 14.0 %collective-permute-start.22 = (bf16[576,128]{1,0:T(8,128)(2,1)S(1)}, bf16[576,128]{1,0:T(8,128)(2,1)S(1)}, u32[]{:S(2)}, u32[]{:S(2)}) collective-permute-start(bf16[576,128]{1,0:T(8,128)(2,1)S(1)} %shard_map.174), channel_id=1, source_target_pairs={{0,4},{2,6},{4,0},{6,2},{1,5},{3,7},{5,1},{7,3},{8,12},{10,14},{12... | collective-permute-start | bytes 442376 | tf_op jit(solution)/shard_map/ppermute | solution.py:583
  105.1 11.2 %collective-permute-start.24 = (bf16[592,128]{1,0:T(8,128)(2,1)S(1)}, bf16[592,128]{1,0:T(8,128)(2,1)S(1)}, u32[]{:S(2)}, u32[]{:S(2)}) collective-permute-start(bf16[592,128]{1,0:T(8,128)(2,1)S(1)} %shard_map.175), channel_id=1, source_target_pairs={{0,4},{2,6},{4,0},{6,2},{1,5},{3,7},{5,1},{7,3},{8,12},{10,14},{12... | collective-permute-start | bytes 454664 | tf_op jit(solution)/shard_map/ppermute | solution.py:583
  105.2 12.0 %copy-start.7 = (bf16[1,8,1536]{2,1,0:T(8,128)(2,1)}, bf16[1,8,1536]{2,1,0:T(8,128)(2,1)S(1)}, u32[]{:S(2)}) copy-start(bf16[1,8,1536]{2,1,0:T(8,128)(2,1)S(1)} %fusion.1) | copy-start | bytes 73732

commit v11 on v10

--- a/solution.py
+++ b/solution.py
@@ -22,7 +22,7 @@
 ANY = pl.BlockSpec(memory_space=pl.ANY)
 
 
-def params(mib=24):
+def params(mib=16):
     return pltpu.CompilerParams(vmem_limit_bytes=int(mib * 1024 * 1024))
 
 
@@ -292,18 +292,18 @@
     )(*far, *blocks)
 
 
-def assemble_kernel(groups, n_after, meta_ref, *refs):
-    pieces, out_ref = refs[:groups], refs[groups + n_after]
+def assemble_kernel(places, meta_ref, *refs):
+    pieces, out_ref = refs[: len(places)], refs[-1]
     rows, width = out_ref.shape[0], pieces[0].shape[1]
-    for k, piece in enumerate(pieces):
+    for k, piece in zip(places, pieces):
         at = pl.multiple_of((meta_ref[0] ^ k) * width, 128)
         out_ref[:, pl.ds(at, width)] = piece[:rows, :]
 
 
-def assemble(meta, pieces, after, rows):
+def assemble(meta, pieces, places, after, rows):
     groups, width = len(pieces), pieces[0].shape[1]
     return pl.pallas_call(
-        functools.partial(assemble_kernel, groups, len(after)),
+        functools.partial(assemble_kernel, tuple(places)),
         out_shape=jax.ShapeDtypeStruct((rows, groups * width), bf16),
         in_specs=[SMEM] + [VMEM] * groups + [ANY] * len(after),
         out_specs=VMEM,
@@ -497,7 +497,10 @@
     )(*lefts, *pieces, term)
 
 
-def pair_kernel(gate_width, own_ref, got_ref, out_ref):
+def pair_kernel(gate_width, n_through, own_ref, got_ref, *refs):
+    out_ref = refs[n_through]
+    for ref, out in zip(refs[:n_through], refs[n_through + 1 :]):
+        out[...] = ref[...]
     total = own_ref[...] + got_ref[...].astype(f32)
     if not gate_width:
         out_ref[...] = total.astype(bf16)
@@ -508,15 +511,15 @@
         out_ref[end:, :] = split_gate(gate, total.shape[1]).astype(bf16)
 
 
-def pair_sum(own, got, gate_width):
-    return pl.pallas_call(
-        functools.partial(pair_kernel, gate_width),
-        out_shape=jax.ShapeDtypeStruct(got.shape, bf16),
-        in_specs=[VMEM] * 2,
-        out_specs=VMEM,
+def pair_sum(own, got, gate_width, through):
+    return pl.pallas_call(
+        functools.partial(pair_kernel, gate_width, len(through)),
+        out_shape=[jax.ShapeDtypeStruct(x.shape, bf16) for x in [got] + through],
+        in_specs=[VMEM] * (2 + len(through)),
+        out_specs=[VMEM] * (1 + len(through)),
         compiler_params=params(),
         cost_estimate=cost(0, 8 * own.size),
-    )(own, got)
+    )(own, got, *through)
 
 
 def final_kernel(own_ref, far_low, far_high, near_low, near_high, out_ref, gate_ref):
@@ -613,7 +616,7 @@
     images = {0: packed[0]}
     for k in order:
         images[k] = to_z(packed[k], k)
-    images = [images[k] for k in range(G)]
+    images = [images[k] for k in [0] + order]
     got = [to_oc(x, j + 1) for j, x in enumerate(sent)]
     own, sent = text_sum(own, got, text_rows)
     own, sent = text_sum(own, [to_z(sent, 1)], text_rows)
@@ -624,20 +627,21 @@
     block = block_of(own, got, gg_dp[1:], images, DT5, heads)
     blocks = [block] + [to_oc(block, j) for j in range(1, OC)]
     *outs, text_out = attention(images[1:], blocks, heads, image_local, text_rows)
+    outs = dict(zip([0] + order, outs))
 
     back = {}
     for k in order + [0]:
         rows = jnp.concatenate([outs[k], part(text_out, z ^ k, slot_local, 0)], axis=0)
         back[k] = to_z(rows, k) if k else rows
-    back = [back[k] for k in range(G)]
+    back = [back[k] for k in order + [0]]
     gg_dp += [to_dp(gg[k], k) for k in range(2, n_dp)]
     lefts = [g[:1] for g in gg_dp]
     lefts += [to_oc(g, j + 1) for j, g in enumerate(gather_parts(gg_dp))]
-    image_attn = assemble(meta, back, gg_dp[1:], image_local)
+    image_attn = assemble(meta, back, order + [0], gg_dp[1:], image_local)
     text_attn = jnp.zeros((slot_local, inner_width), bf16)
     own_usable = part(slot_source[0] < caption_len[0], seq, slot_local, 0)
-    for k in range(G):
-        rows = jnp.where(own_usable[:, None], back[k][image_local:], jnp.zeros((), bf16))
+    for k, got in zip(order + [0], back):
+        rows = jnp.where(own_usable[:, None], got[image_local:], jnp.zeros((), bf16))
         text_attn = lax.dynamic_update_slice_in_dim(text_attn, rows, (z ^ k) * gw, 1)
 
     pieces = [image_attn] + [to_dp(image_attn, k) for k in range(1, n_dp)]
@@ -650,9 +654,10 @@
     gate_width = model_width // n_seq
     own, *blocks = grad_product(lefts, pieces, term)
     got = [to_z(x, 1) for x in blocks[4:]]
-    pairs = [pair_sum(blocks[2], got[0], 0), pair_sum(blocks[3], got[1], gate_width)]
-    far = [to_z(x, 2) for x in pairs]
-    near = [to_z(x, 1) for x in blocks[:2]]
+    (low,) = pair_sum(blocks[2], got[0], 0, [])
+    high, *near = pair_sum(blocks[3], got[1], gate_width, blocks[:2])
+    far = [to_z(x, 2) for x in (low, high)]
+    near = [to_z(x, 1) for x in near]
     grad_wo, grad_gate = final_sum(own, far, near, R, inner_width, gate_width)
     return (image_out[None], text_attn[None], d_attn[None], grad_wo, grad_gate)
 

time: 118 us -> 113 us (0.958)
  starting transfers between devices: 31.7 us -> 29.5 us
  Pallas kernels: 24.2 us -> 22.4 us
    ppermute x14, starting transfers between devices: 22 us -> 19.6 us  [to_z(): return lax.ppermute(x, 'seq', perm)]
    ppermute x14, waiting for transfers between devices: 46.2 us -> 44.4 us  [to_z(): return lax.ppermute(x, 'seq', perm)]
    pallas_call x1, Pallas kernels: 3.11 us -> 1.39 us  [grad_product(): pl.pallas_call(functools.partial(grad_kernel, len(lefts), len(pieces)), o...]
    ppermute x6, waiting for transfers between devices: 4.74 us -> 6.18 us  [to_dp(): return lax.ppermute(x, 'dp', [(a, a ^ k) for a in range(n_dp)])]
  transfers between devices with their start and end apart: 27 -> 27, of which waited for: 13 -> 11; matrix products, arithmetic and copies ran while one was open for 0% -> 0% of each run, Pallas kernels for 12% -> 12%
where the time goes in v11:
time: 113 us
  waiting for transfers between devices  52.3 us (46%)
  starting transfers between devices  29.5 us (26%)
  Pallas kernels  22.4 us (20%)
  local copies, waits for them, and re-layouts  5.9 us (5%)
  between operations  1.62 us (1%)
    ppermute x14, waiting for transfers between devices, to_z(): return lax.ppermute(x, 'seq', perm)  44.4 us
    ppermute x14, starting transfers between devices, to_z(): return lax.ppermute(x, 'seq', perm)  19.6 us
    ppermute x6, starting transfers between devices, to_dp(): return lax.ppermute(x, 'dp', [(a, a ^ k) for a in range(n_dp)])  8.14 us
    ppermute x6, waiting for transfers between devices, to_dp(): return lax.ppermute(x, 'dp', [(a, a ^ k) for a in range(n_dp)])  6.18 us
    unnamed x18, local copies, waits for them, and re-layouts  5.77 us
    pallas_call x1, Pallas kernels, project(): pl.pallas_call(functools.partial(project_kernel, groups, parts, place_of)...  5.7 us
    pallas_call x1, Pallas kernels, text_project(): pl.pallas_call(functools.partial(text_kernel, groups, heads, place_of), o...  5.66 us
    pallas_call x1, Pallas kernels, attention(): pl.pallas_call(functools.partial(attention_kernel, len(far), len(blocks),...  5.15 us
  transfers between devices with their start and end apart: 27, of which 11 were waited for; matrix products, arithmetic and copies ran while one was open for 0% of the time, Pallas kernels for 12%

profile of v11, /device:TPU:0, one launch (start us, length us, event | category | flops | bytes accessed | tf_op | source)
XLA Modules:
  0.0 112.6 jit_solution(11439696809949641813)
XLA Ops:
  1.4 0.6 pad_add_fusion.meta_ref
  2.0 5.7 %shard_map.164 = (f32[4,336,128]{2,1,0:T(8,128)}, bf16[1152,128]{1,0:T(8,128)(2,1)}, bf16[1152,128]{1,0:T(8,128)(2,1)}, bf16[1152,128]{1,0:T(8,128)(2,1)}, bf16[...) custom-call(s32[3]{0:T(128)} %pad_add_fusion.meta_ref, s32[1]{0:T(128)} %copy.22.len_ref, s32[1,64]{1,0:T(1,128)} %src_ref.1, ...), custom_call_target="tpu_custom_call" | custom-call | flops 301989888 | bytes 4718592 | tf_op jit(solution)/shard_map/pallas_call | solution.py:132
  7.7 0.5 collective-permute-start.3
  8.2 3.7 %collective-permute-start = (bf16[1152,128]{1,0:T(8,128)(2,1)}, bf16[1152,128]{1,0:T(8,128)(2,1)S(1)}, u32[]{:S(2)}, u32[]{:S(2)}) collective-permute-start(bf16[1152,128]{1,0:T(8,128)(2,1)} %get-tuple-element.40), channel_id=1, source_target_pairs={{0,4},{2,6},{4,0},{6,2},{1,5},{3,7},{5,1},{7,3},{8,12},{10,14},{12... | collective-permute-start | bytes 884744 | tf_op jit(solution)/shard_map/ppermute | solution.py:586
  11.9 1.3 %collective-permute-start.1 = (bf16[1152,128]{1,0:T(8,128)(2,1)}, bf16[1152,128]{1,0:T(8,128)(2,1)S(1)}, u32[]{:S(2)}, u32[]{:S(2)}) collective-permute-start(bf16[1152,128]{1,0:T(8,128)(2,1)} %get-tuple-element.41), channel_id=1, source_target_pairs={{0,6},{2,4},{4,2},{6,0},{1,7},{3,5},{5,3},{7,1},{8,14},{10,12},{12... | collective-permute-start | bytes 884744 | tf_op jit(solution)/shard_map/ppermute | solution.py:586
  13.2 0.2 collective-permute-start.2
  13.5 1.1 copy-done.2
  14.5 0.2 shard_map.165
  14.7 1.9 %collective-permute-start.4 = (bf16[2,320,128]{2,1,0:T(8,128)(2,1)S(1)}, bf16[2,320,128]{2,1,0:T(8,128)(2,1)S(1)}, u32[]{:S(2)}, u32[]{:S(2)}) collective-permute-start(bf16[2,320,128]{2,1,0:T(8,128)(2,1)S(1)} %get-tuple-element.46), channel_id=1, source_target_pairs={{0,2},{2,0},{4,6},{6,4},{1,3},{3,1},{5,7},{7,5},{8,10},{10,8},{12,... | collective-permute-start | bytes 491528 | tf_op jit(solution)/shard_map/ppermute | solution.py:586
  16.6 2.3 %shard_map.167 = (bf16[2,4,96,128]{3,2,1,0:T(8,128)(2,1)}, bf16[2,4,96,128]{3,2,1,0:T(8,128)(2,1)}, bf16[2,4,96,128]{3,2,1,0:T(8,128)(2,1)}, bf16[2,4,96,128]{3,2,1,0:T(8,128)(2,1)}) custom-call(s32[3]{0:T(128)} %pad_add_fusion.meta_ref, f32[1,3072]{1,0:T(1,128)} %gate_ref.3, bf16[128,3072]{1,0:T(8,128)(2,1)} %bitcast.31), custom_call_target="tpu_custom_call" | custom-call | bytes 1572864 | tf_op jit(solution)/shard_map/pallas_call | solution.py:331
  18.9 1.5 %collective-permute-start.6 = (bf16[2,4,96,128]{3,2,1,0:T(8,128)(2,1)}, bf16[2,4,96,128]{3,2,1,0:T(8,128)(2,1)S(1)}, u32[]{:S(2)}, u32[]{:S(2)}) collective-permute-start(bf16[2,4,96,128]{3,2,1,0:T(8,128)(2,1)} %get-tuple-element.50), channel_id=1, source_target_pairs={{0,8},{8,0},{16,24},{24,16},{1,9},{9,1},{17,25},{25,17},{2,10},{10... | collective-permute-start | bytes 589832 | tf_op jit(solution)/shard_map/ppermute | solution.py:593
  20.4 16.8 %collective-permute-done.4.refs_0_ = bf16[2,320,128]{2,1,0:T(8,128)(2,1)S(1)} collective-permute-done((bf16[2,320,128]{2,1,0:T(8,128)(2,1)S(1)}, bf16[2,320,128]{2,1,0:T(8,128)(2,1)S(1)}, u32[]{:S(2)}, u32[]{:S(2)}) %collective-permute-start.4) | collective-permute-done | bytes 163872 | tf_op jit(solution)/shard_map/ppermute | solution.py:586
  37.2 0.2 shard_map.166
  37.4 1.7 %collective-permute-start.5 = (bf16[1,320,128]{2,1,0:T(8,128)(2,1)S(1)}, bf16[1,320,128]{2,1,0:T(8,128)(2,1)S(1)}, u32[]{:S(2)}, u32[]{:S(2)}) collective-permute-start(bf16[1,320,128]{2,1,0:T(8,128)(2,1)S(1)} %get-tuple-element.48), channel_id=1, source_target_pairs={{0,4},{2,6},{4,0},{6,2},{1,5},{3,7},{5,1},{7,3},{8,12},{10,14},{12... | collective-permute-start | bytes 245768 | tf_op jit(solution)/shard_map/ppermute | solution.py:586
  39.1 4.6 %collective-permute-done.5.got_ref = bf16[1,320,128]{2,1,0:T(8,128)(2,1)S(1)} collective-permute-done((bf16[1,320,128]{2,1,0:T(8,128)(2,1)S(1)}, bf16[1,320,128]{2,1,0:T(8,128)(2,1)S(1)}, u32[]{:S(2)}, u32[]{:S(2)}) %collective-permute-start.5) | collective-permute-done | bytes 81952 | tf_op jit(solution)/shard_map/ppermute | solution.py:586
  43.6 1.0 copy-done.4
  44.6 0.3 shard_map.168.refs_3_
  45.0 1.7 %collective-permute-start.11 = (bf16[2,4,96,128]{3,2,1,0:T(8,128)(2,1)}, bf16[2,4,96,128]{3,2,1,0:T(8,128)(2,1)S(1)}, u32[]{:S(2)}, u32[]{:S(2)}) collective-permute-start(bf16[2,4,96,128]{3,2,1,0:T(8,128)(2,1)} %get-tuple-element.56), channel_id=1, source_target_pairs={{0,16},{8,24},{16,0},{24,8},{1,17},{9,25},{17,1},{25,9},{2,18},{10... | collective-permute-start | bytes 589832 | tf_op jit(solution)/shard_map/ppermute | solution.py:593
  46.6 1.4 %collective-permute-start.12 = (bf16[2,4,96,128]{3,2,1,0:T(8,128)(2,1)}, bf16[2,4,96,128]{3,2,1,0:T(8,128)(2,1)S(1)}, u32[]{:S(2)}, u32[]{:S(2)}) collective-permute-start(bf16[2,4,96,128]{3,2,1,0:T(8,128)(2,1)} %get-tuple-element.57), channel_id=1, source_target_pairs={{0,24},{8,16},{16,8},{24,0},{1,25},{9,17},{17,9},{25,1},{2,26},{10... | collective-permute-start | bytes 589832 | tf_op jit(solution)/shard_map/ppermute | solution.py:593
  48.1 5.2 %shard_map.169 = (bf16[128,384]{1,0:T(8,128)(2,1)S(1)}, bf16[128,384]{1,0:T(8,128)(2,1)S(1)}, bf16[128,384]{1,0:T(8,128)(2,1)S(1)}, bf16[128,384]{1,0:T(8,128)(2,1)S(1)}, bf16[32,384]{1,0:T(8,128)(2,1)S(1)}) custom-call(bf16[1152,128]{1,0:T(8,128)(2,1)S(1)} %collective-permute-done.refs_1_.refs_0_, ...), custom_call_target="tpu_custom_call" | custom-call | flops 909115392 | bytes 2506752 | tf_op jit(solution)/shard_map/pallas_call | solution.py:281
  53.3 0.8 collective-permute-start.8
  54.1 2.1 %collective-permute-start.9 = (bf16[136,384]{1,0:T(8,128)(2,1)S(1)}, bf16[136,384]{1,0:T(8,128)(2,1)S(1)}, u32[]{:S(2)}, u32[]{:S(2)}) collective-permute-start(bf16[136,384]{1,0:T(8,128)(2,1)S(1)} %pad_maximum_fusion.1), channel_id=1, source_target_pairs={{0,6},{2,4},{4,2},{6,0},{1,7},{3,5},{5,3},{7,1},{8,14},{10,12},{12... | collective-permute-start | bytes 313352 | tf_op jit(solution)/shard_map/ppermute | solution.py:586
  56.2 0.8 collective-permute-start.10
  57.0 6.6 %collective-permute-done.8.refs_0_ = bf16[136,384]{1,0:T(8,128)(2,1)S(1)} collective-permute-done((bf16[136,384]{1,0:T(8,128)(2,1)S(1)}, bf16[136,384]{1,0:T(8,128)(2,1)S(1)}, u32[]{:S(2)}, u32[]{:S(2)}) %collective-permute-start.8) | collective-permute-done | bytes 104480 | tf_op jit(solution)/shard_map/ppermute | solution.py:586
  63.6 0.1 fusion.5
  63.8 1.2 %collective-permute-done.10.refs_2_ = bf16[136,384]{1,0:T(8,128)(2,1)S(1)} collective-permute-done((bf16[136,384]{1,0:T(8,128)(2,1)S(1)}, bf16[136,384]{1,0:T(8,128)(2,1)S(1)}, u32[]{:S(2)}, u32[]{:S(2)}) %collective-permute-start.10) | collective-permute-done | bytes 104480 | tf_op jit(solution)/shard_map/ppermute | solution.py:586
  65.2 0.6 shard_map.170.attn_ref.refs_5_
  65.7 2.4 %collective-permute-start.16 = (bf16[128,1536]{1,0:T(8,128)(2,1)S(1)}, bf16[128,1536]{1,0:T(8,128)(2,1)S(1)}, u32[]{:S(2)}, u32[]{:S(2)}) collective-permute-start(bf16[128,1536]{1,0:T(8,128)(2,1)S(1)} %shard_map.170.attn_ref.refs_5_), channel_id=1, source_target_pairs={{0,24},{8,16},{16,8},{24,0},{1,25},{9,17},{17,9},{25,1},{2,26},{10... | collective-permute-start | bytes 1179656 | tf_op jit(solution)/shard_map/ppermute | solution.py:593
  68.1 0.5 collective-permute-start.15
  68.6 0.7 collective-permute-start.14
  69.3 3.7 %copy-done = bf16[3072,1536]{1,0:T(8,128)(2,1)S(1)} copy-done((bf16[3072,1536]{1,0:T(8,128)(2,1)S(1)}, bf16[3072,1536]{1,0:T(8,128)(2,1)}, u32[]{:S(2)}) %copy-start) | copy-done | bytes 9437208
  73.0 5.7 %shard_map.171 = (bf16[128,3072]{1,0:T(8,128)(2,1)}, bf16[128,1536]{1,0:T(8,128)(2,1)}, f32[4,384]{1,0:T(4,128)S(1)}, bf16[144,1536]{1,0:T(8,128)(2,1)S(1)}) custom-call(s32[3]{0:T(128)S(1)} %copy-done.6, bf16[128,1536]{1,0:T(8,128)(2,1)S(1)} %shard_map.170.attn_ref.refs_5_, bf16[3072,1536]{1,0:T(8,128)(2,1)S(1)} %copy-done, f32[1,3072]{1,0:T(1,128)S(1)} %copy-done.5, ...), custom_call_target="tpu_custom_call" | custom-call | flops 2415919104 | bytes 9437184 | tf_op jit(solution)/shard_map/pallas_call | solution.py:412
  78.7 0.6 collective-permute-start.13
  79.3 0.1 collective-permute-start.20
  79.4 6.1 %collective-permute-done.15.refs_7_ = bf16[128,1536]{1,0:T(8,128)(2,1)S(1)} collective-permute-done((bf16[128,1536]{1,0:T(8,128)(2,1)S(1)}, bf16[128,1536]{1,0:T(8,128)(2,1)S(1)}, u32[]{:S(2)}, u32[]{:S(2)}) %collective-permute-start.15) | collective-permute-done | bytes 393248 | tf_op jit(solution)/shard_map/ppermute | solution.py:593
  85.5 0.1 collective-permute-done.14.refs_6_
  85.6 0.4 collective-permute-start.18
  86.1 1.1 collective-permute-done.19.refs_11_
  87.2 0.6 collective-permute-done.18.refs_10_
  87.8 1.4 %shard_map.173 = (f32[1168,128]{1,0:T(8,128)S(1)}, bf16[576,128]{1,0:T(8,128)(2,1)S(1)}, bf16[592,128]{1,0:T(8,128)(2,1)S(1)}, f32[576,128]{1,0:T(8,128)S(1)}, f...) custom-call(bf16[1,4,96,128]{3,2,1,0:T(8,128)(2,1)S(1)} %slice.24.refs_0_, ...), custom_call_target="tpu_custom_call" | custom-call | flops 1207959552 | bytes 5111808 | tf_op jit(solution)/shard_map/pallas_call | solution.py:488
  89.2 2.2 %collective-permute-start.23 = (bf16[592,128]{1,0:T(8,128)(2,1)S(1)}, bf16[592,128]{1,0:T(8,128)(2,1)S(1)}, u32[]{:S(2)}, u32[]{:S(2)}) collective-permute-start(bf16[592,128]{1,0:T(8,128)(2,1)S(1)} %get-tuple-element.67), channel_id=1, source_target_pairs={{0,2},{2,0},{4,6},{6,4},{1,3},{3,1},{5,7},{7,5},{8,10},{10,8},{12,... | collective-permute-start | bytes 454664 | tf_op jit(solution)/shard_map/ppermute | solution.py:586
  91.4 4.6 %collective-permute-done.23.got_ref = bf16[592,128]{1,0:T(8,128)(2,1)S(1)} collective-permute-done((bf16[592,128]{1,0:T(8,128)(2,1)S(1)}, bf16[592,128]{1,0:T(8,128)(2,1)S(1)}, u32[]{:S(2)}, u32[]{:S(2)}) %collective-permute-start.23) | collective-permute-done | bytes 151584 | tf_op jit(solution)/shard_map/ppermute | solution.py:586
  96.2 2.2 %collective-permute-start.24 = (bf16[592,128]{1,0:T(8,128)(2,1)S(1)}, bf16[592,128]{1,0:T(8,128)(2,1)S(1)}, u32[]{:S(2)}, u32[]{:S(2)}) collective-permute-start(bf16[592,128]{1,0:T(8,128)(2,1)S(1)} %get-tuple-element.70), channel_id=1, source_target_pairs={{0,4},{2,6},{4,0},{6,2},{1,5},{3,7},{5,1},{7,3},{8,12},{10,14},{12... | collective-permute-start | bytes 454664 | tf_op jit(solution)/shard_map/ppermute | solution.py:586
  98.4 0.4 collective-permute-done.21.got_ref
  98.9 2.5 %collective-permute-start.22 = (bf16[576,128]{1,0:T(8,128)(2,1)S(1)}, bf16[576,128]{1,0:T(8,128)(2,1)S(1)}, u32[]{:S(2)}, u32[]{:S(2)}) collective-permute-start(bf16[576,128]{1,0:T(8,128)(2,1)S(1)} %shard_map.174), channel_id=1, source_target_pairs={{0,4},{2,6},{4,0},{6,2},{1,5},{3,7},{5,1},{7,3},{8,12},{10,14},{12... | collective-permute-start | bytes 442376 | tf_op jit(solution)/shard_map/ppermute | solution.py:586
  101.3 0.2 collective-permute-start.25
  101.5 10.2 %collective-permute-done.22.far_low = bf16[576,128]{1,0:T(8,128)(2,1)S(1)} collective-permute-done((bf16[576,128]{1,0:T(8,128)(2,1)S(1)}, bf16[576,128]{1,0:T(8,128)(2,1)S(1)}, u32[]{:S(2)}, u32[]{:S(2)}) %collective-permute-start.22) | collective-permute-done | bytes 147488 | tf_op jit(solution)/shard_map/ppermute | solution.py:586
  111.7 0.9 shard_map.176
  (54 shorter events, 0.8 us)
Async XLA Ops:
  0.6 47.4 %copy-start.8 = (s32[1,64]{1,0:T(1,128)S(1)}, s32[1,64]{1,0:T(1,128)}, u32[]{:S(2)}) copy-start(s32[1,64]{1,0:T(1,128)} %src_ref.1) | copy-start | bytes 772
  0.6 68.7 %copy-start.5 = (f32[1,3072]{1,0:T(1,128)S(1)}, f32[1,3072]{1,0:T(1,128)}, u32[]{:S(2)}) copy-start(f32[1,3072]{1,0:T(1,128)} %gate_ref.3) | copy-start | bytes 36868
  0.7 68.6 %copy-start.1 = (bf16[1,128,3072]{2,1,0:T(8,128)(2,1)S(1)}, bf16[1,128,3072]{2,1,0:T(8,128)(2,1)}, u32[]{:S(2)}) copy-start(bf16[1,128,3072]{2,1,0:T(8,128)(2,1)} %param.25) | copy-start | bytes 2359300
  2.0 63.1 %copy-start.6 = (s32[3]{0:T(128)S(1)}, s32[3]{0:T(128)}, u32[]{:S(2)}) copy-start(s32[3]{0:T(128)} %pad_add_fusion.meta_ref) | copy-start | bytes 40
  7.7 5.8 %collective-permute-start.3 = (bf16[4,320,128]{2,1,0:T(8,128)(2,1)}, bf16[4,320,128]{2,1,0:T(8,128)(2,1)S(1)}, u32[]{:S(2)}, u32[]{:S(2)}) collective-permute-start(bf16[4,320,128]{2,1,0:T(8,128)(2,1)} %get-tuple-element.44), channel_id=1, source_target_pairs={{0,1},{2,3},{4,5},{6,7},{1,0},{3,2},{5,4},{7,6},{8,9},{10,11},{12,... | collective-permute-start | bytes 983048 | tf_op jit(solution)/shard_map/ppermute | solution.py:590
  8.2 30.9 %collective-permute-start = (bf16[1152,128]{1,0:T(8,128)(2,1)}, bf16[1152,128]{1,0:T(8,128)(2,1)S(1)}, u32[]{:S(2)}, u32[]{:S(2)}) collective-permute-start(bf16[1152,128]{1,0:T(8,128)(2,1)} %get-tuple-element.40), channel_id=1, source_target_pairs={{0,4},{2,6},{4,0},{6,2},{1,5},{3,7},{5,1},{7,3},{8,12},{10,14},{12... | collective-permute-start | bytes 884744 | tf_op jit(solution)/shard_map/ppermute | solution.py:586
  11.9 27.2 %collective-permute-start.1 = (bf16[1152,128]{1,0:T(8,128)(2,1)}, bf16[1152,128]{1,0:T(8,128)(2,1)S(1)}, u32[]{:S(2)}, u32[]{:S(2)}) collective-permute-start(bf16[1152,128]{1,0:T(8,128)(2,1)} %get-tuple-element.41), channel_id=1, source_target_pairs={{0,6},{2,4},{4,2},{6,0},{1,7},{3,5},{5,3},{7,1},{8,14},{10,12},{12... | collective-permute-start | bytes 884744 | tf_op jit(solution)/shard_map/ppermute | solution.py:586
  13.2 25.9 %collective-permute-start.2 = (bf16[1152,128]{1,0:T(8,128)(2,1)}, bf16[1152,128]{1,0:T(8,128)(2,1)S(1)}, u32[]{:S(2)}, u32[]{:S(2)}) collective-permute-start(bf16[1152,128]{1,0:T(8,128)(2,1)} %get-tuple-element.42), channel_id=1, source_target_pairs={{0,2},{2,0},{4,6},{6,4},{1,3},{3,1},{5,7},{7,5},{8,10},{10,8},{12,... | collective-permute-start | bytes 884744 | tf_op jit(solution)/shard_map/ppermute | solution.py:586
  13.4 1.1 copy-start.2
  14.7 22.5 %collective-permute-start.4 = (bf16[2,320,128]{2,1,0:T(8,128)(2,1)S(1)}, bf16[2,320,128]{2,1,0:T(8,128)(2,1)S(1)}, u32[]{:S(2)}, u32[]{:S(2)}) collective-permute-start(bf16[2,320,128]{2,1,0:T(8,128)(2,1)S(1)} %get-tuple-element.46), channel_id=1, source_target_pairs={{0,2},{2,0},{4,6},{6,4},{1,3},{3,1},{5,7},{7,5},{8,10},{10,8},{12,... | collective-permute-start | bytes 491528 | tf_op jit(solution)/shard_map/ppermute | solution.py:586
  18.9 20.2 %collective-permute-start.6 = (bf16[2,4,96,128]{3,2,1,0:T(8,128)(2,1)}, bf16[2,4,96,128]{3,2,1,0:T(8,128)(2,1)S(1)}, u32[]{:S(2)}, u32[]{:S(2)}) collective-permute-start(bf16[2,4,96,128]{3,2,1,0:T(8,128)(2,1)} %get-tuple-element.50), channel_id=1, source_target_pairs={{0,8},{8,0},{16,24},{24,16},{1,9},{9,1},{17,25},{25,17},{2,10},{10... | collective-permute-start | bytes 589832 | tf_op jit(solution)/shard_map/ppermute | solution.py:593
  37.4 6.3 %collective-permute-start.5 = (bf16[1,320,128]{2,1,0:T(8,128)(2,1)S(1)}, bf16[1,320,128]{2,1,0:T(8,128)(2,1)S(1)}, u32[]{:S(2)}, u32[]{:S(2)}) collective-permute-start(bf16[1,320,128]{2,1,0:T(8,128)(2,1)S(1)} %get-tuple-element.48), channel_id=1, source_target_pairs={{0,4},{2,6},{4,0},{6,2},{1,5},{3,7},{5,1},{7,3},{8,12},{10,14},{12... | collective-permute-start | bytes 245768 | tf_op jit(solution)/shard_map/ppermute | solution.py:586
  43.6 1.0 copy-start.4
  44.6 34.1 %copy-start.3 = (bf16[2,4,96,128]{3,2,1,0:T(8,128)(2,1)S(1)}, bf16[2,4,96,128]{3,2,1,0:T(8,128)(2,1)}, u32[]{:S(2)}) copy-start(bf16[2,4,96,128]{3,2,1,0:T(8,128)(2,1)} %get-tuple-element.60.refs_0_) | copy-start | bytes 589828
  44.9 3.3 %collective-permute-start.7 = (bf16[3760,128]{1,0:T(8,128)(2,1)S(1)}, bf16[3760,128]{1,0:T(8,128)(2,1)}, u32[]{:S(2)}, u32[]{:S(2)}) collective-permute-start(bf16[3760,128]{1,0:T(8,128)(2,1)S(1)} %shard_map.168.refs_3_), channel_id=1, source_target_pairs={{0,1},{2,3},{4,5},{6,7},{1,0},{3,2},{5,4},{7,6},{8,9},{10,11},{12,... | collective-permute-start | bytes 2887688 | tf_op jit(solution)/shard_map/ppermute | solution.py:590
  45.0 20.2 %collective-permute-start.11 = (bf16[2,4,96,128]{3,2,1,0:T(8,128)(2,1)}, bf16[2,4,96,128]{3,2,1,0:T(8,128)(2,1)S(1)}, u32[]{:S(2)}, u32[]{:S(2)}) collective-permute-start(bf16[2,4,96,128]{3,2,1,0:T(8,128)(2,1)} %get-tuple-element.56), channel_id=1, source_target_pairs={{0,16},{8,24},{16,0},{24,8},{1,17},{9,25},{17,1},{25,9},{2,18},{10... | collective-permute-start | bytes 589832 | tf_op jit(solution)/shard_map/ppermute | solution.py:593
  46.6 18.5 %collective-permute-start.12 = (bf16[2,4,96,128]{3,2,1,0:T(8,128)(2,1)}, bf16[2,4,96,128]{3,2,1,0:T(8,128)(2,1)S(1)}, u32[]{:S(2)}, u32[]{:S(2)}) collective-permute-start(bf16[2,4,96,128]{3,2,1,0:T(8,128)(2,1)} %get-tuple-element.57), channel_id=1, source_target_pairs={{0,24},{8,16},{16,8},{24,0},{1,25},{9,17},{17,9},{25,1},{2,26},{10... | collective-permute-start | bytes 589832 | tf_op jit(solution)/shard_map/ppermute | solution.py:593
  53.3 10.3 %collective-permute-start.8 = (bf16[136,384]{1,0:T(8,128)(2,1)S(1)}, bf16[136,384]{1,0:T(8,128)(2,1)S(1)}, u32[]{:S(2)}, u32[]{:S(2)}) collective-permute-start(bf16[136,384]{1,0:T(8,128)(2,1)S(1)} %pad_maximum_fusion), channel_id=1, source_target_pairs={{0,4},{2,6},{4,0},{6,2},{1,5},{3,7},{5,1},{7,3},{8,12},{10,14},{12... | collective-permute-start | bytes 313352 | tf_op jit(solution)/shard_map/ppermute | solution.py:586
  54.1 9.6 %collective-permute-start.9 = (bf16[136,384]{1,0:T(8,128)(2,1)S(1)}, bf16[136,384]{1,0:T(8,128)(2,1)S(1)}, u32[]{:S(2)}, u32[]{:S(2)}) collective-permute-start(bf16[136,384]{1,0:T(8,128)(2,1)S(1)} %pad_maximum_fusion.1), channel_id=1, source_target_pairs={{0,6},{2,4},{4,2},{6,0},{1,7},{3,5},{5,3},{7,1},{8,14},{10,12},{12... | collective-permute-start | bytes 313352 | tf_op jit(solution)/shard_map/ppermute | solution.py:586
  56.2 8.7 %collective-permute-start.10 = (bf16[136,384]{1,0:T(8,128)(2,1)S(1)}, bf16[136,384]{1,0:T(8,128)(2,1)S(1)}, u32[]{:S(2)}, u32[]{:S(2)}) collective-permute-start(bf16[136,384]{1,0:T(8,128)(2,1)S(1)} %pad_maximum_fusion.2), channel_id=1, source_target_pairs={{0,2},{2,0},{4,6},{6,4},{1,3},{3,1},{5,7},{7,5},{8,10},{10,8},{12,... | collective-permute-start | bytes 313352 | tf_op jit(solution)/shard_map/ppermute | solution.py:586
  65.1 31.0 %copy-start.7 = (bf16[1,8,1536]{2,1,0:T(8,128)(2,1)}, bf16[1,8,1536]{2,1,0:T(8,128)(2,1)S(1)}, u32[]{:S(2)}) copy-start(bf16[1,8,1536]{2,1,0:T(8,128)(2,1)S(1)} %get-tuple-element.75) | copy-start | bytes 73732
  65.7 13.6 %collective-permute-start.16 = (bf16[128,1536]{1,0:T(8,128)(2,1)S(1)}, bf16[128,1536]{1,0:T(8,128)(2,1)S(1)}, u32[]{:S(2)}, u32[]{:S(2)}) collective-permute-start(bf16[128,1536]{1,0:T(8,128)(2,1)S(1)} %shard_map.170.attn_ref.refs_5_), channel_id=1, source_target_pairs={{0,24},{8,16},{16,8},{24,0},{1,25},{9,17},{17,9},{25,1},{2,26},{10... | collective-permute-start | bytes 1179656 | tf_op jit(solution)/shard_map/ppermute | solution.py:593
  68.1 17.4 %collective-permute-start.15 = (bf16[128,1536]{1,0:T(8,128)(2,1)S(1)}, bf16[128,1536]{1,0:T(8,128)(2,1)S(1)}, u32[]{:S(2)}, u32[]{:S(2)}) collective-permute-start(bf16[128,1536]{1,0:T(8,128)(2,1)S(1)} %shard_map.170.attn_ref.refs_5_), channel_id=1, source_target_pairs={{0,16},{8,24},{16,0},{24,8},{1,17},{9,25},{17,1},{25,9},{2,18},{10... | collective-permute-start | bytes 1179656 | tf_op jit(solution)/shard_map/ppermute | solution.py:593
  68.6 17.0 %collective-permute-start.14 = (bf16[128,1536]{1,0:T(8,128)(2,1)S(1)}, bf16[128,1536]{1,0:T(8,128)(2,1)S(1)}, u32[]{:S(2)}, u32[]{:S(2)}) collective-permute-start(bf16[128,1536]{1,0:T(8,128)(2,1)S(1)} %shard_map.170.attn_ref.refs_5_), channel_id=1, source_target_pairs={{0,8},{8,0},{16,24},{24,16},{1,9},{9,1},{17,25},{25,17},{2,10},{10... | collective-permute-start | bytes 1179656 | tf_op jit(solution)/shard_map/ppermute | solution.py:593
  69.3 3.7 %copy-start = (bf16[3072,1536]{1,0:T(8,128)(2,1)S(1)}, bf16[3072,1536]{1,0:T(8,128)(2,1)}, u32[]{:S(2)}) copy-start(bf16[3072,1536]{1,0:T(8,128)(2,1)} %w_ref.3) | copy-start | bytes 28311556
  78.7 7.4 %collective-permute-start.17 = (bf16[144,1536]{1,0:T(8,128)(2,1)S(1)}, bf16[144,1536]{1,0:T(8,128)(2,1)S(1)}, u32[]{:S(2)}, u32[]{:S(2)}) collective-permute-start(bf16[144,1536]{1,0:T(8,128)(2,1)S(1)} %get-tuple-element.61), channel_id=1, source_target_pairs={{0,1},{2,3},{4,5},{6,7},{1,0},{3,2},{5,4},{7,6},{8,9},{10,11},{12,... | collective-permute-start | bytes 1327112 | tf_op jit(solution)/shard_map/ppermute | solution.py:590
  78.7 7.3 %collective-permute-start.13 = (bf16[4,4,96,128]{3,2,1,0:T(8,128)(2,1)S(1)}, bf16[4,4,96,128]{3,2,1,0:T(8,128)(2,1)S(1)}, u32[]{:S(2)}, u32[]{:S(2)}) collective-permute-start(bf16[4,4,96,128]{3,2,1,0:T(8,128)(2,1)S(1)} %shard_map.172), channel_id=1, source_target_pairs={{0,1},{2,3},{4,5},{6,7},{1,0},{3,2},{5,4},{7,6},{8,9},{10,11},{12,... | collective-permute-start | bytes 1179656 | tf_op jit(solution)/shard_map/ppermute | solution.py:590
  79.3 6.8 %collective-permute-start.20 = (bf16[128,1536]{1,0:T(8,128)(2,1)S(1)}, bf16[128,1536]{1,0:T(8,128)(2,1)S(1)}, u32[]{:S(2)}, u32[]{:S(2)}) collective-permute-start(bf16[128,1536]{1,0:T(8,128)(2,1)S(1)} %collective-permute-done.16.refs_8_), channel_id=1, source_target_pairs={{0,1},{2,3},{4,5},{6,7},{1,0},{3,2},{5,4},{7,6},{8,9},{10,11},{12,... | collective-permute-start | bytes 1179656 | tf_op jit(solution)/shard_map/ppermute | solution.py:590
  85.5 1.7 %collective-permute-start.19 = (bf16[128,1536]{1,0:T(8,128)(2,1)S(1)}, bf16[128,1536]{1,0:T(8,128)(2,1)S(1)}, u32[]{:S(2)}, u32[]{:S(2)}) collective-permute-start(bf16[128,1536]{1,0:T(8,128)(2,1)S(1)} %collective-permute-done.15.refs_7_), channel_id=1, source_target_pairs={{0,1},{2,3},{4,5},{6,7},{1,0},{3,2},{5,4},{7,6},{8,9},{10,11},{12,... | collective-permute-start | bytes 1179656 | tf_op jit(solution)/shard_map/ppermute | solution.py:590
  85.6 2.2 %collective-permute-start.18 = (bf16[128,1536]{1,0:T(8,128)(2,1)S(1)}, bf16[128,1536]{1,0:T(8,128)(2,1)S(1)}, u32[]{:S(2)}, u32[]{:S(2)}) collective-permute-start(bf16[128,1536]{1,0:T(8,128)(2,1)S(1)} %collective-permute-done.14.refs_6_), channel_id=1, source_target_pairs={{0,1},{2,3},{4,5},{6,7},{1,0},{3,2},{5,4},{7,6},{8,9},{10,11},{12,... | collective-permute-start | bytes 1179656 | tf_op jit(solution)/shard_map/ppermute | solution.py:590
  89.2 6.9 %collective-permute-start.23 = (bf16[592,128]{1,0:T(8,128)(2,1)S(1)}, bf16[592,128]{1,0:T(8,128)(2,1)S(1)}, u32[]{:S(2)}, u32[]{:S(2)}) collective-permute-start(bf16[592,128]{1,0:T(8,128)(2,1)S(1)} %get-tuple-element.67), channel_id=1, source_target_pairs={{0,2},{2,0},{4,6},{6,4},{1,3},{3,1},{5,7},{7,5},{8,10},{10,8},{12,... | collective-permute-start | bytes 454664 | tf_op jit(solution)/shard_map/ppermute | solution.py:586
  91.4 7.5 %collective-permute-start.21 = (bf16[576,128]{1,0:T(8,128)(2,1)S(1)}, bf16[576,128]{1,0:T(8,128)(2,1)S(1)}, u32[]{:S(2)}, u32[]{:S(2)}) collective-permute-start(bf16[576,128]{1,0:T(8,128)(2,1)S(1)} %get-tuple-element.65), channel_id=1, source_target_pairs={{0,2},{2,0},{4,6},{6,4},{1,3},{3,1},{5,7},{7,5},{8,10},{10,8},{12,... | collective-permute-start | bytes 442376 | tf_op jit(solution)/shard_map/ppermute | solution.py:586
  96.2 15.6 %collective-permute-start.24 = (bf16[592,128]{1,0:T(8,128)(2,1)S(1)}, bf16[592,128]{1,0:T(8,128)(2,1)S(1)}, u32[]{:S(2)}, u32[]{:S(2)}) collective-permute-start(bf16[592,128]{1,0:T(8,128)(2,1)S(1)} %get-tuple-element.70), channel_id=1, source_target_pairs={{0,4},{2,6},{4,0},{6,2},{1,5},{3,7},{5,1},{7,3},{8,12},{10,14},{12... | collective-permute-start | bytes 454664 | tf_op jit(solution)/shard_map/ppermute | solution.py:586
  98.4 13.3 %collective-permute-start.26 = (bf16[592,128]{1,0:T(8,128)(2,1)S(1)}, bf16[592,128]{1,0:T(8,128)(2,1)S(1)}, u32[]{:S(2)}, u32[]{:S(2)}) collective-permute-start(bf16[592,128]{1,0:T(8,128)(2,1)S(1)} %get-tuple-element.72), channel_id=1, source_target_pairs={{0,2},{2,0},{4,6},{6,4},{1,3},{3,1},{5,7},{7,5},{8,10},{10,8},{12,... | collective-permute-start | bytes 454664 | tf_op jit(solution)/shard_map/ppermute | solution.py:586
  98.9 12.9 %collective-permute-start.22 = (bf16[576,128]{1,0:T(8,128)(2,1)S(1)}, bf16[576,128]{1,0:T(8,128)(2,1)S(1)}, u32[]{:S(2)}, u32[]{:S(2)}) collective-permute-start(bf16[576,128]{1,0:T(8,128)(2,1)S(1)} %shard_map.174), channel_id=1, source_target_pairs={{0,4},{2,6},{4,0},{6,2},{1,5},{3,7},{5,1},{7,3},{8,12},{10,14},{12... | collective-permute-start | bytes 442376 | tf_op jit(solution)/shard_map/ppermute | solution.py:586
  101.3 10.4 %collective-permute-start.25 = (bf16[576,128]{1,0:T(8,128)(2,1)S(1)}, bf16[576,128]{1,0:T(8,128)(2,1)S(1)}, u32[]{:S(2)}, u32[]{:S(2)}) collective-permute-start(bf16[576,128]{1,0:T(8,128)(2,1)S(1)} %get-tuple-element.71), channel_id=1, source_target_pairs={{0,2},{2,0},{4,6},{6,4},{1,3},{3,1},{5,7},{7,5},{8,10},{10,8},{12,... | collective-permute-start | bytes 442376 | tf_op jit(solution)/shard_map/ppermute | solution.py:586

commit v12 on v11

--- a/solution.py
+++ b/solution.py
@@ -44,9 +44,10 @@
 
 
 def text_kernel(
-    groups, heads, place_of, meta_ref, len_ref, src_ref, states_ref, gain_ref, qg_ref, kg_ref,
+    groups, heads, place_of, where, len_ref, src_ref, states_ref, gain_ref, qg_ref, kg_ref,
     k_ref, v_ref, q_ref, w_ref, own_ref, *refs
 ):
+    meta_ref = where()
     packed, refs = refs[:groups], refs[groups:]
     msgs, (w_all, loaded, stage, w_sems, in_sems, out_sems) = refs[:-6], refs[-6:]
     size = own_ref.shape[2]
@@ -119,8 +120,8 @@
 
 
 def text_project(
-    meta, length, sources, states, gain, query_gain, key_gain, keys, values, queries, text_proj,
-    groups, parts, place_of
+    length, sources, states, gain, query_gain, key_gain, keys, values, queries, text_proj,
+    groups, parts, place_of, where
 ):
     slots, depth = states.shape
     size = query_gain.shape[1]
@@ -130,9 +131,9 @@
     shapes += [jax.ShapeDtypeStruct((3 * heads * keys.shape[0], size), bf16)] * groups
     shapes += [jax.ShapeDtypeStruct((groups, text_rows, size), bf16)] * (parts - 1)
     return pl.pallas_call(
-        functools.partial(text_kernel, groups, heads, place_of),
+        functools.partial(text_kernel, groups, heads, place_of, where),
         out_shape=shapes,
-        in_specs=[SMEM, SMEM] + [VMEM] * 5 + [ANY] * 4,
+        in_specs=[SMEM] + [VMEM] * 5 + [ANY] * 4,
         out_specs=[VMEM] + [ANY] * groups + [VMEM] * (parts - 1),
         scratch_shapes=[
             pltpu.VMEM(text_proj.shape, bf16),
@@ -147,7 +148,7 @@
             2 * slots * depth * text_proj.shape[1], 2 * depth * text_proj.shape[1]
         ),
     )(
-        meta, length, sources, states, gain, query_gain, key_gain, keys, values, queries, text_proj
+        length, sources, states, gain, query_gain, key_gain, keys, values, queries, text_proj
     )
 
 
@@ -226,10 +227,11 @@
     )(own, got, *pieces, *after)
 
 
-def attention_kernel(n_far, n_cores, heads, rows, text_rows, *refs):
-    far, refs = refs[:n_far], refs[n_far:]
-    blocks, refs = refs[:n_cores], refs[n_cores:]
-    out_refs, tout_ref = refs[:-1], refs[-1]
+def attention_kernel(n_far, n_cores, queries, heads, rows, text_rows, *refs):
+    far, refs = refs[: queries[0]], refs[queries[0] :]
+    blocks, refs = refs[:n_cores], refs[n_cores + 1 :]
+    out_refs, mark_ref = refs[:-1], refs[-1]
+    mark_ref[0] = 0
     size = blocks[0].shape[1]
     factor = size ** (-0.5) * math.log2(math.e)
     nt = (((1,), (1,)), ((), ()))
@@ -255,41 +257,49 @@
         tkeys, tvalues = tkv[0], with_ones(tkv[1])
         cols = slice(head * size, (head + 1) * size)
         q_at = (2 * heads + head) * rows
-        work = [(ref[q_at : q_at + rows, :], out) for ref, out in zip((blocks[0],) + tuple(far), out_refs)]
-        tq_at = text + head * text_rows
-        work.append((blocks[0][tq_at : tq_at + text_rows, :], tout_ref))
-        for q, out_ref in work:
-            s_img = lax.dot_general(q, keys, nt, preferred_element_type=f32)
-            s_txt = lax.dot_general(q, tkeys, nt, preferred_element_type=f32) + bias
-            top = jnp.maximum(
-                jnp.max(s_img, axis=1, keepdims=True), jnp.max(s_txt, axis=1, keepdims=True)
-            )
-            p_img = jnp.exp2((s_img - top) * factor).astype(bf16)
-            p_txt = jnp.exp2((s_txt - top) * factor).astype(bf16)
-            acc = jnp.dot(p_img, values, preferred_element_type=f32)
-            acc = acc + jnp.dot(p_txt, tvalues, preferred_element_type=f32)
-            out_ref[:, cols] = (acc[:, :size] / acc[:, size:]).astype(bf16)
-
-
-def attention(far, blocks, heads, rows, text_rows):
+        asked = [ref[q_at : q_at + rows, :] for ref in far]
+        if queries[1]:
+            asked.append(blocks[0][q_at : q_at + rows, :])
+        if queries[2]:
+            tq_at = text + head * text_rows
+            asked.append(blocks[0][tq_at : tq_at + text_rows, :])
+        q = jnp.concatenate(asked, axis=0)
+        s_img = lax.dot_general(q, keys, nt, preferred_element_type=f32)
+        s_txt = lax.dot_general(q, tkeys, nt, preferred_element_type=f32) + bias
+        top = jnp.maximum(
+            jnp.max(s_img, axis=1, keepdims=True), jnp.max(s_txt, axis=1, keepdims=True)
+        )
+        p_img = jnp.exp2((s_img - top) * factor).astype(bf16)
+        p_txt = jnp.exp2((s_txt - top) * factor).astype(bf16)
+        acc = jnp.dot(p_img, values, preferred_element_type=f32)
+        acc = acc + jnp.dot(p_txt, tvalues, preferred_element_type=f32)
+        done = (acc[:, :size] / acc[:, size:]).astype(bf16)
+        at = 0
+        for out_ref in out_refs:
+            out_ref[:, cols] = done[at : at + out_ref.shape[0]]
+            at += out_ref.shape[0]
+
+
+def attention(far, near, text, blocks, mark, n_far, heads, rows, text_rows):
     size = blocks[0].shape[1]
-    n = 1 + len(far)
-    queries = n * rows + text_rows
-    keys = len(blocks) * queries
-    shapes = [jax.ShapeDtypeStruct((rows, heads * size), bf16)] * n
-    shapes += [jax.ShapeDtypeStruct((text_rows, heads * size), bf16)]
-    return pl.pallas_call(
-        functools.partial(attention_kernel, len(far), len(blocks), heads, rows, text_rows),
-        out_shape=shapes,
-        in_specs=[VMEM] * (len(far) + len(blocks)),
-        out_specs=[VMEM] * len(shapes),
+    counts = [rows] * (len(far) + near) + [text_rows] * text
+    queries = sum(counts)
+    keys = len(blocks) * ((n_far + 1) * rows + text_rows)
+    shapes = [jax.ShapeDtypeStruct((n, heads * size), bf16) for n in counts]
+    return pl.pallas_call(
+        functools.partial(
+            attention_kernel, n_far, len(blocks), (len(far), near, text), heads, rows, text_rows
+        ),
+        out_shape=shapes + [jax.ShapeDtypeStruct((1,), jnp.int32)],
+        in_specs=[VMEM] * (len(far) + len(blocks)) + [SMEM],
+        out_specs=[VMEM] * len(shapes) + [SMEM],
         compiler_params=params(),
         cost_estimate=cost(
             4 * queries * keys * heads * size,
             4 * (queries + keys) * heads * size,
             queries * keys * heads,
         ),
-    )(*far, *blocks)
+    )(*far, *blocks, mark)
 
 
 def assemble_kernel(places, meta_ref, *refs):
@@ -575,8 +585,12 @@
     OC = O * C
     dp = lax.axis_index("dp")
     seq = lax.axis_index("seq")
-    z = (seq // C) % G
-    oc = (seq // (G * C)) * C + seq % C
+
+    def where():
+        at = lax.axis_index("seq")
+        return (at // C) % G, (at // (G * C)) * C + at % C
+
+    z, oc = where()
 
     def place(oc_at, z_at):
         return ((oc_at // C) * G + z_at) * C + oc_at % C
@@ -608,9 +622,9 @@
     heads = gw // head_size
     text_rows = G * slot_local
     own, *rest = text_project(
-        meta, caption_len, slot_source, caption_states[0], caption_gain[None],
+        caption_len, slot_source, caption_states[0], caption_gain[None],
         query_gain[None], key_gain[None], image_k[0], image_v[0], image_q[0], text_proj,
-        G, OC, place,
+        G, OC, place, where,
     )
     packed, sent = rest[:G], rest[G:]
     images = {0: packed[0]}
@@ -626,8 +640,14 @@
     gg_dp = [gg[0], to_dp(gg[1], 1)]
     block = block_of(own, got, gg_dp[1:], images, DT5, heads)
     blocks = [block] + [to_oc(block, j) for j in range(1, OC)]
-    *outs, text_out = attention(images[1:], blocks, heads, image_local, text_rows)
-    outs = dict(zip([0] + order, outs))
+    far = images[1:]
+    *first, text_out, mark = attention(
+        far[:2], 0, 1, blocks, caption_len, len(far), heads, image_local, text_rows
+    )
+    *second, _ = attention(
+        far[2:], 1, 0, blocks, mark, len(far), heads, image_local, text_rows
+    )
+    outs = dict(zip(order + [0], first + second))
 
     back = {}
     for k in order + [0]:

time: 113 us -> 114 us (level)
  local copies, waits for them, and re-layouts: 5.9 us -> 10.9 us
  waiting for transfers between devices: 52.3 us -> 50.2 us
  starting transfers between devices: 29.5 us -> 28.1 us
    unnamed x18 -> x30, local copies, waits for them, and re-layouts: 5.77 us -> 10.8 us
    ppermute x14, waiting for transfers between devices: 44.4 us -> 41.5 us  [to_z(): return lax.ppermute(x, 'seq', perm)]
    ppermute x14, starting transfers between devices: 19.6 us -> 18.4 us  [to_z(): return lax.ppermute(x, 'seq', perm)]
    pallas_call x2 -> x3, Pallas kernels: 10.8 us -> 10.5 us  [the longest x1 5.66 us: text_project(): pl.pallas_call(functools.partial(text_kernel, groups, heads, place_of, wh...]
  transfers between devices with their start and end apart: 27 -> 27, of which waited for: 11 -> 12; matrix products, arithmetic and copies ran while one was open for 0% -> 1% of each run, Pallas kernels for 12% -> 12%
where the time goes in v12:
time: 114 us
  waiting for transfers between devices  50.2 us (44%)
  starting transfers between devices  28.1 us (25%)
  Pallas kernels  22.1 us (19%)
  local copies, waits for them, and re-layouts  10.9 us (10%)
  between operations  1.6 us (1%)
    ppermute x14, waiting for transfers between devices, to_z(): return lax.ppermute(x, 'seq', perm)  41.5 us
    ppermute x14, starting transfers between devices, to_z(): return lax.ppermute(x, 'seq', perm)  18.4 us
    unnamed x30, local copies, waits for them, and re-layouts  10.8 us
    ppermute x6, starting transfers between devices, to_dp(): return lax.ppermute(x, 'dp', [(a, a ^ k) for a in range(n_dp)])  8.07 us
    ppermute x6, waiting for transfers between devices, to_dp(): return lax.ppermute(x, 'dp', [(a, a ^ k) for a in range(n_dp)])  6.93 us
    pallas_call x1, Pallas kernels, text_project(): pl.pallas_call(functools.partial(text_kernel, groups, heads, place_of, wh...  5.66 us
    pallas_call x1, Pallas kernels, project(): pl.pallas_call(functools.partial(project_kernel, groups, parts, place_of)...  5.65 us
    pallas_call x2, Pallas kernels, attention(): pl.pallas_call(functools.partial(attention_kernel, n_far, len(blocks), (l...  4.83 us
  transfers between devices with their start and end apart: 27, of which 12 were waited for; matrix products, arithmetic and copies ran while one was open for 1% of the time, Pallas kernels for 12%

profile of v12, /device:TPU:0, one launch (start us, length us, event | category | flops | bytes accessed | tf_op | source)
XLA Modules:
  0.0 113.8 jit_solution(11999310890862625937)
XLA Ops:
  1.4 5.7 %shard_map.164 = (f32[4,336,128]{2,1,0:T(8,128)}, bf16[1152,128]{1,0:T(8,128)(2,1)}, bf16[1152,128]{1,0:T(8,128)(2,1)}, bf16[1152,128]{1,0:T(8,128)(2,1)}, bf16[...) custom-call(s32[1]{0:T(128)} %copy.22.len_ref.refs_4_, s32[1,64]{1,0:T(1,128)} %src_ref.1, bf16[64,512]{1,0:T(8,128)(2,1)} %bitcast.36, ...), custom_call_target="tpu_custom_call" | custom-call | flops 301989888 | bytes 4718592 | tf_op jit(solution)/shard_map/pallas_call | solution.py:133
  7.1 0.5 collective-permute-start.2
  7.6 3.7 %collective-permute-start = (bf16[1152,128]{1,0:T(8,128)(2,1)}, bf16[1152,128]{1,0:T(8,128)(2,1)S(1)}, u32[]{:S(2)}, u32[]{:S(2)}) collective-permute-start(bf16[1152,128]{1,0:T(8,128)(2,1)} %get-tuple-element.41), channel_id=1, source_target_pairs={{0,4},{2,6},{4,0},{6,2},{1,5},{3,7},{5,1},{7,3},{8,12},{10,14},{12... | collective-permute-start | bytes 884744 | tf_op jit(solution)/shard_map/ppermute | solution.py:600
  11.2 1.4 %collective-permute-start.1 = (bf16[1152,128]{1,0:T(8,128)(2,1)}, bf16[1152,128]{1,0:T(8,128)(2,1)S(1)}, u32[]{:S(2)}, u32[]{:S(2)}) collective-permute-start(bf16[1152,128]{1,0:T(8,128)(2,1)} %get-tuple-element.42), channel_id=1, source_target_pairs={{0,6},{2,4},{4,2},{6,0},{1,7},{3,5},{5,3},{7,1},{8,14},{10,12},{12... | collective-permute-start | bytes 884744 | tf_op jit(solution)/shard_map/ppermute | solution.py:600
  12.8 1.1 copy-done.8
  14.1 1.9 %collective-permute-start.3 = (bf16[2,320,128]{2,1,0:T(8,128)(2,1)S(1)}, bf16[2,320,128]{2,1,0:T(8,128)(2,1)S(1)}, u32[]{:S(2)}, u32[]{:S(2)}) collective-permute-start(bf16[2,320,128]{2,1,0:T(8,128)(2,1)S(1)} %get-tuple-element.46), channel_id=1, source_target_pairs={{0,2},{2,0},{4,6},{6,4},{1,3},{3,1},{5,7},{7,5},{8,10},{10,8},{12,... | collective-permute-start | bytes 491528 | tf_op jit(solution)/shard_map/ppermute | solution.py:600
  16.0 0.6 pad_add_fusion.meta_ref
  16.6 2.3 %shard_map.167 = (bf16[2,4,96,128]{3,2,1,0:T(8,128)(2,1)}, bf16[2,4,96,128]{3,2,1,0:T(8,128)(2,1)}, bf16[2,4,96,128]{3,2,1,0:T(8,128)(2,1)}, bf16[2,4,96,128]{3,2,1,0:T(8,128)(2,1)}) custom-call(s32[3]{0:T(128)} %pad_add_fusion.meta_ref, f32[1,3072]{1,0:T(1,128)} %gate_ref.3, bf16[128,3072]{1,0:T(8,128)(2,1)} %bitcast.31), custom_call_target="tpu_custom_call" | custom-call | bytes 1572864 | tf_op jit(solution)/shard_map/pallas_call | solution.py:341
  18.9 1.5 %collective-permute-start.6 = (bf16[2,4,96,128]{3,2,1,0:T(8,128)(2,1)}, bf16[2,4,96,128]{3,2,1,0:T(8,128)(2,1)S(1)}, u32[]{:S(2)}, u32[]{:S(2)}) collective-permute-start(bf16[2,4,96,128]{3,2,1,0:T(8,128)(2,1)} %get-tuple-element.51), channel_id=1, source_target_pairs={{0,8},{8,0},{16,24},{24,16},{1,9},{9,1},{17,25},{25,17},{2,10},{10... | collective-permute-start | bytes 589832 | tf_op jit(solution)/shard_map/ppermute | solution.py:607
  20.4 16.2 %collective-permute-done.3.refs_0_ = bf16[2,320,128]{2,1,0:T(8,128)(2,1)S(1)} collective-permute-done((bf16[2,320,128]{2,1,0:T(8,128)(2,1)S(1)}, bf16[2,320,128]{2,1,0:T(8,128)(2,1)S(1)}, u32[]{:S(2)}, u32[]{:S(2)}) %collective-permute-start.3) | collective-permute-done | bytes 163872 | tf_op jit(solution)/shard_map/ppermute | solution.py:600
  36.7 1.7 %collective-permute-start.4 = (bf16[1,320,128]{2,1,0:T(8,128)(2,1)S(1)}, bf16[1,320,128]{2,1,0:T(8,128)(2,1)S(1)}, u32[]{:S(2)}, u32[]{:S(2)}) collective-permute-start(bf16[1,320,128]{2,1,0:T(8,128)(2,1)S(1)} %get-tuple-element.48), channel_id=1, source_target_pairs={{0,4},{2,6},{4,0},{6,2},{1,5},{3,7},{5,1},{7,3},{8,12},{10,14},{12... | collective-permute-start | bytes 245768 | tf_op jit(solution)/shard_map/ppermute | solution.py:600
  38.5 4.6 %collective-permute-done.4.got_ref = bf16[1,320,128]{2,1,0:T(8,128)(2,1)S(1)} collective-permute-done((bf16[1,320,128]{2,1,0:T(8,128)(2,1)S(1)}, bf16[1,320,128]{2,1,0:T(8,128)(2,1)S(1)}, u32[]{:S(2)}, u32[]{:S(2)}) %collective-permute-start.4) | collective-permute-done | bytes 81952 | tf_op jit(solution)/shard_map/ppermute | solution.py:600
  43.0 1.0 copy-done.10
  44.2 0.7 copy-done.2
  45.0 0.7 copy-done.4
  45.7 0.7 copy-done.6
  46.4 1.6 %collective-permute-start.11 = (bf16[2,4,96,128]{3,2,1,0:T(8,128)(2,1)}, bf16[2,4,96,128]{3,2,1,0:T(8,128)(2,1)S(1)}, u32[]{:S(2)}, u32[]{:S(2)}) collective-permute-start(bf16[2,4,96,128]{3,2,1,0:T(8,128)(2,1)} %get-tuple-element.58), channel_id=1, source_target_pairs={{0,16},{8,24},{16,0},{24,8},{1,17},{9,25},{17,1},{25,9},{2,18},{10... | collective-permute-start | bytes 589832 | tf_op jit(solution)/shard_map/ppermute | solution.py:607
  48.0 1.4 %collective-permute-start.12 = (bf16[2,4,96,128]{3,2,1,0:T(8,128)(2,1)}, bf16[2,4,96,128]{3,2,1,0:T(8,128)(2,1)S(1)}, u32[]{:S(2)}, u32[]{:S(2)}) collective-permute-start(bf16[2,4,96,128]{3,2,1,0:T(8,128)(2,1)} %get-tuple-element.59), channel_id=1, source_target_pairs={{0,24},{8,16},{16,8},{24,0},{1,25},{9,17},{17,9},{25,1},{2,26},{10... | collective-permute-start | bytes 589832 | tf_op jit(solution)/shard_map/ppermute | solution.py:607
  49.5 1.0 copy-done.5
  50.5 1.0 copy-done.7
  51.4 2.0 %shard_map.169 = (bf16[128,384]{1,0:T(8,128)(2,1)S(1)}, bf16[128,384]{1,0:T(8,128)(2,1)S(1)}, bf16[32,384]{1,0:T(8,128)(2,1)S(1)}, s32[1]{0:T(128)}) custom-call(bf16[1152,128]{1,0:T(8,128)(2,1)S(1)} %copy-done.5, bf16[1152,128]{1,0:T(8,128)(2,1)S(1)} %copy-done.7, bf16[3760,128]{1,0:T(8,128)(2,1)S(1)} %shard_map.168.refs_2_.refs_1_, ...), custom_call_target="tpu_custom_call" | custom-call | flops 481296384 | bytes 2113536 | tf_op jit(solution)/shard_map/pallas_call | solution.py:289
  53.5 0.8 collective-permute-start.8
  54.3 2.1 %collective-permute-start.9 = (bf16[136,384]{1,0:T(8,128)(2,1)S(1)}, bf16[136,384]{1,0:T(8,128)(2,1)S(1)}, u32[]{:S(2)}, u32[]{:S(2)}) collective-permute-start(bf16[136,384]{1,0:T(8,128)(2,1)S(1)} %pad_maximum_fusion.1), channel_id=1, source_target_pairs={{0,6},{2,4},{4,2},{6,0},{1,7},{3,5},{5,3},{7,1},{8,14},{10,12},{12... | collective-permute-start | bytes 313352 | tf_op jit(solution)/shard_map/ppermute | solution.py:600
  56.4 1.0 copy-done.3
  57.3 2.8 %shard_map.170 = (bf16[128,384]{1,0:T(8,128)(2,1)S(1)}, bf16[128,384]{1,0:T(8,128)(2,1)S(1)}, s32[1]{0:T(128)}) custom-call(bf16[1152,128]{1,0:T(8,128)(2,1)S(1)} %copy-done.3, bf16[3760,128]{1,0:T(8,128)(2,1)S(1)} %shard_map.168.refs_2_.refs_1_, bf16[3760,128]{1,0:T(8,128)(2,1)S(1)} %collective-permute-done.7.refs_3_.refs_2_, s32[1]{0:T(128)} %get-tuple-element.55.refs_3_), custom_call_target="tpu_custom_call" | custom-call | flops 427819008 | bytes 2064384 | tf_op jit(solution)/shard_map/pallas_call | solution.py:289
  60.2 0.8 collective-permute-start.10
  61.0 2.8 %collective-permute-done.8.refs_0_ = bf16[136,384]{1,0:T(8,128)(2,1)S(1)} collective-permute-done((bf16[136,384]{1,0:T(8,128)(2,1)S(1)}, bf16[136,384]{1,0:T(8,128)(2,1)S(1)}, u32[]{:S(2)}, u32[]{:S(2)}) %collective-permute-start.8) | collective-permute-done | bytes 104480 | tf_op jit(solution)/shard_map/ppermute | solution.py:600
  64.0 2.0 %collective-permute-done.10.refs_2_ = bf16[136,384]{1,0:T(8,128)(2,1)S(1)} collective-permute-done((bf16[136,384]{1,0:T(8,128)(2,1)S(1)}, bf16[136,384]{1,0:T(8,128)(2,1)S(1)}, u32[]{:S(2)}, u32[]{:S(2)}) %collective-permute-start.10) | collective-permute-done | bytes 104480 | tf_op jit(solution)/shard_map/ppermute | solution.py:600
  66.2 0.6 shard_map.171.attn_ref.refs_5_
  66.7 2.2 %collective-permute-start.16 = (bf16[128,1536]{1,0:T(8,128)(2,1)S(1)}, bf16[128,1536]{1,0:T(8,128)(2,1)S(1)}, u32[]{:S(2)}, u32[]{:S(2)}) collective-permute-start(bf16[128,1536]{1,0:T(8,128)(2,1)S(1)} %shard_map.171.attn_ref.refs_5_), channel_id=1, source_target_pairs={{0,24},{8,16},{16,8},{24,0},{1,25},{9,17},{17,9},{25,1},{2,26},{10... | collective-permute-start | bytes 1179656 | tf_op jit(solution)/shard_map/ppermute | solution.py:607
  68.9 0.5 collective-permute-start.15
  69.4 0.9 collective-permute-start.14
  70.3 3.7 %copy-done = bf16[3072,1536]{1,0:T(8,128)(2,1)S(1)} copy-done((bf16[3072,1536]{1,0:T(8,128)(2,1)S(1)}, bf16[3072,1536]{1,0:T(8,128)(2,1)}, u32[]{:S(2)}) %copy-start) | copy-done | bytes 9437208
  74.0 5.6 %shard_map.172 = (bf16[128,3072]{1,0:T(8,128)(2,1)}, bf16[128,1536]{1,0:T(8,128)(2,1)}, f32[4,384]{1,0:T(4,128)S(1)}, bf16[144,1536]{1,0:T(8,128)(2,1)S(1)}) custom-call(s32[3]{0:T(128)S(1)} %copy-done.12, bf16[128,1536]{1,0:T(8,128)(2,1)S(1)} %shard_map.171.attn_ref.refs_5_, bf16[3072,1536]{1,0:T(8,128)(2,1)S(1)} %copy-done, f32[1,3072]{1,0:T(1,128)S(1)} %copy-done.11, ...), custom_call_target="tpu_custom_call" | custom-call | flops 2415919104 | bytes 9437184 | tf_op jit(solution)/shard_map/pallas_call | solution.py:422
  79.7 0.6 collective-permute-start.13
  80.3 6.8 %collective-permute-done.15.refs_7_ = bf16[128,1536]{1,0:T(8,128)(2,1)S(1)} collective-permute-done((bf16[128,1536]{1,0:T(8,128)(2,1)S(1)}, bf16[128,1536]{1,0:T(8,128)(2,1)S(1)}, u32[]{:S(2)}, u32[]{:S(2)}) %collective-permute-start.15) | collective-permute-done | bytes 393248 | tf_op jit(solution)/shard_map/ppermute | solution.py:607
  87.8 1.1 collective-permute-done.19.refs_11_
  88.9 0.6 collective-permute-done.18.refs_10_
  89.5 1.4 %shard_map.174 = (f32[1168,128]{1,0:T(8,128)S(1)}, bf16[576,128]{1,0:T(8,128)(2,1)S(1)}, bf16[592,128]{1,0:T(8,128)(2,1)S(1)}, f32[576,128]{1,0:T(8,128)S(1)}, f...) custom-call(bf16[1,4,96,128]{3,2,1,0:T(8,128)(2,1)S(1)} %slice.24.refs_0_, ...), custom_call_target="tpu_custom_call" | custom-call | flops 1207959552 | bytes 5111808 | tf_op jit(solution)/shard_map/pallas_call | solution.py:498
  90.8 0.7 collective-permute-start.23
  91.6 1.4 %collective-permute-start.21 = (bf16[576,128]{1,0:T(8,128)(2,1)S(1)}, bf16[576,128]{1,0:T(8,128)(2,1)S(1)}, u32[]{:S(2)}, u32[]{:S(2)}) collective-permute-start(bf16[576,128]{1,0:T(8,128)(2,1)S(1)} %get-tuple-element.67), channel_id=1, source_target_pairs={{0,2},{2,0},{4,6},{6,4},{1,3},{3,1},{5,7},{7,5},{8,10},{10,8},{12,... | collective-permute-start | bytes 442376 | tf_op jit(solution)/shard_map/ppermute | solution.py:600
  92.9 4.8 %collective-permute-done.23.got_ref = bf16[592,128]{1,0:T(8,128)(2,1)S(1)} collective-permute-done((bf16[592,128]{1,0:T(8,128)(2,1)S(1)}, bf16[592,128]{1,0:T(8,128)(2,1)S(1)}, u32[]{:S(2)}, u32[]{:S(2)}) %collective-permute-start.23) | collective-permute-done | bytes 151584 | tf_op jit(solution)/shard_map/ppermute | solution.py:600
  97.8 0.9 collective-permute-start.24
  98.6 1.2 %collective-permute-start.26 = (bf16[592,128]{1,0:T(8,128)(2,1)S(1)}, bf16[592,128]{1,0:T(8,128)(2,1)S(1)}, u32[]{:S(2)}, u32[]{:S(2)}) collective-permute-start(bf16[592,128]{1,0:T(8,128)(2,1)S(1)} %get-tuple-element.74), channel_id=1, source_target_pairs={{0,2},{2,0},{4,6},{6,4},{1,3},{3,1},{5,7},{7,5},{8,10},{10,8},{12,... | collective-permute-start | bytes 454664 | tf_op jit(solution)/shard_map/ppermute | solution.py:600
  99.8 1.3 %collective-permute-done.21.got_ref = bf16[576,128]{1,0:T(8,128)(2,1)S(1)} collective-permute-done((bf16[576,128]{1,0:T(8,128)(2,1)S(1)}, bf16[576,128]{1,0:T(8,128)(2,1)S(1)}, u32[]{:S(2)}, u32[]{:S(2)}) %collective-permute-start.21) | collective-permute-done | bytes 147488 | tf_op jit(solution)/shard_map/ppermute | solution.py:600
  101.5 1.4 %collective-permute-start.25 = (bf16[576,128]{1,0:T(8,128)(2,1)S(1)}, bf16[576,128]{1,0:T(8,128)(2,1)S(1)}, u32[]{:S(2)}, u32[]{:S(2)}) collective-permute-start(bf16[576,128]{1,0:T(8,128)(2,1)S(1)} %get-tuple-element.73), channel_id=1, source_target_pairs={{0,2},{2,0},{4,6},{6,4},{1,3},{3,1},{5,7},{7,5},{8,10},{10,8},{12,... | collective-permute-start | bytes 442376 | tf_op jit(solution)/shard_map/ppermute | solution.py:600
  102.9 9.9 %collective-permute-done.22.far_low = bf16[576,128]{1,0:T(8,128)(2,1)S(1)} collective-permute-done((bf16[576,128]{1,0:T(8,128)(2,1)S(1)}, bf16[576,128]{1,0:T(8,128)(2,1)S(1)}, u32[]{:S(2)}, u32[]{:S(2)}) %collective-permute-start.22) | collective-permute-done | bytes 147488 | tf_op jit(solution)/shard_map/ppermute | solution.py:600
  112.9 0.9 shard_map.177
  (67 shorter events, 2.5 us)
Async XLA Ops:
  0.6 48.8 %copy-start.14 = (s32[1,64]{1,0:T(1,128)S(1)}, s32[1,64]{1,0:T(1,128)}, u32[]{:S(2)}) copy-start(s32[1,64]{1,0:T(1,128)} %src_ref.1) | copy-start | bytes 772
  0.6 69.7 %copy-start.11 = (f32[1,3072]{1,0:T(1,128)S(1)}, f32[1,3072]{1,0:T(1,128)}, u32[]{:S(2)}) copy-start(f32[1,3072]{1,0:T(1,128)} %gate_ref.3) | copy-start | bytes 36868
  0.7 69.6 %copy-start.1 = (bf16[1,128,3072]{2,1,0:T(8,128)(2,1)S(1)}, bf16[1,128,3072]{2,1,0:T(8,128)(2,1)}, u32[]{:S(2)}) copy-start(bf16[1,128,3072]{2,1,0:T(8,128)(2,1)} %param.25) | copy-start | bytes 2359300
  7.1 5.8 %collective-permute-start.2 = (bf16[4,320,128]{2,1,0:T(8,128)(2,1)}, bf16[4,320,128]{2,1,0:T(8,128)(2,1)S(1)}, u32[]{:S(2)}, u32[]{:S(2)}) collective-permute-start(bf16[4,320,128]{2,1,0:T(8,128)(2,1)} %get-tuple-element.44), channel_id=1, source_target_pairs={{0,1},{2,3},{4,5},{6,7},{1,0},{3,2},{5,4},{7,6},{8,9},{10,11},{12,... | collective-permute-start | bytes 983048 | tf_op jit(solution)/shard_map/ppermute | solution.py:604
  7.6 30.9 %collective-permute-start = (bf16[1152,128]{1,0:T(8,128)(2,1)}, bf16[1152,128]{1,0:T(8,128)(2,1)S(1)}, u32[]{:S(2)}, u32[]{:S(2)}) collective-permute-start(bf16[1152,128]{1,0:T(8,128)(2,1)} %get-tuple-element.41), channel_id=1, source_target_pairs={{0,4},{2,6},{4,0},{6,2},{1,5},{3,7},{5,1},{7,3},{8,12},{10,14},{12... | collective-permute-start | bytes 884744 | tf_op jit(solution)/shard_map/ppermute | solution.py:600
  11.2 27.2 %collective-permute-start.1 = (bf16[1152,128]{1,0:T(8,128)(2,1)}, bf16[1152,128]{1,0:T(8,128)(2,1)S(1)}, u32[]{:S(2)}, u32[]{:S(2)}) collective-permute-start(bf16[1152,128]{1,0:T(8,128)(2,1)} %get-tuple-element.42), channel_id=1, source_target_pairs={{0,6},{2,4},{4,2},{6,0},{1,7},{3,5},{5,3},{7,1},{8,14},{10,12},{12... | collective-permute-start | bytes 884744 | tf_op jit(solution)/shard_map/ppermute | solution.py:600
  12.6 25.9 %collective-permute-start.5 = (bf16[1152,128]{1,0:T(8,128)(2,1)}, bf16[1152,128]{1,0:T(8,128)(2,1)S(1)}, u32[]{:S(2)}, u32[]{:S(2)}) collective-permute-start(bf16[1152,128]{1,0:T(8,128)(2,1)} %get-tuple-element.50), channel_id=1, source_target_pairs={{0,2},{2,0},{4,6},{6,4},{1,3},{3,1},{5,7},{7,5},{8,10},{10,8},{12,... | collective-permute-start | bytes 884744 | tf_op jit(solution)/shard_map/ppermute | solution.py:600
  12.8 1.1 copy-start.8
  14.1 22.5 %collective-permute-start.3 = (bf16[2,320,128]{2,1,0:T(8,128)(2,1)S(1)}, bf16[2,320,128]{2,1,0:T(8,128)(2,1)S(1)}, u32[]{:S(2)}, u32[]{:S(2)}) collective-permute-start(bf16[2,320,128]{2,1,0:T(8,128)(2,1)S(1)} %get-tuple-element.46), channel_id=1, source_target_pairs={{0,2},{2,0},{4,6},{6,4},{1,3},{3,1},{5,7},{7,5},{8,10},{10,8},{12,... | collective-permute-start | bytes 491528 | tf_op jit(solution)/shard_map/ppermute | solution.py:600
  16.6 49.6 %copy-start.12 = (s32[3]{0:T(128)S(1)}, s32[3]{0:T(128)}, u32[]{:S(2)}) copy-start(s32[3]{0:T(128)} %pad_add_fusion.meta_ref) | copy-start | bytes 40
  18.9 19.5 %collective-permute-start.6 = (bf16[2,4,96,128]{3,2,1,0:T(8,128)(2,1)}, bf16[2,4,96,128]{3,2,1,0:T(8,128)(2,1)S(1)}, u32[]{:S(2)}, u32[]{:S(2)}) collective-permute-start(bf16[2,4,96,128]{3,2,1,0:T(8,128)(2,1)} %get-tuple-element.51), channel_id=1, source_target_pairs={{0,8},{8,0},{16,24},{24,16},{1,9},{9,1},{17,25},{25,17},{2,10},{10... | collective-permute-start | bytes 589832 | tf_op jit(solution)/shard_map/ppermute | solution.py:607
  36.7 6.3 %collective-permute-start.4 = (bf16[1,320,128]{2,1,0:T(8,128)(2,1)S(1)}, bf16[1,320,128]{2,1,0:T(8,128)(2,1)S(1)}, u32[]{:S(2)}, u32[]{:S(2)}) collective-permute-start(bf16[1,320,128]{2,1,0:T(8,128)(2,1)S(1)} %get-tuple-element.48), channel_id=1, source_target_pairs={{0,4},{2,6},{4,0},{6,2},{1,5},{3,7},{5,1},{7,3},{8,12},{10,14},{12... | collective-permute-start | bytes 245768 | tf_op jit(solution)/shard_map/ppermute | solution.py:600
  43.0 1.0 copy-start.10
  44.0 35.7 %copy-start.9 = (bf16[2,4,96,128]{3,2,1,0:T(8,128)(2,1)S(1)}, bf16[2,4,96,128]{3,2,1,0:T(8,128)(2,1)}, u32[]{:S(2)}) copy-start(bf16[2,4,96,128]{3,2,1,0:T(8,128)(2,1)} %get-tuple-element.62.refs_0_) | copy-start | bytes 589828
  44.2 0.7 copy-start.2
  45.0 0.7 copy-start.4
  45.7 0.7 copy-start.6
  46.4 3.1 %collective-permute-start.7 = (bf16[3760,128]{1,0:T(8,128)(2,1)S(1)}, bf16[3760,128]{1,0:T(8,128)(2,1)S(1)}, u32[]{:S(2)}, u32[]{:S(2)}) collective-permute-start(bf16[3760,128]{1,0:T(8,128)(2,1)S(1)} %shard_map.168.refs_2_.refs_1_), channel_id=1, source_target_pairs={{0,1},{2,3},{4,5},{6,7},{1,0},{3,2},{5,4},{7,6},{8,9},{10,11},{12,... | collective-permute-start | bytes 2887688 | tf_op jit(solution)/shard_map/ppermute | solution.py:604
  46.4 19.7 %collective-permute-start.11 = (bf16[2,4,96,128]{3,2,1,0:T(8,128)(2,1)}, bf16[2,4,96,128]{3,2,1,0:T(8,128)(2,1)S(1)}, u32[]{:S(2)}, u32[]{:S(2)}) collective-permute-start(bf16[2,4,96,128]{3,2,1,0:T(8,128)(2,1)} %get-tuple-element.58), channel_id=1, source_target_pairs={{0,16},{8,24},{16,0},{24,8},{1,17},{9,25},{17,1},{25,9},{2,18},{10... | collective-permute-start | bytes 589832 | tf_op jit(solution)/shard_map/ppermute | solution.py:607
  48.0 18.2 %collective-permute-start.12 = (bf16[2,4,96,128]{3,2,1,0:T(8,128)(2,1)}, bf16[2,4,96,128]{3,2,1,0:T(8,128)(2,1)S(1)}, u32[]{:S(2)}, u32[]{:S(2)}) collective-permute-start(bf16[2,4,96,128]{3,2,1,0:T(8,128)(2,1)} %get-tuple-element.59), channel_id=1, source_target_pairs={{0,24},{8,16},{16,8},{24,0},{1,25},{9,17},{17,9},{25,1},{2,26},{10... | collective-permute-start | bytes 589832 | tf_op jit(solution)/shard_map/ppermute | solution.py:607
  49.5 1.0 copy-start.5
  50.5 1.0 copy-start.7
  53.5 10.3 %collective-permute-start.8 = (bf16[136,384]{1,0:T(8,128)(2,1)S(1)}, bf16[136,384]{1,0:T(8,128)(2,1)S(1)}, u32[]{:S(2)}, u32[]{:S(2)}) collective-permute-start(bf16[136,384]{1,0:T(8,128)(2,1)S(1)} %pad_maximum_fusion), channel_id=1, source_target_pairs={{0,4},{2,6},{4,0},{6,2},{1,5},{3,7},{5,1},{7,3},{8,12},{10,14},{12... | collective-permute-start | bytes 313352 | tf_op jit(solution)/shard_map/ppermute | solution.py:600
  54.3 9.6 %collective-permute-start.9 = (bf16[136,384]{1,0:T(8,128)(2,1)S(1)}, bf16[136,384]{1,0:T(8,128)(2,1)S(1)}, u32[]{:S(2)}, u32[]{:S(2)}) collective-permute-start(bf16[136,384]{1,0:T(8,128)(2,1)S(1)} %pad_maximum_fusion.1), channel_id=1, source_target_pairs={{0,6},{2,4},{4,2},{6,0},{1,7},{3,5},{5,3},{7,1},{8,14},{10,12},{12... | collective-permute-start | bytes 313352 | tf_op jit(solution)/shard_map/ppermute | solution.py:600
  56.4 1.0 copy-start.3
  60.2 5.8 %collective-permute-start.10 = (bf16[136,384]{1,0:T(8,128)(2,1)S(1)}, bf16[136,384]{1,0:T(8,128)(2,1)S(1)}, u32[]{:S(2)}, u32[]{:S(2)}) collective-permute-start(bf16[136,384]{1,0:T(8,128)(2,1)S(1)} %pad_maximum_fusion.2), channel_id=1, source_target_pairs={{0,2},{2,0},{4,6},{6,4},{1,3},{3,1},{5,7},{7,5},{8,10},{10,8},{12,... | collective-permute-start | bytes 313352 | tf_op jit(solution)/shard_map/ppermute | solution.py:600
  66.1 31.6 %copy-start.13 = (bf16[1,8,1536]{2,1,0:T(8,128)(2,1)}, bf16[1,8,1536]{2,1,0:T(8,128)(2,1)S(1)}, u32[]{:S(2)}) copy-start(bf16[1,8,1536]{2,1,0:T(8,128)(2,1)S(1)} %get-tuple-element.77) | copy-start | bytes 73732
  66.7 13.5 %collective-permute-start.16 = (bf16[128,1536]{1,0:T(8,128)(2,1)S(1)}, bf16[128,1536]{1,0:T(8,128)(2,1)S(1)}, u32[]{:S(2)}, u32[]{:S(2)}) collective-permute-start(bf16[128,1536]{1,0:T(8,128)(2,1)S(1)} %shard_map.171.attn_ref.refs_5_), channel_id=1, source_target_pairs={{0,24},{8,16},{16,8},{24,0},{1,25},{9,17},{17,9},{25,1},{2,26},{10... | collective-permute-start | bytes 1179656 | tf_op jit(solution)/shard_map/ppermute | solution.py:607
  68.9 18.2 %collective-permute-start.15 = (bf16[128,1536]{1,0:T(8,128)(2,1)S(1)}, bf16[128,1536]{1,0:T(8,128)(2,1)S(1)}, u32[]{:S(2)}, u32[]{:S(2)}) collective-permute-start(bf16[128,1536]{1,0:T(8,128)(2,1)S(1)} %shard_map.171.attn_ref.refs_5_), channel_id=1, source_target_pairs={{0,16},{8,24},{16,0},{24,8},{1,17},{9,25},{17,1},{25,9},{2,18},{10... | collective-permute-start | bytes 1179656 | tf_op jit(solution)/shard_map/ppermute | solution.py:607
  69.4 17.8 %collective-permute-start.14 = (bf16[128,1536]{1,0:T(8,128)(2,1)S(1)}, bf16[128,1536]{1,0:T(8,128)(2,1)S(1)}, u32[]{:S(2)}, u32[]{:S(2)}) collective-permute-start(bf16[128,1536]{1,0:T(8,128)(2,1)S(1)} %shard_map.171.attn_ref.refs_5_), channel_id=1, source_target_pairs={{0,8},{8,0},{16,24},{24,16},{1,9},{9,1},{17,25},{25,17},{2,10},{10... | collective-permute-start | bytes 1179656 | tf_op jit(solution)/shard_map/ppermute | solution.py:607
  70.3 3.7 %copy-start = (bf16[3072,1536]{1,0:T(8,128)(2,1)S(1)}, bf16[3072,1536]{1,0:T(8,128)(2,1)}, u32[]{:S(2)}) copy-start(bf16[3072,1536]{1,0:T(8,128)(2,1)} %w_ref.3) | copy-start | bytes 28311556
  79.6 8.1 %collective-permute-start.17 = (bf16[144,1536]{1,0:T(8,128)(2,1)S(1)}, bf16[144,1536]{1,0:T(8,128)(2,1)S(1)}, u32[]{:S(2)}, u32[]{:S(2)}) collective-permute-start(bf16[144,1536]{1,0:T(8,128)(2,1)S(1)} %get-tuple-element.63), channel_id=1, source_target_pairs={{0,1},{2,3},{4,5},{6,7},{1,0},{3,2},{5,4},{7,6},{8,9},{10,11},{12,... | collective-permute-start | bytes 1327112 | tf_op jit(solution)/shard_map/ppermute | solution.py:604
  79.7 8.1 %collective-permute-start.13 = (bf16[4,4,96,128]{3,2,1,0:T(8,128)(2,1)S(1)}, bf16[4,4,96,128]{3,2,1,0:T(8,128)(2,1)S(1)}, u32[]{:S(2)}, u32[]{:S(2)}) collective-permute-start(bf16[4,4,96,128]{3,2,1,0:T(8,128)(2,1)S(1)} %shard_map.173), channel_id=1, source_target_pairs={{0,1},{2,3},{4,5},{6,7},{1,0},{3,2},{5,4},{7,6},{8,9},{10,11},{12,... | collective-permute-start | bytes 1179656 | tf_op jit(solution)/shard_map/ppermute | solution.py:604
  80.2 7.5 %collective-permute-start.20 = (bf16[128,1536]{1,0:T(8,128)(2,1)S(1)}, bf16[128,1536]{1,0:T(8,128)(2,1)S(1)}, u32[]{:S(2)}, u32[]{:S(2)}) collective-permute-start(bf16[128,1536]{1,0:T(8,128)(2,1)S(1)} %collective-permute-done.16.refs_8_), channel_id=1, source_target_pairs={{0,1},{2,3},{4,5},{6,7},{1,0},{3,2},{5,4},{7,6},{8,9},{10,11},{12,... | collective-permute-start | bytes 1179656 | tf_op jit(solution)/shard_map/ppermute | solution.py:604
  87.2 1.7 %collective-permute-start.19 = (bf16[128,1536]{1,0:T(8,128)(2,1)S(1)}, bf16[128,1536]{1,0:T(8,128)(2,1)S(1)}, u32[]{:S(2)}, u32[]{:S(2)}) collective-permute-start(bf16[128,1536]{1,0:T(8,128)(2,1)S(1)} %collective-permute-done.15.refs_7_), channel_id=1, source_target_pairs={{0,1},{2,3},{4,5},{6,7},{1,0},{3,2},{5,4},{7,6},{8,9},{10,11},{12,... | collective-permute-start | bytes 1179656 | tf_op jit(solution)/shard_map/ppermute | solution.py:604
  87.3 2.2 %collective-permute-start.18 = (bf16[128,1536]{1,0:T(8,128)(2,1)S(1)}, bf16[128,1536]{1,0:T(8,128)(2,1)S(1)}, u32[]{:S(2)}, u32[]{:S(2)}) collective-permute-start(bf16[128,1536]{1,0:T(8,128)(2,1)S(1)} %collective-permute-done.14.refs_6_), channel_id=1, source_target_pairs={{0,1},{2,3},{4,5},{6,7},{1,0},{3,2},{5,4},{7,6},{8,9},{10,11},{12,... | collective-permute-start | bytes 1179656 | tf_op jit(solution)/shard_map/ppermute | solution.py:604
  90.8 6.8 %collective-permute-start.23 = (bf16[592,128]{1,0:T(8,128)(2,1)S(1)}, bf16[592,128]{1,0:T(8,128)(2,1)S(1)}, u32[]{:S(2)}, u32[]{:S(2)}) collective-permute-start(bf16[592,128]{1,0:T(8,128)(2,1)S(1)} %get-tuple-element.69), channel_id=1, source_target_pairs={{0,2},{2,0},{4,6},{6,4},{1,3},{3,1},{5,7},{7,5},{8,10},{10,8},{12,... | collective-permute-start | bytes 454664 | tf_op jit(solution)/shard_map/ppermute | solution.py:600
  91.6 9.6 %collective-permute-start.21 = (bf16[576,128]{1,0:T(8,128)(2,1)S(1)}, bf16[576,128]{1,0:T(8,128)(2,1)S(1)}, u32[]{:S(2)}, u32[]{:S(2)}) collective-permute-start(bf16[576,128]{1,0:T(8,128)(2,1)S(1)} %get-tuple-element.67), channel_id=1, source_target_pairs={{0,2},{2,0},{4,6},{6,4},{1,3},{3,1},{5,7},{7,5},{8,10},{10,8},{12,... | collective-permute-start | bytes 442376 | tf_op jit(solution)/shard_map/ppermute | solution.py:600
  97.8 15.1 %collective-permute-start.24 = (bf16[592,128]{1,0:T(8,128)(2,1)S(1)}, bf16[592,128]{1,0:T(8,128)(2,1)S(1)}, u32[]{:S(2)}, u32[]{:S(2)}) collective-permute-start(bf16[592,128]{1,0:T(8,128)(2,1)S(1)} %get-tuple-element.72), channel_id=1, source_target_pairs={{0,4},{2,6},{4,0},{6,2},{1,5},{3,7},{5,1},{7,3},{8,12},{10,14},{12... | collective-permute-start | bytes 454664 | tf_op jit(solution)/shard_map/ppermute | solution.py:600
  98.6 14.2 %collective-permute-start.26 = (bf16[592,128]{1,0:T(8,128)(2,1)S(1)}, bf16[592,128]{1,0:T(8,128)(2,1)S(1)}, u32[]{:S(2)}, u32[]{:S(2)}) collective-permute-start(bf16[592,128]{1,0:T(8,128)(2,1)S(1)} %get-tuple-element.74), channel_id=1, source_target_pairs={{0,2},{2,0},{4,6},{6,4},{1,3},{3,1},{5,7},{7,5},{8,10},{10,8},{12,... | collective-permute-start | bytes 454664 | tf_op jit(solution)/shard_map/ppermute | solution.py:600
  101.2 11.6 %collective-permute-start.22 = (bf16[576,128]{1,0:T(8,128)(2,1)S(1)}, bf16[576,128]{1,0:T(8,128)(2,1)S(1)}, u32[]{:S(2)}, u32[]{:S(2)}) collective-permute-start(bf16[576,128]{1,0:T(8,128)(2,1)S(1)} %shard_map.175), channel_id=1, source_target_pairs={{0,4},{2,6},{4,0},{6,2},{1,5},{3,7},{5,1},{7,3},{8,12},{10,14},{12... | collective-permute-start | bytes 442376 | tf_op jit(solution)/shard_map/ppermute | solution.py:600
  101.5 11.3 %collective-permute-start.25 = (bf16[576,128]{1,0:T(8,128)(2,1)S(1)}, bf16[576,128]{1,0:T(8,128)(2,1)S(1)}, u32[]{:S(2)}, u32[]{:S(2)}) collective-permute-start(bf16[576,128]{1,0:T(8,128)(2,1)S(1)} %get-tuple-element.73), channel_id=1, source_target_pairs={{0,2},{2,0},{4,6},{6,4},{1,3},{3,1},{5,7},{7,5},{8,10},{10,8},{12,... | collective-permute-start | bytes 442376 | tf_op jit(solution)/shard_map/ppermute | solution.py:600

commit v13 on v12

--- a/solution.py
+++ b/solution.py
@@ -186,13 +186,17 @@
 
 
 def block_kernel(features, heads, n_pieces, own_ref, got_ref, *refs):
-    pieces, out_ref = refs[:n_pieces], refs[-1]
+    pieces, (out_ref, first_ref, second_ref) = refs[:n_pieces], refs[-3:]
     near_rows = pieces[0].shape[0]
     kv_rows = near_rows // 3 * 2
     out_ref[:near_rows, :] = pieces[0][...]
     for k, ref in enumerate(pieces[1:]):
         at = near_rows + k * kv_rows
         out_ref[at : at + kv_rows, :] = ref[:kv_rows, :]
+    q_rows = near_rows - kv_rows
+    first_ref[:q_rows, :] = pieces[1][kv_rows:, :]
+    first_ref[q_rows:, :] = pieces[2][kv_rows:, :]
+    second_ref[...] = pieces[3][kv_rows:, :]
     size = own_ref.shape[2]
     text_rows = got_ref.shape[1]
     rows = text_rows // (3 * heads + 1)
@@ -216,22 +220,21 @@
 def block_of(own, got, after, pieces, features, heads):
     rows, size = own.shape[1:]
     total = (rows - EXTRA) // (3 * heads + 1) * 3 * heads + EXTRA
-    total += pieces[0].shape[0] // 3 * (2 * len(pieces) + 1)
+    q_rows = pieces[0].shape[0] // 3
+    total += q_rows * (2 * len(pieces) + 1)
     return pl.pallas_call(
         functools.partial(block_kernel, features, heads, len(pieces)),
-        out_shape=jax.ShapeDtypeStruct((total, size), bf16),
+        out_shape=[jax.ShapeDtypeStruct((n, size), bf16) for n in (total, 2 * q_rows, q_rows)],
         in_specs=[VMEM] * (2 + len(pieces)) + [ANY] * len(after),
-        out_specs=VMEM,
+        out_specs=[VMEM] * 3,
         compiler_params=params(),
         cost_estimate=cost(0, 4 * total * size),
     )(own, got, *pieces, *after)
 
 
-def attention_kernel(n_far, n_cores, queries, heads, rows, text_rows, *refs):
-    far, refs = refs[: queries[0]], refs[queries[0] :]
-    blocks, refs = refs[:n_cores], refs[n_cores + 1 :]
-    out_refs, mark_ref = refs[:-1], refs[-1]
-    mark_ref[0] = 0
+def attention_kernel(n_far, n_cores, n_after, queries, heads, rows, text_rows, *refs):
+    far_ref, blocks = refs[0], refs[1 : 1 + n_cores]
+    out_refs = refs[1 + n_cores + n_after :]
     size = blocks[0].shape[1]
     factor = size ** (-0.5) * math.log2(math.e)
     nt = (((1,), (1,)), ((), ()))
@@ -257,7 +260,10 @@
         tkeys, tvalues = tkv[0], with_ones(tkv[1])
         cols = slice(head * size, (head + 1) * size)
         q_at = (2 * heads + head) * rows
-        asked = [ref[q_at : q_at + rows, :] for ref in far]
+        asked = [
+            far_ref[(k * heads + head) * rows : (k * heads + head + 1) * rows, :]
+            for k in range(queries[0])
+        ]
         if queries[1]:
             asked.append(blocks[0][q_at : q_at + rows, :])
         if queries[2]:
@@ -280,46 +286,55 @@
             at += out_ref.shape[0]
 
 
-def attention(far, near, text, blocks, mark, n_far, heads, rows, text_rows):
+def attention(far, near, text, blocks, after, n_far, heads, rows, text_rows):
     size = blocks[0].shape[1]
-    counts = [rows] * (len(far) + near) + [text_rows] * text
+    asked = far.shape[0] // (heads * rows)
+    counts = [rows] * (asked + near) + [text_rows] * text
     queries = sum(counts)
     keys = len(blocks) * ((n_far + 1) * rows + text_rows)
     shapes = [jax.ShapeDtypeStruct((n, heads * size), bf16) for n in counts]
     return pl.pallas_call(
         functools.partial(
-            attention_kernel, n_far, len(blocks), (len(far), near, text), heads, rows, text_rows
+            attention_kernel,
+            n_far,
+            len(blocks),
+            len(after),
+            (asked, near, text),
+            heads,
+            rows,
+            text_rows,
         ),
-        out_shape=shapes + [jax.ShapeDtypeStruct((1,), jnp.int32)],
-        in_specs=[VMEM] * (len(far) + len(blocks)) + [SMEM],
-        out_specs=[VMEM] * len(shapes) + [SMEM],
+        out_shape=shapes,
+        in_specs=[VMEM] * (1 + len(blocks)) + [ANY] * len(after),
+        out_specs=[VMEM] * len(shapes),
         compiler_params=params(),
         cost_estimate=cost(
             4 * queries * keys * heads * size,
             4 * (queries + keys) * heads * size,
             queries * keys * heads,
         ),
-    )(*far, *blocks, mark)
-
-
-def assemble_kernel(places, meta_ref, *refs):
+    )(far, *blocks, *after)
+
+
+def assemble_kernel(places, where, *refs):
     pieces, out_ref = refs[: len(places)], refs[-1]
+    z = where()[0]
     rows, width = out_ref.shape[0], pieces[0].shape[1]
     for k, piece in zip(places, pieces):
-        at = pl.multiple_of((meta_ref[0] ^ k) * width, 128)
+        at = pl.multiple_of((z ^ k) * width, 128)
         out_ref[:, pl.ds(at, width)] = piece[:rows, :]
 
 
-def assemble(meta, pieces, places, after, rows):
+def assemble(where, pieces, places, after, rows):
     groups, width = len(pieces), pieces[0].shape[1]
     return pl.pallas_call(
-        functools.partial(assemble_kernel, tuple(places)),
+        functools.partial(assemble_kernel, tuple(places), where),
         out_shape=jax.ShapeDtypeStruct((rows, groups * width), bf16),
-        in_specs=[SMEM] + [VMEM] * groups + [ANY] * len(after),
+        in_specs=[VMEM] * groups + [ANY] * len(after),
         out_specs=VMEM,
         compiler_params=params(),
         cost_estimate=cost(0, 4 * rows * groups * width),
-    )(meta, *pieces, *after)
+    )(*pieces, *after)
 
 
 def gated_kernel(groups, parts, place_of, meta_ref, gate_ref, d_out_ref, *refs):
@@ -638,15 +653,15 @@
 
     gg = gated_parts(meta, gate, d_out[0], n_dp, G, OC, place)
     gg_dp = [gg[0], to_dp(gg[1], 1)]
-    block = block_of(own, got, gg_dp[1:], images, DT5, heads)
+    block, far_first, far_second = block_of(own, got, gg_dp[1:], images, DT5, heads)
     blocks = [block] + [to_oc(block, j) for j in range(1, OC)]
-    far = images[1:]
-    *first, text_out, mark = attention(
-        far[:2], 0, 1, blocks, caption_len, len(far), heads, image_local, text_rows
-    )
-    *second, _ = attention(
-        far[2:], 1, 0, blocks, mark, len(far), heads, image_local, text_rows
-    )
+    *first, text_out = attention(
+        far_first, 0, 1, blocks, [], G - 1, heads, image_local, text_rows
+    )
+    second = attention(
+        far_second, 1, 0, blocks, [text_out], G - 1, heads, image_local, text_rows
+    )
+    second = list(second)
     outs = dict(zip(order + [0], first + second))
 
     back = {}
@@ -657,7 +672,7 @@
     gg_dp += [to_dp(gg[k], k) for k in range(2, n_dp)]
     lefts = [g[:1] for g in gg_dp]
     lefts += [to_oc(g, j + 1) for j, g in enumerate(gather_parts(gg_dp))]
-    image_attn = assemble(meta, back, order + [0], gg_dp[1:], image_local)
+    image_attn = assemble(where, back, order + [0], gg_dp[1:], image_local)
     text_attn = jnp.zeros((slot_local, inner_width), bf16)
     own_usable = part(slot_source[0] < caption_len[0], seq, slot_local, 0)
     for k, got in zip(order + [0], back):

time: 114 us -> 112 us (0.982)
  local copies, waits for them, and re-layouts: 10.9 us -> 9.02 us
  Pallas kernels: 22.1 us -> 20.6 us
    unnamed x30 -> x26, local copies, waits for them, and re-layouts: 10.8 us -> 8.9 us
    pallas_call x3, Pallas kernels: 5.41 us -> 3.94 us  [the longest x2 3.88 us: attention(): pl.pallas_call(functools.partial(attention_kernel, n_far, len(blocks), le...]
  transfers between devices with their start and end apart: 27 -> 27, of which waited for: 12 -> 12; matrix products, arithmetic and copies ran while one was open for 1% -> 1% of each run, Pallas kernels for 12% -> 11%
where the time goes in v13:
time: 112 us; the launch traced here: 111 us
  waiting for transfers between devices  50.9 us (45%)
  starting transfers between devices  28.3 us (25%)
  Pallas kernels  20.6 us (18%)
  local copies, waits for them, and re-layouts  9.02 us (8%)
  between operations  1.59 us (1%)
    ppermute x14, waiting for transfers between devices, to_z(): return lax.ppermute(x, 'seq', perm)  42.3 us
    ppermute x14, starting transfers between devices, to_z(): return lax.ppermute(x, 'seq', perm)  18.6 us
    unnamed x26, local copies, waits for them, and re-layouts  8.9 us
    ppermute x6, starting transfers between devices, to_dp(): return lax.ppermute(x, 'dp', [(a, a ^ k) for a in range(n_dp)])  8.07 us
    ppermute x6, waiting for transfers between devices, to_dp(): return lax.ppermute(x, 'dp', [(a, a ^ k) for a in range(n_dp)])  6.93 us
    pallas_call x1, Pallas kernels, text_project(): pl.pallas_call(functools.partial(text_kernel, groups, heads, place_of, wh...  5.66 us
    pallas_call x1, Pallas kernels, project(): pl.pallas_call(functools.partial(project_kernel, groups, parts, place_of)...  5.65 us
    pallas_call x2, Pallas kernels, attention(): pl.pallas_call(functools.partial(attention_kernel, n_far, len(blocks), le...  3.88 us
  transfers between devices with their start and end apart: 27, of which 12 were waited for; matrix products, arithmetic and copies ran while one was open for 1% of the time, Pallas kernels for 11%

profile of v13, /device:TPU:0, one launch (start us, length us, event | category | flops | bytes accessed | tf_op | source)
XLA Modules:
  0.0 111.4 jit_solution(8360617622091779622)
XLA Ops:
  1.4 5.7 %shard_map.164 = (f32[4,336,128]{2,1,0:T(8,128)}, bf16[1152,128]{1,0:T(8,128)(2,1)}, bf16[1152,128]{1,0:T(8,128)(2,1)}, bf16[1152,128]{1,0:T(8,128)(2,1)}, bf16[...) custom-call(s32[1]{0:T(128)} %copy.22.len_ref, s32[1,64]{1,0:T(1,128)} %src_ref.1, bf16[64,512]{1,0:T(8,128)(2,1)} %bitcast.36, ...), custom_call_target="tpu_custom_call" | custom-call | flops 301989888 | bytes 4718592 | tf_op jit(solution)/shard_map/pallas_call | solution.py:133
  7.1 0.5 collective-permute-start
  7.6 3.7 %collective-permute-start.3 = (bf16[1152,128]{1,0:T(8,128)(2,1)}, bf16[1152,128]{1,0:T(8,128)(2,1)S(1)}, u32[]{:S(2)}, u32[]{:S(2)}) collective-permute-start(bf16[1152,128]{1,0:T(8,128)(2,1)} %get-tuple-element.50), channel_id=1, source_target_pairs={{0,4},{2,6},{4,0},{6,2},{1,5},{3,7},{5,1},{7,3},{8,12},{10,14},{12... | collective-permute-start | bytes 884744 | tf_op jit(solution)/shard_map/ppermute | solution.py:615
  11.2 1.4 %collective-permute-start.4 = (bf16[1152,128]{1,0:T(8,128)(2,1)}, bf16[1152,128]{1,0:T(8,128)(2,1)S(1)}, u32[]{:S(2)}, u32[]{:S(2)}) collective-permute-start(bf16[1152,128]{1,0:T(8,128)(2,1)} %get-tuple-element.51), channel_id=1, source_target_pairs={{0,6},{2,4},{4,2},{6,0},{1,7},{3,5},{5,3},{7,1},{8,14},{10,12},{12... | collective-permute-start | bytes 884744 | tf_op jit(solution)/shard_map/ppermute | solution.py:615
  12.8 1.1 copy-done.2
  14.1 1.9 %collective-permute-start.1 = (bf16[2,320,128]{2,1,0:T(8,128)(2,1)S(1)}, bf16[2,320,128]{2,1,0:T(8,128)(2,1)S(1)}, u32[]{:S(2)}, u32[]{:S(2)}) collective-permute-start(bf16[2,320,128]{2,1,0:T(8,128)(2,1)S(1)} %get-tuple-element.46), channel_id=1, source_target_pairs={{0,2},{2,0},{4,6},{6,4},{1,3},{3,1},{5,7},{7,5},{8,10},{10,8},{12,... | collective-permute-start | bytes 491528 | tf_op jit(solution)/shard_map/ppermute | solution.py:615
  16.0 0.6 pad_add_fusion.meta_ref
  16.6 2.3 %shard_map.167 = (bf16[2,4,96,128]{3,2,1,0:T(8,128)(2,1)}, bf16[2,4,96,128]{3,2,1,0:T(8,128)(2,1)}, bf16[2,4,96,128]{3,2,1,0:T(8,128)(2,1)}, bf16[2,4,96,128]{3,2,1,0:T(8,128)(2,1)}) custom-call(s32[3]{0:T(128)} %pad_add_fusion.meta_ref, f32[1,3072]{1,0:T(1,128)} %gate_ref.3, bf16[128,3072]{1,0:T(8,128)(2,1)} %bitcast.31), custom_call_target="tpu_custom_call" | custom-call | bytes 1572864 | tf_op jit(solution)/shard_map/pallas_call | solution.py:356
  18.9 1.5 %collective-permute-start.6 = (bf16[2,4,96,128]{3,2,1,0:T(8,128)(2,1)}, bf16[2,4,96,128]{3,2,1,0:T(8,128)(2,1)S(1)}, u32[]{:S(2)}, u32[]{:S(2)}) collective-permute-start(bf16[2,4,96,128]{3,2,1,0:T(8,128)(2,1)} %get-tuple-element.53), channel_id=1, source_target_pairs={{0,8},{8,0},{16,24},{24,16},{1,9},{9,1},{17,25},{25,17},{2,10},{10... | collective-permute-start | bytes 589832 | tf_op jit(solution)/shard_map/ppermute | solution.py:622
  20.4 16.2 %collective-permute-done.1.refs_0_ = bf16[2,320,128]{2,1,0:T(8,128)(2,1)S(1)} collective-permute-done((bf16[2,320,128]{2,1,0:T(8,128)(2,1)S(1)}, bf16[2,320,128]{2,1,0:T(8,128)(2,1)S(1)}, u32[]{:S(2)}, u32[]{:S(2)}) %collective-permute-start.1) | collective-permute-done | bytes 163872 | tf_op jit(solution)/shard_map/ppermute | solution.py:615
  36.7 1.7 %collective-permute-start.2 = (bf16[1,320,128]{2,1,0:T(8,128)(2,1)S(1)}, bf16[1,320,128]{2,1,0:T(8,128)(2,1)S(1)}, u32[]{:S(2)}, u32[]{:S(2)}) collective-permute-start(bf16[1,320,128]{2,1,0:T(8,128)(2,1)S(1)} %get-tuple-element.48), channel_id=1, source_target_pairs={{0,4},{2,6},{4,0},{6,2},{1,5},{3,7},{5,1},{7,3},{8,12},{10,14},{12... | collective-permute-start | bytes 245768 | tf_op jit(solution)/shard_map/ppermute | solution.py:615
  38.5 4.6 %collective-permute-done.2.got_ref = bf16[1,320,128]{2,1,0:T(8,128)(2,1)S(1)} collective-permute-done((bf16[1,320,128]{2,1,0:T(8,128)(2,1)S(1)}, bf16[1,320,128]{2,1,0:T(8,128)(2,1)S(1)}, u32[]{:S(2)}, u32[]{:S(2)}) %collective-permute-start.2) | collective-permute-done | bytes 81952 | tf_op jit(solution)/shard_map/ppermute | solution.py:615
  43.0 1.0 copy-done.4
  44.0 0.3 shard_map.168
  44.2 0.7 copy-done.5
  44.9 0.6 copy-done.7
  45.6 1.6 %collective-permute-start.11 = (bf16[2,4,96,128]{3,2,1,0:T(8,128)(2,1)}, bf16[2,4,96,128]{3,2,1,0:T(8,128)(2,1)S(1)}, u32[]{:S(2)}, u32[]{:S(2)}) collective-permute-start(bf16[2,4,96,128]{3,2,1,0:T(8,128)(2,1)} %get-tuple-element.62), channel_id=1, source_target_pairs={{0,16},{8,24},{16,0},{24,8},{1,17},{9,25},{17,1},{25,9},{2,18},{10... | collective-permute-start | bytes 589832 | tf_op jit(solution)/shard_map/ppermute | solution.py:622
  47.2 1.4 %collective-permute-start.12 = (bf16[2,4,96,128]{3,2,1,0:T(8,128)(2,1)}, bf16[2,4,96,128]{3,2,1,0:T(8,128)(2,1)S(1)}, u32[]{:S(2)}, u32[]{:S(2)}) collective-permute-start(bf16[2,4,96,128]{3,2,1,0:T(8,128)(2,1)} %get-tuple-element.63), channel_id=1, source_target_pairs={{0,24},{8,16},{16,8},{24,0},{1,25},{9,17},{17,9},{25,1},{2,26},{10... | collective-permute-start | bytes 589832 | tf_op jit(solution)/shard_map/ppermute | solution.py:622
  48.7 0.9 copy-done.6
  49.6 2.0 %shard_map.169 = (bf16[128,384]{1,0:T(8,128)(2,1)S(1)}, bf16[128,384]{1,0:T(8,128)(2,1)S(1)}, bf16[32,384]{1,0:T(8,128)(2,1)S(1)}) custom-call(bf16[768,128]{1,0:T(8,128)(2,1)S(1)} %copy-done.6, bf16[3760,128]{1,0:T(8,128)(2,1)S(1)} %get-tuple-element.55.refs_1_, bf16[3760,128]{1,0:T(8,128)(2,1)S(1)} %collective-permute-done.7.refs_2_), custom_call_target="tpu_custom_call" | custom-call | flops 481296384 | bytes 2113536 | tf_op jit(solution)/shard_map/pallas_call | solution.py:296
  51.7 0.8 collective-permute-start.8
  52.5 2.1 %collective-permute-start.9 = (bf16[136,384]{1,0:T(8,128)(2,1)S(1)}, bf16[136,384]{1,0:T(8,128)(2,1)S(1)}, u32[]{:S(2)}, u32[]{:S(2)}) collective-permute-start(bf16[136,384]{1,0:T(8,128)(2,1)S(1)} %pad_maximum_fusion.1), channel_id=1, source_target_pairs={{0,6},{2,4},{4,2},{6,0},{1,7},{3,5},{5,3},{7,1},{8,14},{10,12},{12... | collective-permute-start | bytes 313352 | tf_op jit(solution)/shard_map/ppermute | solution.py:615
  54.5 0.9 copy-done.8
  55.4 1.9 %shard_map.170 = (bf16[128,384]{1,0:T(8,128)(2,1)S(1)}, bf16[128,384]{1,0:T(8,128)(2,1)S(1)}) custom-call(bf16[384,128]{1,0:T(8,128)(2,1)S(1)} %copy-done.8, bf16[3760,128]{1,0:T(8,128)(2,1)S(1)} %get-tuple-element.55.refs_1_, bf16[3760,128]{1,0:T(8,128)(2,1)S(1)} %collective-permute-done.7.refs_2_, bf16[32,384]{1,0:T(8,128)(2,1)S(1)} %get-tuple-element.57.refs_3_), custom_call_target="tpu_custom_call" | custom-call | flops 427819008 | bytes 2064384 | tf_op jit(solution)/shard_map/pallas_call | solution.py:296
  57.3 0.8 collective-permute-start.10
  58.2 3.9 %collective-permute-done.8.refs_0_ = bf16[136,384]{1,0:T(8,128)(2,1)S(1)} collective-permute-done((bf16[136,384]{1,0:T(8,128)(2,1)S(1)}, bf16[136,384]{1,0:T(8,128)(2,1)S(1)}, u32[]{:S(2)}, u32[]{:S(2)}) %collective-permute-start.8) | collective-permute-done | bytes 104480 | tf_op jit(solution)/shard_map/ppermute | solution.py:615
  62.2 1.9 %collective-permute-done.10.refs_2_ = bf16[136,384]{1,0:T(8,128)(2,1)S(1)} collective-permute-done((bf16[136,384]{1,0:T(8,128)(2,1)S(1)}, bf16[136,384]{1,0:T(8,128)(2,1)S(1)}, u32[]{:S(2)}, u32[]{:S(2)}) %collective-permute-start.10) | collective-permute-done | bytes 104480 | tf_op jit(solution)/shard_map/ppermute | solution.py:615
  64.4 2.2 %collective-permute-start.16 = (bf16[128,1536]{1,0:T(8,128)(2,1)S(1)}, bf16[128,1536]{1,0:T(8,128)(2,1)S(1)}, u32[]{:S(2)}, u32[]{:S(2)}) collective-permute-start(bf16[128,1536]{1,0:T(8,128)(2,1)S(1)} %shard_map.171.attn_ref.refs_5_), channel_id=1, source_target_pairs={{0,24},{8,16},{16,8},{24,0},{1,25},{9,17},{17,9},{25,1},{2,26},{10... | collective-permute-start | bytes 1179656 | tf_op jit(solution)/shard_map/ppermute | solution.py:622
  66.6 0.5 collective-permute-start.15
  67.1 0.9 collective-permute-start.14
  67.9 3.7 %copy-done = bf16[3072,1536]{1,0:T(8,128)(2,1)S(1)} copy-done((bf16[3072,1536]{1,0:T(8,128)(2,1)S(1)}, bf16[3072,1536]{1,0:T(8,128)(2,1)}, u32[]{:S(2)}) %copy-start) | copy-done | bytes 9437208
  71.6 5.6 %shard_map.172 = (bf16[128,3072]{1,0:T(8,128)(2,1)}, bf16[128,1536]{1,0:T(8,128)(2,1)}, f32[4,384]{1,0:T(4,128)S(1)}, bf16[144,1536]{1,0:T(8,128)(2,1)S(1)}) custom-call(s32[3]{0:T(128)S(1)} %copy-done.10, bf16[128,1536]{1,0:T(8,128)(2,1)S(1)} %shard_map.171.attn_ref.refs_5_, bf16[3072,1536]{1,0:T(8,128)(2,1)S(1)} %copy-done, f32[1,3072]{1,0:T(1,128)S(1)} %copy-done.9, ...), custom_call_target="tpu_custom_call" | custom-call | flops 2415919104 | bytes 9437184 | tf_op jit(solution)/shard_map/pallas_call | solution.py:437
  77.3 0.6 collective-permute-start.13
  78.0 6.8 %collective-permute-done.15.refs_7_ = bf16[128,1536]{1,0:T(8,128)(2,1)S(1)} collective-permute-done((bf16[128,1536]{1,0:T(8,128)(2,1)S(1)}, bf16[128,1536]{1,0:T(8,128)(2,1)S(1)}, u32[]{:S(2)}, u32[]{:S(2)}) %collective-permute-start.15) | collective-permute-done | bytes 393248 | tf_op jit(solution)/shard_map/ppermute | solution.py:622
  84.9 0.4 collective-permute-start.18
  85.4 1.1 %collective-permute-done.19.refs_11_ = bf16[128,1536]{1,0:T(8,128)(2,1)S(1)} collective-permute-done((bf16[128,1536]{1,0:T(8,128)(2,1)S(1)}, bf16[128,1536]{1,0:T(8,128)(2,1)S(1)}, u32[]{:S(2)}, u32[]{:S(2)}) %collective-permute-start.19) | collective-permute-done | bytes 393248 | tf_op jit(solution)/shard_map/ppermute | solution.py:619
  86.5 0.6 collective-permute-done.18.refs_10_
  87.1 1.4 %shard_map.174 = (f32[1168,128]{1,0:T(8,128)S(1)}, bf16[576,128]{1,0:T(8,128)(2,1)S(1)}, bf16[592,128]{1,0:T(8,128)(2,1)S(1)}, f32[576,128]{1,0:T(8,128)S(1)}, f...) custom-call(bf16[1,4,96,128]{3,2,1,0:T(8,128)(2,1)S(1)} %slice.24.refs_0_, ...), custom_call_target="tpu_custom_call" | custom-call | flops 1207959552 | bytes 5111808 | tf_op jit(solution)/shard_map/pallas_call | solution.py:513
  88.5 0.8 collective-permute-start.23
  89.2 1.3 %collective-permute-start.21 = (bf16[576,128]{1,0:T(8,128)(2,1)S(1)}, bf16[576,128]{1,0:T(8,128)(2,1)S(1)}, u32[]{:S(2)}, u32[]{:S(2)}) collective-permute-start(bf16[576,128]{1,0:T(8,128)(2,1)S(1)} %get-tuple-element.71), channel_id=1, source_target_pairs={{0,2},{2,0},{4,6},{6,4},{1,3},{3,1},{5,7},{7,5},{8,10},{10,8},{12,... | collective-permute-start | bytes 442376 | tf_op jit(solution)/shard_map/ppermute | solution.py:615
  90.6 4.8 %collective-permute-done.23.got_ref = bf16[592,128]{1,0:T(8,128)(2,1)S(1)} collective-permute-done((bf16[592,128]{1,0:T(8,128)(2,1)S(1)}, bf16[592,128]{1,0:T(8,128)(2,1)S(1)}, u32[]{:S(2)}, u32[]{:S(2)}) %collective-permute-start.23) | collective-permute-done | bytes 151584 | tf_op jit(solution)/shard_map/ppermute | solution.py:615
  95.4 0.9 collective-permute-start.24
  96.3 1.3 %collective-permute-start.26 = (bf16[592,128]{1,0:T(8,128)(2,1)S(1)}, bf16[592,128]{1,0:T(8,128)(2,1)S(1)}, u32[]{:S(2)}, u32[]{:S(2)}) collective-permute-start(bf16[592,128]{1,0:T(8,128)(2,1)S(1)} %get-tuple-element.78), channel_id=1, source_target_pairs={{0,2},{2,0},{4,6},{6,4},{1,3},{3,1},{5,7},{7,5},{8,10},{10,8},{12,... | collective-permute-start | bytes 454664 | tf_op jit(solution)/shard_map/ppermute | solution.py:615
  97.6 1.1 collective-permute-done.21.got_ref
  98.8 0.4 collective-permute-start.22
  99.2 1.4 %collective-permute-start.25 = (bf16[576,128]{1,0:T(8,128)(2,1)S(1)}, bf16[576,128]{1,0:T(8,128)(2,1)S(1)}, u32[]{:S(2)}, u32[]{:S(2)}) collective-permute-start(bf16[576,128]{1,0:T(8,128)(2,1)S(1)} %get-tuple-element.77), channel_id=1, source_target_pairs={{0,2},{2,0},{4,6},{6,4},{1,3},{3,1},{5,7},{7,5},{8,10},{10,8},{12,... | collective-permute-start | bytes 442376 | tf_op jit(solution)/shard_map/ppermute | solution.py:615
  100.6 9.9 %collective-permute-done.22.far_low = bf16[576,128]{1,0:T(8,128)(2,1)S(1)} collective-permute-done((bf16[576,128]{1,0:T(8,128)(2,1)S(1)}, bf16[576,128]{1,0:T(8,128)(2,1)S(1)}, u32[]{:S(2)}, u32[]{:S(2)}) %collective-permute-start.22) | collective-permute-done | bytes 147488 | tf_op jit(solution)/shard_map/ppermute | solution.py:615
  110.5 0.9 shard_map.177
  (63 shorter events, 1.6 us)
Async XLA Ops:
  0.6 48.0 %copy-start.12 = (s32[1,64]{1,0:T(1,128)S(1)}, s32[1,64]{1,0:T(1,128)}, u32[]{:S(2)}) copy-start(s32[1,64]{1,0:T(1,128)} %src_ref.1) | copy-start | bytes 772
  0.6 67.3 %copy-start.9 = (f32[1,3072]{1,0:T(1,128)S(1)}, f32[1,3072]{1,0:T(1,128)}, u32[]{:S(2)}) copy-start(f32[1,3072]{1,0:T(1,128)} %gate_ref.3) | copy-start | bytes 36868
  0.7 67.3 %copy-start.1 = (bf16[1,128,3072]{2,1,0:T(8,128)(2,1)S(1)}, bf16[1,128,3072]{2,1,0:T(8,128)(2,1)}, u32[]{:S(2)}) copy-start(bf16[1,128,3072]{2,1,0:T(8,128)(2,1)} %param.25) | copy-start | bytes 2359300
  7.1 5.8 %collective-permute-start = (bf16[4,320,128]{2,1,0:T(8,128)(2,1)}, bf16[4,320,128]{2,1,0:T(8,128)(2,1)S(1)}, u32[]{:S(2)}, u32[]{:S(2)}) collective-permute-start(bf16[4,320,128]{2,1,0:T(8,128)(2,1)} %get-tuple-element.44), channel_id=1, source_target_pairs={{0,1},{2,3},{4,5},{6,7},{1,0},{3,2},{5,4},{7,6},{8,9},{10,11},{12,... | collective-permute-start | bytes 983048 | tf_op jit(solution)/shard_map/ppermute | solution.py:619
  7.6 30.9 %collective-permute-start.3 = (bf16[1152,128]{1,0:T(8,128)(2,1)}, bf16[1152,128]{1,0:T(8,128)(2,1)S(1)}, u32[]{:S(2)}, u32[]{:S(2)}) collective-permute-start(bf16[1152,128]{1,0:T(8,128)(2,1)} %get-tuple-element.50), channel_id=1, source_target_pairs={{0,4},{2,6},{4,0},{6,2},{1,5},{3,7},{5,1},{7,3},{8,12},{10,14},{12... | collective-permute-start | bytes 884744 | tf_op jit(solution)/shard_map/ppermute | solution.py:615
  11.2 27.2 %collective-permute-start.4 = (bf16[1152,128]{1,0:T(8,128)(2,1)}, bf16[1152,128]{1,0:T(8,128)(2,1)S(1)}, u32[]{:S(2)}, u32[]{:S(2)}) collective-permute-start(bf16[1152,128]{1,0:T(8,128)(2,1)} %get-tuple-element.51), channel_id=1, source_target_pairs={{0,6},{2,4},{4,2},{6,0},{1,7},{3,5},{5,3},{7,1},{8,14},{10,12},{12... | collective-permute-start | bytes 884744 | tf_op jit(solution)/shard_map/ppermute | solution.py:615
  12.6 25.9 %collective-permute-start.5 = (bf16[1152,128]{1,0:T(8,128)(2,1)}, bf16[1152,128]{1,0:T(8,128)(2,1)S(1)}, u32[]{:S(2)}, u32[]{:S(2)}) collective-permute-start(bf16[1152,128]{1,0:T(8,128)(2,1)} %get-tuple-element.52), channel_id=1, source_target_pairs={{0,2},{2,0},{4,6},{6,4},{1,3},{3,1},{5,7},{7,5},{8,10},{10,8},{12,... | collective-permute-start | bytes 884744 | tf_op jit(solution)/shard_map/ppermute | solution.py:615
  12.8 1.1 copy-start.2
  14.1 22.5 %collective-permute-start.1 = (bf16[2,320,128]{2,1,0:T(8,128)(2,1)S(1)}, bf16[2,320,128]{2,1,0:T(8,128)(2,1)S(1)}, u32[]{:S(2)}, u32[]{:S(2)}) collective-permute-start(bf16[2,320,128]{2,1,0:T(8,128)(2,1)S(1)} %get-tuple-element.46), channel_id=1, source_target_pairs={{0,2},{2,0},{4,6},{6,4},{1,3},{3,1},{5,7},{7,5},{8,10},{10,8},{12,... | collective-permute-start | bytes 491528 | tf_op jit(solution)/shard_map/ppermute | solution.py:615
  16.6 51.3 %copy-start.10 = (s32[3]{0:T(128)S(1)}, s32[3]{0:T(128)}, u32[]{:S(2)}) copy-start(s32[3]{0:T(128)} %pad_add_fusion.meta_ref) | copy-start | bytes 40
  18.9 19.5 %collective-permute-start.6 = (bf16[2,4,96,128]{3,2,1,0:T(8,128)(2,1)}, bf16[2,4,96,128]{3,2,1,0:T(8,128)(2,1)S(1)}, u32[]{:S(2)}, u32[]{:S(2)}) collective-permute-start(bf16[2,4,96,128]{3,2,1,0:T(8,128)(2,1)} %get-tuple-element.53), channel_id=1, source_target_pairs={{0,8},{8,0},{16,24},{24,16},{1,9},{9,1},{17,25},{25,17},{2,10},{10... | collective-permute-start | bytes 589832 | tf_op jit(solution)/shard_map/ppermute | solution.py:622
  36.7 6.3 %collective-permute-start.2 = (bf16[1,320,128]{2,1,0:T(8,128)(2,1)S(1)}, bf16[1,320,128]{2,1,0:T(8,128)(2,1)S(1)}, u32[]{:S(2)}, u32[]{:S(2)}) collective-permute-start(bf16[1,320,128]{2,1,0:T(8,128)(2,1)S(1)} %get-tuple-element.48), channel_id=1, source_target_pairs={{0,4},{2,6},{4,0},{6,2},{1,5},{3,7},{5,1},{7,3},{8,12},{10,14},{12... | collective-permute-start | bytes 245768 | tf_op jit(solution)/shard_map/ppermute | solution.py:615
  43.0 1.0 copy-start.4
  44.0 33.3 %copy-start.3 = (bf16[2,4,96,128]{3,2,1,0:T(8,128)(2,1)S(1)}, bf16[2,4,96,128]{3,2,1,0:T(8,128)(2,1)}, u32[]{:S(2)}) copy-start(bf16[2,4,96,128]{3,2,1,0:T(8,128)(2,1)} %get-tuple-element.66.refs_0_) | copy-start | bytes 589828
  44.2 0.7 copy-start.5
  44.9 0.6 copy-start.7
  45.6 3.1 %collective-permute-start.7 = (bf16[3760,128]{1,0:T(8,128)(2,1)S(1)}, bf16[3760,128]{1,0:T(8,128)(2,1)S(1)}, u32[]{:S(2)}, u32[]{:S(2)}) collective-permute-start(bf16[3760,128]{1,0:T(8,128)(2,1)S(1)} %get-tuple-element.55.refs_1_), channel_id=1, source_target_pairs={{0,1},{2,3},{4,5},{6,7},{1,0},{3,2},{5,4},{7,6},{8,9},{10,11},{12,... | collective-permute-start | bytes 2887688 | tf_op jit(solution)/shard_map/ppermute | solution.py:619
  45.6 18.7 %collective-permute-start.11 = (bf16[2,4,96,128]{3,2,1,0:T(8,128)(2,1)}, bf16[2,4,96,128]{3,2,1,0:T(8,128)(2,1)S(1)}, u32[]{:S(2)}, u32[]{:S(2)}) collective-permute-start(bf16[2,4,96,128]{3,2,1,0:T(8,128)(2,1)} %get-tuple-element.62), channel_id=1, source_target_pairs={{0,16},{8,24},{16,0},{24,8},{1,17},{9,25},{17,1},{25,9},{2,18},{10... | collective-permute-start | bytes 589832 | tf_op jit(solution)/shard_map/ppermute | solution.py:622
  47.2 17.1 %collective-permute-start.12 = (bf16[2,4,96,128]{3,2,1,0:T(8,128)(2,1)}, bf16[2,4,96,128]{3,2,1,0:T(8,128)(2,1)S(1)}, u32[]{:S(2)}, u32[]{:S(2)}) collective-permute-start(bf16[2,4,96,128]{3,2,1,0:T(8,128)(2,1)} %get-tuple-element.63), channel_id=1, source_target_pairs={{0,24},{8,16},{16,8},{24,0},{1,25},{9,17},{17,9},{25,1},{2,26},{10... | collective-permute-start | bytes 589832 | tf_op jit(solution)/shard_map/ppermute | solution.py:622
  48.7 0.9 copy-start.6
  51.7 10.3 %collective-permute-start.8 = (bf16[136,384]{1,0:T(8,128)(2,1)S(1)}, bf16[136,384]{1,0:T(8,128)(2,1)S(1)}, u32[]{:S(2)}, u32[]{:S(2)}) collective-permute-start(bf16[136,384]{1,0:T(8,128)(2,1)S(1)} %pad_maximum_fusion), channel_id=1, source_target_pairs={{0,4},{2,6},{4,0},{6,2},{1,5},{3,7},{5,1},{7,3},{8,12},{10,14},{12... | collective-permute-start | bytes 313352 | tf_op jit(solution)/shard_map/ppermute | solution.py:615
  52.5 9.6 %collective-permute-start.9 = (bf16[136,384]{1,0:T(8,128)(2,1)S(1)}, bf16[136,384]{1,0:T(8,128)(2,1)S(1)}, u32[]{:S(2)}, u32[]{:S(2)}) collective-permute-start(bf16[136,384]{1,0:T(8,128)(2,1)S(1)} %pad_maximum_fusion.1), channel_id=1, source_target_pairs={{0,6},{2,4},{4,2},{6,0},{1,7},{3,5},{5,3},{7,1},{8,14},{10,12},{12... | collective-permute-start | bytes 313352 | tf_op jit(solution)/shard_map/ppermute | solution.py:615
  54.5 0.9 copy-start.8
  57.3 6.8 %collective-permute-start.10 = (bf16[136,384]{1,0:T(8,128)(2,1)S(1)}, bf16[136,384]{1,0:T(8,128)(2,1)S(1)}, u32[]{:S(2)}, u32[]{:S(2)}) collective-permute-start(bf16[136,384]{1,0:T(8,128)(2,1)S(1)} %pad_maximum_fusion.2), channel_id=1, source_target_pairs={{0,2},{2,0},{4,6},{6,4},{1,3},{3,1},{5,7},{7,5},{8,10},{10,8},{12,... | collective-permute-start | bytes 313352 | tf_op jit(solution)/shard_map/ppermute | solution.py:615
  64.3 31.1 %copy-start.11 = (bf16[1,8,1536]{2,1,0:T(8,128)(2,1)}, bf16[1,8,1536]{2,1,0:T(8,128)(2,1)S(1)}, u32[]{:S(2)}) copy-start(bf16[1,8,1536]{2,1,0:T(8,128)(2,1)S(1)} %get-tuple-element.81) | copy-start | bytes 73732
  64.4 13.5 %collective-permute-start.16 = (bf16[128,1536]{1,0:T(8,128)(2,1)S(1)}, bf16[128,1536]{1,0:T(8,128)(2,1)S(1)}, u32[]{:S(2)}, u32[]{:S(2)}) collective-permute-start(bf16[128,1536]{1,0:T(8,128)(2,1)S(1)} %shard_map.171.attn_ref.refs_5_), channel_id=1, source_target_pairs={{0,24},{8,16},{16,8},{24,0},{1,25},{9,17},{17,9},{25,1},{2,26},{10... | collective-permute-start | bytes 1179656 | tf_op jit(solution)/shard_map/ppermute | solution.py:622
  66.6 18.2 %collective-permute-start.15 = (bf16[128,1536]{1,0:T(8,128)(2,1)S(1)}, bf16[128,1536]{1,0:T(8,128)(2,1)S(1)}, u32[]{:S(2)}, u32[]{:S(2)}) collective-permute-start(bf16[128,1536]{1,0:T(8,128)(2,1)S(1)} %shard_map.171.attn_ref.refs_5_), channel_id=1, source_target_pairs={{0,16},{8,24},{16,0},{24,8},{1,17},{9,25},{17,1},{25,9},{2,18},{10... | collective-permute-start | bytes 1179656 | tf_op jit(solution)/shard_map/ppermute | solution.py:622
  67.1 17.8 %collective-permute-start.14 = (bf16[128,1536]{1,0:T(8,128)(2,1)S(1)}, bf16[128,1536]{1,0:T(8,128)(2,1)S(1)}, u32[]{:S(2)}, u32[]{:S(2)}) collective-permute-start(bf16[128,1536]{1,0:T(8,128)(2,1)S(1)} %shard_map.171.attn_ref.refs_5_), channel_id=1, source_target_pairs={{0,8},{8,0},{16,24},{24,16},{1,9},{9,1},{17,25},{25,17},{2,10},{10... | collective-permute-start | bytes 1179656 | tf_op jit(solution)/shard_map/ppermute | solution.py:622
  67.9 3.7 %copy-start = (bf16[3072,1536]{1,0:T(8,128)(2,1)S(1)}, bf16[3072,1536]{1,0:T(8,128)(2,1)}, u32[]{:S(2)}) copy-start(bf16[3072,1536]{1,0:T(8,128)(2,1)} %w_ref.3) | copy-start | bytes 28311556
  77.3 8.1 %collective-permute-start.17 = (bf16[144,1536]{1,0:T(8,128)(2,1)S(1)}, bf16[144,1536]{1,0:T(8,128)(2,1)S(1)}, u32[]{:S(2)}, u32[]{:S(2)}) collective-permute-start(bf16[144,1536]{1,0:T(8,128)(2,1)S(1)} %get-tuple-element.67), channel_id=1, source_target_pairs={{0,1},{2,3},{4,5},{6,7},{1,0},{3,2},{5,4},{7,6},{8,9},{10,11},{12,... | collective-permute-start | bytes 1327112 | tf_op jit(solution)/shard_map/ppermute | solution.py:619
  77.3 8.1 %collective-permute-start.13 = (bf16[4,4,96,128]{3,2,1,0:T(8,128)(2,1)S(1)}, bf16[4,4,96,128]{3,2,1,0:T(8,128)(2,1)S(1)}, u32[]{:S(2)}, u32[]{:S(2)}) collective-permute-start(bf16[4,4,96,128]{3,2,1,0:T(8,128)(2,1)S(1)} %shard_map.173), channel_id=1, source_target_pairs={{0,1},{2,3},{4,5},{6,7},{1,0},{3,2},{5,4},{7,6},{8,9},{10,11},{12,... | collective-permute-start | bytes 1179656 | tf_op jit(solution)/shard_map/ppermute | solution.py:619
  77.9 7.5 %collective-permute-start.20 = (bf16[128,1536]{1,0:T(8,128)(2,1)S(1)}, bf16[128,1536]{1,0:T(8,128)(2,1)S(1)}, u32[]{:S(2)}, u32[]{:S(2)}) collective-permute-start(bf16[128,1536]{1,0:T(8,128)(2,1)S(1)} %collective-permute-done.16.refs_8_), channel_id=1, source_target_pairs={{0,1},{2,3},{4,5},{6,7},{1,0},{3,2},{5,4},{7,6},{8,9},{10,11},{12,... | collective-permute-start | bytes 1179656 | tf_op jit(solution)/shard_map/ppermute | solution.py:619
  84.8 1.7 %collective-permute-start.19 = (bf16[128,1536]{1,0:T(8,128)(2,1)S(1)}, bf16[128,1536]{1,0:T(8,128)(2,1)S(1)}, u32[]{:S(2)}, u32[]{:S(2)}) collective-permute-start(bf16[128,1536]{1,0:T(8,128)(2,1)S(1)} %collective-permute-done.15.refs_7_), channel_id=1, source_target_pairs={{0,1},{2,3},{4,5},{6,7},{1,0},{3,2},{5,4},{7,6},{8,9},{10,11},{12,... | collective-permute-start | bytes 1179656 | tf_op jit(solution)/shard_map/ppermute | solution.py:619
  84.9 2.2 %collective-permute-start.18 = (bf16[128,1536]{1,0:T(8,128)(2,1)S(1)}, bf16[128,1536]{1,0:T(8,128)(2,1)S(1)}, u32[]{:S(2)}, u32[]{:S(2)}) collective-permute-start(bf16[128,1536]{1,0:T(8,128)(2,1)S(1)} %collective-permute-done.14.refs_6_), channel_id=1, source_target_pairs={{0,1},{2,3},{4,5},{6,7},{1,0},{3,2},{5,4},{7,6},{8,9},{10,11},{12,... | collective-permute-start | bytes 1179656 | tf_op jit(solution)/shard_map/ppermute | solution.py:619
  88.5 6.8 %collective-permute-start.23 = (bf16[592,128]{1,0:T(8,128)(2,1)S(1)}, bf16[592,128]{1,0:T(8,128)(2,1)S(1)}, u32[]{:S(2)}, u32[]{:S(2)}) collective-permute-start(bf16[592,128]{1,0:T(8,128)(2,1)S(1)} %get-tuple-element.73), channel_id=1, source_target_pairs={{0,2},{2,0},{4,6},{6,4},{1,3},{3,1},{5,7},{7,5},{8,10},{10,8},{12,... | collective-permute-start | bytes 454664 | tf_op jit(solution)/shard_map/ppermute | solution.py:615
  89.2 9.5 %collective-permute-start.21 = (bf16[576,128]{1,0:T(8,128)(2,1)S(1)}, bf16[576,128]{1,0:T(8,128)(2,1)S(1)}, u32[]{:S(2)}, u32[]{:S(2)}) collective-permute-start(bf16[576,128]{1,0:T(8,128)(2,1)S(1)} %get-tuple-element.71), channel_id=1, source_target_pairs={{0,2},{2,0},{4,6},{6,4},{1,3},{3,1},{5,7},{7,5},{8,10},{10,8},{12,... | collective-permute-start | bytes 442376 | tf_op jit(solution)/shard_map/ppermute | solution.py:615
  95.4 15.1 %collective-permute-start.24 = (bf16[592,128]{1,0:T(8,128)(2,1)S(1)}, bf16[592,128]{1,0:T(8,128)(2,1)S(1)}, u32[]{:S(2)}, u32[]{:S(2)}) collective-permute-start(bf16[592,128]{1,0:T(8,128)(2,1)S(1)} %get-tuple-element.76), channel_id=1, source_target_pairs={{0,4},{2,6},{4,0},{6,2},{1,5},{3,7},{5,1},{7,3},{8,12},{10,14},{12... | collective-permute-start | bytes 454664 | tf_op jit(solution)/shard_map/ppermute | solution.py:615
  96.3 14.2 %collective-permute-start.26 = (bf16[592,128]{1,0:T(8,128)(2,1)S(1)}, bf16[592,128]{1,0:T(8,128)(2,1)S(1)}, u32[]{:S(2)}, u32[]{:S(2)}) collective-permute-start(bf16[592,128]{1,0:T(8,128)(2,1)S(1)} %get-tuple-element.78), channel_id=1, source_target_pairs={{0,2},{2,0},{4,6},{6,4},{1,3},{3,1},{5,7},{7,5},{8,10},{10,8},{12,... | collective-permute-start | bytes 454664 | tf_op jit(solution)/shard_map/ppermute | solution.py:615
  98.8 11.6 %collective-permute-start.22 = (bf16[576,128]{1,0:T(8,128)(2,1)S(1)}, bf16[576,128]{1,0:T(8,128)(2,1)S(1)}, u32[]{:S(2)}, u32[]{:S(2)}) collective-permute-start(bf16[576,128]{1,0:T(8,128)(2,1)S(1)} %shard_map.175), channel_id=1, source_target_pairs={{0,4},{2,6},{4,0},{6,2},{1,5},{3,7},{5,1},{7,3},{8,12},{10,14},{12... | collective-permute-start | bytes 442376 | tf_op jit(solution)/shard_map/ppermute | solution.py:615
  99.2 11.3 %collective-permute-start.25 = (bf16[576,128]{1,0:T(8,128)(2,1)S(1)}, bf16[576,128]{1,0:T(8,128)(2,1)S(1)}, u32[]{:S(2)}, u32[]{:S(2)}) collective-permute-start(bf16[576,128]{1,0:T(8,128)(2,1)S(1)} %get-tuple-element.77), channel_id=1, source_target_pairs={{0,2},{2,0},{4,6},{6,4},{1,3},{3,1},{5,7},{7,5},{8,10},{10,8},{12,... | collective-permute-start | bytes 442376 | tf_op jit(solution)/shard_map/ppermute | solution.py:615

commit v14 on v13

--- a/solution.py
+++ b/solution.py
@@ -186,23 +186,16 @@
 
 
 def block_kernel(features, heads, n_pieces, own_ref, got_ref, *refs):
-    pieces, (out_ref, first_ref, second_ref) = refs[:n_pieces], refs[-3:]
-    near_rows = pieces[0].shape[0]
-    kv_rows = near_rows // 3 * 2
-    out_ref[:near_rows, :] = pieces[0][...]
-    for k, ref in enumerate(pieces[1:]):
-        at = near_rows + k * kv_rows
-        out_ref[at : at + kv_rows, :] = ref[:kv_rows, :]
-    q_rows = near_rows - kv_rows
-    first_ref[:q_rows, :] = pieces[1][kv_rows:, :]
-    first_ref[q_rows:, :] = pieces[2][kv_rows:, :]
-    second_ref[...] = pieces[3][kv_rows:, :]
+    pieces, out_ref = refs[:n_pieces], refs[-1]
+    each = pieces[0].shape[0]
+    for k, ref in enumerate(pieces):
+        out_ref[k * each : (k + 1) * each, :] = ref[...]
     size = own_ref.shape[2]
     text_rows = got_ref.shape[1]
     rows = text_rows // (3 * heads + 1)
     total = own_ref[0, :text_rows, :] + got_ref[0].astype(f32)
     rate = lax.rsqrt(joined(total[3 * heads * rows :]) / features + eps_norm)
-    start = near_rows + (n_pieces - 1) * kv_rows
+    start = n_pieces * each
     for i in range(3):
         for head in range(heads):
             at = (i * heads + head) * rows
@@ -220,28 +213,25 @@
 def block_of(own, got, after, pieces, features, heads):
     rows, size = own.shape[1:]
     total = (rows - EXTRA) // (3 * heads + 1) * 3 * heads + EXTRA
-    q_rows = pieces[0].shape[0] // 3
-    total += q_rows * (2 * len(pieces) + 1)
+    total += pieces[0].shape[0] * len(pieces)
     return pl.pallas_call(
         functools.partial(block_kernel, features, heads, len(pieces)),
-        out_shape=[jax.ShapeDtypeStruct((n, size), bf16) for n in (total, 2 * q_rows, q_rows)],
+        out_shape=jax.ShapeDtypeStruct((total, size), bf16),
         in_specs=[VMEM] * (2 + len(pieces)) + [ANY] * len(after),
-        out_specs=[VMEM] * 3,
+        out_specs=VMEM,
         compiler_params=params(),
         cost_estimate=cost(0, 4 * total * size),
     )(own, got, *pieces, *after)
 
 
-def attention_kernel(n_far, n_cores, n_after, queries, heads, rows, text_rows, *refs):
-    far_ref, blocks = refs[0], refs[1 : 1 + n_cores]
-    out_refs = refs[1 + n_cores + n_after :]
+def attention_kernel(n_pieces, n_cores, n_after, asked_of, heads, rows, text_rows, *refs):
+    blocks, out_refs = refs[:n_cores], refs[n_cores + n_after :]
     size = blocks[0].shape[1]
     factor = size ** (-0.5) * math.log2(math.e)
     nt = (((1,), (1,)), ((), ()))
-    kv_rows = 2 * heads * rows
-    near_rows = 3 * heads * rows
-    starts = [0] + [near_rows + k * kv_rows for k in range(n_far)]
-    text = near_rows + n_far * kv_rows
+    each = 3 * heads * rows
+    starts = [k * each for k in range(n_pieces)]
+    text = n_pieces * each
     end = text + 3 * heads * text_rows
     bias = blocks[0][end : end + EXTRA, :][:1, : n_cores * text_rows].astype(f32)
 
@@ -260,15 +250,13 @@
         tkeys, tvalues = tkv[0], with_ones(tkv[1])
         cols = slice(head * size, (head + 1) * size)
         q_at = (2 * heads + head) * rows
-        asked = [
-            far_ref[(k * heads + head) * rows : (k * heads + head + 1) * rows, :]
-            for k in range(queries[0])
-        ]
-        if queries[1]:
-            asked.append(blocks[0][q_at : q_at + rows, :])
-        if queries[2]:
-            tq_at = text + head * text_rows
-            asked.append(blocks[0][tq_at : tq_at + text_rows, :])
+        asked = []
+        for k in asked_of:
+            if k < n_pieces:
+                asked.append(blocks[0][starts[k] + q_at : starts[k] + q_at + rows, :])
+            else:
+                tq_at = text + head * text_rows
+                asked.append(blocks[0][tq_at : tq_at + text_rows, :])
         q = jnp.concatenate(asked, axis=0)
         s_img = lax.dot_general(q, keys, nt, preferred_element_type=f32)
         s_txt = lax.dot_general(q, tkeys, nt, preferred_element_type=f32) + bias
@@ -286,26 +274,25 @@
             at += out_ref.shape[0]
 
 
-def attention(far, near, text, blocks, after, n_far, heads, rows, text_rows):
+def attention(blocks, asked_of, after, n_pieces, heads, rows, text_rows):
     size = blocks[0].shape[1]
-    asked = far.shape[0] // (heads * rows)
-    counts = [rows] * (asked + near) + [text_rows] * text
+    counts = [rows if k < n_pieces else text_rows for k in asked_of]
     queries = sum(counts)
-    keys = len(blocks) * ((n_far + 1) * rows + text_rows)
+    keys = len(blocks) * (n_pieces * rows + text_rows)
     shapes = [jax.ShapeDtypeStruct((n, heads * size), bf16) for n in counts]
     return pl.pallas_call(
         functools.partial(
             attention_kernel,
-            n_far,
+            n_pieces,
             len(blocks),
             len(after),
-            (asked, near, text),
+            tuple(asked_of),
             heads,
             rows,
             text_rows,
         ),
         out_shape=shapes,
-        in_specs=[VMEM] * (1 + len(blocks)) + [ANY] * len(after),
+        in_specs=[VMEM] * len(blocks) + [ANY] * len(after),
         out_specs=[VMEM] * len(shapes),
         compiler_params=params(),
         cost_estimate=cost(
@@ -313,7 +300,7 @@
             4 * (queries + keys) * heads * size,
             queries * keys * heads,
         ),
-    )(far, *blocks, *after)
+    )(*blocks, *after)
 
 
 def assemble_kernel(places, where, *refs):
@@ -653,16 +640,15 @@
 
     gg = gated_parts(meta, gate, d_out[0], n_dp, G, OC, place)
     gg_dp = [gg[0], to_dp(gg[1], 1)]
-    block, far_first, far_second = block_of(own, got, gg_dp[1:], images, DT5, heads)
+    block = block_of(own, got, gg_dp[1:], images, DT5, heads)
     blocks = [block] + [to_oc(block, j) for j in range(1, OC)]
     *first, text_out = attention(
-        far_first, 0, 1, blocks, [], G - 1, heads, image_local, text_rows
+        blocks, [1, 2, G], [], G, heads, image_local, text_rows
     )
     second = attention(
-        far_second, 1, 0, blocks, [text_out], G - 1, heads, image_local, text_rows
-    )
-    second = list(second)
-    outs = dict(zip(order + [0], first + second))
+        blocks, [3, 0], [text_out], G, heads, image_local, text_rows
+    )
+    outs = dict(zip(order + [0], first + list(second)))
 
     back = {}
     for k in order + [0]:

time: 112 us -> 110 us (0.982)
  waiting for transfers between devices: 50.9 us -> 49 us
  local copies, waits for them, and re-layouts: 9.02 us -> 7.67 us
    unnamed x26 -> x18, local copies, waits for them, and re-layouts: 8.9 us -> 5.76 us
    slice x4, local copies, waits for them, and re-layouts: 0.03 us -> 1.81 us  [on_device(): lefts = [g[:1] for g in gg_dp]]
    ppermute x7, waiting for transfers between devices: 1.7 us -> 0.02 us  [to_oc(): return lax.ppermute(x, 'seq', perm)]
  transfers between devices with their start and end apart: 27 -> 27, of which waited for: 12 -> 10; matrix products, arithmetic and copies ran while one was open for 1% -> 3% of each run, Pallas kernels for 11% -> 12%
where the time goes in v14:
time: 110 us; the launch traced here: 109 us
  waiting for transfers between devices  49 us (45%)
  starting transfers between devices  28.6 us (26%)
  Pallas kernels  21.6 us (20%)
  local copies, waits for them, and re-layouts  7.67 us (7%)
  between operations  1.5 us (1%)
    ppermute x14, waiting for transfers between devices, to_z(): return lax.ppermute(x, 'seq', perm)  43 us
    ppermute x14, starting transfers between devices, to_z(): return lax.ppermute(x, 'seq', perm)  18.9 us
    ppermute x6, starting transfers between devices, to_dp(): return lax.ppermute(x, 'dp', [(a, a ^ k) for a in range(n_dp)])  8.12 us
    ppermute x6, waiting for transfers between devices, to_dp(): return lax.ppermute(x, 'dp', [(a, a ^ k) for a in range(n_dp)])  5.95 us
    unnamed x18, local copies, waits for them, and re-layouts  5.76 us
    pallas_call x1, Pallas kernels, text_project(): pl.pallas_call(functools.partial(text_kernel, groups, heads, place_of, wh...  5.65 us
    pallas_call x1, Pallas kernels, project(): pl.pallas_call(functools.partial(project_kernel, groups, parts, place_of)...  5.64 us
    pallas_call x2, Pallas kernels, attention(): pl.pallas_call(functools.partial(attention_kernel, n_pieces, len(blocks),...  3.88 us
  transfers between devices with their start and end apart: 27, of which 10 were waited for; matrix products, arithmetic and copies ran while one was open for 3% of the time, Pallas kernels for 12%

profile of v14, /device:TPU:0, one launch (start us, length us, event | category | flops | bytes accessed | tf_op | source)
XLA Modules:
  0.0 109.3 jit_solution(8667715172391719976)
XLA Ops:
  1.3 5.7 %shard_map.164 = (f32[4,336,128]{2,1,0:T(8,128)}, bf16[1152,128]{1,0:T(8,128)(2,1)}, bf16[1152,128]{1,0:T(8,128)(2,1)}, bf16[1152,128]{1,0:T(8,128)(2,1)}, bf16[...) custom-call(s32[1]{0:T(128)} %copy.22.len_ref, s32[1,64]{1,0:T(1,128)} %src_ref.1, bf16[64,512]{1,0:T(8,128)(2,1)} %bitcast.36, ...), custom_call_target="tpu_custom_call" | custom-call | flops 301989888 | bytes 4718592 | tf_op jit(solution)/shard_map/pallas_call | solution.py:133
  7.0 0.5 collective-permute-start
  7.5 3.7 %collective-permute-start.3 = (bf16[1152,128]{1,0:T(8,128)(2,1)}, bf16[1152,128]{1,0:T(8,128)(2,1)S(1)}, u32[]{:S(2)}, u32[]{:S(2)}) collective-permute-start(bf16[1152,128]{1,0:T(8,128)(2,1)} %get-tuple-element.47), channel_id=1, source_target_pairs={{0,4},{2,6},{4,0},{6,2},{1,5},{3,7},{5,1},{7,3},{8,12},{10,14},{12... | collective-permute-start | bytes 884744 | tf_op jit(solution)/shard_map/ppermute | solution.py:602
  11.1 1.3 %collective-permute-start.4 = (bf16[1152,128]{1,0:T(8,128)(2,1)}, bf16[1152,128]{1,0:T(8,128)(2,1)S(1)}, u32[]{:S(2)}, u32[]{:S(2)}) collective-permute-start(bf16[1152,128]{1,0:T(8,128)(2,1)} %get-tuple-element.48), channel_id=1, source_target_pairs={{0,6},{2,4},{4,2},{6,0},{1,7},{3,5},{5,3},{7,1},{8,14},{10,12},{12... | collective-permute-start | bytes 884744 | tf_op jit(solution)/shard_map/ppermute | solution.py:602
  12.5 0.2 collective-permute-start.5
  12.7 1.1 %copy-done.2 = f32[4,336,128]{2,1,0:T(8,128)S(1)} copy-done((f32[4,336,128]{2,1,0:T(8,128)S(1)}, f32[4,336,128]{2,1,0:T(8,128)}, u32[]{:S(2)}) %copy-start.2) | copy-done | bytes 688152
  13.8 0.2 shard_map.165
  14.0 1.9 %collective-permute-start.1 = (bf16[2,320,128]{2,1,0:T(8,128)(2,1)S(1)}, bf16[2,320,128]{2,1,0:T(8,128)(2,1)S(1)}, u32[]{:S(2)}, u32[]{:S(2)}) collective-permute-start(bf16[2,320,128]{2,1,0:T(8,128)(2,1)S(1)} %get-tuple-element.43), channel_id=1, source_target_pairs={{0,2},{2,0},{4,6},{6,4},{1,3},{3,1},{5,7},{7,5},{8,10},{10,8},{12,... | collective-permute-start | bytes 491528 | tf_op jit(solution)/shard_map/ppermute | solution.py:602
  15.9 0.6 pad_add_fusion.meta_ref
  16.4 2.3 %shard_map.167 = (bf16[2,4,96,128]{3,2,1,0:T(8,128)(2,1)}, bf16[2,4,96,128]{3,2,1,0:T(8,128)(2,1)}, bf16[2,4,96,128]{3,2,1,0:T(8,128)(2,1)}, bf16[2,4,96,128]{3,2,1,0:T(8,128)(2,1)}) custom-call(s32[3]{0:T(128)} %pad_add_fusion.meta_ref, f32[1,3072]{1,0:T(1,128)} %gate_ref.3, bf16[128,3072]{1,0:T(8,128)(2,1)} %bitcast.31), custom_call_target="tpu_custom_call" | custom-call | bytes 1572864 | tf_op jit(solution)/shard_map/pallas_call | solution.py:343
  18.8 1.5 %collective-permute-start.6 = (bf16[2,4,96,128]{3,2,1,0:T(8,128)(2,1)}, bf16[2,4,96,128]{3,2,1,0:T(8,128)(2,1)S(1)}, u32[]{:S(2)}, u32[]{:S(2)}) collective-permute-start(bf16[2,4,96,128]{3,2,1,0:T(8,128)(2,1)} %get-tuple-element.50), channel_id=1, source_target_pairs={{0,8},{8,0},{16,24},{24,16},{1,9},{9,1},{17,25},{25,17},{2,10},{10... | collective-permute-start | bytes 589832 | tf_op jit(solution)/shard_map/ppermute | solution.py:609
  20.3 16.2 %collective-permute-done.1.refs_0_ = bf16[2,320,128]{2,1,0:T(8,128)(2,1)S(1)} collective-permute-done((bf16[2,320,128]{2,1,0:T(8,128)(2,1)S(1)}, bf16[2,320,128]{2,1,0:T(8,128)(2,1)S(1)}, u32[]{:S(2)}, u32[]{:S(2)}) %collective-permute-start.1) | collective-permute-done | bytes 163872 | tf_op jit(solution)/shard_map/ppermute | solution.py:602
  36.5 0.2 shard_map.166
  36.6 1.7 %collective-permute-start.2 = (bf16[1,320,128]{2,1,0:T(8,128)(2,1)S(1)}, bf16[1,320,128]{2,1,0:T(8,128)(2,1)S(1)}, u32[]{:S(2)}, u32[]{:S(2)}) collective-permute-start(bf16[1,320,128]{2,1,0:T(8,128)(2,1)S(1)} %get-tuple-element.45), channel_id=1, source_target_pairs={{0,4},{2,6},{4,0},{6,2},{1,5},{3,7},{5,1},{7,3},{8,12},{10,14},{12... | collective-permute-start | bytes 245768 | tf_op jit(solution)/shard_map/ppermute | solution.py:602
  38.4 4.6 %collective-permute-done.2.got_ref = bf16[1,320,128]{2,1,0:T(8,128)(2,1)S(1)} collective-permute-done((bf16[1,320,128]{2,1,0:T(8,128)(2,1)S(1)}, bf16[1,320,128]{2,1,0:T(8,128)(2,1)S(1)}, u32[]{:S(2)}, u32[]{:S(2)}) %collective-permute-start.2) | collective-permute-done | bytes 81952 | tf_op jit(solution)/shard_map/ppermute | solution.py:602
  42.9 1.0 copy-done.4
  43.9 0.3 shard_map.168.refs_0_
  44.2 1.6 %collective-permute-start.11 = (bf16[2,4,96,128]{3,2,1,0:T(8,128)(2,1)}, bf16[2,4,96,128]{3,2,1,0:T(8,128)(2,1)}, u32[]{:S(2)}, u32[]{:S(2)}) collective-permute-start(bf16[2,4,96,128]{3,2,1,0:T(8,128)(2,1)} %get-tuple-element.56), channel_id=1, source_target_pairs={{0,16},{8,24},{16,0},{24,8},{1,17},{9,25},{17,1},{25,9},{2,18},{10... | collective-permute-start | bytes 589832 | tf_op jit(solution)/shard_map/ppermute | solution.py:609
  45.9 1.4 %collective-permute-start.12 = (bf16[2,4,96,128]{3,2,1,0:T(8,128)(2,1)}, bf16[2,4,96,128]{3,2,1,0:T(8,128)(2,1)}, u32[]{:S(2)}, u32[]{:S(2)}) collective-permute-start(bf16[2,4,96,128]{3,2,1,0:T(8,128)(2,1)} %get-tuple-element.57), channel_id=1, source_target_pairs={{0,24},{8,16},{16,8},{24,0},{1,25},{9,17},{17,9},{25,1},{2,26},{10... | collective-permute-start | bytes 589832 | tf_op jit(solution)/shard_map/ppermute | solution.py:609
  47.4 2.0 %shard_map.169 = (bf16[128,384]{1,0:T(8,128)(2,1)S(1)}, bf16[128,384]{1,0:T(8,128)(2,1)S(1)}, bf16[32,384]{1,0:T(8,128)(2,1)S(1)}) custom-call(bf16[4912,128]{1,0:T(8,128)(2,1)S(1)} %shard_map.168.refs_0_, bf16[4912,128]{1,0:T(8,128)(2,1)S(1)} %collective-permute-done.7.refs_1_), custom_call_target="tpu_custom_call" | custom-call | flops 481296384 | bytes 2113536 | tf_op jit(solution)/shard_map/pallas_call | solution.py:283
  49.5 0.8 collective-permute-start.8
  50.3 2.1 %collective-permute-start.9 = (bf16[136,384]{1,0:T(8,128)(2,1)S(1)}, bf16[136,384]{1,0:T(8,128)(2,1)S(1)}, u32[]{:S(2)}, u32[]{:S(2)}) collective-permute-start(bf16[136,384]{1,0:T(8,128)(2,1)S(1)} %pad_maximum_fusion.1), channel_id=1, source_target_pairs={{0,6},{2,4},{4,2},{6,0},{1,7},{3,5},{5,3},{7,1},{8,14},{10,12},{12... | collective-permute-start | bytes 313352 | tf_op jit(solution)/shard_map/ppermute | solution.py:602
  52.3 1.9 %shard_map.170 = (bf16[128,384]{1,0:T(8,128)(2,1)S(1)}, bf16[128,384]{1,0:T(8,128)(2,1)S(1)}) custom-call(bf16[4912,128]{1,0:T(8,128)(2,1)S(1)} %shard_map.168.refs_0_, bf16[4912,128]{1,0:T(8,128)(2,1)S(1)} %collective-permute-done.7.refs_1_, bf16[32,384]{1,0:T(8,128)(2,1)S(1)} %get-tuple-element.52.refs_2_), custom_call_target="tpu_custom_call" | custom-call | flops 427819008 | bytes 2064384 | tf_op jit(solution)/shard_map/pallas_call | solution.py:283
  54.2 0.8 collective-permute-start.10
  55.1 4.8 %collective-permute-done.8.refs_0_ = bf16[136,384]{1,0:T(8,128)(2,1)S(1)} collective-permute-done((bf16[136,384]{1,0:T(8,128)(2,1)S(1)}, bf16[136,384]{1,0:T(8,128)(2,1)S(1)}, u32[]{:S(2)}, u32[]{:S(2)}) %collective-permute-start.8) | collective-permute-done | bytes 104480 | tf_op jit(solution)/shard_map/ppermute | solution.py:602
  60.0 1.9 %collective-permute-done.10.refs_2_ = bf16[136,384]{1,0:T(8,128)(2,1)S(1)} collective-permute-done((bf16[136,384]{1,0:T(8,128)(2,1)S(1)}, bf16[136,384]{1,0:T(8,128)(2,1)S(1)}, u32[]{:S(2)}, u32[]{:S(2)}) %collective-permute-start.10) | collective-permute-done | bytes 104480 | tf_op jit(solution)/shard_map/ppermute | solution.py:602
  62.2 2.5 %collective-permute-start.16 = (bf16[128,1536]{1,0:T(8,128)(2,1)S(1)}, bf16[128,1536]{1,0:T(8,128)(2,1)S(1)}, u32[]{:S(2)}, u32[]{:S(2)}) collective-permute-start(bf16[128,1536]{1,0:T(8,128)(2,1)S(1)} %shard_map.171.attn_ref.refs_5_), channel_id=1, source_target_pairs={{0,24},{8,16},{16,8},{24,0},{1,25},{9,17},{17,9},{25,1},{2,26},{10... | collective-permute-start | bytes 1179656 | tf_op jit(solution)/shard_map/ppermute | solution.py:609
  64.7 0.5 collective-permute-start.15
  65.2 0.5 collective-permute-start.14
  65.7 3.7 %copy-done = bf16[3072,1536]{1,0:T(8,128)(2,1)S(1)} copy-done((bf16[3072,1536]{1,0:T(8,128)(2,1)S(1)}, bf16[3072,1536]{1,0:T(8,128)(2,1)}, u32[]{:S(2)}) %copy-start) | copy-done | bytes 9437208
  69.4 5.6 %shard_map.172 = (bf16[128,3072]{1,0:T(8,128)(2,1)}, bf16[128,1536]{1,0:T(8,128)(2,1)}, f32[4,384]{1,0:T(4,128)S(1)}, bf16[144,1536]{1,0:T(8,128)(2,1)S(1)}) custom-call(s32[3]{0:T(128)S(1)} %copy-done.6, bf16[128,1536]{1,0:T(8,128)(2,1)S(1)} %shard_map.171.attn_ref.refs_5_, bf16[3072,1536]{1,0:T(8,128)(2,1)S(1)} %copy-done, f32[1,3072]{1,0:T(1,128)S(1)} %copy-done.5, ...), custom_call_target="tpu_custom_call" | custom-call | flops 2415919104 | bytes 9437184 | tf_op jit(solution)/shard_map/pallas_call | solution.py:424
  75.1 1.0 shard_map.173
  76.1 0.6 collective-permute-start.13
  76.8 5.8 %collective-permute-done.15.refs_7_ = bf16[128,1536]{1,0:T(8,128)(2,1)S(1)} collective-permute-done((bf16[128,1536]{1,0:T(8,128)(2,1)S(1)}, bf16[128,1536]{1,0:T(8,128)(2,1)S(1)}, u32[]{:S(2)}, u32[]{:S(2)}) %collective-permute-start.15) | collective-permute-done | bytes 393248 | tf_op jit(solution)/shard_map/ppermute | solution.py:609
  82.7 0.4 collective-permute-start.18
  83.1 0.9 slice.32.refs_2_
  84.0 0.9 slice.33.refs_3_
  85.0 1.4 %shard_map.174 = (f32[1168,128]{1,0:T(8,128)S(1)}, bf16[576,128]{1,0:T(8,128)(2,1)S(1)}, bf16[592,128]{1,0:T(8,128)(2,1)S(1)}, f32[576,128]{1,0:T(8,128)S(1)}, f...) custom-call(bf16[1,4,96,128]{3,2,1,0:T(8,128)(2,1)S(1)} %slice.24.refs_0_, ...), custom_call_target="tpu_custom_call" | custom-call | flops 1207959552 | bytes 5111808 | tf_op jit(solution)/shard_map/pallas_call | solution.py:500
  86.4 0.7 collective-permute-start.23
  87.1 1.4 %collective-permute-start.21 = (bf16[576,128]{1,0:T(8,128)(2,1)S(1)}, bf16[576,128]{1,0:T(8,128)(2,1)S(1)}, u32[]{:S(2)}, u32[]{:S(2)}) collective-permute-start(bf16[576,128]{1,0:T(8,128)(2,1)S(1)} %get-tuple-element.65), channel_id=1, source_target_pairs={{0,2},{2,0},{4,6},{6,4},{1,3},{3,1},{5,7},{7,5},{8,10},{10,8},{12,... | collective-permute-start | bytes 442376 | tf_op jit(solution)/shard_map/ppermute | solution.py:602
  88.5 4.8 %collective-permute-done.23.got_ref = bf16[592,128]{1,0:T(8,128)(2,1)S(1)} collective-permute-done((bf16[592,128]{1,0:T(8,128)(2,1)S(1)}, bf16[592,128]{1,0:T(8,128)(2,1)S(1)}, u32[]{:S(2)}, u32[]{:S(2)}) %collective-permute-start.23) | collective-permute-done | bytes 151584 | tf_op jit(solution)/shard_map/ppermute | solution.py:602
  93.3 1.0 collective-permute-start.24
  94.2 1.3 %collective-permute-start.26 = (bf16[592,128]{1,0:T(8,128)(2,1)S(1)}, bf16[592,128]{1,0:T(8,128)(2,1)S(1)}, u32[]{:S(2)}, u32[]{:S(2)}) collective-permute-start(bf16[592,128]{1,0:T(8,128)(2,1)S(1)} %get-tuple-element.72), channel_id=1, source_target_pairs={{0,2},{2,0},{4,6},{6,4},{1,3},{3,1},{5,7},{7,5},{8,10},{10,8},{12,... | collective-permute-start | bytes 454664 | tf_op jit(solution)/shard_map/ppermute | solution.py:602
  95.6 1.1 %collective-permute-done.21.got_ref = bf16[576,128]{1,0:T(8,128)(2,1)S(1)} collective-permute-done((bf16[576,128]{1,0:T(8,128)(2,1)S(1)}, bf16[576,128]{1,0:T(8,128)(2,1)S(1)}, u32[]{:S(2)}, u32[]{:S(2)}) %collective-permute-start.21) | collective-permute-done | bytes 147488 | tf_op jit(solution)/shard_map/ppermute | solution.py:602
  96.8 0.3 collective-permute-start.22
  97.0 1.7 %collective-permute-start.25 = (bf16[576,128]{1,0:T(8,128)(2,1)S(1)}, bf16[576,128]{1,0:T(8,128)(2,1)S(1)}, u32[]{:S(2)}, u32[]{:S(2)}) collective-permute-start(bf16[576,128]{1,0:T(8,128)(2,1)S(1)} %get-tuple-element.71), channel_id=1, source_target_pairs={{0,2},{2,0},{4,6},{6,4},{1,3},{3,1},{5,7},{7,5},{8,10},{10,8},{12,... | collective-permute-start | bytes 442376 | tf_op jit(solution)/shard_map/ppermute | solution.py:602
  98.7 9.5 %collective-permute-done.22.far_low = bf16[576,128]{1,0:T(8,128)(2,1)S(1)} collective-permute-done((bf16[576,128]{1,0:T(8,128)(2,1)S(1)}, bf16[576,128]{1,0:T(8,128)(2,1)S(1)}, u32[]{:S(2)}, u32[]{:S(2)}) %collective-permute-start.22) | collective-permute-done | bytes 147488 | tf_op jit(solution)/shard_map/ppermute | solution.py:602
  108.4 0.9 shard_map.177
  (55 shorter events, 1.1 us)
Async XLA Ops:
  1.3 46.0 %copy-start.8 = (s32[1,64]{1,0:T(1,128)S(1)}, s32[1,64]{1,0:T(1,128)}, u32[]{:S(2)}) copy-start(s32[1,64]{1,0:T(1,128)} %src_ref.1) | copy-start | bytes 772
  7.0 5.8 %collective-permute-start = (bf16[4,320,128]{2,1,0:T(8,128)(2,1)}, bf16[4,320,128]{2,1,0:T(8,128)(2,1)S(1)}, u32[]{:S(2)}, u32[]{:S(2)}) collective-permute-start(bf16[4,320,128]{2,1,0:T(8,128)(2,1)} %get-tuple-element.41), channel_id=1, source_target_pairs={{0,1},{2,3},{4,5},{6,7},{1,0},{3,2},{5,4},{7,6},{8,9},{10,11},{12,... | collective-permute-start | bytes 983048 | tf_op jit(solution)/shard_map/ppermute | solution.py:606
  7.5 30.9 %collective-permute-start.3 = (bf16[1152,128]{1,0:T(8,128)(2,1)}, bf16[1152,128]{1,0:T(8,128)(2,1)S(1)}, u32[]{:S(2)}, u32[]{:S(2)}) collective-permute-start(bf16[1152,128]{1,0:T(8,128)(2,1)} %get-tuple-element.47), channel_id=1, source_target_pairs={{0,4},{2,6},{4,0},{6,2},{1,5},{3,7},{5,1},{7,3},{8,12},{10,14},{12... | collective-permute-start | bytes 884744 | tf_op jit(solution)/shard_map/ppermute | solution.py:602
  11.1 27.2 %collective-permute-start.4 = (bf16[1152,128]{1,0:T(8,128)(2,1)}, bf16[1152,128]{1,0:T(8,128)(2,1)S(1)}, u32[]{:S(2)}, u32[]{:S(2)}) collective-permute-start(bf16[1152,128]{1,0:T(8,128)(2,1)} %get-tuple-element.48), channel_id=1, source_target_pairs={{0,6},{2,4},{4,2},{6,0},{1,7},{3,5},{5,3},{7,1},{8,14},{10,12},{12... | collective-permute-start | bytes 884744 | tf_op jit(solution)/shard_map/ppermute | solution.py:602
  12.5 25.9 %collective-permute-start.5 = (bf16[1152,128]{1,0:T(8,128)(2,1)}, bf16[1152,128]{1,0:T(8,128)(2,1)S(1)}, u32[]{:S(2)}, u32[]{:S(2)}) collective-permute-start(bf16[1152,128]{1,0:T(8,128)(2,1)} %get-tuple-element.49), channel_id=1, source_target_pairs={{0,2},{2,0},{4,6},{6,4},{1,3},{3,1},{5,7},{7,5},{8,10},{10,8},{12,... | collective-permute-start | bytes 884744 | tf_op jit(solution)/shard_map/ppermute | solution.py:602
  12.7 1.1 %copy-start.2 = (f32[4,336,128]{2,1,0:T(8,128)S(1)}, f32[4,336,128]{2,1,0:T(8,128)}, u32[]{:S(2)}) copy-start(f32[4,336,128]{2,1,0:T(8,128)} %get-tuple-element.40.own_ref) | copy-start | bytes 2064388
  14.0 22.5 %collective-permute-start.1 = (bf16[2,320,128]{2,1,0:T(8,128)(2,1)S(1)}, bf16[2,320,128]{2,1,0:T(8,128)(2,1)S(1)}, u32[]{:S(2)}, u32[]{:S(2)}) collective-permute-start(bf16[2,320,128]{2,1,0:T(8,128)(2,1)S(1)} %get-tuple-element.43), channel_id=1, source_target_pairs={{0,2},{2,0},{4,6},{6,4},{1,3},{3,1},{5,7},{7,5},{8,10},{10,8},{12,... | collective-permute-start | bytes 491528 | tf_op jit(solution)/shard_map/ppermute | solution.py:602
  18.8 19.6 %collective-permute-start.6 = (bf16[2,4,96,128]{3,2,1,0:T(8,128)(2,1)}, bf16[2,4,96,128]{3,2,1,0:T(8,128)(2,1)S(1)}, u32[]{:S(2)}, u32[]{:S(2)}) collective-permute-start(bf16[2,4,96,128]{3,2,1,0:T(8,128)(2,1)} %get-tuple-element.50), channel_id=1, source_target_pairs={{0,8},{8,0},{16,24},{24,16},{1,9},{9,1},{17,25},{25,17},{2,10},{10... | collective-permute-start | bytes 589832 | tf_op jit(solution)/shard_map/ppermute | solution.py:609
  36.6 6.3 %collective-permute-start.2 = (bf16[1,320,128]{2,1,0:T(8,128)(2,1)S(1)}, bf16[1,320,128]{2,1,0:T(8,128)(2,1)S(1)}, u32[]{:S(2)}, u32[]{:S(2)}) collective-permute-start(bf16[1,320,128]{2,1,0:T(8,128)(2,1)S(1)} %get-tuple-element.45), channel_id=1, source_target_pairs={{0,4},{2,6},{4,0},{6,2},{1,5},{3,7},{5,1},{7,3},{8,12},{10,14},{12... | collective-permute-start | bytes 245768 | tf_op jit(solution)/shard_map/ppermute | solution.py:602
  42.9 1.0 copy-start.4
  43.9 21.8 %copy-start.1 = (bf16[1,128,3072]{2,1,0:T(8,128)(2,1)S(1)}, bf16[1,128,3072]{2,1,0:T(8,128)(2,1)}, u32[]{:S(2)}) copy-start(bf16[1,128,3072]{2,1,0:T(8,128)(2,1)} %param.25) | copy-start | bytes 2359300
  43.9 21.8 %copy-start.5 = (f32[1,3072]{1,0:T(1,128)S(1)}, f32[1,3072]{1,0:T(1,128)}, u32[]{:S(2)}) copy-start(f32[1,3072]{1,0:T(1,128)} %gate_ref.3) | copy-start | bytes 36868
  43.9 21.8 %copy-start.6 = (s32[3]{0:T(128)S(1)}, s32[3]{0:T(128)}, u32[]{:S(2)}) copy-start(s32[3]{0:T(128)} %pad_add_fusion.meta_ref) | copy-start | bytes 40
  44.1 3.2 %collective-permute-start.7 = (bf16[4912,128]{1,0:T(8,128)(2,1)S(1)}, bf16[4912,128]{1,0:T(8,128)(2,1)S(1)}, u32[]{:S(2)}, u32[]{:S(2)}) collective-permute-start(bf16[4912,128]{1,0:T(8,128)(2,1)S(1)} %shard_map.168.refs_0_), channel_id=1, source_target_pairs={{0,1},{2,3},{4,5},{6,7},{1,0},{3,2},{5,4},{7,6},{8,9},{10,11},{12,... | collective-permute-start | bytes 3772424 | tf_op jit(solution)/shard_map/ppermute | solution.py:606
  44.2 17.8 %collective-permute-start.11 = (bf16[2,4,96,128]{3,2,1,0:T(8,128)(2,1)}, bf16[2,4,96,128]{3,2,1,0:T(8,128)(2,1)}, u32[]{:S(2)}, u32[]{:S(2)}) collective-permute-start(bf16[2,4,96,128]{3,2,1,0:T(8,128)(2,1)} %get-tuple-element.56), channel_id=1, source_target_pairs={{0,16},{8,24},{16,0},{24,8},{1,17},{9,25},{17,1},{25,9},{2,18},{10... | collective-permute-start | bytes 589832 | tf_op jit(solution)/shard_map/ppermute | solution.py:609
  45.9 16.2 %collective-permute-start.12 = (bf16[2,4,96,128]{3,2,1,0:T(8,128)(2,1)}, bf16[2,4,96,128]{3,2,1,0:T(8,128)(2,1)}, u32[]{:S(2)}, u32[]{:S(2)}) collective-permute-start(bf16[2,4,96,128]{3,2,1,0:T(8,128)(2,1)} %get-tuple-element.57), channel_id=1, source_target_pairs={{0,24},{8,16},{16,8},{24,0},{1,25},{9,17},{17,9},{25,1},{2,26},{10... | collective-permute-start | bytes 589832 | tf_op jit(solution)/shard_map/ppermute | solution.py:609
  49.5 10.4 %collective-permute-start.8 = (bf16[136,384]{1,0:T(8,128)(2,1)S(1)}, bf16[136,384]{1,0:T(8,128)(2,1)S(1)}, u32[]{:S(2)}, u32[]{:S(2)}) collective-permute-start(bf16[136,384]{1,0:T(8,128)(2,1)S(1)} %pad_maximum_fusion), channel_id=1, source_target_pairs={{0,4},{2,6},{4,0},{6,2},{1,5},{3,7},{5,1},{7,3},{8,12},{10,14},{12... | collective-permute-start | bytes 313352 | tf_op jit(solution)/shard_map/ppermute | solution.py:602
  50.3 9.7 %collective-permute-start.9 = (bf16[136,384]{1,0:T(8,128)(2,1)S(1)}, bf16[136,384]{1,0:T(8,128)(2,1)S(1)}, u32[]{:S(2)}, u32[]{:S(2)}) collective-permute-start(bf16[136,384]{1,0:T(8,128)(2,1)S(1)} %pad_maximum_fusion.1), channel_id=1, source_target_pairs={{0,6},{2,4},{4,2},{6,0},{1,7},{3,5},{5,3},{7,1},{8,14},{10,12},{12... | collective-permute-start | bytes 313352 | tf_op jit(solution)/shard_map/ppermute | solution.py:602
  54.2 7.7 %collective-permute-start.10 = (bf16[136,384]{1,0:T(8,128)(2,1)S(1)}, bf16[136,384]{1,0:T(8,128)(2,1)S(1)}, u32[]{:S(2)}, u32[]{:S(2)}) collective-permute-start(bf16[136,384]{1,0:T(8,128)(2,1)S(1)} %pad_maximum_fusion.2), channel_id=1, source_target_pairs={{0,2},{2,0},{4,6},{6,4},{1,3},{3,1},{5,7},{7,5},{8,10},{10,8},{12,... | collective-permute-start | bytes 313352 | tf_op jit(solution)/shard_map/ppermute | solution.py:602
  62.0 13.0 %copy-start.7 = (bf16[1,8,1536]{2,1,0:T(8,128)(2,1)}, bf16[1,8,1536]{2,1,0:T(8,128)(2,1)S(1)}, u32[]{:S(2)}) copy-start(bf16[1,8,1536]{2,1,0:T(8,128)(2,1)S(1)} %get-tuple-element.75) | copy-start | bytes 73732
  62.1 13.0 %copy-start.3 = (bf16[2,4,96,128]{3,2,1,0:T(8,128)(2,1)S(1)}, bf16[2,4,96,128]{3,2,1,0:T(8,128)(2,1)}, u32[]{:S(2)}) copy-start(bf16[2,4,96,128]{3,2,1,0:T(8,128)(2,1)} %get-tuple-element.60.refs_0_) | copy-start | bytes 589828
  62.2 14.5 %collective-permute-start.16 = (bf16[128,1536]{1,0:T(8,128)(2,1)S(1)}, bf16[128,1536]{1,0:T(8,128)(2,1)S(1)}, u32[]{:S(2)}, u32[]{:S(2)}) collective-permute-start(bf16[128,1536]{1,0:T(8,128)(2,1)S(1)} %shard_map.171.attn_ref.refs_5_), channel_id=1, source_target_pairs={{0,24},{8,16},{16,8},{24,0},{1,25},{9,17},{17,9},{25,1},{2,26},{10... | collective-permute-start | bytes 1179656 | tf_op jit(solution)/shard_map/ppermute | solution.py:609
  64.7 17.9 %collective-permute-start.15 = (bf16[128,1536]{1,0:T(8,128)(2,1)S(1)}, bf16[128,1536]{1,0:T(8,128)(2,1)S(1)}, u32[]{:S(2)}, u32[]{:S(2)}) collective-permute-start(bf16[128,1536]{1,0:T(8,128)(2,1)S(1)} %shard_map.171.attn_ref.refs_5_), channel_id=1, source_target_pairs={{0,16},{8,24},{16,0},{24,8},{1,17},{9,25},{17,1},{25,9},{2,18},{10... | collective-permute-start | bytes 1179656 | tf_op jit(solution)/shard_map/ppermute | solution.py:609
  65.2 17.5 %collective-permute-start.14 = (bf16[128,1536]{1,0:T(8,128)(2,1)S(1)}, bf16[128,1536]{1,0:T(8,128)(2,1)S(1)}, u32[]{:S(2)}, u32[]{:S(2)}) collective-permute-start(bf16[128,1536]{1,0:T(8,128)(2,1)S(1)} %shard_map.171.attn_ref.refs_5_), channel_id=1, source_target_pairs={{0,8},{8,0},{16,24},{24,16},{1,9},{9,1},{17,25},{25,17},{2,10},{10... | collective-permute-start | bytes 1179656 | tf_op jit(solution)/shard_map/ppermute | solution.py:609
  65.7 3.7 %copy-start = (bf16[3072,1536]{1,0:T(8,128)(2,1)S(1)}, bf16[3072,1536]{1,0:T(8,128)(2,1)}, u32[]{:S(2)}) copy-start(bf16[3072,1536]{1,0:T(8,128)(2,1)} %w_ref.3) | copy-start | bytes 28311556
  75.1 9.9 %collective-permute-start.17 = (bf16[144,1536]{1,0:T(8,128)(2,1)S(1)}, bf16[144,1536]{1,0:T(8,128)(2,1)S(1)}, u32[]{:S(2)}, u32[]{:S(2)}) collective-permute-start(bf16[144,1536]{1,0:T(8,128)(2,1)S(1)} %get-tuple-element.61), channel_id=1, source_target_pairs={{0,1},{2,3},{4,5},{6,7},{1,0},{3,2},{5,4},{7,6},{8,9},{10,11},{12,... | collective-permute-start | bytes 1327112 | tf_op jit(solution)/shard_map/ppermute | solution.py:606
  76.1 8.8 %collective-permute-start.13 = (bf16[4,4,96,128]{3,2,1,0:T(8,128)(2,1)S(1)}, bf16[4,4,96,128]{3,2,1,0:T(8,128)(2,1)S(1)}, u32[]{:S(2)}, u32[]{:S(2)}) collective-permute-start(bf16[4,4,96,128]{3,2,1,0:T(8,128)(2,1)S(1)} %shard_map.173), channel_id=1, source_target_pairs={{0,1},{2,3},{4,5},{6,7},{1,0},{3,2},{5,4},{7,6},{8,9},{10,11},{12,... | collective-permute-start | bytes 1179656 | tf_op jit(solution)/shard_map/ppermute | solution.py:606
  76.7 8.3 %collective-permute-start.20 = (bf16[128,1536]{1,0:T(8,128)(2,1)S(1)}, bf16[128,1536]{1,0:T(8,128)(2,1)S(1)}, u32[]{:S(2)}, u32[]{:S(2)}) collective-permute-start(bf16[128,1536]{1,0:T(8,128)(2,1)S(1)} %collective-permute-done.16.refs_8_), channel_id=1, source_target_pairs={{0,1},{2,3},{4,5},{6,7},{1,0},{3,2},{5,4},{7,6},{8,9},{10,11},{12,... | collective-permute-start | bytes 1179656 | tf_op jit(solution)/shard_map/ppermute | solution.py:606
  82.6 2.4 %collective-permute-start.19 = (bf16[128,1536]{1,0:T(8,128)(2,1)S(1)}, bf16[128,1536]{1,0:T(8,128)(2,1)S(1)}, u32[]{:S(2)}, u32[]{:S(2)}) collective-permute-start(bf16[128,1536]{1,0:T(8,128)(2,1)S(1)} %collective-permute-done.15.refs_7_), channel_id=1, source_target_pairs={{0,1},{2,3},{4,5},{6,7},{1,0},{3,2},{5,4},{7,6},{8,9},{10,11},{12,... | collective-permute-start | bytes 1179656 | tf_op jit(solution)/shard_map/ppermute | solution.py:606
  82.7 2.2 %collective-permute-start.18 = (bf16[128,1536]{1,0:T(8,128)(2,1)S(1)}, bf16[128,1536]{1,0:T(8,128)(2,1)S(1)}, u32[]{:S(2)}, u32[]{:S(2)}) collective-permute-start(bf16[128,1536]{1,0:T(8,128)(2,1)S(1)} %collective-permute-done.14.refs_6_), channel_id=1, source_target_pairs={{0,1},{2,3},{4,5},{6,7},{1,0},{3,2},{5,4},{7,6},{8,9},{10,11},{12,... | collective-permute-start | bytes 1179656 | tf_op jit(solution)/shard_map/ppermute | solution.py:606
  86.4 6.8 %collective-permute-start.23 = (bf16[592,128]{1,0:T(8,128)(2,1)S(1)}, bf16[592,128]{1,0:T(8,128)(2,1)S(1)}, u32[]{:S(2)}, u32[]{:S(2)}) collective-permute-start(bf16[592,128]{1,0:T(8,128)(2,1)S(1)} %get-tuple-element.67), channel_id=1, source_target_pairs={{0,2},{2,0},{4,6},{6,4},{1,3},{3,1},{5,7},{7,5},{8,10},{10,8},{12,... | collective-permute-start | bytes 454664 | tf_op jit(solution)/shard_map/ppermute | solution.py:602
  87.1 9.6 %collective-permute-start.21 = (bf16[576,128]{1,0:T(8,128)(2,1)S(1)}, bf16[576,128]{1,0:T(8,128)(2,1)S(1)}, u32[]{:S(2)}, u32[]{:S(2)}) collective-permute-start(bf16[576,128]{1,0:T(8,128)(2,1)S(1)} %get-tuple-element.65), channel_id=1, source_target_pairs={{0,2},{2,0},{4,6},{6,4},{1,3},{3,1},{5,7},{7,5},{8,10},{10,8},{12,... | collective-permute-start | bytes 442376 | tf_op jit(solution)/shard_map/ppermute | solution.py:602
  93.3 15.1 %collective-permute-start.24 = (bf16[592,128]{1,0:T(8,128)(2,1)S(1)}, bf16[592,128]{1,0:T(8,128)(2,1)S(1)}, u32[]{:S(2)}, u32[]{:S(2)}) collective-permute-start(bf16[592,128]{1,0:T(8,128)(2,1)S(1)} %get-tuple-element.70), channel_id=1, source_target_pairs={{0,4},{2,6},{4,0},{6,2},{1,5},{3,7},{5,1},{7,3},{8,12},{10,14},{12... | collective-permute-start | bytes 454664 | tf_op jit(solution)/shard_map/ppermute | solution.py:602
  94.2 14.2 %collective-permute-start.26 = (bf16[592,128]{1,0:T(8,128)(2,1)S(1)}, bf16[592,128]{1,0:T(8,128)(2,1)S(1)}, u32[]{:S(2)}, u32[]{:S(2)}) collective-permute-start(bf16[592,128]{1,0:T(8,128)(2,1)S(1)} %get-tuple-element.72), channel_id=1, source_target_pairs={{0,2},{2,0},{4,6},{6,4},{1,3},{3,1},{5,7},{7,5},{8,10},{10,8},{12,... | collective-permute-start | bytes 454664 | tf_op jit(solution)/shard_map/ppermute | solution.py:602
  96.8 11.5 %collective-permute-start.22 = (bf16[576,128]{1,0:T(8,128)(2,1)S(1)}, bf16[576,128]{1,0:T(8,128)(2,1)S(1)}, u32[]{:S(2)}, u32[]{:S(2)}) collective-permute-start(bf16[576,128]{1,0:T(8,128)(2,1)S(1)} %shard_map.175), channel_id=1, source_target_pairs={{0,4},{2,6},{4,0},{6,2},{1,5},{3,7},{5,1},{7,3},{8,12},{10,14},{12... | collective-permute-start | bytes 442376 | tf_op jit(solution)/shard_map/ppermute | solution.py:602
  97.0 11.4 %collective-permute-start.25 = (bf16[576,128]{1,0:T(8,128)(2,1)S(1)}, bf16[576,128]{1,0:T(8,128)(2,1)S(1)}, u32[]{:S(2)}, u32[]{:S(2)}) collective-permute-start(bf16[576,128]{1,0:T(8,128)(2,1)S(1)} %get-tuple-element.71), channel_id=1, source_target_pairs={{0,2},{2,0},{4,6},{6,4},{1,3},{3,1},{5,7},{7,5},{8,10},{10,8},{12,... | collective-permute-start | bytes 442376 | tf_op jit(solution)/shard_map/ppermute | solution.py:602

commit v15 on v14

--- a/solution.py
+++ b/solution.py
@@ -49,7 +49,7 @@
 ):
     meta_ref = where()
     packed, refs = refs[:groups], refs[groups:]
-    msgs, (w_all, loaded, stage, w_sems, in_sems, out_sems) = refs[:-6], refs[-6:]
+    msgs, (w_all, sums, loaded, stage, w_sems, in_sems, out_sems) = refs[:-7], refs[-7:]
     size = own_ref.shape[2]
     rows = (own_ref.shape[1] - EXTRA) // (3 * heads + 1)
     width = heads * size
@@ -99,13 +99,20 @@
                 stage[g, to : to + local, :] = loaded[i, :, pl.ds(pl.multiple_of(at, 128), size)]
         stores.append(pltpu.make_async_copy(stage.at[g], packed[g], out_sems.at[g]))
         stores[-1].start()
-    for copy in copies:
-        copy.wait()
+    def product(part, g, i):
+        at = (i * groups + (meta_ref[0] ^ g)) * width
+        columns = pl.ds(pl.multiple_of(at, 128), width)
+        rows_of = slice(part * block, (part + 1) * block)
+        return jnp.dot(scaled[:, rows_of], w_all[rows_of, columns], preferred_element_type=f32)
+
+    copies[0].wait()
     for g in range(groups):
         for i in range(3):
-            at = (i * groups + (meta_ref[0] ^ g)) * width
-            columns = pl.ds(pl.multiple_of(at, 128), width)
-            got = jnp.dot(scaled, w_all[:, columns], preferred_element_type=f32)
+            sums[3 * g + i] = product(0, g, i)
+    copies[1].wait()
+    for g in range(groups):
+        for i in range(3):
+            got = sums[3 * g + i] + product(1, g, i)
             for head in range(heads):
                 part = got[:, head * size : (head + 1) * size]
                 to = slice((i * heads + head) * rows, (i * heads + head + 1) * rows)
@@ -137,9 +144,10 @@
         out_specs=[VMEM] + [ANY] * groups + [VMEM] * (parts - 1),
         scratch_shapes=[
             pltpu.VMEM(text_proj.shape, bf16),
+            pltpu.VMEM((3 * groups, slots, heads * size), f32),
             pltpu.VMEM((3,) + keys.shape, bf16),
             pltpu.VMEM((groups, 3 * heads * keys.shape[0], size), bf16),
-            pltpu.SemaphoreType.DMA((4,)),
+            pltpu.SemaphoreType.DMA((2,)),
             pltpu.SemaphoreType.DMA((3,)),
             pltpu.SemaphoreType.DMA((groups,)),
         ],
@@ -656,8 +664,9 @@
         back[k] = to_z(rows, k) if k else rows
     back = [back[k] for k in order + [0]]
     gg_dp += [to_dp(gg[k], k) for k in range(2, n_dp)]
-    lefts = [g[:1] for g in gg_dp]
-    lefts += [to_oc(g, j + 1) for j, g in enumerate(gather_parts(gg_dp))]
+    dp_order = [0] + list(range(n_dp - 1, 0, -1))
+    lefts = [gg_dp[k][:1] for k in dp_order]
+    lefts += [to_oc(g, j + 1) for j, g in enumerate(gather_parts([gg_dp[k] for k in dp_order]))]
     image_attn = assemble(where, back, order + [0], gg_dp[1:], image_local)
     text_attn = jnp.zeros((slot_local, inner_width), bf16)
     own_usable = part(slot_source[0] < caption_len[0], seq, slot_local, 0)
@@ -665,7 +674,7 @@
         rows = jnp.where(own_usable[:, None], got[image_local:], jnp.zeros((), bf16))
         text_attn = lax.dynamic_update_slice_in_dim(text_attn, rows, (z ^ k) * gw, 1)
 
-    pieces = [image_attn] + [to_dp(image_attn, k) for k in range(1, n_dp)]
+    pieces = [image_attn] + [to_dp(image_attn, k) for k in dp_order[1:]]
     image_out, d_attn, term, *sent = project(
         meta, image_attn, out_weight, gate, d_out[0], G, OC, place
     )

time: 110 us -> 110 us (level)
  transfers between devices with their start and end apart: 27 -> 27, of which waited for: 10 -> 9; matrix products, arithmetic and copies ran while one was open for 3% -> 3% of each run, Pallas kernels for 12% -> 12%
where the time goes in v15:
time: 110 us
  waiting for transfers between devices  49.2 us (45%)
  starting transfers between devices  28.6 us (26%)
  Pallas kernels  21.6 us (20%)
  local copies, waits for them, and re-layouts  7.67 us (7%)
  between operations  1.5 us (1%)
    ppermute x14, waiting for transfers between devices, to_z(): return lax.ppermute(x, 'seq', perm)  43 us
    ppermute x14, starting transfers between devices, to_z(): return lax.ppermute(x, 'seq', perm)  18.7 us
    ppermute x6, starting transfers between devices, to_dp(): return lax.ppermute(x, 'dp', [(a, a ^ k) for a in range(n_dp)])  8.13 us
    ppermute x6, waiting for transfers between devices, to_dp(): return lax.ppermute(x, 'dp', [(a, a ^ k) for a in range(n_dp)])  6.18 us
    unnamed x18, local copies, waits for them, and re-layouts  5.76 us
    pallas_call x1, Pallas kernels, text_project(): pl.pallas_call(functools.partial(text_kernel, groups, heads, place_of, wh...  5.66 us
    pallas_call x1, Pallas kernels, project(): pl.pallas_call(functools.partial(project_kernel, groups, parts, place_of)...  5.65 us
    pallas_call x2, Pallas kernels, attention(): pl.pallas_call(functools.partial(attention_kernel, n_pieces, len(blocks),...  3.89 us
  transfers between devices with their start and end apart: 27, of which 9 were waited for; matrix products, arithmetic and copies ran while one was open for 3% of the time, Pallas kernels for 12%

profile of v15, /device:TPU:0, one launch (start us, length us, event | category | flops | bytes accessed | tf_op | source)
XLA Modules:
  0.0 109.6 jit_solution(8559434541915925107)
XLA Ops:
  1.3 5.7 %shard_map.164 = (f32[4,336,128]{2,1,0:T(8,128)}, bf16[1152,128]{1,0:T(8,128)(2,1)}, bf16[1152,128]{1,0:T(8,128)(2,1)}, bf16[1152,128]{1,0:T(8,128)(2,1)}, bf16[...) custom-call(s32[1]{0:T(128)} %copy.22.len_ref, s32[1,64]{1,0:T(1,128)} %src_ref.1, bf16[64,512]{1,0:T(8,128)(2,1)} %bitcast.36, ...), custom_call_target="tpu_custom_call" | custom-call | flops 301989888 | bytes 4718592 | tf_op jit(solution)/shard_map/pallas_call | solution.py:140
  7.0 0.5 collective-permute-start
  7.5 3.7 %collective-permute-start.3 = (bf16[1152,128]{1,0:T(8,128)(2,1)}, bf16[1152,128]{1,0:T(8,128)(2,1)S(1)}, u32[]{:S(2)}, u32[]{:S(2)}) collective-permute-start(bf16[1152,128]{1,0:T(8,128)(2,1)} %get-tuple-element.47), channel_id=1, source_target_pairs={{0,4},{2,6},{4,0},{6,2},{1,5},{3,7},{5,1},{7,3},{8,12},{10,14},{12... | collective-permute-start | bytes 884744 | tf_op jit(solution)/shard_map/ppermute | solution.py:610
  11.1 1.4 %collective-permute-start.4 = (bf16[1152,128]{1,0:T(8,128)(2,1)}, bf16[1152,128]{1,0:T(8,128)(2,1)S(1)}, u32[]{:S(2)}, u32[]{:S(2)}) collective-permute-start(bf16[1152,128]{1,0:T(8,128)(2,1)} %get-tuple-element.48), channel_id=1, source_target_pairs={{0,6},{2,4},{4,2},{6,0},{1,7},{3,5},{5,3},{7,1},{8,14},{10,12},{12... | collective-permute-start | bytes 884744 | tf_op jit(solution)/shard_map/ppermute | solution.py:610
  12.5 0.2 collective-permute-start.5
  12.7 1.1 %copy-done.2 = f32[4,336,128]{2,1,0:T(8,128)S(1)} copy-done((f32[4,336,128]{2,1,0:T(8,128)S(1)}, f32[4,336,128]{2,1,0:T(8,128)}, u32[]{:S(2)}) %copy-start.2) | copy-done | bytes 688152
  13.8 0.2 shard_map.165
  14.0 1.9 %collective-permute-start.1 = (bf16[2,320,128]{2,1,0:T(8,128)(2,1)S(1)}, bf16[2,320,128]{2,1,0:T(8,128)(2,1)S(1)}, u32[]{:S(2)}, u32[]{:S(2)}) collective-permute-start(bf16[2,320,128]{2,1,0:T(8,128)(2,1)S(1)} %get-tuple-element.43), channel_id=1, source_target_pairs={{0,2},{2,0},{4,6},{6,4},{1,3},{3,1},{5,7},{7,5},{8,10},{10,8},{12,... | collective-permute-start | bytes 491528 | tf_op jit(solution)/shard_map/ppermute | solution.py:610
  15.9 0.6 pad_add_fusion.meta_ref
  16.4 2.3 %shard_map.167 = (bf16[2,4,96,128]{3,2,1,0:T(8,128)(2,1)}, bf16[2,4,96,128]{3,2,1,0:T(8,128)(2,1)}, bf16[2,4,96,128]{3,2,1,0:T(8,128)(2,1)}, bf16[2,4,96,128]{3,2,1,0:T(8,128)(2,1)}) custom-call(s32[3]{0:T(128)} %pad_add_fusion.meta_ref, f32[1,3072]{1,0:T(1,128)} %gate_ref.3, bf16[128,3072]{1,0:T(8,128)(2,1)} %bitcast.31), custom_call_target="tpu_custom_call" | custom-call | bytes 1572864 | tf_op jit(solution)/shard_map/pallas_call | solution.py:351
  18.8 1.5 %collective-permute-start.6 = (bf16[2,4,96,128]{3,2,1,0:T(8,128)(2,1)}, bf16[2,4,96,128]{3,2,1,0:T(8,128)(2,1)S(1)}, u32[]{:S(2)}, u32[]{:S(2)}) collective-permute-start(bf16[2,4,96,128]{3,2,1,0:T(8,128)(2,1)} %get-tuple-element.50), channel_id=1, source_target_pairs={{0,8},{8,0},{16,24},{24,16},{1,9},{9,1},{17,25},{25,17},{2,10},{10... | collective-permute-start | bytes 589832 | tf_op jit(solution)/shard_map/ppermute | solution.py:617
  20.3 16.2 %collective-permute-done.1.refs_0_ = bf16[2,320,128]{2,1,0:T(8,128)(2,1)S(1)} collective-permute-done((bf16[2,320,128]{2,1,0:T(8,128)(2,1)S(1)}, bf16[2,320,128]{2,1,0:T(8,128)(2,1)S(1)}, u32[]{:S(2)}, u32[]{:S(2)}) %collective-permute-start.1) | collective-permute-done | bytes 163872 | tf_op jit(solution)/shard_map/ppermute | solution.py:610
  36.6 1.7 %collective-permute-start.2 = (bf16[1,320,128]{2,1,0:T(8,128)(2,1)S(1)}, bf16[1,320,128]{2,1,0:T(8,128)(2,1)S(1)}, u32[]{:S(2)}, u32[]{:S(2)}) collective-permute-start(bf16[1,320,128]{2,1,0:T(8,128)(2,1)S(1)} %get-tuple-element.45), channel_id=1, source_target_pairs={{0,4},{2,6},{4,0},{6,2},{1,5},{3,7},{5,1},{7,3},{8,12},{10,14},{12... | collective-permute-start | bytes 245768 | tf_op jit(solution)/shard_map/ppermute | solution.py:610
  38.4 4.6 %collective-permute-done.2.got_ref = bf16[1,320,128]{2,1,0:T(8,128)(2,1)S(1)} collective-permute-done((bf16[1,320,128]{2,1,0:T(8,128)(2,1)S(1)}, bf16[1,320,128]{2,1,0:T(8,128)(2,1)S(1)}, u32[]{:S(2)}, u32[]{:S(2)}) %collective-permute-start.2) | collective-permute-done | bytes 81952 | tf_op jit(solution)/shard_map/ppermute | solution.py:610
  42.9 1.0 copy-done.4
  43.9 0.3 shard_map.168.refs_0_
  44.2 1.7 %collective-permute-start.11 = (bf16[2,4,96,128]{3,2,1,0:T(8,128)(2,1)}, bf16[2,4,96,128]{3,2,1,0:T(8,128)(2,1)}, u32[]{:S(2)}, u32[]{:S(2)}) collective-permute-start(bf16[2,4,96,128]{3,2,1,0:T(8,128)(2,1)} %get-tuple-element.56), channel_id=1, source_target_pairs={{0,16},{8,24},{16,0},{24,8},{1,17},{9,25},{17,1},{25,9},{2,18},{10... | collective-permute-start | bytes 589832 | tf_op jit(solution)/shard_map/ppermute | solution.py:617
  45.9 1.4 %collective-permute-start.12 = (bf16[2,4,96,128]{3,2,1,0:T(8,128)(2,1)}, bf16[2,4,96,128]{3,2,1,0:T(8,128)(2,1)}, u32[]{:S(2)}, u32[]{:S(2)}) collective-permute-start(bf16[2,4,96,128]{3,2,1,0:T(8,128)(2,1)} %get-tuple-element.57), channel_id=1, source_target_pairs={{0,24},{8,16},{16,8},{24,0},{1,25},{9,17},{17,9},{25,1},{2,26},{10... | collective-permute-start | bytes 589832 | tf_op jit(solution)/shard_map/ppermute | solution.py:617
  47.4 2.0 %shard_map.169 = (bf16[128,384]{1,0:T(8,128)(2,1)S(1)}, bf16[128,384]{1,0:T(8,128)(2,1)S(1)}, bf16[32,384]{1,0:T(8,128)(2,1)S(1)}) custom-call(bf16[4912,128]{1,0:T(8,128)(2,1)S(1)} %shard_map.168.refs_0_, bf16[4912,128]{1,0:T(8,128)(2,1)S(1)} %collective-permute-done.7.refs_1_), custom_call_target="tpu_custom_call" | custom-call | flops 481296384 | bytes 2113536 | tf_op jit(solution)/shard_map/pallas_call | solution.py:291
  49.5 0.8 collective-permute-start.8
  50.2 2.1 %collective-permute-start.9 = (bf16[136,384]{1,0:T(8,128)(2,1)S(1)}, bf16[136,384]{1,0:T(8,128)(2,1)S(1)}, u32[]{:S(2)}, u32[]{:S(2)}) collective-permute-start(bf16[136,384]{1,0:T(8,128)(2,1)S(1)} %pad_maximum_fusion.1), channel_id=1, source_target_pairs={{0,6},{2,4},{4,2},{6,0},{1,7},{3,5},{5,3},{7,1},{8,14},{10,12},{12... | collective-permute-start | bytes 313352 | tf_op jit(solution)/shard_map/ppermute | solution.py:610
  52.3 1.9 %shard_map.170 = (bf16[128,384]{1,0:T(8,128)(2,1)S(1)}, bf16[128,384]{1,0:T(8,128)(2,1)S(1)}) custom-call(bf16[4912,128]{1,0:T(8,128)(2,1)S(1)} %shard_map.168.refs_0_, bf16[4912,128]{1,0:T(8,128)(2,1)S(1)} %collective-permute-done.7.refs_1_, bf16[32,384]{1,0:T(8,128)(2,1)S(1)} %get-tuple-element.52.refs_2_), custom_call_target="tpu_custom_call" | custom-call | flops 427819008 | bytes 2064384 | tf_op jit(solution)/shard_map/pallas_call | solution.py:291
  54.2 0.8 collective-permute-start.10
  55.1 4.8 %collective-permute-done.8.refs_0_ = bf16[136,384]{1,0:T(8,128)(2,1)S(1)} collective-permute-done((bf16[136,384]{1,0:T(8,128)(2,1)S(1)}, bf16[136,384]{1,0:T(8,128)(2,1)S(1)}, u32[]{:S(2)}, u32[]{:S(2)}) %collective-permute-start.8) | collective-permute-done | bytes 104480 | tf_op jit(solution)/shard_map/ppermute | solution.py:610
  60.0 1.9 %collective-permute-done.10.refs_2_ = bf16[136,384]{1,0:T(8,128)(2,1)S(1)} collective-permute-done((bf16[136,384]{1,0:T(8,128)(2,1)S(1)}, bf16[136,384]{1,0:T(8,128)(2,1)S(1)}, u32[]{:S(2)}, u32[]{:S(2)}) %collective-permute-start.10) | collective-permute-done | bytes 104480 | tf_op jit(solution)/shard_map/ppermute | solution.py:610
  62.2 1.6 %collective-permute-start.16 = (bf16[128,1536]{1,0:T(8,128)(2,1)S(1)}, bf16[128,1536]{1,0:T(8,128)(2,1)S(1)}, u32[]{:S(2)}, u32[]{:S(2)}) collective-permute-start(bf16[128,1536]{1,0:T(8,128)(2,1)S(1)} %shard_map.171.attn_ref.refs_5_), channel_id=1, source_target_pairs={{0,8},{8,0},{16,24},{24,16},{1,9},{9,1},{17,25},{25,17},{2,10},{10... | collective-permute-start | bytes 1179656 | tf_op jit(solution)/shard_map/ppermute | solution.py:617
  63.8 1.5 %collective-permute-start.15 = (bf16[128,1536]{1,0:T(8,128)(2,1)S(1)}, bf16[128,1536]{1,0:T(8,128)(2,1)S(1)}, u32[]{:S(2)}, u32[]{:S(2)}) collective-permute-start(bf16[128,1536]{1,0:T(8,128)(2,1)S(1)} %shard_map.171.attn_ref.refs_5_), channel_id=1, source_target_pairs={{0,16},{8,24},{16,0},{24,8},{1,17},{9,25},{17,1},{25,9},{2,18},{10... | collective-permute-start | bytes 1179656 | tf_op jit(solution)/shard_map/ppermute | solution.py:617
  65.3 0.4 collective-permute-start.14
  65.7 3.7 %copy-done = bf16[3072,1536]{1,0:T(8,128)(2,1)S(1)} copy-done((bf16[3072,1536]{1,0:T(8,128)(2,1)S(1)}, bf16[3072,1536]{1,0:T(8,128)(2,1)}, u32[]{:S(2)}) %copy-start) | copy-done | bytes 9437208
  69.4 5.7 %shard_map.172 = (bf16[128,3072]{1,0:T(8,128)(2,1)}, bf16[128,1536]{1,0:T(8,128)(2,1)}, f32[4,384]{1,0:T(4,128)S(1)}, bf16[144,1536]{1,0:T(8,128)(2,1)S(1)}) custom-call(s32[3]{0:T(128)S(1)} %copy-done.6, bf16[128,1536]{1,0:T(8,128)(2,1)S(1)} %shard_map.171.attn_ref.refs_5_, bf16[3072,1536]{1,0:T(8,128)(2,1)S(1)} %copy-done, f32[1,3072]{1,0:T(1,128)S(1)} %copy-done.5, ...), custom_call_target="tpu_custom_call" | custom-call | flops 2415919104 | bytes 9437184 | tf_op jit(solution)/shard_map/pallas_call | solution.py:432
  75.1 1.0 shard_map.173
  76.1 0.6 collective-permute-start.13
  76.8 6.2 %collective-permute-done.15.refs_7_ = bf16[128,1536]{1,0:T(8,128)(2,1)S(1)} collective-permute-done((bf16[128,1536]{1,0:T(8,128)(2,1)S(1)}, bf16[128,1536]{1,0:T(8,128)(2,1)S(1)}, u32[]{:S(2)}, u32[]{:S(2)}) %collective-permute-start.15) | collective-permute-done | bytes 393248 | tf_op jit(solution)/shard_map/ppermute | solution.py:617
  82.9 0.5 collective-permute-start.18
  83.5 0.9 slice.32.refs_2_
  84.4 0.9 slice.31.refs_1_
  85.3 1.4 %shard_map.174 = (f32[1168,128]{1,0:T(8,128)S(1)}, bf16[576,128]{1,0:T(8,128)(2,1)S(1)}, bf16[592,128]{1,0:T(8,128)(2,1)S(1)}, f32[576,128]{1,0:T(8,128)S(1)}, f...) custom-call(bf16[1,4,96,128]{3,2,1,0:T(8,128)(2,1)S(1)} %slice.24.refs_0_, ...), custom_call_target="tpu_custom_call" | custom-call | flops 1207959552 | bytes 5111808 | tf_op jit(solution)/shard_map/pallas_call | solution.py:508
  86.7 0.8 collective-permute-start.23
  87.5 1.3 %collective-permute-start.21 = (bf16[576,128]{1,0:T(8,128)(2,1)S(1)}, bf16[576,128]{1,0:T(8,128)(2,1)S(1)}, u32[]{:S(2)}, u32[]{:S(2)}) collective-permute-start(bf16[576,128]{1,0:T(8,128)(2,1)S(1)} %get-tuple-element.65), channel_id=1, source_target_pairs={{0,2},{2,0},{4,6},{6,4},{1,3},{3,1},{5,7},{7,5},{8,10},{10,8},{12,... | collective-permute-start | bytes 442376 | tf_op jit(solution)/shard_map/ppermute | solution.py:610
  88.8 4.8 %collective-permute-done.23.got_ref = bf16[592,128]{1,0:T(8,128)(2,1)S(1)} collective-permute-done((bf16[592,128]{1,0:T(8,128)(2,1)S(1)}, bf16[592,128]{1,0:T(8,128)(2,1)S(1)}, u32[]{:S(2)}, u32[]{:S(2)}) %collective-permute-start.23) | collective-permute-done | bytes 151584 | tf_op jit(solution)/shard_map/ppermute | solution.py:610
  93.7 0.9 collective-permute-start.24
  94.6 1.3 %collective-permute-start.26 = (bf16[592,128]{1,0:T(8,128)(2,1)S(1)}, bf16[592,128]{1,0:T(8,128)(2,1)S(1)}, u32[]{:S(2)}, u32[]{:S(2)}) collective-permute-start(bf16[592,128]{1,0:T(8,128)(2,1)S(1)} %get-tuple-element.72), channel_id=1, source_target_pairs={{0,2},{2,0},{4,6},{6,4},{1,3},{3,1},{5,7},{7,5},{8,10},{10,8},{12,... | collective-permute-start | bytes 454664 | tf_op jit(solution)/shard_map/ppermute | solution.py:610
  95.9 1.3 %collective-permute-done.21.got_ref = bf16[576,128]{1,0:T(8,128)(2,1)S(1)} collective-permute-done((bf16[576,128]{1,0:T(8,128)(2,1)S(1)}, bf16[576,128]{1,0:T(8,128)(2,1)S(1)}, u32[]{:S(2)}, u32[]{:S(2)}) %collective-permute-start.21) | collective-permute-done | bytes 147488 | tf_op jit(solution)/shard_map/ppermute | solution.py:610
  97.2 0.3 collective-permute-start.22
  97.5 1.7 %collective-permute-start.25 = (bf16[576,128]{1,0:T(8,128)(2,1)S(1)}, bf16[576,128]{1,0:T(8,128)(2,1)S(1)}, u32[]{:S(2)}, u32[]{:S(2)}) collective-permute-start(bf16[576,128]{1,0:T(8,128)(2,1)S(1)} %get-tuple-element.71), channel_id=1, source_target_pairs={{0,2},{2,0},{4,6},{6,4},{1,3},{3,1},{5,7},{7,5},{8,10},{10,8},{12,... | collective-permute-start | bytes 442376 | tf_op jit(solution)/shard_map/ppermute | solution.py:610
  99.1 9.3 %collective-permute-done.22.far_low = bf16[576,128]{1,0:T(8,128)(2,1)S(1)} collective-permute-done((bf16[576,128]{1,0:T(8,128)(2,1)S(1)}, bf16[576,128]{1,0:T(8,128)(2,1)S(1)}, u32[]{:S(2)}, u32[]{:S(2)}) %collective-permute-start.22) | collective-permute-done | bytes 147488 | tf_op jit(solution)/shard_map/ppermute | solution.py:610
  108.4 0.2 collective-permute-done.25.near_low
  108.6 0.9 shard_map.177
  (55 shorter events, 1.0 us)
Async XLA Ops:
  1.3 46.0 %copy-start.8 = (s32[1,64]{1,0:T(1,128)S(1)}, s32[1,64]{1,0:T(1,128)}, u32[]{:S(2)}) copy-start(s32[1,64]{1,0:T(1,128)} %src_ref.1) | copy-start | bytes 772
  7.0 5.8 %collective-permute-start = (bf16[4,320,128]{2,1,0:T(8,128)(2,1)}, bf16[4,320,128]{2,1,0:T(8,128)(2,1)S(1)}, u32[]{:S(2)}, u32[]{:S(2)}) collective-permute-start(bf16[4,320,128]{2,1,0:T(8,128)(2,1)} %get-tuple-element.41), channel_id=1, source_target_pairs={{0,1},{2,3},{4,5},{6,7},{1,0},{3,2},{5,4},{7,6},{8,9},{10,11},{12,... | collective-permute-start | bytes 983048 | tf_op jit(solution)/shard_map/ppermute | solution.py:614
  7.5 30.9 %collective-permute-start.3 = (bf16[1152,128]{1,0:T(8,128)(2,1)}, bf16[1152,128]{1,0:T(8,128)(2,1)S(1)}, u32[]{:S(2)}, u32[]{:S(2)}) collective-permute-start(bf16[1152,128]{1,0:T(8,128)(2,1)} %get-tuple-element.47), channel_id=1, source_target_pairs={{0,4},{2,6},{4,0},{6,2},{1,5},{3,7},{5,1},{7,3},{8,12},{10,14},{12... | collective-permute-start | bytes 884744 | tf_op jit(solution)/shard_map/ppermute | solution.py:610
  11.1 27.2 %collective-permute-start.4 = (bf16[1152,128]{1,0:T(8,128)(2,1)}, bf16[1152,128]{1,0:T(8,128)(2,1)S(1)}, u32[]{:S(2)}, u32[]{:S(2)}) collective-permute-start(bf16[1152,128]{1,0:T(8,128)(2,1)} %get-tuple-element.48), channel_id=1, source_target_pairs={{0,6},{2,4},{4,2},{6,0},{1,7},{3,5},{5,3},{7,1},{8,14},{10,12},{12... | collective-permute-start | bytes 884744 | tf_op jit(solution)/shard_map/ppermute | solution.py:610
  12.5 25.9 %collective-permute-start.5 = (bf16[1152,128]{1,0:T(8,128)(2,1)}, bf16[1152,128]{1,0:T(8,128)(2,1)S(1)}, u32[]{:S(2)}, u32[]{:S(2)}) collective-permute-start(bf16[1152,128]{1,0:T(8,128)(2,1)} %get-tuple-element.49), channel_id=1, source_target_pairs={{0,2},{2,0},{4,6},{6,4},{1,3},{3,1},{5,7},{7,5},{8,10},{10,8},{12,... | collective-permute-start | bytes 884744 | tf_op jit(solution)/shard_map/ppermute | solution.py:610
  12.7 1.1 %copy-start.2 = (f32[4,336,128]{2,1,0:T(8,128)S(1)}, f32[4,336,128]{2,1,0:T(8,128)}, u32[]{:S(2)}) copy-start(f32[4,336,128]{2,1,0:T(8,128)} %get-tuple-element.40.own_ref) | copy-start | bytes 2064388
  14.0 22.5 %collective-permute-start.1 = (bf16[2,320,128]{2,1,0:T(8,128)(2,1)S(1)}, bf16[2,320,128]{2,1,0:T(8,128)(2,1)S(1)}, u32[]{:S(2)}, u32[]{:S(2)}) collective-permute-start(bf16[2,320,128]{2,1,0:T(8,128)(2,1)S(1)} %get-tuple-element.43), channel_id=1, source_target_pairs={{0,2},{2,0},{4,6},{6,4},{1,3},{3,1},{5,7},{7,5},{8,10},{10,8},{12,... | collective-permute-start | bytes 491528 | tf_op jit(solution)/shard_map/ppermute | solution.py:610
  18.8 19.6 %collective-permute-start.6 = (bf16[2,4,96,128]{3,2,1,0:T(8,128)(2,1)}, bf16[2,4,96,128]{3,2,1,0:T(8,128)(2,1)S(1)}, u32[]{:S(2)}, u32[]{:S(2)}) collective-permute-start(bf16[2,4,96,128]{3,2,1,0:T(8,128)(2,1)} %get-tuple-element.50), channel_id=1, source_target_pairs={{0,8},{8,0},{16,24},{24,16},{1,9},{9,1},{17,25},{25,17},{2,10},{10... | collective-permute-start | bytes 589832 | tf_op jit(solution)/shard_map/ppermute | solution.py:617
  36.6 6.3 %collective-permute-start.2 = (bf16[1,320,128]{2,1,0:T(8,128)(2,1)S(1)}, bf16[1,320,128]{2,1,0:T(8,128)(2,1)S(1)}, u32[]{:S(2)}, u32[]{:S(2)}) collective-permute-start(bf16[1,320,128]{2,1,0:T(8,128)(2,1)S(1)} %get-tuple-element.45), channel_id=1, source_target_pairs={{0,4},{2,6},{4,0},{6,2},{1,5},{3,7},{5,1},{7,3},{8,12},{10,14},{12... | collective-permute-start | bytes 245768 | tf_op jit(solution)/shard_map/ppermute | solution.py:610
  42.9 1.0 copy-start.4
  43.9 21.8 %copy-start.1 = (bf16[1,128,3072]{2,1,0:T(8,128)(2,1)S(1)}, bf16[1,128,3072]{2,1,0:T(8,128)(2,1)}, u32[]{:S(2)}) copy-start(bf16[1,128,3072]{2,1,0:T(8,128)(2,1)} %param.25) | copy-start | bytes 2359300
  43.9 21.8 %copy-start.5 = (f32[1,3072]{1,0:T(1,128)S(1)}, f32[1,3072]{1,0:T(1,128)}, u32[]{:S(2)}) copy-start(f32[1,3072]{1,0:T(1,128)} %gate_ref.3) | copy-start | bytes 36868
  43.9 21.8 %copy-start.6 = (s32[3]{0:T(128)S(1)}, s32[3]{0:T(128)}, u32[]{:S(2)}) copy-start(s32[3]{0:T(128)} %pad_add_fusion.meta_ref) | copy-start | bytes 40
  44.1 3.3 %collective-permute-start.7 = (bf16[4912,128]{1,0:T(8,128)(2,1)S(1)}, bf16[4912,128]{1,0:T(8,128)(2,1)S(1)}, u32[]{:S(2)}, u32[]{:S(2)}) collective-permute-start(bf16[4912,128]{1,0:T(8,128)(2,1)S(1)} %shard_map.168.refs_0_), channel_id=1, source_target_pairs={{0,1},{2,3},{4,5},{6,7},{1,0},{3,2},{5,4},{7,6},{8,9},{10,11},{12,... | collective-permute-start | bytes 3772424 | tf_op jit(solution)/shard_map/ppermute | solution.py:614
  44.2 17.8 %collective-permute-start.11 = (bf16[2,4,96,128]{3,2,1,0:T(8,128)(2,1)}, bf16[2,4,96,128]{3,2,1,0:T(8,128)(2,1)}, u32[]{:S(2)}, u32[]{:S(2)}) collective-permute-start(bf16[2,4,96,128]{3,2,1,0:T(8,128)(2,1)} %get-tuple-element.56), channel_id=1, source_target_pairs={{0,16},{8,24},{16,0},{24,8},{1,17},{9,25},{17,1},{25,9},{2,18},{10... | collective-permute-start | bytes 589832 | tf_op jit(solution)/shard_map/ppermute | solution.py:617
  45.9 16.2 %collective-permute-start.12 = (bf16[2,4,96,128]{3,2,1,0:T(8,128)(2,1)}, bf16[2,4,96,128]{3,2,1,0:T(8,128)(2,1)}, u32[]{:S(2)}, u32[]{:S(2)}) collective-permute-start(bf16[2,4,96,128]{3,2,1,0:T(8,128)(2,1)} %get-tuple-element.57), channel_id=1, source_target_pairs={{0,24},{8,16},{16,8},{24,0},{1,25},{9,17},{17,9},{25,1},{2,26},{10... | collective-permute-start | bytes 589832 | tf_op jit(solution)/shard_map/ppermute | solution.py:617
  49.5 10.4 %collective-permute-start.8 = (bf16[136,384]{1,0:T(8,128)(2,1)S(1)}, bf16[136,384]{1,0:T(8,128)(2,1)S(1)}, u32[]{:S(2)}, u32[]{:S(2)}) collective-permute-start(bf16[136,384]{1,0:T(8,128)(2,1)S(1)} %pad_maximum_fusion), channel_id=1, source_target_pairs={{0,4},{2,6},{4,0},{6,2},{1,5},{3,7},{5,1},{7,3},{8,12},{10,14},{12... | collective-permute-start | bytes 313352 | tf_op jit(solution)/shard_map/ppermute | solution.py:610
  50.2 9.7 %collective-permute-start.9 = (bf16[136,384]{1,0:T(8,128)(2,1)S(1)}, bf16[136,384]{1,0:T(8,128)(2,1)S(1)}, u32[]{:S(2)}, u32[]{:S(2)}) collective-permute-start(bf16[136,384]{1,0:T(8,128)(2,1)S(1)} %pad_maximum_fusion.1), channel_id=1, source_target_pairs={{0,6},{2,4},{4,2},{6,0},{1,7},{3,5},{5,3},{7,1},{8,14},{10,12},{12... | collective-permute-start | bytes 313352 | tf_op jit(solution)/shard_map/ppermute | solution.py:610
  54.2 7.7 %collective-permute-start.10 = (bf16[136,384]{1,0:T(8,128)(2,1)S(1)}, bf16[136,384]{1,0:T(8,128)(2,1)S(1)}, u32[]{:S(2)}, u32[]{:S(2)}) collective-permute-start(bf16[136,384]{1,0:T(8,128)(2,1)S(1)} %pad_maximum_fusion.2), channel_id=1, source_target_pairs={{0,2},{2,0},{4,6},{6,4},{1,3},{3,1},{5,7},{7,5},{8,10},{10,8},{12,... | collective-permute-start | bytes 313352 | tf_op jit(solution)/shard_map/ppermute | solution.py:610
  62.0 13.0 %copy-start.7 = (bf16[1,8,1536]{2,1,0:T(8,128)(2,1)}, bf16[1,8,1536]{2,1,0:T(8,128)(2,1)S(1)}, u32[]{:S(2)}) copy-start(bf16[1,8,1536]{2,1,0:T(8,128)(2,1)S(1)} %get-tuple-element.75) | copy-start | bytes 73732
  62.1 13.0 %copy-start.3 = (bf16[2,4,96,128]{3,2,1,0:T(8,128)(2,1)S(1)}, bf16[2,4,96,128]{3,2,1,0:T(8,128)(2,1)}, u32[]{:S(2)}) copy-start(bf16[2,4,96,128]{3,2,1,0:T(8,128)(2,1)} %get-tuple-element.60.refs_0_) | copy-start | bytes 589828
  62.2 14.5 %collective-permute-start.16 = (bf16[128,1536]{1,0:T(8,128)(2,1)S(1)}, bf16[128,1536]{1,0:T(8,128)(2,1)S(1)}, u32[]{:S(2)}, u32[]{:S(2)}) collective-permute-start(bf16[128,1536]{1,0:T(8,128)(2,1)S(1)} %shard_map.171.attn_ref.refs_5_), channel_id=1, source_target_pairs={{0,8},{8,0},{16,24},{24,16},{1,9},{9,1},{17,25},{25,17},{2,10},{10... | collective-permute-start | bytes 1179656 | tf_op jit(solution)/shard_map/ppermute | solution.py:617
  63.8 19.2 %collective-permute-start.15 = (bf16[128,1536]{1,0:T(8,128)(2,1)S(1)}, bf16[128,1536]{1,0:T(8,128)(2,1)S(1)}, u32[]{:S(2)}, u32[]{:S(2)}) collective-permute-start(bf16[128,1536]{1,0:T(8,128)(2,1)S(1)} %shard_map.171.attn_ref.refs_5_), channel_id=1, source_target_pairs={{0,16},{8,24},{16,0},{24,8},{1,17},{9,25},{17,1},{25,9},{2,18},{10... | collective-permute-start | bytes 1179656 | tf_op jit(solution)/shard_map/ppermute | solution.py:617
  65.3 17.7 %collective-permute-start.14 = (bf16[128,1536]{1,0:T(8,128)(2,1)S(1)}, bf16[128,1536]{1,0:T(8,128)(2,1)S(1)}, u32[]{:S(2)}, u32[]{:S(2)}) collective-permute-start(bf16[128,1536]{1,0:T(8,128)(2,1)S(1)} %shard_map.171.attn_ref.refs_5_), channel_id=1, source_target_pairs={{0,24},{8,16},{16,8},{24,0},{1,25},{9,17},{17,9},{25,1},{2,26},{10... | collective-permute-start | bytes 1179656 | tf_op jit(solution)/shard_map/ppermute | solution.py:617
  65.7 3.7 %copy-start = (bf16[3072,1536]{1,0:T(8,128)(2,1)S(1)}, bf16[3072,1536]{1,0:T(8,128)(2,1)}, u32[]{:S(2)}) copy-start(bf16[3072,1536]{1,0:T(8,128)(2,1)} %w_ref.3) | copy-start | bytes 28311556
  75.1 10.2 %collective-permute-start.17 = (bf16[144,1536]{1,0:T(8,128)(2,1)S(1)}, bf16[144,1536]{1,0:T(8,128)(2,1)S(1)}, u32[]{:S(2)}, u32[]{:S(2)}) collective-permute-start(bf16[144,1536]{1,0:T(8,128)(2,1)S(1)} %get-tuple-element.61), channel_id=1, source_target_pairs={{0,1},{2,3},{4,5},{6,7},{1,0},{3,2},{5,4},{7,6},{8,9},{10,11},{12,... | collective-permute-start | bytes 1327112 | tf_op jit(solution)/shard_map/ppermute | solution.py:614
  76.1 9.2 %collective-permute-start.13 = (bf16[4,4,96,128]{3,2,1,0:T(8,128)(2,1)S(1)}, bf16[4,4,96,128]{3,2,1,0:T(8,128)(2,1)S(1)}, u32[]{:S(2)}, u32[]{:S(2)}) collective-permute-start(bf16[4,4,96,128]{3,2,1,0:T(8,128)(2,1)S(1)} %shard_map.173), channel_id=1, source_target_pairs={{0,1},{2,3},{4,5},{6,7},{1,0},{3,2},{5,4},{7,6},{8,9},{10,11},{12,... | collective-permute-start | bytes 1179656 | tf_op jit(solution)/shard_map/ppermute | solution.py:614
  76.7 8.6 %collective-permute-start.20 = (bf16[128,1536]{1,0:T(8,128)(2,1)S(1)}, bf16[128,1536]{1,0:T(8,128)(2,1)S(1)}, u32[]{:S(2)}, u32[]{:S(2)}) collective-permute-start(bf16[128,1536]{1,0:T(8,128)(2,1)S(1)} %collective-permute-done.16.refs_8_), channel_id=1, source_target_pairs={{0,1},{2,3},{4,5},{6,7},{1,0},{3,2},{5,4},{7,6},{8,9},{10,11},{12,... | collective-permute-start | bytes 1179656 | tf_op jit(solution)/shard_map/ppermute | solution.py:614
  82.9 2.4 %collective-permute-start.19 = (bf16[128,1536]{1,0:T(8,128)(2,1)S(1)}, bf16[128,1536]{1,0:T(8,128)(2,1)S(1)}, u32[]{:S(2)}, u32[]{:S(2)}) collective-permute-start(bf16[128,1536]{1,0:T(8,128)(2,1)S(1)} %collective-permute-done.15.refs_7_), channel_id=1, source_target_pairs={{0,1},{2,3},{4,5},{6,7},{1,0},{3,2},{5,4},{7,6},{8,9},{10,11},{12,... | collective-permute-start | bytes 1179656 | tf_op jit(solution)/shard_map/ppermute | solution.py:614
  82.9 2.4 %collective-permute-start.18 = (bf16[128,1536]{1,0:T(8,128)(2,1)S(1)}, bf16[128,1536]{1,0:T(8,128)(2,1)S(1)}, u32[]{:S(2)}, u32[]{:S(2)}) collective-permute-start(bf16[128,1536]{1,0:T(8,128)(2,1)S(1)} %collective-permute-done.14.refs_6_), channel_id=1, source_target_pairs={{0,1},{2,3},{4,5},{6,7},{1,0},{3,2},{5,4},{7,6},{8,9},{10,11},{12,... | collective-permute-start | bytes 1179656 | tf_op jit(solution)/shard_map/ppermute | solution.py:614
  86.7 6.9 %collective-permute-start.23 = (bf16[592,128]{1,0:T(8,128)(2,1)S(1)}, bf16[592,128]{1,0:T(8,128)(2,1)S(1)}, u32[]{:S(2)}, u32[]{:S(2)}) collective-permute-start(bf16[592,128]{1,0:T(8,128)(2,1)S(1)} %get-tuple-element.67), channel_id=1, source_target_pairs={{0,2},{2,0},{4,6},{6,4},{1,3},{3,1},{5,7},{7,5},{8,10},{10,8},{12,... | collective-permute-start | bytes 454664 | tf_op jit(solution)/shard_map/ppermute | solution.py:610
  87.5 9.7 %collective-permute-start.21 = (bf16[576,128]{1,0:T(8,128)(2,1)S(1)}, bf16[576,128]{1,0:T(8,128)(2,1)S(1)}, u32[]{:S(2)}, u32[]{:S(2)}) collective-permute-start(bf16[576,128]{1,0:T(8,128)(2,1)S(1)} %get-tuple-element.65), channel_id=1, source_target_pairs={{0,2},{2,0},{4,6},{6,4},{1,3},{3,1},{5,7},{7,5},{8,10},{10,8},{12,... | collective-permute-start | bytes 442376 | tf_op jit(solution)/shard_map/ppermute | solution.py:610
  93.7 15.0 %collective-permute-start.24 = (bf16[592,128]{1,0:T(8,128)(2,1)S(1)}, bf16[592,128]{1,0:T(8,128)(2,1)S(1)}, u32[]{:S(2)}, u32[]{:S(2)}) collective-permute-start(bf16[592,128]{1,0:T(8,128)(2,1)S(1)} %get-tuple-element.70), channel_id=1, source_target_pairs={{0,4},{2,6},{4,0},{6,2},{1,5},{3,7},{5,1},{7,3},{8,12},{10,14},{12... | collective-permute-start | bytes 454664 | tf_op jit(solution)/shard_map/ppermute | solution.py:610
  94.6 14.1 %collective-permute-start.26 = (bf16[592,128]{1,0:T(8,128)(2,1)S(1)}, bf16[592,128]{1,0:T(8,128)(2,1)S(1)}, u32[]{:S(2)}, u32[]{:S(2)}) collective-permute-start(bf16[592,128]{1,0:T(8,128)(2,1)S(1)} %get-tuple-element.72), channel_id=1, source_target_pairs={{0,2},{2,0},{4,6},{6,4},{1,3},{3,1},{5,7},{7,5},{8,10},{10,8},{12,... | collective-permute-start | bytes 454664 | tf_op jit(solution)/shard_map/ppermute | solution.py:610
  97.2 11.2 %collective-permute-start.22 = (bf16[576,128]{1,0:T(8,128)(2,1)S(1)}, bf16[576,128]{1,0:T(8,128)(2,1)S(1)}, u32[]{:S(2)}, u32[]{:S(2)}) collective-permute-start(bf16[576,128]{1,0:T(8,128)(2,1)S(1)} %shard_map.175), channel_id=1, source_target_pairs={{0,4},{2,6},{4,0},{6,2},{1,5},{3,7},{5,1},{7,3},{8,12},{10,14},{12... | collective-permute-start | bytes 442376 | tf_op jit(solution)/shard_map/ppermute | solution.py:610
  97.5 11.2 %collective-permute-start.25 = (bf16[576,128]{1,0:T(8,128)(2,1)S(1)}, bf16[576,128]{1,0:T(8,128)(2,1)S(1)}, u32[]{:S(2)}, u32[]{:S(2)}) collective-permute-start(bf16[576,128]{1,0:T(8,128)(2,1)S(1)} %get-tuple-element.71), channel_id=1, source_target_pairs={{0,2},{2,0},{4,6},{6,4},{1,3},{3,1},{5,7},{7,5},{8,10},{10,8},{12,... | collective-permute-start | bytes 442376 | tf_op jit(solution)/shard_map/ppermute | solution.py:610

commit v16 on v15

--- a/solution.py
+++ b/solution.py
@@ -363,7 +363,7 @@
     pieces, outs = refs[:n_dp], refs[n_dp:]
     for j, out in enumerate(outs):
         for k, piece in enumerate(pieces):
-            out[k] = piece[j + 1]
+            out[k] = piece[j]
 
 
 def gather_parts(pieces):
@@ -371,11 +371,11 @@
     shape = (len(pieces),) + pieces[0].shape[1:]
     return pl.pallas_call(
         functools.partial(gather_kernel, len(pieces)),
-        out_shape=[jax.ShapeDtypeStruct(shape, bf16)] * (parts - 1),
+        out_shape=[jax.ShapeDtypeStruct(shape, bf16)] * parts,
         in_specs=[VMEM] * len(pieces),
-        out_specs=[VMEM] * (parts - 1),
-        compiler_params=params(),
-        cost_estimate=cost(0, 4 * math.prod(shape) * (parts - 1)),
+        out_specs=[VMEM] * parts,
+        compiler_params=params(),
+        cost_estimate=cost(0, 4 * math.prod(shape) * parts),
     )(*pieces)
 
 
@@ -665,8 +665,8 @@
     back = [back[k] for k in order + [0]]
     gg_dp += [to_dp(gg[k], k) for k in range(2, n_dp)]
     dp_order = [0] + list(range(n_dp - 1, 0, -1))
-    lefts = [gg_dp[k][:1] for k in dp_order]
-    lefts += [to_oc(g, j + 1) for j, g in enumerate(gather_parts([gg_dp[k] for k in dp_order]))]
+    lefts = gather_parts([gg_dp[k] for k in dp_order])
+    lefts = [to_oc(g, j) if j else g for j, g in enumerate(lefts)]
     image_attn = assemble(where, back, order + [0], gg_dp[1:], image_local)
     text_attn = jnp.zeros((slot_local, inner_width), bf16)
     own_usable = part(slot_source[0] < caption_len[0], seq, slot_local, 0)

time: 110 us -> 110 us (level)
  waiting for transfers between devices: 49.2 us -> 51.1 us
  local copies, waits for them, and re-layouts: 7.67 us -> 5.86 us
    slice x4 -> x0, local copies, waits for them, and re-layouts: 1.81 us -> none  [on_device(): lefts = [gg_dp[k][:1] for k in dp_order]]
    ppermute x7, waiting for transfers between devices: 0.02 us -> 1.77 us  [to_oc(): return lax.ppermute(x, 'seq', perm)]
  transfers between devices with their start and end apart: 27 -> 27, of which waited for: 9 -> 11; matrix products, arithmetic and copies ran while one was open for 3% -> 1% of each run, Pallas kernels for 12% -> 12%
where the time goes in v16:
time: 110 us
  waiting for transfers between devices  51.1 us (46%)
  starting transfers between devices  28.5 us (26%)
  Pallas kernels  21.7 us (20%)
  local copies, waits for them, and re-layouts  5.86 us (5%)
  between operations  1.46 us (1%)
    ppermute x14, waiting for transfers between devices, to_z(): return lax.ppermute(x, 'seq', perm)  43.2 us
    ppermute x14, starting transfers between devices, to_z(): return lax.ppermute(x, 'seq', perm)  18.6 us
    ppermute x6, starting transfers between devices, to_dp(): return lax.ppermute(x, 'dp', [(a, a ^ k) for a in range(n_dp)])  8.13 us
    ppermute x6, waiting for transfers between devices, to_dp(): return lax.ppermute(x, 'dp', [(a, a ^ k) for a in range(n_dp)])  6.15 us
    unnamed x18, local copies, waits for them, and re-layouts  5.76 us
    pallas_call x1, Pallas kernels, text_project(): pl.pallas_call(functools.partial(text_kernel, groups, heads, place_of, wh...  5.66 us
    pallas_call x1, Pallas kernels, project(): pl.pallas_call(functools.partial(project_kernel, groups, parts, place_of)...  5.65 us
    pallas_call x2, Pallas kernels, attention(): pl.pallas_call(functools.partial(attention_kernel, n_pieces, len(blocks),...  3.89 us
  transfers between devices with their start and end apart: 27, of which 11 were waited for; matrix products, arithmetic and copies ran while one was open for 1% of the time, Pallas kernels for 12%

profile of v16, /device:TPU:0, one launch (start us, length us, event | category | flops | bytes accessed | tf_op | source)
XLA Modules:
  0.0 109.6 jit_solution(7289945708382278203)
XLA Ops:
  1.3 5.7 %shard_map.164 = (f32[4,336,128]{2,1,0:T(8,128)}, bf16[1152,128]{1,0:T(8,128)(2,1)}, bf16[1152,128]{1,0:T(8,128)(2,1)}, bf16[1152,128]{1,0:T(8,128)(2,1)}, bf16[...) custom-call(s32[1]{0:T(128)} %copy.22.len_ref, s32[1,64]{1,0:T(1,128)} %src_ref.1, bf16[64,512]{1,0:T(8,128)(2,1)} %bitcast.36, ...), custom_call_target="tpu_custom_call" | custom-call | flops 301989888 | bytes 4718592 | tf_op jit(solution)/shard_map/pallas_call | solution.py:140
  7.0 0.5 collective-permute-start
  7.5 3.7 %collective-permute-start.3 = (bf16[1152,128]{1,0:T(8,128)(2,1)}, bf16[1152,128]{1,0:T(8,128)(2,1)S(1)}, u32[]{:S(2)}, u32[]{:S(2)}) collective-permute-start(bf16[1152,128]{1,0:T(8,128)(2,1)} %get-tuple-element.49), channel_id=1, source_target_pairs={{0,4},{2,6},{4,0},{6,2},{1,5},{3,7},{5,1},{7,3},{8,12},{10,14},{12... | collective-permute-start | bytes 884744 | tf_op jit(solution)/shard_map/ppermute | solution.py:610
  11.1 1.4 %collective-permute-start.4 = (bf16[1152,128]{1,0:T(8,128)(2,1)}, bf16[1152,128]{1,0:T(8,128)(2,1)S(1)}, u32[]{:S(2)}, u32[]{:S(2)}) collective-permute-start(bf16[1152,128]{1,0:T(8,128)(2,1)} %get-tuple-element.50), channel_id=1, source_target_pairs={{0,6},{2,4},{4,2},{6,0},{1,7},{3,5},{5,3},{7,1},{8,14},{10,12},{12... | collective-permute-start | bytes 884744 | tf_op jit(solution)/shard_map/ppermute | solution.py:610
  12.5 0.2 collective-permute-start.5
  12.7 1.1 %copy-done.2 = f32[4,336,128]{2,1,0:T(8,128)S(1)} copy-done((f32[4,336,128]{2,1,0:T(8,128)S(1)}, f32[4,336,128]{2,1,0:T(8,128)}, u32[]{:S(2)}) %copy-start.2) | copy-done | bytes 688152
  13.8 0.2 shard_map.165
  14.0 1.9 %collective-permute-start.1 = (bf16[2,320,128]{2,1,0:T(8,128)(2,1)S(1)}, bf16[2,320,128]{2,1,0:T(8,128)(2,1)S(1)}, u32[]{:S(2)}, u32[]{:S(2)}) collective-permute-start(bf16[2,320,128]{2,1,0:T(8,128)(2,1)S(1)} %get-tuple-element.45), channel_id=1, source_target_pairs={{0,2},{2,0},{4,6},{6,4},{1,3},{3,1},{5,7},{7,5},{8,10},{10,8},{12,... | collective-permute-start | bytes 491528 | tf_op jit(solution)/shard_map/ppermute | solution.py:610
  15.9 0.6 pad_add_fusion.meta_ref
  16.5 2.3 %shard_map.167 = (bf16[2,4,96,128]{3,2,1,0:T(8,128)(2,1)}, bf16[2,4,96,128]{3,2,1,0:T(8,128)(2,1)}, bf16[2,4,96,128]{3,2,1,0:T(8,128)(2,1)}, bf16[2,4,96,128]{3,2,1,0:T(8,128)(2,1)}) custom-call(s32[3]{0:T(128)} %pad_add_fusion.meta_ref, f32[1,3072]{1,0:T(1,128)} %gate_ref.3, bf16[128,3072]{1,0:T(8,128)(2,1)} %bitcast.31), custom_call_target="tpu_custom_call" | custom-call | bytes 1572864 | tf_op jit(solution)/shard_map/pallas_call | solution.py:351
  18.8 1.5 %collective-permute-start.6 = (bf16[2,4,96,128]{3,2,1,0:T(8,128)(2,1)}, bf16[2,4,96,128]{3,2,1,0:T(8,128)(2,1)S(1)}, u32[]{:S(2)}, u32[]{:S(2)}) collective-permute-start(bf16[2,4,96,128]{3,2,1,0:T(8,128)(2,1)} %get-tuple-element.52), channel_id=1, source_target_pairs={{0,8},{8,0},{16,24},{24,16},{1,9},{9,1},{17,25},{25,17},{2,10},{10... | collective-permute-start | bytes 589832 | tf_op jit(solution)/shard_map/ppermute | solution.py:617
  20.3 16.2 %collective-permute-done.1.refs_0_ = bf16[2,320,128]{2,1,0:T(8,128)(2,1)S(1)} collective-permute-done((bf16[2,320,128]{2,1,0:T(8,128)(2,1)S(1)}, bf16[2,320,128]{2,1,0:T(8,128)(2,1)S(1)}, u32[]{:S(2)}, u32[]{:S(2)}) %collective-permute-start.1) | collective-permute-done | bytes 163872 | tf_op jit(solution)/shard_map/ppermute | solution.py:610
  36.5 0.2 shard_map.166
  36.6 1.7 %collective-permute-start.2 = (bf16[1,320,128]{2,1,0:T(8,128)(2,1)S(1)}, bf16[1,320,128]{2,1,0:T(8,128)(2,1)S(1)}, u32[]{:S(2)}, u32[]{:S(2)}) collective-permute-start(bf16[1,320,128]{2,1,0:T(8,128)(2,1)S(1)} %get-tuple-element.47), channel_id=1, source_target_pairs={{0,4},{2,6},{4,0},{6,2},{1,5},{3,7},{5,1},{7,3},{8,12},{10,14},{12... | collective-permute-start | bytes 245768 | tf_op jit(solution)/shard_map/ppermute | solution.py:610
  38.4 4.6 %collective-permute-done.2.got_ref = bf16[1,320,128]{2,1,0:T(8,128)(2,1)S(1)} collective-permute-done((bf16[1,320,128]{2,1,0:T(8,128)(2,1)S(1)}, bf16[1,320,128]{2,1,0:T(8,128)(2,1)S(1)}, u32[]{:S(2)}, u32[]{:S(2)}) %collective-permute-start.2) | collective-permute-done | bytes 81952 | tf_op jit(solution)/shard_map/ppermute | solution.py:610
  42.9 1.0 copy-done.3
  43.9 0.3 shard_map.168.refs_0_
  44.2 1.7 %collective-permute-start.11 = (bf16[2,4,96,128]{3,2,1,0:T(8,128)(2,1)}, bf16[2,4,96,128]{3,2,1,0:T(8,128)(2,1)}, u32[]{:S(2)}, u32[]{:S(2)}) collective-permute-start(bf16[2,4,96,128]{3,2,1,0:T(8,128)(2,1)} %get-tuple-element.58), channel_id=1, source_target_pairs={{0,16},{8,24},{16,0},{24,8},{1,17},{9,25},{17,1},{25,9},{2,18},{10... | collective-permute-start | bytes 589832 | tf_op jit(solution)/shard_map/ppermute | solution.py:617
  45.9 1.4 %collective-permute-start.12 = (bf16[2,4,96,128]{3,2,1,0:T(8,128)(2,1)}, bf16[2,4,96,128]{3,2,1,0:T(8,128)(2,1)}, u32[]{:S(2)}, u32[]{:S(2)}) collective-permute-start(bf16[2,4,96,128]{3,2,1,0:T(8,128)(2,1)} %get-tuple-element.59), channel_id=1, source_target_pairs={{0,24},{8,16},{16,8},{24,0},{1,25},{9,17},{17,9},{25,1},{2,26},{10... | collective-permute-start | bytes 589832 | tf_op jit(solution)/shard_map/ppermute | solution.py:617
  47.4 2.0 %shard_map.169 = (bf16[128,384]{1,0:T(8,128)(2,1)S(1)}, bf16[128,384]{1,0:T(8,128)(2,1)S(1)}, bf16[32,384]{1,0:T(8,128)(2,1)S(1)}) custom-call(bf16[4912,128]{1,0:T(8,128)(2,1)S(1)} %shard_map.168.refs_0_, bf16[4912,128]{1,0:T(8,128)(2,1)S(1)} %collective-permute-done.7.refs_1_), custom_call_target="tpu_custom_call" | custom-call | flops 481296384 | bytes 2113536 | tf_op jit(solution)/shard_map/pallas_call | solution.py:291
  49.5 0.8 collective-permute-start.8
  50.2 2.1 %collective-permute-start.9 = (bf16[136,384]{1,0:T(8,128)(2,1)S(1)}, bf16[136,384]{1,0:T(8,128)(2,1)S(1)}, u32[]{:S(2)}, u32[]{:S(2)}) collective-permute-start(bf16[136,384]{1,0:T(8,128)(2,1)S(1)} %pad_maximum_fusion.1), channel_id=1, source_target_pairs={{0,6},{2,4},{4,2},{6,0},{1,7},{3,5},{5,3},{7,1},{8,14},{10,12},{12... | collective-permute-start | bytes 313352 | tf_op jit(solution)/shard_map/ppermute | solution.py:610
  52.3 1.9 %shard_map.170 = (bf16[128,384]{1,0:T(8,128)(2,1)S(1)}, bf16[128,384]{1,0:T(8,128)(2,1)S(1)}) custom-call(bf16[4912,128]{1,0:T(8,128)(2,1)S(1)} %shard_map.168.refs_0_, bf16[4912,128]{1,0:T(8,128)(2,1)S(1)} %collective-permute-done.7.refs_1_, bf16[32,384]{1,0:T(8,128)(2,1)S(1)} %get-tuple-element.54.refs_2_), custom_call_target="tpu_custom_call" | custom-call | flops 427819008 | bytes 2064384 | tf_op jit(solution)/shard_map/pallas_call | solution.py:291
  54.2 0.8 collective-permute-start.10
  55.1 4.8 %collective-permute-done.8.refs_0_ = bf16[136,384]{1,0:T(8,128)(2,1)S(1)} collective-permute-done((bf16[136,384]{1,0:T(8,128)(2,1)S(1)}, bf16[136,384]{1,0:T(8,128)(2,1)S(1)}, u32[]{:S(2)}, u32[]{:S(2)}) %collective-permute-start.8) | collective-permute-done | bytes 104480 | tf_op jit(solution)/shard_map/ppermute | solution.py:610
  60.0 1.9 %collective-permute-done.10.refs_2_ = bf16[136,384]{1,0:T(8,128)(2,1)S(1)} collective-permute-done((bf16[136,384]{1,0:T(8,128)(2,1)S(1)}, bf16[136,384]{1,0:T(8,128)(2,1)S(1)}, u32[]{:S(2)}, u32[]{:S(2)}) %collective-permute-start.10) | collective-permute-done | bytes 104480 | tf_op jit(solution)/shard_map/ppermute | solution.py:610
  62.2 1.6 %collective-permute-start.16 = (bf16[128,1536]{1,0:T(8,128)(2,1)S(1)}, bf16[128,1536]{1,0:T(8,128)(2,1)S(1)}, u32[]{:S(2)}, u32[]{:S(2)}) collective-permute-start(bf16[128,1536]{1,0:T(8,128)(2,1)S(1)} %shard_map.171.attn_ref.refs_2_), channel_id=1, source_target_pairs={{0,8},{8,0},{16,24},{24,16},{1,9},{9,1},{17,25},{25,17},{2,10},{10... | collective-permute-start | bytes 1179656 | tf_op jit(solution)/shard_map/ppermute | solution.py:617
  63.8 1.5 %collective-permute-start.15 = (bf16[128,1536]{1,0:T(8,128)(2,1)S(1)}, bf16[128,1536]{1,0:T(8,128)(2,1)S(1)}, u32[]{:S(2)}, u32[]{:S(2)}) collective-permute-start(bf16[128,1536]{1,0:T(8,128)(2,1)S(1)} %shard_map.171.attn_ref.refs_2_), channel_id=1, source_target_pairs={{0,16},{8,24},{16,0},{24,8},{1,17},{9,25},{17,1},{25,9},{2,18},{10... | collective-permute-start | bytes 1179656 | tf_op jit(solution)/shard_map/ppermute | solution.py:617
  65.3 0.4 collective-permute-start.14
  65.7 3.7 %copy-done = bf16[3072,1536]{1,0:T(8,128)(2,1)S(1)} copy-done((bf16[3072,1536]{1,0:T(8,128)(2,1)S(1)}, bf16[3072,1536]{1,0:T(8,128)(2,1)}, u32[]{:S(2)}) %copy-start) | copy-done | bytes 9437208
  69.4 5.7 %shard_map.172 = (bf16[128,3072]{1,0:T(8,128)(2,1)}, bf16[128,1536]{1,0:T(8,128)(2,1)}, f32[4,384]{1,0:T(4,128)S(1)}, bf16[144,1536]{1,0:T(8,128)(2,1)S(1)}) custom-call(s32[3]{0:T(128)S(1)} %copy-done.6, bf16[128,1536]{1,0:T(8,128)(2,1)S(1)} %shard_map.171.attn_ref.refs_2_, bf16[3072,1536]{1,0:T(8,128)(2,1)S(1)} %copy-done, f32[1,3072]{1,0:T(1,128)S(1)} %copy-done.5, ...), custom_call_target="tpu_custom_call" | custom-call | flops 2415919104 | bytes 9437184 | tf_op jit(solution)/shard_map/pallas_call | solution.py:432
  75.1 1.1 shard_map.173
  76.1 0.6 collective-permute-start.13
  76.8 6.1 %collective-permute-done.15.refs_4_ = bf16[128,1536]{1,0:T(8,128)(2,1)S(1)} collective-permute-done((bf16[128,1536]{1,0:T(8,128)(2,1)S(1)}, bf16[128,1536]{1,0:T(8,128)(2,1)S(1)}, u32[]{:S(2)}, u32[]{:S(2)}) %collective-permute-start.15) | collective-permute-done | bytes 393248 | tf_op jit(solution)/shard_map/ppermute | solution.py:617
  82.9 0.5 collective-permute-start.18
  83.5 1.2 %collective-permute-done.19.refs_8_ = bf16[128,1536]{1,0:T(8,128)(2,1)S(1)} collective-permute-done((bf16[128,1536]{1,0:T(8,128)(2,1)S(1)}, bf16[128,1536]{1,0:T(8,128)(2,1)S(1)}, u32[]{:S(2)}, u32[]{:S(2)}) %collective-permute-start.19) | collective-permute-done | bytes 393248 | tf_op jit(solution)/shard_map/ppermute | solution.py:614
  84.7 0.6 collective-permute-done.18.refs_7_
  85.2 1.4 %shard_map.174 = (f32[1168,128]{1,0:T(8,128)S(1)}, bf16[576,128]{1,0:T(8,128)(2,1)S(1)}, bf16[592,128]{1,0:T(8,128)(2,1)S(1)}, f32[576,128]{1,0:T(8,128)S(1)}, f...) custom-call(bf16[4,4,96,128]{3,2,1,0:T(8,128)(2,1)S(1)} %get-tuple-element.63.refs_0_, ...), custom_call_target="tpu_custom_call" | custom-call | flops 1207959552 | bytes 5111808 | tf_op jit(solution)/shard_map/pallas_call | solution.py:508
  86.6 0.8 collective-permute-start.23
  87.4 1.3 %collective-permute-start.21 = (bf16[576,128]{1,0:T(8,128)(2,1)S(1)}, bf16[576,128]{1,0:T(8,128)(2,1)S(1)}, u32[]{:S(2)}, u32[]{:S(2)}) collective-permute-start(bf16[576,128]{1,0:T(8,128)(2,1)S(1)} %get-tuple-element.69), channel_id=1, source_target_pairs={{0,2},{2,0},{4,6},{6,4},{1,3},{3,1},{5,7},{7,5},{8,10},{10,8},{12,... | collective-permute-start | bytes 442376 | tf_op jit(solution)/shard_map/ppermute | solution.py:610
  88.7 4.8 %collective-permute-done.23.got_ref = bf16[592,128]{1,0:T(8,128)(2,1)S(1)} collective-permute-done((bf16[592,128]{1,0:T(8,128)(2,1)S(1)}, bf16[592,128]{1,0:T(8,128)(2,1)S(1)}, u32[]{:S(2)}, u32[]{:S(2)}) %collective-permute-start.23) | collective-permute-done | bytes 151584 | tf_op jit(solution)/shard_map/ppermute | solution.py:610
  93.5 0.9 collective-permute-start.24
  94.5 1.3 %collective-permute-start.26 = (bf16[592,128]{1,0:T(8,128)(2,1)S(1)}, bf16[592,128]{1,0:T(8,128)(2,1)S(1)}, u32[]{:S(2)}, u32[]{:S(2)}) collective-permute-start(bf16[592,128]{1,0:T(8,128)(2,1)S(1)} %get-tuple-element.76), channel_id=1, source_target_pairs={{0,2},{2,0},{4,6},{6,4},{1,3},{3,1},{5,7},{7,5},{8,10},{10,8},{12,... | collective-permute-start | bytes 454664 | tf_op jit(solution)/shard_map/ppermute | solution.py:610
  95.8 1.2 %collective-permute-done.21.got_ref = bf16[576,128]{1,0:T(8,128)(2,1)S(1)} collective-permute-done((bf16[576,128]{1,0:T(8,128)(2,1)S(1)}, bf16[576,128]{1,0:T(8,128)(2,1)S(1)}, u32[]{:S(2)}, u32[]{:S(2)}) %collective-permute-start.21) | collective-permute-done | bytes 147488 | tf_op jit(solution)/shard_map/ppermute | solution.py:610
  97.0 0.4 collective-permute-start.22
  97.3 1.4 %collective-permute-start.25 = (bf16[576,128]{1,0:T(8,128)(2,1)S(1)}, bf16[576,128]{1,0:T(8,128)(2,1)S(1)}, u32[]{:S(2)}, u32[]{:S(2)}) collective-permute-start(bf16[576,128]{1,0:T(8,128)(2,1)S(1)} %get-tuple-element.75), channel_id=1, source_target_pairs={{0,2},{2,0},{4,6},{6,4},{1,3},{3,1},{5,7},{7,5},{8,10},{10,8},{12,... | collective-permute-start | bytes 442376 | tf_op jit(solution)/shard_map/ppermute | solution.py:610
  98.8 9.8 %collective-permute-done.22.far_low = bf16[576,128]{1,0:T(8,128)(2,1)S(1)} collective-permute-done((bf16[576,128]{1,0:T(8,128)(2,1)S(1)}, bf16[576,128]{1,0:T(8,128)(2,1)S(1)}, u32[]{:S(2)}, u32[]{:S(2)}) %collective-permute-start.22) | collective-permute-done | bytes 147488 | tf_op jit(solution)/shard_map/ppermute | solution.py:610
  108.6 0.9 shard_map.177
  (51 shorter events, 0.9 us)
Async XLA Ops:
  1.3 46.0 %copy-start.8 = (s32[1,64]{1,0:T(1,128)S(1)}, s32[1,64]{1,0:T(1,128)}, u32[]{:S(2)}) copy-start(s32[1,64]{1,0:T(1,128)} %src_ref.1) | copy-start | bytes 772
  7.0 5.8 %collective-permute-start = (bf16[4,320,128]{2,1,0:T(8,128)(2,1)}, bf16[4,320,128]{2,1,0:T(8,128)(2,1)S(1)}, u32[]{:S(2)}, u32[]{:S(2)}) collective-permute-start(bf16[4,320,128]{2,1,0:T(8,128)(2,1)} %get-tuple-element.43), channel_id=1, source_target_pairs={{0,1},{2,3},{4,5},{6,7},{1,0},{3,2},{5,4},{7,6},{8,9},{10,11},{12,... | collective-permute-start | bytes 983048 | tf_op jit(solution)/shard_map/ppermute | solution.py:614
  7.5 30.9 %collective-permute-start.3 = (bf16[1152,128]{1,0:T(8,128)(2,1)}, bf16[1152,128]{1,0:T(8,128)(2,1)S(1)}, u32[]{:S(2)}, u32[]{:S(2)}) collective-permute-start(bf16[1152,128]{1,0:T(8,128)(2,1)} %get-tuple-element.49), channel_id=1, source_target_pairs={{0,4},{2,6},{4,0},{6,2},{1,5},{3,7},{5,1},{7,3},{8,12},{10,14},{12... | collective-permute-start | bytes 884744 | tf_op jit(solution)/shard_map/ppermute | solution.py:610
  11.1 27.2 %collective-permute-start.4 = (bf16[1152,128]{1,0:T(8,128)(2,1)}, bf16[1152,128]{1,0:T(8,128)(2,1)S(1)}, u32[]{:S(2)}, u32[]{:S(2)}) collective-permute-start(bf16[1152,128]{1,0:T(8,128)(2,1)} %get-tuple-element.50), channel_id=1, source_target_pairs={{0,6},{2,4},{4,2},{6,0},{1,7},{3,5},{5,3},{7,1},{8,14},{10,12},{12... | collective-permute-start | bytes 884744 | tf_op jit(solution)/shard_map/ppermute | solution.py:610
  12.5 25.9 %collective-permute-start.5 = (bf16[1152,128]{1,0:T(8,128)(2,1)}, bf16[1152,128]{1,0:T(8,128)(2,1)S(1)}, u32[]{:S(2)}, u32[]{:S(2)}) collective-permute-start(bf16[1152,128]{1,0:T(8,128)(2,1)} %get-tuple-element.51), channel_id=1, source_target_pairs={{0,2},{2,0},{4,6},{6,4},{1,3},{3,1},{5,7},{7,5},{8,10},{10,8},{12,... | collective-permute-start | bytes 884744 | tf_op jit(solution)/shard_map/ppermute | solution.py:610
  12.7 1.1 %copy-start.2 = (f32[4,336,128]{2,1,0:T(8,128)S(1)}, f32[4,336,128]{2,1,0:T(8,128)}, u32[]{:S(2)}) copy-start(f32[4,336,128]{2,1,0:T(8,128)} %get-tuple-element.42.own_ref) | copy-start | bytes 2064388
  14.0 22.5 %collective-permute-start.1 = (bf16[2,320,128]{2,1,0:T(8,128)(2,1)S(1)}, bf16[2,320,128]{2,1,0:T(8,128)(2,1)S(1)}, u32[]{:S(2)}, u32[]{:S(2)}) collective-permute-start(bf16[2,320,128]{2,1,0:T(8,128)(2,1)S(1)} %get-tuple-element.45), channel_id=1, source_target_pairs={{0,2},{2,0},{4,6},{6,4},{1,3},{3,1},{5,7},{7,5},{8,10},{10,8},{12,... | collective-permute-start | bytes 491528 | tf_op jit(solution)/shard_map/ppermute | solution.py:610
  18.8 19.5 %collective-permute-start.6 = (bf16[2,4,96,128]{3,2,1,0:T(8,128)(2,1)}, bf16[2,4,96,128]{3,2,1,0:T(8,128)(2,1)S(1)}, u32[]{:S(2)}, u32[]{:S(2)}) collective-permute-start(bf16[2,4,96,128]{3,2,1,0:T(8,128)(2,1)} %get-tuple-element.52), channel_id=1, source_target_pairs={{0,8},{8,0},{16,24},{24,16},{1,9},{9,1},{17,25},{25,17},{2,10},{10... | collective-permute-start | bytes 589832 | tf_op jit(solution)/shard_map/ppermute | solution.py:617
  36.6 6.3 %collective-permute-start.2 = (bf16[1,320,128]{2,1,0:T(8,128)(2,1)S(1)}, bf16[1,320,128]{2,1,0:T(8,128)(2,1)S(1)}, u32[]{:S(2)}, u32[]{:S(2)}) collective-permute-start(bf16[1,320,128]{2,1,0:T(8,128)(2,1)S(1)} %get-tuple-element.47), channel_id=1, source_target_pairs={{0,4},{2,6},{4,0},{6,2},{1,5},{3,7},{5,1},{7,3},{8,12},{10,14},{12... | collective-permute-start | bytes 245768 | tf_op jit(solution)/shard_map/ppermute | solution.py:610
  42.9 1.0 copy-start.3
  43.9 21.8 %copy-start.1 = (bf16[1,128,3072]{2,1,0:T(8,128)(2,1)S(1)}, bf16[1,128,3072]{2,1,0:T(8,128)(2,1)}, u32[]{:S(2)}) copy-start(bf16[1,128,3072]{2,1,0:T(8,128)(2,1)} %param.25) | copy-start | bytes 2359300
  43.9 21.8 %copy-start.5 = (f32[1,3072]{1,0:T(1,128)S(1)}, f32[1,3072]{1,0:T(1,128)}, u32[]{:S(2)}) copy-start(f32[1,3072]{1,0:T(1,128)} %gate_ref.3) | copy-start | bytes 36868
  43.9 21.8 %copy-start.6 = (s32[3]{0:T(128)S(1)}, s32[3]{0:T(128)}, u32[]{:S(2)}) copy-start(s32[3]{0:T(128)} %pad_add_fusion.meta_ref) | copy-start | bytes 40
  44.1 3.3 %collective-permute-start.7 = (bf16[4912,128]{1,0:T(8,128)(2,1)S(1)}, bf16[4912,128]{1,0:T(8,128)(2,1)S(1)}, u32[]{:S(2)}, u32[]{:S(2)}) collective-permute-start(bf16[4912,128]{1,0:T(8,128)(2,1)S(1)} %shard_map.168.refs_0_), channel_id=1, source_target_pairs={{0,1},{2,3},{4,5},{6,7},{1,0},{3,2},{5,4},{7,6},{8,9},{10,11},{12,... | collective-permute-start | bytes 3772424 | tf_op jit(solution)/shard_map/ppermute | solution.py:614
  44.2 17.8 %collective-permute-start.11 = (bf16[2,4,96,128]{3,2,1,0:T(8,128)(2,1)}, bf16[2,4,96,128]{3,2,1,0:T(8,128)(2,1)}, u32[]{:S(2)}, u32[]{:S(2)}) collective-permute-start(bf16[2,4,96,128]{3,2,1,0:T(8,128)(2,1)} %get-tuple-element.58), channel_id=1, source_target_pairs={{0,16},{8,24},{16,0},{24,8},{1,17},{9,25},{17,1},{25,9},{2,18},{10... | collective-permute-start | bytes 589832 | tf_op jit(solution)/shard_map/ppermute | solution.py:617
  45.9 16.2 %collective-permute-start.12 = (bf16[2,4,96,128]{3,2,1,0:T(8,128)(2,1)}, bf16[2,4,96,128]{3,2,1,0:T(8,128)(2,1)}, u32[]{:S(2)}, u32[]{:S(2)}) collective-permute-start(bf16[2,4,96,128]{3,2,1,0:T(8,128)(2,1)} %get-tuple-element.59), channel_id=1, source_target_pairs={{0,24},{8,16},{16,8},{24,0},{1,25},{9,17},{17,9},{25,1},{2,26},{10... | collective-permute-start | bytes 589832 | tf_op jit(solution)/shard_map/ppermute | solution.py:617
  49.5 10.4 %collective-permute-start.8 = (bf16[136,384]{1,0:T(8,128)(2,1)S(1)}, bf16[136,384]{1,0:T(8,128)(2,1)S(1)}, u32[]{:S(2)}, u32[]{:S(2)}) collective-permute-start(bf16[136,384]{1,0:T(8,128)(2,1)S(1)} %pad_maximum_fusion), channel_id=1, source_target_pairs={{0,4},{2,6},{4,0},{6,2},{1,5},{3,7},{5,1},{7,3},{8,12},{10,14},{12... | collective-permute-start | bytes 313352 | tf_op jit(solution)/shard_map/ppermute | solution.py:610
  50.2 9.7 %collective-permute-start.9 = (bf16[136,384]{1,0:T(8,128)(2,1)S(1)}, bf16[136,384]{1,0:T(8,128)(2,1)S(1)}, u32[]{:S(2)}, u32[]{:S(2)}) collective-permute-start(bf16[136,384]{1,0:T(8,128)(2,1)S(1)} %pad_maximum_fusion.1), channel_id=1, source_target_pairs={{0,6},{2,4},{4,2},{6,0},{1,7},{3,5},{5,3},{7,1},{8,14},{10,12},{12... | collective-permute-start | bytes 313352 | tf_op jit(solution)/shard_map/ppermute | solution.py:610
  54.2 7.7 %collective-permute-start.10 = (bf16[136,384]{1,0:T(8,128)(2,1)S(1)}, bf16[136,384]{1,0:T(8,128)(2,1)S(1)}, u32[]{:S(2)}, u32[]{:S(2)}) collective-permute-start(bf16[136,384]{1,0:T(8,128)(2,1)S(1)} %pad_maximum_fusion.2), channel_id=1, source_target_pairs={{0,2},{2,0},{4,6},{6,4},{1,3},{3,1},{5,7},{7,5},{8,10},{10,8},{12,... | collective-permute-start | bytes 313352 | tf_op jit(solution)/shard_map/ppermute | solution.py:610
  62.0 13.0 %copy-start.7 = (bf16[1,8,1536]{2,1,0:T(8,128)(2,1)}, bf16[1,8,1536]{2,1,0:T(8,128)(2,1)S(1)}, u32[]{:S(2)}) copy-start(bf16[1,8,1536]{2,1,0:T(8,128)(2,1)S(1)} %get-tuple-element.79) | copy-start | bytes 73732
  62.1 13.0 %copy-start.4 = (bf16[2,4,96,128]{3,2,1,0:T(8,128)(2,1)S(1)}, bf16[2,4,96,128]{3,2,1,0:T(8,128)(2,1)}, u32[]{:S(2)}) copy-start(bf16[2,4,96,128]{3,2,1,0:T(8,128)(2,1)} %get-tuple-element.62.refs_0_) | copy-start | bytes 589828
  62.2 14.6 %collective-permute-start.16 = (bf16[128,1536]{1,0:T(8,128)(2,1)S(1)}, bf16[128,1536]{1,0:T(8,128)(2,1)S(1)}, u32[]{:S(2)}, u32[]{:S(2)}) collective-permute-start(bf16[128,1536]{1,0:T(8,128)(2,1)S(1)} %shard_map.171.attn_ref.refs_2_), channel_id=1, source_target_pairs={{0,8},{8,0},{16,24},{24,16},{1,9},{9,1},{17,25},{25,17},{2,10},{10... | collective-permute-start | bytes 1179656 | tf_op jit(solution)/shard_map/ppermute | solution.py:617
  63.8 19.2 %collective-permute-start.15 = (bf16[128,1536]{1,0:T(8,128)(2,1)S(1)}, bf16[128,1536]{1,0:T(8,128)(2,1)S(1)}, u32[]{:S(2)}, u32[]{:S(2)}) collective-permute-start(bf16[128,1536]{1,0:T(8,128)(2,1)S(1)} %shard_map.171.attn_ref.refs_2_), channel_id=1, source_target_pairs={{0,16},{8,24},{16,0},{24,8},{1,17},{9,25},{17,1},{25,9},{2,18},{10... | collective-permute-start | bytes 1179656 | tf_op jit(solution)/shard_map/ppermute | solution.py:617
  65.3 17.7 %collective-permute-start.14 = (bf16[128,1536]{1,0:T(8,128)(2,1)S(1)}, bf16[128,1536]{1,0:T(8,128)(2,1)S(1)}, u32[]{:S(2)}, u32[]{:S(2)}) collective-permute-start(bf16[128,1536]{1,0:T(8,128)(2,1)S(1)} %shard_map.171.attn_ref.refs_2_), channel_id=1, source_target_pairs={{0,24},{8,16},{16,8},{24,0},{1,25},{9,17},{17,9},{25,1},{2,26},{10... | collective-permute-start | bytes 1179656 | tf_op jit(solution)/shard_map/ppermute | solution.py:617
  65.7 3.7 %copy-start = (bf16[3072,1536]{1,0:T(8,128)(2,1)S(1)}, bf16[3072,1536]{1,0:T(8,128)(2,1)}, u32[]{:S(2)}) copy-start(bf16[3072,1536]{1,0:T(8,128)(2,1)} %w_ref.3) | copy-start | bytes 28311556
  75.1 8.4 %collective-permute-start.17 = (bf16[144,1536]{1,0:T(8,128)(2,1)S(1)}, bf16[144,1536]{1,0:T(8,128)(2,1)S(1)}, u32[]{:S(2)}, u32[]{:S(2)}) collective-permute-start(bf16[144,1536]{1,0:T(8,128)(2,1)S(1)} %get-tuple-element.65), channel_id=1, source_target_pairs={{0,1},{2,3},{4,5},{6,7},{1,0},{3,2},{5,4},{7,6},{8,9},{10,11},{12,... | collective-permute-start | bytes 1327112 | tf_op jit(solution)/shard_map/ppermute | solution.py:614
  76.1 7.3 %collective-permute-start.13 = (bf16[4,4,96,128]{3,2,1,0:T(8,128)(2,1)S(1)}, bf16[4,4,96,128]{3,2,1,0:T(8,128)(2,1)S(1)}, u32[]{:S(2)}, u32[]{:S(2)}) collective-permute-start(bf16[4,4,96,128]{3,2,1,0:T(8,128)(2,1)S(1)} %get-tuple-element.64), channel_id=1, source_target_pairs={{0,1},{2,3},{4,5},{6,7},{1,0},{3,2},{5,4},{7,6},{8,9},{10,11},{12,... | collective-permute-start | bytes 1179656 | tf_op jit(solution)/shard_map/ppermute | solution.py:614
  76.7 6.7 %collective-permute-start.20 = (bf16[128,1536]{1,0:T(8,128)(2,1)S(1)}, bf16[128,1536]{1,0:T(8,128)(2,1)S(1)}, u32[]{:S(2)}, u32[]{:S(2)}) collective-permute-start(bf16[128,1536]{1,0:T(8,128)(2,1)S(1)} %collective-permute-done.16.refs_5_), channel_id=1, source_target_pairs={{0,1},{2,3},{4,5},{6,7},{1,0},{3,2},{5,4},{7,6},{8,9},{10,11},{12,... | collective-permute-start | bytes 1179656 | tf_op jit(solution)/shard_map/ppermute | solution.py:614
  82.9 1.7 %collective-permute-start.19 = (bf16[128,1536]{1,0:T(8,128)(2,1)S(1)}, bf16[128,1536]{1,0:T(8,128)(2,1)S(1)}, u32[]{:S(2)}, u32[]{:S(2)}) collective-permute-start(bf16[128,1536]{1,0:T(8,128)(2,1)S(1)} %collective-permute-done.15.refs_4_), channel_id=1, source_target_pairs={{0,1},{2,3},{4,5},{6,7},{1,0},{3,2},{5,4},{7,6},{8,9},{10,11},{12,... | collective-permute-start | bytes 1179656 | tf_op jit(solution)/shard_map/ppermute | solution.py:614
  82.9 2.3 %collective-permute-start.18 = (bf16[128,1536]{1,0:T(8,128)(2,1)S(1)}, bf16[128,1536]{1,0:T(8,128)(2,1)S(1)}, u32[]{:S(2)}, u32[]{:S(2)}) collective-permute-start(bf16[128,1536]{1,0:T(8,128)(2,1)S(1)} %collective-permute-done.14.refs_3_), channel_id=1, source_target_pairs={{0,1},{2,3},{4,5},{6,7},{1,0},{3,2},{5,4},{7,6},{8,9},{10,11},{12,... | collective-permute-start | bytes 1179656 | tf_op jit(solution)/shard_map/ppermute | solution.py:614
  86.6 6.8 %collective-permute-start.23 = (bf16[592,128]{1,0:T(8,128)(2,1)S(1)}, bf16[592,128]{1,0:T(8,128)(2,1)S(1)}, u32[]{:S(2)}, u32[]{:S(2)}) collective-permute-start(bf16[592,128]{1,0:T(8,128)(2,1)S(1)} %get-tuple-element.71), channel_id=1, source_target_pairs={{0,2},{2,0},{4,6},{6,4},{1,3},{3,1},{5,7},{7,5},{8,10},{10,8},{12,... | collective-permute-start | bytes 454664 | tf_op jit(solution)/shard_map/ppermute | solution.py:610
  87.4 9.5 %collective-permute-start.21 = (bf16[576,128]{1,0:T(8,128)(2,1)S(1)}, bf16[576,128]{1,0:T(8,128)(2,1)S(1)}, u32[]{:S(2)}, u32[]{:S(2)}) collective-permute-start(bf16[576,128]{1,0:T(8,128)(2,1)S(1)} %get-tuple-element.69), channel_id=1, source_target_pairs={{0,2},{2,0},{4,6},{6,4},{1,3},{3,1},{5,7},{7,5},{8,10},{10,8},{12,... | collective-permute-start | bytes 442376 | tf_op jit(solution)/shard_map/ppermute | solution.py:610
  93.5 15.1 %collective-permute-start.24 = (bf16[592,128]{1,0:T(8,128)(2,1)S(1)}, bf16[592,128]{1,0:T(8,128)(2,1)S(1)}, u32[]{:S(2)}, u32[]{:S(2)}) collective-permute-start(bf16[592,128]{1,0:T(8,128)(2,1)S(1)} %get-tuple-element.74), channel_id=1, source_target_pairs={{0,4},{2,6},{4,0},{6,2},{1,5},{3,7},{5,1},{7,3},{8,12},{10,14},{12... | collective-permute-start | bytes 454664 | tf_op jit(solution)/shard_map/ppermute | solution.py:610
  94.5 14.2 %collective-permute-start.26 = (bf16[592,128]{1,0:T(8,128)(2,1)S(1)}, bf16[592,128]{1,0:T(8,128)(2,1)S(1)}, u32[]{:S(2)}, u32[]{:S(2)}) collective-permute-start(bf16[592,128]{1,0:T(8,128)(2,1)S(1)} %get-tuple-element.76), channel_id=1, source_target_pairs={{0,2},{2,0},{4,6},{6,4},{1,3},{3,1},{5,7},{7,5},{8,10},{10,8},{12,... | collective-permute-start | bytes 454664 | tf_op jit(solution)/shard_map/ppermute | solution.py:610
  97.0 11.6 %collective-permute-start.22 = (bf16[576,128]{1,0:T(8,128)(2,1)S(1)}, bf16[576,128]{1,0:T(8,128)(2,1)S(1)}, u32[]{:S(2)}, u32[]{:S(2)}) collective-permute-start(bf16[576,128]{1,0:T(8,128)(2,1)S(1)} %shard_map.175), channel_id=1, source_target_pairs={{0,4},{2,6},{4,0},{6,2},{1,5},{3,7},{5,1},{7,3},{8,12},{10,14},{12... | collective-permute-start | bytes 442376 | tf_op jit(solution)/shard_map/ppermute | solution.py:610
  97.3 11.3 %collective-permute-start.25 = (bf16[576,128]{1,0:T(8,128)(2,1)S(1)}, bf16[576,128]{1,0:T(8,128)(2,1)S(1)}, u32[]{:S(2)}, u32[]{:S(2)}) collective-permute-start(bf16[576,128]{1,0:T(8,128)(2,1)S(1)} %get-tuple-element.75), channel_id=1, source_target_pairs={{0,2},{2,0},{4,6},{6,4},{1,3},{3,1},{5,7},{7,5},{8,10},{10,8},{12,... | collective-permute-start | bytes 442376 | tf_op jit(solution)/shard_map/ppermute | solution.py:610

commit v17 on v16

--- a/solution.py
+++ b/solution.py
@@ -651,10 +651,10 @@
     block = block_of(own, got, gg_dp[1:], images, DT5, heads)
     blocks = [block] + [to_oc(block, j) for j in range(1, OC)]
     *first, text_out = attention(
-        blocks, [1, 2, G], [], G, heads, image_local, text_rows
+        blocks, [1, 2, 3, G], [], G, heads, image_local, text_rows
     )
     second = attention(
-        blocks, [3, 0], [text_out], G, heads, image_local, text_rows
+        blocks, [0], [text_out], G, heads, image_local, text_rows
     )
     outs = dict(zip(order + [0], first + list(second)))
 

time: 110 us -> 110 us (level)
  transfers between devices with their start and end apart: 27 -> 27, of which waited for: 11 -> 10; matrix products, arithmetic and copies ran while one was open for 1% -> 1% of each run, Pallas kernels for 12% -> 12%
where the time goes in v17:
time: 110 us; the launch traced here: 109 us
  waiting for transfers between devices  50.1 us (46%)
  starting transfers between devices  29.4 us (27%)
  Pallas kernels  21.5 us (20%)
  local copies, waits for them, and re-layouts  5.86 us (5%)
  between operations  1.46 us (1%)
    ppermute x14, waiting for transfers between devices, to_z(): return lax.ppermute(x, 'seq', perm)  42.8 us
    ppermute x14, starting transfers between devices, to_z(): return lax.ppermute(x, 'seq', perm)  19.5 us
    ppermute x6, starting transfers between devices, to_dp(): return lax.ppermute(x, 'dp', [(a, a ^ k) for a in range(n_dp)])  8.13 us
    unnamed x18, local copies, waits for them, and re-layouts  5.76 us
    pallas_call x1, Pallas kernels, project(): pl.pallas_call(functools.partial(project_kernel, groups, parts, place_of)...  5.7 us
    pallas_call x1, Pallas kernels, text_project(): pl.pallas_call(functools.partial(text_kernel, groups, heads, place_of, wh...  5.66 us
    ppermute x6, waiting for transfers between devices, to_dp(): return lax.ppermute(x, 'dp', [(a, a ^ k) for a in range(n_dp)])  5.57 us
    pallas_call x2, Pallas kernels, attention(): pl.pallas_call(functools.partial(attention_kernel, n_pieces, len(blocks),...  3.71 us
  transfers between devices with their start and end apart: 27, of which 10 were waited for; matrix products, arithmetic and copies ran while one was open for 1% of the time, Pallas kernels for 12%

profile of v17, /device:TPU:0, one launch (start us, length us, event | category | flops | bytes accessed | tf_op | source)
XLA Modules:
  0.0 109.2 jit_solution(7046871966571228992)
XLA Ops:
  1.3 5.7 %shard_map.164 = (f32[4,336,128]{2,1,0:T(8,128)}, bf16[1152,128]{1,0:T(8,128)(2,1)}, bf16[1152,128]{1,0:T(8,128)(2,1)}, bf16[1152,128]{1,0:T(8,128)(2,1)}, bf16[...) custom-call(s32[1]{0:T(128)} %copy.22.len_ref, s32[1,64]{1,0:T(1,128)} %src_ref.1, bf16[64,512]{1,0:T(8,128)(2,1)} %bitcast.36, ...), custom_call_target="tpu_custom_call" | custom-call | flops 301989888 | bytes 4718592 | tf_op jit(solution)/shard_map/pallas_call | solution.py:140
  7.0 0.5 collective-permute-start
  7.5 3.7 %collective-permute-start.3 = (bf16[1152,128]{1,0:T(8,128)(2,1)}, bf16[1152,128]{1,0:T(8,128)(2,1)S(1)}, u32[]{:S(2)}, u32[]{:S(2)}) collective-permute-start(bf16[1152,128]{1,0:T(8,128)(2,1)} %get-tuple-element.48), channel_id=1, source_target_pairs={{0,4},{2,6},{4,0},{6,2},{1,5},{3,7},{5,1},{7,3},{8,12},{10,14},{12... | collective-permute-start | bytes 884744 | tf_op jit(solution)/shard_map/ppermute | solution.py:610
  11.1 1.4 %collective-permute-start.4 = (bf16[1152,128]{1,0:T(8,128)(2,1)}, bf16[1152,128]{1,0:T(8,128)(2,1)S(1)}, u32[]{:S(2)}, u32[]{:S(2)}) collective-permute-start(bf16[1152,128]{1,0:T(8,128)(2,1)} %get-tuple-element.49), channel_id=1, source_target_pairs={{0,6},{2,4},{4,2},{6,0},{1,7},{3,5},{5,3},{7,1},{8,14},{10,12},{12... | collective-permute-start | bytes 884744 | tf_op jit(solution)/shard_map/ppermute | solution.py:610
  12.5 0.2 collective-permute-start.5
  12.7 1.1 %copy-done.2 = f32[4,336,128]{2,1,0:T(8,128)S(1)} copy-done((f32[4,336,128]{2,1,0:T(8,128)S(1)}, f32[4,336,128]{2,1,0:T(8,128)}, u32[]{:S(2)}) %copy-start.2) | copy-done | bytes 688152
  13.8 0.2 shard_map.165
  14.0 1.9 %collective-permute-start.1 = (bf16[2,320,128]{2,1,0:T(8,128)(2,1)S(1)}, bf16[2,320,128]{2,1,0:T(8,128)(2,1)S(1)}, u32[]{:S(2)}, u32[]{:S(2)}) collective-permute-start(bf16[2,320,128]{2,1,0:T(8,128)(2,1)S(1)} %get-tuple-element.44), channel_id=1, source_target_pairs={{0,2},{2,0},{4,6},{6,4},{1,3},{3,1},{5,7},{7,5},{8,10},{10,8},{12,... | collective-permute-start | bytes 491528 | tf_op jit(solution)/shard_map/ppermute | solution.py:610
  15.9 0.6 pad_add_fusion.meta_ref
  16.4 2.3 %shard_map.167 = (bf16[2,4,96,128]{3,2,1,0:T(8,128)(2,1)}, bf16[2,4,96,128]{3,2,1,0:T(8,128)(2,1)}, bf16[2,4,96,128]{3,2,1,0:T(8,128)(2,1)}, bf16[2,4,96,128]{3,2,1,0:T(8,128)(2,1)}) custom-call(s32[3]{0:T(128)} %pad_add_fusion.meta_ref, f32[1,3072]{1,0:T(1,128)} %gate_ref.3, bf16[128,3072]{1,0:T(8,128)(2,1)} %bitcast.31), custom_call_target="tpu_custom_call" | custom-call | bytes 1572864 | tf_op jit(solution)/shard_map/pallas_call | solution.py:351
  18.8 1.5 %collective-permute-start.6 = (bf16[2,4,96,128]{3,2,1,0:T(8,128)(2,1)}, bf16[2,4,96,128]{3,2,1,0:T(8,128)(2,1)S(1)}, u32[]{:S(2)}, u32[]{:S(2)}) collective-permute-start(bf16[2,4,96,128]{3,2,1,0:T(8,128)(2,1)} %get-tuple-element.51), channel_id=1, source_target_pairs={{0,8},{8,0},{16,24},{24,16},{1,9},{9,1},{17,25},{25,17},{2,10},{10... | collective-permute-start | bytes 589832 | tf_op jit(solution)/shard_map/ppermute | solution.py:617
  20.3 16.2 %collective-permute-done.1.refs_0_ = bf16[2,320,128]{2,1,0:T(8,128)(2,1)S(1)} collective-permute-done((bf16[2,320,128]{2,1,0:T(8,128)(2,1)S(1)}, bf16[2,320,128]{2,1,0:T(8,128)(2,1)S(1)}, u32[]{:S(2)}, u32[]{:S(2)}) %collective-permute-start.1) | collective-permute-done | bytes 163872 | tf_op jit(solution)/shard_map/ppermute | solution.py:610
  36.5 0.2 shard_map.166
  36.6 1.7 %collective-permute-start.2 = (bf16[1,320,128]{2,1,0:T(8,128)(2,1)S(1)}, bf16[1,320,128]{2,1,0:T(8,128)(2,1)S(1)}, u32[]{:S(2)}, u32[]{:S(2)}) collective-permute-start(bf16[1,320,128]{2,1,0:T(8,128)(2,1)S(1)} %get-tuple-element.46), channel_id=1, source_target_pairs={{0,4},{2,6},{4,0},{6,2},{1,5},{3,7},{5,1},{7,3},{8,12},{10,14},{12... | collective-permute-start | bytes 245768 | tf_op jit(solution)/shard_map/ppermute | solution.py:610
  38.4 4.6 %collective-permute-done.2.got_ref = bf16[1,320,128]{2,1,0:T(8,128)(2,1)S(1)} collective-permute-done((bf16[1,320,128]{2,1,0:T(8,128)(2,1)S(1)}, bf16[1,320,128]{2,1,0:T(8,128)(2,1)S(1)}, u32[]{:S(2)}, u32[]{:S(2)}) %collective-permute-start.2) | collective-permute-done | bytes 81952 | tf_op jit(solution)/shard_map/ppermute | solution.py:610
  42.9 1.0 copy-done.3
  43.9 0.3 shard_map.168.refs_0_
  44.2 1.7 %collective-permute-start.11 = (bf16[2,4,96,128]{3,2,1,0:T(8,128)(2,1)}, bf16[2,4,96,128]{3,2,1,0:T(8,128)(2,1)}, u32[]{:S(2)}, u32[]{:S(2)}) collective-permute-start(bf16[2,4,96,128]{3,2,1,0:T(8,128)(2,1)} %get-tuple-element.56), channel_id=1, source_target_pairs={{0,16},{8,24},{16,0},{24,8},{1,17},{9,25},{17,1},{25,9},{2,18},{10... | collective-permute-start | bytes 589832 | tf_op jit(solution)/shard_map/ppermute | solution.py:617
  45.9 1.4 %collective-permute-start.12 = (bf16[2,4,96,128]{3,2,1,0:T(8,128)(2,1)}, bf16[2,4,96,128]{3,2,1,0:T(8,128)(2,1)}, u32[]{:S(2)}, u32[]{:S(2)}) collective-permute-start(bf16[2,4,96,128]{3,2,1,0:T(8,128)(2,1)} %get-tuple-element.57), channel_id=1, source_target_pairs={{0,24},{8,16},{16,8},{24,0},{1,25},{9,17},{17,9},{25,1},{2,26},{10... | collective-permute-start | bytes 589832 | tf_op jit(solution)/shard_map/ppermute | solution.py:617
  47.4 2.7 %shard_map.169 = (bf16[128,384]{1,0:T(8,128)(2,1)S(1)}, bf16[128,384]{1,0:T(8,128)(2,1)S(1)}, bf16[128,384]{1,0:T(8,128)(2,1)S(1)}, bf16[32,384]{1,0:T(8,128)(2,1)S(1)}) custom-call(bf16[4912,128]{1,0:T(8,128)(2,1)S(1)} %shard_map.168.refs_0_, bf16[4912,128]{1,0:T(8,128)(2,1)S(1)} %collective-permute-done.7.refs_1_), custom_call_target="tpu_custom_call" | custom-call | flops 695205888 | bytes 2310144 | tf_op jit(solution)/shard_map/pallas_call | solution.py:291
  50.1 0.8 collective-permute-start.8
  50.9 2.1 %collective-permute-start.9 = (bf16[136,384]{1,0:T(8,128)(2,1)S(1)}, bf16[136,384]{1,0:T(8,128)(2,1)S(1)}, u32[]{:S(2)}, u32[]{:S(2)}) collective-permute-start(bf16[136,384]{1,0:T(8,128)(2,1)S(1)} %pad_maximum_fusion.1), channel_id=1, source_target_pairs={{0,6},{2,4},{4,2},{6,0},{1,7},{3,5},{5,3},{7,1},{8,14},{10,12},{12... | collective-permute-start | bytes 313352 | tf_op jit(solution)/shard_map/ppermute | solution.py:610
  53.0 0.8 collective-permute-start.10
  53.8 1.1 shard_map.170
  54.9 5.6 %collective-permute-done.8.refs_0_ = bf16[136,384]{1,0:T(8,128)(2,1)S(1)} collective-permute-done((bf16[136,384]{1,0:T(8,128)(2,1)S(1)}, bf16[136,384]{1,0:T(8,128)(2,1)S(1)}, u32[]{:S(2)}, u32[]{:S(2)}) %collective-permute-start.8) | collective-permute-done | bytes 104480 | tf_op jit(solution)/shard_map/ppermute | solution.py:610
  60.6 1.1 %collective-permute-done.10.refs_2_ = bf16[136,384]{1,0:T(8,128)(2,1)S(1)} collective-permute-done((bf16[136,384]{1,0:T(8,128)(2,1)S(1)}, bf16[136,384]{1,0:T(8,128)(2,1)S(1)}, u32[]{:S(2)}, u32[]{:S(2)}) %collective-permute-start.10) | collective-permute-done | bytes 104480 | tf_op jit(solution)/shard_map/ppermute | solution.py:610
  62.0 1.6 %collective-permute-start.16 = (bf16[128,1536]{1,0:T(8,128)(2,1)S(1)}, bf16[128,1536]{1,0:T(8,128)(2,1)S(1)}, u32[]{:S(2)}, u32[]{:S(2)}) collective-permute-start(bf16[128,1536]{1,0:T(8,128)(2,1)S(1)} %shard_map.171.attn_ref.refs_2_), channel_id=1, source_target_pairs={{0,8},{8,0},{16,24},{24,16},{1,9},{9,1},{17,25},{25,17},{2,10},{10... | collective-permute-start | bytes 1179656 | tf_op jit(solution)/shard_map/ppermute | solution.py:617
  63.7 1.5 %collective-permute-start.15 = (bf16[128,1536]{1,0:T(8,128)(2,1)S(1)}, bf16[128,1536]{1,0:T(8,128)(2,1)S(1)}, u32[]{:S(2)}, u32[]{:S(2)}) collective-permute-start(bf16[128,1536]{1,0:T(8,128)(2,1)S(1)} %shard_map.171.attn_ref.refs_2_), channel_id=1, source_target_pairs={{0,16},{8,24},{16,0},{24,8},{1,17},{9,25},{17,1},{25,9},{2,18},{10... | collective-permute-start | bytes 1179656 | tf_op jit(solution)/shard_map/ppermute | solution.py:617
  65.2 0.4 collective-permute-start.14
  65.6 3.7 %copy-done = bf16[3072,1536]{1,0:T(8,128)(2,1)S(1)} copy-done((bf16[3072,1536]{1,0:T(8,128)(2,1)S(1)}, bf16[3072,1536]{1,0:T(8,128)(2,1)}, u32[]{:S(2)}) %copy-start) | copy-done | bytes 9437208
  69.3 5.7 %shard_map.172 = (bf16[128,3072]{1,0:T(8,128)(2,1)}, bf16[128,1536]{1,0:T(8,128)(2,1)}, f32[4,384]{1,0:T(4,128)S(1)}, bf16[144,1536]{1,0:T(8,128)(2,1)S(1)}) custom-call(s32[3]{0:T(128)S(1)} %copy-done.6, bf16[128,1536]{1,0:T(8,128)(2,1)S(1)} %shard_map.171.attn_ref.refs_2_, bf16[3072,1536]{1,0:T(8,128)(2,1)S(1)} %copy-done, f32[1,3072]{1,0:T(1,128)S(1)} %copy-done.5, ...), custom_call_target="tpu_custom_call" | custom-call | flops 2415919104 | bytes 9437184 | tf_op jit(solution)/shard_map/pallas_call | solution.py:432
  75.0 1.1 shard_map.173
  76.1 0.6 collective-permute-start.13
  76.7 0.1 collective-permute-start.20
  76.7 5.6 %collective-permute-done.15.refs_4_ = bf16[128,1536]{1,0:T(8,128)(2,1)S(1)} collective-permute-done((bf16[128,1536]{1,0:T(8,128)(2,1)S(1)}, bf16[128,1536]{1,0:T(8,128)(2,1)S(1)}, u32[]{:S(2)}, u32[]{:S(2)}) %collective-permute-start.15) | collective-permute-done | bytes 393248 | tf_op jit(solution)/shard_map/ppermute | solution.py:617
  82.3 0.5 collective-permute-start.18
  82.8 1.2 %collective-permute-done.19.refs_8_ = bf16[128,1536]{1,0:T(8,128)(2,1)S(1)} collective-permute-done((bf16[128,1536]{1,0:T(8,128)(2,1)S(1)}, bf16[128,1536]{1,0:T(8,128)(2,1)S(1)}, u32[]{:S(2)}, u32[]{:S(2)}) %collective-permute-start.19) | collective-permute-done | bytes 393248 | tf_op jit(solution)/shard_map/ppermute | solution.py:614
  84.0 0.6 collective-permute-done.18.refs_7_
  84.6 1.4 %shard_map.174 = (f32[1168,128]{1,0:T(8,128)S(1)}, bf16[576,128]{1,0:T(8,128)(2,1)S(1)}, bf16[592,128]{1,0:T(8,128)(2,1)S(1)}, f32[576,128]{1,0:T(8,128)S(1)}, f...) custom-call(bf16[4,4,96,128]{3,2,1,0:T(8,128)(2,1)S(1)} %get-tuple-element.61.refs_0_, ...), custom_call_target="tpu_custom_call" | custom-call | flops 1207959552 | bytes 5111808 | tf_op jit(solution)/shard_map/pallas_call | solution.py:508
  86.0 2.0 %collective-permute-start.23 = (bf16[592,128]{1,0:T(8,128)(2,1)S(1)}, bf16[592,128]{1,0:T(8,128)(2,1)S(1)}, u32[]{:S(2)}, u32[]{:S(2)}) collective-permute-start(bf16[592,128]{1,0:T(8,128)(2,1)S(1)} %get-tuple-element.69), channel_id=1, source_target_pairs={{0,2},{2,0},{4,6},{6,4},{1,3},{3,1},{5,7},{7,5},{8,10},{10,8},{12,... | collective-permute-start | bytes 454664 | tf_op jit(solution)/shard_map/ppermute | solution.py:610
  88.0 0.1 collective-permute-start.21
  88.1 4.7 %collective-permute-done.23.got_ref = bf16[592,128]{1,0:T(8,128)(2,1)S(1)} collective-permute-done((bf16[592,128]{1,0:T(8,128)(2,1)S(1)}, bf16[592,128]{1,0:T(8,128)(2,1)S(1)}, u32[]{:S(2)}, u32[]{:S(2)}) %collective-permute-start.23) | collective-permute-done | bytes 151584 | tf_op jit(solution)/shard_map/ppermute | solution.py:610
  92.9 2.2 %collective-permute-start.24 = (bf16[592,128]{1,0:T(8,128)(2,1)S(1)}, bf16[592,128]{1,0:T(8,128)(2,1)S(1)}, u32[]{:S(2)}, u32[]{:S(2)}) collective-permute-start(bf16[592,128]{1,0:T(8,128)(2,1)S(1)} %get-tuple-element.72), channel_id=1, source_target_pairs={{0,4},{2,6},{4,0},{6,2},{1,5},{3,7},{5,1},{7,3},{8,12},{10,14},{12... | collective-permute-start | bytes 454664 | tf_op jit(solution)/shard_map/ppermute | solution.py:610
  95.1 0.4 collective-permute-done.21.got_ref
  95.5 2.4 %collective-permute-start.22 = (bf16[576,128]{1,0:T(8,128)(2,1)S(1)}, bf16[576,128]{1,0:T(8,128)(2,1)S(1)}, u32[]{:S(2)}, u32[]{:S(2)}) collective-permute-start(bf16[576,128]{1,0:T(8,128)(2,1)S(1)} %shard_map.175), channel_id=1, source_target_pairs={{0,4},{2,6},{4,0},{6,2},{1,5},{3,7},{5,1},{7,3},{8,12},{10,14},{12... | collective-permute-start | bytes 442376 | tf_op jit(solution)/shard_map/ppermute | solution.py:610
  98.0 0.2 collective-permute-start.25
  98.1 10.2 %collective-permute-done.22.far_low = bf16[576,128]{1,0:T(8,128)(2,1)S(1)} collective-permute-done((bf16[576,128]{1,0:T(8,128)(2,1)S(1)}, bf16[576,128]{1,0:T(8,128)(2,1)S(1)}, u32[]{:S(2)}, u32[]{:S(2)}) %collective-permute-start.22) | collective-permute-done | bytes 147488 | tf_op jit(solution)/shard_map/ppermute | solution.py:610
  108.3 0.9 shard_map.177
  (51 shorter events, 0.8 us)
Async XLA Ops:
  1.3 46.0 %copy-start.8 = (s32[1,64]{1,0:T(1,128)S(1)}, s32[1,64]{1,0:T(1,128)}, u32[]{:S(2)}) copy-start(s32[1,64]{1,0:T(1,128)} %src_ref.1) | copy-start | bytes 772
  7.0 5.8 %collective-permute-start = (bf16[4,320,128]{2,1,0:T(8,128)(2,1)}, bf16[4,320,128]{2,1,0:T(8,128)(2,1)S(1)}, u32[]{:S(2)}, u32[]{:S(2)}) collective-permute-start(bf16[4,320,128]{2,1,0:T(8,128)(2,1)} %get-tuple-element.42), channel_id=1, source_target_pairs={{0,1},{2,3},{4,5},{6,7},{1,0},{3,2},{5,4},{7,6},{8,9},{10,11},{12,... | collective-permute-start | bytes 983048 | tf_op jit(solution)/shard_map/ppermute | solution.py:614
  7.5 30.9 %collective-permute-start.3 = (bf16[1152,128]{1,0:T(8,128)(2,1)}, bf16[1152,128]{1,0:T(8,128)(2,1)S(1)}, u32[]{:S(2)}, u32[]{:S(2)}) collective-permute-start(bf16[1152,128]{1,0:T(8,128)(2,1)} %get-tuple-element.48), channel_id=1, source_target_pairs={{0,4},{2,6},{4,0},{6,2},{1,5},{3,7},{5,1},{7,3},{8,12},{10,14},{12... | collective-permute-start | bytes 884744 | tf_op jit(solution)/shard_map/ppermute | solution.py:610
  11.1 27.2 %collective-permute-start.4 = (bf16[1152,128]{1,0:T(8,128)(2,1)}, bf16[1152,128]{1,0:T(8,128)(2,1)S(1)}, u32[]{:S(2)}, u32[]{:S(2)}) collective-permute-start(bf16[1152,128]{1,0:T(8,128)(2,1)} %get-tuple-element.49), channel_id=1, source_target_pairs={{0,6},{2,4},{4,2},{6,0},{1,7},{3,5},{5,3},{7,1},{8,14},{10,12},{12... | collective-permute-start | bytes 884744 | tf_op jit(solution)/shard_map/ppermute | solution.py:610
  12.5 25.9 %collective-permute-start.5 = (bf16[1152,128]{1,0:T(8,128)(2,1)}, bf16[1152,128]{1,0:T(8,128)(2,1)S(1)}, u32[]{:S(2)}, u32[]{:S(2)}) collective-permute-start(bf16[1152,128]{1,0:T(8,128)(2,1)} %get-tuple-element.50), channel_id=1, source_target_pairs={{0,2},{2,0},{4,6},{6,4},{1,3},{3,1},{5,7},{7,5},{8,10},{10,8},{12,... | collective-permute-start | bytes 884744 | tf_op jit(solution)/shard_map/ppermute | solution.py:610
  12.7 1.1 %copy-start.2 = (f32[4,336,128]{2,1,0:T(8,128)S(1)}, f32[4,336,128]{2,1,0:T(8,128)}, u32[]{:S(2)}) copy-start(f32[4,336,128]{2,1,0:T(8,128)} %get-tuple-element.41.own_ref) | copy-start | bytes 2064388
  14.0 22.5 %collective-permute-start.1 = (bf16[2,320,128]{2,1,0:T(8,128)(2,1)S(1)}, bf16[2,320,128]{2,1,0:T(8,128)(2,1)S(1)}, u32[]{:S(2)}, u32[]{:S(2)}) collective-permute-start(bf16[2,320,128]{2,1,0:T(8,128)(2,1)S(1)} %get-tuple-element.44), channel_id=1, source_target_pairs={{0,2},{2,0},{4,6},{6,4},{1,3},{3,1},{5,7},{7,5},{8,10},{10,8},{12,... | collective-permute-start | bytes 491528 | tf_op jit(solution)/shard_map/ppermute | solution.py:610
  18.8 19.6 %collective-permute-start.6 = (bf16[2,4,96,128]{3,2,1,0:T(8,128)(2,1)}, bf16[2,4,96,128]{3,2,1,0:T(8,128)(2,1)S(1)}, u32[]{:S(2)}, u32[]{:S(2)}) collective-permute-start(bf16[2,4,96,128]{3,2,1,0:T(8,128)(2,1)} %get-tuple-element.51), channel_id=1, source_target_pairs={{0,8},{8,0},{16,24},{24,16},{1,9},{9,1},{17,25},{25,17},{2,10},{10... | collective-permute-start | bytes 589832 | tf_op jit(solution)/shard_map/ppermute | solution.py:617
  36.6 6.3 %collective-permute-start.2 = (bf16[1,320,128]{2,1,0:T(8,128)(2,1)S(1)}, bf16[1,320,128]{2,1,0:T(8,128)(2,1)S(1)}, u32[]{:S(2)}, u32[]{:S(2)}) collective-permute-start(bf16[1,320,128]{2,1,0:T(8,128)(2,1)S(1)} %get-tuple-element.46), channel_id=1, source_target_pairs={{0,4},{2,6},{4,0},{6,2},{1,5},{3,7},{5,1},{7,3},{8,12},{10,14},{12... | collective-permute-start | bytes 245768 | tf_op jit(solution)/shard_map/ppermute | solution.py:610
  42.9 1.0 copy-start.3
  43.9 21.7 %copy-start.1 = (bf16[1,128,3072]{2,1,0:T(8,128)(2,1)S(1)}, bf16[1,128,3072]{2,1,0:T(8,128)(2,1)}, u32[]{:S(2)}) copy-start(bf16[1,128,3072]{2,1,0:T(8,128)(2,1)} %param.25) | copy-start | bytes 2359300
  43.9 21.7 %copy-start.5 = (f32[1,3072]{1,0:T(1,128)S(1)}, f32[1,3072]{1,0:T(1,128)}, u32[]{:S(2)}) copy-start(f32[1,3072]{1,0:T(1,128)} %gate_ref.3) | copy-start | bytes 36868
  43.9 21.7 %copy-start.6 = (s32[3]{0:T(128)S(1)}, s32[3]{0:T(128)}, u32[]{:S(2)}) copy-start(s32[3]{0:T(128)} %pad_add_fusion.meta_ref) | copy-start | bytes 40
  44.1 3.3 %collective-permute-start.7 = (bf16[4912,128]{1,0:T(8,128)(2,1)S(1)}, bf16[4912,128]{1,0:T(8,128)(2,1)S(1)}, u32[]{:S(2)}, u32[]{:S(2)}) collective-permute-start(bf16[4912,128]{1,0:T(8,128)(2,1)S(1)} %shard_map.168.refs_0_), channel_id=1, source_target_pairs={{0,1},{2,3},{4,5},{6,7},{1,0},{3,2},{5,4},{7,6},{8,9},{10,11},{12,... | collective-permute-start | bytes 3772424 | tf_op jit(solution)/shard_map/ppermute | solution.py:614
  44.2 17.7 %collective-permute-start.11 = (bf16[2,4,96,128]{3,2,1,0:T(8,128)(2,1)}, bf16[2,4,96,128]{3,2,1,0:T(8,128)(2,1)}, u32[]{:S(2)}, u32[]{:S(2)}) collective-permute-start(bf16[2,4,96,128]{3,2,1,0:T(8,128)(2,1)} %get-tuple-element.56), channel_id=1, source_target_pairs={{0,16},{8,24},{16,0},{24,8},{1,17},{9,25},{17,1},{25,9},{2,18},{10... | collective-permute-start | bytes 589832 | tf_op jit(solution)/shard_map/ppermute | solution.py:617
  45.9 16.1 %collective-permute-start.12 = (bf16[2,4,96,128]{3,2,1,0:T(8,128)(2,1)}, bf16[2,4,96,128]{3,2,1,0:T(8,128)(2,1)}, u32[]{:S(2)}, u32[]{:S(2)}) collective-permute-start(bf16[2,4,96,128]{3,2,1,0:T(8,128)(2,1)} %get-tuple-element.57), channel_id=1, source_target_pairs={{0,24},{8,16},{16,8},{24,0},{1,25},{9,17},{17,9},{25,1},{2,26},{10... | collective-permute-start | bytes 589832 | tf_op jit(solution)/shard_map/ppermute | solution.py:617
  50.1 10.4 %collective-permute-start.8 = (bf16[136,384]{1,0:T(8,128)(2,1)S(1)}, bf16[136,384]{1,0:T(8,128)(2,1)S(1)}, u32[]{:S(2)}, u32[]{:S(2)}) collective-permute-start(bf16[136,384]{1,0:T(8,128)(2,1)S(1)} %pad_maximum_fusion), channel_id=1, source_target_pairs={{0,4},{2,6},{4,0},{6,2},{1,5},{3,7},{5,1},{7,3},{8,12},{10,14},{12... | collective-permute-start | bytes 313352 | tf_op jit(solution)/shard_map/ppermute | solution.py:610
  50.9 9.7 %collective-permute-start.9 = (bf16[136,384]{1,0:T(8,128)(2,1)S(1)}, bf16[136,384]{1,0:T(8,128)(2,1)S(1)}, u32[]{:S(2)}, u32[]{:S(2)}) collective-permute-start(bf16[136,384]{1,0:T(8,128)(2,1)S(1)} %pad_maximum_fusion.1), channel_id=1, source_target_pairs={{0,6},{2,4},{4,2},{6,0},{1,7},{3,5},{5,3},{7,1},{8,14},{10,12},{12... | collective-permute-start | bytes 313352 | tf_op jit(solution)/shard_map/ppermute | solution.py:610
  53.0 8.8 %collective-permute-start.10 = (bf16[136,384]{1,0:T(8,128)(2,1)S(1)}, bf16[136,384]{1,0:T(8,128)(2,1)S(1)}, u32[]{:S(2)}, u32[]{:S(2)}) collective-permute-start(bf16[136,384]{1,0:T(8,128)(2,1)S(1)} %pad_maximum_fusion.2), channel_id=1, source_target_pairs={{0,2},{2,0},{4,6},{6,4},{1,3},{3,1},{5,7},{7,5},{8,10},{10,8},{12,... | collective-permute-start | bytes 313352 | tf_op jit(solution)/shard_map/ppermute | solution.py:610
  61.9 13.1 %copy-start.7 = (bf16[1,8,1536]{2,1,0:T(8,128)(2,1)}, bf16[1,8,1536]{2,1,0:T(8,128)(2,1)S(1)}, u32[]{:S(2)}) copy-start(bf16[1,8,1536]{2,1,0:T(8,128)(2,1)S(1)} %get-tuple-element.77) | copy-start | bytes 73732
  62.0 13.0 %copy-start.4 = (bf16[2,4,96,128]{3,2,1,0:T(8,128)(2,1)S(1)}, bf16[2,4,96,128]{3,2,1,0:T(8,128)(2,1)}, u32[]{:S(2)}) copy-start(bf16[2,4,96,128]{3,2,1,0:T(8,128)(2,1)} %get-tuple-element.60.refs_0_) | copy-start | bytes 589828
  62.0 14.6 %collective-permute-start.16 = (bf16[128,1536]{1,0:T(8,128)(2,1)S(1)}, bf16[128,1536]{1,0:T(8,128)(2,1)S(1)}, u32[]{:S(2)}, u32[]{:S(2)}) collective-permute-start(bf16[128,1536]{1,0:T(8,128)(2,1)S(1)} %shard_map.171.attn_ref.refs_2_), channel_id=1, source_target_pairs={{0,8},{8,0},{16,24},{24,16},{1,9},{9,1},{17,25},{25,17},{2,10},{10... | collective-permute-start | bytes 1179656 | tf_op jit(solution)/shard_map/ppermute | solution.py:617
  63.7 18.6 %collective-permute-start.15 = (bf16[128,1536]{1,0:T(8,128)(2,1)S(1)}, bf16[128,1536]{1,0:T(8,128)(2,1)S(1)}, u32[]{:S(2)}, u32[]{:S(2)}) collective-permute-start(bf16[128,1536]{1,0:T(8,128)(2,1)S(1)} %shard_map.171.attn_ref.refs_2_), channel_id=1, source_target_pairs={{0,16},{8,24},{16,0},{24,8},{1,17},{9,25},{17,1},{25,9},{2,18},{10... | collective-permute-start | bytes 1179656 | tf_op jit(solution)/shard_map/ppermute | solution.py:617
  65.2 17.1 %collective-permute-start.14 = (bf16[128,1536]{1,0:T(8,128)(2,1)S(1)}, bf16[128,1536]{1,0:T(8,128)(2,1)S(1)}, u32[]{:S(2)}, u32[]{:S(2)}) collective-permute-start(bf16[128,1536]{1,0:T(8,128)(2,1)S(1)} %shard_map.171.attn_ref.refs_2_), channel_id=1, source_target_pairs={{0,24},{8,16},{16,8},{24,0},{1,25},{9,17},{17,9},{25,1},{2,26},{10... | collective-permute-start | bytes 1179656 | tf_op jit(solution)/shard_map/ppermute | solution.py:617
  65.6 3.7 %copy-start = (bf16[3072,1536]{1,0:T(8,128)(2,1)S(1)}, bf16[3072,1536]{1,0:T(8,128)(2,1)}, u32[]{:S(2)}) copy-start(bf16[3072,1536]{1,0:T(8,128)(2,1)} %w_ref.3) | copy-start | bytes 28311556
  75.0 7.8 %collective-permute-start.17 = (bf16[144,1536]{1,0:T(8,128)(2,1)S(1)}, bf16[144,1536]{1,0:T(8,128)(2,1)S(1)}, u32[]{:S(2)}, u32[]{:S(2)}) collective-permute-start(bf16[144,1536]{1,0:T(8,128)(2,1)S(1)} %get-tuple-element.63), channel_id=1, source_target_pairs={{0,1},{2,3},{4,5},{6,7},{1,0},{3,2},{5,4},{7,6},{8,9},{10,11},{12,... | collective-permute-start | bytes 1327112 | tf_op jit(solution)/shard_map/ppermute | solution.py:614
  76.1 6.7 %collective-permute-start.13 = (bf16[4,4,96,128]{3,2,1,0:T(8,128)(2,1)S(1)}, bf16[4,4,96,128]{3,2,1,0:T(8,128)(2,1)S(1)}, u32[]{:S(2)}, u32[]{:S(2)}) collective-permute-start(bf16[4,4,96,128]{3,2,1,0:T(8,128)(2,1)S(1)} %get-tuple-element.62), channel_id=1, source_target_pairs={{0,1},{2,3},{4,5},{6,7},{1,0},{3,2},{5,4},{7,6},{8,9},{10,11},{12,... | collective-permute-start | bytes 1179656 | tf_op jit(solution)/shard_map/ppermute | solution.py:614
  76.7 6.2 %collective-permute-start.20 = (bf16[128,1536]{1,0:T(8,128)(2,1)S(1)}, bf16[128,1536]{1,0:T(8,128)(2,1)S(1)}, u32[]{:S(2)}, u32[]{:S(2)}) collective-permute-start(bf16[128,1536]{1,0:T(8,128)(2,1)S(1)} %collective-permute-done.16.refs_5_), channel_id=1, source_target_pairs={{0,1},{2,3},{4,5},{6,7},{1,0},{3,2},{5,4},{7,6},{8,9},{10,11},{12,... | collective-permute-start | bytes 1179656 | tf_op jit(solution)/shard_map/ppermute | solution.py:614
  82.3 1.7 %collective-permute-start.19 = (bf16[128,1536]{1,0:T(8,128)(2,1)S(1)}, bf16[128,1536]{1,0:T(8,128)(2,1)S(1)}, u32[]{:S(2)}, u32[]{:S(2)}) collective-permute-start(bf16[128,1536]{1,0:T(8,128)(2,1)S(1)} %collective-permute-done.15.refs_4_), channel_id=1, source_target_pairs={{0,1},{2,3},{4,5},{6,7},{1,0},{3,2},{5,4},{7,6},{8,9},{10,11},{12,... | collective-permute-start | bytes 1179656 | tf_op jit(solution)/shard_map/ppermute | solution.py:614
  82.3 2.3 %collective-permute-start.18 = (bf16[128,1536]{1,0:T(8,128)(2,1)S(1)}, bf16[128,1536]{1,0:T(8,128)(2,1)S(1)}, u32[]{:S(2)}, u32[]{:S(2)}) collective-permute-start(bf16[128,1536]{1,0:T(8,128)(2,1)S(1)} %collective-permute-done.14.refs_3_), channel_id=1, source_target_pairs={{0,1},{2,3},{4,5},{6,7},{1,0},{3,2},{5,4},{7,6},{8,9},{10,11},{12,... | collective-permute-start | bytes 1179656 | tf_op jit(solution)/shard_map/ppermute | solution.py:614
  86.0 6.8 %collective-permute-start.23 = (bf16[592,128]{1,0:T(8,128)(2,1)S(1)}, bf16[592,128]{1,0:T(8,128)(2,1)S(1)}, u32[]{:S(2)}, u32[]{:S(2)}) collective-permute-start(bf16[592,128]{1,0:T(8,128)(2,1)S(1)} %get-tuple-element.69), channel_id=1, source_target_pairs={{0,2},{2,0},{4,6},{6,4},{1,3},{3,1},{5,7},{7,5},{8,10},{10,8},{12,... | collective-permute-start | bytes 454664 | tf_op jit(solution)/shard_map/ppermute | solution.py:610
  88.0 7.5 %collective-permute-start.21 = (bf16[576,128]{1,0:T(8,128)(2,1)S(1)}, bf16[576,128]{1,0:T(8,128)(2,1)S(1)}, u32[]{:S(2)}, u32[]{:S(2)}) collective-permute-start(bf16[576,128]{1,0:T(8,128)(2,1)S(1)} %get-tuple-element.67), channel_id=1, source_target_pairs={{0,2},{2,0},{4,6},{6,4},{1,3},{3,1},{5,7},{7,5},{8,10},{10,8},{12,... | collective-permute-start | bytes 442376 | tf_op jit(solution)/shard_map/ppermute | solution.py:610
  92.9 15.5 %collective-permute-start.24 = (bf16[592,128]{1,0:T(8,128)(2,1)S(1)}, bf16[592,128]{1,0:T(8,128)(2,1)S(1)}, u32[]{:S(2)}, u32[]{:S(2)}) collective-permute-start(bf16[592,128]{1,0:T(8,128)(2,1)S(1)} %get-tuple-element.72), channel_id=1, source_target_pairs={{0,4},{2,6},{4,0},{6,2},{1,5},{3,7},{5,1},{7,3},{8,12},{10,14},{12... | collective-permute-start | bytes 454664 | tf_op jit(solution)/shard_map/ppermute | solution.py:610
  95.1 13.2 %collective-permute-start.26 = (bf16[592,128]{1,0:T(8,128)(2,1)S(1)}, bf16[592,128]{1,0:T(8,128)(2,1)S(1)}, u32[]{:S(2)}, u32[]{:S(2)}) collective-permute-start(bf16[592,128]{1,0:T(8,128)(2,1)S(1)} %get-tuple-element.74), channel_id=1, source_target_pairs={{0,2},{2,0},{4,6},{6,4},{1,3},{3,1},{5,7},{7,5},{8,10},{10,8},{12,... | collective-permute-start | bytes 454664 | tf_op jit(solution)/shard_map/ppermute | solution.py:610
  95.5 12.8 %collective-permute-start.22 = (bf16[576,128]{1,0:T(8,128)(2,1)S(1)}, bf16[576,128]{1,0:T(8,128)(2,1)S(1)}, u32[]{:S(2)}, u32[]{:S(2)}) collective-permute-start(bf16[576,128]{1,0:T(8,128)(2,1)S(1)} %shard_map.175), channel_id=1, source_target_pairs={{0,4},{2,6},{4,0},{6,2},{1,5},{3,7},{5,1},{7,3},{8,12},{10,14},{12... | collective-permute-start | bytes 442376 | tf_op jit(solution)/shard_map/ppermute | solution.py:610
  98.0 10.4 %collective-permute-start.25 = (bf16[576,128]{1,0:T(8,128)(2,1)S(1)}, bf16[576,128]{1,0:T(8,128)(2,1)S(1)}, u32[]{:S(2)}, u32[]{:S(2)}) collective-permute-start(bf16[576,128]{1,0:T(8,128)(2,1)S(1)} %get-tuple-element.73), channel_id=1, source_target_pairs={{0,2},{2,0},{4,6},{6,4},{1,3},{3,1},{5,7},{7,5},{8,10},{10,8},{12,... | collective-permute-start | bytes 442376 | tf_op jit(solution)/shard_map/ppermute | solution.py:610

commit v18 on v17

--- a/solution.py
+++ b/solution.py
@@ -160,8 +160,11 @@
     )
 
 
-def text_sum_kernel(n_got, tail_rows, own_ref, *refs):
-    got, (keep_ref, send_ref) = refs[:n_got], refs[n_got:]
+def text_sum_kernel(n_got, tail_rows, n_through, own_ref, *refs):
+    got, refs = refs[:n_got], refs[n_got:]
+    for ref, out in zip(refs[:n_through], refs[n_through + 2 :]):
+        out[...] = ref[...]
+    keep_ref, send_ref = refs[n_through : n_through + 2]
     groups, text_rows, size = got[0].shape
     for g in range(groups):
         total = own_ref[g, :text_rows, :]
@@ -178,19 +181,20 @@
             send_ref[g // 2, end:, :] = tail.astype(bf16)
 
 
-def text_sum(own, got, tail_rows):
+def text_sum(own, got, tail_rows, through=()):
     groups, rows, size = own.shape
     return pl.pallas_call(
-        functools.partial(text_sum_kernel, len(got), tail_rows),
+        functools.partial(text_sum_kernel, len(got), tail_rows, len(through)),
         out_shape=[
             jax.ShapeDtypeStruct((groups // 2, rows, size), f32),
             jax.ShapeDtypeStruct((groups // 2, rows - EXTRA, size), bf16),
-        ],
-        in_specs=[VMEM] * (1 + len(got)),
-        out_specs=[VMEM] * 2,
+        ]
+        + [jax.ShapeDtypeStruct(x.shape, x.dtype) for x in through],
+        in_specs=[VMEM] * (1 + len(got) + len(through)),
+        out_specs=[VMEM] * (2 + len(through)),
         compiler_params=params(),
         cost_estimate=cost(0, 8 * groups * rows * size),
-    )(own, *got)
+    )(own, *got, *through)
 
 
 def block_kernel(features, heads, n_pieces, own_ref, got_ref, *refs):
@@ -643,7 +647,7 @@
     images = [images[k] for k in [0] + order]
     got = [to_oc(x, j + 1) for j, x in enumerate(sent)]
     own, sent = text_sum(own, got, text_rows)
-    own, sent = text_sum(own, [to_z(sent, 1)], text_rows)
+    own, sent, images[0] = text_sum(own, [to_z(sent, 1)], text_rows, [packed[0]])
     got = to_z(sent, 2)
 
     gg = gated_parts(meta, gate, d_out[0], n_dp, G, OC, place)

time: 110 us -> 110 us (level)
  no operation moved by 1% of the time
where the time goes in v18:
time: 110 us; the launch traced here: 109 us
  waiting for transfers between devices  50.1 us (46%)
  starting transfers between devices  29.4 us (27%)
  Pallas kernels  21.5 us (20%)
  local copies, waits for them, and re-layouts  5.86 us (5%)
  between operations  1.46 us (1%)
    ppermute x14, waiting for transfers between devices, to_z(): return lax.ppermute(x, 'seq', perm)  42.8 us
    ppermute x14, starting transfers between devices, to_z(): return lax.ppermute(x, 'seq', perm)  19.5 us
    ppermute x6, starting transfers between devices, to_dp(): return lax.ppermute(x, 'dp', [(a, a ^ k) for a in range(n_dp)])  8.13 us
    unnamed x18, local copies, waits for them, and re-layouts  5.76 us
    pallas_call x1, Pallas kernels, project(): pl.pallas_call(functools.partial(project_kernel, groups, parts, place_of)...  5.7 us
    pallas_call x1, Pallas kernels, text_project(): pl.pallas_call(functools.partial(text_kernel, groups, heads, place_of, wh...  5.66 us
    ppermute x6, waiting for transfers between devices, to_dp(): return lax.ppermute(x, 'dp', [(a, a ^ k) for a in range(n_dp)])  5.57 us
    pallas_call x2, Pallas kernels, attention(): pl.pallas_call(functools.partial(attention_kernel, n_pieces, len(blocks),...  3.71 us
  transfers between devices with their start and end apart: 27, of which 10 were waited for; matrix products, arithmetic and copies ran while one was open for 1% of the time, Pallas kernels for 12%

profile of v18, /device:TPU:0, one launch (start us, length us, event | category | flops | bytes accessed | tf_op | source)
XLA Modules:
  0.0 109.3 jit_solution(15250260082718537859)
XLA Ops:
  1.3 5.7 %shard_map.164 = (f32[4,336,128]{2,1,0:T(8,128)}, bf16[1152,128]{1,0:T(8,128)(2,1)}, bf16[1152,128]{1,0:T(8,128)(2,1)}, bf16[1152,128]{1,0:T(8,128)(2,1)}, bf16[...) custom-call(s32[1]{0:T(128)} %copy.22.len_ref, s32[1,64]{1,0:T(1,128)} %src_ref.1, bf16[64,512]{1,0:T(8,128)(2,1)} %bitcast.36, ...), custom_call_target="tpu_custom_call" | custom-call | flops 301989888 | bytes 4718592 | tf_op jit(solution)/shard_map/pallas_call | solution.py:140
  7.0 0.5 collective-permute-start
  7.5 3.7 %collective-permute-start.3 = (bf16[1152,128]{1,0:T(8,128)(2,1)}, bf16[1152,128]{1,0:T(8,128)(2,1)S(1)}, u32[]{:S(2)}, u32[]{:S(2)}) collective-permute-start(bf16[1152,128]{1,0:T(8,128)(2,1)} %get-tuple-element.50), channel_id=1, source_target_pairs={{0,4},{2,6},{4,0},{6,2},{1,5},{3,7},{5,1},{7,3},{8,12},{10,14},{12... | collective-permute-start | bytes 884744 | tf_op jit(solution)/shard_map/ppermute | solution.py:614
  11.1 1.4 %collective-permute-start.4 = (bf16[1152,128]{1,0:T(8,128)(2,1)}, bf16[1152,128]{1,0:T(8,128)(2,1)S(1)}, u32[]{:S(2)}, u32[]{:S(2)}) collective-permute-start(bf16[1152,128]{1,0:T(8,128)(2,1)} %get-tuple-element.51), channel_id=1, source_target_pairs={{0,6},{2,4},{4,2},{6,0},{1,7},{3,5},{5,3},{7,1},{8,14},{10,12},{12... | collective-permute-start | bytes 884744 | tf_op jit(solution)/shard_map/ppermute | solution.py:614
  12.5 0.2 collective-permute-start.5
  12.7 1.1 %copy-done.2 = f32[4,336,128]{2,1,0:T(8,128)S(1)} copy-done((f32[4,336,128]{2,1,0:T(8,128)S(1)}, f32[4,336,128]{2,1,0:T(8,128)}, u32[]{:S(2)}) %copy-start.2) | copy-done | bytes 688152
  13.8 0.2 shard_map.165
  14.0 1.9 %collective-permute-start.1 = (bf16[2,320,128]{2,1,0:T(8,128)(2,1)S(1)}, bf16[2,320,128]{2,1,0:T(8,128)(2,1)S(1)}, u32[]{:S(2)}, u32[]{:S(2)}) collective-permute-start(bf16[2,320,128]{2,1,0:T(8,128)(2,1)S(1)} %get-tuple-element.45), channel_id=1, source_target_pairs={{0,2},{2,0},{4,6},{6,4},{1,3},{3,1},{5,7},{7,5},{8,10},{10,8},{12,... | collective-permute-start | bytes 491528 | tf_op jit(solution)/shard_map/ppermute | solution.py:614
  15.9 0.6 pad_add_fusion.meta_ref
  16.4 2.3 %shard_map.167 = (bf16[2,4,96,128]{3,2,1,0:T(8,128)(2,1)}, bf16[2,4,96,128]{3,2,1,0:T(8,128)(2,1)}, bf16[2,4,96,128]{3,2,1,0:T(8,128)(2,1)}, bf16[2,4,96,128]{3,2,1,0:T(8,128)(2,1)}) custom-call(s32[3]{0:T(128)} %pad_add_fusion.meta_ref, f32[1,3072]{1,0:T(1,128)} %gate_ref.3, bf16[128,3072]{1,0:T(8,128)(2,1)} %bitcast.31), custom_call_target="tpu_custom_call" | custom-call | bytes 1572864 | tf_op jit(solution)/shard_map/pallas_call | solution.py:355
  18.8 1.5 %collective-permute-start.6 = (bf16[2,4,96,128]{3,2,1,0:T(8,128)(2,1)}, bf16[2,4,96,128]{3,2,1,0:T(8,128)(2,1)S(1)}, u32[]{:S(2)}, u32[]{:S(2)}) collective-permute-start(bf16[2,4,96,128]{3,2,1,0:T(8,128)(2,1)} %get-tuple-element.53), channel_id=1, source_target_pairs={{0,8},{8,0},{16,24},{24,16},{1,9},{9,1},{17,25},{25,17},{2,10},{10... | collective-permute-start | bytes 589832 | tf_op jit(solution)/shard_map/ppermute | solution.py:621
  20.3 16.2 %collective-permute-done.1.refs_0_ = bf16[2,320,128]{2,1,0:T(8,128)(2,1)S(1)} collective-permute-done((bf16[2,320,128]{2,1,0:T(8,128)(2,1)S(1)}, bf16[2,320,128]{2,1,0:T(8,128)(2,1)S(1)}, u32[]{:S(2)}, u32[]{:S(2)}) %collective-permute-start.1) | collective-permute-done | bytes 163872 | tf_op jit(solution)/shard_map/ppermute | solution.py:614
  36.5 1.0 copy-done.3
  37.4 0.2 shard_map.166
  37.6 1.7 %collective-permute-start.2 = (bf16[1,320,128]{2,1,0:T(8,128)(2,1)S(1)}, bf16[1,320,128]{2,1,0:T(8,128)(2,1)S(1)}, u32[]{:S(2)}, u32[]{:S(2)}) collective-permute-start(bf16[1,320,128]{2,1,0:T(8,128)(2,1)S(1)} %get-tuple-element.48), channel_id=1, source_target_pairs={{0,4},{2,6},{4,0},{6,2},{1,5},{3,7},{5,1},{7,3},{8,12},{10,14},{12... | collective-permute-start | bytes 245768 | tf_op jit(solution)/shard_map/ppermute | solution.py:614
  39.3 4.6 %collective-permute-done.2.got_ref = bf16[1,320,128]{2,1,0:T(8,128)(2,1)S(1)} collective-permute-done((bf16[1,320,128]{2,1,0:T(8,128)(2,1)S(1)}, bf16[1,320,128]{2,1,0:T(8,128)(2,1)S(1)}, u32[]{:S(2)}, u32[]{:S(2)}) %collective-permute-start.2) | collective-permute-done | bytes 81952 | tf_op jit(solution)/shard_map/ppermute | solution.py:614
  43.9 0.3 shard_map.168.refs_0_
  44.2 1.7 %collective-permute-start.11 = (bf16[2,4,96,128]{3,2,1,0:T(8,128)(2,1)}, bf16[2,4,96,128]{3,2,1,0:T(8,128)(2,1)}, u32[]{:S(2)}, u32[]{:S(2)}) collective-permute-start(bf16[2,4,96,128]{3,2,1,0:T(8,128)(2,1)} %get-tuple-element.58), channel_id=1, source_target_pairs={{0,16},{8,24},{16,0},{24,8},{1,17},{9,25},{17,1},{25,9},{2,18},{10... | collective-permute-start | bytes 589832 | tf_op jit(solution)/shard_map/ppermute | solution.py:621
  45.9 1.4 %collective-permute-start.12 = (bf16[2,4,96,128]{3,2,1,0:T(8,128)(2,1)}, bf16[2,4,96,128]{3,2,1,0:T(8,128)(2,1)}, u32[]{:S(2)}, u32[]{:S(2)}) collective-permute-start(bf16[2,4,96,128]{3,2,1,0:T(8,128)(2,1)} %get-tuple-element.59), channel_id=1, source_target_pairs={{0,24},{8,16},{16,8},{24,0},{1,25},{9,17},{17,9},{25,1},{2,26},{10... | collective-permute-start | bytes 589832 | tf_op jit(solution)/shard_map/ppermute | solution.py:621
  47.4 2.7 %shard_map.169 = (bf16[128,384]{1,0:T(8,128)(2,1)S(1)}, bf16[128,384]{1,0:T(8,128)(2,1)S(1)}, bf16[128,384]{1,0:T(8,128)(2,1)S(1)}, bf16[32,384]{1,0:T(8,128)(2,1)S(1)}) custom-call(bf16[4912,128]{1,0:T(8,128)(2,1)S(1)} %shard_map.168.refs_0_, bf16[4912,128]{1,0:T(8,128)(2,1)S(1)} %collective-permute-done.7.refs_1_), custom_call_target="tpu_custom_call" | custom-call | flops 695205888 | bytes 2310144 | tf_op jit(solution)/shard_map/pallas_call | solution.py:295
  50.1 0.8 collective-permute-start.8
  50.9 2.1 %collective-permute-start.9 = (bf16[136,384]{1,0:T(8,128)(2,1)S(1)}, bf16[136,384]{1,0:T(8,128)(2,1)S(1)}, u32[]{:S(2)}, u32[]{:S(2)}) collective-permute-start(bf16[136,384]{1,0:T(8,128)(2,1)S(1)} %pad_maximum_fusion.1), channel_id=1, source_target_pairs={{0,6},{2,4},{4,2},{6,0},{1,7},{3,5},{5,3},{7,1},{8,14},{10,12},{12... | collective-permute-start | bytes 313352 | tf_op jit(solution)/shard_map/ppermute | solution.py:614
  53.0 0.8 collective-permute-start.10
  53.8 1.1 shard_map.170
  54.9 5.6 %collective-permute-done.8.refs_0_ = bf16[136,384]{1,0:T(8,128)(2,1)S(1)} collective-permute-done((bf16[136,384]{1,0:T(8,128)(2,1)S(1)}, bf16[136,384]{1,0:T(8,128)(2,1)S(1)}, u32[]{:S(2)}, u32[]{:S(2)}) %collective-permute-start.8) | collective-permute-done | bytes 104480 | tf_op jit(solution)/shard_map/ppermute | solution.py:614
  60.6 1.1 %collective-permute-done.10.refs_2_ = bf16[136,384]{1,0:T(8,128)(2,1)S(1)} collective-permute-done((bf16[136,384]{1,0:T(8,128)(2,1)S(1)}, bf16[136,384]{1,0:T(8,128)(2,1)S(1)}, u32[]{:S(2)}, u32[]{:S(2)}) %collective-permute-start.10) | collective-permute-done | bytes 104480 | tf_op jit(solution)/shard_map/ppermute | solution.py:614
  62.0 1.6 %collective-permute-start.16 = (bf16[128,1536]{1,0:T(8,128)(2,1)S(1)}, bf16[128,1536]{1,0:T(8,128)(2,1)S(1)}, u32[]{:S(2)}, u32[]{:S(2)}) collective-permute-start(bf16[128,1536]{1,0:T(8,128)(2,1)S(1)} %shard_map.171.attn_ref.refs_2_), channel_id=1, source_target_pairs={{0,8},{8,0},{16,24},{24,16},{1,9},{9,1},{17,25},{25,17},{2,10},{10... | collective-permute-start | bytes 1179656 | tf_op jit(solution)/shard_map/ppermute | solution.py:621
  63.7 1.5 %collective-permute-start.15 = (bf16[128,1536]{1,0:T(8,128)(2,1)S(1)}, bf16[128,1536]{1,0:T(8,128)(2,1)S(1)}, u32[]{:S(2)}, u32[]{:S(2)}) collective-permute-start(bf16[128,1536]{1,0:T(8,128)(2,1)S(1)} %shard_map.171.attn_ref.refs_2_), channel_id=1, source_target_pairs={{0,16},{8,24},{16,0},{24,8},{1,17},{9,25},{17,1},{25,9},{2,18},{10... | collective-permute-start | bytes 1179656 | tf_op jit(solution)/shard_map/ppermute | solution.py:621
  65.2 0.4 collective-permute-start.14
  65.6 3.7 %copy-done = bf16[3072,1536]{1,0:T(8,128)(2,1)S(1)} copy-done((bf16[3072,1536]{1,0:T(8,128)(2,1)S(1)}, bf16[3072,1536]{1,0:T(8,128)(2,1)}, u32[]{:S(2)}) %copy-start) | copy-done | bytes 9437208
  69.3 5.7 %shard_map.172 = (bf16[128,3072]{1,0:T(8,128)(2,1)}, bf16[128,1536]{1,0:T(8,128)(2,1)}, f32[4,384]{1,0:T(4,128)S(1)}, bf16[144,1536]{1,0:T(8,128)(2,1)S(1)}) custom-call(s32[3]{0:T(128)S(1)} %copy-done.6, bf16[128,1536]{1,0:T(8,128)(2,1)S(1)} %shard_map.171.attn_ref.refs_2_, bf16[3072,1536]{1,0:T(8,128)(2,1)S(1)} %copy-done, f32[1,3072]{1,0:T(1,128)S(1)} %copy-done.5, ...), custom_call_target="tpu_custom_call" | custom-call | flops 2415919104 | bytes 9437184 | tf_op jit(solution)/shard_map/pallas_call | solution.py:436
  75.0 1.1 shard_map.173
  76.1 0.6 collective-permute-start.13
  76.7 0.1 collective-permute-start.20
  76.7 5.6 %collective-permute-done.15.refs_4_ = bf16[128,1536]{1,0:T(8,128)(2,1)S(1)} collective-permute-done((bf16[128,1536]{1,0:T(8,128)(2,1)S(1)}, bf16[128,1536]{1,0:T(8,128)(2,1)S(1)}, u32[]{:S(2)}, u32[]{:S(2)}) %collective-permute-start.15) | collective-permute-done | bytes 393248 | tf_op jit(solution)/shard_map/ppermute | solution.py:621
  82.3 0.5 collective-permute-start.18
  82.8 1.2 %collective-permute-done.19.refs_8_ = bf16[128,1536]{1,0:T(8,128)(2,1)S(1)} collective-permute-done((bf16[128,1536]{1,0:T(8,128)(2,1)S(1)}, bf16[128,1536]{1,0:T(8,128)(2,1)S(1)}, u32[]{:S(2)}, u32[]{:S(2)}) %collective-permute-start.19) | collective-permute-done | bytes 393248 | tf_op jit(solution)/shard_map/ppermute | solution.py:618
  84.0 0.6 collective-permute-done.18.refs_7_
  84.6 1.4 %shard_map.174 = (f32[1168,128]{1,0:T(8,128)S(1)}, bf16[576,128]{1,0:T(8,128)(2,1)S(1)}, bf16[592,128]{1,0:T(8,128)(2,1)S(1)}, f32[576,128]{1,0:T(8,128)S(1)}, f...) custom-call(bf16[4,4,96,128]{3,2,1,0:T(8,128)(2,1)S(1)} %get-tuple-element.63.refs_0_, ...), custom_call_target="tpu_custom_call" | custom-call | flops 1207959552 | bytes 5111808 | tf_op jit(solution)/shard_map/pallas_call | solution.py:512
  86.0 2.0 %collective-permute-start.23 = (bf16[592,128]{1,0:T(8,128)(2,1)S(1)}, bf16[592,128]{1,0:T(8,128)(2,1)S(1)}, u32[]{:S(2)}, u32[]{:S(2)}) collective-permute-start(bf16[592,128]{1,0:T(8,128)(2,1)S(1)} %get-tuple-element.71), channel_id=1, source_target_pairs={{0,2},{2,0},{4,6},{6,4},{1,3},{3,1},{5,7},{7,5},{8,10},{10,8},{12,... | collective-permute-start | bytes 454664 | tf_op jit(solution)/shard_map/ppermute | solution.py:614
  88.0 0.1 collective-permute-start.21
  88.1 4.7 %collective-permute-done.23.got_ref = bf16[592,128]{1,0:T(8,128)(2,1)S(1)} collective-permute-done((bf16[592,128]{1,0:T(8,128)(2,1)S(1)}, bf16[592,128]{1,0:T(8,128)(2,1)S(1)}, u32[]{:S(2)}, u32[]{:S(2)}) %collective-permute-start.23) | collective-permute-done | bytes 151584 | tf_op jit(solution)/shard_map/ppermute | solution.py:614
  92.9 2.2 %collective-permute-start.24 = (bf16[592,128]{1,0:T(8,128)(2,1)S(1)}, bf16[592,128]{1,0:T(8,128)(2,1)S(1)}, u32[]{:S(2)}, u32[]{:S(2)}) collective-permute-start(bf16[592,128]{1,0:T(8,128)(2,1)S(1)} %get-tuple-element.74), channel_id=1, source_target_pairs={{0,4},{2,6},{4,0},{6,2},{1,5},{3,7},{5,1},{7,3},{8,12},{10,14},{12... | collective-permute-start | bytes 454664 | tf_op jit(solution)/shard_map/ppermute | solution.py:614
  95.1 0.4 collective-permute-done.21.got_ref
  95.5 2.4 %collective-permute-start.22 = (bf16[576,128]{1,0:T(8,128)(2,1)S(1)}, bf16[576,128]{1,0:T(8,128)(2,1)S(1)}, u32[]{:S(2)}, u32[]{:S(2)}) collective-permute-start(bf16[576,128]{1,0:T(8,128)(2,1)S(1)} %shard_map.175), channel_id=1, source_target_pairs={{0,4},{2,6},{4,0},{6,2},{1,5},{3,7},{5,1},{7,3},{8,12},{10,14},{12... | collective-permute-start | bytes 442376 | tf_op jit(solution)/shard_map/ppermute | solution.py:614
  98.0 0.2 collective-permute-start.25
  98.1 10.2 %collective-permute-done.22.far_low = bf16[576,128]{1,0:T(8,128)(2,1)S(1)} collective-permute-done((bf16[576,128]{1,0:T(8,128)(2,1)S(1)}, bf16[576,128]{1,0:T(8,128)(2,1)S(1)}, u32[]{:S(2)}, u32[]{:S(2)}) %collective-permute-start.22) | collective-permute-done | bytes 147488 | tf_op jit(solution)/shard_map/ppermute | solution.py:614
  108.3 0.9 shard_map.177
  (51 shorter events, 0.8 us)
Async XLA Ops:
  1.3 46.0 %copy-start.8 = (s32[1,64]{1,0:T(1,128)S(1)}, s32[1,64]{1,0:T(1,128)}, u32[]{:S(2)}) copy-start(s32[1,64]{1,0:T(1,128)} %src_ref.1) | copy-start | bytes 772
  7.0 5.8 %collective-permute-start = (bf16[4,320,128]{2,1,0:T(8,128)(2,1)}, bf16[4,320,128]{2,1,0:T(8,128)(2,1)S(1)}, u32[]{:S(2)}, u32[]{:S(2)}) collective-permute-start(bf16[4,320,128]{2,1,0:T(8,128)(2,1)} %get-tuple-element.43), channel_id=1, source_target_pairs={{0,1},{2,3},{4,5},{6,7},{1,0},{3,2},{5,4},{7,6},{8,9},{10,11},{12,... | collective-permute-start | bytes 983048 | tf_op jit(solution)/shard_map/ppermute | solution.py:618
  7.5 31.8 %collective-permute-start.3 = (bf16[1152,128]{1,0:T(8,128)(2,1)}, bf16[1152,128]{1,0:T(8,128)(2,1)S(1)}, u32[]{:S(2)}, u32[]{:S(2)}) collective-permute-start(bf16[1152,128]{1,0:T(8,128)(2,1)} %get-tuple-element.50), channel_id=1, source_target_pairs={{0,4},{2,6},{4,0},{6,2},{1,5},{3,7},{5,1},{7,3},{8,12},{10,14},{12... | collective-permute-start | bytes 884744 | tf_op jit(solution)/shard_map/ppermute | solution.py:614
  11.1 28.2 %collective-permute-start.4 = (bf16[1152,128]{1,0:T(8,128)(2,1)}, bf16[1152,128]{1,0:T(8,128)(2,1)S(1)}, u32[]{:S(2)}, u32[]{:S(2)}) collective-permute-start(bf16[1152,128]{1,0:T(8,128)(2,1)} %get-tuple-element.51), channel_id=1, source_target_pairs={{0,6},{2,4},{4,2},{6,0},{1,7},{3,5},{5,3},{7,1},{8,14},{10,12},{12... | collective-permute-start | bytes 884744 | tf_op jit(solution)/shard_map/ppermute | solution.py:614
  12.5 26.8 %collective-permute-start.5 = (bf16[1152,128]{1,0:T(8,128)(2,1)}, bf16[1152,128]{1,0:T(8,128)(2,1)S(1)}, u32[]{:S(2)}, u32[]{:S(2)}) collective-permute-start(bf16[1152,128]{1,0:T(8,128)(2,1)} %get-tuple-element.52), channel_id=1, source_target_pairs={{0,2},{2,0},{4,6},{6,4},{1,3},{3,1},{5,7},{7,5},{8,10},{10,8},{12,... | collective-permute-start | bytes 884744 | tf_op jit(solution)/shard_map/ppermute | solution.py:614
  12.7 1.1 %copy-start.2 = (f32[4,336,128]{2,1,0:T(8,128)S(1)}, f32[4,336,128]{2,1,0:T(8,128)}, u32[]{:S(2)}) copy-start(f32[4,336,128]{2,1,0:T(8,128)} %get-tuple-element.42.own_ref) | copy-start | bytes 2064388
  14.0 22.5 %collective-permute-start.1 = (bf16[2,320,128]{2,1,0:T(8,128)(2,1)S(1)}, bf16[2,320,128]{2,1,0:T(8,128)(2,1)S(1)}, u32[]{:S(2)}, u32[]{:S(2)}) collective-permute-start(bf16[2,320,128]{2,1,0:T(8,128)(2,1)S(1)} %get-tuple-element.45), channel_id=1, source_target_pairs={{0,2},{2,0},{4,6},{6,4},{1,3},{3,1},{5,7},{7,5},{8,10},{10,8},{12,... | collective-permute-start | bytes 491528 | tf_op jit(solution)/shard_map/ppermute | solution.py:614
  18.8 20.5 %collective-permute-start.6 = (bf16[2,4,96,128]{3,2,1,0:T(8,128)(2,1)}, bf16[2,4,96,128]{3,2,1,0:T(8,128)(2,1)S(1)}, u32[]{:S(2)}, u32[]{:S(2)}) collective-permute-start(bf16[2,4,96,128]{3,2,1,0:T(8,128)(2,1)} %get-tuple-element.53), channel_id=1, source_target_pairs={{0,8},{8,0},{16,24},{24,16},{1,9},{9,1},{17,25},{25,17},{2,10},{10... | collective-permute-start | bytes 589832 | tf_op jit(solution)/shard_map/ppermute | solution.py:621
  36.5 1.0 copy-start.3
  37.6 6.3 %collective-permute-start.2 = (bf16[1,320,128]{2,1,0:T(8,128)(2,1)S(1)}, bf16[1,320,128]{2,1,0:T(8,128)(2,1)S(1)}, u32[]{:S(2)}, u32[]{:S(2)}) collective-permute-start(bf16[1,320,128]{2,1,0:T(8,128)(2,1)S(1)} %get-tuple-element.48), channel_id=1, source_target_pairs={{0,4},{2,6},{4,0},{6,2},{1,5},{3,7},{5,1},{7,3},{8,12},{10,14},{12... | collective-permute-start | bytes 245768 | tf_op jit(solution)/shard_map/ppermute | solution.py:614
  43.9 21.7 %copy-start.1 = (bf16[1,128,3072]{2,1,0:T(8,128)(2,1)S(1)}, bf16[1,128,3072]{2,1,0:T(8,128)(2,1)}, u32[]{:S(2)}) copy-start(bf16[1,128,3072]{2,1,0:T(8,128)(2,1)} %param.25) | copy-start | bytes 2359300
  43.9 21.7 %copy-start.5 = (f32[1,3072]{1,0:T(1,128)S(1)}, f32[1,3072]{1,0:T(1,128)}, u32[]{:S(2)}) copy-start(f32[1,3072]{1,0:T(1,128)} %gate_ref.3) | copy-start | bytes 36868
  43.9 21.7 %copy-start.6 = (s32[3]{0:T(128)S(1)}, s32[3]{0:T(128)}, u32[]{:S(2)}) copy-start(s32[3]{0:T(128)} %pad_add_fusion.meta_ref) | copy-start | bytes 40
  44.1 3.3 %collective-permute-start.7 = (bf16[4912,128]{1,0:T(8,128)(2,1)S(1)}, bf16[4912,128]{1,0:T(8,128)(2,1)S(1)}, u32[]{:S(2)}, u32[]{:S(2)}) collective-permute-start(bf16[4912,128]{1,0:T(8,128)(2,1)S(1)} %shard_map.168.refs_0_), channel_id=1, source_target_pairs={{0,1},{2,3},{4,5},{6,7},{1,0},{3,2},{5,4},{7,6},{8,9},{10,11},{12,... | collective-permute-start | bytes 3772424 | tf_op jit(solution)/shard_map/ppermute | solution.py:618
  44.2 17.7 %collective-permute-start.11 = (bf16[2,4,96,128]{3,2,1,0:T(8,128)(2,1)}, bf16[2,4,96,128]{3,2,1,0:T(8,128)(2,1)}, u32[]{:S(2)}, u32[]{:S(2)}) collective-permute-start(bf16[2,4,96,128]{3,2,1,0:T(8,128)(2,1)} %get-tuple-element.58), channel_id=1, source_target_pairs={{0,16},{8,24},{16,0},{24,8},{1,17},{9,25},{17,1},{25,9},{2,18},{10... | collective-permute-start | bytes 589832 | tf_op jit(solution)/shard_map/ppermute | solution.py:621
  45.9 16.1 %collective-permute-start.12 = (bf16[2,4,96,128]{3,2,1,0:T(8,128)(2,1)}, bf16[2,4,96,128]{3,2,1,0:T(8,128)(2,1)}, u32[]{:S(2)}, u32[]{:S(2)}) collective-permute-start(bf16[2,4,96,128]{3,2,1,0:T(8,128)(2,1)} %get-tuple-element.59), channel_id=1, source_target_pairs={{0,24},{8,16},{16,8},{24,0},{1,25},{9,17},{17,9},{25,1},{2,26},{10... | collective-permute-start | bytes 589832 | tf_op jit(solution)/shard_map/ppermute | solution.py:621
  50.1 10.4 %collective-permute-start.8 = (bf16[136,384]{1,0:T(8,128)(2,1)S(1)}, bf16[136,384]{1,0:T(8,128)(2,1)S(1)}, u32[]{:S(2)}, u32[]{:S(2)}) collective-permute-start(bf16[136,384]{1,0:T(8,128)(2,1)S(1)} %pad_maximum_fusion), channel_id=1, source_target_pairs={{0,4},{2,6},{4,0},{6,2},{1,5},{3,7},{5,1},{7,3},{8,12},{10,14},{12... | collective-permute-start | bytes 313352 | tf_op jit(solution)/shard_map/ppermute | solution.py:614
  50.9 9.7 %collective-permute-start.9 = (bf16[136,384]{1,0:T(8,128)(2,1)S(1)}, bf16[136,384]{1,0:T(8,128)(2,1)S(1)}, u32[]{:S(2)}, u32[]{:S(2)}) collective-permute-start(bf16[136,384]{1,0:T(8,128)(2,1)S(1)} %pad_maximum_fusion.1), channel_id=1, source_target_pairs={{0,6},{2,4},{4,2},{6,0},{1,7},{3,5},{5,3},{7,1},{8,14},{10,12},{12... | collective-permute-start | bytes 313352 | tf_op jit(solution)/shard_map/ppermute | solution.py:614
  53.0 8.8 %collective-permute-start.10 = (bf16[136,384]{1,0:T(8,128)(2,1)S(1)}, bf16[136,384]{1,0:T(8,128)(2,1)S(1)}, u32[]{:S(2)}, u32[]{:S(2)}) collective-permute-start(bf16[136,384]{1,0:T(8,128)(2,1)S(1)} %pad_maximum_fusion.2), channel_id=1, source_target_pairs={{0,2},{2,0},{4,6},{6,4},{1,3},{3,1},{5,7},{7,5},{8,10},{10,8},{12,... | collective-permute-start | bytes 313352 | tf_op jit(solution)/shard_map/ppermute | solution.py:614
  61.9 13.1 %copy-start.7 = (bf16[1,8,1536]{2,1,0:T(8,128)(2,1)}, bf16[1,8,1536]{2,1,0:T(8,128)(2,1)S(1)}, u32[]{:S(2)}) copy-start(bf16[1,8,1536]{2,1,0:T(8,128)(2,1)S(1)} %get-tuple-element.79) | copy-start | bytes 73732
  62.0 13.0 %copy-start.4 = (bf16[2,4,96,128]{3,2,1,0:T(8,128)(2,1)S(1)}, bf16[2,4,96,128]{3,2,1,0:T(8,128)(2,1)}, u32[]{:S(2)}) copy-start(bf16[2,4,96,128]{3,2,1,0:T(8,128)(2,1)} %get-tuple-element.62.refs_0_) | copy-start | bytes 589828
  62.0 14.6 %collective-permute-start.16 = (bf16[128,1536]{1,0:T(8,128)(2,1)S(1)}, bf16[128,1536]{1,0:T(8,128)(2,1)S(1)}, u32[]{:S(2)}, u32[]{:S(2)}) collective-permute-start(bf16[128,1536]{1,0:T(8,128)(2,1)S(1)} %shard_map.171.attn_ref.refs_2_), channel_id=1, source_target_pairs={{0,8},{8,0},{16,24},{24,16},{1,9},{9,1},{17,25},{25,17},{2,10},{10... | collective-permute-start | bytes 1179656 | tf_op jit(solution)/shard_map/ppermute | solution.py:621
  63.7 18.6 %collective-permute-start.15 = (bf16[128,1536]{1,0:T(8,128)(2,1)S(1)}, bf16[128,1536]{1,0:T(8,128)(2,1)S(1)}, u32[]{:S(2)}, u32[]{:S(2)}) collective-permute-start(bf16[128,1536]{1,0:T(8,128)(2,1)S(1)} %shard_map.171.attn_ref.refs_2_), channel_id=1, source_target_pairs={{0,16},{8,24},{16,0},{24,8},{1,17},{9,25},{17,1},{25,9},{2,18},{10... | collective-permute-start | bytes 1179656 | tf_op jit(solution)/shard_map/ppermute | solution.py:621
  65.2 17.1 %collective-permute-start.14 = (bf16[128,1536]{1,0:T(8,128)(2,1)S(1)}, bf16[128,1536]{1,0:T(8,128)(2,1)S(1)}, u32[]{:S(2)}, u32[]{:S(2)}) collective-permute-start(bf16[128,1536]{1,0:T(8,128)(2,1)S(1)} %shard_map.171.attn_ref.refs_2_), channel_id=1, source_target_pairs={{0,24},{8,16},{16,8},{24,0},{1,25},{9,17},{17,9},{25,1},{2,26},{10... | collective-permute-start | bytes 1179656 | tf_op jit(solution)/shard_map/ppermute | solution.py:621
  65.6 3.7 %copy-start = (bf16[3072,1536]{1,0:T(8,128)(2,1)S(1)}, bf16[3072,1536]{1,0:T(8,128)(2,1)}, u32[]{:S(2)}) copy-start(bf16[3072,1536]{1,0:T(8,128)(2,1)} %w_ref.3) | copy-start | bytes 28311556
  75.0 7.8 %collective-permute-start.17 = (bf16[144,1536]{1,0:T(8,128)(2,1)S(1)}, bf16[144,1536]{1,0:T(8,128)(2,1)S(1)}, u32[]{:S(2)}, u32[]{:S(2)}) collective-permute-start(bf16[144,1536]{1,0:T(8,128)(2,1)S(1)} %get-tuple-element.65), channel_id=1, source_target_pairs={{0,1},{2,3},{4,5},{6,7},{1,0},{3,2},{5,4},{7,6},{8,9},{10,11},{12,... | collective-permute-start | bytes 1327112 | tf_op jit(solution)/shard_map/ppermute | solution.py:618
  76.1 6.7 %collective-permute-start.13 = (bf16[4,4,96,128]{3,2,1,0:T(8,128)(2,1)S(1)}, bf16[4,4,96,128]{3,2,1,0:T(8,128)(2,1)S(1)}, u32[]{:S(2)}, u32[]{:S(2)}) collective-permute-start(bf16[4,4,96,128]{3,2,1,0:T(8,128)(2,1)S(1)} %get-tuple-element.64), channel_id=1, source_target_pairs={{0,1},{2,3},{4,5},{6,7},{1,0},{3,2},{5,4},{7,6},{8,9},{10,11},{12,... | collective-permute-start | bytes 1179656 | tf_op jit(solution)/shard_map/ppermute | solution.py:618
  76.7 6.2 %collective-permute-start.20 = (bf16[128,1536]{1,0:T(8,128)(2,1)S(1)}, bf16[128,1536]{1,0:T(8,128)(2,1)S(1)}, u32[]{:S(2)}, u32[]{:S(2)}) collective-permute-start(bf16[128,1536]{1,0:T(8,128)(2,1)S(1)} %collective-permute-done.16.refs_5_), channel_id=1, source_target_pairs={{0,1},{2,3},{4,5},{6,7},{1,0},{3,2},{5,4},{7,6},{8,9},{10,11},{12,... | collective-permute-start | bytes 1179656 | tf_op jit(solution)/shard_map/ppermute | solution.py:618
  82.3 1.7 %collective-permute-start.19 = (bf16[128,1536]{1,0:T(8,128)(2,1)S(1)}, bf16[128,1536]{1,0:T(8,128)(2,1)S(1)}, u32[]{:S(2)}, u32[]{:S(2)}) collective-permute-start(bf16[128,1536]{1,0:T(8,128)(2,1)S(1)} %collective-permute-done.15.refs_4_), channel_id=1, source_target_pairs={{0,1},{2,3},{4,5},{6,7},{1,0},{3,2},{5,4},{7,6},{8,9},{10,11},{12,... | collective-permute-start | bytes 1179656 | tf_op jit(solution)/shard_map/ppermute | solution.py:618
  82.3 2.3 %collective-permute-start.18 = (bf16[128,1536]{1,0:T(8,128)(2,1)S(1)}, bf16[128,1536]{1,0:T(8,128)(2,1)S(1)}, u32[]{:S(2)}, u32[]{:S(2)}) collective-permute-start(bf16[128,1536]{1,0:T(8,128)(2,1)S(1)} %collective-permute-done.14.refs_3_), channel_id=1, source_target_pairs={{0,1},{2,3},{4,5},{6,7},{1,0},{3,2},{5,4},{7,6},{8,9},{10,11},{12,... | collective-permute-start | bytes 1179656 | tf_op jit(solution)/shard_map/ppermute | solution.py:618
  86.0 6.8 %collective-permute-start.23 = (bf16[592,128]{1,0:T(8,128)(2,1)S(1)}, bf16[592,128]{1,0:T(8,128)(2,1)S(1)}, u32[]{:S(2)}, u32[]{:S(2)}) collective-permute-start(bf16[592,128]{1,0:T(8,128)(2,1)S(1)} %get-tuple-element.71), channel_id=1, source_target_pairs={{0,2},{2,0},{4,6},{6,4},{1,3},{3,1},{5,7},{7,5},{8,10},{10,8},{12,... | collective-permute-start | bytes 454664 | tf_op jit(solution)/shard_map/ppermute | solution.py:614
  88.0 7.5 %collective-permute-start.21 = (bf16[576,128]{1,0:T(8,128)(2,1)S(1)}, bf16[576,128]{1,0:T(8,128)(2,1)S(1)}, u32[]{:S(2)}, u32[]{:S(2)}) collective-permute-start(bf16[576,128]{1,0:T(8,128)(2,1)S(1)} %get-tuple-element.69), channel_id=1, source_target_pairs={{0,2},{2,0},{4,6},{6,4},{1,3},{3,1},{5,7},{7,5},{8,10},{10,8},{12,... | collective-permute-start | bytes 442376 | tf_op jit(solution)/shard_map/ppermute | solution.py:614
  92.9 15.5 %collective-permute-start.24 = (bf16[592,128]{1,0:T(8,128)(2,1)S(1)}, bf16[592,128]{1,0:T(8,128)(2,1)S(1)}, u32[]{:S(2)}, u32[]{:S(2)}) collective-permute-start(bf16[592,128]{1,0:T(8,128)(2,1)S(1)} %get-tuple-element.74), channel_id=1, source_target_pairs={{0,4},{2,6},{4,0},{6,2},{1,5},{3,7},{5,1},{7,3},{8,12},{10,14},{12... | collective-permute-start | bytes 454664 | tf_op jit(solution)/shard_map/ppermute | solution.py:614
  95.1 13.2 %collective-permute-start.26 = (bf16[592,128]{1,0:T(8,128)(2,1)S(1)}, bf16[592,128]{1,0:T(8,128)(2,1)S(1)}, u32[]{:S(2)}, u32[]{:S(2)}) collective-permute-start(bf16[592,128]{1,0:T(8,128)(2,1)S(1)} %get-tuple-element.76), channel_id=1, source_target_pairs={{0,2},{2,0},{4,6},{6,4},{1,3},{3,1},{5,7},{7,5},{8,10},{10,8},{12,... | collective-permute-start | bytes 454664 | tf_op jit(solution)/shard_map/ppermute | solution.py:614
  95.5 12.8 %collective-permute-start.22 = (bf16[576,128]{1,0:T(8,128)(2,1)S(1)}, bf16[576,128]{1,0:T(8,128)(2,1)S(1)}, u32[]{:S(2)}, u32[]{:S(2)}) collective-permute-start(bf16[576,128]{1,0:T(8,128)(2,1)S(1)} %shard_map.175), channel_id=1, source_target_pairs={{0,4},{2,6},{4,0},{6,2},{1,5},{3,7},{5,1},{7,3},{8,12},{10,14},{12... | collective-permute-start | bytes 442376 | tf_op jit(solution)/shard_map/ppermute | solution.py:614
  98.0 10.4 %collective-permute-start.25 = (bf16[576,128]{1,0:T(8,128)(2,1)S(1)}, bf16[576,128]{1,0:T(8,128)(2,1)S(1)}, u32[]{:S(2)}, u32[]{:S(2)}) collective-permute-start(bf16[576,128]{1,0:T(8,128)(2,1)S(1)} %get-tuple-element.75), channel_id=1, source_target_pairs={{0,2},{2,0},{4,6},{6,4},{1,3},{3,1},{5,7},{7,5},{8,10},{10,8},{12,... | collective-permute-start | bytes 442376 | tf_op jit(solution)/shard_map/ppermute | solution.py:614

commit v19 on v18

--- a/solution.py
+++ b/solution.py
@@ -646,8 +646,8 @@
         images[k] = to_z(packed[k], k)
     images = [images[k] for k in [0] + order]
     got = [to_oc(x, j + 1) for j, x in enumerate(sent)]
-    own, sent = text_sum(own, got, text_rows)
-    own, sent, images[0] = text_sum(own, [to_z(sent, 1)], text_rows, [packed[0]])
+    own, sent, images[0] = text_sum(own, got, text_rows, [packed[0]])
+    own, sent = text_sum(own, [to_z(sent, 1)], text_rows)
     got = to_z(sent, 2)
 
     gg = gated_parts(meta, gate, d_out[0], n_dp, G, OC, place)

time: 110 us -> 109 us (level)
  no operation moved by 1% of the time
where the time goes in v19:
time: 109 us; the launch traced here: 108 us
  waiting for transfers between devices  49.1 us (45%)
  starting transfers between devices  29.4 us (27%)
  Pallas kernels  21.5 us (20%)
  local copies, waits for them, and re-layouts  5.86 us (5%)
  between operations  1.46 us (1%)
    ppermute x14, waiting for transfers between devices, to_z(): return lax.ppermute(x, 'seq', perm)  41.7 us
    ppermute x14, starting transfers between devices, to_z(): return lax.ppermute(x, 'seq', perm)  19.5 us
    ppermute x6, starting transfers between devices, to_dp(): return lax.ppermute(x, 'dp', [(a, a ^ k) for a in range(n_dp)])  8.13 us
    unnamed x18, local copies, waits for them, and re-layouts  5.76 us
    pallas_call x1, Pallas kernels, project(): pl.pallas_call(functools.partial(project_kernel, groups, parts, place_of)...  5.7 us
    pallas_call x1, Pallas kernels, text_project(): pl.pallas_call(functools.partial(text_kernel, groups, heads, place_of, wh...  5.66 us
    ppermute x6, waiting for transfers between devices, to_dp(): return lax.ppermute(x, 'dp', [(a, a ^ k) for a in range(n_dp)])  5.58 us
    pallas_call x2, Pallas kernels, attention(): pl.pallas_call(functools.partial(attention_kernel, n_pieces, len(blocks),...  3.71 us
  transfers between devices with their start and end apart: 27, of which 10 were waited for; matrix products, arithmetic and copies ran while one was open for 1% of the time, Pallas kernels for 12%

profile of v19, /device:TPU:0, one launch (start us, length us, event | category | flops | bytes accessed | tf_op | source)
XLA Modules:
  0.0 108.3 jit_solution(11364784129706846361)
XLA Ops:
  1.3 5.7 %shard_map.164 = (f32[4,336,128]{2,1,0:T(8,128)}, bf16[1152,128]{1,0:T(8,128)(2,1)}, bf16[1152,128]{1,0:T(8,128)(2,1)}, bf16[1152,128]{1,0:T(8,128)(2,1)}, bf16[...) custom-call(s32[1]{0:T(128)} %copy.22.len_ref, s32[1,64]{1,0:T(1,128)} %src_ref.1, bf16[64,512]{1,0:T(8,128)(2,1)} %bitcast.36, ...), custom_call_target="tpu_custom_call" | custom-call | flops 301989888 | bytes 4718592 | tf_op jit(solution)/shard_map/pallas_call | solution.py:140
  7.0 0.5 collective-permute-start
  7.5 3.7 %collective-permute-start.3 = (bf16[1152,128]{1,0:T(8,128)(2,1)}, bf16[1152,128]{1,0:T(8,128)(2,1)S(1)}, u32[]{:S(2)}, u32[]{:S(2)}) collective-permute-start(bf16[1152,128]{1,0:T(8,128)(2,1)} %get-tuple-element.50), channel_id=1, source_target_pairs={{0,4},{2,6},{4,0},{6,2},{1,5},{3,7},{5,1},{7,3},{8,12},{10,14},{12... | collective-permute-start | bytes 884744 | tf_op jit(solution)/shard_map/ppermute | solution.py:614
  11.1 1.4 %collective-permute-start.4 = (bf16[1152,128]{1,0:T(8,128)(2,1)}, bf16[1152,128]{1,0:T(8,128)(2,1)S(1)}, u32[]{:S(2)}, u32[]{:S(2)}) collective-permute-start(bf16[1152,128]{1,0:T(8,128)(2,1)} %get-tuple-element.51), channel_id=1, source_target_pairs={{0,6},{2,4},{4,2},{6,0},{1,7},{3,5},{5,3},{7,1},{8,14},{10,12},{12... | collective-permute-start | bytes 884744 | tf_op jit(solution)/shard_map/ppermute | solution.py:614
  12.5 0.2 collective-permute-start.5
  12.7 1.1 %copy-done.2 = f32[4,336,128]{2,1,0:T(8,128)S(1)} copy-done((f32[4,336,128]{2,1,0:T(8,128)S(1)}, f32[4,336,128]{2,1,0:T(8,128)}, u32[]{:S(2)}) %copy-start.2) | copy-done | bytes 688152
  13.8 1.0 copy-done.3
  14.8 0.2 shard_map.165
  15.0 1.9 %collective-permute-start.1 = (bf16[2,320,128]{2,1,0:T(8,128)(2,1)S(1)}, bf16[2,320,128]{2,1,0:T(8,128)(2,1)S(1)}, u32[]{:S(2)}, u32[]{:S(2)}) collective-permute-start(bf16[2,320,128]{2,1,0:T(8,128)(2,1)S(1)} %get-tuple-element.46), channel_id=1, source_target_pairs={{0,2},{2,0},{4,6},{6,4},{1,3},{3,1},{5,7},{7,5},{8,10},{10,8},{12,... | collective-permute-start | bytes 491528 | tf_op jit(solution)/shard_map/ppermute | solution.py:614
  16.8 0.6 pad_add_fusion.meta_ref
  17.5 2.3 %shard_map.167 = (bf16[2,4,96,128]{3,2,1,0:T(8,128)(2,1)}, bf16[2,4,96,128]{3,2,1,0:T(8,128)(2,1)}, bf16[2,4,96,128]{3,2,1,0:T(8,128)(2,1)}, bf16[2,4,96,128]{3,2,1,0:T(8,128)(2,1)}) custom-call(s32[3]{0:T(128)} %pad_add_fusion.meta_ref, f32[1,3072]{1,0:T(1,128)} %gate_ref.3, bf16[128,3072]{1,0:T(8,128)(2,1)} %bitcast.31), custom_call_target="tpu_custom_call" | custom-call | bytes 1572864 | tf_op jit(solution)/shard_map/pallas_call | solution.py:355
  19.8 1.5 %collective-permute-start.6 = (bf16[2,4,96,128]{3,2,1,0:T(8,128)(2,1)}, bf16[2,4,96,128]{3,2,1,0:T(8,128)(2,1)S(1)}, u32[]{:S(2)}, u32[]{:S(2)}) collective-permute-start(bf16[2,4,96,128]{3,2,1,0:T(8,128)(2,1)} %get-tuple-element.53), channel_id=1, source_target_pairs={{0,8},{8,0},{16,24},{24,16},{1,9},{9,1},{17,25},{25,17},{2,10},{10... | collective-permute-start | bytes 589832 | tf_op jit(solution)/shard_map/ppermute | solution.py:621
  21.3 15.2 %collective-permute-done.1.refs_0_ = bf16[2,320,128]{2,1,0:T(8,128)(2,1)S(1)} collective-permute-done((bf16[2,320,128]{2,1,0:T(8,128)(2,1)S(1)}, bf16[2,320,128]{2,1,0:T(8,128)(2,1)S(1)}, u32[]{:S(2)}, u32[]{:S(2)}) %collective-permute-start.1) | collective-permute-done | bytes 163872 | tf_op jit(solution)/shard_map/ppermute | solution.py:614
  36.5 0.2 shard_map.166
  36.6 1.7 %collective-permute-start.2 = (bf16[1,320,128]{2,1,0:T(8,128)(2,1)S(1)}, bf16[1,320,128]{2,1,0:T(8,128)(2,1)S(1)}, u32[]{:S(2)}, u32[]{:S(2)}) collective-permute-start(bf16[1,320,128]{2,1,0:T(8,128)(2,1)S(1)} %get-tuple-element.48), channel_id=1, source_target_pairs={{0,4},{2,6},{4,0},{6,2},{1,5},{3,7},{5,1},{7,3},{8,12},{10,14},{12... | collective-permute-start | bytes 245768 | tf_op jit(solution)/shard_map/ppermute | solution.py:614
  38.4 4.6 %collective-permute-done.2.got_ref = bf16[1,320,128]{2,1,0:T(8,128)(2,1)S(1)} collective-permute-done((bf16[1,320,128]{2,1,0:T(8,128)(2,1)S(1)}, bf16[1,320,128]{2,1,0:T(8,128)(2,1)S(1)}, u32[]{:S(2)}, u32[]{:S(2)}) %collective-permute-start.2) | collective-permute-done | bytes 81952 | tf_op jit(solution)/shard_map/ppermute | solution.py:614
  42.9 0.3 shard_map.168.refs_0_
  43.3 1.7 %collective-permute-start.11 = (bf16[2,4,96,128]{3,2,1,0:T(8,128)(2,1)}, bf16[2,4,96,128]{3,2,1,0:T(8,128)(2,1)}, u32[]{:S(2)}, u32[]{:S(2)}) collective-permute-start(bf16[2,4,96,128]{3,2,1,0:T(8,128)(2,1)} %get-tuple-element.58), channel_id=1, source_target_pairs={{0,16},{8,24},{16,0},{24,8},{1,17},{9,25},{17,1},{25,9},{2,18},{10... | collective-permute-start | bytes 589832 | tf_op jit(solution)/shard_map/ppermute | solution.py:621
  44.9 1.4 %collective-permute-start.12 = (bf16[2,4,96,128]{3,2,1,0:T(8,128)(2,1)}, bf16[2,4,96,128]{3,2,1,0:T(8,128)(2,1)}, u32[]{:S(2)}, u32[]{:S(2)}) collective-permute-start(bf16[2,4,96,128]{3,2,1,0:T(8,128)(2,1)} %get-tuple-element.59), channel_id=1, source_target_pairs={{0,24},{8,16},{16,8},{24,0},{1,25},{9,17},{17,9},{25,1},{2,26},{10... | collective-permute-start | bytes 589832 | tf_op jit(solution)/shard_map/ppermute | solution.py:621
  46.4 2.6 %shard_map.169 = (bf16[128,384]{1,0:T(8,128)(2,1)S(1)}, bf16[128,384]{1,0:T(8,128)(2,1)S(1)}, bf16[128,384]{1,0:T(8,128)(2,1)S(1)}, bf16[32,384]{1,0:T(8,128)(2,1)S(1)}) custom-call(bf16[4912,128]{1,0:T(8,128)(2,1)S(1)} %shard_map.168.refs_0_, bf16[4912,128]{1,0:T(8,128)(2,1)S(1)} %collective-permute-done.7.refs_1_), custom_call_target="tpu_custom_call" | custom-call | flops 695205888 | bytes 2310144 | tf_op jit(solution)/shard_map/pallas_call | solution.py:295
  49.1 0.8 collective-permute-start.8
  49.9 2.1 %collective-permute-start.9 = (bf16[136,384]{1,0:T(8,128)(2,1)S(1)}, bf16[136,384]{1,0:T(8,128)(2,1)S(1)}, u32[]{:S(2)}, u32[]{:S(2)}) collective-permute-start(bf16[136,384]{1,0:T(8,128)(2,1)S(1)} %pad_maximum_fusion.1), channel_id=1, source_target_pairs={{0,6},{2,4},{4,2},{6,0},{1,7},{3,5},{5,3},{7,1},{8,14},{10,12},{12... | collective-permute-start | bytes 313352 | tf_op jit(solution)/shard_map/ppermute | solution.py:614
  52.0 0.8 collective-permute-start.10
  52.9 1.1 shard_map.170
  53.9 5.6 %collective-permute-done.8.refs_0_ = bf16[136,384]{1,0:T(8,128)(2,1)S(1)} collective-permute-done((bf16[136,384]{1,0:T(8,128)(2,1)S(1)}, bf16[136,384]{1,0:T(8,128)(2,1)S(1)}, u32[]{:S(2)}, u32[]{:S(2)}) %collective-permute-start.8) | collective-permute-done | bytes 104480 | tf_op jit(solution)/shard_map/ppermute | solution.py:614
  59.7 1.1 %collective-permute-done.10.refs_2_ = bf16[136,384]{1,0:T(8,128)(2,1)S(1)} collective-permute-done((bf16[136,384]{1,0:T(8,128)(2,1)S(1)}, bf16[136,384]{1,0:T(8,128)(2,1)S(1)}, u32[]{:S(2)}, u32[]{:S(2)}) %collective-permute-start.10) | collective-permute-done | bytes 104480 | tf_op jit(solution)/shard_map/ppermute | solution.py:614
  61.1 1.6 %collective-permute-start.16 = (bf16[128,1536]{1,0:T(8,128)(2,1)S(1)}, bf16[128,1536]{1,0:T(8,128)(2,1)S(1)}, u32[]{:S(2)}, u32[]{:S(2)}) collective-permute-start(bf16[128,1536]{1,0:T(8,128)(2,1)S(1)} %shard_map.171.attn_ref.refs_2_), channel_id=1, source_target_pairs={{0,8},{8,0},{16,24},{24,16},{1,9},{9,1},{17,25},{25,17},{2,10},{10... | collective-permute-start | bytes 1179656 | tf_op jit(solution)/shard_map/ppermute | solution.py:621
  62.7 1.5 %collective-permute-start.15 = (bf16[128,1536]{1,0:T(8,128)(2,1)S(1)}, bf16[128,1536]{1,0:T(8,128)(2,1)S(1)}, u32[]{:S(2)}, u32[]{:S(2)}) collective-permute-start(bf16[128,1536]{1,0:T(8,128)(2,1)S(1)} %shard_map.171.attn_ref.refs_2_), channel_id=1, source_target_pairs={{0,16},{8,24},{16,0},{24,8},{1,17},{9,25},{17,1},{25,9},{2,18},{10... | collective-permute-start | bytes 1179656 | tf_op jit(solution)/shard_map/ppermute | solution.py:621
  64.2 0.4 collective-permute-start.14
  64.6 3.7 %copy-done = bf16[3072,1536]{1,0:T(8,128)(2,1)S(1)} copy-done((bf16[3072,1536]{1,0:T(8,128)(2,1)S(1)}, bf16[3072,1536]{1,0:T(8,128)(2,1)}, u32[]{:S(2)}) %copy-start) | copy-done | bytes 9437208
  68.3 5.7 %shard_map.172 = (bf16[128,3072]{1,0:T(8,128)(2,1)}, bf16[128,1536]{1,0:T(8,128)(2,1)}, f32[4,384]{1,0:T(4,128)S(1)}, bf16[144,1536]{1,0:T(8,128)(2,1)S(1)}) custom-call(s32[3]{0:T(128)S(1)} %copy-done.6, bf16[128,1536]{1,0:T(8,128)(2,1)S(1)} %shard_map.171.attn_ref.refs_2_, bf16[3072,1536]{1,0:T(8,128)(2,1)S(1)} %copy-done, f32[1,3072]{1,0:T(1,128)S(1)} %copy-done.5, ...), custom_call_target="tpu_custom_call" | custom-call | flops 2415919104 | bytes 9437184 | tf_op jit(solution)/shard_map/pallas_call | solution.py:436
  74.0 1.1 shard_map.173
  75.1 0.6 collective-permute-start.13
  75.7 0.1 collective-permute-start.20
  75.8 5.6 %collective-permute-done.15.refs_4_ = bf16[128,1536]{1,0:T(8,128)(2,1)S(1)} collective-permute-done((bf16[128,1536]{1,0:T(8,128)(2,1)S(1)}, bf16[128,1536]{1,0:T(8,128)(2,1)S(1)}, u32[]{:S(2)}, u32[]{:S(2)}) %collective-permute-start.15) | collective-permute-done | bytes 393248 | tf_op jit(solution)/shard_map/ppermute | solution.py:621
  81.3 0.5 collective-permute-start.18
  81.9 1.2 %collective-permute-done.19.refs_8_ = bf16[128,1536]{1,0:T(8,128)(2,1)S(1)} collective-permute-done((bf16[128,1536]{1,0:T(8,128)(2,1)S(1)}, bf16[128,1536]{1,0:T(8,128)(2,1)S(1)}, u32[]{:S(2)}, u32[]{:S(2)}) %collective-permute-start.19) | collective-permute-done | bytes 393248 | tf_op jit(solution)/shard_map/ppermute | solution.py:618
  83.1 0.6 collective-permute-done.18.refs_7_
  83.6 1.4 %shard_map.174 = (f32[1168,128]{1,0:T(8,128)S(1)}, bf16[576,128]{1,0:T(8,128)(2,1)S(1)}, bf16[592,128]{1,0:T(8,128)(2,1)S(1)}, f32[576,128]{1,0:T(8,128)S(1)}, f...) custom-call(bf16[4,4,96,128]{3,2,1,0:T(8,128)(2,1)S(1)} %get-tuple-element.63.refs_0_, ...), custom_call_target="tpu_custom_call" | custom-call | flops 1207959552 | bytes 5111808 | tf_op jit(solution)/shard_map/pallas_call | solution.py:512
  85.0 2.0 %collective-permute-start.23 = (bf16[592,128]{1,0:T(8,128)(2,1)S(1)}, bf16[592,128]{1,0:T(8,128)(2,1)S(1)}, u32[]{:S(2)}, u32[]{:S(2)}) collective-permute-start(bf16[592,128]{1,0:T(8,128)(2,1)S(1)} %get-tuple-element.71), channel_id=1, source_target_pairs={{0,2},{2,0},{4,6},{6,4},{1,3},{3,1},{5,7},{7,5},{8,10},{10,8},{12,... | collective-permute-start | bytes 454664 | tf_op jit(solution)/shard_map/ppermute | solution.py:614
  87.1 0.1 collective-permute-start.21
  87.1 4.7 %collective-permute-done.23.got_ref = bf16[592,128]{1,0:T(8,128)(2,1)S(1)} collective-permute-done((bf16[592,128]{1,0:T(8,128)(2,1)S(1)}, bf16[592,128]{1,0:T(8,128)(2,1)S(1)}, u32[]{:S(2)}, u32[]{:S(2)}) %collective-permute-start.23) | collective-permute-done | bytes 151584 | tf_op jit(solution)/shard_map/ppermute | solution.py:614
  91.9 2.2 %collective-permute-start.24 = (bf16[592,128]{1,0:T(8,128)(2,1)S(1)}, bf16[592,128]{1,0:T(8,128)(2,1)S(1)}, u32[]{:S(2)}, u32[]{:S(2)}) collective-permute-start(bf16[592,128]{1,0:T(8,128)(2,1)S(1)} %get-tuple-element.74), channel_id=1, source_target_pairs={{0,4},{2,6},{4,0},{6,2},{1,5},{3,7},{5,1},{7,3},{8,12},{10,14},{12... | collective-permute-start | bytes 454664 | tf_op jit(solution)/shard_map/ppermute | solution.py:614
  94.1 0.4 collective-permute-done.21.got_ref
  94.6 2.4 %collective-permute-start.22 = (bf16[576,128]{1,0:T(8,128)(2,1)S(1)}, bf16[576,128]{1,0:T(8,128)(2,1)S(1)}, u32[]{:S(2)}, u32[]{:S(2)}) collective-permute-start(bf16[576,128]{1,0:T(8,128)(2,1)S(1)} %shard_map.175), channel_id=1, source_target_pairs={{0,4},{2,6},{4,0},{6,2},{1,5},{3,7},{5,1},{7,3},{8,12},{10,14},{12... | collective-permute-start | bytes 442376 | tf_op jit(solution)/shard_map/ppermute | solution.py:614
  97.0 0.2 collective-permute-start.25
  97.2 10.2 %collective-permute-done.22.far_low = bf16[576,128]{1,0:T(8,128)(2,1)S(1)} collective-permute-done((bf16[576,128]{1,0:T(8,128)(2,1)S(1)}, bf16[576,128]{1,0:T(8,128)(2,1)S(1)}, u32[]{:S(2)}, u32[]{:S(2)}) %collective-permute-start.22) | collective-permute-done | bytes 147488 | tf_op jit(solution)/shard_map/ppermute | solution.py:614
  107.4 0.9 shard_map.177
  (51 shorter events, 0.8 us)
Async XLA Ops:
  1.3 45.1 %copy-start.8 = (s32[1,64]{1,0:T(1,128)S(1)}, s32[1,64]{1,0:T(1,128)}, u32[]{:S(2)}) copy-start(s32[1,64]{1,0:T(1,128)} %src_ref.1) | copy-start | bytes 772
  7.0 5.8 %collective-permute-start = (bf16[4,320,128]{2,1,0:T(8,128)(2,1)}, bf16[4,320,128]{2,1,0:T(8,128)(2,1)S(1)}, u32[]{:S(2)}, u32[]{:S(2)}) collective-permute-start(bf16[4,320,128]{2,1,0:T(8,128)(2,1)} %get-tuple-element.43), channel_id=1, source_target_pairs={{0,1},{2,3},{4,5},{6,7},{1,0},{3,2},{5,4},{7,6},{8,9},{10,11},{12,... | collective-permute-start | bytes 983048 | tf_op jit(solution)/shard_map/ppermute | solution.py:618
  7.5 30.9 %collective-permute-start.3 = (bf16[1152,128]{1,0:T(8,128)(2,1)}, bf16[1152,128]{1,0:T(8,128)(2,1)S(1)}, u32[]{:S(2)}, u32[]{:S(2)}) collective-permute-start(bf16[1152,128]{1,0:T(8,128)(2,1)} %get-tuple-element.50), channel_id=1, source_target_pairs={{0,4},{2,6},{4,0},{6,2},{1,5},{3,7},{5,1},{7,3},{8,12},{10,14},{12... | collective-permute-start | bytes 884744 | tf_op jit(solution)/shard_map/ppermute | solution.py:614
  11.1 27.2 %collective-permute-start.4 = (bf16[1152,128]{1,0:T(8,128)(2,1)}, bf16[1152,128]{1,0:T(8,128)(2,1)S(1)}, u32[]{:S(2)}, u32[]{:S(2)}) collective-permute-start(bf16[1152,128]{1,0:T(8,128)(2,1)} %get-tuple-element.51), channel_id=1, source_target_pairs={{0,6},{2,4},{4,2},{6,0},{1,7},{3,5},{5,3},{7,1},{8,14},{10,12},{12... | collective-permute-start | bytes 884744 | tf_op jit(solution)/shard_map/ppermute | solution.py:614
  12.5 25.9 %collective-permute-start.5 = (bf16[1152,128]{1,0:T(8,128)(2,1)}, bf16[1152,128]{1,0:T(8,128)(2,1)S(1)}, u32[]{:S(2)}, u32[]{:S(2)}) collective-permute-start(bf16[1152,128]{1,0:T(8,128)(2,1)} %get-tuple-element.52), channel_id=1, source_target_pairs={{0,2},{2,0},{4,6},{6,4},{1,3},{3,1},{5,7},{7,5},{8,10},{10,8},{12,... | collective-permute-start | bytes 884744 | tf_op jit(solution)/shard_map/ppermute | solution.py:614
  12.7 1.1 %copy-start.2 = (f32[4,336,128]{2,1,0:T(8,128)S(1)}, f32[4,336,128]{2,1,0:T(8,128)}, u32[]{:S(2)}) copy-start(f32[4,336,128]{2,1,0:T(8,128)} %get-tuple-element.42.own_ref) | copy-start | bytes 2064388
  13.8 1.0 copy-start.3
  15.0 21.5 %collective-permute-start.1 = (bf16[2,320,128]{2,1,0:T(8,128)(2,1)S(1)}, bf16[2,320,128]{2,1,0:T(8,128)(2,1)S(1)}, u32[]{:S(2)}, u32[]{:S(2)}) collective-permute-start(bf16[2,320,128]{2,1,0:T(8,128)(2,1)S(1)} %get-tuple-element.46), channel_id=1, source_target_pairs={{0,2},{2,0},{4,6},{6,4},{1,3},{3,1},{5,7},{7,5},{8,10},{10,8},{12,... | collective-permute-start | bytes 491528 | tf_op jit(solution)/shard_map/ppermute | solution.py:614
  19.8 18.5 %collective-permute-start.6 = (bf16[2,4,96,128]{3,2,1,0:T(8,128)(2,1)}, bf16[2,4,96,128]{3,2,1,0:T(8,128)(2,1)S(1)}, u32[]{:S(2)}, u32[]{:S(2)}) collective-permute-start(bf16[2,4,96,128]{3,2,1,0:T(8,128)(2,1)} %get-tuple-element.53), channel_id=1, source_target_pairs={{0,8},{8,0},{16,24},{24,16},{1,9},{9,1},{17,25},{25,17},{2,10},{10... | collective-permute-start | bytes 589832 | tf_op jit(solution)/shard_map/ppermute | solution.py:621
  36.6 6.3 %collective-permute-start.2 = (bf16[1,320,128]{2,1,0:T(8,128)(2,1)S(1)}, bf16[1,320,128]{2,1,0:T(8,128)(2,1)S(1)}, u32[]{:S(2)}, u32[]{:S(2)}) collective-permute-start(bf16[1,320,128]{2,1,0:T(8,128)(2,1)S(1)} %get-tuple-element.48), channel_id=1, source_target_pairs={{0,4},{2,6},{4,0},{6,2},{1,5},{3,7},{5,1},{7,3},{8,12},{10,14},{12... | collective-permute-start | bytes 245768 | tf_op jit(solution)/shard_map/ppermute | solution.py:614
  42.9 21.7 %copy-start.1 = (bf16[1,128,3072]{2,1,0:T(8,128)(2,1)S(1)}, bf16[1,128,3072]{2,1,0:T(8,128)(2,1)}, u32[]{:S(2)}) copy-start(bf16[1,128,3072]{2,1,0:T(8,128)(2,1)} %param.25) | copy-start | bytes 2359300
  42.9 21.7 %copy-start.5 = (f32[1,3072]{1,0:T(1,128)S(1)}, f32[1,3072]{1,0:T(1,128)}, u32[]{:S(2)}) copy-start(f32[1,3072]{1,0:T(1,128)} %gate_ref.3) | copy-start | bytes 36868
  42.9 21.7 %copy-start.6 = (s32[3]{0:T(128)S(1)}, s32[3]{0:T(128)}, u32[]{:S(2)}) copy-start(s32[3]{0:T(128)} %pad_add_fusion.meta_ref) | copy-start | bytes 40
  43.2 3.3 %collective-permute-start.7 = (bf16[4912,128]{1,0:T(8,128)(2,1)S(1)}, bf16[4912,128]{1,0:T(8,128)(2,1)S(1)}, u32[]{:S(2)}, u32[]{:S(2)}) collective-permute-start(bf16[4912,128]{1,0:T(8,128)(2,1)S(1)} %shard_map.168.refs_0_), channel_id=1, source_target_pairs={{0,1},{2,3},{4,5},{6,7},{1,0},{3,2},{5,4},{7,6},{8,9},{10,11},{12,... | collective-permute-start | bytes 3772424 | tf_op jit(solution)/shard_map/ppermute | solution.py:618
  43.3 17.7 %collective-permute-start.11 = (bf16[2,4,96,128]{3,2,1,0:T(8,128)(2,1)}, bf16[2,4,96,128]{3,2,1,0:T(8,128)(2,1)}, u32[]{:S(2)}, u32[]{:S(2)}) collective-permute-start(bf16[2,4,96,128]{3,2,1,0:T(8,128)(2,1)} %get-tuple-element.58), channel_id=1, source_target_pairs={{0,16},{8,24},{16,0},{24,8},{1,17},{9,25},{17,1},{25,9},{2,18},{10... | collective-permute-start | bytes 589832 | tf_op jit(solution)/shard_map/ppermute | solution.py:621
  44.9 16.1 %collective-permute-start.12 = (bf16[2,4,96,128]{3,2,1,0:T(8,128)(2,1)}, bf16[2,4,96,128]{3,2,1,0:T(8,128)(2,1)}, u32[]{:S(2)}, u32[]{:S(2)}) collective-permute-start(bf16[2,4,96,128]{3,2,1,0:T(8,128)(2,1)} %get-tuple-element.59), channel_id=1, source_target_pairs={{0,24},{8,16},{16,8},{24,0},{1,25},{9,17},{17,9},{25,1},{2,26},{10... | collective-permute-start | bytes 589832 | tf_op jit(solution)/shard_map/ppermute | solution.py:621
  49.1 10.4 %collective-permute-start.8 = (bf16[136,384]{1,0:T(8,128)(2,1)S(1)}, bf16[136,384]{1,0:T(8,128)(2,1)S(1)}, u32[]{:S(2)}, u32[]{:S(2)}) collective-permute-start(bf16[136,384]{1,0:T(8,128)(2,1)S(1)} %pad_maximum_fusion), channel_id=1, source_target_pairs={{0,4},{2,6},{4,0},{6,2},{1,5},{3,7},{5,1},{7,3},{8,12},{10,14},{12... | collective-permute-start | bytes 313352 | tf_op jit(solution)/shard_map/ppermute | solution.py:614
  49.9 9.7 %collective-permute-start.9 = (bf16[136,384]{1,0:T(8,128)(2,1)S(1)}, bf16[136,384]{1,0:T(8,128)(2,1)S(1)}, u32[]{:S(2)}, u32[]{:S(2)}) collective-permute-start(bf16[136,384]{1,0:T(8,128)(2,1)S(1)} %pad_maximum_fusion.1), channel_id=1, source_target_pairs={{0,6},{2,4},{4,2},{6,0},{1,7},{3,5},{5,3},{7,1},{8,14},{10,12},{12... | collective-permute-start | bytes 313352 | tf_op jit(solution)/shard_map/ppermute | solution.py:614
  52.0 8.8 %collective-permute-start.10 = (bf16[136,384]{1,0:T(8,128)(2,1)S(1)}, bf16[136,384]{1,0:T(8,128)(2,1)S(1)}, u32[]{:S(2)}, u32[]{:S(2)}) collective-permute-start(bf16[136,384]{1,0:T(8,128)(2,1)S(1)} %pad_maximum_fusion.2), channel_id=1, source_target_pairs={{0,2},{2,0},{4,6},{6,4},{1,3},{3,1},{5,7},{7,5},{8,10},{10,8},{12,... | collective-permute-start | bytes 313352 | tf_op jit(solution)/shard_map/ppermute | solution.py:614
  61.0 13.1 %copy-start.7 = (bf16[1,8,1536]{2,1,0:T(8,128)(2,1)}, bf16[1,8,1536]{2,1,0:T(8,128)(2,1)S(1)}, u32[]{:S(2)}) copy-start(bf16[1,8,1536]{2,1,0:T(8,128)(2,1)S(1)} %get-tuple-element.79) | copy-start | bytes 73732
  61.0 13.0 %copy-start.4 = (bf16[2,4,96,128]{3,2,1,0:T(8,128)(2,1)S(1)}, bf16[2,4,96,128]{3,2,1,0:T(8,128)(2,1)}, u32[]{:S(2)}) copy-start(bf16[2,4,96,128]{3,2,1,0:T(8,128)(2,1)} %get-tuple-element.62.refs_0_) | copy-start | bytes 589828
  61.1 14.6 %collective-permute-start.16 = (bf16[128,1536]{1,0:T(8,128)(2,1)S(1)}, bf16[128,1536]{1,0:T(8,128)(2,1)S(1)}, u32[]{:S(2)}, u32[]{:S(2)}) collective-permute-start(bf16[128,1536]{1,0:T(8,128)(2,1)S(1)} %shard_map.171.attn_ref.refs_2_), channel_id=1, source_target_pairs={{0,8},{8,0},{16,24},{24,16},{1,9},{9,1},{17,25},{25,17},{2,10},{10... | collective-permute-start | bytes 1179656 | tf_op jit(solution)/shard_map/ppermute | solution.py:621
  62.7 18.6 %collective-permute-start.15 = (bf16[128,1536]{1,0:T(8,128)(2,1)S(1)}, bf16[128,1536]{1,0:T(8,128)(2,1)S(1)}, u32[]{:S(2)}, u32[]{:S(2)}) collective-permute-start(bf16[128,1536]{1,0:T(8,128)(2,1)S(1)} %shard_map.171.attn_ref.refs_2_), channel_id=1, source_target_pairs={{0,16},{8,24},{16,0},{24,8},{1,17},{9,25},{17,1},{25,9},{2,18},{10... | collective-permute-start | bytes 1179656 | tf_op jit(solution)/shard_map/ppermute | solution.py:621
  64.2 17.1 %collective-permute-start.14 = (bf16[128,1536]{1,0:T(8,128)(2,1)S(1)}, bf16[128,1536]{1,0:T(8,128)(2,1)S(1)}, u32[]{:S(2)}, u32[]{:S(2)}) collective-permute-start(bf16[128,1536]{1,0:T(8,128)(2,1)S(1)} %shard_map.171.attn_ref.refs_2_), channel_id=1, source_target_pairs={{0,24},{8,16},{16,8},{24,0},{1,25},{9,17},{17,9},{25,1},{2,26},{10... | collective-permute-start | bytes 1179656 | tf_op jit(solution)/shard_map/ppermute | solution.py:621
  64.6 3.7 %copy-start = (bf16[3072,1536]{1,0:T(8,128)(2,1)S(1)}, bf16[3072,1536]{1,0:T(8,128)(2,1)}, u32[]{:S(2)}) copy-start(bf16[3072,1536]{1,0:T(8,128)(2,1)} %w_ref.3) | copy-start | bytes 28311556
  74.0 7.8 %collective-permute-start.17 = (bf16[144,1536]{1,0:T(8,128)(2,1)S(1)}, bf16[144,1536]{1,0:T(8,128)(2,1)S(1)}, u32[]{:S(2)}, u32[]{:S(2)}) collective-permute-start(bf16[144,1536]{1,0:T(8,128)(2,1)S(1)} %get-tuple-element.65), channel_id=1, source_target_pairs={{0,1},{2,3},{4,5},{6,7},{1,0},{3,2},{5,4},{7,6},{8,9},{10,11},{12,... | collective-permute-start | bytes 1327112 | tf_op jit(solution)/shard_map/ppermute | solution.py:618
  75.1 6.7 %collective-permute-start.13 = (bf16[4,4,96,128]{3,2,1,0:T(8,128)(2,1)S(1)}, bf16[4,4,96,128]{3,2,1,0:T(8,128)(2,1)S(1)}, u32[]{:S(2)}, u32[]{:S(2)}) collective-permute-start(bf16[4,4,96,128]{3,2,1,0:T(8,128)(2,1)S(1)} %get-tuple-element.64), channel_id=1, source_target_pairs={{0,1},{2,3},{4,5},{6,7},{1,0},{3,2},{5,4},{7,6},{8,9},{10,11},{12,... | collective-permute-start | bytes 1179656 | tf_op jit(solution)/shard_map/ppermute | solution.py:618
  75.7 6.2 %collective-permute-start.20 = (bf16[128,1536]{1,0:T(8,128)(2,1)S(1)}, bf16[128,1536]{1,0:T(8,128)(2,1)S(1)}, u32[]{:S(2)}, u32[]{:S(2)}) collective-permute-start(bf16[128,1536]{1,0:T(8,128)(2,1)S(1)} %collective-permute-done.16.refs_5_), channel_id=1, source_target_pairs={{0,1},{2,3},{4,5},{6,7},{1,0},{3,2},{5,4},{7,6},{8,9},{10,11},{12,... | collective-permute-start | bytes 1179656 | tf_op jit(solution)/shard_map/ppermute | solution.py:618
  81.3 1.7 %collective-permute-start.19 = (bf16[128,1536]{1,0:T(8,128)(2,1)S(1)}, bf16[128,1536]{1,0:T(8,128)(2,1)S(1)}, u32[]{:S(2)}, u32[]{:S(2)}) collective-permute-start(bf16[128,1536]{1,0:T(8,128)(2,1)S(1)} %collective-permute-done.15.refs_4_), channel_id=1, source_target_pairs={{0,1},{2,3},{4,5},{6,7},{1,0},{3,2},{5,4},{7,6},{8,9},{10,11},{12,... | collective-permute-start | bytes 1179656 | tf_op jit(solution)/shard_map/ppermute | solution.py:618
  81.3 2.3 %collective-permute-start.18 = (bf16[128,1536]{1,0:T(8,128)(2,1)S(1)}, bf16[128,1536]{1,0:T(8,128)(2,1)S(1)}, u32[]{:S(2)}, u32[]{:S(2)}) collective-permute-start(bf16[128,1536]{1,0:T(8,128)(2,1)S(1)} %collective-permute-done.14.refs_3_), channel_id=1, source_target_pairs={{0,1},{2,3},{4,5},{6,7},{1,0},{3,2},{5,4},{7,6},{8,9},{10,11},{12,... | collective-permute-start | bytes 1179656 | tf_op jit(solution)/shard_map/ppermute | solution.py:618
  85.0 6.8 %collective-permute-start.23 = (bf16[592,128]{1,0:T(8,128)(2,1)S(1)}, bf16[592,128]{1,0:T(8,128)(2,1)S(1)}, u32[]{:S(2)}, u32[]{:S(2)}) collective-permute-start(bf16[592,128]{1,0:T(8,128)(2,1)S(1)} %get-tuple-element.71), channel_id=1, source_target_pairs={{0,2},{2,0},{4,6},{6,4},{1,3},{3,1},{5,7},{7,5},{8,10},{10,8},{12,... | collective-permute-start | bytes 454664 | tf_op jit(solution)/shard_map/ppermute | solution.py:614
  87.1 7.5 %collective-permute-start.21 = (bf16[576,128]{1,0:T(8,128)(2,1)S(1)}, bf16[576,128]{1,0:T(8,128)(2,1)S(1)}, u32[]{:S(2)}, u32[]{:S(2)}) collective-permute-start(bf16[576,128]{1,0:T(8,128)(2,1)S(1)} %get-tuple-element.69), channel_id=1, source_target_pairs={{0,2},{2,0},{4,6},{6,4},{1,3},{3,1},{5,7},{7,5},{8,10},{10,8},{12,... | collective-permute-start | bytes 442376 | tf_op jit(solution)/shard_map/ppermute | solution.py:614
  91.9 15.5 %collective-permute-start.24 = (bf16[592,128]{1,0:T(8,128)(2,1)S(1)}, bf16[592,128]{1,0:T(8,128)(2,1)S(1)}, u32[]{:S(2)}, u32[]{:S(2)}) collective-permute-start(bf16[592,128]{1,0:T(8,128)(2,1)S(1)} %get-tuple-element.74), channel_id=1, source_target_pairs={{0,4},{2,6},{4,0},{6,2},{1,5},{3,7},{5,1},{7,3},{8,12},{10,14},{12... | collective-permute-start | bytes 454664 | tf_op jit(solution)/shard_map/ppermute | solution.py:614
  94.1 13.2 %collective-permute-start.26 = (bf16[592,128]{1,0:T(8,128)(2,1)S(1)}, bf16[592,128]{1,0:T(8,128)(2,1)S(1)}, u32[]{:S(2)}, u32[]{:S(2)}) collective-permute-start(bf16[592,128]{1,0:T(8,128)(2,1)S(1)} %get-tuple-element.76), channel_id=1, source_target_pairs={{0,2},{2,0},{4,6},{6,4},{1,3},{3,1},{5,7},{7,5},{8,10},{10,8},{12,... | collective-permute-start | bytes 454664 | tf_op jit(solution)/shard_map/ppermute | solution.py:614
  94.6 12.8 %collective-permute-start.22 = (bf16[576,128]{1,0:T(8,128)(2,1)S(1)}, bf16[576,128]{1,0:T(8,128)(2,1)S(1)}, u32[]{:S(2)}, u32[]{:S(2)}) collective-permute-start(bf16[576,128]{1,0:T(8,128)(2,1)S(1)} %shard_map.175), channel_id=1, source_target_pairs={{0,4},{2,6},{4,0},{6,2},{1,5},{3,7},{5,1},{7,3},{8,12},{10,14},{12... | collective-permute-start | bytes 442376 | tf_op jit(solution)/shard_map/ppermute | solution.py:614
  97.0 10.4 %collective-permute-start.25 = (bf16[576,128]{1,0:T(8,128)(2,1)S(1)}, bf16[576,128]{1,0:T(8,128)(2,1)S(1)}, u32[]{:S(2)}, u32[]{:S(2)}) collective-permute-start(bf16[576,128]{1,0:T(8,128)(2,1)S(1)} %get-tuple-element.75), channel_id=1, source_target_pairs={{0,2},{2,0},{4,6},{6,4},{1,3},{3,1},{5,7},{7,5},{8,10},{10,8},{12,... | collective-permute-start | bytes 442376 | tf_op jit(solution)/shard_map/ppermute | solution.py:614

commit v20 on v19

--- a/solution.py
+++ b/solution.py
@@ -641,12 +641,10 @@
         G, OC, place, where,
     )
     packed, sent = rest[:G], rest[G:]
-    images = {0: packed[0]}
-    for k in order:
-        images[k] = to_z(packed[k], k)
-    images = [images[k] for k in [0] + order]
+    far = [to_z(packed[k], k) for k in order[:2]]
     got = [to_oc(x, j + 1) for j, x in enumerate(sent)]
-    own, sent, images[0] = text_sum(own, got, text_rows, [packed[0]])
+    own, sent, near, neighbour = text_sum(own, got, text_rows, [packed[0], packed[1]])
+    images = [near] + far + [to_z(neighbour, 1)]
     own, sent = text_sum(own, [to_z(sent, 1)], text_rows)
     got = to_z(sent, 2)
 

time: 109 us -> 107 us (0.982)
  waiting for transfers between devices: 49.1 us -> 44.1 us
  starting transfers between devices: 29.4 us -> 31.7 us
    ppermute x14, waiting for transfers between devices: 41.7 us -> 36.7 us  [to_z(): return lax.ppermute(x, 'seq', perm)]
    ppermute x14, starting transfers between devices: 19.5 us -> 21.8 us  [to_z(): return lax.ppermute(x, 'seq', perm)]
    unnamed x18 -> x20, local copies, waits for them, and re-layouts: 5.76 us -> 6.72 us
  transfers between devices with their start and end apart: 27 -> 27, of which waited for: 10 -> 11; matrix products, arithmetic and copies ran while one was open for 1% -> 1% of each run, Pallas kernels for 12% -> 12%
where the time goes in v20:
time: 107 us
  waiting for transfers between devices  44.1 us (41%)
  starting transfers between devices  31.7 us (30%)
  Pallas kernels  21.6 us (20%)
  local copies, waits for them, and re-layouts  6.82 us (6%)
  between operations  1.46 us (1%)
    ppermute x14, waiting for transfers between devices, to_z(): return lax.ppermute(x, 'seq', perm)  36.7 us
    ppermute x14, starting transfers between devices, to_z(): return lax.ppermute(x, 'seq', perm)  21.8 us
    ppermute x6, starting transfers between devices, to_dp(): return lax.ppermute(x, 'dp', [(a, a ^ k) for a in range(n_dp)])  8.13 us
    unnamed x20, local copies, waits for them, and re-layouts  6.72 us
    pallas_call x1, Pallas kernels, project(): pl.pallas_call(functools.partial(project_kernel, groups, parts, place_of)...  5.7 us
    pallas_call x1, Pallas kernels, text_project(): pl.pallas_call(functools.partial(text_kernel, groups, heads, place_of, wh...  5.66 us
    ppermute x6, waiting for transfers between devices, to_dp(): return lax.ppermute(x, 'dp', [(a, a ^ k) for a in range(n_dp)])  5.55 us
    pallas_call x2, Pallas kernels, attention(): pl.pallas_call(functools.partial(attention_kernel, n_pieces, len(blocks),...  3.71 us
  transfers between devices with their start and end apart: 27, of which 11 were waited for; matrix products, arithmetic and copies ran while one was open for 1% of the time, Pallas kernels for 12%

profile of v20, /device:TPU:0, one launch (start us, length us, event | category | flops | bytes accessed | tf_op | source)
XLA Modules:
  0.0 106.6 jit_solution(14140241176492159622)
XLA Ops:
  1.3 5.7 %shard_map.164 = (f32[4,336,128]{2,1,0:T(8,128)}, bf16[1152,128]{1,0:T(8,128)(2,1)}, bf16[1152,128]{1,0:T(8,128)(2,1)}, bf16[1152,128]{1,0:T(8,128)(2,1)}, bf16[...) custom-call(s32[1]{0:T(128)} %copy.22.len_ref, s32[1,64]{1,0:T(1,128)} %src_ref.1, bf16[64,512]{1,0:T(8,128)(2,1)} %bitcast.36, ...), custom_call_target="tpu_custom_call" | custom-call | flops 301989888 | bytes 4718592 | tf_op jit(solution)/shard_map/pallas_call | solution.py:140
  7.0 0.5 collective-permute-start
  7.5 3.7 %collective-permute-start.3 = (bf16[1152,128]{1,0:T(8,128)(2,1)}, bf16[1152,128]{1,0:T(8,128)(2,1)S(1)}, u32[]{:S(2)}, u32[]{:S(2)}) collective-permute-start(bf16[1152,128]{1,0:T(8,128)(2,1)} %get-tuple-element.52), channel_id=1, source_target_pairs={{0,4},{2,6},{4,0},{6,2},{1,5},{3,7},{5,1},{7,3},{8,12},{10,14},{12... | collective-permute-start | bytes 884744 | tf_op jit(solution)/shard_map/ppermute | solution.py:614
  11.1 1.4 %collective-permute-start.4 = (bf16[1152,128]{1,0:T(8,128)(2,1)}, bf16[1152,128]{1,0:T(8,128)(2,1)S(1)}, u32[]{:S(2)}, u32[]{:S(2)}) collective-permute-start(bf16[1152,128]{1,0:T(8,128)(2,1)} %get-tuple-element.53), channel_id=1, source_target_pairs={{0,6},{2,4},{4,2},{6,0},{1,7},{3,5},{5,3},{7,1},{8,14},{10,12},{12... | collective-permute-start | bytes 884744 | tf_op jit(solution)/shard_map/ppermute | solution.py:614
  12.5 1.1 %copy-done.2 = f32[4,336,128]{2,1,0:T(8,128)S(1)} copy-done((f32[4,336,128]{2,1,0:T(8,128)S(1)}, f32[4,336,128]{2,1,0:T(8,128)}, u32[]{:S(2)}) %copy-start.2) | copy-done | bytes 688152
  13.6 1.0 copy-done.3
  14.6 1.0 copy-done.4
  15.5 0.2 shard_map.165
  15.7 0.3 collective-permute-start.1
  16.0 1.8 %collective-permute-start.5 = (bf16[1152,128]{1,0:T(8,128)(2,1)S(1)}, bf16[1152,128]{1,0:T(8,128)(2,1)S(1)}, u32[]{:S(2)}, u32[]{:S(2)}) collective-permute-start(bf16[1152,128]{1,0:T(8,128)(2,1)S(1)} %get-tuple-element.54), channel_id=1, source_target_pairs={{0,2},{2,0},{4,6},{6,4},{1,3},{3,1},{5,7},{7,5},{8,10},{10,8},{12,... | collective-permute-start | bytes 884744 | tf_op jit(solution)/shard_map/ppermute | solution.py:614
  17.8 0.7 pad_add_fusion.meta_ref
  18.4 2.4 %shard_map.167 = (bf16[2,4,96,128]{3,2,1,0:T(8,128)(2,1)}, bf16[2,4,96,128]{3,2,1,0:T(8,128)(2,1)}, bf16[2,4,96,128]{3,2,1,0:T(8,128)(2,1)}, bf16[2,4,96,128]{3,2,1,0:T(8,128)(2,1)}) custom-call(s32[3]{0:T(128)} %pad_add_fusion.meta_ref, f32[1,3072]{1,0:T(1,128)} %gate_ref.3, bf16[128,3072]{1,0:T(8,128)(2,1)} %bitcast.31), custom_call_target="tpu_custom_call" | custom-call | bytes 1572864 | tf_op jit(solution)/shard_map/pallas_call | solution.py:355
  20.8 1.5 %collective-permute-start.6 = (bf16[2,4,96,128]{3,2,1,0:T(8,128)(2,1)}, bf16[2,4,96,128]{3,2,1,0:T(8,128)(2,1)S(1)}, u32[]{:S(2)}, u32[]{:S(2)}) collective-permute-start(bf16[2,4,96,128]{3,2,1,0:T(8,128)(2,1)} %get-tuple-element.55), channel_id=1, source_target_pairs={{0,8},{8,0},{16,24},{24,16},{1,9},{9,1},{17,25},{25,17},{2,10},{10... | collective-permute-start | bytes 589832 | tf_op jit(solution)/shard_map/ppermute | solution.py:621
  22.3 12.0 %collective-permute-done.1.refs_0_ = bf16[2,320,128]{2,1,0:T(8,128)(2,1)S(1)} collective-permute-done((bf16[2,320,128]{2,1,0:T(8,128)(2,1)S(1)}, bf16[2,320,128]{2,1,0:T(8,128)(2,1)S(1)}, u32[]{:S(2)}, u32[]{:S(2)}) %collective-permute-start.1) | collective-permute-done | bytes 163872 | tf_op jit(solution)/shard_map/ppermute | solution.py:614
  34.5 1.7 %collective-permute-start.2 = (bf16[1,320,128]{2,1,0:T(8,128)(2,1)S(1)}, bf16[1,320,128]{2,1,0:T(8,128)(2,1)S(1)}, u32[]{:S(2)}, u32[]{:S(2)}) collective-permute-start(bf16[1,320,128]{2,1,0:T(8,128)(2,1)S(1)} %get-tuple-element.50), channel_id=1, source_target_pairs={{0,4},{2,6},{4,0},{6,2},{1,5},{3,7},{5,1},{7,3},{8,12},{10,14},{12... | collective-permute-start | bytes 245768 | tf_op jit(solution)/shard_map/ppermute | solution.py:614
  36.2 5.3 %collective-permute-done.2.got_ref = bf16[1,320,128]{2,1,0:T(8,128)(2,1)S(1)} collective-permute-done((bf16[1,320,128]{2,1,0:T(8,128)(2,1)S(1)}, bf16[1,320,128]{2,1,0:T(8,128)(2,1)S(1)}, u32[]{:S(2)}, u32[]{:S(2)}) %collective-permute-start.2) | collective-permute-done | bytes 81952 | tf_op jit(solution)/shard_map/ppermute | solution.py:614
  41.5 0.3 shard_map.168.refs_0_
  41.8 1.7 %collective-permute-start.11 = (bf16[2,4,96,128]{3,2,1,0:T(8,128)(2,1)}, bf16[2,4,96,128]{3,2,1,0:T(8,128)(2,1)}, u32[]{:S(2)}, u32[]{:S(2)}) collective-permute-start(bf16[2,4,96,128]{3,2,1,0:T(8,128)(2,1)} %get-tuple-element.60), channel_id=1, source_target_pairs={{0,16},{8,24},{16,0},{24,8},{1,17},{9,25},{17,1},{25,9},{2,18},{10... | collective-permute-start | bytes 589832 | tf_op jit(solution)/shard_map/ppermute | solution.py:621
  43.5 1.4 %collective-permute-start.12 = (bf16[2,4,96,128]{3,2,1,0:T(8,128)(2,1)}, bf16[2,4,96,128]{3,2,1,0:T(8,128)(2,1)}, u32[]{:S(2)}, u32[]{:S(2)}) collective-permute-start(bf16[2,4,96,128]{3,2,1,0:T(8,128)(2,1)} %get-tuple-element.61), channel_id=1, source_target_pairs={{0,24},{8,16},{16,8},{24,0},{1,25},{9,17},{17,9},{25,1},{2,26},{10... | collective-permute-start | bytes 589832 | tf_op jit(solution)/shard_map/ppermute | solution.py:621
  45.0 2.7 %shard_map.169 = (bf16[128,384]{1,0:T(8,128)(2,1)S(1)}, bf16[128,384]{1,0:T(8,128)(2,1)S(1)}, bf16[128,384]{1,0:T(8,128)(2,1)S(1)}, bf16[32,384]{1,0:T(8,128)(2,1)S(1)}) custom-call(bf16[4912,128]{1,0:T(8,128)(2,1)S(1)} %shard_map.168.refs_0_, bf16[4912,128]{1,0:T(8,128)(2,1)S(1)} %collective-permute-done.7.refs_1_), custom_call_target="tpu_custom_call" | custom-call | flops 695205888 | bytes 2310144 | tf_op jit(solution)/shard_map/pallas_call | solution.py:295
  47.7 1.0 collective-permute-start.8
  48.7 2.7 %collective-permute-start.9 = (bf16[136,384]{1,0:T(8,128)(2,1)S(1)}, bf16[136,384]{1,0:T(8,128)(2,1)S(1)}, u32[]{:S(2)}, u32[]{:S(2)}) collective-permute-start(bf16[136,384]{1,0:T(8,128)(2,1)S(1)} %pad_maximum_fusion.1), channel_id=1, source_target_pairs={{0,6},{2,4},{4,2},{6,0},{1,7},{3,5},{5,3},{7,1},{8,14},{10,12},{12... | collective-permute-start | bytes 313352 | tf_op jit(solution)/shard_map/ppermute | solution.py:614
  51.4 0.6 collective-permute-start.10
  52.0 1.1 shard_map.170
  53.1 5.9 %collective-permute-done.8.refs_0_ = bf16[136,384]{1,0:T(8,128)(2,1)S(1)} collective-permute-done((bf16[136,384]{1,0:T(8,128)(2,1)S(1)}, bf16[136,384]{1,0:T(8,128)(2,1)S(1)}, u32[]{:S(2)}, u32[]{:S(2)}) %collective-permute-start.8) | collective-permute-done | bytes 104480 | tf_op jit(solution)/shard_map/ppermute | solution.py:614
  59.1 0.3 collective-permute-done.10.refs_2_
  59.7 1.6 %collective-permute-start.16 = (bf16[128,1536]{1,0:T(8,128)(2,1)S(1)}, bf16[128,1536]{1,0:T(8,128)(2,1)S(1)}, u32[]{:S(2)}, u32[]{:S(2)}) collective-permute-start(bf16[128,1536]{1,0:T(8,128)(2,1)S(1)} %shard_map.171.attn_ref.refs_2_), channel_id=1, source_target_pairs={{0,8},{8,0},{16,24},{24,16},{1,9},{9,1},{17,25},{25,17},{2,10},{10... | collective-permute-start | bytes 1179656 | tf_op jit(solution)/shard_map/ppermute | solution.py:621
  61.3 1.5 %collective-permute-start.15 = (bf16[128,1536]{1,0:T(8,128)(2,1)S(1)}, bf16[128,1536]{1,0:T(8,128)(2,1)S(1)}, u32[]{:S(2)}, u32[]{:S(2)}) collective-permute-start(bf16[128,1536]{1,0:T(8,128)(2,1)S(1)} %shard_map.171.attn_ref.refs_2_), channel_id=1, source_target_pairs={{0,16},{8,24},{16,0},{24,8},{1,17},{9,25},{17,1},{25,9},{2,18},{10... | collective-permute-start | bytes 1179656 | tf_op jit(solution)/shard_map/ppermute | solution.py:621
  62.8 0.4 collective-permute-start.14
  63.3 3.7 %copy-done = bf16[3072,1536]{1,0:T(8,128)(2,1)S(1)} copy-done((bf16[3072,1536]{1,0:T(8,128)(2,1)S(1)}, bf16[3072,1536]{1,0:T(8,128)(2,1)}, u32[]{:S(2)}) %copy-start) | copy-done | bytes 9437208
  66.9 5.7 %shard_map.172 = (bf16[128,3072]{1,0:T(8,128)(2,1)}, bf16[128,1536]{1,0:T(8,128)(2,1)}, f32[4,384]{1,0:T(4,128)S(1)}, bf16[144,1536]{1,0:T(8,128)(2,1)S(1)}) custom-call(s32[3]{0:T(128)S(1)} %copy-done.7, bf16[128,1536]{1,0:T(8,128)(2,1)S(1)} %shard_map.171.attn_ref.refs_2_, bf16[3072,1536]{1,0:T(8,128)(2,1)S(1)} %copy-done, f32[1,3072]{1,0:T(1,128)S(1)} %copy-done.6, ...), custom_call_target="tpu_custom_call" | custom-call | flops 2415919104 | bytes 9437184 | tf_op jit(solution)/shard_map/pallas_call | solution.py:436
  72.7 1.1 %shard_map.173 = (bf16[4,4,96,128]{3,2,1,0:T(8,128)(2,1)S(1)}, bf16[4,4,96,128]{3,2,1,0:T(8,128)(2,1)S(1)}) custom-call(bf16[2,4,96,128]{3,2,1,0:T(8,128)(2,1)S(1)} %copy-done.5, bf16[2,4,96,128]{3,2,1,0:T(8,128)(2,1)} %collective-permute-done.12.refs_6_.refs_1_, bf16[2,4,96,128]{3,2,1,0:T(8,128)(2,1)} %collective-permute-done.11.refs_5_.refs_2_, ...), custom_call_target="tpu_custom_call" | custom-call | bytes 1572864 | tf_op jit(solution)/shard_map/pallas_call | solution.py:376
  73.7 0.6 collective-permute-start.13
  74.4 5.5 %collective-permute-done.15.refs_4_ = bf16[128,1536]{1,0:T(8,128)(2,1)S(1)} collective-permute-done((bf16[128,1536]{1,0:T(8,128)(2,1)S(1)}, bf16[128,1536]{1,0:T(8,128)(2,1)S(1)}, u32[]{:S(2)}, u32[]{:S(2)}) %collective-permute-start.15) | collective-permute-done | bytes 393248 | tf_op jit(solution)/shard_map/ppermute | solution.py:621
  79.9 0.5 collective-permute-start.18
  80.4 1.2 %collective-permute-done.19.refs_8_ = bf16[128,1536]{1,0:T(8,128)(2,1)S(1)} collective-permute-done((bf16[128,1536]{1,0:T(8,128)(2,1)S(1)}, bf16[128,1536]{1,0:T(8,128)(2,1)S(1)}, u32[]{:S(2)}, u32[]{:S(2)}) %collective-permute-start.19) | collective-permute-done | bytes 393248 | tf_op jit(solution)/shard_map/ppermute | solution.py:618
  81.6 0.6 collective-permute-done.18.refs_7_
  82.2 1.4 %shard_map.174 = (f32[1168,128]{1,0:T(8,128)S(1)}, bf16[576,128]{1,0:T(8,128)(2,1)S(1)}, bf16[592,128]{1,0:T(8,128)(2,1)S(1)}, f32[576,128]{1,0:T(8,128)S(1)}, f...) custom-call(bf16[4,4,96,128]{3,2,1,0:T(8,128)(2,1)S(1)} %get-tuple-element.65.refs_0_, ...), custom_call_target="tpu_custom_call" | custom-call | flops 1207959552 | bytes 5111808 | tf_op jit(solution)/shard_map/pallas_call | solution.py:512
  83.6 1.3 %collective-permute-start.23 = (bf16[592,128]{1,0:T(8,128)(2,1)S(1)}, bf16[592,128]{1,0:T(8,128)(2,1)S(1)}, u32[]{:S(2)}, u32[]{:S(2)}) collective-permute-start(bf16[592,128]{1,0:T(8,128)(2,1)S(1)} %get-tuple-element.73), channel_id=1, source_target_pairs={{0,2},{2,0},{4,6},{6,4},{1,3},{3,1},{5,7},{7,5},{8,10},{10,8},{12,... | collective-permute-start | bytes 454664 | tf_op jit(solution)/shard_map/ppermute | solution.py:614
  84.9 0.8 collective-permute-start.21
  85.7 4.8 %collective-permute-done.23.got_ref = bf16[592,128]{1,0:T(8,128)(2,1)S(1)} collective-permute-done((bf16[592,128]{1,0:T(8,128)(2,1)S(1)}, bf16[592,128]{1,0:T(8,128)(2,1)S(1)}, u32[]{:S(2)}, u32[]{:S(2)}) %collective-permute-start.23) | collective-permute-done | bytes 151584 | tf_op jit(solution)/shard_map/ppermute | solution.py:614
  90.5 2.2 %collective-permute-start.24 = (bf16[592,128]{1,0:T(8,128)(2,1)S(1)}, bf16[592,128]{1,0:T(8,128)(2,1)S(1)}, u32[]{:S(2)}, u32[]{:S(2)}) collective-permute-start(bf16[592,128]{1,0:T(8,128)(2,1)S(1)} %get-tuple-element.76), channel_id=1, source_target_pairs={{0,4},{2,6},{4,0},{6,2},{1,5},{3,7},{5,1},{7,3},{8,12},{10,14},{12... | collective-permute-start | bytes 454664 | tf_op jit(solution)/shard_map/ppermute | solution.py:614
  92.7 1.2 %collective-permute-start.26 = (bf16[592,128]{1,0:T(8,128)(2,1)S(1)}, bf16[592,128]{1,0:T(8,128)(2,1)S(1)}, u32[]{:S(2)}, u32[]{:S(2)}) collective-permute-start(bf16[592,128]{1,0:T(8,128)(2,1)S(1)} %get-tuple-element.78), channel_id=1, source_target_pairs={{0,2},{2,0},{4,6},{6,4},{1,3},{3,1},{5,7},{7,5},{8,10},{10,8},{12,... | collective-permute-start | bytes 454664 | tf_op jit(solution)/shard_map/ppermute | solution.py:614
  94.1 1.7 %collective-permute-start.22 = (bf16[576,128]{1,0:T(8,128)(2,1)S(1)}, bf16[576,128]{1,0:T(8,128)(2,1)S(1)}, u32[]{:S(2)}, u32[]{:S(2)}) collective-permute-start(bf16[576,128]{1,0:T(8,128)(2,1)S(1)} %shard_map.175), channel_id=1, source_target_pairs={{0,4},{2,6},{4,0},{6,2},{1,5},{3,7},{5,1},{7,3},{8,12},{10,14},{12... | collective-permute-start | bytes 442376 | tf_op jit(solution)/shard_map/ppermute | solution.py:614
  95.8 1.5 %collective-permute-start.25 = (bf16[576,128]{1,0:T(8,128)(2,1)S(1)}, bf16[576,128]{1,0:T(8,128)(2,1)S(1)}, u32[]{:S(2)}, u32[]{:S(2)}) collective-permute-start(bf16[576,128]{1,0:T(8,128)(2,1)S(1)} %get-tuple-element.77), channel_id=1, source_target_pairs={{0,2},{2,0},{4,6},{6,4},{1,3},{3,1},{5,7},{7,5},{8,10},{10,8},{12,... | collective-permute-start | bytes 442376 | tf_op jit(solution)/shard_map/ppermute | solution.py:614
  97.4 8.1 %collective-permute-done.22.far_low = bf16[576,128]{1,0:T(8,128)(2,1)S(1)} collective-permute-done((bf16[576,128]{1,0:T(8,128)(2,1)S(1)}, bf16[576,128]{1,0:T(8,128)(2,1)S(1)}, u32[]{:S(2)}, u32[]{:S(2)}) %collective-permute-start.22) | collective-permute-done | bytes 147488 | tf_op jit(solution)/shard_map/ppermute | solution.py:614
  105.5 0.2 collective-permute-done.25.near_low
  105.7 0.9 shard_map.177
  (53 shorter events, 1.2 us)
Async XLA Ops:
  1.3 43.6 %copy-start.9 = (s32[1,64]{1,0:T(1,128)S(1)}, s32[1,64]{1,0:T(1,128)}, u32[]{:S(2)}) copy-start(s32[1,64]{1,0:T(1,128)} %src_ref.1) | copy-start | bytes 772
  7.0 5.5 %collective-permute-start = (bf16[4,320,128]{2,1,0:T(8,128)(2,1)}, bf16[4,320,128]{2,1,0:T(8,128)(2,1)S(1)}, u32[]{:S(2)}, u32[]{:S(2)}) collective-permute-start(bf16[4,320,128]{2,1,0:T(8,128)(2,1)} %get-tuple-element.44), channel_id=1, source_target_pairs={{0,1},{2,3},{4,5},{6,7},{1,0},{3,2},{5,4},{7,6},{8,9},{10,11},{12,... | collective-permute-start | bytes 983048 | tf_op jit(solution)/shard_map/ppermute | solution.py:618
  7.5 28.7 %collective-permute-start.3 = (bf16[1152,128]{1,0:T(8,128)(2,1)}, bf16[1152,128]{1,0:T(8,128)(2,1)S(1)}, u32[]{:S(2)}, u32[]{:S(2)}) collective-permute-start(bf16[1152,128]{1,0:T(8,128)(2,1)} %get-tuple-element.52), channel_id=1, source_target_pairs={{0,4},{2,6},{4,0},{6,2},{1,5},{3,7},{5,1},{7,3},{8,12},{10,14},{12... | collective-permute-start | bytes 884744 | tf_op jit(solution)/shard_map/ppermute | solution.py:614
  11.1 25.0 %collective-permute-start.4 = (bf16[1152,128]{1,0:T(8,128)(2,1)}, bf16[1152,128]{1,0:T(8,128)(2,1)S(1)}, u32[]{:S(2)}, u32[]{:S(2)}) collective-permute-start(bf16[1152,128]{1,0:T(8,128)(2,1)} %get-tuple-element.53), channel_id=1, source_target_pairs={{0,6},{2,4},{4,2},{6,0},{1,7},{3,5},{5,3},{7,1},{8,14},{10,12},{12... | collective-permute-start | bytes 884744 | tf_op jit(solution)/shard_map/ppermute | solution.py:614
  12.5 1.1 %copy-start.2 = (f32[4,336,128]{2,1,0:T(8,128)S(1)}, f32[4,336,128]{2,1,0:T(8,128)}, u32[]{:S(2)}) copy-start(f32[4,336,128]{2,1,0:T(8,128)} %get-tuple-element.43.own_ref) | copy-start | bytes 2064388
  13.6 1.0 copy-start.3
  14.6 1.0 copy-start.4
  15.7 18.6 %collective-permute-start.1 = (bf16[2,320,128]{2,1,0:T(8,128)(2,1)S(1)}, bf16[2,320,128]{2,1,0:T(8,128)(2,1)S(1)}, u32[]{:S(2)}, u32[]{:S(2)}) collective-permute-start(bf16[2,320,128]{2,1,0:T(8,128)(2,1)S(1)} %get-tuple-element.48), channel_id=1, source_target_pairs={{0,2},{2,0},{4,6},{6,4},{1,3},{3,1},{5,7},{7,5},{8,10},{10,8},{12,... | collective-permute-start | bytes 491528 | tf_op jit(solution)/shard_map/ppermute | solution.py:614
  16.0 25.5 %collective-permute-start.5 = (bf16[1152,128]{1,0:T(8,128)(2,1)S(1)}, bf16[1152,128]{1,0:T(8,128)(2,1)S(1)}, u32[]{:S(2)}, u32[]{:S(2)}) collective-permute-start(bf16[1152,128]{1,0:T(8,128)(2,1)S(1)} %get-tuple-element.54), channel_id=1, source_target_pairs={{0,2},{2,0},{4,6},{6,4},{1,3},{3,1},{5,7},{7,5},{8,10},{10,8},{12,... | collective-permute-start | bytes 884744 | tf_op jit(solution)/shard_map/ppermute | solution.py:614
  20.8 15.4 %collective-permute-start.6 = (bf16[2,4,96,128]{3,2,1,0:T(8,128)(2,1)}, bf16[2,4,96,128]{3,2,1,0:T(8,128)(2,1)S(1)}, u32[]{:S(2)}, u32[]{:S(2)}) collective-permute-start(bf16[2,4,96,128]{3,2,1,0:T(8,128)(2,1)} %get-tuple-element.55), channel_id=1, source_target_pairs={{0,8},{8,0},{16,24},{24,16},{1,9},{9,1},{17,25},{25,17},{2,10},{10... | collective-permute-start | bytes 589832 | tf_op jit(solution)/shard_map/ppermute | solution.py:621
  34.5 7.0 %collective-permute-start.2 = (bf16[1,320,128]{2,1,0:T(8,128)(2,1)S(1)}, bf16[1,320,128]{2,1,0:T(8,128)(2,1)S(1)}, u32[]{:S(2)}, u32[]{:S(2)}) collective-permute-start(bf16[1,320,128]{2,1,0:T(8,128)(2,1)S(1)} %get-tuple-element.50), channel_id=1, source_target_pairs={{0,4},{2,6},{4,0},{6,2},{1,5},{3,7},{5,1},{7,3},{8,12},{10,14},{12... | collective-permute-start | bytes 245768 | tf_op jit(solution)/shard_map/ppermute | solution.py:614
  41.5 21.8 %copy-start.1 = (bf16[1,128,3072]{2,1,0:T(8,128)(2,1)S(1)}, bf16[1,128,3072]{2,1,0:T(8,128)(2,1)}, u32[]{:S(2)}) copy-start(bf16[1,128,3072]{2,1,0:T(8,128)(2,1)} %param.25) | copy-start | bytes 2359300
  41.5 21.8 %copy-start.6 = (f32[1,3072]{1,0:T(1,128)S(1)}, f32[1,3072]{1,0:T(1,128)}, u32[]{:S(2)}) copy-start(f32[1,3072]{1,0:T(1,128)} %gate_ref.3) | copy-start | bytes 36868
  41.5 21.8 %copy-start.7 = (s32[3]{0:T(128)S(1)}, s32[3]{0:T(128)}, u32[]{:S(2)}) copy-start(s32[3]{0:T(128)} %pad_add_fusion.meta_ref) | copy-start | bytes 40
  41.7 3.3 %collective-permute-start.7 = (bf16[4912,128]{1,0:T(8,128)(2,1)S(1)}, bf16[4912,128]{1,0:T(8,128)(2,1)S(1)}, u32[]{:S(2)}, u32[]{:S(2)}) collective-permute-start(bf16[4912,128]{1,0:T(8,128)(2,1)S(1)} %shard_map.168.refs_0_), channel_id=1, source_target_pairs={{0,1},{2,3},{4,5},{6,7},{1,0},{3,2},{5,4},{7,6},{8,9},{10,11},{12,... | collective-permute-start | bytes 3772424 | tf_op jit(solution)/shard_map/ppermute | solution.py:618
  41.8 17.8 %collective-permute-start.11 = (bf16[2,4,96,128]{3,2,1,0:T(8,128)(2,1)}, bf16[2,4,96,128]{3,2,1,0:T(8,128)(2,1)}, u32[]{:S(2)}, u32[]{:S(2)}) collective-permute-start(bf16[2,4,96,128]{3,2,1,0:T(8,128)(2,1)} %get-tuple-element.60), channel_id=1, source_target_pairs={{0,16},{8,24},{16,0},{24,8},{1,17},{9,25},{17,1},{25,9},{2,18},{10... | collective-permute-start | bytes 589832 | tf_op jit(solution)/shard_map/ppermute | solution.py:621
  43.5 16.1 %collective-permute-start.12 = (bf16[2,4,96,128]{3,2,1,0:T(8,128)(2,1)}, bf16[2,4,96,128]{3,2,1,0:T(8,128)(2,1)}, u32[]{:S(2)}, u32[]{:S(2)}) collective-permute-start(bf16[2,4,96,128]{3,2,1,0:T(8,128)(2,1)} %get-tuple-element.61), channel_id=1, source_target_pairs={{0,24},{8,16},{16,8},{24,0},{1,25},{9,17},{17,9},{25,1},{2,26},{10... | collective-permute-start | bytes 589832 | tf_op jit(solution)/shard_map/ppermute | solution.py:621
  47.7 11.2 %collective-permute-start.8 = (bf16[136,384]{1,0:T(8,128)(2,1)S(1)}, bf16[136,384]{1,0:T(8,128)(2,1)S(1)}, u32[]{:S(2)}, u32[]{:S(2)}) collective-permute-start(bf16[136,384]{1,0:T(8,128)(2,1)S(1)} %pad_maximum_fusion), channel_id=1, source_target_pairs={{0,4},{2,6},{4,0},{6,2},{1,5},{3,7},{5,1},{7,3},{8,12},{10,14},{12... | collective-permute-start | bytes 313352 | tf_op jit(solution)/shard_map/ppermute | solution.py:614
  48.7 10.4 %collective-permute-start.9 = (bf16[136,384]{1,0:T(8,128)(2,1)S(1)}, bf16[136,384]{1,0:T(8,128)(2,1)S(1)}, u32[]{:S(2)}, u32[]{:S(2)}) collective-permute-start(bf16[136,384]{1,0:T(8,128)(2,1)S(1)} %pad_maximum_fusion.1), channel_id=1, source_target_pairs={{0,6},{2,4},{4,2},{6,0},{1,7},{3,5},{5,3},{7,1},{8,14},{10,12},{12... | collective-permute-start | bytes 313352 | tf_op jit(solution)/shard_map/ppermute | solution.py:614
  51.4 8.1 %collective-permute-start.10 = (bf16[136,384]{1,0:T(8,128)(2,1)S(1)}, bf16[136,384]{1,0:T(8,128)(2,1)S(1)}, u32[]{:S(2)}, u32[]{:S(2)}) collective-permute-start(bf16[136,384]{1,0:T(8,128)(2,1)S(1)} %pad_maximum_fusion.2), channel_id=1, source_target_pairs={{0,2},{2,0},{4,6},{6,4},{1,3},{3,1},{5,7},{7,5},{8,10},{10,8},{12,... | collective-permute-start | bytes 313352 | tf_op jit(solution)/shard_map/ppermute | solution.py:614
  59.6 13.1 %copy-start.8 = (bf16[1,8,1536]{2,1,0:T(8,128)(2,1)}, bf16[1,8,1536]{2,1,0:T(8,128)(2,1)S(1)}, u32[]{:S(2)}) copy-start(bf16[1,8,1536]{2,1,0:T(8,128)(2,1)S(1)} %get-tuple-element.81) | copy-start | bytes 73732
  59.6 13.0 %copy-start.5 = (bf16[2,4,96,128]{3,2,1,0:T(8,128)(2,1)S(1)}, bf16[2,4,96,128]{3,2,1,0:T(8,128)(2,1)}, u32[]{:S(2)}) copy-start(bf16[2,4,96,128]{3,2,1,0:T(8,128)(2,1)} %get-tuple-element.64.refs_0_) | copy-start | bytes 589828
  59.7 14.6 %collective-permute-start.16 = (bf16[128,1536]{1,0:T(8,128)(2,1)S(1)}, bf16[128,1536]{1,0:T(8,128)(2,1)S(1)}, u32[]{:S(2)}, u32[]{:S(2)}) collective-permute-start(bf16[128,1536]{1,0:T(8,128)(2,1)S(1)} %shard_map.171.attn_ref.refs_2_), channel_id=1, source_target_pairs={{0,8},{8,0},{16,24},{24,16},{1,9},{9,1},{17,25},{25,17},{2,10},{10... | collective-permute-start | bytes 1179656 | tf_op jit(solution)/shard_map/ppermute | solution.py:621
  61.3 18.6 %collective-permute-start.15 = (bf16[128,1536]{1,0:T(8,128)(2,1)S(1)}, bf16[128,1536]{1,0:T(8,128)(2,1)S(1)}, u32[]{:S(2)}, u32[]{:S(2)}) collective-permute-start(bf16[128,1536]{1,0:T(8,128)(2,1)S(1)} %shard_map.171.attn_ref.refs_2_), channel_id=1, source_target_pairs={{0,16},{8,24},{16,0},{24,8},{1,17},{9,25},{17,1},{25,9},{2,18},{10... | collective-permute-start | bytes 1179656 | tf_op jit(solution)/shard_map/ppermute | solution.py:621
  62.8 17.1 %collective-permute-start.14 = (bf16[128,1536]{1,0:T(8,128)(2,1)S(1)}, bf16[128,1536]{1,0:T(8,128)(2,1)S(1)}, u32[]{:S(2)}, u32[]{:S(2)}) collective-permute-start(bf16[128,1536]{1,0:T(8,128)(2,1)S(1)} %shard_map.171.attn_ref.refs_2_), channel_id=1, source_target_pairs={{0,24},{8,16},{16,8},{24,0},{1,25},{9,17},{17,9},{25,1},{2,26},{10... | collective-permute-start | bytes 1179656 | tf_op jit(solution)/shard_map/ppermute | solution.py:621
  63.3 3.7 %copy-start = (bf16[3072,1536]{1,0:T(8,128)(2,1)S(1)}, bf16[3072,1536]{1,0:T(8,128)(2,1)}, u32[]{:S(2)}) copy-start(bf16[3072,1536]{1,0:T(8,128)(2,1)} %w_ref.3) | copy-start | bytes 28311556
  72.6 7.8 %collective-permute-start.17 = (bf16[144,1536]{1,0:T(8,128)(2,1)S(1)}, bf16[144,1536]{1,0:T(8,128)(2,1)S(1)}, u32[]{:S(2)}, u32[]{:S(2)}) collective-permute-start(bf16[144,1536]{1,0:T(8,128)(2,1)S(1)} %get-tuple-element.67), channel_id=1, source_target_pairs={{0,1},{2,3},{4,5},{6,7},{1,0},{3,2},{5,4},{7,6},{8,9},{10,11},{12,... | collective-permute-start | bytes 1327112 | tf_op jit(solution)/shard_map/ppermute | solution.py:618
  73.7 6.7 %collective-permute-start.13 = (bf16[4,4,96,128]{3,2,1,0:T(8,128)(2,1)S(1)}, bf16[4,4,96,128]{3,2,1,0:T(8,128)(2,1)S(1)}, u32[]{:S(2)}, u32[]{:S(2)}) collective-permute-start(bf16[4,4,96,128]{3,2,1,0:T(8,128)(2,1)S(1)} %get-tuple-element.66), channel_id=1, source_target_pairs={{0,1},{2,3},{4,5},{6,7},{1,0},{3,2},{5,4},{7,6},{8,9},{10,11},{12,... | collective-permute-start | bytes 1179656 | tf_op jit(solution)/shard_map/ppermute | solution.py:618
  74.3 6.1 %collective-permute-start.20 = (bf16[128,1536]{1,0:T(8,128)(2,1)S(1)}, bf16[128,1536]{1,0:T(8,128)(2,1)S(1)}, u32[]{:S(2)}, u32[]{:S(2)}) collective-permute-start(bf16[128,1536]{1,0:T(8,128)(2,1)S(1)} %collective-permute-done.16.refs_5_), channel_id=1, source_target_pairs={{0,1},{2,3},{4,5},{6,7},{1,0},{3,2},{5,4},{7,6},{8,9},{10,11},{12,... | collective-permute-start | bytes 1179656 | tf_op jit(solution)/shard_map/ppermute | solution.py:618
  79.9 1.7 %collective-permute-start.19 = (bf16[128,1536]{1,0:T(8,128)(2,1)S(1)}, bf16[128,1536]{1,0:T(8,128)(2,1)S(1)}, u32[]{:S(2)}, u32[]{:S(2)}) collective-permute-start(bf16[128,1536]{1,0:T(8,128)(2,1)S(1)} %collective-permute-done.15.refs_4_), channel_id=1, source_target_pairs={{0,1},{2,3},{4,5},{6,7},{1,0},{3,2},{5,4},{7,6},{8,9},{10,11},{12,... | collective-permute-start | bytes 1179656 | tf_op jit(solution)/shard_map/ppermute | solution.py:618
  79.9 2.3 %collective-permute-start.18 = (bf16[128,1536]{1,0:T(8,128)(2,1)S(1)}, bf16[128,1536]{1,0:T(8,128)(2,1)S(1)}, u32[]{:S(2)}, u32[]{:S(2)}) collective-permute-start(bf16[128,1536]{1,0:T(8,128)(2,1)S(1)} %collective-permute-done.14.refs_3_), channel_id=1, source_target_pairs={{0,1},{2,3},{4,5},{6,7},{1,0},{3,2},{5,4},{7,6},{8,9},{10,11},{12,... | collective-permute-start | bytes 1179656 | tf_op jit(solution)/shard_map/ppermute | solution.py:618
  83.6 6.8 %collective-permute-start.23 = (bf16[592,128]{1,0:T(8,128)(2,1)S(1)}, bf16[592,128]{1,0:T(8,128)(2,1)S(1)}, u32[]{:S(2)}, u32[]{:S(2)}) collective-permute-start(bf16[592,128]{1,0:T(8,128)(2,1)S(1)} %get-tuple-element.73), channel_id=1, source_target_pairs={{0,2},{2,0},{4,6},{6,4},{1,3},{3,1},{5,7},{7,5},{8,10},{10,8},{12,... | collective-permute-start | bytes 454664 | tf_op jit(solution)/shard_map/ppermute | solution.py:614
  84.9 9.1 %collective-permute-start.21 = (bf16[576,128]{1,0:T(8,128)(2,1)S(1)}, bf16[576,128]{1,0:T(8,128)(2,1)S(1)}, u32[]{:S(2)}, u32[]{:S(2)}) collective-permute-start(bf16[576,128]{1,0:T(8,128)(2,1)S(1)} %get-tuple-element.71), channel_id=1, source_target_pairs={{0,2},{2,0},{4,6},{6,4},{1,3},{3,1},{5,7},{7,5},{8,10},{10,8},{12,... | collective-permute-start | bytes 442376 | tf_op jit(solution)/shard_map/ppermute | solution.py:614
  90.5 15.2 %collective-permute-start.24 = (bf16[592,128]{1,0:T(8,128)(2,1)S(1)}, bf16[592,128]{1,0:T(8,128)(2,1)S(1)}, u32[]{:S(2)}, u32[]{:S(2)}) collective-permute-start(bf16[592,128]{1,0:T(8,128)(2,1)S(1)} %get-tuple-element.76), channel_id=1, source_target_pairs={{0,4},{2,6},{4,0},{6,2},{1,5},{3,7},{5,1},{7,3},{8,12},{10,14},{12... | collective-permute-start | bytes 454664 | tf_op jit(solution)/shard_map/ppermute | solution.py:614
  92.7 13.0 %collective-permute-start.26 = (bf16[592,128]{1,0:T(8,128)(2,1)S(1)}, bf16[592,128]{1,0:T(8,128)(2,1)S(1)}, u32[]{:S(2)}, u32[]{:S(2)}) collective-permute-start(bf16[592,128]{1,0:T(8,128)(2,1)S(1)} %get-tuple-element.78), channel_id=1, source_target_pairs={{0,2},{2,0},{4,6},{6,4},{1,3},{3,1},{5,7},{7,5},{8,10},{10,8},{12,... | collective-permute-start | bytes 454664 | tf_op jit(solution)/shard_map/ppermute | solution.py:614
  94.1 11.4 %collective-permute-start.22 = (bf16[576,128]{1,0:T(8,128)(2,1)S(1)}, bf16[576,128]{1,0:T(8,128)(2,1)S(1)}, u32[]{:S(2)}, u32[]{:S(2)}) collective-permute-start(bf16[576,128]{1,0:T(8,128)(2,1)S(1)} %shard_map.175), channel_id=1, source_target_pairs={{0,4},{2,6},{4,0},{6,2},{1,5},{3,7},{5,1},{7,3},{8,12},{10,14},{12... | collective-permute-start | bytes 442376 | tf_op jit(solution)/shard_map/ppermute | solution.py:614
  95.8 9.9 %collective-permute-start.25 = (bf16[576,128]{1,0:T(8,128)(2,1)S(1)}, bf16[576,128]{1,0:T(8,128)(2,1)S(1)}, u32[]{:S(2)}, u32[]{:S(2)}) collective-permute-start(bf16[576,128]{1,0:T(8,128)(2,1)S(1)} %get-tuple-element.77), channel_id=1, source_target_pairs={{0,2},{2,0},{4,6},{6,4},{1,3},{3,1},{5,7},{7,5},{8,10},{10,8},{12,... | collective-permute-start | bytes 442376 | tf_op jit(solution)/shard_map/ppermute | solution.py:614
